TPU v7x, 32 devices: a whole 2x2x4 slice. The times are simulated.
32 devices in a mesh: user: 16 (over z, y, core), item: 2 (over x).
Axes of the slice: x: 2, y: 2, z: 4, core: 2. Of those that a mesh axis runs over, the one named last changes fastest.
Arguments:
- user_feat: bfloat16 [32768, 512], P('user'), may hold values from -6 to 6
- cotangent: bfloat16 [32768, 512], P('user'), may hold values from -6 to 6
- gain: float32 [512], replicated, may hold values from 0.25 to 1.75
- item_feat: bfloat16 [2, 2048, 512], P('item', 'user'), may hold values from -6 to 6
- categories: int32 [2, 2048], P('item', 'user'), may hold values from 0 to 7, as said below
- expert_w: bfloat16 [8, 512, 512], P('item'), may hold values from -0.25 to 0.25
- tile_place: int32 [16, 2, 80], P('user', 'item'), may hold values from 0 to 255, as said below
- tile_level: int32 [16, 2, 80, 128, 128], P('user', 'item'), may hold values from 0 to 15
- tile_count: int32 [16, 2], P('user', 'item'), may hold values from 1 to 80, as said below
Outputs:
- user_grad: bfloat16 [32768, 512], P('user', 'item')
- item_grad: bfloat16 [2, 2048, 512], P('item', 'user')
- expert_grad: float32 [8, 512, 512], P('item', 'user')
- gain_grad: float32 [512], P('item')
Inputs may be any that keep to these rules, and one draw needn't show every extreme that they name: The categories of items of item shard j lie in j * 4 to (j + 1) * 4 - 1. `tile_place`: within one device the 80 slots name distinct positions. `tile_count`: slots at or past the count are unused; some device has all 80 slots live.
All inputs are finite; a program needn't handle non-finite values.
Results may differ from a plain program's by a relative error of at most 0.0065.
Values may be sent and summed in bfloat16 or wider, within the bound.
No kernel may reach another device: no remote copies, remote signals or barrier semaphores. Data moves between devices by JAX's collectives and lax.ppermute only.
A program may use at most 128 MiB of HBM per device.

v0:
```python
import jax
import jax.numpy as jnp
from jax import lax
from jax.sharding import PartitionSpec as P

D = 512
TILE = 128


def on_device(
    user_feat, cotangent, gain, item_feat, categories, expert_w, tile_place, tile_level, tile_count
):
    column_index = lax.axis_index("item")
    col_width = D // lax.axis_size("item")
    first_col = column_index * col_width
    own_rows = item_feat[0]
    own_cats = categories[0]
    experts_here = expert_w.shape[0]
    chosen_list = [
        own_cats == column_index * experts_here + expert for expert in range(experts_here)
    ]
    projected = jnp.zeros((own_rows.shape[0], D), jnp.float32)
    for expert in range(experts_here):
        projected = projected + jnp.where(
            chosen_list[expert][:, None],
            jnp.dot(own_rows, expert_w[expert], preferred_element_type=jnp.float32),
            0.0,
        )
    queries = lax.all_gather(projected.astype(jnp.bfloat16), "user", axis=0, tiled=True)
    user_blocks = user_feat.shape[0] // TILE
    item_blocks = queries.shape[0] // TILE
    slot_place = tile_place[0, 0]
    live_count = tile_count[0, 0]
    live_mask = (jnp.arange(slot_place.shape[0], dtype=jnp.int32) < live_count).astype(jnp.float32)
    tile_weights = (
        tile_level[0, 0].astype(jnp.float32) * (1.0 / (2.0 * TILE)) * live_mask[:, None, None]
    ).astype(jnp.bfloat16)
    row_block = slot_place // item_blocks
    col_block = slot_place % item_blocks
    picked = jnp.take(queries.reshape(item_blocks, TILE, D), col_block, axis=0)
    products = jnp.einsum("sij,sjd->sid", tile_weights, picked, preferred_element_type=jnp.float32)
    row_onehot = (row_block[:, None] == jnp.arange(user_blocks, dtype=jnp.int32)[None, :]).astype(
        jnp.float32
    )
    partial_value = jnp.einsum(
        "su,sid->uid", row_onehot, products, precision=lax.Precision.HIGHEST
    ).reshape(user_blocks * TILE, D)
    summed = lax.psum_scatter(partial_value, "item", scatter_dimension=1, tiled=True)
    pre_norm = (
        lax.dynamic_slice_in_dim(user_feat, first_col, col_width, 1).astype(jnp.float32) + summed
    )
    grad_float = lax.dynamic_slice_in_dim(cotangent, first_col, col_width, 1).astype(jnp.float32)
    scaled_grad = lax.dynamic_slice_in_dim(gain, first_col, col_width, 0)[None, :] * grad_float
    squares, crossed = lax.psum(
        (jnp.sum(pre_norm * pre_norm, axis=-1), jnp.sum(scaled_grad * pre_norm, axis=-1)), "item"
    )
    inv_rms = lax.rsqrt(squares / D + 1e-05)[:, None]
    cross_mean = (crossed / D)[:, None]
    user_grad = (inv_rms * scaled_grad - inv_rms**3 * pre_norm * cross_mean).astype(jnp.bfloat16)
    gain_term = jnp.sum(grad_float * pre_norm * inv_rms, axis=0)
    state_grad = lax.all_gather(user_grad, "item", axis=1, tiled=True)
    gain_grad = lax.psum(gain_term, "user")
    lifted = jnp.take(state_grad.reshape(user_blocks, TILE, D), row_block, axis=0)
    back_prod = jnp.einsum("sij,sid->sjd", tile_weights, lifted, preferred_element_type=jnp.float32)
    col_onehot = (col_block[:, None] == jnp.arange(item_blocks, dtype=jnp.int32)[None, :]).astype(
        jnp.float32
    )
    item_term = jnp.einsum(
        "sc,sjd->cjd", col_onehot, back_prod, precision=lax.Precision.HIGHEST
    ).reshape(item_blocks * TILE, D)
    item_sums = lax.psum_scatter(item_term, "user", scatter_dimension=0, tiled=True).astype(
        jnp.bfloat16
    )
    item_total = jnp.zeros((own_rows.shape[0], D), jnp.float32)
    for expert in range(experts_here):
        item_total = item_total + jnp.where(
            chosen_list[expert][:, None],
            jnp.dot(item_sums, expert_w[expert].T, preferred_element_type=jnp.float32),
            0.0,
        )
    grad_list = []
    for expert in range(experts_here):
        masked = jnp.where(chosen_list[expert][:, None], own_rows, jnp.zeros_like(own_rows))
        grad_list.append(
            lax.dot_general(
                masked, item_sums, (((0,), (0,)), ((), ())), preferred_element_type=jnp.float32
            )
        )
    expert_grad = lax.psum_scatter(jnp.stack(grad_list), "user", scatter_dimension=1, tiled=True)
    return (user_grad, item_total.astype(jnp.bfloat16)[None], expert_grad, gain_grad)


def solution(mesh):
    placed = (
        P("user", None),
        P("user", None),
        P(),
        P("item", "user", None),
        P("item", "user"),
        P("item", None, None),
        P("user", "item", None),
        P("user", "item", None, None, None),
        P("user", "item"),
    )
    return jax.shard_map(
        on_device,
        mesh=mesh,
        in_specs=placed,
        out_specs=(P("user", "item"), P("item", "user", None), P("item", "user", None), P("item")),
        check_vma=False,
    )
```

profile of v0, /device:TPU:0, one launch (start us, length us, event | category | flops | bytes accessed | tf_op | source)
XLA Modules:
  0.0 422.0 jit_solution(10154189149470587536)
XLA Ops:
  7.2 0.0 copy-start.1
  7.2 0.0 copy-start.3
  7.2 0.0 all-gather.3.cloned.1.call-start
  7.2 0.7 compare_bitcast_fusion
  7.9 1.3 convolution_select_fusion.6
  9.3 1.3 fusion.20
  10.6 1.3 fusion.21
  12.0 1.9 fusion.27
  13.9 0.0 all-gather.3.cloned.1.call-update
  13.9 0.0 reduce-scatter.4.cloned.1.call-start
  14.7 43.5 %all-gather.3.cloned.1.call-done = bf16[2048,512]{1,0:T(8,128)(2,1)} async-done(((bf16[128,512]{1,0:T(8,128)(2,1)}), bf16[2048,512]{1,0:T(8,128)(2,1)}) %all-gather.3.cloned.1.call-update) | async-done | bytes 2097168 | tf_op jit(solution)/shard_map/all_gather | solution.py:29
  58.2 7.9 %gather_fusion = bf16[80,128,512]{2,1,0:T(8,128)(2,1)} fusion(bf16[16,128,512]{2,1,0:T(8,128)(2,1)} %bitcast.98, s32[1024]{0:T(1024)S(1)} %pad_clamp_fusion.1), kind=kCustom, calls=%fused_computation.clone | custom fusion | bytes 20971840 | tf_op jit(solution)/shard_map/jit(_take)/gather | solution.py:40
  66.1 15.5 %fusion.6 = f32[80,128,512]{2,1,0:T(8,128)} fusion(bf16[80,128,512]{2,1,0:T(8,128)(2,1)} %gather_fusion, pred[80]{0:T(512)(128)(4,1)S(1)} %get-tuple-element.13, s32[1,1,80,128,128]{4,3,2,1,0:T(8,128)} %param.18, f32[80]{0:T(128)S(1)} %compare_select_fusion.2), kind=kOutput, calls=%fused_computation.8 | convolution fusion | flops 1351352320 | bytes 36700560 | tf_op jit(solution)/shard_map/sij,sjd->sid/dot_general | solution.py:41
  81.6 23.9 %fusion.2 = f32[16,128,512]{2,0,1:T(8,128)S(1)} fusion(f32[80,128,512]{2,1,0:T(8,128)} %fusion.6, s32[80]{0:T(128)S(1)} %get-tuple-element.8), kind=kOutput, calls=%fused_computation.4 | convolution fusion | flops 1006634240 | bytes 25166144 | tf_op jit(solution)/shard_map/su,sid->uid/dot_general | solution.py:45
  105.5 4.4 %copy.13 = f32[16,128,512]{2,1,0:T(8,128)} copy(f32[16,128,512]{2,0,1:T(8,128)S(1)} %fusion.2) | data formatting | bytes 8388608 | tf_op jit(solution)/shard_map/su,sid->uid/dot_general | solution.py:45
  109.8 0.0 reduce-scatter.4.cloned.1.call-update
  109.9 0.0 all-gather.5.cloned.1.call-start
  109.9 0.6 copy-done.4
  110.5 0.1 dynamic_slice.10
  110.6 52.5 %reduce-scatter.4.cloned.1.call-done = f32[2048,256]{1,0:T(8,128)} async-done(((f32[2048,512]{1,0:T(8,128)}), f32[2048,256]{1,0:T(8,128)}) %reduce-scatter.4.cloned.1.call-update) | async-done | bytes 2097168 | tf_op jit(solution)/shard_map/reduce_scatter | solution.py:48
  163.1 2.4 multiply_reduce_fusion
  165.4 5.0 %psum.21 = f32[2048]{0:T(1024)S(1)} all-reduce(f32[2048]{0:T(1024)S(1)} %multiply_reduce_fusion), channel_id=1, replica_groups=mesh['user'=16,'item'=2] {'item'}, use_global_device_ids=true, to_apply=%region_2.4 | all-reduce | flops 2048 | bytes 16384 | tf_op jit(solution)/shard_map/psum | solution.py:54
  170.5 2.4 fusion.19
  172.9 5.0 %psum.22 = f32[2048]{0:T(1024)S(1)} all-reduce(f32[2048]{0:T(1024)S(1)} %get-tuple-element.6), channel_id=1, replica_groups=mesh['user'=16,'item'=2] {'item'}, use_global_device_ids=true, to_apply=%region_4.6 | all-reduce | flops 2048 | bytes 16384 | tf_op jit(solution)/shard_map/psum | solution.py:54
  177.9 3.0 fusion.16
  180.9 0.0 all-gather.5.cloned.1.call-update
  180.9 0.0 reduce-scatter.6.cloned.1.call-start
  181.0 33.2 %all-gather.5.cloned.1.call-done = bf16[2048,512]{1,0:T(8,128)(2,1)} async-done(((bf16[2048,256]{1,0:T(8,128)(2,1)}), bf16[2048,512]{1,0:T(8,128)(2,1)}) %all-gather.5.cloned.1.call-update) | async-done | bytes 2097168 | tf_op jit(solution)/shard_map/all_gather | solution.py:61
  214.2 7.9 %gather_fusion.1 = bf16[80,128,512]{2,1,0:T(8,128)(2,1)} fusion(bf16[16,128,512]{2,1,0:T(8,128)(2,1)} %bitcast.99, s32[1024]{0:T(1024)S(1)} %pad_clamp_fusion), kind=kCustom, calls=%fused_computation.1.clone | custom fusion | bytes 20971840 | tf_op jit(solution)/shard_map/jit(_take)/gather | solution.py:63
  222.0 15.6 %fusion.4 = f32[80,128,512]{2,1,0:T(8,128)} fusion(bf16[80,128,512]{2,1,0:T(8,128)(2,1)} %gather_fusion.1, pred[80]{0:T(512)(128)(4,1)S(1)} %get-tuple-element.7, s32[1,1,80,128,128]{4,3,2,1,0:T(8,128)} %param.18, f32[80]{0:T(128)S(1)} %compare_select_fusion.2), kind=kOutput, calls=%fused_computation.6 | convolution fusion | flops 1351352320 | bytes 36700560 | tf_op jit(solution)/shard_map/sij,sid->sjd/dot_general | solution.py:64
  237.6 24.0 %fusion = f32[16,128,512]{2,0,1:T(8,128)S(1)} fusion(f32[80,128,512]{2,1,0:T(8,128)} %fusion.4, s32[80]{0:T(128)S(1)} %get-tuple-element.14), kind=kOutput, calls=%fused_computation.2 | convolution fusion | flops 1006634240 | bytes 25166144 | tf_op jit(solution)/shard_map/sc,sjd->cjd/dot_general | solution.py:68
  261.6 4.4 %copy.14 = f32[16,128,512]{2,1,0:T(8,128)} copy(f32[16,128,512]{2,0,1:T(8,128)S(1)} %fusion) | data formatting | bytes 8388608 | tf_op jit(solution)/shard_map/sc,sjd->cjd/dot_general | solution.py:68
  266.0 0.0 reduce-scatter.6.cloned.1.call-update
  266.0 0.0 reduce-scatter.8.cloned.1.call-start
  266.0 72.5 %reduce-scatter.6.cloned.1.call-done = f32[128,512]{1,0:T(8,128)} async-done(((f32[2048,512]{1,0:T(8,128)}), f32[128,512]{1,0:T(8,128)}) %reduce-scatter.6.cloned.1.call-update) | async-done | bytes 262160 | tf_op jit(solution)/shard_map/reduce_scatter | solution.py:71
  338.5 1.0 convert_element_type.41
  339.5 0.4 convolution_bitcast_fusion
  339.9 0.4 convolution_bitcast_fusion.1
  340.3 0.4 convolution_bitcast_fusion.3
  340.7 0.4 convolution_bitcast_fusion.2
  341.1 2.4 pad_maximum_fusion
  343.4 0.0 reduce-scatter.8.cloned.1.call-update
  343.4 30.9 %psum.23 = f32[256]{0:T(256)} all-reduce(f32[256]{0:T(256)S(1)} %get-tuple-element.5), channel_id=1, replica_groups=mesh['user'=16,'item'=2] {'user'}, use_global_device_ids=true, to_apply=%region_8.10 | all-reduce | flops 256 | bytes 2048 | tf_op jit(solution)/shard_map/psum | solution.py:62
  374.3 0.3 convolution_select_fusion.2
  374.6 0.3 fusion.23
  374.9 0.3 fusion.24
  375.3 1.0 fusion.28
  376.2 39.3 %reduce-scatter.8.cloned.1.call-done = f32[4,32,512]{2,1,0:T(8,128)} async-done(((f32[4,512,512]{2,1,0:T(8,128)}), f32[4,32,512]{2,1,0:T(8,128)}) %reduce-scatter.8.cloned.1.call-update) | async-done | bytes 262160 | tf_op jit(solution)/shard_map/reduce_scatter | solution.py:89
  (15 shorter events, 0.1 us)
Async XLA Ops:
  7.2 4.8 %copy-start.1 = (bf16[1,128,512]{2,1,0:T(8,128)(2,1)S(1)}, bf16[1,128,512]{2,1,0:T(8,128)(2,1)}, u32[]{:S(2)}) copy-start(bf16[1,128,512]{2,1,0:T(8,128)(2,1)} %param.14) | copy-start | bytes 393220
  7.2 7.5 %copy-start.3 = (s32[1,1,80]{2,1,0:T(1,128)S(1)}, s32[1,1,80]{2,1,0:T(1,128)}, u32[]{:S(2)}) copy-start(s32[1,1,80]{2,1,0:T(1,128)} %param.17) | copy-start | bytes 964
  7.2 51.0 %all-gather.3.cloned.1.call-start = ((), (), s32[]{:S(2)}) async-start(), calls=%async_computation.3 | async-start | bytes 2228224 | tf_op jit(solution)/shard_map/all_gather | solution.py:29
  13.9 149.1 %reduce-scatter.4.cloned.1.call-start = ((), (), s32[]{:S(2)}) async-start(), calls=%async_computation.4 | async-start | bytes 6291456 | tf_op jit(solution)/shard_map/reduce_scatter | solution.py:48
  109.8 0.7 copy-start.4
  109.9 104.3 %all-gather.5.cloned.1.call-start = ((), (), s32[]{:S(2)}) async-start(), calls=%async_computation.5 | async-start | bytes 3145728 | tf_op jit(solution)/shard_map/all_gather | solution.py:61
  163.1 7.4 %copy-start = (f32[2048,256]{1,0:T(8,128)S(1)}, f32[2048,256]{1,0:T(8,128)}, u32[]{:S(2)}) copy-start(f32[2048,256]{1,0:T(8,128)} %reduce-scatter.4.cloned.1.call-done) | copy-start | bytes 6291460
  180.9 157.6 %reduce-scatter.6.cloned.1.call-start = ((), (), s32[]{:S(2)}) async-start(), calls=%async_computation.6 | async-start | bytes 4456448 | tf_op jit(solution)/shard_map/reduce_scatter | solution.py:71
  266.0 149.5 %reduce-scatter.8.cloned.1.call-start = ((), (), s32[]{:S(2)}) async-start(), calls=%async_computation.7 | async-start | bytes 4456448 | tf_op jit(solution)/shard_map/reduce_scatter | solution.py:89
  343.4 30.9 %copy-start.2 = (bf16[4,512,512]{2,1,0:T(8,128)(2,1)S(1)}, bf16[4,512,512]{2,1,0:T(8,128)(2,1)}, u32[]{:S(2)}) copy-start(bf16[4,512,512]{2,1,0:T(8,128)(2,1)} %param.16) | copy-start | bytes 6291460
Sparse Core Ops, SparseCore 0:
  14.1 44.0 all-gather.2
  110.0 53.0 reduce-scatter.3
  181.0 33.1 all-gather.4
  266.1 72.3 reduce-scatter.5
  343.6 71.9 reduce-scatter.7
where the time goes:
time: 422 us
  waiting for transfers between devices  241 us (57%)
  matrix products  88.4 us (21%)
  blocking collectives  40.9 us (10%)
  local copies, waits for them, and re-layouts  25.1 us (6%)
  between operations  14.6 us (3%)
  other arithmetic  11.8 us (3%)
    reduce_scatter x1, waiting for transfers between devices, on_device(): lax.psum_scatter(item_term, 'user', scatter_dimension=0, tiled=True)  72.5 us
    reduce_scatter x1, waiting for transfers between devices, on_device(): lax.psum_scatter(partial_value, 'item', scatter_dimension=1, tiled=True)  52.5 us
    all_gather x1, waiting for transfers between devices, on_device(): lax.all_gather(projected.astype(jnp.bfloat16), 'user', axis=0, tiled=True)  43.5 us
    reduce_scatter x1, waiting for transfers between devices, on_device(): lax.psum_scatter(jnp.stack(grad_list), 'user', scatter_dimension=1, tiled...  39.3 us
    all_gather x1, waiting for transfers between devices, on_device(): state_grad = lax.all_gather(user_grad, 'item', axis=1, tiled=True)  33.2 us
    psum x1, blocking collectives, on_device(): gain_grad = lax.psum(gain_term, 'user')  30.9 us
    dot_general x1, matrix products, on_device(): jnp.einsum('sc,sjd->cjd', col_onehot, back_prod, precision=lax.Precision....  24 us
    dot_general x1, matrix products, on_device(): jnp.einsum('su,sid->uid', row_onehot, products, precision=lax.Precision.H...  23.9 us
  transfers between devices with their start and end apart: 5, of which 5 were waited for; matrix products, arithmetic and copies ran while one was open for 0% of the time, Pallas kernels for 0%

commit v1 on v0

v1 whole, which is shorter than its diff:
```python
import functools

import jax
import jax.numpy as jnp
from jax import lax
from jax.experimental import pallas as pl
from jax.experimental.pallas import tpu as pltpu
from jax.sharding import PartitionSpec as P

TILE = 128
SLOTS_PER_STEP = 8
ROW_CHUNKS = 4


def place_tiles(item_blocks, place_ref, count_ref, level_ref, dense_ref):
    step = pl.program_id(0)

    @pl.when(step == 0)
    def _():
        dense_ref[...] = jnp.zeros_like(dense_ref)

    for offset in range(level_ref.shape[0]):
        slot = step * level_ref.shape[0] + offset

        @pl.when(slot < count_ref[0])
        def _():
            place = place_ref[slot]
            row = pl.multiple_of((place // item_blocks) * TILE, TILE)
            col = pl.multiple_of((place % item_blocks) * TILE, TILE)
            weights = level_ref[offset].astype(jnp.float32) * (1.0 / (2.0 * TILE))
            dense_ref[pl.ds(row, TILE), pl.ds(col, TILE)] = weights.astype(jnp.bfloat16)


def dense_tiles(place, count, level, users, items):
    slots = level.shape[0]
    per_step = SLOTS_PER_STEP if slots % SLOTS_PER_STEP == 0 else 1
    return pl.pallas_call(
        functools.partial(place_tiles, items // TILE),
        out_shape=jax.ShapeDtypeStruct((users, items), jnp.bfloat16),
        grid_spec=pltpu.PrefetchScalarGridSpec(
            num_scalar_prefetch=2,
            grid=(slots // per_step,),
            in_specs=[
                pl.BlockSpec((per_step, TILE, TILE), lambda step, place_ref, count_ref: (step, 0, 0))
            ],
            out_specs=pl.BlockSpec((users, items), lambda step, place_ref, count_ref: (0, 0)),
        ),
        compiler_params=pltpu.CompilerParams(
            dimension_semantics=("arbitrary",), vmem_limit_bytes=40 * 1024 * 1024
        ),
        cost_estimate=pl.CostEstimate(
            flops=slots * TILE * TILE,
            bytes_accessed=slots * TILE * TILE * 4 + users * items * 2,
            transcendentals=0,
        ),
        name="place_tiles",
    )(place, count, level)


def over_items(partial, size):
    total = None
    for shift in range(1, size):
        pairs = [(source, (source + shift) % size) for source in range(size)]
        arrived = lax.ppermute(partial, "item", pairs).astype(jnp.float32)
        total = arrived if total is None else total + arrived
    return total


def scatter_sum(terms, size):
    cores, sides = 2, 2
    layers = size // (cores * sides)
    index = lax.axis_index("user")
    core, side, layer = index % cores, (index // cores) % sides, index // (cores * sides)
    rest = terms.shape[1:]
    terms = terms.reshape((layers, sides, cores) + rest)

    def flip(value, bit):
        return lax.ppermute(value, "user", [(source, source ^ bit) for source in range(size)])

    own = lax.dynamic_index_in_dim(terms, core, 2, keepdims=False)
    away = lax.dynamic_index_in_dim(terms, 1 - core, 2, keepdims=False).astype(jnp.bfloat16)
    terms = own + flip(away, 1).astype(jnp.float32)
    own = lax.dynamic_index_in_dim(terms, side, 1, keepdims=False)
    away = lax.dynamic_index_in_dim(terms, 1 - side, 1, keepdims=False).astype(jnp.bfloat16)
    terms = own + flip(away, 2).astype(jnp.float32)
    total = lax.dynamic_index_in_dim(terms, layer, 0, keepdims=False)
    step = cores * sides
    for shift in range(1, layers):
        away = lax.dynamic_index_in_dim(terms, (layer + shift) % layers, 0, keepdims=False)
        pairs = [(source, (source + shift * step) % size) for source in range(size)]
        total = total + lax.ppermute(away.astype(jnp.bfloat16), "user", pairs).astype(jnp.float32)
    return total


def on_device(
    user_feat, cotangent, gain, item_feat, categories, expert_w, tile_place, tile_level, tile_count
):
    users, width = user_feat.shape
    user_size, item_size = lax.axis_size("user"), lax.axis_size("item")
    item_index = lax.axis_index("item")
    own_items = item_feat.shape[1]
    items = own_items * user_size
    experts_here = expert_w.shape[0]
    first_expert = item_index * experts_here
    own_cats = categories[0]

    feats = lax.all_gather(item_feat[0], "user", axis=0, tiled=True)
    all_cats = lax.all_gather(own_cats, "user", axis=0, tiled=True)
    dense = dense_tiles(tile_place[0, 0], tile_count[0], tile_level[0, 0], users, items)

    queries = jnp.zeros((items, width), jnp.float32)
    for expert in range(experts_here):
        queries = queries + jnp.where(
            (all_cats == first_expert + expert)[:, None],
            jnp.dot(feats, expert_w[expert], preferred_element_type=jnp.float32),
            0.0,
        )
    queries = queries.astype(jnp.bfloat16)

    rows = users // ROW_CHUNKS
    grads, gain_term = [], jnp.zeros((width,), jnp.float32)
    for chunk in range(ROW_CHUNKS):
        part = slice(chunk * rows, (chunk + 1) * rows)
        partial = jnp.dot(dense[part], queries, preferred_element_type=jnp.float32)
        partial = partial.astype(jnp.bfloat16)
        pre_norm = user_feat[part].astype(jnp.float32) + partial.astype(jnp.float32)
        pre_norm = pre_norm + over_items(partial, item_size)
        grad_float = cotangent[part].astype(jnp.float32)
        scaled_grad = gain[None, :] * grad_float
        inv_rms = lax.rsqrt(jnp.mean(pre_norm * pre_norm, axis=-1, keepdims=True) + 1e-05)
        cross_mean = jnp.mean(scaled_grad * pre_norm, axis=-1, keepdims=True)
        grads.append(
            (inv_rms * scaled_grad - inv_rms**3 * pre_norm * cross_mean).astype(jnp.bfloat16)
        )
        gain_term = gain_term + jnp.sum(grad_float * pre_norm * inv_rms, axis=0)
    state_grad = jnp.concatenate(grads, axis=0)
    col_width = width // item_size
    user_grad = lax.dynamic_slice_in_dim(state_grad, item_index * col_width, col_width, 1)
    gain_own = lax.dynamic_slice_in_dim(gain_term, item_index * col_width, col_width, 0)
    gain_grad = jnp.sum(lax.all_gather(gain_own, "user", axis=0), axis=0)

    item_terms = lax.dot_general(
        state_grad, dense, (((0,), (0,)), ((), ())), preferred_element_type=jnp.float32
    )
    own_width = width // user_size
    sums = scatter_sum(item_terms.reshape(user_size, own_width, items), user_size)
    sums = sums.astype(jnp.bfloat16)

    chosen = all_cats[None, :] == first_expert + jnp.arange(experts_here, dtype=jnp.int32)[:, None]
    masked = jnp.where(chosen[:, None, :], sums[None], jnp.zeros_like(sums)[None])
    expert_cols = lax.dot_general(
        feats,
        masked.reshape(experts_here * own_width, items),
        (((0,), (1,)), ((), ())),
        preferred_element_type=jnp.float32,
    )
    swapped = lax.all_to_all(
        expert_cols.reshape(user_size, own_width, experts_here * own_width), "user", 0, 0
    )
    expert_grad = (
        swapped.reshape(user_size, own_width, experts_here, own_width)
        .transpose(2, 1, 0, 3)
        .reshape(experts_here, own_width, width)
    )

    by_item = sums.reshape(own_width, user_size, own_items).transpose(1, 0, 2)
    own_sums = lax.all_to_all(by_item, "user", 0, 0).reshape(width, own_items)
    item_total = jnp.zeros((own_items, width), jnp.float32)
    for expert in range(experts_here):
        item_total = item_total + jnp.where(
            (own_cats == first_expert + expert)[:, None],
            lax.dot_general(
                own_sums,
                expert_w[expert],
                (((0,), (1,)), ((), ())),
                preferred_element_type=jnp.float32,
            ),
            0.0,
        )
    return (user_grad, item_total.astype(jnp.bfloat16)[None], expert_grad, gain_grad)


def solution(mesh):
    placed = (
        P("user", None),
        P("user", None),
        P(),
        P("item", "user", None),
        P("item", "user"),
        P("item", None, None),
        P("user", "item", None),
        P("user", "item", None, None, None),
        P("user", "item"),
    )
    return jax.shard_map(
        on_device,
        mesh=mesh,
        in_specs=placed,
        out_specs=(P("user", "item"), P("item", "user", None), P("item", "user", None), P("item")),
        check_vma=False,
    )
```

time: 422 us -> 220 us (0.52)
  waiting for transfers between devices: 241 us -> 76.3 us
  matrix products: 88.4 us -> 26.8 us
  starting transfers between devices: 0.21 us -> 16.4 us
  local copies, waits for them, and re-layouts: 25.1 us -> 16.9 us
  blocking collectives: 40.9 us -> 48.8 us
  other arithmetic: 11.8 us -> 16.8 us
    reduce_scatter x3 -> x0, waiting for transfers between devices: 164 us -> none  [the longest x1 72.5 us: on_device(): lax.psum_scatter(item_term, 'user', scatter_dimension=0, tiled=True)]
    all_gather x2 -> x1, waiting for transfers between devices: 76.7 us -> 14.1 us  [on_device(): feats = lax.all_gather(item_feat[0], 'user', axis=0, tiled=True)]
    dot_general x16 -> x14, matrix products: 88.4 us -> 26.8 us  [the longest x4 8.95 us: on_device(): partial = jnp.dot(dense[part], queries, preferred_element_type=jnp.float32)]
    ppermute x0 -> x9, waiting for transfers between devices: none -> 48.9 us  [the longest x4 37.9 us: over_items(): arrived = lax.ppermute(partial, 'item', pairs).astype(jnp.float32)]
    all_gather x0 -> x2, blocking collectives: none -> 48.8 us  [the longest x1 25.9 us: on_device(): gain_grad = jnp.sum(lax.all_gather(gain_own, 'user', axis=0), axis=0)]
    psum x3 -> x0, blocking collectives: 40.9 us -> none  [the longest x1 30.9 us: on_device(): gain_grad = lax.psum(gain_term, 'user')]
    gather x2 -> x0, local copies, waits for them, and re-layouts: 15.7 us -> none  [the longest x1 7.87 us: on_device(): picked = jnp.take(queries.reshape(item_blocks, TILE, D), col_block, axis=0)]
    all_to_all x0 -> x2, waiting for transfers between devices: none -> 12.6 us  [the longest x1 6.63 us: on_device(): own_sums = lax.all_to_all(by_item, 'user', 0, 0).reshape(width, own_items)]
  transfers between devices with their start and end apart: 5 -> 12, of which waited for: 5 -> 10; matrix products, arithmetic and copies ran while one was open for 0% -> 7% of each run, Pallas kernels for 0% -> 1%
where the time goes in v1:
time: 220 us
  waiting for transfers between devices  76.3 us (35%)
  blocking collectives  48.8 us (22%)
  matrix products  26.8 us (12%)
  local copies, waits for them, and re-layouts  16.9 us (8%)
  other arithmetic  16.8 us (8%)
  starting transfers between devices  16.4 us (7%)
  between operations  15.2 us (7%)
  Pallas kernels  2.35 us (1%)
    ppermute x4, waiting for transfers between devices, over_items(): arrived = lax.ppermute(partial, 'item', pairs).astype(jnp.float32)  37.9 us
    all_gather x1, blocking collectives, on_device(): gain_grad = jnp.sum(lax.all_gather(gain_own, 'user', axis=0), axis=0)  25.9 us
    all_gather x1, blocking collectives, on_device(): all_cats = lax.all_gather(own_cats, 'user', axis=0, tiled=True)  22.9 us
    all_gather x1, waiting for transfers between devices, on_device(): feats = lax.all_gather(item_feat[0], 'user', axis=0, tiled=True)  14.1 us
    unnamed x49, local copies, waits for them, and re-layouts  10.2 us
    dot_general x4, matrix products, on_device(): partial = jnp.dot(dense[part], queries, preferred_element_type=jnp.float32)  8.95 us
    dot_general x4, matrix products, on_device(): jnp.dot(feats, expert_w[expert], preferred_element_type=jnp.float32)  8.81 us
    ppermute x3, waiting for transfers between devices, scatter_sum(): lax.ppermute(away.astype(jnp.bfloat16), 'user', pairs).astype(jnp.float32)  8.1 us
  transfers between devices with their start and end apart: 12, of which 10 were waited for; matrix products, arithmetic and copies ran while one was open for 7% of the time, Pallas kernels for 1%

profile of v1, /device:TPU:0, one launch (start us, length us, event | category | flops | bytes accessed | tf_op | source)
XLA Modules:
  0.0 219.6 jit_solution(14793082558537522296)
XLA Ops:
  8.6 2.5 %copy-done.1 = s32[1,1,80,128,128]{4,3,2,1,0:T(8,128)S(1)} copy-done((s32[1,1,80,128,128]{4,3,2,1,0:T(8,128)S(1)}, s32[1,1,80,128,128]{4,3,2,1,0:T(8,128)}, u32[]{:S(2)}) %copy-start.1) | copy-done | bytes 5242904
  11.7 2.3 %place_tiles.1 = bf16[2048,2048]{1,0:T(8,128)(2,1)S(1)} custom-call(s32[80]{0:T(128)S(1)} %bitcast.99, s32[1]{0:T(128)} %bitcast.93.count_ref, s32[80,128,128]{2,1,0:T(8,128)S(1)} %bitcast.98), custom_call_target="tpu_custom_call" | custom-call | flops 1310720 | bytes 13631488 | tf_op jit(solution)/shard_map/place_tiles/pallas_call | solution.py:37
  14.1 3.2 %copy-done = bf16[2048,2048]{1,0:T(8,128)(2,1)} copy-done((bf16[2048,2048]{1,0:T(8,128)(2,1)}, bf16[2048,2048]{1,0:T(8,128)(2,1)S(1)}, u32[]{:S(2)}) %copy-start) | copy-done | bytes 8388632
  17.3 22.9 %all-gather = s32[1,2048]{1,0:T(1,128)S(1)} all-gather(s32[1,128]{1,0:T(1,128)S(1)} %copy-done.19), channel_id=2, replica_groups=mesh['user'=16,'item'=2] {'user'}, dimensions={1}, use_global_device_ids=true | all-gather | bytes 8704 | tf_op jit(solution)/shard_map/all_gather | solution.py:108
  40.2 14.1 %all-gather.6.cloned.1.call-done = bf16[1,2048,512]{2,1,0:T(8,128)(2,1)} async-done(((bf16[1,128,512]{2,1,0:T(8,128)(2,1)}), bf16[1,2048,512]{2,1,0:T(8,128)(2,1)}) %all-gather.6.cloned.1.call-update) | async-done | bytes 2097168 | tf_op jit(solution)/shard_map/all_gather | solution.py:107
  54.3 3.1 %fusion.11 = f32[2048,512]{1,0:T(8,128)S(1)} fusion(bf16[1,2048,512]{2,1,0:T(8,128)(2,1)} %all-gather.6.cloned.1.call-done, bf16[4,512,512]{2,1,0:T(8,128)(2,1)} %param.14), kind=kOutput, calls=%fused_computation.15 | convolution fusion | flops 1073741824 | bytes 6815744 | tf_op jit(solution)/shard_map/dot_general | solution.py:115
  57.4 1.2 fusion.13
  58.6 1.3 fusion.15
  59.9 3.2 %add_convert_fusion = bf16[2048,512]{1,0:T(8,128)(2,1)S(1)} fusion(f32[2048,512]{1,0:T(8,128)S(1)} %fusion.11, f32[2048,512]{1,0:T(8,128)S(1)} %fusion.13, f32[2048,512]{1,0:T(8,128)S(1)} %fusion.15, bf16[1,2048,512]{2,1,0:T(8,128)(2,1)S(1)} %copy-done.3, pred[2048]{0:T(1024)(128)(4,1)S(1)} %get-tuple-element.28, pred[2048]{0:T(1024)(128)(4,1)S(1)} %get-tuple-element.29, ...), kind=kOutput, calls=%fused_computation | convolution fusion | flops 1082130432 | bytes 17309696 | tf_op jit(solution)/shard_map/dot_general | solution.py:115
  63.2 2.0 fusion.17
  65.2 2.0 fusion.23
  67.3 1.2 fusion.26
  68.5 1.5 collective-permute-start
  70.6 1.5 collective-permute-start.3
  72.1 3.6 %fusion.20 = bf16[512,512]{1,0:T(8,128)(2,1)S(1)} fusion(bf16[2048,512]{1,0:T(8,128)(2,1)} %copy-done.11, bf16[2048,2048]{1,0:T(8,128)(2,1)} %copy-done), kind=kOutput, calls=%fused_computation.30 | convolution fusion | flops 1074003968 | bytes 4718592 | tf_op jit(solution)/shard_map/dot_general | solution.py:124
  76.4 7.3 %collective-permute-done = bf16[512,512]{1,0:T(8,128)(2,1)} collective-permute-done((bf16[512,512]{1,0:T(8,128)(2,1)}, bf16[512,512]{1,0:T(8,128)(2,1)}, u32[]{:S(2)}, u32[]{:S(2)}) %collective-permute-start) | collective-permute-done | bytes 524320 | tf_op jit(solution)/shard_map/ppermute | solution.py:64
  83.7 11.2 %collective-permute-done.2 = bf16[512,512]{1,0:T(8,128)(2,1)} collective-permute-done((bf16[512,512]{1,0:T(8,128)(2,1)}, bf16[512,512]{1,0:T(8,128)(2,1)}, u32[]{:S(2)}, u32[]{:S(2)}) %collective-permute-start.2) | collective-permute-done | bytes 524320 | tf_op jit(solution)/shard_map/ppermute | solution.py:64
  94.9 11.1 %collective-permute-done.3 = bf16[512,512]{1,0:T(8,128)(2,1)S(1)} collective-permute-done((bf16[512,512]{1,0:T(8,128)(2,1)S(1)}, bf16[512,512]{1,0:T(8,128)(2,1)S(1)}, u32[]{:S(2)}, u32[]{:S(2)}) %collective-permute-start.3) | collective-permute-done | bytes 524320 | tf_op jit(solution)/shard_map/ppermute | solution.py:64
  106.0 2.3 %multiply_reduce_fusion.3 = (f32[512]{0:T(512)S(1)}, f32[512]{0:T(512)S(1)}, f32[512]{0:T(512)S(1)}) fusion(bf16[512,512]{1,0:T(8,128)(2,1)} %collective-permute-done, bf16[512,512]{1,0:T(8,128)(2,1)} %fusion.17, bf16[2048,512]{1,0:T(8,128)(2,1)S(1)} %copy-done.4, bf16[512,512]{1,0:T(8,128)(2,1)S(1)} %collective-permute-done.3, ...), kind=kLoop, calls=%fused_computation.80 | loop fusion | flops 5503488 | bytes 4724736 | tf_op jit(solution)/shard_map/reduce_sum | solution.py:130
  108.4 8.2 %collective-permute-done.1 = bf16[512,512]{1,0:T(8,128)(2,1)S(1)} collective-permute-done((bf16[512,512]{1,0:T(8,128)(2,1)S(1)}, bf16[512,512]{1,0:T(8,128)(2,1)S(1)}, u32[]{:S(2)}, u32[]{:S(2)}) %collective-permute-start.1) | collective-permute-done | bytes 524320 | tf_op jit(solution)/shard_map/ppermute | solution.py:64
  116.6 3.0 %fusion.62 = (f32[512]{0:T(512)S(1)}, f32[512]{0:T(512)S(1)}, f32[512]{0:T(512)S(1)}, f32[512]{0:T(512)S(1)}, f32[512]{0:T(512)S(1)}) fusion(f32[512]{0:T(512)S(1)} %get-tuple-element.43, bf16[2048,512]{1,0:T(8,128)(2,1)S(1)} %copy-done.7, bf16[512,512]{1,0:T(8,128)(2,1)} %collective-permute-done.2, bf16[512,512]{1,0:T(8,128)(2,1)} %fusion.23, ...), kind=kLoop, calls=%fused_computation.68 | loop fusion | flops 8123904 | bytes 5783552 | tf_op jit(solution)/shard_map/reduce_sum | solution.py:135
  119.6 1.1 fusion.64
  120.8 2.2 fusion.52
  123.0 2.6 %fusion.55 = (bf16[512,512]{1,0:T(8,128)(2,1)S(1)}, bf16[512,512]{1,0:T(8,128)(2,1)S(1)}) fusion(f32[512]{0:T(512)S(1)} %broadcast_multiply_fusion.3, f32[512]{0:T(512)S(1)} %get-tuple-element.31, f32[512]{0:T(512)S(1)} %copy-done.18, f32[512]{0:T(512)S(1)} %get-tuple-element.32, bf16[2048,512]{1,0:T(8,128)(2,1)S(1)} %copy-done.7, ...), kind=kLoop, calls=%fused_computation.61 | loop fusion | flops 6291456 | bytes 5257216 | tf_op jit(solution)/shard_map/convert_element_type | solution.py:133
  125.6 4.6 %fusion.89 = f32[512,2048]{1,0:T(8,128)S(1)} fusion(bf16[2048,2048]{1,0:T(8,128)(2,1)S(1)} %bitcast.97, bf16[512,512]{1,0:T(8,128)(2,1)S(1)} %get-tuple-element.21, bf16[512,512]{1,0:T(8,128)(2,1)S(1)} %get-tuple-element.23, bf16[512,512]{1,0:T(8,128)(2,1)S(1)} %get-tuple-element.22, bf16[512,512]{1,0:T(8,128)(2,1)S(1)} %get-tuple-element.20), kind=kOutput, calls=%fused_computation.136 | convolution fusion | flops 4303355904 | bytes 14680064 | tf_op jit(solution)/shard_map/dot_general | solution.py:142
  130.3 2.0 copy-done.10
  132.2 1.1 fusion.65
  133.4 2.9 %collective-permute-done.4 = bf16[4,2,32,2048]{3,2,0,1:T(8,128)(2,1)} collective-permute-done((bf16[4,2,32,2048]{3,2,0,1:T(8,128)(2,1)}, bf16[4,2,32,2048]{3,2,0,1:T(8,128)(2,1)}, u32[]{:S(2)}, u32[]{:S(2)}) %collective-permute-start.4) | collective-permute-done | bytes 1048608 | tf_op jit(solution)/shard_map/ppermute | solution.py:78
  136.3 2.2 bitcast_add_fusion
  138.5 1.3 copy-done.8
  139.8 0.9 fusion.66
  141.3 25.9 %all-gather.3 = f32[16,1,256]{2,1,0:T(1,128)S(1)} all-gather(f32[1,1,256]{2,1,0:T(1,128)S(1)} %bitcast.112), channel_id=4, replica_groups=mesh['user'=16,'item'=2] {'user'}, dimensions={0}, use_global_device_ids=true | all-gather | bytes 17408 | tf_op jit(solution)/shard_map/all_gather | solution.py:140
  167.9 1.5 pad_maximum_fusion
  169.8 1.1 bitcast_add_fusion.1
  171.1 3.7 %collective-permute-start.8 = (bf16[32,2048]{1,0:T(8,128)(2,1)S(1)}, bf16[32,2048]{1,0:T(8,128)(2,1)S(1)}, u32[]{:S(2)}, u32[]{:S(2)}) collective-permute-start(bf16[32,2048]{1,0:T(8,128)(2,1)S(1)} %get-tuple-element.25), channel_id=1, source_target_pairs={{0,24},{2,26},{4,28},{6,30},{8,0},{10,2},{12,4},{14,6},{16,8},{18,... | collective-permute-start | bytes 393224 | tf_op jit(solution)/shard_map/ppermute | solution.py:91
  174.9 1.0 constant_dynamic-slice_fusion.2
  175.9 3.4 %collective-permute-done.6 = bf16[32,2048]{1,0:T(8,128)(2,1)S(1)} collective-permute-done((bf16[32,2048]{1,0:T(8,128)(2,1)S(1)}, bf16[32,2048]{1,0:T(8,128)(2,1)S(1)}, u32[]{:S(2)}, u32[]{:S(2)}) %collective-permute-start.6) | collective-permute-done | bytes 131104 | tf_op jit(solution)/shard_map/ppermute | solution.py:91
  179.3 4.7 %collective-permute-done.7 = bf16[32,2048]{1,0:T(8,128)(2,1)S(1)} collective-permute-done((bf16[32,2048]{1,0:T(8,128)(2,1)S(1)}, bf16[32,2048]{1,0:T(8,128)(2,1)S(1)}, u32[]{:S(2)}, u32[]{:S(2)}) %collective-permute-start.7) | collective-permute-done | bytes 131104 | tf_op jit(solution)/shard_map/ppermute | solution.py:91
  184.2 0.7 copy.23
  184.9 4.2 %all-to-all-start = ((bf16[16,32,128]{2,1,0:T(8,128)(2,1)}), bf16[16,32,128]{2,1,0:T(8,128)(2,1)S(1)}, u32[]{:S(2)}, u32[]{:S(2)}) async-start(bf16[16,32,128]{2,1,0:T(8,128)(2,1)} %copy.23), calls=%async_computation | async-start | bytes 262144 | tf_op jit(solution)/shard_map/all_to_all | solution.py:167
  189.5 0.8 copy.24
  190.4 6.6 %all-to-all-done = bf16[16,32,128]{2,1,0:T(8,128)(2,1)S(1)} async-done(((bf16[16,32,128]{2,1,0:T(8,128)(2,1)}), bf16[16,32,128]{2,1,0:T(8,128)(2,1)S(1)}, u32[]{:S(2)}, u32[]{:S(2)}) %all-to-all-start) | async-done | bytes 131104 | tf_op jit(solution)/shard_map/all_to_all | solution.py:167
  197.0 3.5 %all-to-all-start.1 = ((f32[16,32,128]{2,1,0:T(8,128)}), f32[16,32,128]{2,1,0:T(8,128)S(1)}, u32[]{:S(2)}, u32[]{:S(2)}) async-start(f32[16,32,128]{2,1,0:T(8,128)} %bitcast.27), calls=%async_computation.1 | async-start | bytes 524288 | tf_op jit(solution)/shard_map/all_to_all | solution.py:157
  200.5 1.3 convolution_select_fusion.2
  201.9 1.4 fusion.40
  203.6 1.0 fusion.44
  204.6 6.0 %all-to-all-done.1 = f32[16,32,128]{2,1,0:T(8,128)S(1)} async-done(((f32[16,32,128]{2,1,0:T(8,128)}), f32[16,32,128]{2,1,0:T(8,128)S(1)}, u32[]{:S(2)}, u32[]{:S(2)}) %all-to-all-start.1) | async-done | bytes 262176 | tf_op jit(solution)/shard_map/all_to_all | solution.py:157
  211.6 1.1 reshape.164
  (78 shorter events, 6.6 us)
Async XLA Ops:
  7.2 47.1 %all-gather.6.cloned.1.call-start = ((), (), s32[]{:S(2)}) async-start(), calls=%async_computation.2 | async-start | bytes 2228224 | tf_op jit(solution)/shard_map/all_gather | solution.py:107
  8.6 2.5 %copy-start.1 = (s32[1,1,80,128,128]{4,3,2,1,0:T(8,128)S(1)}, s32[1,1,80,128,128]{4,3,2,1,0:T(8,128)}, u32[]{:S(2)}) copy-start(s32[1,1,80,128,128]{4,3,2,1,0:T(8,128)} %param.16) | copy-start | bytes 15728644
  11.0 0.7 copy-start.2
  11.7 5.6 %copy-start.19 = (s32[1,128]{1,0:T(1,128)S(1)}, s32[1,128]{1,0:T(1,128)}, u32[]{:S(2)}) copy-start(s32[1,128]{1,0:T(1,128)} %param.13) | copy-start | bytes 1540
  14.1 3.2 %copy-start = (bf16[2048,2048]{1,0:T(8,128)(2,1)}, bf16[2048,2048]{1,0:T(8,128)(2,1)S(1)}, u32[]{:S(2)}) copy-start(bf16[2048,2048]{1,0:T(8,128)(2,1)S(1)} %place_tiles.1) | copy-start | bytes 25165828
  54.3 3.1 %copy-start.3 = (bf16[1,2048,512]{2,1,0:T(8,128)(2,1)S(1)}, bf16[1,2048,512]{2,1,0:T(8,128)(2,1)}, u32[]{:S(2)}) copy-start(bf16[1,2048,512]{2,1,0:T(8,128)(2,1)} %all-gather.6.cloned.1.call-done) | copy-start | bytes 6291460
  54.3 3.1 %copy-start.5 = (bf16[4,512,512]{2,1,0:T(8,128)(2,1)S(1)}, bf16[4,512,512]{2,1,0:T(8,128)(2,1)}, u32[]{:S(2)}) copy-start(bf16[4,512,512]{2,1,0:T(8,128)(2,1)} %param.14) | copy-start | bytes 6291460
  58.6 4.5 %slice-start = ((s8[8388608]{0:T(1024)(128)(4,1)}), s8[4194304]{0:T(1024)(128)(4,1)S(1)}, s32[]{:S(2)}) async-start(s8[8388608]{0:T(1024)(128)(4,1)} %bitcast.94), calls=%async_computation.3 | async-start | bytes 8388608
  59.9 3.3 %slice-start.1 = ((s8[8388608]{0:T(1024)(128)(4,1)}), s8[4194304]{0:T(1024)(128)(4,1)S(1)}, s32[]{:S(2)}) async-start(s8[8388608]{0:T(1024)(128)(4,1)} %bitcast.94), calls=%async_computation.4 | async-start | bytes 8388608
  63.2 4.1 %copy-start.11 = (bf16[2048,512]{1,0:T(8,128)(2,1)}, bf16[2048,512]{1,0:T(8,128)(2,1)S(1)}, u32[]{:S(2)}) copy-start(bf16[2048,512]{1,0:T(8,128)(2,1)S(1)} %add_convert_fusion) | copy-start | bytes 6291460
  68.5 15.1 %collective-permute-start = (bf16[512,512]{1,0:T(8,128)(2,1)}, bf16[512,512]{1,0:T(8,128)(2,1)}, u32[]{:S(2)}, u32[]{:S(2)}) collective-permute-start(bf16[512,512]{1,0:T(8,128)(2,1)} %fusion.17), channel_id=1, source_target_pairs={{0,1},{1,0},{2,3},{3,2},{4,5},{5,4},{6,7},{7,6},{8,9},{9,8},{10,11... | collective-permute-start | bytes 1572872 | tf_op jit(solution)/shard_map/ppermute | solution.py:64
  70.1 24.8 %collective-permute-start.2 = (bf16[512,512]{1,0:T(8,128)(2,1)}, bf16[512,512]{1,0:T(8,128)(2,1)}, u32[]{:S(2)}, u32[]{:S(2)}) collective-permute-start(bf16[512,512]{1,0:T(8,128)(2,1)} %fusion.23), channel_id=1, source_target_pairs={{0,1},{1,0},{2,3},{3,2},{4,5},{5,4},{6,7},{7,6},{8,9},{9,8},{10,11... | collective-permute-start | bytes 1572872 | tf_op jit(solution)/shard_map/ppermute | solution.py:64
  70.6 35.4 %collective-permute-start.3 = (bf16[512,512]{1,0:T(8,128)(2,1)S(1)}, bf16[512,512]{1,0:T(8,128)(2,1)S(1)}, u32[]{:S(2)}, u32[]{:S(2)}) collective-permute-start(bf16[512,512]{1,0:T(8,128)(2,1)S(1)} %fusion.26), channel_id=1, source_target_pairs={{0,1},{1,0},{2,3},{3,2},{4,5},{5,4},{6,7},{7,6},{8,9},{9,8},{10,11... | collective-permute-start | bytes 1572872 | tf_op jit(solution)/shard_map/ppermute | solution.py:64
  72.1 33.9 %copy-start.4 = (bf16[2048,512]{1,0:T(8,128)(2,1)S(1)}, bf16[2048,512]{1,0:T(8,128)(2,1)}, u32[]{:S(2)}) copy-start(bf16[2048,512]{1,0:T(8,128)(2,1)} %param.9) | copy-start | bytes 6291460
  75.7 40.9 %copy-start.7 = (bf16[2048,512]{1,0:T(8,128)(2,1)S(1)}, bf16[2048,512]{1,0:T(8,128)(2,1)}, u32[]{:S(2)}) copy-start(bf16[2048,512]{1,0:T(8,128)(2,1)} %param.10) | copy-start | bytes 6291460
  75.7 40.9 %copy-start.18 = (f32[512]{0:T(512)S(1)}, f32[512]{0:T(512)}, u32[]{:S(2)}) copy-start(f32[512]{0:T(512)} %param.11) | copy-start | bytes 6148
  75.7 40.9 %collective-permute-start.1 = (bf16[512,512]{1,0:T(8,128)(2,1)S(1)}, bf16[512,512]{1,0:T(8,128)(2,1)S(1)}, u32[]{:S(2)}, u32[]{:S(2)}) collective-permute-start(bf16[512,512]{1,0:T(8,128)(2,1)S(1)} %fusion.20), channel_id=1, source_target_pairs={{0,1},{1,0},{2,3},{3,2},{4,5},{5,4},{6,7},{7,6},{8,9},{9,8},{10,11... | collective-permute-start | bytes 1572872 | tf_op jit(solution)/shard_map/ppermute | solution.py:64
  116.6 9.0 %slice-start.2 = ((s8[8388608]{0:T(1024)(128)(4,1)}), s8[4194304]{0:T(1024)(128)(4,1)S(1)}, s32[]{:S(2)}) async-start(s8[8388608]{0:T(1024)(128)(4,1)} %bitcast.96), calls=%async_computation.5 | async-start | bytes 8388608
  120.8 4.8 %slice-start.3 = ((s8[8388608]{0:T(1024)(128)(4,1)}), s8[4194304]{0:T(1024)(128)(4,1)S(1)}, s32[]{:S(2)}) async-start(s8[8388608]{0:T(1024)(128)(4,1)} %bitcast.96), calls=%async_computation.6 | async-start | bytes 8388608
  122.9 2.6 %copy-start.12 = (bf16[512,512]{1,0:T(8,128)(2,1)}, bf16[512,512]{1,0:T(8,128)(2,1)S(1)}, u32[]{:S(2)}) copy-start(bf16[512,512]{1,0:T(8,128)(2,1)S(1)} %get-tuple-element.22) | copy-start | bytes 1572868
  123.0 2.6 %copy-start.14 = (bf16[512,512]{1,0:T(8,128)(2,1)}, bf16[512,512]{1,0:T(8,128)(2,1)S(1)}, u32[]{:S(2)}) copy-start(bf16[512,512]{1,0:T(8,128)(2,1)S(1)} %get-tuple-element.23) | copy-start | bytes 1572868
  125.5 4.7 %copy-start.16 = (bf16[512,512]{1,0:T(8,128)(2,1)}, bf16[512,512]{1,0:T(8,128)(2,1)S(1)}, u32[]{:S(2)}) copy-start(bf16[512,512]{1,0:T(8,128)(2,1)S(1)} %get-tuple-element.20) | copy-start | bytes 1572868
  125.6 4.7 %copy-start.17 = (bf16[512,512]{1,0:T(8,128)(2,1)}, bf16[512,512]{1,0:T(8,128)(2,1)S(1)}, u32[]{:S(2)}) copy-start(bf16[512,512]{1,0:T(8,128)(2,1)S(1)} %get-tuple-element.21) | copy-start | bytes 1572868
  130.2 2.0 copy-start.10
  133.3 3.0 %collective-permute-start.4 = (bf16[4,2,32,2048]{3,2,0,1:T(8,128)(2,1)}, bf16[4,2,32,2048]{3,2,0,1:T(8,128)(2,1)}, u32[]{:S(2)}, u32[]{:S(2)}) collective-permute-start(bf16[4,2,32,2048]{3,2,0,1:T(8,128)(2,1)} %fusion.65), channel_id=1, source_target_pairs={{0,2},{2,0},{4,6},{6,4},{8,10},{10,8},{12,14},{14,12},{16,18},{18,... | collective-permute-start | bytes 3145736 | tf_op jit(solution)/shard_map/ppermute | solution.py:78
  133.4 34.5 %copy-start.13 = (bf16[512,512]{1,0:T(8,128)(2,1)S(1)}, bf16[512,512]{1,0:T(8,128)(2,1)}, u32[]{:S(2)}) copy-start(bf16[512,512]{1,0:T(8,128)(2,1)} %copy-done.12) | copy-start | bytes 1572868
  133.4 34.5 %copy-start.15 = (bf16[512,512]{1,0:T(8,128)(2,1)S(1)}, bf16[512,512]{1,0:T(8,128)(2,1)}, u32[]{:S(2)}) copy-start(bf16[512,512]{1,0:T(8,128)(2,1)} %copy-done.14) | copy-start | bytes 1572868
  138.5 1.3 copy-start.8
  140.7 28.7 %collective-permute-start.5 = (bf16[4,32,2048]{2,1,0:T(8,128)(2,1)}, bf16[4,32,2048]{2,1,0:T(8,128)(2,1)}, u32[]{:S(2)}, u32[]{:S(2)}) collective-permute-start(bf16[4,32,2048]{2,1,0:T(8,128)(2,1)} %fusion.66), channel_id=1, source_target_pairs={{0,4},{2,6},{4,0},{6,2},{8,12},{10,14},{12,8},{14,10},{16,20},{18,... | collective-permute-start | bytes 1572872 | tf_op jit(solution)/shard_map/ppermute | solution.py:78
  167.9 1.9 copy-start.9
  171.0 8.3 %collective-permute-start.6 = (bf16[32,2048]{1,0:T(8,128)(2,1)S(1)}, bf16[32,2048]{1,0:T(8,128)(2,1)S(1)}, u32[]{:S(2)}, u32[]{:S(2)}) collective-permute-start(bf16[32,2048]{1,0:T(8,128)(2,1)S(1)} %get-tuple-element.24), channel_id=1, source_target_pairs={{0,8},{2,10},{4,12},{6,14},{8,16},{10,18},{12,20},{14,22},{16,24},... | collective-permute-start | bytes 393224 | tf_op jit(solution)/shard_map/ppermute | solution.py:91
  171.1 12.9 %collective-permute-start.7 = (bf16[32,2048]{1,0:T(8,128)(2,1)S(1)}, bf16[32,2048]{1,0:T(8,128)(2,1)S(1)}, u32[]{:S(2)}, u32[]{:S(2)}) collective-permute-start(bf16[32,2048]{1,0:T(8,128)(2,1)S(1)} %get-tuple-element.26), channel_id=1, source_target_pairs={{0,16},{2,18},{4,20},{6,22},{8,24},{10,26},{12,28},{14,30},{16,0},... | collective-permute-start | bytes 393224 | tf_op jit(solution)/shard_map/ppermute | solution.py:91
  171.1 12.9 %collective-permute-start.8 = (bf16[32,2048]{1,0:T(8,128)(2,1)S(1)}, bf16[32,2048]{1,0:T(8,128)(2,1)S(1)}, u32[]{:S(2)}, u32[]{:S(2)}) collective-permute-start(bf16[32,2048]{1,0:T(8,128)(2,1)S(1)} %get-tuple-element.25), channel_id=1, source_target_pairs={{0,24},{2,26},{4,28},{6,30},{8,0},{10,2},{12,4},{14,6},{16,8},{18,... | collective-permute-start | bytes 393224 | tf_op jit(solution)/shard_map/ppermute | solution.py:91
  184.9 12.1 %all-to-all-start = ((bf16[16,32,128]{2,1,0:T(8,128)(2,1)}), bf16[16,32,128]{2,1,0:T(8,128)(2,1)S(1)}, u32[]{:S(2)}, u32[]{:S(2)}) async-start(bf16[16,32,128]{2,1,0:T(8,128)(2,1)} %copy.23), calls=%async_computation | async-start | bytes 262144 | tf_op jit(solution)/shard_map/all_to_all | solution.py:167
  189.5 13.7 %copy-start.6 = (bf16[4,512,512]{2,1,0:T(8,128)(2,1)S(1)}, bf16[4,512,512]{2,1,0:T(8,128)(2,1)}, u32[]{:S(2)}) copy-start(bf16[4,512,512]{2,1,0:T(8,128)(2,1)} %param.14) | copy-start | bytes 6291460
  197.0 13.5 %all-to-all-start.1 = ((f32[16,32,128]{2,1,0:T(8,128)}), f32[16,32,128]{2,1,0:T(8,128)S(1)}, u32[]{:S(2)}, u32[]{:S(2)}) async-start(f32[16,32,128]{2,1,0:T(8,128)} %bitcast.27), calls=%async_computation.1 | async-start | bytes 524288 | tf_op jit(solution)/shard_map/all_to_all | solution.py:157
Sparse Core Ops, SparseCore 0:
  10.2 44.0 all-gather.5

commit v2 on v1

v2 whole, which is shorter than its diff:
```python
import functools

import jax
import jax.numpy as jnp
from jax import lax
from jax.experimental import pallas as pl
from jax.experimental.pallas import tpu as pltpu
from jax.sharding import PartitionSpec as P

TILE = 128
SLOTS_PER_STEP = 8
HALVES = 2
ROW_CHUNKS = 4
BLOCK_ROWS = 256
MIB = 1024 * 1024


def place_tiles(item_blocks, place_ref, count_ref, level_ref, dense_ref):
    step = pl.program_id(0)

    @pl.when(step == 0)
    def _():
        dense_ref[...] = jnp.zeros_like(dense_ref)

    for offset in range(level_ref.shape[0]):
        slot = step * level_ref.shape[0] + offset

        @pl.when(slot < count_ref[0])
        def _():
            place = place_ref[slot]
            row = pl.multiple_of((place // item_blocks) * TILE, TILE)
            col = pl.multiple_of((place % item_blocks) * TILE, TILE)
            weights = level_ref[offset].astype(jnp.float32) * (1.0 / (2.0 * TILE))
            dense_ref[pl.ds(row, TILE), pl.ds(col, TILE)] = weights.astype(jnp.bfloat16)


def dense_tiles(place, count, level, users, items):
    slots = level.shape[0]
    per_step = SLOTS_PER_STEP if slots % SLOTS_PER_STEP == 0 else 1
    return pl.pallas_call(
        functools.partial(place_tiles, items // TILE),
        out_shape=jax.ShapeDtypeStruct((users, items), jnp.bfloat16),
        grid_spec=pltpu.PrefetchScalarGridSpec(
            num_scalar_prefetch=2,
            grid=(slots // per_step,),
            in_specs=[
                pl.BlockSpec((per_step, TILE, TILE), lambda step, place_ref, count_ref: (step, 0, 0))
            ],
            out_specs=pl.BlockSpec((users, items), lambda step, place_ref, count_ref: (0, 0)),
        ),
        compiler_params=pltpu.CompilerParams(
            dimension_semantics=("arbitrary",), vmem_limit_bytes=40 * MIB
        ),
        cost_estimate=pl.CostEstimate(
            flops=slots * TILE * TILE,
            bytes_accessed=slots * TILE * TILE * 4 + users * items * 2,
            transcendentals=0,
        ),
        name="place_tiles",
    )(place, count, level)


def project_own(first_ref, cats_ref, feat_ref, weight_ref, *rest):
    out_refs, total_ref = rest[:-1], rest[-1]
    expert = pl.program_id(0)
    own = feat_ref.shape[0]
    on_diagonal = lax.broadcasted_iota(jnp.int32, (own, own), 0) == lax.broadcasted_iota(
        jnp.int32, (own, own), 1
    )
    cats = jnp.sum(
        jnp.where(on_diagonal, cats_ref[...].astype(jnp.float32), 0.0), axis=1, keepdims=True
    )
    chosen = cats == (first_ref[0] + expert).astype(jnp.float32)
    part = jnp.dot(feat_ref[...], weight_ref[0], preferred_element_type=jnp.float32)
    part = jnp.where(chosen, part, 0.0)

    @pl.when(expert == 0)
    def _():
        total_ref[...] = part

    @pl.when(expert > 0)
    def _():
        total_ref[...] += part

    @pl.when(expert == pl.num_programs(0) - 1)
    def _():
        cols = out_refs[0].shape[1]
        for half, out_ref in enumerate(out_refs):
            out_ref[...] = total_ref[:, half * cols : (half + 1) * cols].astype(out_ref.dtype)


def own_queries(first_expert, cats, feat, weights):
    own, width = feat.shape
    experts = weights.shape[0]
    half = jax.ShapeDtypeStruct((own, width // HALVES), jnp.bfloat16)
    half_spec = pl.BlockSpec((own, width // HALVES), lambda expert, first_ref: (0, 0))
    return pl.pallas_call(
        project_own,
        out_shape=[half] * HALVES,
        grid_spec=pltpu.PrefetchScalarGridSpec(
            num_scalar_prefetch=1,
            grid=(experts,),
            in_specs=[
                pl.BlockSpec((1, own), lambda expert, first_ref: (0, 0)),
                pl.BlockSpec((own, width), lambda expert, first_ref: (0, 0)),
                pl.BlockSpec((1, width, width), lambda expert, first_ref: (expert, 0, 0)),
            ],
            out_specs=[half_spec] * HALVES,
            scratch_shapes=[pltpu.VMEM((own, width), jnp.float32)],
        ),
        compiler_params=pltpu.CompilerParams(dimension_semantics=("arbitrary",)),
        cost_estimate=pl.CostEstimate(
            flops=2 * own * width * width * experts,
            bytes_accessed=weights.size * 2 + own * width * 4,
            transcendentals=0,
        ),
        name="own_queries",
    )(first_expert.reshape(1), cats.reshape(1, own), feat, weights)


def spread(blocks, order_ref, *rest):
    query_refs, dense_ref, out_ref = rest[:blocks], rest[blocks], rest[blocks + 1]
    all_ref, sems = rest[blocks + 2 :]
    own = query_refs[0].shape[0]

    @pl.when(pl.program_id(0) == 0)
    def _():
        copies = []
        for place, query_ref in enumerate(query_refs):
            start = pl.multiple_of(order_ref[place] * own, own)
            copy = pltpu.make_async_copy(query_ref, all_ref.at[pl.ds(start, own)], sems.at[place])
            copy.start()
            copies.append(copy)
        for copy in copies:
            copy.wait()

    out_ref[...] = jnp.dot(
        dense_ref[...], all_ref[...], preferred_element_type=jnp.float32
    ).astype(out_ref.dtype)


def spread_items(order, queries, dense, first, rows):
    items = dense.shape[1]
    own, cols = queries[0].shape
    blocks = len(queries)
    block_rows = min(BLOCK_ROWS, rows)
    first_block = first // block_rows
    return pl.pallas_call(
        functools.partial(spread, blocks),
        out_shape=jax.ShapeDtypeStruct((rows, cols), jnp.bfloat16),
        grid_spec=pltpu.PrefetchScalarGridSpec(
            num_scalar_prefetch=1,
            grid=(rows // block_rows,),
            in_specs=[pl.BlockSpec(memory_space=pl.ANY)] * blocks
            + [pl.BlockSpec((block_rows, items), lambda step, order_ref: (first_block + step, 0))],
            out_specs=pl.BlockSpec((block_rows, cols), lambda step, order_ref: (step, 0)),
            scratch_shapes=[
                pltpu.VMEM((items, cols), jnp.bfloat16),
                pltpu.SemaphoreType.DMA((blocks,)),
            ],
        ),
        compiler_params=pltpu.CompilerParams(
            dimension_semantics=("arbitrary",), vmem_limit_bytes=24 * MIB
        ),
        cost_estimate=pl.CostEstimate(
            flops=2 * rows * items * cols,
            bytes_accessed=rows * items * 2 + items * cols * 2 + rows * cols * 2,
            transcendentals=0,
        ),
        name="spread_items",
    )(order, *queries, dense)


def norm_backward(pieces, user_ref, grad_ref, gain_ref, *rest):
    piece_refs, out_ref, term_ref = rest[: pieces * HALVES], rest[-2], rest[-1]
    summed = []
    for half in range(HALVES):
        total = piece_refs[half * pieces][...].astype(jnp.float32)
        for piece in range(1, pieces):
            total = total + piece_refs[half * pieces + piece][...].astype(jnp.float32)
        summed.append(total)
    width = out_ref.shape[1]
    pre_norm = user_ref[...].astype(jnp.float32) + jnp.concatenate(summed, axis=1)
    grad = grad_ref[...].astype(jnp.float32)
    scaled_grad = gain_ref[...] * grad
    inv_rms = lax.rsqrt(jnp.sum(pre_norm * pre_norm, axis=1, keepdims=True) / width + 1e-05)
    cross_mean = jnp.sum(scaled_grad * pre_norm, axis=1, keepdims=True) / width
    out_ref[...] = (
        inv_rms * scaled_grad - pre_norm * (inv_rms * inv_rms * inv_rms * cross_mean)
    ).astype(out_ref.dtype)
    term = jnp.sum(grad * pre_norm * inv_rms, axis=0, keepdims=True)

    @pl.when(pl.program_id(0) == 0)
    def _():
        term_ref[...] = term

    @pl.when(pl.program_id(0) > 0)
    def _():
        term_ref[...] += term


def user_gradient(user_feat, cotangent, gain, pieces, first, rows):
    width = user_feat.shape[1]
    block_rows = min(BLOCK_ROWS, rows)
    first_block = first // block_rows
    flat = [piece for half in pieces for piece in half]
    whole = pl.BlockSpec((block_rows, width), lambda step: (first_block + step, 0))
    part = pl.BlockSpec((block_rows, width // HALVES), lambda step: (step, 0))
    return pl.pallas_call(
        functools.partial(norm_backward, len(pieces[0])),
        out_shape=[
            jax.ShapeDtypeStruct((rows, width), jnp.bfloat16),
            jax.ShapeDtypeStruct((1, width), jnp.float32),
        ],
        grid=(rows // block_rows,),
        in_specs=[whole, whole, pl.BlockSpec((1, width), lambda step: (0, 0))] + [part] * len(flat),
        out_specs=[
            pl.BlockSpec((block_rows, width), lambda step: (step, 0)),
            pl.BlockSpec((1, width), lambda step: (0, 0)),
        ],
        compiler_params=pltpu.CompilerParams(
            dimension_semantics=("arbitrary",), vmem_limit_bytes=24 * MIB
        ),
        cost_estimate=pl.CostEstimate(
            flops=16 * rows * width,
            bytes_accessed=rows * width * 2 * (3 + len(pieces[0])),
            transcendentals=rows,
        ),
        name="user_gradient",
    )(user_feat, cotangent, gain.reshape(1, width), *flat)


def flip(value, size, bits):
    return lax.ppermute(value, "user", [(source, source ^ bits) for source in range(size)])


def gather_parts(own, size):
    same_core = [own] + [flip(own, size, 2 * chip) for chip in range(1, size // 2)]
    parts = [None] * size
    for chip, part in enumerate(same_core):
        parts[2 * chip] = part
        parts[2 * chip + 1] = flip(part, size, 1)
    return parts


def scatter_sum(terms, size):
    cores, sides = 2, 2
    layers = size // (cores * sides)
    index = lax.axis_index("user")
    core, side, layer = index % cores, (index // cores) % sides, index // (cores * sides)
    rest = terms.shape[1:]
    terms = terms.reshape((layers, sides, cores) + rest)
    own = lax.dynamic_index_in_dim(terms, core, 2, keepdims=False)
    away = lax.dynamic_index_in_dim(terms, 1 - core, 2, keepdims=False).astype(jnp.bfloat16)
    terms = own + flip(away, size, 1).astype(jnp.float32)
    own = lax.dynamic_index_in_dim(terms, side, 1, keepdims=False)
    away = lax.dynamic_index_in_dim(terms, 1 - side, 1, keepdims=False).astype(jnp.bfloat16)
    terms = own + flip(away, size, 2).astype(jnp.float32)
    total = lax.dynamic_index_in_dim(terms, layer, 0, keepdims=False)
    for other in range(1, layers):
        away = lax.dynamic_index_in_dim(terms, layer ^ other, 0, keepdims=False)
        arrived = flip(away.astype(jnp.bfloat16), size, other * cores * sides)
        total = total + arrived.astype(jnp.float32)
    return total


def as_rows(value, size):
    count = value.shape[1]
    padded = -(-count // TILE) * TILE
    return jnp.pad(value, ((0, 0), (0, padded - count))).reshape(size, padded // TILE, TILE)


def on_device(
    user_feat, cotangent, gain, item_feat, categories, expert_w, tile_place, tile_level, tile_count
):
    users, width = user_feat.shape
    user_size, item_size = lax.axis_size("user"), lax.axis_size("item")
    user_index, item_index = lax.axis_index("user"), lax.axis_index("item")
    own_items = item_feat.shape[1]
    items = own_items * user_size
    experts_here = expert_w.shape[0]
    first_expert = item_index * experts_here
    own_cats, own_feat = categories[0], item_feat[0]
    rows, half_width = users // ROW_CHUNKS, width // HALVES

    own_halves = own_queries(first_expert, own_cats, own_feat, expert_w)
    order = user_index ^ jnp.arange(user_size, dtype=jnp.int32)
    queries = [gather_parts(own, user_size) for own in own_halves]
    dense = dense_tiles(tile_place[0, 0], tile_count[0], tile_level[0, 0], users, items)

    local_cats = (own_cats - first_expert).astype(jnp.bfloat16)
    packed = jnp.concatenate(
        [own_feat, jnp.broadcast_to(local_cats[:, None], (own_items, TILE))], axis=1
    )
    packed, _ = lax.optimization_barrier((packed, queries[-1][-1]))
    packed = lax.all_gather(packed, "user", axis=0, tiled=True)
    feats, all_cats = packed[:, :width], packed[:, width].astype(jnp.int32)

    partials = [[None] * ROW_CHUNKS for _ in range(HALVES)]
    for half in range(HALVES):
        for chunk in range(ROW_CHUNKS):
            partial = spread_items(order, queries[half], dense, chunk * rows, rows)
            pieces = [partial]
            for shift in range(1, item_size):
                pairs = [(source, (source + shift) % item_size) for source in range(item_size)]
                pieces.append(lax.ppermute(partial, "item", pairs))
            partials[half][chunk] = pieces

    grads, gain_term, item_terms = [], 0.0, 0.0
    for chunk in range(ROW_CHUNKS):
        grad, term = user_gradient(
            user_feat,
            cotangent,
            gain,
            [partials[half][chunk] for half in range(HALVES)],
            chunk * rows,
            rows,
        )
        grads.append(grad)
        gain_term = gain_term + term[0]
        if chunk < ROW_CHUNKS - 1:
            item_terms = item_terms + lax.dot_general(
                grad,
                dense[chunk * rows : (chunk + 1) * rows],
                (((0,), (0,)), ((), ())),
                preferred_element_type=jnp.float32,
            )
    own_width = width // user_size
    part_width = own_width // HALVES
    sums = []
    for half in range(HALVES):
        part = slice(half * half_width, (half + 1) * half_width)
        terms = item_terms[part] + lax.dot_general(
            grads[-1][:, part],
            dense[users - rows :],
            (((0,), (0,)), ((), ())),
            preferred_element_type=jnp.float32,
        )
        terms = terms.reshape(user_size, part_width, items)
        sums.append(scatter_sum(terms, user_size).astype(jnp.bfloat16))
    sums = jnp.concatenate(sums, axis=0)

    col_width = width // item_size
    user_grad = jnp.concatenate(
        [lax.dynamic_slice_in_dim(grad, item_index * col_width, col_width, 1) for grad in grads],
        axis=0,
    )
    gain_own = lax.dynamic_slice_in_dim(gain_term, item_index * col_width, col_width, 0)

    chosen = all_cats[None, :] == jnp.arange(experts_here, dtype=jnp.int32)[:, None]
    masked = jnp.where(chosen[:, None, :], sums[None], jnp.zeros_like(sums)[None])
    expert_cols = lax.dot_general(
        feats,
        masked.reshape(experts_here * own_width, items),
        (((0,), (1,)), ((), ())),
        preferred_element_type=jnp.float32,
    ).astype(jnp.bfloat16)
    by_item = sums.reshape(own_width, user_size, own_items).transpose(1, 0, 2)
    gain_sent = jnp.broadcast_to(gain_own.astype(jnp.bfloat16)[None], (user_size, col_width))
    pieces = [
        as_rows(by_item.reshape(user_size, -1), user_size),
        as_rows(expert_cols.reshape(user_size, -1), user_size),
        as_rows(gain_sent, user_size),
    ]
    swapped = lax.all_to_all(jnp.concatenate(pieces, axis=1), "user", 0, 0)
    ends = [pieces[0].shape[1], pieces[0].shape[1] + pieces[1].shape[1]]

    own_sums = (
        swapped[:, : ends[0]]
        .reshape(user_size, HALVES, part_width, own_items)
        .transpose(1, 0, 2, 3)
        .reshape(width, own_items)
    )
    expert_grad = (
        swapped[:, ends[0] : ends[1]]
        .reshape(user_size, own_width, experts_here, HALVES, part_width)
        .transpose(2, 1, 3, 0, 4)
        .reshape(experts_here, own_width, width)
        .astype(jnp.float32)
    )
    gain_grad = jnp.sum(
        swapped[:, ends[1] :].reshape(user_size, -1)[:, :col_width].astype(jnp.float32), axis=0
    )
    item_total = jnp.zeros((own_items, width), jnp.float32)
    for expert in range(experts_here):
        item_total = item_total + jnp.where(
            (own_cats == first_expert + expert)[:, None],
            lax.dot_general(
                own_sums,
                expert_w[expert],
                (((0,), (1,)), ((), ())),
                preferred_element_type=jnp.float32,
            ),
            0.0,
        )
    return (user_grad, item_total.astype(jnp.bfloat16)[None], expert_grad, gain_grad)


def solution(mesh):
    placed = (
        P("user", None),
        P("user", None),
        P(),
        P("item", "user", None),
        P("item", "user"),
        P("item", None, None),
        P("user", "item", None),
        P("user", "item", None, None, None),
        P("user", "item"),
    )
    return jax.shard_map(
        on_device,
        mesh=mesh,
        in_specs=placed,
        out_specs=(P("user", "item"), P("item", "user", None), P("item", "user", None), P("item")),
        check_vma=False,
    )
```

time: 220 us -> 165 us (0.75)
  blocking collectives: 48.8 us -> 0 us
  waiting for transfers between devices: 76.3 us -> 35.1 us
  starting transfers between devices: 16.4 us -> 53.2 us
  Pallas kernels: 2.35 us -> 37 us
  matrix products: 26.8 us -> 9.81 us
  other arithmetic: 16.8 us -> 4.42 us
  local copies, waits for them, and re-layouts: 16.9 us -> 10.2 us
    all_gather x2 -> x0, blocking collectives: 48.8 us -> none  [the longest x1 25.9 us: on_device(): gain_grad = jnp.sum(lax.all_gather(gain_own, 'user', axis=0), axis=0)]
    ppermute x9 -> x48, starting transfers between devices: 8.61 us -> 49.6 us  [the longest x40 41.1 us: flip(): lax.ppermute(value, 'user', [(source, source ^ bits) for source in range(...]
    pallas_call x0 -> x13, Pallas kernels: none -> 34.7 us  [the longest x8 25.2 us: spread_items(): pl.pallas_call(functools.partial(spread, blocks), out_shape=jax.ShapeDtyp...]
    ppermute x9 -> x48, waiting for transfers between devices: 48.9 us -> 25.7 us  [the longest x40 19.3 us: flip(): lax.ppermute(value, 'user', [(source, source ^ bits) for source in range(...]
    dot_general x9 -> x5, matrix products: 22.4 us -> 5.54 us  [the longest x3 4.03 us: on_device(): lax.dot_general(grad, dense[chunk * rows:(chunk + 1) * rows], (((0,), (0,...]
    all_gather x1, waiting for transfers between devices: 14.1 us -> 0.02 us  [on_device(): packed = lax.all_gather(packed, 'user', axis=0, tiled=True)]
    reduce_sum x4 -> x1, other arithmetic: 7 us -> 0.59 us  [on_device(): jnp.sum(swapped[:, ends[1]:].reshape(user_size, -1)[:, :col_width].astype...]
    all_to_all x2 -> x1, starting transfers between devices: 7.74 us -> 3.54 us  [on_device(): swapped = lax.all_to_all(jnp.concatenate(pieces, axis=1), 'user', 0, 0)]
  transfers between devices with their start and end apart: 12 -> 50, of which waited for: 10 -> 16; matrix products, arithmetic and copies ran while one was open for 7% -> 5% of each run, Pallas kernels for 1% -> 20%
where the time goes in v2:
time: 165 us
  starting transfers between devices  53.2 us (32%)
  Pallas kernels  37 us (22%)
  waiting for transfers between devices  35.1 us (21%)
  between operations  15.4 us (9%)
  local copies, waits for them, and re-layouts  10.2 us (6%)
  matrix products  9.81 us (6%)
  other arithmetic  4.42 us (3%)
    ppermute x40, starting transfers between devices, flip(): lax.ppermute(value, 'user', [(source, source ^ bits) for source in range(...  41.1 us
    pallas_call x8, Pallas kernels, spread_items(): pl.pallas_call(functools.partial(spread, blocks), out_shape=jax.ShapeDtyp...  25.2 us
    ppermute x40, waiting for transfers between devices, flip(): lax.ppermute(value, 'user', [(source, source ^ bits) for source in range(...  19.3 us
    all_to_all x1, waiting for transfers between devices, on_device(): swapped = lax.all_to_all(jnp.concatenate(pieces, axis=1), 'user', 0, 0)  9.37 us
    ppermute x8, starting transfers between devices, on_device(): pieces.append(lax.ppermute(partial, 'item', pairs))  8.56 us
    unnamed x31, local copies, waits for them, and re-layouts  7.24 us
    ppermute x8, waiting for transfers between devices, on_device(): pieces.append(lax.ppermute(partial, 'item', pairs))  6.35 us
    pallas_call x4, Pallas kernels, user_gradient(): pl.pallas_call(functools.partial(norm_backward, len(pieces[0])), out_shap...  5.92 us
  transfers between devices with their start and end apart: 50, of which 16 were waited for; matrix products, arithmetic and copies ran while one was open for 5% of the time, Pallas kernels for 20%

profile of v2, /device:TPU:0, one launch (start us, length us, event | category | flops | bytes accessed | tf_op | source)
XLA Modules:
  0.0 165.1 jit_solution(15939525862715099135)
XLA Ops:
  7.2 3.6 %own_queries.1 = (bf16[128,256]{1,0:T(8,128)(2,1)}, bf16[128,256]{1,0:T(8,128)(2,1)}) custom-call(s32[1]{0:T(128)} %bitcast.1.first_ref, s32[1,128]{1,0:T(1,128)} %cats_ref.1, bf16[128,512]{1,0:T(8,128)(2,1)} %bitcast.121, bf16[4,512,512]{2,1,0:T(8,128)(2,1)} %weight_ref.1), custom_call_target="tpu_custom_call" | custom-call | flops 268435456 | bytes 2359296 | tf_op jit(solution)/shard_map/own_queries/pallas_call | solution.py:97
  10.9 5.0 %collective-permute-start.9 = (bf16[128,256]{1,0:T(8,128)(2,1)}, bf16[128,256]{1,0:T(8,128)(2,1)S(1)}, u32[]{:S(2)}, u32[]{:S(2)}) collective-permute-start(bf16[128,256]{1,0:T(8,128)(2,1)} %get-tuple-element.15.rest_0_), channel_id=1, source_target_pairs={{0,20},{2,22},{4,16},{6,18},{8,28},{10,30},{12,24},{14,26},{16,4},... | collective-permute-start | bytes 196616 | tf_op jit(solution)/shard_map/ppermute | solution.py:234
  15.9 1.3 collective-permute-start.11
  17.2 2.4 %collective-permute-start.13 = (bf16[128,256]{1,0:T(8,128)(2,1)}, bf16[128,256]{1,0:T(8,128)(2,1)S(1)}, u32[]{:S(2)}, u32[]{:S(2)}) collective-permute-start(bf16[128,256]{1,0:T(8,128)(2,1)} %get-tuple-element.15.rest_0_), channel_id=1, source_target_pairs={{0,28},{2,30},{4,24},{6,26},{8,20},{10,22},{12,16},{14,18},{16,12}... | collective-permute-start | bytes 196616 | tf_op jit(solution)/shard_map/ppermute | solution.py:234
  19.6 1.5 collective-permute-start.1
  21.2 2.0 %collective-permute-start.5 = (bf16[128,256]{1,0:T(8,128)(2,1)}, bf16[128,256]{1,0:T(8,128)(2,1)S(1)}, u32[]{:S(2)}, u32[]{:S(2)}) collective-permute-start(bf16[128,256]{1,0:T(8,128)(2,1)} %get-tuple-element.15.rest_0_), channel_id=1, source_target_pairs={{0,12},{2,14},{4,8},{6,10},{8,4},{10,6},{12,0},{14,2},{16,28},{18,... | collective-permute-start | bytes 196616 | tf_op jit(solution)/shard_map/ppermute | solution.py:234
  23.1 4.6 %collective-permute-start.7 = (bf16[128,256]{1,0:T(8,128)(2,1)}, bf16[128,256]{1,0:T(8,128)(2,1)S(1)}, u32[]{:S(2)}, u32[]{:S(2)}) collective-permute-start(bf16[128,256]{1,0:T(8,128)(2,1)} %get-tuple-element.15.rest_0_), channel_id=1, source_target_pairs={{0,16},{2,18},{4,20},{6,22},{8,24},{10,26},{12,28},{14,30},{16,0},... | collective-permute-start | bytes 196616 | tf_op jit(solution)/shard_map/ppermute | solution.py:234
  27.9 1.0 collective-permute-start.17
  28.9 1.2 collective-permute-start.19
  31.4 2.4 %collective-permute-start.23 = (bf16[128,256]{1,0:T(8,128)(2,1)}, bf16[128,256]{1,0:T(8,128)(2,1)S(1)}, u32[]{:S(2)}, u32[]{:S(2)}) collective-permute-start(bf16[128,256]{1,0:T(8,128)(2,1)} %get-tuple-element.16.rest_0_), channel_id=1, source_target_pairs={{0,16},{2,18},{4,20},{6,22},{8,24},{10,26},{12,28},{14,30},{16,0},... | collective-permute-start | bytes 196616 | tf_op jit(solution)/shard_map/ppermute | solution.py:234
  33.8 1.8 %collective-permute-done.29.rest_14_ = bf16[128,256]{1,0:T(8,128)(2,1)S(1)} collective-permute-done((bf16[128,256]{1,0:T(8,128)(2,1)}, bf16[128,256]{1,0:T(8,128)(2,1)S(1)}, u32[]{:S(2)}, u32[]{:S(2)}) %collective-permute-start.29) | collective-permute-done | bytes 65568 | tf_op jit(solution)/shard_map/ppermute | solution.py:234
  36.7 2.4 %collective-permute-start.27 = (bf16[128,256]{1,0:T(8,128)(2,1)}, bf16[128,256]{1,0:T(8,128)(2,1)S(1)}, u32[]{:S(2)}, u32[]{:S(2)}) collective-permute-start(bf16[128,256]{1,0:T(8,128)(2,1)} %get-tuple-element.16.rest_0_), channel_id=1, source_target_pairs={{0,24},{2,26},{4,28},{6,30},{8,16},{10,18},{12,20},{14,22},{16,8},... | collective-permute-start | bytes 196616 | tf_op jit(solution)/shard_map/ppermute | solution.py:234
  39.7 4.1 %collective-permute-done.25.rest_10_ = bf16[128,256]{1,0:T(8,128)(2,1)S(1)} collective-permute-done((bf16[128,256]{1,0:T(8,128)(2,1)}, bf16[128,256]{1,0:T(8,128)(2,1)S(1)}, u32[]{:S(2)}, u32[]{:S(2)}) %collective-permute-start.25) | collective-permute-done | bytes 65568 | tf_op jit(solution)/shard_map/ppermute | solution.py:234
  48.4 2.5 %copy-done.4 = s32[1,1,80,128,128]{4,3,2,1,0:T(8,128)S(1)} copy-done((s32[1,1,80,128,128]{4,3,2,1,0:T(8,128)S(1)}, s32[1,1,80,128,128]{4,3,2,1,0:T(8,128)}, u32[]{:S(2)}) %copy-start.4) | copy-done | bytes 5242904
  50.9 2.2 %place_tiles.1.rest_16_ = bf16[2048,2048]{1,0:T(8,128)(2,1)S(1)} custom-call(s32[80]{0:T(128)S(1)} %bitcast.110, s32[1]{0:T(128)} %bitcast.102.count_ref, s32[80,128,128]{2,1,0:T(8,128)S(1)} %bitcast.105), custom_call_target="tpu_custom_call" | custom-call | flops 1310720 | bytes 13631488 | tf_op jit(solution)/shard_map/place_tiles/pallas_call | solution.py:40
  53.2 3.2 %spread_items.10.rest_0_ = bf16[512,256]{1,0:T(8,128)(2,1)S(1)} custom-call(s32[16]{0:T(128)S(1)} %iota_xor_fusion.order_ref, bf16[128,256]{1,0:T(8,128)(2,1)S(1)} %copy-done.5, bf16[128,256]{1,0:T(8,128)(2,1)S(1)} %collective-permute-done.rest_1_, bf16[128,256]{1,0:T(8,128)(2,1)S(1)} %collective-permute-done.1.rest_2_, ...), custom_call_target="tpu_custom_call" | custom-call | flops 536870912 | bytes 3407872 | tf_op jit(solution)/shard_map/spread_items/pallas_call | solution.py:148
  56.4 1.5 collective-permute-start.32
  57.9 3.2 %spread_items.11.rest_2_ = bf16[512,256]{1,0:T(8,128)(2,1)S(1)} custom-call(s32[16]{0:T(128)S(1)} %iota_xor_fusion.order_ref, bf16[128,256]{1,0:T(8,128)(2,1)S(1)} %copy-done.6, bf16[128,256]{1,0:T(8,128)(2,1)S(1)} %collective-permute-done.16.rest_1_, bf16[128,256]{1,0:T(8,128)(2,1)S(1)} %collective-permute-done.17.rest_2_, ...), custom_call_target="tpu_custom_call" | custom-call | flops 536870912 | bytes 3407872 | tf_op jit(solution)/shard_map/spread_items/pallas_call | solution.py:148
  61.7 3.1 %spread_items.8.rest_0_ = bf16[512,256]{1,0:T(8,128)(2,1)S(1)} custom-call(s32[16]{0:T(128)S(1)} %iota_xor_fusion.order_ref, bf16[128,256]{1,0:T(8,128)(2,1)S(1)} %copy-done.5, bf16[128,256]{1,0:T(8,128)(2,1)S(1)} %collective-permute-done.rest_1_, bf16[128,256]{1,0:T(8,128)(2,1)S(1)} %collective-permute-done.1.rest_2_, ...), custom_call_target="tpu_custom_call" | custom-call | flops 536870912 | bytes 3407872 | tf_op jit(solution)/shard_map/spread_items/pallas_call | solution.py:148
  64.9 1.5 collective-permute-start.15
  66.4 3.1 %spread_items.9.rest_2_ = bf16[512,256]{1,0:T(8,128)(2,1)S(1)} custom-call(s32[16]{0:T(128)S(1)} %iota_xor_fusion.order_ref, bf16[128,256]{1,0:T(8,128)(2,1)S(1)} %copy-done.6, bf16[128,256]{1,0:T(8,128)(2,1)S(1)} %collective-permute-done.16.rest_1_, bf16[128,256]{1,0:T(8,128)(2,1)S(1)} %collective-permute-done.17.rest_2_, ...), custom_call_target="tpu_custom_call" | custom-call | flops 536870912 | bytes 3407872 | tf_op jit(solution)/shard_map/spread_items/pallas_call | solution.py:148
  70.2 3.1 %spread_items.12.rest_0_ = bf16[512,256]{1,0:T(8,128)(2,1)S(1)} custom-call(s32[16]{0:T(128)S(1)} %iota_xor_fusion.order_ref, bf16[128,256]{1,0:T(8,128)(2,1)S(1)} %copy-done.5, bf16[128,256]{1,0:T(8,128)(2,1)S(1)} %collective-permute-done.rest_1_, bf16[128,256]{1,0:T(8,128)(2,1)S(1)} %collective-permute-done.1.rest_2_, ...), custom_call_target="tpu_custom_call" | custom-call | flops 536870912 | bytes 3407872 | tf_op jit(solution)/shard_map/spread_items/pallas_call | solution.py:148
  73.4 1.5 collective-permute-start.34
  74.9 3.4 %copy-done.1 = bf16[2048,2048]{1,0:T(8,128)(2,1)S(1)} copy-done((bf16[2048,2048]{1,0:T(8,128)(2,1)S(1)}, bf16[2048,2048]{1,0:T(8,128)(2,1)}, u32[]{:S(2)}) %copy-start.1) | copy-done | bytes 8388632
  78.3 3.1 %spread_items.13.rest_2_ = bf16[512,256]{1,0:T(8,128)(2,1)S(1)} custom-call(s32[16]{0:T(128)S(1)} %iota_xor_fusion.order_ref, bf16[128,256]{1,0:T(8,128)(2,1)S(1)} %copy-done.6, bf16[128,256]{1,0:T(8,128)(2,1)S(1)} %collective-permute-done.16.rest_1_, bf16[128,256]{1,0:T(8,128)(2,1)S(1)} %collective-permute-done.17.rest_2_, ...), custom_call_target="tpu_custom_call" | custom-call | flops 536870912 | bytes 3407872 | tf_op jit(solution)/shard_map/spread_items/pallas_call | solution.py:148
  81.4 3.1 %spread_items.15.rest_2_ = bf16[512,256]{1,0:T(8,128)(2,1)S(1)} custom-call(s32[16]{0:T(128)S(1)} %iota_xor_fusion.order_ref, bf16[128,256]{1,0:T(8,128)(2,1)S(1)} %copy-done.6, bf16[128,256]{1,0:T(8,128)(2,1)S(1)} %collective-permute-done.16.rest_1_, bf16[128,256]{1,0:T(8,128)(2,1)S(1)} %collective-permute-done.17.rest_2_, ...), custom_call_target="tpu_custom_call" | custom-call | flops 536870912 | bytes 3407872 | tf_op jit(solution)/shard_map/spread_items/pallas_call | solution.py:148
  84.6 3.1 %spread_items.14.rest_0_ = bf16[512,256]{1,0:T(8,128)(2,1)S(1)} custom-call(s32[16]{0:T(128)S(1)} %iota_xor_fusion.order_ref, bf16[128,256]{1,0:T(8,128)(2,1)S(1)} %copy-done.5, bf16[128,256]{1,0:T(8,128)(2,1)S(1)} %collective-permute-done.rest_1_, bf16[128,256]{1,0:T(8,128)(2,1)S(1)} %collective-permute-done.1.rest_2_, ...), custom_call_target="tpu_custom_call" | custom-call | flops 536870912 | bytes 3407872 | tf_op jit(solution)/shard_map/spread_items/pallas_call | solution.py:148
  88.5 1.4 collective-permute-start.37
  89.9 1.7 %user_gradient.5 = (bf16[512,512]{1,0:T(8,128)(2,1)S(1)}, f32[1,512]{1,0:T(1,128)S(1)}) custom-call(bf16[2048,512]{1,0:T(8,128)(2,1)S(1)} %copy-done.2, bf16[2048,512]{1,0:T(8,128)(2,1)S(1)} %copy-done.3, f32[1,512]{1,0:T(1,128)S(1)} %bitcast.106, bf16[512,256]{1,0:T(8,128)(2,1)S(1)} %spread_items.10.rest_0_, ...), custom_call_target="tpu_custom_call" | custom-call | flops 4194304 | bytes 2621440 | tf_op jit(solution)/shard_map/user_gradient/pallas_call | solution.py:209
  91.6 1.3 fusion.6
  93.6 1.7 %user_gradient.4 = (bf16[512,512]{1,0:T(8,128)(2,1)S(1)}, f32[1,512]{1,0:T(1,128)S(1)}) custom-call(bf16[2048,512]{1,0:T(8,128)(2,1)S(1)} %copy-done.2, bf16[2048,512]{1,0:T(8,128)(2,1)S(1)} %copy-done.3, f32[1,512]{1,0:T(1,128)S(1)} %bitcast.107, bf16[512,256]{1,0:T(8,128)(2,1)S(1)} %spread_items.8.rest_0_, ...), custom_call_target="tpu_custom_call" | custom-call | flops 4194304 | bytes 2621440 | tf_op jit(solution)/shard_map/user_gradient/pallas_call | solution.py:209
  95.3 1.3 fusion.8
  97.1 1.8 %user_gradient.6 = (bf16[512,512]{1,0:T(8,128)(2,1)S(1)}, f32[1,512]{1,0:T(1,128)S(1)}) custom-call(bf16[2048,512]{1,0:T(8,128)(2,1)S(1)} %copy-done.2, bf16[2048,512]{1,0:T(8,128)(2,1)S(1)} %copy-done.3, f32[1,512]{1,0:T(1,128)S(1)} %bitcast.108, bf16[512,256]{1,0:T(8,128)(2,1)S(1)} %spread_items.12.rest_0_, ...), custom_call_target="tpu_custom_call" | custom-call | flops 4194304 | bytes 2621440 | tf_op jit(solution)/shard_map/user_gradient/pallas_call | solution.py:209
  98.9 1.4 add_add_fusion
  100.3 2.4 %collective-permute-done.37.rest_3_ = bf16[512,256]{1,0:T(8,128)(2,1)S(1)} collective-permute-done((bf16[512,256]{1,0:T(8,128)(2,1)S(1)}, bf16[512,256]{1,0:T(8,128)(2,1)S(1)}, u32[]{:S(2)}, u32[]{:S(2)}) %collective-permute-start.37) | collective-permute-done | bytes 262176 | tf_op jit(solution)/shard_map/ppermute | solution.py:306
  102.7 3.5 %collective-permute-done.36.rest_1_ = bf16[512,256]{1,0:T(8,128)(2,1)S(1)} collective-permute-done((bf16[512,256]{1,0:T(8,128)(2,1)S(1)}, bf16[512,256]{1,0:T(8,128)(2,1)S(1)}, u32[]{:S(2)}, u32[]{:S(2)}) %collective-permute-start.36) | collective-permute-done | bytes 262176 | tf_op jit(solution)/shard_map/ppermute | solution.py:306
  110.9 1.3 collective-permute-start.44
  112.2 6.9 %collective-permute-done.39 = bf16[4,16,2048]{2,1,0:T(8,128)(2,1)S(1)} collective-permute-done((bf16[4,16,2048]{2,1,0:T(8,128)(2,1)S(1)}, bf16[4,16,2048]{2,1,0:T(8,128)(2,1)S(1)}, u32[]{:S(2)}, u32[]{:S(2)}) %collective-permute-start.39) | collective-permute-done | bytes 262176 | tf_op jit(solution)/shard_map/ppermute | solution.py:234
  120.0 2.6 %collective-permute-start.41 = (bf16[16,2048]{1,0:T(8,128)(2,1)S(1)}, bf16[16,2048]{1,0:T(8,128)(2,1)S(1)}, u32[]{:S(2)}, u32[]{:S(2)}) collective-permute-start(bf16[16,2048]{1,0:T(8,128)(2,1)S(1)} %get-tuple-element.44), channel_id=1, source_target_pairs={{0,16},{2,18},{4,20},{6,22},{8,24},{10,26},{12,28},{14,30},{16,0},... | collective-permute-start | bytes 196616 | tf_op jit(solution)/shard_map/ppermute | solution.py:234
  122.6 1.1 collective-permute-start.42
  124.8 2.6 %collective-permute-start.46 = (bf16[16,2048]{1,0:T(8,128)(2,1)S(1)}, bf16[16,2048]{1,0:T(8,128)(2,1)S(1)}, u32[]{:S(2)}, u32[]{:S(2)}) collective-permute-start(bf16[16,2048]{1,0:T(8,128)(2,1)S(1)} %get-tuple-element.47), channel_id=1, source_target_pairs={{0,16},{2,18},{4,20},{6,22},{8,24},{10,26},{12,28},{14,30},{16,0},... | collective-permute-start | bytes 196616 | tf_op jit(solution)/shard_map/ppermute | solution.py:234
  127.4 1.1 collective-permute-start.47
  129.5 3.1 %collective-permute-done.46 = bf16[16,2048]{1,0:T(8,128)(2,1)S(1)} collective-permute-done((bf16[16,2048]{1,0:T(8,128)(2,1)S(1)}, bf16[16,2048]{1,0:T(8,128)(2,1)S(1)}, u32[]{:S(2)}, u32[]{:S(2)}) %collective-permute-start.46) | collective-permute-done | bytes 65568 | tf_op jit(solution)/shard_map/ppermute | solution.py:234
  133.7 1.4 convert_reduce_fusion
  135.2 2.3 %fusion.21 = bf16[512,128]{1,0:T(8,128)(2,1)S(1)} fusion(bf16[128,2048]{1,0:T(8,128)(2,1)S(1)} %bitcast.123, bf16[2048,640]{1,0:T(8,128)(2,1)} %all-gather.2.cloned.1.call-done), kind=kOutput, calls=%fused_computation.22 | convolution fusion | flops 268500992 | bytes 2752512 | tf_op jit(solution)/shard_map/dot_general | solution.py:352
  138.4 3.5 %all-to-all-start = ((bf16[16,66,128]{2,1,0:T(8,128)(2,1)}), bf16[16,66,128]{2,1,0:T(8,128)(2,1)S(1)}, u32[]{:S(2)}, u32[]{:S(2)}) async-start(bf16[16,66,128]{2,1,0:T(8,128)(2,1)} %copy.45), calls=%async_computation | async-start | bytes 589824 | tf_op jit(solution)/shard_map/all_to_all | solution.py:365
  142.1 1.0 pad_maximum_fusion
  143.1 9.4 %all-to-all-done = bf16[16,66,128]{2,1,0:T(8,128)(2,1)S(1)} async-done(((bf16[16,66,128]{2,1,0:T(8,128)(2,1)}), bf16[16,66,128]{2,1,0:T(8,128)(2,1)S(1)}, u32[]{:S(2)}, u32[]{:S(2)}) %all-to-all-start) | async-done | bytes 270368 | tf_op jit(solution)/shard_map/all_to_all | solution.py:365
  (143 shorter events, 25.6 us)
Async XLA Ops:
  7.2 126.5 %all-gather.2.cloned.1.call-start = ((), (), s32[]{:S(2)}) async-start(), calls=%async_computation.1 | async-start | bytes 2785280 | tf_op jit(solution)/shard_map/all_gather | solution.py:296
  10.9 10.3 %collective-permute-start.9 = (bf16[128,256]{1,0:T(8,128)(2,1)}, bf16[128,256]{1,0:T(8,128)(2,1)S(1)}, u32[]{:S(2)}, u32[]{:S(2)}) collective-permute-start(bf16[128,256]{1,0:T(8,128)(2,1)} %get-tuple-element.15.rest_0_), channel_id=1, source_target_pairs={{0,20},{2,22},{4,16},{6,18},{8,28},{10,30},{12,24},{14,26},{16,4},... | collective-permute-start | bytes 196616 | tf_op jit(solution)/shard_map/ppermute | solution.py:234
  15.9 7.3 %collective-permute-start.11 = (bf16[128,256]{1,0:T(8,128)(2,1)}, bf16[128,256]{1,0:T(8,128)(2,1)S(1)}, u32[]{:S(2)}, u32[]{:S(2)}) collective-permute-start(bf16[128,256]{1,0:T(8,128)(2,1)} %get-tuple-element.15.rest_0_), channel_id=1, source_target_pairs={{0,24},{2,26},{4,28},{6,30},{8,16},{10,18},{12,20},{14,22},{16,8},... | collective-permute-start | bytes 196616 | tf_op jit(solution)/shard_map/ppermute | solution.py:234
  17.2 10.6 %collective-permute-start.13 = (bf16[128,256]{1,0:T(8,128)(2,1)}, bf16[128,256]{1,0:T(8,128)(2,1)S(1)}, u32[]{:S(2)}, u32[]{:S(2)}) collective-permute-start(bf16[128,256]{1,0:T(8,128)(2,1)} %get-tuple-element.15.rest_0_), channel_id=1, source_target_pairs={{0,28},{2,30},{4,24},{6,26},{8,20},{10,22},{12,16},{14,18},{16,12}... | collective-permute-start | bytes 196616 | tf_op jit(solution)/shard_map/ppermute | solution.py:234
  19.6 8.1 %collective-permute-start.1 = (bf16[128,256]{1,0:T(8,128)(2,1)}, bf16[128,256]{1,0:T(8,128)(2,1)S(1)}, u32[]{:S(2)}, u32[]{:S(2)}) collective-permute-start(bf16[128,256]{1,0:T(8,128)(2,1)} %get-tuple-element.15.rest_0_), channel_id=1, source_target_pairs={{0,4},{2,6},{4,0},{6,2},{8,12},{10,14},{12,8},{14,10},{16,20},{18,... | collective-permute-start | bytes 196616 | tf_op jit(solution)/shard_map/ppermute | solution.py:234
  21.2 6.7 %collective-permute-start.3 = (bf16[128,256]{1,0:T(8,128)(2,1)}, bf16[128,256]{1,0:T(8,128)(2,1)S(1)}, u32[]{:S(2)}, u32[]{:S(2)}) collective-permute-start(bf16[128,256]{1,0:T(8,128)(2,1)} %get-tuple-element.15.rest_0_), channel_id=1, source_target_pairs={{0,8},{2,10},{4,12},{6,14},{8,0},{10,2},{12,4},{14,6},{16,24},{18,... | collective-permute-start | bytes 196616 | tf_op jit(solution)/shard_map/ppermute | solution.py:234
  21.2 7.7 %collective-permute-start.5 = (bf16[128,256]{1,0:T(8,128)(2,1)}, bf16[128,256]{1,0:T(8,128)(2,1)S(1)}, u32[]{:S(2)}, u32[]{:S(2)}) collective-permute-start(bf16[128,256]{1,0:T(8,128)(2,1)} %get-tuple-element.15.rest_0_), channel_id=1, source_target_pairs={{0,12},{2,14},{4,8},{6,10},{8,4},{10,6},{12,0},{14,2},{16,28},{18,... | collective-permute-start | bytes 196616 | tf_op jit(solution)/shard_map/ppermute | solution.py:234
  23.1 7.4 %collective-permute-start.7 = (bf16[128,256]{1,0:T(8,128)(2,1)}, bf16[128,256]{1,0:T(8,128)(2,1)S(1)}, u32[]{:S(2)}, u32[]{:S(2)}) collective-permute-start(bf16[128,256]{1,0:T(8,128)(2,1)} %get-tuple-element.15.rest_0_), channel_id=1, source_target_pairs={{0,16},{2,18},{4,20},{6,22},{8,24},{10,26},{12,28},{14,30},{16,0},... | collective-permute-start | bytes 196616 | tf_op jit(solution)/shard_map/ppermute | solution.py:234
  27.8 3.7 %collective-permute-start = (bf16[128,256]{1,0:T(8,128)(2,1)}, bf16[128,256]{1,0:T(8,128)(2,1)S(1)}, u32[]{:S(2)}, u32[]{:S(2)}) collective-permute-start(bf16[128,256]{1,0:T(8,128)(2,1)} %get-tuple-element.15.rest_0_), channel_id=1, source_target_pairs={{0,2},{2,0},{4,6},{6,4},{8,10},{10,8},{12,14},{14,12},{16,18},{18,... | collective-permute-start | bytes 196616 | tf_op jit(solution)/shard_map/ppermute | solution.py:234
  27.8 7.9 %collective-permute-start.29 = (bf16[128,256]{1,0:T(8,128)(2,1)}, bf16[128,256]{1,0:T(8,128)(2,1)S(1)}, u32[]{:S(2)}, u32[]{:S(2)}) collective-permute-start(bf16[128,256]{1,0:T(8,128)(2,1)} %get-tuple-element.16.rest_0_), channel_id=1, source_target_pairs={{0,28},{2,30},{4,24},{6,26},{8,20},{10,22},{12,16},{14,18},{16,12}... | collective-permute-start | bytes 196616 | tf_op jit(solution)/shard_map/ppermute | solution.py:234
  27.9 8.8 %collective-permute-start.17 = (bf16[128,256]{1,0:T(8,128)(2,1)}, bf16[128,256]{1,0:T(8,128)(2,1)S(1)}, u32[]{:S(2)}, u32[]{:S(2)}) collective-permute-start(bf16[128,256]{1,0:T(8,128)(2,1)} %get-tuple-element.16.rest_0_), channel_id=1, source_target_pairs={{0,4},{2,6},{4,0},{6,2},{8,12},{10,14},{12,8},{14,10},{16,20},{18,... | collective-permute-start | bytes 196616 | tf_op jit(solution)/shard_map/ppermute | solution.py:234
  28.9 10.2 %collective-permute-start.19 = (bf16[128,256]{1,0:T(8,128)(2,1)}, bf16[128,256]{1,0:T(8,128)(2,1)S(1)}, u32[]{:S(2)}, u32[]{:S(2)}) collective-permute-start(bf16[128,256]{1,0:T(8,128)(2,1)} %get-tuple-element.16.rest_0_), channel_id=1, source_target_pairs={{0,8},{2,10},{4,12},{6,14},{8,0},{10,2},{12,4},{14,6},{16,24},{18,... | collective-permute-start | bytes 196616 | tf_op jit(solution)/shard_map/ppermute | solution.py:234
  30.5 8.6 %collective-permute-start.21 = (bf16[128,256]{1,0:T(8,128)(2,1)}, bf16[128,256]{1,0:T(8,128)(2,1)S(1)}, u32[]{:S(2)}, u32[]{:S(2)}) collective-permute-start(bf16[128,256]{1,0:T(8,128)(2,1)} %get-tuple-element.16.rest_0_), channel_id=1, source_target_pairs={{0,12},{2,14},{4,8},{6,10},{8,4},{10,6},{12,0},{14,2},{16,28},{18,... | collective-permute-start | bytes 196616 | tf_op jit(solution)/shard_map/ppermute | solution.py:234
  31.4 8.2 %collective-permute-start.23 = (bf16[128,256]{1,0:T(8,128)(2,1)}, bf16[128,256]{1,0:T(8,128)(2,1)S(1)}, u32[]{:S(2)}, u32[]{:S(2)}) collective-permute-start(bf16[128,256]{1,0:T(8,128)(2,1)} %get-tuple-element.16.rest_0_), channel_id=1, source_target_pairs={{0,16},{2,18},{4,20},{6,22},{8,24},{10,26},{12,28},{14,30},{16,0},... | collective-permute-start | bytes 196616 | tf_op jit(solution)/shard_map/ppermute | solution.py:234
  35.7 8.1 %collective-permute-start.25 = (bf16[128,256]{1,0:T(8,128)(2,1)}, bf16[128,256]{1,0:T(8,128)(2,1)S(1)}, u32[]{:S(2)}, u32[]{:S(2)}) collective-permute-start(bf16[128,256]{1,0:T(8,128)(2,1)} %get-tuple-element.16.rest_0_), channel_id=1, source_target_pairs={{0,20},{2,22},{4,16},{6,18},{8,28},{10,30},{12,24},{14,26},{16,4},... | collective-permute-start | bytes 196616 | tf_op jit(solution)/shard_map/ppermute | solution.py:234
  36.7 7.1 %collective-permute-start.27 = (bf16[128,256]{1,0:T(8,128)(2,1)}, bf16[128,256]{1,0:T(8,128)(2,1)S(1)}, u32[]{:S(2)}, u32[]{:S(2)}) collective-permute-start(bf16[128,256]{1,0:T(8,128)(2,1)} %get-tuple-element.16.rest_0_), channel_id=1, source_target_pairs={{0,24},{2,26},{4,28},{6,30},{8,16},{10,18},{12,20},{14,22},{16,8},... | collective-permute-start | bytes 196616 | tf_op jit(solution)/shard_map/ppermute | solution.py:234
  39.1 5.2 %collective-permute-start.16 = (bf16[128,256]{1,0:T(8,128)(2,1)}, bf16[128,256]{1,0:T(8,128)(2,1)S(1)}, u32[]{:S(2)}, u32[]{:S(2)}) collective-permute-start(bf16[128,256]{1,0:T(8,128)(2,1)} %get-tuple-element.16.rest_0_), channel_id=1, source_target_pairs={{0,2},{2,0},{4,6},{6,4},{8,10},{10,8},{12,14},{14,12},{16,18},{18,... | collective-permute-start | bytes 196616 | tf_op jit(solution)/shard_map/ppermute | solution.py:234
  39.1 5.3 %collective-permute-start.10 = (bf16[128,256]{1,0:T(8,128)(2,1)S(1)}, bf16[128,256]{1,0:T(8,128)(2,1)S(1)}, u32[]{:S(2)}, u32[]{:S(2)}) collective-permute-start(bf16[128,256]{1,0:T(8,128)(2,1)S(1)} %collective-permute-done.9.rest_10_), channel_id=1, source_target_pairs={{0,2},{2,0},{4,6},{6,4},{8,10},{10,8},{12,14},{14,12},{16,18},{18,... | collective-permute-start | bytes 196616 | tf_op jit(solution)/shard_map/ppermute | solution.py:234
  39.6 5.3 %collective-permute-start.12 = (bf16[128,256]{1,0:T(8,128)(2,1)S(1)}, bf16[128,256]{1,0:T(8,128)(2,1)S(1)}, u32[]{:S(2)}, u32[]{:S(2)}) collective-permute-start(bf16[128,256]{1,0:T(8,128)(2,1)S(1)} %collective-permute-done.11.rest_12_), channel_id=1, source_target_pairs={{0,2},{2,0},{4,6},{6,4},{8,10},{10,8},{12,14},{14,12},{16,18},{18,... | collective-permute-start | bytes 196616 | tf_op jit(solution)/shard_map/ppermute | solution.py:234
  44.3 2.0 %collective-permute-start.4 = (bf16[128,256]{1,0:T(8,128)(2,1)S(1)}, bf16[128,256]{1,0:T(8,128)(2,1)S(1)}, u32[]{:S(2)}, u32[]{:S(2)}) collective-permute-start(bf16[128,256]{1,0:T(8,128)(2,1)S(1)} %collective-permute-done.3.rest_4_), channel_id=1, source_target_pairs={{0,2},{2,0},{4,6},{6,4},{8,10},{10,8},{12,14},{14,12},{16,18},{18,... | collective-permute-start | bytes 196616 | tf_op jit(solution)/shard_map/ppermute | solution.py:234
  44.4 2.3 %collective-permute-start.6 = (bf16[128,256]{1,0:T(8,128)(2,1)S(1)}, bf16[128,256]{1,0:T(8,128)(2,1)S(1)}, u32[]{:S(2)}, u32[]{:S(2)}) collective-permute-start(bf16[128,256]{1,0:T(8,128)(2,1)S(1)} %collective-permute-done.5.rest_6_), channel_id=1, source_target_pairs={{0,2},{2,0},{4,6},{6,4},{8,10},{10,8},{12,14},{14,12},{16,18},{18,... | collective-permute-start | bytes 196616 | tf_op jit(solution)/shard_map/ppermute | solution.py:234
  44.9 2.0 %collective-permute-start.8 = (bf16[128,256]{1,0:T(8,128)(2,1)S(1)}, bf16[128,256]{1,0:T(8,128)(2,1)S(1)}, u32[]{:S(2)}, u32[]{:S(2)}) collective-permute-start(bf16[128,256]{1,0:T(8,128)(2,1)S(1)} %collective-permute-done.7.rest_8_), channel_id=1, source_target_pairs={{0,2},{2,0},{4,6},{6,4},{8,10},{10,8},{12,14},{14,12},{16,18},{18,... | collective-permute-start | bytes 196616 | tf_op jit(solution)/shard_map/ppermute | solution.py:234
  45.0 2.2 %collective-permute-start.30 = (bf16[128,256]{1,0:T(8,128)(2,1)S(1)}, bf16[128,256]{1,0:T(8,128)(2,1)S(1)}, u32[]{:S(2)}, u32[]{:S(2)}) collective-permute-start(bf16[128,256]{1,0:T(8,128)(2,1)S(1)} %collective-permute-done.29.rest_14_), channel_id=1, source_target_pairs={{0,2},{2,0},{4,6},{6,4},{8,10},{10,8},{12,14},{14,12},{16,18},{18,... | collective-permute-start | bytes 196616 | tf_op jit(solution)/shard_map/ppermute | solution.py:234
  45.4 2.0 %collective-permute-start.18 = (bf16[128,256]{1,0:T(8,128)(2,1)S(1)}, bf16[128,256]{1,0:T(8,128)(2,1)S(1)}, u32[]{:S(2)}, u32[]{:S(2)}) collective-permute-start(bf16[128,256]{1,0:T(8,128)(2,1)S(1)} %collective-permute-done.17.rest_2_), channel_id=1, source_target_pairs={{0,2},{2,0},{4,6},{6,4},{8,10},{10,8},{12,14},{14,12},{16,18},{18,... | collective-permute-start | bytes 196616 | tf_op jit(solution)/shard_map/ppermute | solution.py:234
  46.3 10.1 %collective-permute-start.20 = (bf16[128,256]{1,0:T(8,128)(2,1)S(1)}, bf16[128,256]{1,0:T(8,128)(2,1)S(1)}, u32[]{:S(2)}, u32[]{:S(2)}) collective-permute-start(bf16[128,256]{1,0:T(8,128)(2,1)S(1)} %collective-permute-done.19.rest_4_), channel_id=1, source_target_pairs={{0,2},{2,0},{4,6},{6,4},{8,10},{10,8},{12,14},{14,12},{16,18},{18,... | collective-permute-start | bytes 196616 | tf_op jit(solution)/shard_map/ppermute | solution.py:234
  46.7 11.2 %collective-permute-start.22 = (bf16[128,256]{1,0:T(8,128)(2,1)S(1)}, bf16[128,256]{1,0:T(8,128)(2,1)S(1)}, u32[]{:S(2)}, u32[]{:S(2)}) collective-permute-start(bf16[128,256]{1,0:T(8,128)(2,1)S(1)} %collective-permute-done.21.rest_6_), channel_id=1, source_target_pairs={{0,2},{2,0},{4,6},{6,4},{8,10},{10,8},{12,14},{14,12},{16,18},{18,... | collective-permute-start | bytes 196616 | tf_op jit(solution)/shard_map/ppermute | solution.py:234
  46.8 11.0 %collective-permute-start.24 = (bf16[128,256]{1,0:T(8,128)(2,1)S(1)}, bf16[128,256]{1,0:T(8,128)(2,1)S(1)}, u32[]{:S(2)}, u32[]{:S(2)}) collective-permute-start(bf16[128,256]{1,0:T(8,128)(2,1)S(1)} %collective-permute-done.23.rest_8_), channel_id=1, source_target_pairs={{0,2},{2,0},{4,6},{6,4},{8,10},{10,8},{12,14},{14,12},{16,18},{18,... | collective-permute-start | bytes 196616 | tf_op jit(solution)/shard_map/ppermute | solution.py:234
  47.2 10.7 %collective-permute-start.26 = (bf16[128,256]{1,0:T(8,128)(2,1)S(1)}, bf16[128,256]{1,0:T(8,128)(2,1)S(1)}, u32[]{:S(2)}, u32[]{:S(2)}) collective-permute-start(bf16[128,256]{1,0:T(8,128)(2,1)S(1)} %collective-permute-done.25.rest_10_), channel_id=1, source_target_pairs={{0,2},{2,0},{4,6},{6,4},{8,10},{10,8},{12,14},{14,12},{16,18},{18,... | collective-permute-start | bytes 196616 | tf_op jit(solution)/shard_map/ppermute | solution.py:234
  47.4 10.5 %collective-permute-start.28 = (bf16[128,256]{1,0:T(8,128)(2,1)S(1)}, bf16[128,256]{1,0:T(8,128)(2,1)S(1)}, u32[]{:S(2)}, u32[]{:S(2)}) collective-permute-start(bf16[128,256]{1,0:T(8,128)(2,1)S(1)} %collective-permute-done.27.rest_12_), channel_id=1, source_target_pairs={{0,2},{2,0},{4,6},{6,4},{8,10},{10,8},{12,14},{14,12},{16,18},{18,... | collective-permute-start | bytes 196616 | tf_op jit(solution)/shard_map/ppermute | solution.py:234
  56.4 31.4 %collective-permute-start.32 = (bf16[512,256]{1,0:T(8,128)(2,1)S(1)}, bf16[512,256]{1,0:T(8,128)(2,1)}, u32[]{:S(2)}, u32[]{:S(2)}) collective-permute-start(bf16[512,256]{1,0:T(8,128)(2,1)S(1)} %spread_items.10.rest_0_), channel_id=1, source_target_pairs={{0,1},{1,0},{2,3},{3,2},{4,5},{5,4},{6,7},{7,6},{8,9},{9,8},{10,11... | collective-permute-start | bytes 786440 | tf_op jit(solution)/shard_map/ppermute | solution.py:306
  61.1 27.4 %collective-permute-start.33 = (bf16[512,256]{1,0:T(8,128)(2,1)S(1)}, bf16[512,256]{1,0:T(8,128)(2,1)}, u32[]{:S(2)}, u32[]{:S(2)}) collective-permute-start(bf16[512,256]{1,0:T(8,128)(2,1)S(1)} %spread_items.11.rest_2_), channel_id=1, source_target_pairs={{0,1},{1,0},{2,3},{3,2},{4,5},{5,4},{6,7},{7,6},{8,9},{9,8},{10,11... | collective-permute-start | bytes 786440 | tf_op jit(solution)/shard_map/ppermute | solution.py:306
  64.9 28.0 %collective-permute-start.15 = (bf16[512,256]{1,0:T(8,128)(2,1)S(1)}, bf16[512,256]{1,0:T(8,128)(2,1)}, u32[]{:S(2)}, u32[]{:S(2)}) collective-permute-start(bf16[512,256]{1,0:T(8,128)(2,1)S(1)} %spread_items.8.rest_0_), channel_id=1, source_target_pairs={{0,1},{1,0},{2,3},{3,2},{4,5},{5,4},{6,7},{7,6},{8,9},{9,8},{10,11... | collective-permute-start | bytes 786440 | tf_op jit(solution)/shard_map/ppermute | solution.py:306
  69.5 24.1 %collective-permute-start.31 = (bf16[512,256]{1,0:T(8,128)(2,1)S(1)}, bf16[512,256]{1,0:T(8,128)(2,1)}, u32[]{:S(2)}, u32[]{:S(2)}) collective-permute-start(bf16[512,256]{1,0:T(8,128)(2,1)S(1)} %spread_items.9.rest_2_), channel_id=1, source_target_pairs={{0,1},{1,0},{2,3},{3,2},{4,5},{5,4},{6,7},{7,6},{8,9},{9,8},{10,11... | collective-permute-start | bytes 786440 | tf_op jit(solution)/shard_map/ppermute | solution.py:306
  73.4 23.2 %collective-permute-start.34 = (bf16[512,256]{1,0:T(8,128)(2,1)S(1)}, bf16[512,256]{1,0:T(8,128)(2,1)}, u32[]{:S(2)}, u32[]{:S(2)}) collective-permute-start(bf16[512,256]{1,0:T(8,128)(2,1)S(1)} %spread_items.12.rest_0_), channel_id=1, source_target_pairs={{0,1},{1,0},{2,3},{3,2},{4,5},{5,4},{6,7},{7,6},{8,9},{9,8},{10,11... | collective-permute-start | bytes 786440 | tf_op jit(solution)/shard_map/ppermute | solution.py:306
  87.8 9.3 %collective-permute-start.35 = (bf16[512,256]{1,0:T(8,128)(2,1)S(1)}, bf16[512,256]{1,0:T(8,128)(2,1)S(1)}, u32[]{:S(2)}, u32[]{:S(2)}) collective-permute-start(bf16[512,256]{1,0:T(8,128)(2,1)S(1)} %spread_items.13.rest_2_), channel_id=1, source_target_pairs={{0,1},{1,0},{2,3},{3,2},{4,5},{5,4},{6,7},{7,6},{8,9},{9,8},{10,11... | collective-permute-start | bytes 786440 | tf_op jit(solution)/shard_map/ppermute | solution.py:306
  88.5 14.3 %collective-permute-start.37 = (bf16[512,256]{1,0:T(8,128)(2,1)S(1)}, bf16[512,256]{1,0:T(8,128)(2,1)S(1)}, u32[]{:S(2)}, u32[]{:S(2)}) collective-permute-start(bf16[512,256]{1,0:T(8,128)(2,1)S(1)} %spread_items.15.rest_2_), channel_id=1, source_target_pairs={{0,1},{1,0},{2,3},{3,2},{4,5},{5,4},{6,7},{7,6},{8,9},{9,8},{10,11... | collective-permute-start | bytes 786440 | tf_op jit(solution)/shard_map/ppermute | solution.py:306
  92.9 13.3 %collective-permute-start.36 = (bf16[512,256]{1,0:T(8,128)(2,1)S(1)}, bf16[512,256]{1,0:T(8,128)(2,1)S(1)}, u32[]{:S(2)}, u32[]{:S(2)}) collective-permute-start(bf16[512,256]{1,0:T(8,128)(2,1)S(1)} %spread_items.14.rest_0_), channel_id=1, source_target_pairs={{0,1},{1,0},{2,3},{3,2},{4,5},{5,4},{6,7},{7,6},{8,9},{9,8},{10,11... | collective-permute-start | bytes 786440 | tf_op jit(solution)/shard_map/ppermute | solution.py:306
  107.8 2.0 %collective-permute-start.38 = (bf16[4,2,16,2048]{3,2,0,1:T(8,128)(2,1)S(1)}, bf16[4,2,16,2048]{3,2,0,1:T(8,128)(2,1)S(1)}, u32[]{:S(2)}, u32[]{:S(2)}) collective-permute-start(bf16[4,2,16,2048]{3,2,0,1:T(8,128)(2,1)S(1)} %fusion.26), channel_id=1, source_target_pairs={{0,2},{2,0},{4,6},{6,4},{8,10},{10,8},{12,14},{14,12},{16,18},{18,... | collective-permute-start | bytes 1572872 | tf_op jit(solution)/shard_map/ppermute | solution.py:234
  108.7 2.1 %collective-permute-start.43 = (bf16[4,2,16,2048]{3,2,0,1:T(8,128)(2,1)S(1)}, bf16[4,2,16,2048]{3,2,0,1:T(8,128)(2,1)S(1)}, u32[]{:S(2)}, u32[]{:S(2)}) collective-permute-start(bf16[4,2,16,2048]{3,2,0,1:T(8,128)(2,1)S(1)} %fusion.27), channel_id=1, source_target_pairs={{0,2},{2,0},{4,6},{6,4},{8,10},{10,8},{12,14},{14,12},{16,18},{18,... | collective-permute-start | bytes 1572872 | tf_op jit(solution)/shard_map/ppermute | solution.py:234
  109.9 9.2 %collective-permute-start.39 = (bf16[4,16,2048]{2,1,0:T(8,128)(2,1)S(1)}, bf16[4,16,2048]{2,1,0:T(8,128)(2,1)S(1)}, u32[]{:S(2)}, u32[]{:S(2)}) collective-permute-start(bf16[4,16,2048]{2,1,0:T(8,128)(2,1)S(1)} %fusion.36), channel_id=1, source_target_pairs={{0,4},{2,6},{4,0},{6,2},{8,12},{10,14},{12,8},{14,10},{16,20},{18,... | collective-permute-start | bytes 786440 | tf_op jit(solution)/shard_map/ppermute | solution.py:234
  110.9 13.0 %collective-permute-start.44 = (bf16[4,16,2048]{2,1,0:T(8,128)(2,1)S(1)}, bf16[4,16,2048]{2,1,0:T(8,128)(2,1)S(1)}, u32[]{:S(2)}, u32[]{:S(2)}) collective-permute-start(bf16[4,16,2048]{2,1,0:T(8,128)(2,1)S(1)} %fusion.37), channel_id=1, source_target_pairs={{0,4},{2,6},{4,0},{6,2},{8,12},{10,14},{12,8},{14,10},{16,20},{18,... | collective-permute-start | bytes 786440 | tf_op jit(solution)/shard_map/ppermute | solution.py:234
  119.2 8.2 %collective-permute-start.40 = (bf16[16,2048]{1,0:T(8,128)(2,1)S(1)}, bf16[16,2048]{1,0:T(8,128)(2,1)S(1)}, u32[]{:S(2)}, u32[]{:S(2)}) collective-permute-start(bf16[16,2048]{1,0:T(8,128)(2,1)S(1)} %get-tuple-element.42), channel_id=1, source_target_pairs={{0,8},{2,10},{4,12},{6,14},{8,0},{10,2},{12,4},{14,6},{16,24},{18,... | collective-permute-start | bytes 196616 | tf_op jit(solution)/shard_map/ppermute | solution.py:234
  120.0 8.5 %collective-permute-start.41 = (bf16[16,2048]{1,0:T(8,128)(2,1)S(1)}, bf16[16,2048]{1,0:T(8,128)(2,1)S(1)}, u32[]{:S(2)}, u32[]{:S(2)}) collective-permute-start(bf16[16,2048]{1,0:T(8,128)(2,1)S(1)} %get-tuple-element.44), channel_id=1, source_target_pairs={{0,16},{2,18},{4,20},{6,22},{8,24},{10,26},{12,28},{14,30},{16,0},... | collective-permute-start | bytes 196616 | tf_op jit(solution)/shard_map/ppermute | solution.py:234
  122.6 6.8 %collective-permute-start.42 = (bf16[16,2048]{1,0:T(8,128)(2,1)S(1)}, bf16[16,2048]{1,0:T(8,128)(2,1)S(1)}, u32[]{:S(2)}, u32[]{:S(2)}) collective-permute-start(bf16[16,2048]{1,0:T(8,128)(2,1)S(1)} %get-tuple-element.43), channel_id=1, source_target_pairs={{0,24},{2,26},{4,28},{6,30},{8,16},{10,18},{12,20},{14,22},{16,8},... | collective-permute-start | bytes 196616 | tf_op jit(solution)/shard_map/ppermute | solution.py:234
  124.1 5.4 %collective-permute-start.45 = (bf16[16,2048]{1,0:T(8,128)(2,1)S(1)}, bf16[16,2048]{1,0:T(8,128)(2,1)S(1)}, u32[]{:S(2)}, u32[]{:S(2)}) collective-permute-start(bf16[16,2048]{1,0:T(8,128)(2,1)S(1)} %get-tuple-element.45), channel_id=1, source_target_pairs={{0,8},{2,10},{4,12},{6,14},{8,0},{10,2},{12,4},{14,6},{16,24},{18,... | collective-permute-start | bytes 196616 | tf_op jit(solution)/shard_map/ppermute | solution.py:234
  124.8 7.8 %collective-permute-start.46 = (bf16[16,2048]{1,0:T(8,128)(2,1)S(1)}, bf16[16,2048]{1,0:T(8,128)(2,1)S(1)}, u32[]{:S(2)}, u32[]{:S(2)}) collective-permute-start(bf16[16,2048]{1,0:T(8,128)(2,1)S(1)} %get-tuple-element.47), channel_id=1, source_target_pairs={{0,16},{2,18},{4,20},{6,22},{8,24},{10,26},{12,28},{14,30},{16,0},... | collective-permute-start | bytes 196616 | tf_op jit(solution)/shard_map/ppermute | solution.py:234
  127.4 6.2 %collective-permute-start.47 = (bf16[16,2048]{1,0:T(8,128)(2,1)S(1)}, bf16[16,2048]{1,0:T(8,128)(2,1)S(1)}, u32[]{:S(2)}, u32[]{:S(2)}) collective-permute-start(bf16[16,2048]{1,0:T(8,128)(2,1)S(1)} %get-tuple-element.46), channel_id=1, source_target_pairs={{0,24},{2,26},{4,28},{6,30},{8,16},{10,18},{12,20},{14,22},{16,8},... | collective-permute-start | bytes 196616 | tf_op jit(solution)/shard_map/ppermute | solution.py:234
  138.4 14.1 %all-to-all-start = ((bf16[16,66,128]{2,1,0:T(8,128)(2,1)}), bf16[16,66,128]{2,1,0:T(8,128)(2,1)S(1)}, u32[]{:S(2)}, u32[]{:S(2)}) async-start(bf16[16,66,128]{2,1,0:T(8,128)(2,1)} %copy.45), calls=%async_computation | async-start | bytes 589824 | tf_op jit(solution)/shard_map/all_to_all | solution.py:365
  (16 other events, 184.7 us)
Sparse Core Ops, SparseCore 0:
  75.0 42.1 all-gather.1

commit v3 on v2

--- a/solution.py
+++ b/solution.py
@@ -118,42 +118,51 @@
     )(first_expert.reshape(1), cats.reshape(1, own), feat, weights)
 
 
-def spread(blocks, order_ref, *rest):
-    query_refs, dense_ref, out_ref = rest[:blocks], rest[blocks], rest[blocks + 1]
-    all_ref, sems = rest[blocks + 2 :]
-    own = query_refs[0].shape[0]
-
-    @pl.when(pl.program_id(0) == 0)
-    def _():
-        copies = []
-        for place, query_ref in enumerate(query_refs):
-            start = pl.multiple_of(order_ref[place] * own, own)
-            copy = pltpu.make_async_copy(query_ref, all_ref.at[pl.ds(start, own)], sems.at[place])
-            copy.start()
-            copies.append(copy)
-        for copy in copies:
-            copy.wait()
-
-    out_ref[...] = jnp.dot(
-        dense_ref[...], all_ref[...], preferred_element_type=jnp.float32
-    ).astype(out_ref.dtype)
-
-
-def spread_items(order, queries, dense, first, rows):
+def fetch_in_order(order_ref, sources, all_ref, sems):
+    per_source = len(sems) // len(sources)
+    own = sources[0].shape[0] // per_source
+    copies = []
+    for place in range(len(sems)):
+        source = sources[place // per_source].at[pl.ds((place % per_source) * own, own)]
+        start = pl.multiple_of(order_ref[place] * own, own)
+        copy = pltpu.make_async_copy(source, all_ref.at[pl.ds(start, own)], sems[place])
+        copy.start()
+        copies.append(copy)
+    for copy in copies:
+        copy.wait()
+
+
+def spread(blocks, order_ref, same_ref, other_ref, dense_ref, *rest):
+    out_refs, all_ref, sems = rest[:-2], rest[-2], rest[-1]
+    step = pl.program_id(0)
+
+    @pl.when(step == 0)
+    def _():
+        fetch_in_order(
+            order_ref, (same_ref, other_ref), all_ref, [sems.at[place] for place in range(blocks)]
+        )
+
+    product = jnp.dot(dense_ref[...], all_ref[...], preferred_element_type=jnp.float32)
+    for chunk, out_ref in enumerate(out_refs):
+
+        @pl.when(step == chunk)
+        def _():
+            out_ref[...] = product.astype(out_ref.dtype)
+
+
+def spread_items(order, queries, dense, first, chunks, rows):
     items = dense.shape[1]
-    own, cols = queries[0].shape
-    blocks = len(queries)
-    block_rows = min(BLOCK_ROWS, rows)
-    first_block = first // block_rows
+    cols = queries[0].shape[1]
+    blocks = order.shape[0]
     return pl.pallas_call(
         functools.partial(spread, blocks),
-        out_shape=jax.ShapeDtypeStruct((rows, cols), jnp.bfloat16),
+        out_shape=[jax.ShapeDtypeStruct((rows, cols), jnp.bfloat16)] * chunks,
         grid_spec=pltpu.PrefetchScalarGridSpec(
             num_scalar_prefetch=1,
-            grid=(rows // block_rows,),
-            in_specs=[pl.BlockSpec(memory_space=pl.ANY)] * blocks
-            + [pl.BlockSpec((block_rows, items), lambda step, order_ref: (first_block + step, 0))],
-            out_specs=pl.BlockSpec((block_rows, cols), lambda step, order_ref: (step, 0)),
+            grid=(chunks,),
+            in_specs=[pl.BlockSpec(memory_space=pl.ANY)] * 2
+            + [pl.BlockSpec((rows, items), lambda step, order_ref: (first + step, 0))],
+            out_specs=[pl.BlockSpec((rows, cols), lambda step, order_ref: (0, 0))] * chunks,
             scratch_shapes=[
                 pltpu.VMEM((items, cols), jnp.bfloat16),
                 pltpu.SemaphoreType.DMA((blocks,)),
@@ -163,12 +172,57 @@
             dimension_semantics=("arbitrary",), vmem_limit_bytes=24 * MIB
         ),
         cost_estimate=pl.CostEstimate(
-            flops=2 * rows * items * cols,
-            bytes_accessed=rows * items * 2 + items * cols * 2 + rows * cols * 2,
+            flops=2 * chunks * rows * items * cols,
+            bytes_accessed=chunks * rows * (items + cols) * 2 + items * cols * 2,
             transcendentals=0,
         ),
         name="spread_items",
     )(order, *queries, dense)
+
+
+def order_items(blocks, order_ref, same_ref, other_ref, feat_ref, mask_ref, all_ref, sems):
+    fetch_in_order(
+        order_ref, (same_ref, other_ref), all_ref, [sems.at[place] for place in range(blocks)]
+    )
+    width = feat_ref.shape[1]
+    experts, own_width = mask_ref.shape[0], mask_ref.shape[1]
+    feat_ref[...] = all_ref[:, :width]
+    for start in range(0, feat_ref.shape[0], TILE):
+        cats = all_ref[pl.ds(start, TILE), pl.ds(width, TILE)].astype(jnp.float32)
+        cats = jnp.transpose(cats)[:own_width]
+        for expert in range(experts):
+            mask_ref[expert, :, pl.ds(start, TILE)] = (cats == expert).astype(mask_ref.dtype)
+
+
+def ordered_items(order, packed, experts, own_width, width):
+    items, blocks = 2 * packed[0].shape[0], order.shape[0]
+    return pl.pallas_call(
+        functools.partial(order_items, blocks),
+        out_shape=[
+            jax.ShapeDtypeStruct((items, width), jnp.bfloat16),
+            jax.ShapeDtypeStruct((experts, own_width, items), jnp.bfloat16),
+        ],
+        grid_spec=pltpu.PrefetchScalarGridSpec(
+            num_scalar_prefetch=1,
+            grid=(1,),
+            in_specs=[pl.BlockSpec(memory_space=pl.ANY)] * 2,
+            out_specs=[
+                pl.BlockSpec((items, width), lambda step, order_ref: (0, 0)),
+                pl.BlockSpec((experts, own_width, items), lambda step, order_ref: (0, 0, 0)),
+            ],
+            scratch_shapes=[
+                pltpu.VMEM((items, packed[0].shape[1]), jnp.bfloat16),
+                pltpu.SemaphoreType.DMA((blocks,)),
+            ],
+        ),
+        compiler_params=pltpu.CompilerParams(
+            dimension_semantics=("arbitrary",), vmem_limit_bytes=24 * MIB
+        ),
+        cost_estimate=pl.CostEstimate(
+            flops=0, bytes_accessed=items * width * 6, transcendentals=0
+        ),
+        name="order_items",
+    )(order, *packed)
 
 
 def norm_backward(pieces, user_ref, grad_ref, gain_ref, *rest):
@@ -234,13 +288,22 @@
     return lax.ppermute(value, "user", [(source, source ^ bits) for source in range(size)])
 
 
-def gather_parts(own, size):
-    same_core = [own] + [flip(own, size, 2 * chip) for chip in range(1, size // 2)]
-    parts = [None] * size
-    for chip, part in enumerate(same_core):
-        parts[2 * chip] = part
-        parts[2 * chip + 1] = flip(part, size, 1)
-    return parts
+def gather_layers(own, size):
+    return jnp.concatenate(
+        [own] + [flip(own, size, 4 * layer) for layer in range(1, size // 4)], axis=0
+    )
+
+
+def gather_sides(own, size):
+    own = jnp.concatenate([own, flip(own, size, 2)], axis=0)
+    return own, flip(own, size, 1)
+
+
+def gather_order(size):
+    layers = size // 4
+    place = jnp.arange(size, dtype=jnp.int32)
+    core, side, layer = place // (size // 2), (place // layers) % 2, place % layers
+    return lax.axis_index("user") ^ (layer * 4 + side * 2 + core)
 
 
 def scatter_sum(terms, size):
@@ -275,7 +338,7 @@
 ):
     users, width = user_feat.shape
     user_size, item_size = lax.axis_size("user"), lax.axis_size("item")
-    user_index, item_index = lax.axis_index("user"), lax.axis_index("item")
+    item_index = lax.axis_index("item")
     own_items = item_feat.shape[1]
     items = own_items * user_size
     experts_here = expert_w.shape[0]
@@ -284,27 +347,32 @@
     rows, half_width = users // ROW_CHUNKS, width // HALVES
 
     own_halves = own_queries(first_expert, own_cats, own_feat, expert_w)
-    order = user_index ^ jnp.arange(user_size, dtype=jnp.int32)
-    queries = [gather_parts(own, user_size) for own in own_halves]
+    order = gather_order(user_size)
     dense = dense_tiles(tile_place[0, 0], tile_count[0], tile_level[0, 0], users, items)
+    layers = [gather_layers(own, user_size) for own in own_halves]
+    layers[0], dense = lax.optimization_barrier((layers[0], dense))
+    queries = [gather_sides(part, user_size) for part in layers]
 
     local_cats = (own_cats - first_expert).astype(jnp.bfloat16)
     packed = jnp.concatenate(
         [own_feat, jnp.broadcast_to(local_cats[:, None], (own_items, TILE))], axis=1
     )
-    packed, _ = lax.optimization_barrier((packed, queries[-1][-1]))
-    packed = lax.all_gather(packed, "user", axis=0, tiled=True)
-    feats, all_cats = packed[:, :width], packed[:, width].astype(jnp.int32)
-
-    partials = [[None] * ROW_CHUNKS for _ in range(HALVES)]
+    packed, _ = lax.optimization_barrier((packed, queries[-1][1]))
+    packed = gather_sides(gather_layers(packed, user_size), user_size)
+    own_width = width // user_size
+    feats, mask = ordered_items(order, packed, experts_here, own_width, width)
+
+    partials = []
     for half in range(HALVES):
-        for chunk in range(ROW_CHUNKS):
-            partial = spread_items(order, queries[half], dense, chunk * rows, rows)
-            pieces = [partial]
-            for shift in range(1, item_size):
-                pairs = [(source, (source + shift) % item_size) for source in range(item_size)]
-                pieces.append(lax.ppermute(partial, "item", pairs))
-            partials[half][chunk] = pieces
+        first = [0, 1] if half == 0 else [0]
+        partials.append([])
+        for start, end in zip(first, first[1:] + [ROW_CHUNKS]):
+            for partial in spread_items(order, queries[half], dense, start, end - start, rows):
+                pieces = [partial]
+                for shift in range(1, item_size):
+                    pairs = [(source, (source + shift) % item_size) for source in range(item_size)]
+                    pieces.append(lax.ppermute(partial, "item", pairs))
+                partials[half].append(pieces)
 
     grads, gain_term, item_terms = [], 0.0, 0.0
     for chunk in range(ROW_CHUNKS):
@@ -325,7 +393,6 @@
                 (((0,), (0,)), ((), ())),
                 preferred_element_type=jnp.float32,
             )
-    own_width = width // user_size
     part_width = own_width // HALVES
     sums = []
     for half in range(HALVES):
@@ -347,8 +414,7 @@
     )
     gain_own = lax.dynamic_slice_in_dim(gain_term, item_index * col_width, col_width, 0)
 
-    chosen = all_cats[None, :] == jnp.arange(experts_here, dtype=jnp.int32)[:, None]
-    masked = jnp.where(chosen[:, None, :], sums[None], jnp.zeros_like(sums)[None])
+    masked = mask * sums[None]
     expert_cols = lax.dot_general(
         feats,
         masked.reshape(experts_here * own_width, items),

time: 165 us -> 145 us (0.88)
  waiting for transfers between devices: 35.1 us -> 53.2 us
  between operations: 15.4 us -> 1.96 us
  Pallas kernels: 37 us -> 25.6 us
  starting transfers between devices: 53.2 us -> 45.1 us
  local copies, waits for them, and re-layouts: 10.2 us -> 7.91 us
  other arithmetic: 4.42 us -> 2.44 us
    ppermute x8, waiting for transfers between devices: 6.35 us -> 22.4 us  [on_device(): pieces.append(lax.ppermute(partial, 'item', pairs))]
    ppermute x40 -> x25, starting transfers between devices: 41.1 us -> 32.1 us  [flip(): lax.ppermute(value, 'user', [(source, source ^ bits) for source in range(...]
    pallas_call x8 -> x4, Pallas kernels: 25.2 us -> 16.8 us  [the longest x3 12.3 us: spread_items(): pl.pallas_call(functools.partial(spread, blocks), out_shape=[jax.ShapeDty...]
    pallas_call x4, Pallas kernels: 5.92 us -> 2.97 us  [user_gradient(): pl.pallas_call(functools.partial(norm_backward, len(pieces[0])), out_shap...]
    unnamed x31 -> x32, local copies, waits for them, and re-layouts: 7.24 us -> 4.81 us
    ppermute x40 -> x25, waiting for transfers between devices: 19.3 us -> 21.5 us  [flip(): lax.ppermute(value, 'user', [(source, source ^ bits) for source in range(...]
  transfers between devices with their start and end apart: 50 -> 34, of which waited for: 16 -> 16; matrix products, arithmetic and copies ran while one was open for 5% -> 6% of each run, Pallas kernels for 20% -> 12%
where the time goes in v3:
time: 145 us
  waiting for transfers between devices  53.2 us (37%)
  starting transfers between devices  45.1 us (31%)
  Pallas kernels  25.6 us (18%)
  matrix products  8.3 us (6%)
  local copies, waits for them, and re-layouts  7.91 us (5%)
  other arithmetic  2.44 us (2%)
  between operations  1.96 us (1%)
    ppermute x25, starting transfers between devices, flip(): lax.ppermute(value, 'user', [(source, source ^ bits) for source in range(...  32.1 us
    ppermute x8, waiting for transfers between devices, on_device(): pieces.append(lax.ppermute(partial, 'item', pairs))  22.4 us
    ppermute x25, waiting for transfers between devices, flip(): lax.ppermute(value, 'user', [(source, source ^ bits) for source in range(...  21.5 us
    pallas_call x3, Pallas kernels, spread_items(): pl.pallas_call(functools.partial(spread, blocks), out_shape=[jax.ShapeDty...  12.3 us
    ppermute x8, starting transfers between devices, on_device(): pieces.append(lax.ppermute(partial, 'item', pairs))  9.46 us
    all_to_all x1, waiting for transfers between devices, on_device(): swapped = lax.all_to_all(jnp.concatenate(pieces, axis=1), 'user', 0, 0)  9.37 us
    unnamed x32, local copies, waits for them, and re-layouts  4.81 us
    pallas_call x1, Pallas kernels, ordered_items(): pl.pallas_call(functools.partial(order_items, blocks), out_shape=[jax.Sha...  4.51 us
  transfers between devices with their start and end apart: 34, of which 16 were waited for; matrix products, arithmetic and copies ran while one was open for 6% of the time, Pallas kernels for 12%

profile of v3, /device:TPU:0, one launch (start us, length us, event | category | flops | bytes accessed | tf_op | source)
XLA Modules:
  0.0 144.6 jit_solution(8827247413659028426)
XLA Ops:
  0.6 3.6 %own_queries.1 = (bf16[128,256]{1,0:T(8,128)(2,1)}, bf16[128,256]{1,0:T(8,128)(2,1)}) custom-call(s32[1]{0:T(128)} %bitcast.1.first_ref, s32[1,128]{1,0:T(1,128)} %cats_ref.1, bf16[128,512]{1,0:T(8,128)(2,1)} %bitcast.121, bf16[4,512,512]{2,1,0:T(8,128)(2,1)} %weight_ref.1), custom_call_target="tpu_custom_call" | custom-call | flops 268435456 | bytes 2359296 | tf_op jit(solution)/shard_map/own_queries/pallas_call | solution.py:97
  4.3 3.0 %collective-permute-start.6 = (bf16[128,256]{1,0:T(8,128)(2,1)}, bf16[128,256]{1,0:T(8,128)(2,1)S(1)}, u32[]{:S(2)}, u32[]{:S(2)}) collective-permute-start(bf16[128,256]{1,0:T(8,128)(2,1)} %get-tuple-element.29), channel_id=1, source_target_pairs={{0,8},{2,10},{4,12},{6,14},{8,0},{10,2},{12,4},{14,6},{16,24},{18,... | collective-permute-start | bytes 196616 | tf_op jit(solution)/shard_map/ppermute | solution.py:288
  7.3 2.6 %collective-permute-start.7 = (bf16[128,256]{1,0:T(8,128)(2,1)}, bf16[128,256]{1,0:T(8,128)(2,1)S(1)}, u32[]{:S(2)}, u32[]{:S(2)}) collective-permute-start(bf16[128,256]{1,0:T(8,128)(2,1)} %get-tuple-element.29), channel_id=1, source_target_pairs={{0,16},{2,18},{4,20},{6,22},{8,24},{10,26},{12,28},{14,30},{16,0},... | collective-permute-start | bytes 196616 | tf_op jit(solution)/shard_map/ppermute | solution.py:288
  9.9 0.9 collective-permute-start
  10.8 3.5 %collective-permute-start.1 = (bf16[128,256]{1,0:T(8,128)(2,1)}, bf16[128,256]{1,0:T(8,128)(2,1)S(1)}, u32[]{:S(2)}, u32[]{:S(2)}) collective-permute-start(bf16[128,256]{1,0:T(8,128)(2,1)} %get-tuple-element.26), channel_id=1, source_target_pairs={{0,16},{2,18},{4,20},{6,22},{8,24},{10,26},{12,28},{14,30},{16,0},... | collective-permute-start | bytes 196616 | tf_op jit(solution)/shard_map/ppermute | solution.py:288
  14.3 0.8 constant_dynamic-update-slice_fusion.6
  15.8 2.5 %copy-done.2 = s32[1,1,80,128,128]{4,3,2,1,0:T(8,128)S(1)} copy-done((s32[1,1,80,128,128]{4,3,2,1,0:T(8,128)S(1)}, s32[1,1,80,128,128]{4,3,2,1,0:T(8,128)}, u32[]{:S(2)}) %copy-start.2) | copy-done | bytes 5242904
  18.3 2.2 %place_tiles.1.dense_ref = bf16[2048,2048]{1,0:T(8,128)(2,1)S(1)} custom-call(s32[80]{0:T(128)S(1)} %bitcast.109, s32[1]{0:T(128)} %bitcast.103.count_ref, s32[80,128,128]{2,1,0:T(8,128)S(1)} %bitcast.104), custom_call_target="tpu_custom_call" | custom-call | flops 1310720 | bytes 13631488 | tf_op jit(solution)/shard_map/place_tiles/pallas_call | solution.py:40
  20.7 1.8 %collective-permute-start.9 = (bf16[512,256]{1,0:T(8,128)(2,1)S(1)}, bf16[512,256]{1,0:T(8,128)(2,1)S(1)}, u32[]{:S(2)}, u32[]{:S(2)}) collective-permute-start(bf16[512,256]{1,0:T(8,128)(2,1)S(1)} %pad_maximum_fusion.4), channel_id=1, source_target_pairs={{0,4},{2,6},{4,0},{6,2},{8,12},{10,14},{12,8},{14,10},{16,20},{18,... | collective-permute-start | bytes 786440 | tf_op jit(solution)/shard_map/ppermute | solution.py:288
  22.5 4.2 %collective-permute-done.2 = bf16[128,256]{1,0:T(8,128)(2,1)S(1)} collective-permute-done((bf16[128,256]{1,0:T(8,128)(2,1)S(1)}, bf16[128,256]{1,0:T(8,128)(2,1)S(1)}, u32[]{:S(2)}, u32[]{:S(2)}) %collective-permute-start.2) | collective-permute-done | bytes 65568 | tf_op jit(solution)/shard_map/ppermute | solution.py:288
  26.7 1.7 %collective-permute-start.3 = (bf16[512,256]{1,0:T(8,128)(2,1)S(1)}, bf16[512,256]{1,0:T(8,128)(2,1)S(1)}, u32[]{:S(2)}, u32[]{:S(2)}) collective-permute-start(bf16[512,256]{1,0:T(8,128)(2,1)S(1)} %pad_maximum_fusion.3), channel_id=1, source_target_pairs={{0,4},{2,6},{4,0},{6,2},{8,12},{10,14},{12,8},{14,10},{16,20},{18,... | collective-permute-start | bytes 786440 | tf_op jit(solution)/shard_map/ppermute | solution.py:288
  28.6 4.5 %collective-permute-done.3 = bf16[512,256]{1,0:T(8,128)(2,1)S(1)} collective-permute-done((bf16[512,256]{1,0:T(8,128)(2,1)S(1)}, bf16[512,256]{1,0:T(8,128)(2,1)S(1)}, u32[]{:S(2)}, u32[]{:S(2)}) %collective-permute-start.3) | collective-permute-done | bytes 262176 | tf_op jit(solution)/shard_map/ppermute | solution.py:288
  33.8 3.6 %collective-permute-start.29 = (bf16[128,640]{1,0:T(8,128)(2,1)S(1)}, bf16[128,640]{1,0:T(8,128)(2,1)S(1)}, u32[]{:S(2)}, u32[]{:S(2)}) collective-permute-start(bf16[128,640]{1,0:T(8,128)(2,1)S(1)} %pad_maximum_fusion.5), channel_id=1, source_target_pairs={{0,16},{2,18},{4,20},{6,22},{8,24},{10,26},{12,28},{14,30},{16,0},... | collective-permute-start | bytes 491528 | tf_op jit(solution)/shard_map/ppermute | solution.py:288
  37.9 5.1 %spread_items.4 = (bf16[512,256]{1,0:T(8,128)(2,1)S(1)}, bf16[512,256]{1,0:T(8,128)(2,1)S(1)}, bf16[512,256]{1,0:T(8,128)(2,1)S(1)}, bf16[512,256]{1,0:T(8,128)(2,1)S(1)}) custom-call(s32[16]{0:T(128)S(1)} %fusion.55.order_ref, bf16[1024,256]{1,0:T(8,128)(2,1)S(1)} %constant_dynamic-update-slice_fusion.2.same_ref, ...), custom_call_target="tpu_custom_call" | custom-call | flops 2147483648 | bytes 10485760 | tf_op jit(solution)/shard_map/spread_items/pallas_call | solution.py:157
  43.0 1.5 %collective-permute-start.11 = (bf16[512,256]{1,0:T(8,128)(2,1)S(1)}, bf16[512,256]{1,0:T(8,128)(2,1)S(1)}, u32[]{:S(2)}, u32[]{:S(2)}) collective-permute-start(bf16[512,256]{1,0:T(8,128)(2,1)S(1)} %get-tuple-element.30.rest_2_), channel_id=1, source_target_pairs={{0,1},{1,0},{2,3},{3,2},{4,5},{5,4},{6,7},{7,6},{8,9},{9,8},{10,11... | collective-permute-start | bytes 786440 | tf_op jit(solution)/shard_map/ppermute | solution.py:374
  44.6 2.8 %spread_items.3.rest_0_ = bf16[512,256]{1,0:T(8,128)(2,1)S(1)} custom-call(s32[16]{0:T(128)S(1)} %fusion.55.order_ref, bf16[1024,256]{1,0:T(8,128)(2,1)S(1)} %constant_dynamic-update-slice_fusion.same_ref, bf16[1024,256]{1,0:T(8,128)(2,1)S(1)} %collective-permute-done.4.other_ref, bf16[2048,2048]{1,0:T(8,128)(2,1)S(1)} %place_tiles.1.dense_ref), custom_call_target="tpu_custom_call" | custom-call | flops 536870912 | bytes 3407872 | tf_op jit(solution)/shard_map/spread_items/pallas_call | solution.py:157
  48.0 4.4 %spread_items.5 = (bf16[512,256]{1,0:T(8,128)(2,1)S(1)}, bf16[512,256]{1,0:T(8,128)(2,1)S(1)}, bf16[512,256]{1,0:T(8,128)(2,1)S(1)}) custom-call(s32[16]{0:T(128)S(1)} %fusion.55.order_ref, bf16[1024,256]{1,0:T(8,128)(2,1)S(1)} %constant_dynamic-update-slice_fusion.same_ref, bf16[1024,256]{1,0:T(8,128)(2,1)S(1)} %collective-permute-done.4.other_ref, ...), custom_call_target="tpu_custom_call" | custom-call | flops 1610612736 | bytes 8126464 | tf_op jit(solution)/shard_map/spread_items/pallas_call | solution.py:157
  52.5 1.5 %collective-permute-start.13 = (bf16[512,256]{1,0:T(8,128)(2,1)S(1)}, bf16[512,256]{1,0:T(8,128)(2,1)S(1)}, u32[]{:S(2)}, u32[]{:S(2)}) collective-permute-start(bf16[512,256]{1,0:T(8,128)(2,1)S(1)} %get-tuple-element.33.rest_2_), channel_id=1, source_target_pairs={{0,1},{1,0},{2,3},{3,2},{4,5},{5,4},{6,7},{7,6},{8,9},{9,8},{10,11... | collective-permute-start | bytes 786440 | tf_op jit(solution)/shard_map/ppermute | solution.py:374
  54.7 1.5 %collective-permute-start.15 = (bf16[512,256]{1,0:T(8,128)(2,1)S(1)}, bf16[512,256]{1,0:T(8,128)(2,1)S(1)}, u32[]{:S(2)}, u32[]{:S(2)}) collective-permute-start(bf16[512,256]{1,0:T(8,128)(2,1)S(1)} %get-tuple-element.36.rest_2_), channel_id=1, source_target_pairs={{0,1},{1,0},{2,3},{3,2},{4,5},{5,4},{6,7},{7,6},{8,9},{9,8},{10,11... | collective-permute-start | bytes 786440 | tf_op jit(solution)/shard_map/ppermute | solution.py:374
  57.0 1.0 collective-permute-done.5.rest_1_
  57.9 1.5 %collective-permute-start.17 = (bf16[512,256]{1,0:T(8,128)(2,1)S(1)}, bf16[512,256]{1,0:T(8,128)(2,1)S(1)}, u32[]{:S(2)}, u32[]{:S(2)}) collective-permute-start(bf16[512,256]{1,0:T(8,128)(2,1)S(1)} %get-tuple-element.39.rest_2_), channel_id=1, source_target_pairs={{0,1},{1,0},{2,3},{3,2},{4,5},{5,4},{6,7},{7,6},{8,9},{9,8},{10,11... | collective-permute-start | bytes 786440 | tf_op jit(solution)/shard_map/ppermute | solution.py:374
  60.1 1.3 fusion.6
  61.4 2.1 %collective-permute-done.13.rest_3_ = bf16[512,256]{1,0:T(8,128)(2,1)S(1)} collective-permute-done((bf16[512,256]{1,0:T(8,128)(2,1)S(1)}, bf16[512,256]{1,0:T(8,128)(2,1)S(1)}, u32[]{:S(2)}, u32[]{:S(2)}) %collective-permute-start.13) | collective-permute-done | bytes 262176 | tf_op jit(solution)/shard_map/ppermute | solution.py:374
  63.5 1.5 %collective-permute-start.16 = (bf16[512,256]{1,0:T(8,128)(2,1)S(1)}, bf16[512,256]{1,0:T(8,128)(2,1)S(1)}, u32[]{:S(2)}, u32[]{:S(2)}) collective-permute-start(bf16[512,256]{1,0:T(8,128)(2,1)S(1)} %get-tuple-element.38.rest_0_), channel_id=1, source_target_pairs={{0,1},{1,0},{2,3},{3,2},{4,5},{5,4},{6,7},{7,6},{8,9},{9,8},{10,11... | collective-permute-start | bytes 786440 | tf_op jit(solution)/shard_map/ppermute | solution.py:374
  65.0 4.1 %collective-permute-done.12.rest_1_ = bf16[512,256]{1,0:T(8,128)(2,1)S(1)} collective-permute-done((bf16[512,256]{1,0:T(8,128)(2,1)S(1)}, bf16[512,256]{1,0:T(8,128)(2,1)S(1)}, u32[]{:S(2)}, u32[]{:S(2)}) %collective-permute-start.12) | collective-permute-done | bytes 262176 | tf_op jit(solution)/shard_map/ppermute | solution.py:374
  69.2 1.7 %collective-permute-start.31 = (bf16[512,640]{1,0:T(8,128)(2,1)S(1)}, bf16[512,640]{1,0:T(8,128)(2,1)S(1)}, u32[]{:S(2)}, u32[]{:S(2)}) collective-permute-start(bf16[512,640]{1,0:T(8,128)(2,1)S(1)} %pad_maximum_fusion.1), channel_id=1, source_target_pairs={{0,4},{2,6},{4,0},{6,2},{8,12},{10,14},{12,8},{14,10},{16,20},{18,... | collective-permute-start | bytes 1966088 | tf_op jit(solution)/shard_map/ppermute | solution.py:288
  71.5 1.3 fusion.4
  72.8 2.0 %collective-permute-done.15.rest_3_ = bf16[512,256]{1,0:T(8,128)(2,1)S(1)} collective-permute-done((bf16[512,256]{1,0:T(8,128)(2,1)S(1)}, bf16[512,256]{1,0:T(8,128)(2,1)S(1)}, u32[]{:S(2)}, u32[]{:S(2)}) %collective-permute-start.15) | collective-permute-done | bytes 262176 | tf_op jit(solution)/shard_map/ppermute | solution.py:374
  74.8 5.6 %collective-permute-done.14.rest_1_ = bf16[512,256]{1,0:T(8,128)(2,1)S(1)} collective-permute-done((bf16[512,256]{1,0:T(8,128)(2,1)S(1)}, bf16[512,256]{1,0:T(8,128)(2,1)S(1)}, u32[]{:S(2)}, u32[]{:S(2)}) %collective-permute-start.14) | collective-permute-done | bytes 262176 | tf_op jit(solution)/shard_map/ppermute | solution.py:374
  81.1 1.6 %add_add_fusion = f32[512,2048]{1,0:T(8,128)S(1)} fusion(f32[512,2048]{1,0:T(8,128)S(1)} %fusion.6, f32[512,2048]{1,0:T(8,128)S(1)} %fusion.4, bf16[512,512]{1,0:T(8,128)(2,1)S(1)} %get-tuple-element.37, bf16[2048,2048]{1,0:T(8,128)(2,1)S(1)} %place_tiles.1.dense_ref), kind=kOutput, calls=%fused_computation | convolution fusion | flops 1075838976 | bytes 15204352 | tf_op jit(solution)/shard_map/dot_general | solution.py:390
  82.7 3.4 %collective-permute-done.17.rest_3_ = bf16[512,256]{1,0:T(8,128)(2,1)S(1)} collective-permute-done((bf16[512,256]{1,0:T(8,128)(2,1)S(1)}, bf16[512,256]{1,0:T(8,128)(2,1)S(1)}, u32[]{:S(2)}, u32[]{:S(2)}) %collective-permute-start.17) | collective-permute-done | bytes 262176 | tf_op jit(solution)/shard_map/ppermute | solution.py:374
  86.0 4.3 %collective-permute-done.16.rest_1_ = bf16[512,256]{1,0:T(8,128)(2,1)S(1)} collective-permute-done((bf16[512,256]{1,0:T(8,128)(2,1)S(1)}, bf16[512,256]{1,0:T(8,128)(2,1)S(1)}, u32[]{:S(2)}, u32[]{:S(2)}) %collective-permute-start.16) | collective-permute-done | bytes 262176 | tf_op jit(solution)/shard_map/ppermute | solution.py:374
  90.3 0.9 user_gradient.7
  94.1 1.7 %collective-permute-start.19 = (bf16[4,16,2048]{2,1,0:T(8,128)(2,1)S(1)}, bf16[4,16,2048]{2,1,0:T(8,128)(2,1)S(1)}, u32[]{:S(2)}, u32[]{:S(2)}) collective-permute-start(bf16[4,16,2048]{2,1,0:T(8,128)(2,1)S(1)} %fusion.31), channel_id=1, source_target_pairs={{0,4},{2,6},{4,0},{6,2},{8,12},{10,14},{12,8},{14,10},{16,20},{18,... | collective-permute-start | bytes 786440 | tf_op jit(solution)/shard_map/ppermute | solution.py:288
  96.0 0.9 collective-permute-start.24
  97.1 6.2 %collective-permute-done.19 = bf16[4,16,2048]{2,1,0:T(8,128)(2,1)S(1)} collective-permute-done((bf16[4,16,2048]{2,1,0:T(8,128)(2,1)S(1)}, bf16[4,16,2048]{2,1,0:T(8,128)(2,1)S(1)}, u32[]{:S(2)}, u32[]{:S(2)}) %collective-permute-start.19) | collective-permute-done | bytes 262176 | tf_op jit(solution)/shard_map/ppermute | solution.py:288
  103.9 3.5 %collective-permute-start.21 = (bf16[16,2048]{1,0:T(8,128)(2,1)S(1)}, bf16[16,2048]{1,0:T(8,128)(2,1)S(1)}, u32[]{:S(2)}, u32[]{:S(2)}) collective-permute-start(bf16[16,2048]{1,0:T(8,128)(2,1)S(1)} %get-tuple-element.66), channel_id=1, source_target_pairs={{0,16},{2,18},{4,20},{6,22},{8,24},{10,26},{12,28},{14,30},{16,0},... | collective-permute-start | bytes 196616 | tf_op jit(solution)/shard_map/ppermute | solution.py:288
  108.7 3.5 %collective-permute-start.26 = (bf16[16,2048]{1,0:T(8,128)(2,1)S(1)}, bf16[16,2048]{1,0:T(8,128)(2,1)S(1)}, u32[]{:S(2)}, u32[]{:S(2)}) collective-permute-start(bf16[16,2048]{1,0:T(8,128)(2,1)S(1)} %get-tuple-element.69), channel_id=1, source_target_pairs={{0,16},{2,18},{4,20},{6,22},{8,24},{10,26},{12,28},{14,30},{16,0},... | collective-permute-start | bytes 196616 | tf_op jit(solution)/shard_map/ppermute | solution.py:288
  112.7 1.4 collective-permute-done.22
  114.1 2.8 %collective-permute-done.26 = bf16[16,2048]{1,0:T(8,128)(2,1)S(1)} collective-permute-done((bf16[16,2048]{1,0:T(8,128)(2,1)S(1)}, bf16[16,2048]{1,0:T(8,128)(2,1)S(1)}, u32[]{:S(2)}, u32[]{:S(2)}) %collective-permute-start.26) | collective-permute-done | bytes 65568 | tf_op jit(solution)/shard_map/ppermute | solution.py:288
  117.0 1.5 %collective-permute-done.27 = bf16[16,2048]{1,0:T(8,128)(2,1)S(1)} collective-permute-done((bf16[16,2048]{1,0:T(8,128)(2,1)S(1)}, bf16[16,2048]{1,0:T(8,128)(2,1)S(1)}, u32[]{:S(2)}, u32[]{:S(2)}) %collective-permute-start.27) | collective-permute-done | bytes 65568 | tf_op jit(solution)/shard_map/ppermute | solution.py:288
  118.6 4.5 %order_items.1 = (bf16[2048,512]{1,0:T(8,128)(2,1)S(1)}, bf16[4,32,2048]{2,1,0:T(8,128)(2,1)S(1)}) custom-call(s32[16]{0:T(128)S(1)} %fusion.55.order_ref, bf16[1024,640]{1,0:T(8,128)(2,1)S(1)} %constant_dynamic-update-slice_fusion.7.same_ref, bf16[1024,640]{1,0:T(8,128)(2,1)S(1)} %collective-permute-done.32.other_ref), custom_call_target="tpu_custom_call" | custom-call | bytes 6291456 | tf_op jit(solution)/shard_map/order_items/pallas_call | solution.py:199
  124.8 3.5 %all-to-all-start = ((bf16[16,66,128]{2,1,0:T(8,128)(2,1)}), bf16[16,66,128]{2,1,0:T(8,128)(2,1)S(1)}, u32[]{:S(2)}, u32[]{:S(2)}) async-start(bf16[16,66,128]{2,1,0:T(8,128)(2,1)} %copy.51), calls=%async_computation | async-start | bytes 589824 | tf_op jit(solution)/shard_map/all_to_all | solution.py:431
  128.5 1.0 pad_maximum_fusion
  129.5 9.4 %all-to-all-done = bf16[16,66,128]{2,1,0:T(8,128)(2,1)S(1)} async-done(((bf16[16,66,128]{2,1,0:T(8,128)(2,1)}), bf16[16,66,128]{2,1,0:T(8,128)(2,1)S(1)}, u32[]{:S(2)}, u32[]{:S(2)}) %all-to-all-start) | async-done | bytes 270368 | tf_op jit(solution)/shard_map/all_to_all | solution.py:431
  140.1 1.0 copy.55
  141.1 0.9 copy.52
  143.0 1.0 fusion.20
  (110 shorter events, 15.7 us)
Async XLA Ops:
  0.6 15.2 %copy-start.4 = (s32[1,1,80]{2,1,0:T(1,128)S(1)}, s32[1,1,80]{2,1,0:T(1,128)}, u32[]{:S(2)}) copy-start(s32[1,1,80]{2,1,0:T(1,128)} %param.15) | copy-start | bytes 964
  4.3 16.3 %collective-permute-start.6 = (bf16[128,256]{1,0:T(8,128)(2,1)}, bf16[128,256]{1,0:T(8,128)(2,1)S(1)}, u32[]{:S(2)}, u32[]{:S(2)}) collective-permute-start(bf16[128,256]{1,0:T(8,128)(2,1)} %get-tuple-element.29), channel_id=1, source_target_pairs={{0,8},{2,10},{4,12},{6,14},{8,0},{10,2},{12,4},{14,6},{16,24},{18,... | collective-permute-start | bytes 196616 | tf_op jit(solution)/shard_map/ppermute | solution.py:288
  7.3 13.3 %collective-permute-start.7 = (bf16[128,256]{1,0:T(8,128)(2,1)}, bf16[128,256]{1,0:T(8,128)(2,1)S(1)}, u32[]{:S(2)}, u32[]{:S(2)}) collective-permute-start(bf16[128,256]{1,0:T(8,128)(2,1)} %get-tuple-element.29), channel_id=1, source_target_pairs={{0,16},{2,18},{4,20},{6,22},{8,24},{10,26},{12,28},{14,30},{16,0},... | collective-permute-start | bytes 196616 | tf_op jit(solution)/shard_map/ppermute | solution.py:288
  9.9 10.8 %collective-permute-start.8 = (bf16[128,256]{1,0:T(8,128)(2,1)}, bf16[128,256]{1,0:T(8,128)(2,1)S(1)}, u32[]{:S(2)}, u32[]{:S(2)}) collective-permute-start(bf16[128,256]{1,0:T(8,128)(2,1)} %get-tuple-element.29), channel_id=1, source_target_pairs={{0,24},{2,26},{4,28},{6,30},{8,16},{10,18},{12,20},{14,22},{16,8},... | collective-permute-start | bytes 196616 | tf_op jit(solution)/shard_map/ppermute | solution.py:288
  9.9 12.6 %collective-permute-start = (bf16[128,256]{1,0:T(8,128)(2,1)}, bf16[128,256]{1,0:T(8,128)(2,1)S(1)}, u32[]{:S(2)}, u32[]{:S(2)}) collective-permute-start(bf16[128,256]{1,0:T(8,128)(2,1)} %get-tuple-element.26), channel_id=1, source_target_pairs={{0,8},{2,10},{4,12},{6,14},{8,0},{10,2},{12,4},{14,6},{16,24},{18,... | collective-permute-start | bytes 196616 | tf_op jit(solution)/shard_map/ppermute | solution.py:288
  10.8 11.7 %collective-permute-start.1 = (bf16[128,256]{1,0:T(8,128)(2,1)}, bf16[128,256]{1,0:T(8,128)(2,1)S(1)}, u32[]{:S(2)}, u32[]{:S(2)}) collective-permute-start(bf16[128,256]{1,0:T(8,128)(2,1)} %get-tuple-element.26), channel_id=1, source_target_pairs={{0,16},{2,18},{4,20},{6,22},{8,24},{10,26},{12,28},{14,30},{16,0},... | collective-permute-start | bytes 196616 | tf_op jit(solution)/shard_map/ppermute | solution.py:288
  15.8 2.5 %copy-start.2 = (s32[1,1,80,128,128]{4,3,2,1,0:T(8,128)S(1)}, s32[1,1,80,128,128]{4,3,2,1,0:T(8,128)}, u32[]{:S(2)}) copy-start(s32[1,1,80,128,128]{4,3,2,1,0:T(8,128)} %param.16) | copy-start | bytes 15728644
  18.3 2.3 %copy-start.8 = (bf16[128,256]{1,0:T(8,128)(2,1)S(1)}, bf16[128,256]{1,0:T(8,128)(2,1)}, u32[]{:S(2)}) copy-start(bf16[128,256]{1,0:T(8,128)(2,1)} %get-tuple-element.26) | copy-start | bytes 196612
  18.3 2.4 %copy-start.7 = (bf16[128,256]{1,0:T(8,128)(2,1)S(1)}, bf16[128,256]{1,0:T(8,128)(2,1)}, u32[]{:S(2)}) copy-start(bf16[128,256]{1,0:T(8,128)(2,1)} %get-tuple-element.29) | copy-start | bytes 196612
  20.5 12.8 %copy-start.9 = (s32[1,128]{1,0:T(1,128)S(1)}, s32[1,128]{1,0:T(1,128)}, u32[]{:S(2)}) copy-start(s32[1,128]{1,0:T(1,128)} %cats_ref.1) | copy-start | bytes 1540
  20.5 12.8 %copy-start.6 = (bf16[1,128,512]{2,1,0:T(8,128)(2,1)S(1)}, bf16[1,128,512]{2,1,0:T(8,128)(2,1)}, u32[]{:S(2)}) copy-start(bf16[1,128,512]{2,1,0:T(8,128)(2,1)} %param.12) | copy-start | bytes 393220
  20.6 6.1 %collective-permute-start.2 = (bf16[128,256]{1,0:T(8,128)(2,1)S(1)}, bf16[128,256]{1,0:T(8,128)(2,1)S(1)}, u32[]{:S(2)}, u32[]{:S(2)}) collective-permute-start(bf16[128,256]{1,0:T(8,128)(2,1)S(1)} %copy-done.8), channel_id=1, source_target_pairs={{0,24},{2,26},{4,28},{6,30},{8,16},{10,18},{12,20},{14,22},{16,8},... | collective-permute-start | bytes 196616 | tf_op jit(solution)/shard_map/ppermute | solution.py:288
  20.7 7.8 %collective-permute-start.9 = (bf16[512,256]{1,0:T(8,128)(2,1)S(1)}, bf16[512,256]{1,0:T(8,128)(2,1)S(1)}, u32[]{:S(2)}, u32[]{:S(2)}) collective-permute-start(bf16[512,256]{1,0:T(8,128)(2,1)S(1)} %pad_maximum_fusion.4), channel_id=1, source_target_pairs={{0,4},{2,6},{4,0},{6,2},{8,12},{10,14},{12,8},{14,10},{16,20},{18,... | collective-permute-start | bytes 786440 | tf_op jit(solution)/shard_map/ppermute | solution.py:288
  26.7 6.4 %collective-permute-start.3 = (bf16[512,256]{1,0:T(8,128)(2,1)S(1)}, bf16[512,256]{1,0:T(8,128)(2,1)S(1)}, u32[]{:S(2)}, u32[]{:S(2)}) collective-permute-start(bf16[512,256]{1,0:T(8,128)(2,1)S(1)} %pad_maximum_fusion.3), channel_id=1, source_target_pairs={{0,4},{2,6},{4,0},{6,2},{8,12},{10,14},{12,8},{14,10},{16,20},{18,... | collective-permute-start | bytes 786440 | tf_op jit(solution)/shard_map/ppermute | solution.py:288
  28.5 4.9 %collective-permute-start.10 = (bf16[1024,256]{1,0:T(8,128)(2,1)S(1)}, bf16[1024,256]{1,0:T(8,128)(2,1)S(1)}, u32[]{:S(2)}, u32[]{:S(2)}) collective-permute-start(bf16[1024,256]{1,0:T(8,128)(2,1)S(1)} %constant_dynamic-update-slice_fusion.2.same_ref), channel_id=1, source_target_pairs={{0,2},{2,0},{4,6},{6,4},{8,10},{10,8},{12,14},{14,12},{16,18},{18,... | collective-permute-start | bytes 1572872 | tf_op jit(solution)/shard_map/ppermute | solution.py:288
  33.2 11.4 %collective-permute-start.4 = (bf16[1024,256]{1,0:T(8,128)(2,1)S(1)}, bf16[1024,256]{1,0:T(8,128)(2,1)S(1)}, u32[]{:S(2)}, u32[]{:S(2)}) collective-permute-start(bf16[1024,256]{1,0:T(8,128)(2,1)S(1)} %constant_dynamic-update-slice_fusion.same_ref), channel_id=1, source_target_pairs={{0,2},{2,0},{4,6},{6,4},{8,10},{10,8},{12,14},{14,12},{16,18},{18,... | collective-permute-start | bytes 1572872 | tf_op jit(solution)/shard_map/ppermute | solution.py:288
  33.4 19.0 %collective-permute-start.28 = (bf16[128,640]{1,0:T(8,128)(2,1)S(1)}, bf16[128,640]{1,0:T(8,128)(2,1)S(1)}, u32[]{:S(2)}, u32[]{:S(2)}) collective-permute-start(bf16[128,640]{1,0:T(8,128)(2,1)S(1)} %pad_maximum_fusion.5), channel_id=1, source_target_pairs={{0,8},{2,10},{4,12},{6,14},{8,0},{10,2},{12,4},{14,6},{16,24},{18,... | collective-permute-start | bytes 491528 | tf_op jit(solution)/shard_map/ppermute | solution.py:288
  33.8 20.2 %collective-permute-start.29 = (bf16[128,640]{1,0:T(8,128)(2,1)S(1)}, bf16[128,640]{1,0:T(8,128)(2,1)S(1)}, u32[]{:S(2)}, u32[]{:S(2)}) collective-permute-start(bf16[128,640]{1,0:T(8,128)(2,1)S(1)} %pad_maximum_fusion.5), channel_id=1, source_target_pairs={{0,16},{2,18},{4,20},{6,22},{8,24},{10,26},{12,28},{14,30},{16,0},... | collective-permute-start | bytes 491528 | tf_op jit(solution)/shard_map/ppermute | solution.py:288
  37.5 17.2 %collective-permute-start.30 = (bf16[128,640]{1,0:T(8,128)(2,1)S(1)}, bf16[128,640]{1,0:T(8,128)(2,1)S(1)}, u32[]{:S(2)}, u32[]{:S(2)}) collective-permute-start(bf16[128,640]{1,0:T(8,128)(2,1)S(1)} %pad_maximum_fusion.5), channel_id=1, source_target_pairs={{0,24},{2,26},{4,28},{6,30},{8,16},{10,18},{12,20},{14,22},{16,8},... | collective-permute-start | bytes 491528 | tf_op jit(solution)/shard_map/ppermute | solution.py:288
  43.0 13.3 %collective-permute-start.11 = (bf16[512,256]{1,0:T(8,128)(2,1)S(1)}, bf16[512,256]{1,0:T(8,128)(2,1)S(1)}, u32[]{:S(2)}, u32[]{:S(2)}) collective-permute-start(bf16[512,256]{1,0:T(8,128)(2,1)S(1)} %get-tuple-element.30.rest_2_), channel_id=1, source_target_pairs={{0,1},{1,0},{2,3},{3,2},{4,5},{5,4},{6,7},{7,6},{8,9},{9,8},{10,11... | collective-permute-start | bytes 786440 | tf_op jit(solution)/shard_map/ppermute | solution.py:374
  47.4 10.5 %collective-permute-start.5 = (bf16[512,256]{1,0:T(8,128)(2,1)S(1)}, bf16[512,256]{1,0:T(8,128)(2,1)S(1)}, u32[]{:S(2)}, u32[]{:S(2)}) collective-permute-start(bf16[512,256]{1,0:T(8,128)(2,1)S(1)} %spread_items.3.rest_0_), channel_id=1, source_target_pairs={{0,1},{1,0},{2,3},{3,2},{4,5},{5,4},{6,7},{7,6},{8,9},{9,8},{10,11... | collective-permute-start | bytes 786440 | tf_op jit(solution)/shard_map/ppermute | solution.py:374
  48.0 11.4 %copy-start.1 = (bf16[2048,512]{1,0:T(8,128)(2,1)S(1)}, bf16[2048,512]{1,0:T(8,128)(2,1)}, u32[]{:S(2)}) copy-start(bf16[2048,512]{1,0:T(8,128)(2,1)} %grad_ref.7) | copy-start | bytes 6291460
  52.4 7.0 %copy-start = (bf16[2048,512]{1,0:T(8,128)(2,1)S(1)}, bf16[2048,512]{1,0:T(8,128)(2,1)}, u32[]{:S(2)}) copy-start(bf16[2048,512]{1,0:T(8,128)(2,1)} %user_ref.7) | copy-start | bytes 6291460
  52.4 7.0 %copy-start.3 = (f32[512]{0:T(512)S(1)}, f32[512]{0:T(512)}, u32[]{:S(2)}) copy-start(f32[512]{0:T(512)} %param.11) | copy-start | bytes 6148
  52.5 11.1 %collective-permute-start.13 = (bf16[512,256]{1,0:T(8,128)(2,1)S(1)}, bf16[512,256]{1,0:T(8,128)(2,1)S(1)}, u32[]{:S(2)}, u32[]{:S(2)}) collective-permute-start(bf16[512,256]{1,0:T(8,128)(2,1)S(1)} %get-tuple-element.33.rest_2_), channel_id=1, source_target_pairs={{0,1},{1,0},{2,3},{3,2},{4,5},{5,4},{6,7},{7,6},{8,9},{9,8},{10,11... | collective-permute-start | bytes 786440 | tf_op jit(solution)/shard_map/ppermute | solution.py:374
  54.0 15.1 %collective-permute-start.12 = (bf16[512,256]{1,0:T(8,128)(2,1)S(1)}, bf16[512,256]{1,0:T(8,128)(2,1)S(1)}, u32[]{:S(2)}, u32[]{:S(2)}) collective-permute-start(bf16[512,256]{1,0:T(8,128)(2,1)S(1)} %get-tuple-element.32.rest_0_), channel_id=1, source_target_pairs={{0,1},{1,0},{2,3},{3,2},{4,5},{5,4},{6,7},{7,6},{8,9},{9,8},{10,11... | collective-permute-start | bytes 786440 | tf_op jit(solution)/shard_map/ppermute | solution.py:374
  54.7 20.1 %collective-permute-start.15 = (bf16[512,256]{1,0:T(8,128)(2,1)S(1)}, bf16[512,256]{1,0:T(8,128)(2,1)S(1)}, u32[]{:S(2)}, u32[]{:S(2)}) collective-permute-start(bf16[512,256]{1,0:T(8,128)(2,1)S(1)} %get-tuple-element.36.rest_2_), channel_id=1, source_target_pairs={{0,1},{1,0},{2,3},{3,2},{4,5},{5,4},{6,7},{7,6},{8,9},{9,8},{10,11... | collective-permute-start | bytes 786440 | tf_op jit(solution)/shard_map/ppermute | solution.py:374
  56.3 24.1 %collective-permute-start.14 = (bf16[512,256]{1,0:T(8,128)(2,1)S(1)}, bf16[512,256]{1,0:T(8,128)(2,1)S(1)}, u32[]{:S(2)}, u32[]{:S(2)}) collective-permute-start(bf16[512,256]{1,0:T(8,128)(2,1)S(1)} %get-tuple-element.35.rest_0_), channel_id=1, source_target_pairs={{0,1},{1,0},{2,3},{3,2},{4,5},{5,4},{6,7},{7,6},{8,9},{9,8},{10,11... | collective-permute-start | bytes 786440 | tf_op jit(solution)/shard_map/ppermute | solution.py:374
  57.9 28.1 %collective-permute-start.17 = (bf16[512,256]{1,0:T(8,128)(2,1)S(1)}, bf16[512,256]{1,0:T(8,128)(2,1)S(1)}, u32[]{:S(2)}, u32[]{:S(2)}) collective-permute-start(bf16[512,256]{1,0:T(8,128)(2,1)S(1)} %get-tuple-element.39.rest_2_), channel_id=1, source_target_pairs={{0,1},{1,0},{2,3},{3,2},{4,5},{5,4},{6,7},{7,6},{8,9},{9,8},{10,11... | collective-permute-start | bytes 786440 | tf_op jit(solution)/shard_map/ppermute | solution.py:374
  63.5 26.7 %collective-permute-start.16 = (bf16[512,256]{1,0:T(8,128)(2,1)S(1)}, bf16[512,256]{1,0:T(8,128)(2,1)S(1)}, u32[]{:S(2)}, u32[]{:S(2)}) collective-permute-start(bf16[512,256]{1,0:T(8,128)(2,1)S(1)} %get-tuple-element.38.rest_0_), channel_id=1, source_target_pairs={{0,1},{1,0},{2,3},{3,2},{4,5},{5,4},{6,7},{7,6},{8,9},{9,8},{10,11... | collective-permute-start | bytes 786440 | tf_op jit(solution)/shard_map/ppermute | solution.py:374
  69.2 27.7 %collective-permute-start.31 = (bf16[512,640]{1,0:T(8,128)(2,1)S(1)}, bf16[512,640]{1,0:T(8,128)(2,1)S(1)}, u32[]{:S(2)}, u32[]{:S(2)}) collective-permute-start(bf16[512,640]{1,0:T(8,128)(2,1)S(1)} %pad_maximum_fusion.1), channel_id=1, source_target_pairs={{0,4},{2,6},{4,0},{6,2},{8,12},{10,14},{12,8},{14,10},{16,20},{18,... | collective-permute-start | bytes 1966088 | tf_op jit(solution)/shard_map/ppermute | solution.py:288
  92.0 2.0 %collective-permute-start.18 = (bf16[4,2,16,2048]{3,2,0,1:T(8,128)(2,1)S(1)}, bf16[4,2,16,2048]{3,2,0,1:T(8,128)(2,1)S(1)}, u32[]{:S(2)}, u32[]{:S(2)}) collective-permute-start(bf16[4,2,16,2048]{3,2,0,1:T(8,128)(2,1)S(1)} %fusion.21), channel_id=1, source_target_pairs={{0,2},{2,0},{4,6},{6,4},{8,10},{10,8},{12,14},{14,12},{16,18},{18,... | collective-permute-start | bytes 1572872 | tf_op jit(solution)/shard_map/ppermute | solution.py:288
  92.9 3.0 %collective-permute-start.23 = (bf16[4,2,16,2048]{3,2,0,1:T(8,128)(2,1)S(1)}, bf16[4,2,16,2048]{3,2,0,1:T(8,128)(2,1)S(1)}, u32[]{:S(2)}, u32[]{:S(2)}) collective-permute-start(bf16[4,2,16,2048]{3,2,0,1:T(8,128)(2,1)S(1)} %fusion.22), channel_id=1, source_target_pairs={{0,2},{2,0},{4,6},{6,4},{8,10},{10,8},{12,14},{14,12},{16,18},{18,... | collective-permute-start | bytes 1572872 | tf_op jit(solution)/shard_map/ppermute | solution.py:288
  94.1 9.2 %collective-permute-start.19 = (bf16[4,16,2048]{2,1,0:T(8,128)(2,1)S(1)}, bf16[4,16,2048]{2,1,0:T(8,128)(2,1)S(1)}, u32[]{:S(2)}, u32[]{:S(2)}) collective-permute-start(bf16[4,16,2048]{2,1,0:T(8,128)(2,1)S(1)} %fusion.31), channel_id=1, source_target_pairs={{0,4},{2,6},{4,0},{6,2},{8,12},{10,14},{12,8},{14,10},{16,20},{18,... | collective-permute-start | bytes 786440 | tf_op jit(solution)/shard_map/ppermute | solution.py:288
  96.0 12.1 %collective-permute-start.24 = (bf16[4,16,2048]{2,1,0:T(8,128)(2,1)S(1)}, bf16[4,16,2048]{2,1,0:T(8,128)(2,1)S(1)}, u32[]{:S(2)}, u32[]{:S(2)}) collective-permute-start(bf16[4,16,2048]{2,1,0:T(8,128)(2,1)S(1)} %fusion.32), channel_id=1, source_target_pairs={{0,4},{2,6},{4,0},{6,2},{8,12},{10,14},{12,8},{14,10},{16,20},{18,... | collective-permute-start | bytes 786440 | tf_op jit(solution)/shard_map/ppermute | solution.py:288
  97.0 21.6 %collective-permute-start.32 = (bf16[1024,640]{1,0:T(8,128)(2,1)S(1)}, bf16[1024,640]{1,0:T(8,128)(2,1)S(1)}, u32[]{:S(2)}, u32[]{:S(2)}) collective-permute-start(bf16[1024,640]{1,0:T(8,128)(2,1)S(1)} %constant_dynamic-update-slice_fusion.7.same_ref), channel_id=1, source_target_pairs={{0,2},{2,0},{4,6},{6,4},{8,10},{10,8},{12,14},{14,12},{16,18},{18,... | collective-permute-start | bytes 3932168 | tf_op jit(solution)/shard_map/ppermute | solution.py:288
  103.4 5.3 %collective-permute-start.20 = (bf16[16,2048]{1,0:T(8,128)(2,1)S(1)}, bf16[16,2048]{1,0:T(8,128)(2,1)S(1)}, u32[]{:S(2)}, u32[]{:S(2)}) collective-permute-start(bf16[16,2048]{1,0:T(8,128)(2,1)S(1)} %get-tuple-element.64), channel_id=1, source_target_pairs={{0,8},{2,10},{4,12},{6,14},{8,0},{10,2},{12,4},{14,6},{16,24},{18,... | collective-permute-start | bytes 196616 | tf_op jit(solution)/shard_map/ppermute | solution.py:288
  103.9 8.4 %collective-permute-start.21 = (bf16[16,2048]{1,0:T(8,128)(2,1)S(1)}, bf16[16,2048]{1,0:T(8,128)(2,1)S(1)}, u32[]{:S(2)}, u32[]{:S(2)}) collective-permute-start(bf16[16,2048]{1,0:T(8,128)(2,1)S(1)} %get-tuple-element.66), channel_id=1, source_target_pairs={{0,16},{2,18},{4,20},{6,22},{8,24},{10,26},{12,28},{14,30},{16,0},... | collective-permute-start | bytes 196616 | tf_op jit(solution)/shard_map/ppermute | solution.py:288
  107.5 6.6 %collective-permute-start.22 = (bf16[16,2048]{1,0:T(8,128)(2,1)S(1)}, bf16[16,2048]{1,0:T(8,128)(2,1)S(1)}, u32[]{:S(2)}, u32[]{:S(2)}) collective-permute-start(bf16[16,2048]{1,0:T(8,128)(2,1)S(1)} %get-tuple-element.65), channel_id=1, source_target_pairs={{0,24},{2,26},{4,28},{6,30},{8,16},{10,18},{12,20},{14,22},{16,8},... | collective-permute-start | bytes 196616 | tf_op jit(solution)/shard_map/ppermute | solution.py:288
  108.2 5.9 %collective-permute-start.25 = (bf16[16,2048]{1,0:T(8,128)(2,1)S(1)}, bf16[16,2048]{1,0:T(8,128)(2,1)S(1)}, u32[]{:S(2)}, u32[]{:S(2)}) collective-permute-start(bf16[16,2048]{1,0:T(8,128)(2,1)S(1)} %get-tuple-element.67), channel_id=1, source_target_pairs={{0,8},{2,10},{4,12},{6,14},{8,0},{10,2},{12,4},{14,6},{16,24},{18,... | collective-permute-start | bytes 196616 | tf_op jit(solution)/shard_map/ppermute | solution.py:288
  108.7 8.2 %collective-permute-start.26 = (bf16[16,2048]{1,0:T(8,128)(2,1)S(1)}, bf16[16,2048]{1,0:T(8,128)(2,1)S(1)}, u32[]{:S(2)}, u32[]{:S(2)}) collective-permute-start(bf16[16,2048]{1,0:T(8,128)(2,1)S(1)} %get-tuple-element.69), channel_id=1, source_target_pairs={{0,16},{2,18},{4,20},{6,22},{8,24},{10,26},{12,28},{14,30},{16,0},... | collective-permute-start | bytes 196616 | tf_op jit(solution)/shard_map/ppermute | solution.py:288
  112.3 6.2 %collective-permute-start.27 = (bf16[16,2048]{1,0:T(8,128)(2,1)S(1)}, bf16[16,2048]{1,0:T(8,128)(2,1)S(1)}, u32[]{:S(2)}, u32[]{:S(2)}) collective-permute-start(bf16[16,2048]{1,0:T(8,128)(2,1)S(1)} %get-tuple-element.68), channel_id=1, source_target_pairs={{0,24},{2,26},{4,28},{6,30},{8,16},{10,18},{12,20},{14,22},{16,8},... | collective-permute-start | bytes 196616 | tf_op jit(solution)/shard_map/ppermute | solution.py:288
  124.8 14.1 %all-to-all-start = ((bf16[16,66,128]{2,1,0:T(8,128)(2,1)}), bf16[16,66,128]{2,1,0:T(8,128)(2,1)S(1)}, u32[]{:S(2)}, u32[]{:S(2)}) async-start(bf16[16,66,128]{2,1,0:T(8,128)(2,1)} %copy.51), calls=%async_computation | async-start | bytes 589824 | tf_op jit(solution)/shard_map/all_to_all | solution.py:431
  140.0 2.0 %copy-start.5 = (bf16[4,512,512]{2,1,0:T(8,128)(2,1)S(1)}, bf16[4,512,512]{2,1,0:T(8,128)(2,1)}, u32[]{:S(2)}) copy-start(bf16[4,512,512]{2,1,0:T(8,128)(2,1)} %weight_ref.1) | copy-start | bytes 6291460

commit v4 on v3

--- a/solution.py
+++ b/solution.py
@@ -61,8 +61,14 @@
 
 
 def project_own(first_ref, cats_ref, feat_ref, weight_ref, *rest):
-    out_refs, total_ref = rest[:-1], rest[-1]
-    expert = pl.program_id(0)
+    out_refs, fetched_ref, sems = rest[:-2], rest[-2], rest[-1]
+    experts, width = weight_ref.shape[:2]
+    copies = [
+        pltpu.make_async_copy(weight_ref.at[expert], fetched_ref.at[expert], sems.at[expert])
+        for expert in range(experts)
+    ]
+    for copy in copies:
+        copy.start()
     own = feat_ref.shape[0]
     on_diagonal = lax.broadcasted_iota(jnp.int32, (own, own), 0) == lax.broadcasted_iota(
         jnp.int32, (own, own), 1
@@ -70,45 +76,42 @@
     cats = jnp.sum(
         jnp.where(on_diagonal, cats_ref[...].astype(jnp.float32), 0.0), axis=1, keepdims=True
     )
-    chosen = cats == (first_ref[0] + expert).astype(jnp.float32)
-    part = jnp.dot(feat_ref[...], weight_ref[0], preferred_element_type=jnp.float32)
-    part = jnp.where(chosen, part, 0.0)
-
-    @pl.when(expert == 0)
-    def _():
-        total_ref[...] = part
-
-    @pl.when(expert > 0)
-    def _():
-        total_ref[...] += part
-
-    @pl.when(expert == pl.num_programs(0) - 1)
-    def _():
-        cols = out_refs[0].shape[1]
-        for half, out_ref in enumerate(out_refs):
-            out_ref[...] = total_ref[:, half * cols : (half + 1) * cols].astype(out_ref.dtype)
+    total = jnp.zeros((own, width), jnp.float32)
+    for expert in range(experts):
+        copies[expert].wait()
+        part = jnp.dot(feat_ref[...], fetched_ref[expert], preferred_element_type=jnp.float32)
+        chosen = cats == (first_ref[0] + expert).astype(jnp.float32)
+        total = total + jnp.where(chosen, part, 0.0)
+    cols = out_refs[0].shape[1]
+    for half, out_ref in enumerate(out_refs):
+        out_ref[...] = total[:, half * cols : (half + 1) * cols].astype(out_ref.dtype)
 
 
 def own_queries(first_expert, cats, feat, weights):
     own, width = feat.shape
     experts = weights.shape[0]
     half = jax.ShapeDtypeStruct((own, width // HALVES), jnp.bfloat16)
-    half_spec = pl.BlockSpec((own, width // HALVES), lambda expert, first_ref: (0, 0))
+    half_spec = pl.BlockSpec((own, width // HALVES), lambda step, first_ref: (0, 0))
     return pl.pallas_call(
         project_own,
         out_shape=[half] * HALVES,
         grid_spec=pltpu.PrefetchScalarGridSpec(
             num_scalar_prefetch=1,
-            grid=(experts,),
+            grid=(1,),
             in_specs=[
-                pl.BlockSpec((1, own), lambda expert, first_ref: (0, 0)),
-                pl.BlockSpec((own, width), lambda expert, first_ref: (0, 0)),
-                pl.BlockSpec((1, width, width), lambda expert, first_ref: (expert, 0, 0)),
+                pl.BlockSpec((1, own), lambda step, first_ref: (0, 0)),
+                pl.BlockSpec((own, width), lambda step, first_ref: (0, 0)),
+                pl.BlockSpec(memory_space=pl.ANY),
             ],
             out_specs=[half_spec] * HALVES,
-            scratch_shapes=[pltpu.VMEM((own, width), jnp.float32)],
-        ),
-        compiler_params=pltpu.CompilerParams(dimension_semantics=("arbitrary",)),
+            scratch_shapes=[
+                pltpu.VMEM((experts, width, width), jnp.bfloat16),
+                pltpu.SemaphoreType.DMA((experts,)),
+            ],
+        ),
+        compiler_params=pltpu.CompilerParams(
+            dimension_semantics=("arbitrary",), vmem_limit_bytes=16 * MIB
+        ),
         cost_estimate=pl.CostEstimate(
             flops=2 * own * width * width * experts,
             bytes_accessed=weights.size * 2 + own * width * 4,
@@ -133,14 +136,16 @@
 
 
 def spread(blocks, order_ref, same_ref, other_ref, dense_ref, *rest):
-    out_refs, all_ref, sems = rest[:-2], rest[-2], rest[-1]
+    out_refs, all_ref = rest[:-1], rest[-1]
     step = pl.program_id(0)
 
     @pl.when(step == 0)
     def _():
-        fetch_in_order(
-            order_ref, (same_ref, other_ref), all_ref, [sems.at[place] for place in range(blocks)]
-        )
+        own = all_ref.shape[0] // blocks
+        for place in range(blocks):
+            source = (same_ref, other_ref)[2 * place // blocks]
+            start = pl.multiple_of(order_ref[place] * own, own)
+            all_ref[pl.ds(start, own)] = source[pl.ds((place % (blocks // 2)) * own, own)]
 
     product = jnp.dot(dense_ref[...], all_ref[...], preferred_element_type=jnp.float32)
     for chunk, out_ref in enumerate(out_refs):
@@ -160,13 +165,10 @@
         grid_spec=pltpu.PrefetchScalarGridSpec(
             num_scalar_prefetch=1,
             grid=(chunks,),
-            in_specs=[pl.BlockSpec(memory_space=pl.ANY)] * 2
+            in_specs=[pl.BlockSpec(queries[0].shape, lambda step, order_ref: (0, 0))] * 2
             + [pl.BlockSpec((rows, items), lambda step, order_ref: (first + step, 0))],
             out_specs=[pl.BlockSpec((rows, cols), lambda step, order_ref: (0, 0))] * chunks,
-            scratch_shapes=[
-                pltpu.VMEM((items, cols), jnp.bfloat16),
-                pltpu.SemaphoreType.DMA((blocks,)),
-            ],
+            scratch_shapes=[pltpu.VMEM((items, cols), jnp.bfloat16)],
         ),
         compiler_params=pltpu.CompilerParams(
             dimension_semantics=("arbitrary",), vmem_limit_bytes=24 * MIB
@@ -295,8 +297,7 @@
 
 
 def gather_sides(own, size):
-    own = jnp.concatenate([own, flip(own, size, 2)], axis=0)
-    return own, flip(own, size, 1)
+    return jnp.concatenate([own, flip(own, size, 2)], axis=0)
 
 
 def gather_order(size):
@@ -306,25 +307,28 @@
     return lax.axis_index("user") ^ (layer * 4 + side * 2 + core)
 
 
-def scatter_sum(terms, size):
-    cores, sides = 2, 2
-    layers = size // (cores * sides)
+def sum_flipped(terms, size, bit, axis, index):
+    own = lax.dynamic_index_in_dim(terms, index, axis, keepdims=False)
+    away = lax.dynamic_index_in_dim(terms, 1 - index, axis, keepdims=False)
+    return own + flip(away.astype(jnp.bfloat16), size, bit).astype(jnp.float32)
+
+
+def sum_layers(terms, size, layer):
+    total = lax.dynamic_index_in_dim(terms, layer, 0, keepdims=False)
+    for other in range(1, terms.shape[0]):
+        away = lax.dynamic_index_in_dim(terms, layer ^ other, 0, keepdims=False)
+        total = total + flip(away.astype(jnp.bfloat16), size, other * 4).astype(jnp.float32)
+    return total
+
+
+def scatter_sum(terms, size, sides_first):
     index = lax.axis_index("user")
-    core, side, layer = index % cores, (index // cores) % sides, index // (cores * sides)
-    rest = terms.shape[1:]
-    terms = terms.reshape((layers, sides, cores) + rest)
-    own = lax.dynamic_index_in_dim(terms, core, 2, keepdims=False)
-    away = lax.dynamic_index_in_dim(terms, 1 - core, 2, keepdims=False).astype(jnp.bfloat16)
-    terms = own + flip(away, size, 1).astype(jnp.float32)
-    own = lax.dynamic_index_in_dim(terms, side, 1, keepdims=False)
-    away = lax.dynamic_index_in_dim(terms, 1 - side, 1, keepdims=False).astype(jnp.bfloat16)
-    terms = own + flip(away, size, 2).astype(jnp.float32)
-    total = lax.dynamic_index_in_dim(terms, layer, 0, keepdims=False)
-    for other in range(1, layers):
-        away = lax.dynamic_index_in_dim(terms, layer ^ other, 0, keepdims=False)
-        arrived = flip(away.astype(jnp.bfloat16), size, other * cores * sides)
-        total = total + arrived.astype(jnp.float32)
-    return total
+    core, side, layer = index % 2, (index // 2) % 2, index // 4
+    terms = terms.reshape((size // 4, 2, 2) + terms.shape[1:])
+    terms = sum_flipped(terms, size, 1, 2, core)
+    if sides_first:
+        return sum_layers(sum_flipped(terms, size, 2, 1, side), size, layer)
+    return sum_flipped(sum_layers(terms, size, layer), size, 2, 0, side)
 
 
 def as_rows(value, size):
@@ -348,31 +352,41 @@
 
     own_halves = own_queries(first_expert, own_cats, own_feat, expert_w)
     order = gather_order(user_size)
-    dense = dense_tiles(tile_place[0, 0], tile_count[0], tile_level[0, 0], users, items)
-    layers = [gather_layers(own, user_size) for own in own_halves]
-    layers[0], dense = lax.optimization_barrier((layers[0], dense))
-    queries = [gather_sides(part, user_size) for part in layers]
-
-    local_cats = (own_cats - first_expert).astype(jnp.bfloat16)
-    packed = jnp.concatenate(
-        [own_feat, jnp.broadcast_to(local_cats[:, None], (own_items, TILE))], axis=1
-    )
-    packed, _ = lax.optimization_barrier((packed, queries[-1][1]))
-    packed = gather_sides(gather_layers(packed, user_size), user_size)
-    own_width = width // user_size
-    feats, mask = ordered_items(order, packed, experts_here, own_width, width)
+    tile_index = tile_place[0, 0]
+    layers = gather_layers(own_halves[0], user_size)
+    layers, tile_index = lax.optimization_barrier((layers, tile_index))
+    dense = dense_tiles(tile_index, tile_count[0], tile_level[0, 0], users, items)
+    same = gather_sides(layers, user_size)
+    same, dense, own_second = lax.optimization_barrier((same, dense, own_halves[1]))
+    queries = [(same, flip(same, user_size, 1))]
+    same = gather_sides(gather_layers(own_second, user_size), user_size)
+    queries.append((same, flip(same, user_size, 1)))
 
     partials = []
     for half in range(HALVES):
-        first = [0, 1] if half == 0 else [0]
         partials.append([])
-        for start, end in zip(first, first[1:] + [ROW_CHUNKS]):
-            for partial in spread_items(order, queries[half], dense, start, end - start, rows):
+        first = [0, 1, ROW_CHUNKS] if half == 0 else [0, ROW_CHUNKS]
+        for start, end in zip(first, first[1:]):
+            here = spread_items(order, queries[half], dense, start, end - start, rows)
+            order, *here = lax.optimization_barrier((order, *here))
+            for partial in here:
                 pieces = [partial]
                 for shift in range(1, item_size):
                     pairs = [(source, (source + shift) % item_size) for source in range(item_size)]
                     pieces.append(lax.ppermute(partial, "item", pairs))
                 partials[half].append(pieces)
+
+    local_cats = (own_cats - first_expert).astype(jnp.bfloat16)
+    local_cats, order = lax.optimization_barrier((local_cats, order))
+    packed = jnp.concatenate(
+        [own_feat, jnp.broadcast_to(local_cats[:, None], (own_items, TILE))], axis=1
+    )
+    packed = gather_sides(gather_layers(packed, user_size), user_size)
+    own_width = width // user_size
+    feats, mask = ordered_items(
+        order, (packed, flip(packed, user_size, 1)), experts_here, own_width, width
+    )
+    partials[-1][-2][1], feats, mask = lax.optimization_barrier((partials[-1][-2][1], feats, mask))
 
     grads, gain_term, item_terms = [], 0.0, 0.0
     for chunk in range(ROW_CHUNKS):
@@ -404,7 +418,7 @@
             preferred_element_type=jnp.float32,
         )
         terms = terms.reshape(user_size, part_width, items)
-        sums.append(scatter_sum(terms, user_size).astype(jnp.bfloat16))
+        sums.append(scatter_sum(terms, user_size, half == 0).astype(jnp.bfloat16))
     sums = jnp.concatenate(sums, axis=0)
 
     col_width = width // item_size

time: 145 us -> 172 us (1.19)
  waiting for transfers between devices: 53.2 us -> 70.8 us
  local copies, waits for them, and re-layouts: 7.91 us -> 17.3 us
  Pallas kernels: 25.6 us -> 22.9 us
  starting transfers between devices: 45.1 us -> 47 us
    ppermute x25, waiting for transfers between devices: 21.5 us -> 50.2 us  [flip(): lax.ppermute(value, 'user', [(source, source ^ bits) for source in range(...]
    ppermute x8, waiting for transfers between devices: 22.4 us -> 11.2 us  [on_device(): pieces.append(lax.ppermute(partial, 'item', pairs))]
    unnamed x32 -> x78, local copies, waits for them, and re-layouts: 4.81 us -> 15.8 us
    pallas_call x1, Pallas kernels: 3.64 us -> 1.21 us  [own_queries(): pl.pallas_call(project_own, out_shape=[half] * HALVES, grid_spec=pltpu.Pr...]
    pallas_call x3, Pallas kernels: 12.3 us -> 10.1 us  [spread_items(): pl.pallas_call(functools.partial(spread, blocks), out_shape=[jax.ShapeDty...]
    pallas_call x4, Pallas kernels: 2.97 us -> 5.21 us  [user_gradient(): pl.pallas_call(functools.partial(norm_backward, len(pieces[0])), out_shap...]
  transfers between devices with their start and end apart: 34 -> 34, of which waited for: 16 -> 19; matrix products, arithmetic and copies ran while one was open for 6% -> 3% of each run, Pallas kernels for 12% -> 10%
where the time goes in v4:
time: 172 us; the launch traced here: 171 us
  waiting for transfers between devices  70.8 us (41%)
  starting transfers between devices  47 us (27%)
  Pallas kernels  22.9 us (13%)
  local copies, waits for them, and re-layouts  17.3 us (10%)
  matrix products  8.19 us (5%)
  other arithmetic  3.26 us (2%)
  between operations  2.01 us (1%)
    ppermute x25, waiting for transfers between devices, flip(): lax.ppermute(value, 'user', [(source, source ^ bits) for source in range(...  50.2 us
    ppermute x25, starting transfers between devices, flip(): lax.ppermute(value, 'user', [(source, source ^ bits) for source in range(...  33.5 us
    unnamed x78, local copies, waits for them, and re-layouts  15.8 us
    ppermute x8, waiting for transfers between devices, on_device(): pieces.append(lax.ppermute(partial, 'item', pairs))  11.2 us
    pallas_call x3, Pallas kernels, spread_items(): pl.pallas_call(functools.partial(spread, blocks), out_shape=[jax.ShapeDty...  10.1 us
    ppermute x8, starting transfers between devices, on_device(): pieces.append(lax.ppermute(partial, 'item', pairs))  9.6 us
    all_to_all x1, waiting for transfers between devices, on_device(): swapped = lax.all_to_all(jnp.concatenate(pieces, axis=1), 'user', 0, 0)  9.38 us
    pallas_call x4, Pallas kernels, user_gradient(): pl.pallas_call(functools.partial(norm_backward, len(pieces[0])), out_shap...  5.21 us
  transfers between devices with their start and end apart: 34, of which 19 were waited for; matrix products, arithmetic and copies ran while one was open for 3% of the time, Pallas kernels for 10%

profile of v4, /device:TPU:0, one launch (start us, length us, event | category | flops | bytes accessed | tf_op | source)
XLA Modules:
  0.0 171.5 jit_solution(7985213973232384247)
XLA Ops:
  0.7 1.6 copy-done.4
  5.0 5.1 %collective-permute-start.2 = (bf16[128,256]{1,0:T(8,128)(2,1)S(1)}, bf16[128,256]{1,0:T(8,128)(2,1)S(1)}, u32[]{:S(2)}, u32[]{:S(2)}) collective-permute-start(bf16[128,256]{1,0:T(8,128)(2,1)S(1)} %get-tuple-element.44), channel_id=1, source_target_pairs={{0,24},{2,26},{4,28},{6,30},{8,16},{10,18},{12,20},{14,22},{16,8},... | collective-permute-start | bytes 196616 | tf_op jit(solution)/shard_map/ppermute | solution.py:290
  10.8 1.9 %collective-permute-done.2 = bf16[128,256]{1,0:T(8,128)(2,1)S(1)} collective-permute-done((bf16[128,256]{1,0:T(8,128)(2,1)S(1)}, bf16[128,256]{1,0:T(8,128)(2,1)S(1)}, u32[]{:S(2)}, u32[]{:S(2)}) %collective-permute-start.2) | collective-permute-done | bytes 65568 | tf_op jit(solution)/shard_map/ppermute | solution.py:290
  12.7 3.0 %collective-permute-done.1 = bf16[128,256]{1,0:T(8,128)(2,1)S(1)} collective-permute-done((bf16[128,256]{1,0:T(8,128)(2,1)S(1)}, bf16[128,256]{1,0:T(8,128)(2,1)S(1)}, u32[]{:S(2)}, u32[]{:S(2)}) %collective-permute-start.1) | collective-permute-done | bytes 65568 | tf_op jit(solution)/shard_map/ppermute | solution.py:290
  15.8 1.6 collective-permute-start.3
  18.0 2.5 %copy-done.6 = s32[1,1,80,128,128]{4,3,2,1,0:T(8,128)S(1)} copy-done((s32[1,1,80,128,128]{4,3,2,1,0:T(8,128)S(1)}, s32[1,1,80,128,128]{4,3,2,1,0:T(8,128)}, u32[]{:S(2)}) %copy-start.6) | copy-done | bytes 5242904
  20.5 2.3 %place_tiles.1.dense_ref = bf16[2048,2048]{1,0:T(8,128)(2,1)S(1)} custom-call(s32[80]{0:T(128)S(1)} %bitcast.118, s32[1]{0:T(128)} %bitcast.107.count_ref, s32[80,128,128]{2,1,0:T(8,128)S(1)} %bitcast.110), custom_call_target="tpu_custom_call" | custom-call | flops 1310720 | bytes 13631488 | tf_op jit(solution)/shard_map/place_tiles/pallas_call | solution.py:40
  24.0 2.1 %collective-permute-start.7 = (bf16[128,256]{1,0:T(8,128)(2,1)S(1)}, bf16[128,256]{1,0:T(8,128)(2,1)S(1)}, u32[]{:S(2)}, u32[]{:S(2)}) collective-permute-start(bf16[128,256]{1,0:T(8,128)(2,1)S(1)} %get-tuple-element.56), channel_id=1, source_target_pairs={{0,16},{2,18},{4,20},{6,22},{8,24},{10,26},{12,28},{14,30},{16,0},... | collective-permute-start | bytes 196616 | tf_op jit(solution)/shard_map/ppermute | solution.py:290
  26.0 2.2 %collective-permute-start.8 = (bf16[128,256]{1,0:T(8,128)(2,1)S(1)}, bf16[128,256]{1,0:T(8,128)(2,1)S(1)}, u32[]{:S(2)}, u32[]{:S(2)}) collective-permute-start(bf16[128,256]{1,0:T(8,128)(2,1)S(1)} %get-tuple-element.56), channel_id=1, source_target_pairs={{0,24},{2,26},{4,28},{6,30},{8,16},{10,18},{12,20},{14,22},{16,8},... | collective-permute-start | bytes 196616 | tf_op jit(solution)/shard_map/ppermute | solution.py:290
  28.2 2.4 %collective-permute-done.7 = bf16[128,256]{1,0:T(8,128)(2,1)S(1)} collective-permute-done((bf16[128,256]{1,0:T(8,128)(2,1)S(1)}, bf16[128,256]{1,0:T(8,128)(2,1)S(1)}, u32[]{:S(2)}, u32[]{:S(2)}) %collective-permute-start.7) | collective-permute-done | bytes 65568 | tf_op jit(solution)/shard_map/ppermute | solution.py:290
  30.6 1.5 collective-permute-done.8
  32.1 1.7 collective-permute-start.9
  33.8 4.7 %collective-permute-done.9 = bf16[512,256]{1,0:T(8,128)(2,1)S(1)} collective-permute-done((bf16[512,256]{1,0:T(8,128)(2,1)S(1)}, bf16[512,256]{1,0:T(8,128)(2,1)S(1)}, u32[]{:S(2)}, u32[]{:S(2)}) %collective-permute-start.9) | collective-permute-done | bytes 262176 | tf_op jit(solution)/shard_map/ppermute | solution.py:290
  38.7 2.0 %spread_items.3.rest_0_ = bf16[512,256]{1,0:T(8,128)(2,1)} custom-call(s32[16]{0:T(128)S(1)} %fusion.55.order_ref, bf16[1024,256]{1,0:T(8,128)(2,1)S(1)} %pad_maximum_fusion.2.same_ref, bf16[1024,256]{1,0:T(8,128)(2,1)S(1)} %collective-permute-done.4.other_ref, bf16[2048,2048]{1,0:T(8,128)(2,1)S(1)} %place_tiles.1.dense_ref), custom_call_target="tpu_custom_call" | custom-call | flops 536870912 | bytes 3407872 | tf_op jit(solution)/shard_map/spread_items/pallas_call | solution.py:162
  40.7 3.6 %spread_items.4 = (bf16[512,256]{1,0:T(8,128)(2,1)}, bf16[512,256]{1,0:T(8,128)(2,1)S(1)}, bf16[512,256]{1,0:T(8,128)(2,1)S(1)}) custom-call(s32[16]{0:T(128)S(1)} %fusion.55.order_ref, bf16[1024,256]{1,0:T(8,128)(2,1)S(1)} %pad_maximum_fusion.2.same_ref, bf16[1024,256]{1,0:T(8,128)(2,1)S(1)} %collective-permute-done.4.other_ref, ...), custom_call_target="tpu_custom_call" | custom-call | flops 1610612736 | bytes 8126464 | tf_op jit(solution)/shard_map/spread_items/pallas_call | solution.py:162
  45.0 4.5 %spread_items.5 = (bf16[512,256]{1,0:T(8,128)(2,1)}, bf16[512,256]{1,0:T(8,128)(2,1)}, bf16[512,256]{1,0:T(8,128)(2,1)S(1)}, bf16[512,256]{1,0:T(8,128)(2,1)S(1)}) custom-call(s32[16]{0:T(128)S(1)} %fusion.55.order_ref, bf16[1024,256]{1,0:T(8,128)(2,1)S(1)} %constant_dynamic-update-slice_fusion.same_ref, ...), custom_call_target="tpu_custom_call" | custom-call | flops 2147483648 | bytes 10485760 | tf_op jit(solution)/shard_map/spread_items/pallas_call | solution.py:162
  49.7 2.7 %collective-permute-start.17 = (bf16[128,640]{1,0:T(8,128)(2,1)S(1)}, bf16[128,640]{1,0:T(8,128)(2,1)S(1)}, u32[]{:S(2)}, u32[]{:S(2)}) collective-permute-start(bf16[128,640]{1,0:T(8,128)(2,1)S(1)} %get-tuple-element.108), channel_id=1, source_target_pairs={{0,16},{2,18},{4,20},{6,22},{8,24},{10,26},{12,28},{14,30},{16,0},... | collective-permute-start | bytes 491528 | tf_op jit(solution)/shard_map/ppermute | solution.py:290
  52.5 1.7 collective-permute-start.18
  54.1 5.2 %collective-permute-done.16 = bf16[128,640]{1,0:T(8,128)(2,1)S(1)} collective-permute-done((bf16[128,640]{1,0:T(8,128)(2,1)S(1)}, bf16[128,640]{1,0:T(8,128)(2,1)S(1)}, u32[]{:S(2)}, u32[]{:S(2)}) %collective-permute-start.16) | collective-permute-done | bytes 163872 | tf_op jit(solution)/shard_map/ppermute | solution.py:290
  59.3 5.4 %collective-permute-done.17 = bf16[128,640]{1,0:T(8,128)(2,1)S(1)} collective-permute-done((bf16[128,640]{1,0:T(8,128)(2,1)S(1)}, bf16[128,640]{1,0:T(8,128)(2,1)S(1)}, u32[]{:S(2)}, u32[]{:S(2)}) %collective-permute-start.17) | collective-permute-done | bytes 163872 | tf_op jit(solution)/shard_map/ppermute | solution.py:290
  64.8 1.7 collective-permute-start.19
  66.5 1.5 collective-permute-start.21
  68.6 12.2 %collective-permute-done.19 = bf16[512,640]{1,0:T(8,128)(2,1)S(1)} collective-permute-done((bf16[512,640]{1,0:T(8,128)(2,1)S(1)}, bf16[512,640]{1,0:T(8,128)(2,1)S(1)}, u32[]{:S(2)}, u32[]{:S(2)}) %collective-permute-start.19) | collective-permute-done | bytes 655392 | tf_op jit(solution)/shard_map/ppermute | solution.py:290
  81.0 1.8 %collective-permute-start.12 = (bf16[512,256]{1,0:T(8,128)(2,1)}, bf16[512,256]{1,0:T(8,128)(2,1)}, u32[]{:S(2)}, u32[]{:S(2)}) collective-permute-start(bf16[512,256]{1,0:T(8,128)(2,1)} %get-tuple-element.63.rest_0_), channel_id=1, source_target_pairs={{0,1},{1,0},{2,3},{3,2},{4,5},{5,4},{6,7},{7,6},{8,9},{9,8},{10,11... | collective-permute-start | bytes 786440 | tf_op jit(solution)/shard_map/ppermute | solution.py:376
  83.8 1.7 %collective-permute-start.5 = (bf16[512,256]{1,0:T(8,128)(2,1)}, bf16[512,256]{1,0:T(8,128)(2,1)}, u32[]{:S(2)}, u32[]{:S(2)}) collective-permute-start(bf16[512,256]{1,0:T(8,128)(2,1)} %spread_items.3.rest_0_), channel_id=1, source_target_pairs={{0,1},{1,0},{2,3},{3,2},{4,5},{5,4},{6,7},{7,6},{8,9},{9,8},{10,11... | collective-permute-start | bytes 786440 | tf_op jit(solution)/shard_map/ppermute | solution.py:376
  86.6 1.6 copy-done.2
  92.9 1.7 %collective-permute-start.14 = (bf16[512,256]{1,0:T(8,128)(2,1)S(1)}, bf16[512,256]{1,0:T(8,128)(2,1)S(1)}, u32[]{:S(2)}, u32[]{:S(2)}) collective-permute-start(bf16[512,256]{1,0:T(8,128)(2,1)S(1)} %copy-done.16), channel_id=1, source_target_pairs={{0,1},{1,0},{2,3},{3,2},{4,5},{5,4},{6,7},{7,6},{8,9},{9,8},{10,11... | collective-permute-start | bytes 786440 | tf_op jit(solution)/shard_map/ppermute | solution.py:376
  94.6 1.5 collective-permute-done.13.rest_3_
  96.1 1.7 %collective-permute-start.15 = (bf16[512,256]{1,0:T(8,128)(2,1)S(1)}, bf16[512,256]{1,0:T(8,128)(2,1)S(1)}, u32[]{:S(2)}, u32[]{:S(2)}) collective-permute-start(bf16[512,256]{1,0:T(8,128)(2,1)S(1)} %copy-done.18), channel_id=1, source_target_pairs={{0,1},{1,0},{2,3},{3,2},{4,5},{5,4},{6,7},{7,6},{8,9},{9,8},{10,11... | collective-permute-start | bytes 786440 | tf_op jit(solution)/shard_map/ppermute | solution.py:376
  97.9 1.8 %user_gradient.5 = (bf16[512,512]{1,0:T(8,128)(2,1)S(1)}, f32[1,512]{1,0:T(1,128)S(1)}) custom-call(bf16[2048,512]{1,0:T(8,128)(2,1)S(1)} %copy-done.1, bf16[2048,512]{1,0:T(8,128)(2,1)S(1)} %copy-done.2, f32[1,512]{1,0:T(1,128)S(1)} %bitcast.115, bf16[512,256]{1,0:T(8,128)(2,1)} %get-tuple-element.63.rest_0_, ...), custom_call_target="tpu_custom_call" | custom-call | flops 4194304 | bytes 2621440 | tf_op jit(solution)/shard_map/user_gradient/pallas_call | solution.py:265
  99.7 2.1 %collective-permute-done.5.rest_1_ = bf16[512,256]{1,0:T(8,128)(2,1)} collective-permute-done((bf16[512,256]{1,0:T(8,128)(2,1)}, bf16[512,256]{1,0:T(8,128)(2,1)}, u32[]{:S(2)}, u32[]{:S(2)}) %collective-permute-start.5) | collective-permute-done | bytes 262176 | tf_op jit(solution)/shard_map/ppermute | solution.py:376
  101.8 5.6 %collective-permute-done.11.rest_3_ = bf16[512,256]{1,0:T(8,128)(2,1)} collective-permute-done((bf16[512,256]{1,0:T(8,128)(2,1)}, bf16[512,256]{1,0:T(8,128)(2,1)}, u32[]{:S(2)}, u32[]{:S(2)}) %collective-permute-start.11) | collective-permute-done | bytes 262176 | tf_op jit(solution)/shard_map/ppermute | solution.py:376
  107.4 1.8 %user_gradient.4 = (bf16[512,512]{1,0:T(8,128)(2,1)S(1)}, f32[1,512]{1,0:T(1,128)S(1)}) custom-call(bf16[2048,512]{1,0:T(8,128)(2,1)S(1)} %copy-done.1, bf16[2048,512]{1,0:T(8,128)(2,1)S(1)} %copy-done.2, f32[1,512]{1,0:T(1,128)S(1)} %bitcast.116, bf16[512,256]{1,0:T(8,128)(2,1)} %spread_items.3.rest_0_, bf16[512,256]{1,0:T(8,128)(2,1)} %collective-permute-done.5.rest_1_, ...), custom_call_target="tpu_custom_call" | custom-call | flops 4194304 | bytes 2621440 | tf_op jit(solution)/shard_map/user_gradient/pallas_call | solution.py:265
  111.9 4.1 %order_items.1 = (bf16[2048,512]{1,0:T(8,128)(2,1)S(1)}, bf16[4,32,2048]{2,1,0:T(8,128)(2,1)S(1)}) custom-call(s32[16]{0:T(128)S(1)} %fusion.55.order_ref, bf16[1024,640]{1,0:T(8,128)(2,1)S(1)} %constant_dynamic-update-slice_fusion.5.same_ref, bf16[1024,640]{1,0:T(8,128)(2,1)} %collective-permute-done.20.other_ref), custom_call_target="tpu_custom_call" | custom-call | bytes 6291456 | tf_op jit(solution)/shard_map/order_items/pallas_call | solution.py:201
  116.1 2.0 %collective-permute-done.15.rest_3_ = bf16[512,256]{1,0:T(8,128)(2,1)S(1)} collective-permute-done((bf16[512,256]{1,0:T(8,128)(2,1)S(1)}, bf16[512,256]{1,0:T(8,128)(2,1)S(1)}, u32[]{:S(2)}, u32[]{:S(2)}) %collective-permute-start.15) | collective-permute-done | bytes 262176 | tf_op jit(solution)/shard_map/ppermute | solution.py:376
  119.0 1.4 add_add_fusion
  123.4 2.2 %collective-permute-start.31 = (bf16[2,16,2048]{2,1,0:T(8,128)(2,1)S(1)}, bf16[2,16,2048]{2,1,0:T(8,128)(2,1)S(1)}, u32[]{:S(2)}, u32[]{:S(2)}) collective-permute-start(bf16[2,16,2048]{2,1,0:T(8,128)(2,1)S(1)} %get-tuple-element.101), channel_id=1, source_target_pairs={{0,24},{2,26},{4,28},{6,30},{8,16},{10,18},{12,20},{14,22},{16,8},... | collective-permute-start | bytes 393224 | tf_op jit(solution)/shard_map/ppermute | solution.py:290
  125.6 3.4 %collective-permute-start.30 = (bf16[2,16,2048]{2,1,0:T(8,128)(2,1)S(1)}, bf16[2,16,2048]{2,1,0:T(8,128)(2,1)S(1)}, u32[]{:S(2)}, u32[]{:S(2)}) collective-permute-start(bf16[2,16,2048]{2,1,0:T(8,128)(2,1)S(1)} %get-tuple-element.102), channel_id=1, source_target_pairs={{0,16},{2,18},{4,20},{6,22},{8,24},{10,26},{12,28},{14,30},{16,0},... | collective-permute-start | bytes 393224 | tf_op jit(solution)/shard_map/ppermute | solution.py:290
  129.2 1.6 collective-permute-start.24
  130.9 8.3 %collective-permute-done.30 = bf16[2,16,2048]{2,1,0:T(8,128)(2,1)S(1)} collective-permute-done((bf16[2,16,2048]{2,1,0:T(8,128)(2,1)S(1)}, bf16[2,16,2048]{2,1,0:T(8,128)(2,1)S(1)}, u32[]{:S(2)}, u32[]{:S(2)}) %collective-permute-start.30) | collective-permute-done | bytes 131104 | tf_op jit(solution)/shard_map/ppermute | solution.py:290
  139.3 1.4 collective-permute-start.32
  140.8 2.6 %collective-permute-start.27 = (bf16[16,2048]{1,0:T(8,128)(2,1)S(1)}, bf16[16,2048]{1,0:T(8,128)(2,1)S(1)}, u32[]{:S(2)}, u32[]{:S(2)}) collective-permute-start(bf16[16,2048]{1,0:T(8,128)(2,1)S(1)} %get-tuple-element.104), channel_id=1, source_target_pairs={{0,24},{2,26},{4,28},{6,30},{8,16},{10,18},{12,20},{14,22},{16,8},... | collective-permute-start | bytes 196616 | tf_op jit(solution)/shard_map/ppermute | solution.py:290
  143.4 1.9 %collective-permute-start.25 = (bf16[16,2048]{1,0:T(8,128)(2,1)S(1)}, bf16[16,2048]{1,0:T(8,128)(2,1)S(1)}, u32[]{:S(2)}, u32[]{:S(2)}) collective-permute-start(bf16[16,2048]{1,0:T(8,128)(2,1)S(1)} %get-tuple-element.103), channel_id=1, source_target_pairs={{0,8},{2,10},{4,12},{6,14},{8,0},{10,2},{12,4},{14,6},{16,24},{18,... | collective-permute-start | bytes 196616 | tf_op jit(solution)/shard_map/ppermute | solution.py:290
  145.3 1.9 %collective-permute-done.27 = bf16[16,2048]{1,0:T(8,128)(2,1)S(1)} collective-permute-done((bf16[16,2048]{1,0:T(8,128)(2,1)S(1)}, bf16[16,2048]{1,0:T(8,128)(2,1)S(1)}, u32[]{:S(2)}, u32[]{:S(2)}) %collective-permute-start.27) | collective-permute-done | bytes 65568 | tf_op jit(solution)/shard_map/ppermute | solution.py:290
  147.2 2.0 %collective-permute-done.26 = bf16[16,2048]{1,0:T(8,128)(2,1)S(1)} collective-permute-done((bf16[16,2048]{1,0:T(8,128)(2,1)S(1)}, bf16[16,2048]{1,0:T(8,128)(2,1)S(1)}, u32[]{:S(2)}, u32[]{:S(2)}) %collective-permute-start.26) | collective-permute-done | bytes 65568 | tf_op jit(solution)/shard_map/ppermute | solution.py:290
  151.1 3.9 %all-to-all-start = ((bf16[16,66,128]{2,1,0:T(8,128)(2,1)}), bf16[16,66,128]{2,1,0:T(8,128)(2,1)S(1)}, u32[]{:S(2)}, u32[]{:S(2)}) async-start(bf16[16,66,128]{2,1,0:T(8,128)(2,1)} %copy.46), calls=%async_computation | async-start | bytes 589824 | tf_op jit(solution)/shard_map/all_to_all | solution.py:445
  156.2 9.4 %all-to-all-done = bf16[16,66,128]{2,1,0:T(8,128)(2,1)S(1)} async-done(((bf16[16,66,128]{2,1,0:T(8,128)(2,1)}), bf16[16,66,128]{2,1,0:T(8,128)(2,1)S(1)}, u32[]{:S(2)}, u32[]{:S(2)}) %all-to-all-start) | async-done | bytes 270368 | tf_op jit(solution)/shard_map/all_to_all | solution.py:445
  170.1 1.3 convert_reduce_fusion
  (157 shorter events, 27.5 us)
Async XLA Ops:
  0.6 17.4 %copy-start.30 = (s32[1,1,80]{2,1,0:T(1,128)S(1)}, s32[1,1,80]{2,1,0:T(1,128)}, u32[]{:S(2)}) copy-start(s32[1,1,80]{2,1,0:T(1,128)} %param.15) | copy-start | bytes 964
  5.0 7.7 %collective-permute-start.2 = (bf16[128,256]{1,0:T(8,128)(2,1)S(1)}, bf16[128,256]{1,0:T(8,128)(2,1)S(1)}, u32[]{:S(2)}, u32[]{:S(2)}) collective-permute-start(bf16[128,256]{1,0:T(8,128)(2,1)S(1)} %get-tuple-element.44), channel_id=1, source_target_pairs={{0,24},{2,26},{4,28},{6,30},{8,16},{10,18},{12,20},{14,22},{16,8},... | collective-permute-start | bytes 196616 | tf_op jit(solution)/shard_map/ppermute | solution.py:290
  10.1 5.6 %collective-permute-start.1 = (bf16[128,256]{1,0:T(8,128)(2,1)S(1)}, bf16[128,256]{1,0:T(8,128)(2,1)S(1)}, u32[]{:S(2)}, u32[]{:S(2)}) collective-permute-start(bf16[128,256]{1,0:T(8,128)(2,1)S(1)} %get-tuple-element.44), channel_id=1, source_target_pairs={{0,16},{2,18},{4,20},{6,22},{8,24},{10,26},{12,28},{14,30},{16,0},... | collective-permute-start | bytes 196616 | tf_op jit(solution)/shard_map/ppermute | solution.py:290
  10.1 5.6 %collective-permute-start = (bf16[128,256]{1,0:T(8,128)(2,1)S(1)}, bf16[128,256]{1,0:T(8,128)(2,1)S(1)}, u32[]{:S(2)}, u32[]{:S(2)}) collective-permute-start(bf16[128,256]{1,0:T(8,128)(2,1)S(1)} %get-tuple-element.44), channel_id=1, source_target_pairs={{0,8},{2,10},{4,12},{6,14},{8,0},{10,2},{12,4},{14,6},{16,24},{18,... | collective-permute-start | bytes 196616 | tf_op jit(solution)/shard_map/ppermute | solution.py:290
  15.8 7.9 %collective-permute-start.3 = (bf16[512,256]{1,0:T(8,128)(2,1)S(1)}, bf16[512,256]{1,0:T(8,128)(2,1)S(1)}, u32[]{:S(2)}, u32[]{:S(2)}) collective-permute-start(bf16[512,256]{1,0:T(8,128)(2,1)S(1)} %pad_maximum_fusion.4), channel_id=1, source_target_pairs={{0,4},{2,6},{4,0},{6,2},{8,12},{10,14},{12,8},{14,10},{16,20},{18,... | collective-permute-start | bytes 786440 | tf_op jit(solution)/shard_map/ppermute | solution.py:290
  22.8 22.2 %copy-start = (bf16[2048,2048]{1,0:T(8,128)(2,1)}, bf16[2048,2048]{1,0:T(8,128)(2,1)S(1)}, u32[]{:S(2)}) copy-start(bf16[2048,2048]{1,0:T(8,128)(2,1)S(1)} %place_tiles.1.dense_ref) | copy-start | bytes 25165828
  22.8 15.9 %copy-start.29 = (s32[1,128]{1,0:T(1,128)S(1)}, s32[1,128]{1,0:T(1,128)}, u32[]{:S(2)}) copy-start(s32[1,128]{1,0:T(1,128)} %cats_ref.1) | copy-start | bytes 1540
  23.7 4.5 %collective-permute-start.6 = (bf16[128,256]{1,0:T(8,128)(2,1)S(1)}, bf16[128,256]{1,0:T(8,128)(2,1)S(1)}, u32[]{:S(2)}, u32[]{:S(2)}) collective-permute-start(bf16[128,256]{1,0:T(8,128)(2,1)S(1)} %get-tuple-element.56), channel_id=1, source_target_pairs={{0,8},{2,10},{4,12},{6,14},{8,0},{10,2},{12,4},{14,6},{16,24},{18,... | collective-permute-start | bytes 196616 | tf_op jit(solution)/shard_map/ppermute | solution.py:290
  24.0 6.6 %collective-permute-start.7 = (bf16[128,256]{1,0:T(8,128)(2,1)S(1)}, bf16[128,256]{1,0:T(8,128)(2,1)S(1)}, u32[]{:S(2)}, u32[]{:S(2)}) collective-permute-start(bf16[128,256]{1,0:T(8,128)(2,1)S(1)} %get-tuple-element.56), channel_id=1, source_target_pairs={{0,16},{2,18},{4,20},{6,22},{8,24},{10,26},{12,28},{14,30},{16,0},... | collective-permute-start | bytes 196616 | tf_op jit(solution)/shard_map/ppermute | solution.py:290
  26.0 6.1 %collective-permute-start.8 = (bf16[128,256]{1,0:T(8,128)(2,1)S(1)}, bf16[128,256]{1,0:T(8,128)(2,1)S(1)}, u32[]{:S(2)}, u32[]{:S(2)}) collective-permute-start(bf16[128,256]{1,0:T(8,128)(2,1)S(1)} %get-tuple-element.56), channel_id=1, source_target_pairs={{0,24},{2,26},{4,28},{6,30},{8,16},{10,18},{12,20},{14,22},{16,8},... | collective-permute-start | bytes 196616 | tf_op jit(solution)/shard_map/ppermute | solution.py:290
  28.2 10.5 %collective-permute-start.4 = (bf16[1024,256]{1,0:T(8,128)(2,1)S(1)}, bf16[1024,256]{1,0:T(8,128)(2,1)S(1)}, u32[]{:S(2)}, u32[]{:S(2)}) collective-permute-start(bf16[1024,256]{1,0:T(8,128)(2,1)S(1)} %pad_maximum_fusion.2.same_ref), channel_id=1, source_target_pairs={{0,2},{2,0},{4,6},{6,4},{8,10},{10,8},{12,14},{14,12},{16,18},{18,... | collective-permute-start | bytes 1572872 | tf_op jit(solution)/shard_map/ppermute | solution.py:290
  32.1 6.4 %collective-permute-start.9 = (bf16[512,256]{1,0:T(8,128)(2,1)S(1)}, bf16[512,256]{1,0:T(8,128)(2,1)S(1)}, u32[]{:S(2)}, u32[]{:S(2)}) collective-permute-start(bf16[512,256]{1,0:T(8,128)(2,1)S(1)} %pad_maximum_fusion.5), channel_id=1, source_target_pairs={{0,4},{2,6},{4,0},{6,2},{8,12},{10,14},{12,8},{14,10},{16,20},{18,... | collective-permute-start | bytes 786440 | tf_op jit(solution)/shard_map/ppermute | solution.py:290
  38.6 6.4 %collective-permute-start.10 = (bf16[1024,256]{1,0:T(8,128)(2,1)S(1)}, bf16[1024,256]{1,0:T(8,128)(2,1)S(1)}, u32[]{:S(2)}, u32[]{:S(2)}) collective-permute-start(bf16[1024,256]{1,0:T(8,128)(2,1)S(1)} %constant_dynamic-update-slice_fusion.same_ref), channel_id=1, source_target_pairs={{0,2},{2,0},{4,6},{6,4},{8,10},{10,8},{12,14},{14,12},{16,18},{18,... | collective-permute-start | bytes 1572872 | tf_op jit(solution)/shard_map/ppermute | solution.py:290
  45.0 21.5 %copy-start.19 = (bf16[512,256]{1,0:T(8,128)(2,1)}, bf16[512,256]{1,0:T(8,128)(2,1)S(1)}, u32[]{:S(2)}) copy-start(bf16[512,256]{1,0:T(8,128)(2,1)S(1)} %get-tuple-element.75.rest_0_) | copy-start | bytes 786436
  49.5 31.4 %copy-start.17 = (bf16[512,256]{1,0:T(8,128)(2,1)}, bf16[512,256]{1,0:T(8,128)(2,1)S(1)}, u32[]{:S(2)}) copy-start(bf16[512,256]{1,0:T(8,128)(2,1)S(1)} %get-tuple-element.67.rest_2_) | copy-start | bytes 786436
  49.5 33.6 %copy-start.21 = (bf16[512,256]{1,0:T(8,128)(2,1)}, bf16[512,256]{1,0:T(8,128)(2,1)S(1)}, u32[]{:S(2)}) copy-start(bf16[512,256]{1,0:T(8,128)(2,1)S(1)} %get-tuple-element.76.rest_2_) | copy-start | bytes 786436
  49.6 37.0 %copy-start.1 = (bf16[2048,512]{1,0:T(8,128)(2,1)S(1)}, bf16[2048,512]{1,0:T(8,128)(2,1)}, u32[]{:S(2)}) copy-start(bf16[2048,512]{1,0:T(8,128)(2,1)} %user_ref.7) | copy-start | bytes 6291460
  49.6 36.9 %copy-start.27 = (f32[512]{0:T(512)S(1)}, f32[512]{0:T(512)}, u32[]{:S(2)}) copy-start(f32[512]{0:T(512)} %param.11) | copy-start | bytes 6148
  49.7 9.7 %collective-permute-start.16 = (bf16[128,640]{1,0:T(8,128)(2,1)S(1)}, bf16[128,640]{1,0:T(8,128)(2,1)S(1)}, u32[]{:S(2)}, u32[]{:S(2)}) collective-permute-start(bf16[128,640]{1,0:T(8,128)(2,1)S(1)} %get-tuple-element.108), channel_id=1, source_target_pairs={{0,8},{2,10},{4,12},{6,14},{8,0},{10,2},{12,4},{14,6},{16,24},{18,... | collective-permute-start | bytes 491528 | tf_op jit(solution)/shard_map/ppermute | solution.py:290
  49.7 15.0 %collective-permute-start.17 = (bf16[128,640]{1,0:T(8,128)(2,1)S(1)}, bf16[128,640]{1,0:T(8,128)(2,1)S(1)}, u32[]{:S(2)}, u32[]{:S(2)}) collective-permute-start(bf16[128,640]{1,0:T(8,128)(2,1)S(1)} %get-tuple-element.108), channel_id=1, source_target_pairs={{0,16},{2,18},{4,20},{6,22},{8,24},{10,26},{12,28},{14,30},{16,0},... | collective-permute-start | bytes 491528 | tf_op jit(solution)/shard_map/ppermute | solution.py:290
  52.5 12.3 %collective-permute-start.18 = (bf16[128,640]{1,0:T(8,128)(2,1)S(1)}, bf16[128,640]{1,0:T(8,128)(2,1)S(1)}, u32[]{:S(2)}, u32[]{:S(2)}) collective-permute-start(bf16[128,640]{1,0:T(8,128)(2,1)S(1)} %get-tuple-element.108), channel_id=1, source_target_pairs={{0,24},{2,26},{4,28},{6,30},{8,16},{10,18},{12,20},{14,22},{16,8},... | collective-permute-start | bytes 491528 | tf_op jit(solution)/shard_map/ppermute | solution.py:290
  64.8 16.0 %collective-permute-start.19 = (bf16[512,640]{1,0:T(8,128)(2,1)S(1)}, bf16[512,640]{1,0:T(8,128)(2,1)S(1)}, u32[]{:S(2)}, u32[]{:S(2)}) collective-permute-start(bf16[512,640]{1,0:T(8,128)(2,1)S(1)} %pad_maximum_fusion.1), channel_id=1, source_target_pairs={{0,4},{2,6},{4,0},{6,2},{8,12},{10,14},{12,8},{14,10},{16,20},{18,... | collective-permute-start | bytes 1966088 | tf_op jit(solution)/shard_map/ppermute | solution.py:290
  66.5 16.6 %collective-permute-start.21 = (bf16[512,256]{1,0:T(8,128)(2,1)S(1)}, bf16[512,256]{1,0:T(8,128)(2,1)S(1)}, u32[]{:S(2)}, u32[]{:S(2)}) collective-permute-start(bf16[512,256]{1,0:T(8,128)(2,1)S(1)} %get-tuple-element.75.rest_0_), channel_id=1, source_target_pairs={{0,1},{1,0},{2,3},{3,2},{4,5},{5,4},{6,7},{7,6},{8,9},{9,8},{10,11... | collective-permute-start | bytes 786440 | tf_op jit(solution)/shard_map/ppermute | solution.py:376
  68.0 17.6 %collective-permute-start.22 = (bf16[512,256]{1,0:T(8,128)(2,1)S(1)}, bf16[512,256]{1,0:T(8,128)(2,1)S(1)}, u32[]{:S(2)}, u32[]{:S(2)}) collective-permute-start(bf16[512,256]{1,0:T(8,128)(2,1)S(1)} %get-tuple-element.76.rest_2_), channel_id=1, source_target_pairs={{0,1},{1,0},{2,3},{3,2},{4,5},{5,4},{6,7},{7,6},{8,9},{9,8},{10,11... | collective-permute-start | bytes 786440 | tf_op jit(solution)/shard_map/ppermute | solution.py:376
  81.0 30.9 %collective-permute-start.20 = (bf16[1024,640]{1,0:T(8,128)(2,1)S(1)}, bf16[1024,640]{1,0:T(8,128)(2,1)}, u32[]{:S(2)}, u32[]{:S(2)}) collective-permute-start(bf16[1024,640]{1,0:T(8,128)(2,1)S(1)} %constant_dynamic-update-slice_fusion.5.same_ref), channel_id=1, source_target_pairs={{0,2},{2,0},{4,6},{6,4},{8,10},{10,8},{12,14},{14,12},{16,18},{18,... | collective-permute-start | bytes 3932168 | tf_op jit(solution)/shard_map/ppermute | solution.py:290
  81.0 11.7 %collective-permute-start.12 = (bf16[512,256]{1,0:T(8,128)(2,1)}, bf16[512,256]{1,0:T(8,128)(2,1)}, u32[]{:S(2)}, u32[]{:S(2)}) collective-permute-start(bf16[512,256]{1,0:T(8,128)(2,1)} %get-tuple-element.63.rest_0_), channel_id=1, source_target_pairs={{0,1},{1,0},{2,3},{3,2},{4,5},{5,4},{6,7},{7,6},{8,9},{9,8},{10,11... | collective-permute-start | bytes 786440 | tf_op jit(solution)/shard_map/ppermute | solution.py:376
  82.8 13.3 %collective-permute-start.13 = (bf16[512,256]{1,0:T(8,128)(2,1)}, bf16[512,256]{1,0:T(8,128)(2,1)}, u32[]{:S(2)}, u32[]{:S(2)}) collective-permute-start(bf16[512,256]{1,0:T(8,128)(2,1)} %get-tuple-element.64.rest_2_), channel_id=1, source_target_pairs={{0,1},{1,0},{2,3},{3,2},{4,5},{5,4},{6,7},{7,6},{8,9},{9,8},{10,11... | collective-permute-start | bytes 786440 | tf_op jit(solution)/shard_map/ppermute | solution.py:376
  83.8 17.9 %collective-permute-start.5 = (bf16[512,256]{1,0:T(8,128)(2,1)}, bf16[512,256]{1,0:T(8,128)(2,1)}, u32[]{:S(2)}, u32[]{:S(2)}) collective-permute-start(bf16[512,256]{1,0:T(8,128)(2,1)} %spread_items.3.rest_0_), channel_id=1, source_target_pairs={{0,1},{1,0},{2,3},{3,2},{4,5},{5,4},{6,7},{7,6},{8,9},{9,8},{10,11... | collective-permute-start | bytes 786440 | tf_op jit(solution)/shard_map/ppermute | solution.py:376
  86.3 21.1 %collective-permute-start.11 = (bf16[512,256]{1,0:T(8,128)(2,1)}, bf16[512,256]{1,0:T(8,128)(2,1)}, u32[]{:S(2)}, u32[]{:S(2)}) collective-permute-start(bf16[512,256]{1,0:T(8,128)(2,1)} %get-tuple-element.61.rest_2_), channel_id=1, source_target_pairs={{0,1},{1,0},{2,3},{3,2},{4,5},{5,4},{6,7},{7,6},{8,9},{9,8},{10,11... | collective-permute-start | bytes 786440 | tf_op jit(solution)/shard_map/ppermute | solution.py:376
  92.0 17.3 %slice-start = ((s8[8388608]{0:T(1024)(128)(4,1)}), s8[4194304]{0:T(1024)(128)(4,1)S(1)}, s32[]{:S(2)}) async-start(s8[8388608]{0:T(1024)(128)(4,1)} %bitcast.108), calls=%async_computation.1 | async-start | bytes 8388608
  92.7 28.6 %copy-start.7 = (bf16[512,512]{1,0:T(8,128)(2,1)}, bf16[512,512]{1,0:T(8,128)(2,1)S(1)}, u32[]{:S(2)}) copy-start(bf16[512,512]{1,0:T(8,128)(2,1)S(1)} %get-tuple-element.77) | copy-start | bytes 1572868
  92.7 16.6 %slice-start.1 = ((s8[8388608]{0:T(1024)(128)(4,1)}), s8[4194304]{0:T(1024)(128)(4,1)S(1)}, s32[]{:S(2)}) async-start(s8[8388608]{0:T(1024)(128)(4,1)} %bitcast.108), calls=%async_computation.2 | async-start | bytes 8388608
  92.9 25.2 %collective-permute-start.14 = (bf16[512,256]{1,0:T(8,128)(2,1)S(1)}, bf16[512,256]{1,0:T(8,128)(2,1)S(1)}, u32[]{:S(2)}, u32[]{:S(2)}) collective-permute-start(bf16[512,256]{1,0:T(8,128)(2,1)S(1)} %copy-done.16), channel_id=1, source_target_pairs={{0,1},{1,0},{2,3},{3,2},{4,5},{5,4},{6,7},{7,6},{8,9},{9,8},{10,11... | collective-permute-start | bytes 786440 | tf_op jit(solution)/shard_map/ppermute | solution.py:376
  96.1 21.9 %collective-permute-start.15 = (bf16[512,256]{1,0:T(8,128)(2,1)S(1)}, bf16[512,256]{1,0:T(8,128)(2,1)S(1)}, u32[]{:S(2)}, u32[]{:S(2)}) collective-permute-start(bf16[512,256]{1,0:T(8,128)(2,1)S(1)} %copy-done.18), channel_id=1, source_target_pairs={{0,1},{1,0},{2,3},{3,2},{4,5},{5,4},{6,7},{7,6},{8,9},{9,8},{10,11... | collective-permute-start | bytes 786440 | tf_op jit(solution)/shard_map/ppermute | solution.py:376
  99.7 10.9 %copy-start.11 = (bf16[512,512]{1,0:T(8,128)(2,1)}, bf16[512,512]{1,0:T(8,128)(2,1)S(1)}, u32[]{:S(2)}) copy-start(bf16[512,512]{1,0:T(8,128)(2,1)S(1)} %get-tuple-element.65) | copy-start | bytes 1572868
  111.9 6.2 %copy-start.3 = (bf16[2048,512]{1,0:T(8,128)(2,1)S(1)}, bf16[2048,512]{1,0:T(8,128)(2,1)}, u32[]{:S(2)}) copy-start(bf16[2048,512]{1,0:T(8,128)(2,1)} %grad_ref.7) | copy-start | bytes 6291460
  121.2 2.0 %collective-permute-start.28 = (bf16[4,2,16,2048]{3,2,1,0:T(8,128)(2,1)S(1)}, bf16[4,2,16,2048]{3,2,1,0:T(8,128)(2,1)S(1)}, u32[]{:S(2)}, u32[]{:S(2)}) collective-permute-start(bf16[4,2,16,2048]{3,2,1,0:T(8,128)(2,1)S(1)} %fusion.22), channel_id=1, source_target_pairs={{0,2},{2,0},{4,6},{6,4},{8,10},{10,8},{12,14},{14,12},{16,18},{18,... | collective-permute-start | bytes 1572872 | tf_op jit(solution)/shard_map/ppermute | solution.py:290
  122.1 6.9 %collective-permute-start.23 = (bf16[4,2,16,2048]{3,2,0,1:T(8,128)(2,1)S(1)}, bf16[4,2,16,2048]{3,2,0,1:T(8,128)(2,1)S(1)}, u32[]{:S(2)}, u32[]{:S(2)}) collective-permute-start(bf16[4,2,16,2048]{3,2,0,1:T(8,128)(2,1)S(1)} %fusion.21), channel_id=1, source_target_pairs={{0,2},{2,0},{4,6},{6,4},{8,10},{10,8},{12,14},{14,12},{16,18},{18,... | collective-permute-start | bytes 1572872 | tf_op jit(solution)/shard_map/ppermute | solution.py:290
  123.4 7.5 %collective-permute-start.31 = (bf16[2,16,2048]{2,1,0:T(8,128)(2,1)S(1)}, bf16[2,16,2048]{2,1,0:T(8,128)(2,1)S(1)}, u32[]{:S(2)}, u32[]{:S(2)}) collective-permute-start(bf16[2,16,2048]{2,1,0:T(8,128)(2,1)S(1)} %get-tuple-element.101), channel_id=1, source_target_pairs={{0,24},{2,26},{4,28},{6,30},{8,16},{10,18},{12,20},{14,22},{16,8},... | collective-permute-start | bytes 393224 | tf_op jit(solution)/shard_map/ppermute | solution.py:290
  125.6 13.6 %collective-permute-start.30 = (bf16[2,16,2048]{2,1,0:T(8,128)(2,1)S(1)}, bf16[2,16,2048]{2,1,0:T(8,128)(2,1)S(1)}, u32[]{:S(2)}, u32[]{:S(2)}) collective-permute-start(bf16[2,16,2048]{2,1,0:T(8,128)(2,1)S(1)} %get-tuple-element.102), channel_id=1, source_target_pairs={{0,16},{2,18},{4,20},{6,22},{8,24},{10,26},{12,28},{14,30},{16,0},... | collective-permute-start | bytes 393224 | tf_op jit(solution)/shard_map/ppermute | solution.py:290
  129.0 10.2 %collective-permute-start.29 = (bf16[2,16,2048]{2,1,0:T(8,128)(2,1)S(1)}, bf16[2,16,2048]{2,1,0:T(8,128)(2,1)S(1)}, u32[]{:S(2)}, u32[]{:S(2)}) collective-permute-start(bf16[2,16,2048]{2,1,0:T(8,128)(2,1)S(1)} %get-tuple-element.100), channel_id=1, source_target_pairs={{0,8},{2,10},{4,12},{6,14},{8,0},{10,2},{12,4},{14,6},{16,24},{18,... | collective-permute-start | bytes 393224 | tf_op jit(solution)/shard_map/ppermute | solution.py:290
  129.2 11.6 %collective-permute-start.24 = (bf16[4,16,2048]{2,1,0:T(8,128)(2,1)S(1)}, bf16[4,16,2048]{2,1,0:T(8,128)(2,1)S(1)}, u32[]{:S(2)}, u32[]{:S(2)}) collective-permute-start(bf16[4,16,2048]{2,1,0:T(8,128)(2,1)S(1)} %fusion.31), channel_id=1, source_target_pairs={{0,4},{2,6},{4,0},{6,2},{8,12},{10,14},{12,8},{14,10},{16,20},{18,... | collective-permute-start | bytes 786440 | tf_op jit(solution)/shard_map/ppermute | solution.py:290
  139.3 6.0 %collective-permute-start.32 = (bf16[16,2048]{1,0:T(8,128)(2,1)S(1)}, bf16[16,2048]{1,0:T(8,128)(2,1)S(1)}, u32[]{:S(2)}, u32[]{:S(2)}) collective-permute-start(bf16[16,2048]{1,0:T(8,128)(2,1)S(1)} %fusion.46), channel_id=1, source_target_pairs={{0,4},{2,6},{4,0},{6,2},{8,12},{10,14},{12,8},{14,10},{16,20},{18,... | collective-permute-start | bytes 196616 | tf_op jit(solution)/shard_map/ppermute | solution.py:290
  140.8 6.4 %collective-permute-start.27 = (bf16[16,2048]{1,0:T(8,128)(2,1)S(1)}, bf16[16,2048]{1,0:T(8,128)(2,1)S(1)}, u32[]{:S(2)}, u32[]{:S(2)}) collective-permute-start(bf16[16,2048]{1,0:T(8,128)(2,1)S(1)} %get-tuple-element.104), channel_id=1, source_target_pairs={{0,24},{2,26},{4,28},{6,30},{8,16},{10,18},{12,20},{14,22},{16,8},... | collective-permute-start | bytes 196616 | tf_op jit(solution)/shard_map/ppermute | solution.py:290
  143.4 5.8 %collective-permute-start.26 = (bf16[16,2048]{1,0:T(8,128)(2,1)S(1)}, bf16[16,2048]{1,0:T(8,128)(2,1)S(1)}, u32[]{:S(2)}, u32[]{:S(2)}) collective-permute-start(bf16[16,2048]{1,0:T(8,128)(2,1)S(1)} %get-tuple-element.105), channel_id=1, source_target_pairs={{0,16},{2,18},{4,20},{6,22},{8,24},{10,26},{12,28},{14,30},{16,0},... | collective-permute-start | bytes 196616 | tf_op jit(solution)/shard_map/ppermute | solution.py:290
  143.4 5.8 %collective-permute-start.25 = (bf16[16,2048]{1,0:T(8,128)(2,1)S(1)}, bf16[16,2048]{1,0:T(8,128)(2,1)S(1)}, u32[]{:S(2)}, u32[]{:S(2)}) collective-permute-start(bf16[16,2048]{1,0:T(8,128)(2,1)S(1)} %get-tuple-element.103), channel_id=1, source_target_pairs={{0,8},{2,10},{4,12},{6,14},{8,0},{10,2},{12,4},{14,6},{16,24},{18,... | collective-permute-start | bytes 196616 | tf_op jit(solution)/shard_map/ppermute | solution.py:290
  149.4 5.7 %copy-start.12 = (bf16[512,512]{1,0:T(8,128)(2,1)S(1)}, bf16[512,512]{1,0:T(8,128)(2,1)}, u32[]{:S(2)}) copy-start(bf16[512,512]{1,0:T(8,128)(2,1)} %copy-done.11) | copy-start | bytes 1572868
  151.1 14.5 %all-to-all-start = ((bf16[16,66,128]{2,1,0:T(8,128)(2,1)}), bf16[16,66,128]{2,1,0:T(8,128)(2,1)S(1)}, u32[]{:S(2)}, u32[]{:S(2)}) async-start(bf16[16,66,128]{2,1,0:T(8,128)(2,1)} %copy.46), calls=%async_computation | async-start | bytes 589824 | tf_op jit(solution)/shard_map/all_to_all | solution.py:445
  (20 other events, 37.3 us)

commit v5 on v4

--- a/solution.py
+++ b/solution.py
@@ -15,7 +15,7 @@
 MIB = 1024 * 1024
 
 
-def place_tiles(item_blocks, place_ref, count_ref, level_ref, dense_ref):
+def place_tiles(item_blocks, place_ref, count_ref, level_ref, _, dense_ref):
     step = pl.program_id(0)
 
     @pl.when(step == 0)
@@ -34,7 +34,7 @@
             dense_ref[pl.ds(row, TILE), pl.ds(col, TILE)] = weights.astype(jnp.bfloat16)
 
 
-def dense_tiles(place, count, level, users, items):
+def dense_tiles(place, count, level, users, items, earlier):
     slots = level.shape[0]
     per_step = SLOTS_PER_STEP if slots % SLOTS_PER_STEP == 0 else 1
     return pl.pallas_call(
@@ -44,7 +44,8 @@
             num_scalar_prefetch=2,
             grid=(slots // per_step,),
             in_specs=[
-                pl.BlockSpec((per_step, TILE, TILE), lambda step, place_ref, count_ref: (step, 0, 0))
+                pl.BlockSpec((per_step, TILE, TILE), lambda step, place_ref, count_ref: (step, 0, 0)),
+                pl.BlockSpec(memory_space=pl.ANY),
             ],
             out_specs=pl.BlockSpec((users, items), lambda step, place_ref, count_ref: (0, 0)),
         ),
@@ -57,7 +58,7 @@
             transcendentals=0,
         ),
         name="place_tiles",
-    )(place, count, level)
+    )(place, count, level, earlier)
 
 
 def project_own(first_ref, cats_ref, feat_ref, weight_ref, *rest):
@@ -110,7 +111,7 @@
             ],
         ),
         compiler_params=pltpu.CompilerParams(
-            dimension_semantics=("arbitrary",), vmem_limit_bytes=16 * MIB
+            dimension_semantics=("arbitrary",), vmem_limit_bytes=56 * MIB
         ),
         cost_estimate=pl.CostEstimate(
             flops=2 * own * width * width * experts,
@@ -136,11 +137,13 @@
 
 
 def spread(blocks, order_ref, same_ref, other_ref, dense_ref, *rest):
-    out_refs, all_ref = rest[:-1], rest[-1]
+    out_refs, next_ref, all_ref = rest[:-2], rest[-2], rest[-1]
     step = pl.program_id(0)
 
     @pl.when(step == 0)
     def _():
+        for place in range(blocks):
+            next_ref[place] = order_ref[place]
         own = all_ref.shape[0] // blocks
         for place in range(blocks):
             source = (same_ref, other_ref)[2 * place // blocks]
@@ -148,26 +151,34 @@
             all_ref[pl.ds(start, own)] = source[pl.ds((place % (blocks // 2)) * own, own)]
 
     product = jnp.dot(dense_ref[...], all_ref[...], preferred_element_type=jnp.float32)
-    for chunk, out_ref in enumerate(out_refs):
-
-        @pl.when(step == chunk)
+    rows, first = product.shape[0], 0
+    for out_ref in out_refs:
+        chunks = out_ref.shape[0] // rows
+
+        @pl.when((step >= first) & (step < first + chunks))
         def _():
-            out_ref[...] = product.astype(out_ref.dtype)
-
-
-def spread_items(order, queries, dense, first, chunks, rows):
+            start = pl.multiple_of((step - first) * rows, rows)
+            out_ref[pl.ds(start, rows)] = product.astype(out_ref.dtype)
+
+        first += chunks
+
+
+def spread_items(order, queries, dense, first, counts, rows):
     items = dense.shape[1]
     cols = queries[0].shape[1]
-    blocks = order.shape[0]
+    blocks, chunks = order.shape[0], sum(counts)
+    whole = lambda step, order_ref: (0, 0)
     return pl.pallas_call(
         functools.partial(spread, blocks),
-        out_shape=[jax.ShapeDtypeStruct((rows, cols), jnp.bfloat16)] * chunks,
+        out_shape=[jax.ShapeDtypeStruct((count * rows, cols), jnp.bfloat16) for count in counts]
+        + [jax.ShapeDtypeStruct((blocks,), jnp.int32)],
         grid_spec=pltpu.PrefetchScalarGridSpec(
             num_scalar_prefetch=1,
             grid=(chunks,),
-            in_specs=[pl.BlockSpec(queries[0].shape, lambda step, order_ref: (0, 0))] * 2
+            in_specs=[pl.BlockSpec(queries[0].shape, whole)] * 2
             + [pl.BlockSpec((rows, items), lambda step, order_ref: (first + step, 0))],
-            out_specs=[pl.BlockSpec((rows, cols), lambda step, order_ref: (0, 0))] * chunks,
+            out_specs=[pl.BlockSpec((count * rows, cols), whole) for count in counts]
+            + [pl.BlockSpec(memory_space=pltpu.SMEM)],
             scratch_shapes=[pltpu.VMEM((items, cols), jnp.bfloat16)],
         ),
         compiler_params=pltpu.CompilerParams(
@@ -255,21 +266,25 @@
         term_ref[...] += term
 
 
-def user_gradient(user_feat, cotangent, gain, pieces, first, rows):
+def user_gradient(user_feat, cotangent, gain, pieces, first, rows, earlier):
     width = user_feat.shape[1]
     block_rows = min(BLOCK_ROWS, rows)
-    first_block = first // block_rows
-    flat = [piece for half in pieces for piece in half]
-    whole = pl.BlockSpec((block_rows, width), lambda step: (first_block + step, 0))
-    part = pl.BlockSpec((block_rows, width // HALVES), lambda step: (step, 0))
+    whole = pl.BlockSpec((block_rows, width), lambda step: (first // block_rows + step, 0))
+    flat, specs = [], []
+    for arrays, offset in pieces:
+        index_map = lambda step, skipped=(first - offset) // block_rows: (skipped + step, 0)
+        flat += arrays
+        specs += [pl.BlockSpec((block_rows, width // HALVES), index_map)] * len(arrays)
     return pl.pallas_call(
-        functools.partial(norm_backward, len(pieces[0])),
+        functools.partial(norm_backward, len(pieces[0][0])),
         out_shape=[
             jax.ShapeDtypeStruct((rows, width), jnp.bfloat16),
             jax.ShapeDtypeStruct((1, width), jnp.float32),
         ],
         grid=(rows // block_rows,),
-        in_specs=[whole, whole, pl.BlockSpec((1, width), lambda step: (0, 0))] + [part] * len(flat),
+        in_specs=[whole, whole, pl.BlockSpec((1, width), lambda step: (0, 0))]
+        + specs
+        + [pl.BlockSpec(memory_space=pl.ANY)] * len(earlier),
         out_specs=[
             pl.BlockSpec((block_rows, width), lambda step: (step, 0)),
             pl.BlockSpec((1, width), lambda step: (0, 0)),
@@ -279,11 +294,11 @@
         ),
         cost_estimate=pl.CostEstimate(
             flops=16 * rows * width,
-            bytes_accessed=rows * width * 2 * (3 + len(pieces[0])),
+            bytes_accessed=rows * width * 2 * (3 + len(pieces[0][0])),
             transcendentals=rows,
         ),
         name="user_gradient",
-    )(user_feat, cotangent, gain.reshape(1, width), *flat)
+    )(user_feat, cotangent, gain.reshape(1, width), *flat, *earlier)
 
 
 def flip(value, size, bits):
@@ -307,28 +322,33 @@
     return lax.axis_index("user") ^ (layer * 4 + side * 2 + core)
 
 
-def sum_flipped(terms, size, bit, axis, index):
-    own = lax.dynamic_index_in_dim(terms, index, axis, keepdims=False)
-    away = lax.dynamic_index_in_dim(terms, 1 - index, axis, keepdims=False)
-    return own + flip(away.astype(jnp.bfloat16), size, bit).astype(jnp.float32)
-
-
-def sum_layers(terms, size, layer):
-    total = lax.dynamic_index_in_dim(terms, layer, 0, keepdims=False)
-    for other in range(1, terms.shape[0]):
-        away = lax.dynamic_index_in_dim(terms, layer ^ other, 0, keepdims=False)
-        total = total + flip(away.astype(jnp.bfloat16), size, other * 4).astype(jnp.float32)
-    return total
-
-
-def scatter_sum(terms, size, sides_first):
+def exchange(partial, size):
+    pieces = [partial]
+    for shift in range(1, size):
+        pairs = [(source, (source + shift) % size) for source in range(size)]
+        pieces.append(lax.ppermute(partial, "item", pairs))
+    return pieces
+
+
+def scatter_sums(halves, size):
+    bits = size.bit_length() - 1
     index = lax.axis_index("user")
-    core, side, layer = index % 2, (index // 2) % 2, index // 4
-    terms = terms.reshape((size // 4, 2, 2) + terms.shape[1:])
-    terms = sum_flipped(terms, size, 1, 2, core)
-    if sides_first:
-        return sum_layers(sum_flipped(terms, size, 2, 1, side), size, layer)
-    return sum_flipped(sum_layers(terms, size, layer), size, 2, 0, side)
+    orders = [list(range(bits)), [0, 2, 1] + list(range(3, bits))]
+    halves = [terms.reshape((2,) * bits + terms.shape[1:]) for terms in halves]
+    left = [list(reversed(range(bits))) for _ in halves]
+    for stage in range(bits):
+        for half, terms in enumerate(halves):
+            bit = orders[half][stage]
+            axis = left[half].index(bit)
+            left[half].remove(bit)
+            mine = (index >> bit) & 1
+            own = lax.dynamic_index_in_dim(terms, mine, axis, keepdims=False)
+            away = lax.dynamic_index_in_dim(terms, 1 - mine, axis, keepdims=False)
+            arrived = flip(away.astype(jnp.bfloat16), size, 1 << bit)
+            halves[half] = own + arrived.astype(jnp.float32)
+        if 0 < stage < bits - 1:
+            halves = list(lax.optimization_barrier(tuple(halves)))
+    return halves
 
 
 def as_rows(value, size):
@@ -352,51 +372,47 @@
 
     own_halves = own_queries(first_expert, own_cats, own_feat, expert_w)
     order = gather_order(user_size)
-    tile_index = tile_place[0, 0]
     layers = gather_layers(own_halves[0], user_size)
-    layers, tile_index = lax.optimization_barrier((layers, tile_index))
-    dense = dense_tiles(tile_index, tile_count[0], tile_level[0, 0], users, items)
+    dense = dense_tiles(
+        tile_place[0, 0], tile_count[0], tile_level[0, 0], users, items, earlier=layers
+    )
     same = gather_sides(layers, user_size)
     same, dense, own_second = lax.optimization_barrier((same, dense, own_halves[1]))
-    queries = [(same, flip(same, user_size, 1))]
-    same = gather_sides(gather_layers(own_second, user_size), user_size)
-    queries.append((same, flip(same, user_size, 1)))
-
-    partials = []
-    for half in range(HALVES):
-        partials.append([])
-        first = [0, 1, ROW_CHUNKS] if half == 0 else [0, ROW_CHUNKS]
-        for start, end in zip(first, first[1:]):
-            here = spread_items(order, queries[half], dense, start, end - start, rows)
-            order, *here = lax.optimization_barrier((order, *here))
-            for partial in here:
-                pieces = [partial]
-                for shift in range(1, item_size):
-                    pairs = [(source, (source + shift) % item_size) for source in range(item_size)]
-                    pieces.append(lax.ppermute(partial, "item", pairs))
-                partials[half].append(pieces)
-
+    queries = (same, flip(same, user_size, 1))
+    layers = gather_layers(own_second, user_size)
+
+    product, order = spread_items(order, queries, dense, 0, (ROW_CHUNKS,), rows)
+    partials = [[(exchange(product, item_size), 0)], []]
     local_cats = (own_cats - first_expert).astype(jnp.bfloat16)
-    local_cats, order = lax.optimization_barrier((local_cats, order))
+    local_cats, layers, order = lax.optimization_barrier((local_cats, layers, order))
+    same = gather_sides(layers, user_size)
+    queries = (same, flip(same, user_size, 1))
+    counts = (ROW_CHUNKS - 2, 1, 1)
+    *products, order = spread_items(order, queries, dense, 0, counts, rows)
+    for number, product in enumerate(products):
+        partials[1].append((exchange(product, item_size), sum(counts[:number]) * rows))
+
     packed = jnp.concatenate(
         [own_feat, jnp.broadcast_to(local_cats[:, None], (own_items, TILE))], axis=1
     )
-    packed = gather_sides(gather_layers(packed, user_size), user_size)
+    packed = gather_layers(packed, user_size)
+    arrived = partials[0][0][0]
+    packed, order, arrived[-1] = lax.optimization_barrier((packed, order, arrived[-1]))
+    packed = gather_sides(packed, user_size)
     own_width = width // user_size
     feats, mask = ordered_items(
         order, (packed, flip(packed, user_size, 1)), experts_here, own_width, width
     )
-    partials[-1][-2][1], feats, mask = lax.optimization_barrier((partials[-1][-2][1], feats, mask))
 
     grads, gain_term, item_terms = [], 0.0, 0.0
     for chunk in range(ROW_CHUNKS):
+        pieces = [
+            [piece for piece in partials[half] if piece[1] <= chunk * rows][-1]
+            for half in range(HALVES)
+        ]
+        earlier = [mask] if chunk == ROW_CHUNKS - 2 else []
         grad, term = user_gradient(
-            user_feat,
-            cotangent,
-            gain,
-            [partials[half][chunk] for half in range(HALVES)],
-            chunk * rows,
-            rows,
+            user_feat, cotangent, gain, pieces, chunk * rows, rows, earlier
         )
         grads.append(grad)
         gain_term = gain_term + term[0]
@@ -408,7 +424,7 @@
                 preferred_element_type=jnp.float32,
             )
     part_width = own_width // HALVES
-    sums = []
+    halves = []
     for half in range(HALVES):
         part = slice(half * half_width, (half + 1) * half_width)
         terms = item_terms[part] + lax.dot_general(
@@ -417,9 +433,8 @@
             (((0,), (0,)), ((), ())),
             preferred_element_type=jnp.float32,
         )
-        terms = terms.reshape(user_size, part_width, items)
-        sums.append(scatter_sum(terms, user_size, half == 0).astype(jnp.bfloat16))
-    sums = jnp.concatenate(sums, axis=0)
+        halves.append(terms.reshape(user_size, part_width, items))
+    sums = jnp.concatenate(scatter_sums(halves, user_size), axis=0).astype(jnp.bfloat16)
 
     col_width = width // item_size
     user_grad = jnp.concatenate(

time: 172 us -> 166 us (0.965)
  starting transfers between devices: 47 us -> 31.5 us
  waiting for transfers between devices: 70.8 us -> 76.9 us
  local copies, waits for them, and re-layouts: 17.3 us -> 19.5 us
    ppermute x25 -> x23, starting transfers between devices: 33.5 us -> 22.9 us  [flip(): lax.ppermute(value, 'user', [(source, source ^ bits) for source in range(...]
    ppermute x25 -> x23, waiting for transfers between devices: 50.2 us -> 60.1 us  [flip(): lax.ppermute(value, 'user', [(source, source ^ bits) for source in range(...]
    ppermute x8 -> x4, starting transfers between devices: 9.6 us -> 5.1 us  [exchange(): pieces.append(lax.ppermute(partial, 'item', pairs))]
    ppermute x8 -> x4, waiting for transfers between devices: 11.2 us -> 7.4 us  [exchange(): pieces.append(lax.ppermute(partial, 'item', pairs))]
    pallas_call x1, Pallas kernels: 1.21 us -> 3.59 us  [own_queries(): pl.pallas_call(project_own, out_shape=[half] * HALVES, grid_spec=pltpu.Pr...]
    unnamed x78 -> x61, local copies, waits for them, and re-layouts: 15.8 us -> 17.1 us
    pallas_call x3 -> x2, Pallas kernels: 10.1 us -> 8.8 us  [spread_items(): pl.pallas_call(functools.partial(spread, blocks), out_shape=[jax.ShapeDty...]
  transfers between devices with their start and end apart: 34 -> 28, of which waited for: 19 -> 18; matrix products, arithmetic and copies ran while one was open for 3% -> 5% of each run, Pallas kernels for 10% -> 9%
where the time goes in v5:
time: 166 us
  waiting for transfers between devices  76.9 us (46%)
  starting transfers between devices  31.5 us (19%)
  Pallas kernels  24.3 us (15%)
  local copies, waits for them, and re-layouts  19.5 us (12%)
  matrix products  8.13 us (5%)
  other arithmetic  3.2 us (2%)
  between operations  2.09 us (1%)
    ppermute x23, waiting for transfers between devices, flip(): lax.ppermute(value, 'user', [(source, source ^ bits) for source in range(...  60.1 us
    ppermute x23, starting transfers between devices, flip(): lax.ppermute(value, 'user', [(source, source ^ bits) for source in range(...  22.9 us
    unnamed x61, local copies, waits for them, and re-layouts  17.1 us
    all_to_all x1, waiting for transfers between devices, on_device(): swapped = lax.all_to_all(jnp.concatenate(pieces, axis=1), 'user', 0, 0)  9.33 us
    pallas_call x2, Pallas kernels, spread_items(): pl.pallas_call(functools.partial(spread, blocks), out_shape=[jax.ShapeDty...  8.8 us
    ppermute x4, waiting for transfers between devices, exchange(): pieces.append(lax.ppermute(partial, 'item', pairs))  7.4 us
    pallas_call x4, Pallas kernels, user_gradient(): pl.pallas_call(functools.partial(norm_backward, len(pieces[0][0])), out_s...  6.76 us
    ppermute x4, starting transfers between devices, exchange(): pieces.append(lax.ppermute(partial, 'item', pairs))  5.1 us
  transfers between devices with their start and end apart: 28, of which 18 were waited for; matrix products, arithmetic and copies ran while one was open for 5% of the time, Pallas kernels for 9%

profile of v5, /device:TPU:0, one launch (start us, length us, event | category | flops | bytes accessed | tf_op | source)
XLA Modules:
  0.0 165.7 jit_solution(6187250341965412627)
XLA Ops:
  0.6 3.6 %own_queries.1 = (bf16[128,256]{1,0:T(8,128)(2,1)}, bf16[128,256]{1,0:T(8,128)(2,1)}) custom-call(s32[1]{0:T(128)} %bitcast.1.first_ref, s32[1,128]{1,0:T(1,128)} %cats_ref.1, bf16[128,512]{1,0:T(8,128)(2,1)} %bitcast.116, bf16[4,512,512]{2,1,0:T(8,128)(2,1)} %weight_ref.1), custom_call_target="tpu_custom_call" | custom-call | flops 268435456 | bytes 2359296 | tf_op jit(solution)/shard_map/own_queries/pallas_call | solution.py:96
  4.2 3.1 %collective-permute-start = (bf16[128,256]{1,0:T(8,128)(2,1)}, bf16[128,256]{1,0:T(8,128)(2,1)S(1)}, u32[]{:S(2)}, u32[]{:S(2)}) collective-permute-start(bf16[128,256]{1,0:T(8,128)(2,1)} %get-tuple-element.35), channel_id=1, source_target_pairs={{0,8},{2,10},{4,12},{6,14},{8,0},{10,2},{12,4},{14,6},{16,24},{18,... | collective-permute-start | bytes 196616 | tf_op jit(solution)/shard_map/ppermute | solution.py:305
  7.3 2.6 %collective-permute-start.1 = (bf16[128,256]{1,0:T(8,128)(2,1)}, bf16[128,256]{1,0:T(8,128)(2,1)S(1)}, u32[]{:S(2)}, u32[]{:S(2)}) collective-permute-start(bf16[128,256]{1,0:T(8,128)(2,1)} %get-tuple-element.35), channel_id=1, source_target_pairs={{0,16},{2,18},{4,20},{6,22},{8,24},{10,26},{12,28},{14,30},{16,0},... | collective-permute-start | bytes 196616 | tf_op jit(solution)/shard_map/ppermute | solution.py:305
  9.9 0.9 constant_dynamic-update-slice_fusion.3
  10.9 3.9 %collective-permute-done.1 = bf16[128,256]{1,0:T(8,128)(2,1)S(1)} collective-permute-done((bf16[128,256]{1,0:T(8,128)(2,1)}, bf16[128,256]{1,0:T(8,128)(2,1)S(1)}, u32[]{:S(2)}, u32[]{:S(2)}) %collective-permute-start.1) | collective-permute-done | bytes 65568 | tf_op jit(solution)/shard_map/ppermute | solution.py:305
  14.8 1.4 collective-permute-done.2
  16.2 1.6 collective-permute-start.3
  18.5 2.5 %copy-done.8 = s32[1,1,80,128,128]{4,3,2,1,0:T(8,128)S(1)} copy-done((s32[1,1,80,128,128]{4,3,2,1,0:T(8,128)S(1)}, s32[1,1,80,128,128]{4,3,2,1,0:T(8,128)}, u32[]{:S(2)}) %copy-start.8) | copy-done | bytes 5242904
  21.0 2.4 %place_tiles.1.dense_ref = bf16[2048,2048]{1,0:T(8,128)(2,1)S(1)} custom-call(s32[80]{0:T(128)S(1)} %bitcast.104, s32[1]{0:T(128)} %bitcast.96.count_ref, s32[80,128,128]{2,1,0:T(8,128)S(1)} %bitcast.99, bf16[512,256]{1,0:T(8,128)(2,1)S(1)} %get-tuple-element.84._), custom_call_target="tpu_custom_call" | custom-call | flops 1310720 | bytes 13631488 | tf_op jit(solution)/shard_map/place_tiles/pallas_call | solution.py:40
  23.4 3.3 %copy-done = bf16[2048,2048]{1,0:T(8,128)(2,1)} copy-done((bf16[2048,2048]{1,0:T(8,128)(2,1)}, bf16[2048,2048]{1,0:T(8,128)(2,1)S(1)}, u32[]{:S(2)}) %copy-start) | copy-done | bytes 8388632
  26.8 1.6 collective-permute-start.7
  28.4 2.9 %collective-permute-start.5 = (bf16[128,256]{1,0:T(8,128)(2,1)S(1)}, bf16[128,256]{1,0:T(8,128)(2,1)S(1)}, u32[]{:S(2)}, u32[]{:S(2)}) collective-permute-start(bf16[128,256]{1,0:T(8,128)(2,1)S(1)} %copy-done.22), channel_id=1, source_target_pairs={{0,8},{2,10},{4,12},{6,14},{8,0},{10,2},{12,4},{14,6},{16,24},{18,... | collective-permute-start | bytes 196616 | tf_op jit(solution)/shard_map/ppermute | solution.py:305
  31.3 2.4 %collective-permute-done.7 = bf16[128,256]{1,0:T(8,128)(2,1)S(1)} collective-permute-done((bf16[128,256]{1,0:T(8,128)(2,1)S(1)}, bf16[128,256]{1,0:T(8,128)(2,1)S(1)}, u32[]{:S(2)}, u32[]{:S(2)}) %collective-permute-start.7) | collective-permute-done | bytes 65568 | tf_op jit(solution)/shard_map/ppermute | solution.py:305
  33.7 2.3 %collective-permute-done.6 = bf16[128,256]{1,0:T(8,128)(2,1)S(1)} collective-permute-done((bf16[128,256]{1,0:T(8,128)(2,1)S(1)}, bf16[128,256]{1,0:T(8,128)(2,1)S(1)}, u32[]{:S(2)}, u32[]{:S(2)}) %collective-permute-start.6) | collective-permute-done | bytes 65568 | tf_op jit(solution)/shard_map/ppermute | solution.py:305
  36.0 3.4 %copy-done.1 = bf16[2048,2048]{1,0:T(8,128)(2,1)S(1)} copy-done((bf16[2048,2048]{1,0:T(8,128)(2,1)S(1)}, bf16[2048,2048]{1,0:T(8,128)(2,1)}, u32[]{:S(2)}) %copy-start.1) | copy-done | bytes 8388632
  39.4 4.2 %spread_items.2 = (bf16[2048,256]{1,0:T(8,128)(2,1)S(1)}, s32[16]{0:T(128)S(1)}) custom-call(s32[16]{0:T(128)S(1)} %fusion.49.order_ref, bf16[1024,256]{1,0:T(8,128)(2,1)S(1)} %constant_dynamic-update-slice_fusion.4.same_ref, bf16[1024,256]{1,0:T(8,128)(2,1)S(1)} %collective-permute-done.4.other_ref, bf16[2048,2048]{1,0:T(8,128)(2,1)S(1)} %copy-done.1), custom_call_target="tpu_custom_call" | custom-call | flops 2147483648 | bytes 10485760 | tf_op jit(solution)/shard_map/spread_items/pallas_call | solution.py:171
  44.0 1.6 collective-permute-start.13
  45.6 6.3 %collective-permute-done.11 = bf16[512,256]{1,0:T(8,128)(2,1)S(1)} collective-permute-done((bf16[512,256]{1,0:T(8,128)(2,1)S(1)}, bf16[512,256]{1,0:T(8,128)(2,1)S(1)}, u32[]{:S(2)}, u32[]{:S(2)}) %collective-permute-start.11) | collective-permute-done | bytes 262176 | tf_op jit(solution)/shard_map/ppermute | solution.py:305
  52.1 1.8 %collective-permute-start.10 = (bf16[128,640]{1,0:T(8,128)(2,1)S(1)}, bf16[128,640]{1,0:T(8,128)(2,1)S(1)}, u32[]{:S(2)}, u32[]{:S(2)}) collective-permute-start(bf16[128,640]{1,0:T(8,128)(2,1)S(1)} %pad_maximum_fusion.4), channel_id=1, source_target_pairs={{0,24},{2,26},{4,28},{6,30},{8,16},{10,18},{12,20},{14,22},{16,8},... | collective-permute-start | bytes 491528 | tf_op jit(solution)/shard_map/ppermute | solution.py:305
  53.9 2.6 %collective-permute-start.8 = (bf16[128,640]{1,0:T(8,128)(2,1)S(1)}, bf16[128,640]{1,0:T(8,128)(2,1)S(1)}, u32[]{:S(2)}, u32[]{:S(2)}) collective-permute-start(bf16[128,640]{1,0:T(8,128)(2,1)S(1)} %pad_maximum_fusion.4), channel_id=1, source_target_pairs={{0,8},{2,10},{4,12},{6,14},{8,0},{10,2},{12,4},{14,6},{16,24},{18,... | collective-permute-start | bytes 491528 | tf_op jit(solution)/shard_map/ppermute | solution.py:305
  56.6 4.5 %collective-permute-done.10 = bf16[128,640]{1,0:T(8,128)(2,1)S(1)} collective-permute-done((bf16[128,640]{1,0:T(8,128)(2,1)S(1)}, bf16[128,640]{1,0:T(8,128)(2,1)S(1)}, u32[]{:S(2)}, u32[]{:S(2)}) %collective-permute-start.10) | collective-permute-done | bytes 163872 | tf_op jit(solution)/shard_map/ppermute | solution.py:305
  61.1 6.9 %collective-permute-done.9 = bf16[128,640]{1,0:T(8,128)(2,1)S(1)} collective-permute-done((bf16[128,640]{1,0:T(8,128)(2,1)S(1)}, bf16[128,640]{1,0:T(8,128)(2,1)S(1)}, u32[]{:S(2)}, u32[]{:S(2)}) %collective-permute-start.9) | collective-permute-done | bytes 163872 | tf_op jit(solution)/shard_map/ppermute | solution.py:305
  68.1 4.6 %spread_items.3 = (bf16[1024,256]{1,0:T(8,128)(2,1)}, bf16[512,256]{1,0:T(8,128)(2,1)S(1)}, bf16[512,256]{1,0:T(8,128)(2,1)}, s32[16]{0:T(128)S(1)}) custom-call(s32[16]{0:T(128)S(1)} %get-tuple-element.43.order_ref, bf16[1024,256]{1,0:T(8,128)(2,1)S(1)} %constant_dynamic-update-slice_fusion.9.same_ref, ...), custom_call_target="tpu_custom_call" | custom-call | flops 2147483648 | bytes 10485760 | tf_op jit(solution)/shard_map/spread_items/pallas_call | solution.py:171
  72.7 1.0 copy-done.5
  74.4 1.5 collective-permute-start.14
  76.8 13.4 %collective-permute-done.16 = bf16[512,640]{1,0:T(8,128)(2,1)S(1)} collective-permute-done((bf16[512,640]{1,0:T(8,128)(2,1)S(1)}, bf16[512,640]{1,0:T(8,128)(2,1)S(1)}, u32[]{:S(2)}, u32[]{:S(2)}) %collective-permute-start.16) | collective-permute-done | bytes 655392 | tf_op jit(solution)/shard_map/ppermute | solution.py:305
  91.1 1.5 collective-permute-start.18
  93.1 7.4 %collective-permute-done.18.rest_3_ = bf16[512,256]{1,0:T(8,128)(2,1)} collective-permute-done((bf16[512,256]{1,0:T(8,128)(2,1)}, bf16[512,256]{1,0:T(8,128)(2,1)}, u32[]{:S(2)}, u32[]{:S(2)}) %collective-permute-start.18) | collective-permute-done | bytes 262176 | tf_op jit(solution)/shard_map/ppermute | solution.py:329
  100.5 1.6 copy-done.3
  102.1 1.2 copy-done.6
  103.3 1.8 %user_gradient.7 = (bf16[512,512]{1,0:T(8,128)(2,1)S(1)}, f32[1,512]{1,0:T(1,128)S(1)}) custom-call(bf16[2048,512]{1,0:T(8,128)(2,1)S(1)} %copy-done.2, bf16[2048,512]{1,0:T(8,128)(2,1)S(1)} %copy-done.3, f32[1,512]{1,0:T(1,128)S(1)} %bitcast.100, bf16[2048,256]{1,0:T(8,128)(2,1)S(1)} %get-tuple-element.39.rest_0_, bf16[2048,256]{1,0:T(8,128)(2,1)S(1)} %copy-done.6, ...), custom_call_target="tpu_custom_call" | custom-call | flops 4194304 | bytes 2621440 | tf_op jit(solution)/shard_map/user_gradient/pallas_call | solution.py:278
  105.2 2.1 %user_gradient.5 = (bf16[512,512]{1,0:T(8,128)(2,1)S(1)}, f32[1,512]{1,0:T(1,128)S(1)}) custom-call(bf16[2048,512]{1,0:T(8,128)(2,1)S(1)} %copy-done.2, bf16[2048,512]{1,0:T(8,128)(2,1)S(1)} %copy-done.4, f32[1,512]{1,0:T(1,128)S(1)} %bitcast.101, bf16[2048,256]{1,0:T(8,128)(2,1)S(1)} %get-tuple-element.39.rest_0_, bf16[2048,256]{1,0:T(8,128)(2,1)S(1)} %copy-done.6, ...), custom_call_target="tpu_custom_call" | custom-call | flops 4194304 | bytes 2621440 | tf_op jit(solution)/shard_map/user_gradient/pallas_call | solution.py:278
  107.4 1.9 %user_gradient.4 = (bf16[512,512]{1,0:T(8,128)(2,1)S(1)}, f32[1,512]{1,0:T(1,128)S(1)}) custom-call(bf16[2048,512]{1,0:T(8,128)(2,1)S(1)} %copy-done.2, bf16[2048,512]{1,0:T(8,128)(2,1)S(1)} %copy-done.4, f32[1,512]{1,0:T(1,128)S(1)} %bitcast.102, bf16[2048,256]{1,0:T(8,128)(2,1)S(1)} %get-tuple-element.39.rest_0_, bf16[2048,256]{1,0:T(8,128)(2,1)S(1)} %copy-done.6, ...), custom_call_target="tpu_custom_call" | custom-call | flops 4194304 | bytes 2621440 | tf_op jit(solution)/shard_map/user_gradient/pallas_call | solution.py:278
  109.3 1.3 fusion.6
  110.6 1.3 fusion.4
  111.9 2.8 %order_items.1 = (bf16[2048,512]{1,0:T(8,128)(2,1)S(1)}, bf16[4,32,2048]{2,1,0:T(8,128)(2,1)S(1)}) custom-call(s32[16]{0:T(128)S(1)} %get-tuple-element.51.order_ref, bf16[1024,640]{1,0:T(8,128)(2,1)} %constant_dynamic-update-slice_fusion.11.same_ref, bf16[1024,640]{1,0:T(8,128)(2,1)} %collective-permute-done.17.other_ref), custom_call_target="tpu_custom_call" | custom-call | bytes 6291456 | tf_op jit(solution)/shard_map/order_items/pallas_call | solution.py:212
  115.7 1.4 add_add_fusion
  121.2 7.3 %collective-permute-done.20 = bf16[2,2,16,2048]{3,2,0,1:T(8,128)(2,1)S(1)} collective-permute-done((bf16[2,2,16,2048]{3,2,0,1:T(8,128)(2,1)S(1)}, bf16[2,2,16,2048]{3,2,0,1:T(8,128)(2,1)S(1)}, u32[]{:S(2)}, u32[]{:S(2)}) %collective-permute-start.20) | collective-permute-done | bytes 262176 | tf_op jit(solution)/shard_map/ppermute | solution.py:305
  128.5 1.2 collective-permute-done.22
  131.0 3.9 %collective-permute-done.23 = bf16[2,16,2048]{2,1,0:T(8,128)(2,1)S(1)} collective-permute-done((bf16[2,16,2048]{2,1,0:T(8,128)(2,1)S(1)}, bf16[2,16,2048]{2,1,0:T(8,128)(2,1)S(1)}, u32[]{:S(2)}, u32[]{:S(2)}) %collective-permute-start.23) | collective-permute-done | bytes 131104 | tf_op jit(solution)/shard_map/ppermute | solution.py:305
  135.4 2.7 %collective-permute-start.26 = (bf16[16,2048]{1,0:T(8,128)(2,1)S(1)}, bf16[16,2048]{1,0:T(8,128)(2,1)S(1)}, u32[]{:S(2)}, u32[]{:S(2)}) collective-permute-start(bf16[16,2048]{1,0:T(8,128)(2,1)S(1)} %fusion.40), channel_id=1, source_target_pairs={{0,16},{2,18},{4,20},{6,22},{8,24},{10,26},{12,28},{14,30},{16,0},... | collective-permute-start | bytes 196616 | tf_op jit(solution)/shard_map/ppermute | solution.py:305
  138.4 4.8 %collective-permute-done.26 = bf16[16,2048]{1,0:T(8,128)(2,1)S(1)} collective-permute-done((bf16[16,2048]{1,0:T(8,128)(2,1)S(1)}, bf16[16,2048]{1,0:T(8,128)(2,1)S(1)}, u32[]{:S(2)}, u32[]{:S(2)}) %collective-permute-start.26) | collective-permute-done | bytes 65568 | tf_op jit(solution)/shard_map/ppermute | solution.py:305
  145.8 3.5 %all-to-all-start = ((bf16[16,66,128]{2,1,0:T(8,128)(2,1)}), bf16[16,66,128]{2,1,0:T(8,128)(2,1)S(1)}, u32[]{:S(2)}, u32[]{:S(2)}) async-start(bf16[16,66,128]{2,1,0:T(8,128)(2,1)} %copy.53), calls=%async_computation | async-start | bytes 589824 | tf_op jit(solution)/shard_map/all_to_all | solution.py:460
  149.5 1.0 pad_maximum_fusion
  150.5 9.3 %all-to-all-done = bf16[16,66,128]{2,1,0:T(8,128)(2,1)S(1)} async-done(((bf16[16,66,128]{2,1,0:T(8,128)(2,1)}), bf16[16,66,128]{2,1,0:T(8,128)(2,1)S(1)}, u32[]{:S(2)}, u32[]{:S(2)}) %all-to-all-start) | async-done | bytes 270368 | tf_op jit(solution)/shard_map/all_to_all | solution.py:460
  160.8 1.0 copy.57
  163.3 1.0 fusion.20
  164.3 1.3 convert_reduce_fusion
  (132 shorter events, 15.9 us)
Async XLA Ops:
  0.6 17.9 %copy-start.18 = (s32[1,1,80]{2,1,0:T(1,128)S(1)}, s32[1,1,80]{2,1,0:T(1,128)}, u32[]{:S(2)}) copy-start(s32[1,1,80]{2,1,0:T(1,128)} %param.15) | copy-start | bytes 964
  4.2 6.6 %collective-permute-start = (bf16[128,256]{1,0:T(8,128)(2,1)}, bf16[128,256]{1,0:T(8,128)(2,1)S(1)}, u32[]{:S(2)}, u32[]{:S(2)}) collective-permute-start(bf16[128,256]{1,0:T(8,128)(2,1)} %get-tuple-element.35), channel_id=1, source_target_pairs={{0,8},{2,10},{4,12},{6,14},{8,0},{10,2},{12,4},{14,6},{16,24},{18,... | collective-permute-start | bytes 196616 | tf_op jit(solution)/shard_map/ppermute | solution.py:305
  7.3 7.5 %collective-permute-start.1 = (bf16[128,256]{1,0:T(8,128)(2,1)}, bf16[128,256]{1,0:T(8,128)(2,1)S(1)}, u32[]{:S(2)}, u32[]{:S(2)}) collective-permute-start(bf16[128,256]{1,0:T(8,128)(2,1)} %get-tuple-element.35), channel_id=1, source_target_pairs={{0,16},{2,18},{4,20},{6,22},{8,24},{10,26},{12,28},{14,30},{16,0},... | collective-permute-start | bytes 196616 | tf_op jit(solution)/shard_map/ppermute | solution.py:305
  9.9 6.3 %collective-permute-start.2 = (bf16[128,256]{1,0:T(8,128)(2,1)}, bf16[128,256]{1,0:T(8,128)(2,1)S(1)}, u32[]{:S(2)}, u32[]{:S(2)}) collective-permute-start(bf16[128,256]{1,0:T(8,128)(2,1)} %get-tuple-element.35), channel_id=1, source_target_pairs={{0,24},{2,26},{4,28},{6,30},{8,16},{10,18},{12,20},{14,22},{16,8},... | collective-permute-start | bytes 196616 | tf_op jit(solution)/shard_map/ppermute | solution.py:305
  16.2 10.4 %collective-permute-start.3 = (bf16[512,256]{1,0:T(8,128)(2,1)S(1)}, bf16[512,256]{1,0:T(8,128)(2,1)S(1)}, u32[]{:S(2)}, u32[]{:S(2)}) collective-permute-start(bf16[512,256]{1,0:T(8,128)(2,1)S(1)} %get-tuple-element.84._), channel_id=1, source_target_pairs={{0,4},{2,6},{4,0},{6,2},{8,12},{10,14},{12,8},{14,10},{16,20},{18,... | collective-permute-start | bytes 786440 | tf_op jit(solution)/shard_map/ppermute | solution.py:305
  18.5 2.5 %copy-start.8 = (s32[1,1,80,128,128]{4,3,2,1,0:T(8,128)S(1)}, s32[1,1,80,128,128]{4,3,2,1,0:T(8,128)}, u32[]{:S(2)}) copy-start(s32[1,1,80,128,128]{4,3,2,1,0:T(8,128)} %param.16) | copy-start | bytes 15728644
  21.0 5.8 %copy-start.23 = (s32[1,128]{1,0:T(1,128)S(1)}, s32[1,128]{1,0:T(1,128)}, u32[]{:S(2)}) copy-start(s32[1,128]{1,0:T(1,128)} %cats_ref.1) | copy-start | bytes 1540
  21.0 5.8 %copy-start.22 = (bf16[128,256]{1,0:T(8,128)(2,1)S(1)}, bf16[128,256]{1,0:T(8,128)(2,1)}, u32[]{:S(2)}) copy-start(bf16[128,256]{1,0:T(8,128)(2,1)} %get-tuple-element.40) | copy-start | bytes 196612
  23.3 3.3 %copy-start = (bf16[2048,2048]{1,0:T(8,128)(2,1)}, bf16[2048,2048]{1,0:T(8,128)(2,1)S(1)}, u32[]{:S(2)}) copy-start(bf16[2048,2048]{1,0:T(8,128)(2,1)S(1)} %place_tiles.1.dense_ref) | copy-start | bytes 25165828
  26.7 9.3 %collective-permute-start.4 = (bf16[1024,256]{1,0:T(8,128)(2,1)S(1)}, bf16[1024,256]{1,0:T(8,128)(2,1)S(1)}, u32[]{:S(2)}, u32[]{:S(2)}) collective-permute-start(bf16[1024,256]{1,0:T(8,128)(2,1)S(1)} %constant_dynamic-update-slice_fusion.4.same_ref), channel_id=1, source_target_pairs={{0,2},{2,0},{4,6},{6,4},{8,10},{10,8},{12,14},{14,12},{16,18},{18,... | collective-permute-start | bytes 1572872 | tf_op jit(solution)/shard_map/ppermute | solution.py:305
  26.8 6.9 %collective-permute-start.7 = (bf16[128,256]{1,0:T(8,128)(2,1)S(1)}, bf16[128,256]{1,0:T(8,128)(2,1)S(1)}, u32[]{:S(2)}, u32[]{:S(2)}) collective-permute-start(bf16[128,256]{1,0:T(8,128)(2,1)S(1)} %copy-done.22), channel_id=1, source_target_pairs={{0,24},{2,26},{4,28},{6,30},{8,16},{10,18},{12,20},{14,22},{16,8},... | collective-permute-start | bytes 196616 | tf_op jit(solution)/shard_map/ppermute | solution.py:305
  28.4 7.6 %collective-permute-start.6 = (bf16[128,256]{1,0:T(8,128)(2,1)S(1)}, bf16[128,256]{1,0:T(8,128)(2,1)S(1)}, u32[]{:S(2)}, u32[]{:S(2)}) collective-permute-start(bf16[128,256]{1,0:T(8,128)(2,1)S(1)} %copy-done.22), channel_id=1, source_target_pairs={{0,16},{2,18},{4,20},{6,22},{8,24},{10,26},{12,28},{14,30},{16,0},... | collective-permute-start | bytes 196616 | tf_op jit(solution)/shard_map/ppermute | solution.py:305
  28.4 7.6 %collective-permute-start.5 = (bf16[128,256]{1,0:T(8,128)(2,1)S(1)}, bf16[128,256]{1,0:T(8,128)(2,1)S(1)}, u32[]{:S(2)}, u32[]{:S(2)}) collective-permute-start(bf16[128,256]{1,0:T(8,128)(2,1)S(1)} %copy-done.22), channel_id=1, source_target_pairs={{0,8},{2,10},{4,12},{6,14},{8,0},{10,2},{12,4},{14,6},{16,24},{18,... | collective-permute-start | bytes 196616 | tf_op jit(solution)/shard_map/ppermute | solution.py:305
  36.0 3.4 %copy-start.1 = (bf16[2048,2048]{1,0:T(8,128)(2,1)S(1)}, bf16[2048,2048]{1,0:T(8,128)(2,1)}, u32[]{:S(2)}) copy-start(bf16[2048,2048]{1,0:T(8,128)(2,1)} %copy-done) | copy-start | bytes 25165828
  39.4 12.7 %copy-start.20 = (bf16[1,128,512]{2,1,0:T(8,128)(2,1)S(1)}, bf16[1,128,512]{2,1,0:T(8,128)(2,1)}, u32[]{:S(2)}) copy-start(bf16[1,128,512]{2,1,0:T(8,128)(2,1)} %param.12) | copy-start | bytes 393220
  43.6 8.3 %collective-permute-start.11 = (bf16[512,256]{1,0:T(8,128)(2,1)S(1)}, bf16[512,256]{1,0:T(8,128)(2,1)S(1)}, u32[]{:S(2)}, u32[]{:S(2)}) collective-permute-start(bf16[512,256]{1,0:T(8,128)(2,1)S(1)} %pad_maximum_fusion.3), channel_id=1, source_target_pairs={{0,4},{2,6},{4,0},{6,2},{8,12},{10,14},{12,8},{14,10},{16,20},{18,... | collective-permute-start | bytes 786440 | tf_op jit(solution)/shard_map/ppermute | solution.py:305
  44.0 28.7 %collective-permute-start.13 = (bf16[2048,256]{1,0:T(8,128)(2,1)S(1)}, bf16[2048,256]{1,0:T(8,128)(2,1)S(1)}, u32[]{:S(2)}, u32[]{:S(2)}) collective-permute-start(bf16[2048,256]{1,0:T(8,128)(2,1)S(1)} %get-tuple-element.39.rest_0_), channel_id=1, source_target_pairs={{0,1},{1,0},{2,3},{3,2},{4,5},{5,4},{6,7},{7,6},{8,9},{9,8},{10,11... | collective-permute-start | bytes 3145736 | tf_op jit(solution)/shard_map/ppermute | solution.py:329
  51.9 16.1 %collective-permute-start.12 = (bf16[1024,256]{1,0:T(8,128)(2,1)S(1)}, bf16[1024,256]{1,0:T(8,128)(2,1)S(1)}, u32[]{:S(2)}, u32[]{:S(2)}) collective-permute-start(bf16[1024,256]{1,0:T(8,128)(2,1)S(1)} %constant_dynamic-update-slice_fusion.9.same_ref), channel_id=1, source_target_pairs={{0,2},{2,0},{4,6},{6,4},{8,10},{10,8},{12,14},{14,12},{16,18},{18,... | collective-permute-start | bytes 1572872 | tf_op jit(solution)/shard_map/ppermute | solution.py:305
  52.1 9.0 %collective-permute-start.10 = (bf16[128,640]{1,0:T(8,128)(2,1)S(1)}, bf16[128,640]{1,0:T(8,128)(2,1)S(1)}, u32[]{:S(2)}, u32[]{:S(2)}) collective-permute-start(bf16[128,640]{1,0:T(8,128)(2,1)S(1)} %pad_maximum_fusion.4), channel_id=1, source_target_pairs={{0,24},{2,26},{4,28},{6,30},{8,16},{10,18},{12,20},{14,22},{16,8},... | collective-permute-start | bytes 491528 | tf_op jit(solution)/shard_map/ppermute | solution.py:305
  53.9 14.1 %collective-permute-start.9 = (bf16[128,640]{1,0:T(8,128)(2,1)S(1)}, bf16[128,640]{1,0:T(8,128)(2,1)S(1)}, u32[]{:S(2)}, u32[]{:S(2)}) collective-permute-start(bf16[128,640]{1,0:T(8,128)(2,1)S(1)} %pad_maximum_fusion.4), channel_id=1, source_target_pairs={{0,16},{2,18},{4,20},{6,22},{8,24},{10,26},{12,28},{14,30},{16,0},... | collective-permute-start | bytes 491528 | tf_op jit(solution)/shard_map/ppermute | solution.py:305
  53.9 14.1 %collective-permute-start.8 = (bf16[128,640]{1,0:T(8,128)(2,1)S(1)}, bf16[128,640]{1,0:T(8,128)(2,1)S(1)}, u32[]{:S(2)}, u32[]{:S(2)}) collective-permute-start(bf16[128,640]{1,0:T(8,128)(2,1)S(1)} %pad_maximum_fusion.4), channel_id=1, source_target_pairs={{0,8},{2,10},{4,12},{6,14},{8,0},{10,2},{12,4},{14,6},{16,24},{18,... | collective-permute-start | bytes 491528 | tf_op jit(solution)/shard_map/ppermute | solution.py:305
  72.7 27.8 %copy-start.2 = (bf16[2048,512]{1,0:T(8,128)(2,1)S(1)}, bf16[2048,512]{1,0:T(8,128)(2,1)}, u32[]{:S(2)}) copy-start(bf16[2048,512]{1,0:T(8,128)(2,1)} %user_ref.7) | copy-start | bytes 6291460
  72.7 27.8 %copy-start.17 = (f32[512]{0:T(512)S(1)}, f32[512]{0:T(512)}, u32[]{:S(2)}) copy-start(f32[512]{0:T(512)} %param.11) | copy-start | bytes 6148
  73.7 16.5 %collective-permute-start.16 = (bf16[512,640]{1,0:T(8,128)(2,1)S(1)}, bf16[512,640]{1,0:T(8,128)(2,1)S(1)}, u32[]{:S(2)}, u32[]{:S(2)}) collective-permute-start(bf16[512,640]{1,0:T(8,128)(2,1)S(1)} %pad_maximum_fusion.1), channel_id=1, source_target_pairs={{0,4},{2,6},{4,0},{6,2},{8,12},{10,14},{12,8},{14,10},{16,20},{18,... | collective-permute-start | bytes 1966088 | tf_op jit(solution)/shard_map/ppermute | solution.py:305
  74.4 30.8 %collective-permute-start.14 = (bf16[1024,256]{1,0:T(8,128)(2,1)}, bf16[1024,256]{1,0:T(8,128)(2,1)}, u32[]{:S(2)}, u32[]{:S(2)}) collective-permute-start(bf16[1024,256]{1,0:T(8,128)(2,1)} %get-tuple-element.47.rest_2_), channel_id=1, source_target_pairs={{0,1},{1,0},{2,3},{3,2},{4,5},{5,4},{6,7},{7,6},{8,9},{9,8},{10,11... | collective-permute-start | bytes 1572872 | tf_op jit(solution)/shard_map/ppermute | solution.py:329
  91.1 20.9 %collective-permute-start.17 = (bf16[1024,640]{1,0:T(8,128)(2,1)}, bf16[1024,640]{1,0:T(8,128)(2,1)}, u32[]{:S(2)}, u32[]{:S(2)}) collective-permute-start(bf16[1024,640]{1,0:T(8,128)(2,1)} %constant_dynamic-update-slice_fusion.11.same_ref), channel_id=1, source_target_pairs={{0,2},{2,0},{4,6},{6,4},{8,10},{10,8},{12,14},{14,12},{16,18},{18,... | collective-permute-start | bytes 3932168 | tf_op jit(solution)/shard_map/ppermute | solution.py:305
  91.1 9.4 %collective-permute-start.18 = (bf16[512,256]{1,0:T(8,128)(2,1)}, bf16[512,256]{1,0:T(8,128)(2,1)}, u32[]{:S(2)}, u32[]{:S(2)}) collective-permute-start(bf16[512,256]{1,0:T(8,128)(2,1)} %get-tuple-element.55.rest_2_), channel_id=1, source_target_pairs={{0,1},{1,0},{2,3},{3,2},{4,5},{5,4},{6,7},{7,6},{8,9},{9,8},{10,11... | collective-permute-start | bytes 786440 | tf_op jit(solution)/shard_map/ppermute | solution.py:329
  92.6 22.1 %collective-permute-start.15 = (bf16[512,256]{1,0:T(8,128)(2,1)S(1)}, bf16[512,256]{1,0:T(8,128)(2,1)S(1)}, u32[]{:S(2)}, u32[]{:S(2)}) collective-permute-start(bf16[512,256]{1,0:T(8,128)(2,1)S(1)} %get-tuple-element.50.rest_2_), channel_id=1, source_target_pairs={{0,1},{1,0},{2,3},{3,2},{4,5},{5,4},{6,7},{7,6},{8,9},{9,8},{10,11... | collective-permute-start | bytes 786440 | tf_op jit(solution)/shard_map/ppermute | solution.py:329
  103.3 1.9 %copy-start.4 = (bf16[2048,512]{1,0:T(8,128)(2,1)S(1)}, bf16[2048,512]{1,0:T(8,128)(2,1)}, u32[]{:S(2)}) copy-start(bf16[2048,512]{1,0:T(8,128)(2,1)} %grad_ref.7) | copy-start | bytes 6291460
  103.3 5.9 %slice-start = ((s8[8388608]{0:T(1024)(128)(4,1)}), s8[4194304]{0:T(1024)(128)(4,1)S(1)}, s32[]{:S(2)}) async-start(s8[8388608]{0:T(1024)(128)(4,1)} %bitcast.97), calls=%async_computation.1 | async-start | bytes 8388608
  105.2 12.9 %copy-start.9 = (bf16[512,512]{1,0:T(8,128)(2,1)}, bf16[512,512]{1,0:T(8,128)(2,1)S(1)}, u32[]{:S(2)}) copy-start(bf16[512,512]{1,0:T(8,128)(2,1)S(1)} %get-tuple-element.56) | copy-start | bytes 1572868
  105.2 4.1 %slice-start.1 = ((s8[8388608]{0:T(1024)(128)(4,1)}), s8[4194304]{0:T(1024)(128)(4,1)S(1)}, s32[]{:S(2)}) async-start(s8[8388608]{0:T(1024)(128)(4,1)} %bitcast.97), calls=%async_computation.2 | async-start | bytes 8388608
  107.4 3.3 %copy-start.11 = (bf16[512,512]{1,0:T(8,128)(2,1)}, bf16[512,512]{1,0:T(8,128)(2,1)S(1)}, u32[]{:S(2)}) copy-start(bf16[512,512]{1,0:T(8,128)(2,1)S(1)} %get-tuple-element.49) | copy-start | bytes 1572868
  111.9 2.9 %copy-start.7 = (bf16[2048,256]{1,0:T(8,128)(2,1)S(1)}, bf16[2048,256]{1,0:T(8,128)(2,1)}, u32[]{:S(2)}) copy-start(bf16[2048,256]{1,0:T(8,128)(2,1)} %copy-done.5) | copy-start | bytes 3145732
  117.9 2.0 %collective-permute-start.19 = (bf16[2,2,2,16,2048]{4,3,0,1,2:T(8,128)(2,1)S(1)}, bf16[2,2,2,16,2048]{4,3,0,1,2:T(8,128)(2,1)S(1)}, u32[]{:S(2)}, u32[]{:S(2)}) collective-permute-start(bf16[2,2,2,16,2048]{4,3,0,1,2:T(8,128)(2,1)S(1)} %fusion.21), channel_id=1, source_target_pairs={{0,2},{2,0},{4,6},{6,4},{8,10},{10,8},{12,14},{14,12},{16,18},{18,... | collective-permute-start | bytes 1572872 | tf_op jit(solution)/shard_map/ppermute | solution.py:305
  118.9 2.1 %collective-permute-start.21 = (bf16[2,2,2,16,2048]{4,3,0,2,1:T(8,128)(2,1)S(1)}, bf16[2,2,2,16,2048]{4,3,0,2,1:T(8,128)(2,1)S(1)}, u32[]{:S(2)}, u32[]{:S(2)}) collective-permute-start(bf16[2,2,2,16,2048]{4,3,0,2,1:T(8,128)(2,1)S(1)} %fusion.22), channel_id=1, source_target_pairs={{0,2},{2,0},{4,6},{6,4},{8,10},{10,8},{12,14},{14,12},{16,18},{18,... | collective-permute-start | bytes 1572872 | tf_op jit(solution)/shard_map/ppermute | solution.py:305
  120.1 8.4 %collective-permute-start.20 = (bf16[2,2,16,2048]{3,2,0,1:T(8,128)(2,1)S(1)}, bf16[2,2,16,2048]{3,2,0,1:T(8,128)(2,1)S(1)}, u32[]{:S(2)}, u32[]{:S(2)}) collective-permute-start(bf16[2,2,16,2048]{3,2,0,1:T(8,128)(2,1)S(1)} %fusion.31), channel_id=1, source_target_pairs={{0,4},{2,6},{4,0},{6,2},{8,12},{10,14},{12,8},{14,10},{16,20},{18,... | collective-permute-start | bytes 786440 | tf_op jit(solution)/shard_map/ppermute | solution.py:305
  121.1 8.7 %collective-permute-start.22 = (bf16[2,2,16,2048]{3,2,0,1:T(8,128)(2,1)S(1)}, bf16[2,2,16,2048]{3,2,0,1:T(8,128)(2,1)S(1)}, u32[]{:S(2)}, u32[]{:S(2)}) collective-permute-start(bf16[2,2,16,2048]{3,2,0,1:T(8,128)(2,1)S(1)} %fusion.32), channel_id=1, source_target_pairs={{0,8},{2,10},{4,12},{6,14},{8,0},{10,2},{12,4},{14,6},{16,24},{18,... | collective-permute-start | bytes 786440 | tf_op jit(solution)/shard_map/ppermute | solution.py:305
  129.9 5.0 %collective-permute-start.23 = (bf16[2,16,2048]{2,1,0:T(8,128)(2,1)S(1)}, bf16[2,16,2048]{2,1,0:T(8,128)(2,1)S(1)}, u32[]{:S(2)}, u32[]{:S(2)}) collective-permute-start(bf16[2,16,2048]{2,1,0:T(8,128)(2,1)S(1)} %fusion.35), channel_id=1, source_target_pairs={{0,8},{2,10},{4,12},{6,14},{8,0},{10,2},{12,4},{14,6},{16,24},{18,... | collective-permute-start | bytes 393224 | tf_op jit(solution)/shard_map/ppermute | solution.py:305
  130.3 5.0 %collective-permute-start.24 = (bf16[2,16,2048]{2,1,0:T(8,128)(2,1)S(1)}, bf16[2,16,2048]{2,1,0:T(8,128)(2,1)S(1)}, u32[]{:S(2)}, u32[]{:S(2)}) collective-permute-start(bf16[2,16,2048]{2,1,0:T(8,128)(2,1)S(1)} %fusion.36), channel_id=1, source_target_pairs={{0,4},{2,6},{4,0},{6,2},{8,12},{10,14},{12,8},{14,10},{16,20},{18,... | collective-permute-start | bytes 393224 | tf_op jit(solution)/shard_map/ppermute | solution.py:305
  135.4 7.8 %collective-permute-start.26 = (bf16[16,2048]{1,0:T(8,128)(2,1)S(1)}, bf16[16,2048]{1,0:T(8,128)(2,1)S(1)}, u32[]{:S(2)}, u32[]{:S(2)}) collective-permute-start(bf16[16,2048]{1,0:T(8,128)(2,1)S(1)} %fusion.40), channel_id=1, source_target_pairs={{0,16},{2,18},{4,20},{6,22},{8,24},{10,26},{12,28},{14,30},{16,0},... | collective-permute-start | bytes 196616 | tf_op jit(solution)/shard_map/ppermute | solution.py:305
  138.0 5.9 %collective-permute-start.25 = (bf16[16,2048]{1,0:T(8,128)(2,1)S(1)}, bf16[16,2048]{1,0:T(8,128)(2,1)S(1)}, u32[]{:S(2)}, u32[]{:S(2)}) collective-permute-start(bf16[16,2048]{1,0:T(8,128)(2,1)S(1)} %fusion.39), channel_id=1, source_target_pairs={{0,16},{2,18},{4,20},{6,22},{8,24},{10,26},{12,28},{14,30},{16,0},... | collective-permute-start | bytes 196616 | tf_op jit(solution)/shard_map/ppermute | solution.py:305
  144.0 5.4 %copy-start.12 = (bf16[512,512]{1,0:T(8,128)(2,1)S(1)}, bf16[512,512]{1,0:T(8,128)(2,1)}, u32[]{:S(2)}) copy-start(bf16[512,512]{1,0:T(8,128)(2,1)} %copy-done.11) | copy-start | bytes 1572868
  144.0 5.4 %copy-start.14 = (bf16[512,512]{1,0:T(8,128)(2,1)S(1)}, bf16[512,512]{1,0:T(8,128)(2,1)}, u32[]{:S(2)}) copy-start(bf16[512,512]{1,0:T(8,128)(2,1)} %copy-done.13) | copy-start | bytes 1572868
  144.8 4.7 %copy-start.10 = (bf16[512,512]{1,0:T(8,128)(2,1)S(1)}, bf16[512,512]{1,0:T(8,128)(2,1)}, u32[]{:S(2)}) copy-start(bf16[512,512]{1,0:T(8,128)(2,1)} %copy-done.9) | copy-start | bytes 1572868
  144.8 4.7 %copy-start.16 = (bf16[512,512]{1,0:T(8,128)(2,1)S(1)}, bf16[512,512]{1,0:T(8,128)(2,1)}, u32[]{:S(2)}) copy-start(bf16[512,512]{1,0:T(8,128)(2,1)} %copy-done.15) | copy-start | bytes 1572868
  145.8 14.1 %all-to-all-start = ((bf16[16,66,128]{2,1,0:T(8,128)(2,1)}), bf16[16,66,128]{2,1,0:T(8,128)(2,1)S(1)}, u32[]{:S(2)}, u32[]{:S(2)}) async-start(bf16[16,66,128]{2,1,0:T(8,128)(2,1)} %copy.53), calls=%async_computation | async-start | bytes 589824 | tf_op jit(solution)/shard_map/all_to_all | solution.py:460
  160.7 1.7 %copy-start.19 = (bf16[4,512,512]{2,1,0:T(8,128)(2,1)S(1)}, bf16[4,512,512]{2,1,0:T(8,128)(2,1)}, u32[]{:S(2)}) copy-start(bf16[4,512,512]{2,1,0:T(8,128)(2,1)} %weight_ref.1) | copy-start | bytes 6291460
  (6 other events, 7.2 us)

commit v6 on v3

--- a/solution.py
+++ b/solution.py
@@ -15,12 +15,14 @@
 MIB = 1024 * 1024
 
 
-def place_tiles(item_blocks, place_ref, count_ref, level_ref, dense_ref):
+def place_tiles(item_blocks, place_ref, count_ref, order_ref, level_ref, dense_ref, next_ref):
     step = pl.program_id(0)
 
     @pl.when(step == 0)
     def _():
         dense_ref[...] = jnp.zeros_like(dense_ref)
+        for place in range(next_ref.shape[0]):
+            next_ref[place] = order_ref[place]
 
     for offset in range(level_ref.shape[0]):
         slot = step * level_ref.shape[0] + offset
@@ -34,19 +36,23 @@
             dense_ref[pl.ds(row, TILE), pl.ds(col, TILE)] = weights.astype(jnp.bfloat16)
 
 
-def dense_tiles(place, count, level, users, items):
+def dense_tiles(place, count, level, users, items, order):
     slots = level.shape[0]
     per_step = SLOTS_PER_STEP if slots % SLOTS_PER_STEP == 0 else 1
     return pl.pallas_call(
         functools.partial(place_tiles, items // TILE),
-        out_shape=jax.ShapeDtypeStruct((users, items), jnp.bfloat16),
+        out_shape=[
+            jax.ShapeDtypeStruct((users, items), jnp.bfloat16),
+            jax.ShapeDtypeStruct(order.shape, jnp.int32),
+        ],
         grid_spec=pltpu.PrefetchScalarGridSpec(
-            num_scalar_prefetch=2,
+            num_scalar_prefetch=3,
             grid=(slots // per_step,),
-            in_specs=[
-                pl.BlockSpec((per_step, TILE, TILE), lambda step, place_ref, count_ref: (step, 0, 0))
+            in_specs=[pl.BlockSpec((per_step, TILE, TILE), lambda step, *_: (step, 0, 0))],
+            out_specs=[
+                pl.BlockSpec((users, items), lambda step, *_: (0, 0)),
+                pl.BlockSpec(memory_space=pltpu.SMEM),
             ],
-            out_specs=pl.BlockSpec((users, items), lambda step, place_ref, count_ref: (0, 0)),
         ),
         compiler_params=pltpu.CompilerParams(
             dimension_semantics=("arbitrary",), vmem_limit_bytes=40 * MIB
@@ -57,7 +63,7 @@
             transcendentals=0,
         ),
         name="place_tiles",
-    )(place, count, level)
+    )(place, count, order, level)
 
 
 def project_own(first_ref, cats_ref, feat_ref, weight_ref, *rest):
@@ -133,40 +139,49 @@
 
 
 def spread(blocks, order_ref, same_ref, other_ref, dense_ref, *rest):
-    out_refs, all_ref, sems = rest[:-2], rest[-2], rest[-1]
+    out_refs, next_ref, all_ref = rest[:-2], rest[-2], rest[-1]
     step = pl.program_id(0)
 
     @pl.when(step == 0)
     def _():
-        fetch_in_order(
-            order_ref, (same_ref, other_ref), all_ref, [sems.at[place] for place in range(blocks)]
-        )
+        for place in range(blocks):
+            next_ref[place] = order_ref[place]
+        own = all_ref.shape[0] // blocks
+        for place in range(blocks):
+            source = (same_ref, other_ref)[2 * place // blocks]
+            start = pl.multiple_of(order_ref[place] * own, own)
+            all_ref[pl.ds(start, own)] = source[pl.ds((place % (blocks // 2)) * own, own)]
 
     product = jnp.dot(dense_ref[...], all_ref[...], preferred_element_type=jnp.float32)
-    for chunk, out_ref in enumerate(out_refs):
-
-        @pl.when(step == chunk)
+    rows, first = product.shape[0], 0
+    for out_ref in out_refs:
+        chunks = out_ref.shape[0] // rows
+
+        @pl.when((step >= first) & (step < first + chunks))
         def _():
-            out_ref[...] = product.astype(out_ref.dtype)
-
-
-def spread_items(order, queries, dense, first, chunks, rows):
+            start = pl.multiple_of((step - first) * rows, rows)
+            out_ref[pl.ds(start, rows)] = product.astype(out_ref.dtype)
+
+        first += chunks
+
+
+def spread_items(order, queries, dense, first, counts, rows):
     items = dense.shape[1]
     cols = queries[0].shape[1]
-    blocks = order.shape[0]
+    blocks, chunks = order.shape[0], sum(counts)
+    whole = lambda step, order_ref: (0, 0)
     return pl.pallas_call(
         functools.partial(spread, blocks),
-        out_shape=[jax.ShapeDtypeStruct((rows, cols), jnp.bfloat16)] * chunks,
+        out_shape=[jax.ShapeDtypeStruct((count * rows, cols), jnp.bfloat16) for count in counts]
+        + [jax.ShapeDtypeStruct((blocks,), jnp.int32)],
         grid_spec=pltpu.PrefetchScalarGridSpec(
             num_scalar_prefetch=1,
             grid=(chunks,),
-            in_specs=[pl.BlockSpec(memory_space=pl.ANY)] * 2
+            in_specs=[pl.BlockSpec(queries[0].shape, whole)] * 2
             + [pl.BlockSpec((rows, items), lambda step, order_ref: (first + step, 0))],
-            out_specs=[pl.BlockSpec((rows, cols), lambda step, order_ref: (0, 0))] * chunks,
-            scratch_shapes=[
-                pltpu.VMEM((items, cols), jnp.bfloat16),
-                pltpu.SemaphoreType.DMA((blocks,)),
-            ],
+            out_specs=[pl.BlockSpec((count * rows, cols), whole) for count in counts]
+            + [pl.BlockSpec(memory_space=pltpu.SMEM)],
+            scratch_shapes=[pltpu.VMEM((items, cols), jnp.bfloat16)],
         ),
         compiler_params=pltpu.CompilerParams(
             dimension_semantics=("arbitrary",), vmem_limit_bytes=24 * MIB
@@ -180,7 +195,11 @@
     )(order, *queries, dense)
 
 
-def order_items(blocks, order_ref, same_ref, other_ref, feat_ref, mask_ref, all_ref, sems):
+def order_items(
+    blocks, order_ref, same_ref, other_ref, feat_ref, mask_ref, next_ref, all_ref, sems
+):
+    for place in range(blocks):
+        next_ref[place] = order_ref[place]
     fetch_in_order(
         order_ref, (same_ref, other_ref), all_ref, [sems.at[place] for place in range(blocks)]
     )
@@ -201,6 +220,7 @@
         out_shape=[
             jax.ShapeDtypeStruct((items, width), jnp.bfloat16),
             jax.ShapeDtypeStruct((experts, own_width, items), jnp.bfloat16),
+            jax.ShapeDtypeStruct((blocks,), jnp.int32),
         ],
         grid_spec=pltpu.PrefetchScalarGridSpec(
             num_scalar_prefetch=1,
@@ -209,6 +229,7 @@
             out_specs=[
                 pl.BlockSpec((items, width), lambda step, order_ref: (0, 0)),
                 pl.BlockSpec((experts, own_width, items), lambda step, order_ref: (0, 0, 0)),
+                pl.BlockSpec(memory_space=pltpu.SMEM),
             ],
             scratch_shapes=[
                 pltpu.VMEM((items, packed[0].shape[1]), jnp.bfloat16),
@@ -216,7 +237,7 @@
             ],
         ),
         compiler_params=pltpu.CompilerParams(
-            dimension_semantics=("arbitrary",), vmem_limit_bytes=24 * MIB
+            dimension_semantics=("arbitrary",), vmem_limit_bytes=14 * MIB
         ),
         cost_estimate=pl.CostEstimate(
             flops=0, bytes_accessed=items * width * 6, transcendentals=0
@@ -306,31 +327,133 @@
     return lax.axis_index("user") ^ (layer * 4 + side * 2 + core)
 
 
-def scatter_sum(terms, size):
-    cores, sides = 2, 2
-    layers = size // (cores * sides)
+def scatter_sums(halves, size, beside):
+    bits = size.bit_length() - 1
     index = lax.axis_index("user")
-    core, side, layer = index % cores, (index // cores) % sides, index // (cores * sides)
-    rest = terms.shape[1:]
-    terms = terms.reshape((layers, sides, cores) + rest)
-    own = lax.dynamic_index_in_dim(terms, core, 2, keepdims=False)
-    away = lax.dynamic_index_in_dim(terms, 1 - core, 2, keepdims=False).astype(jnp.bfloat16)
-    terms = own + flip(away, size, 1).astype(jnp.float32)
-    own = lax.dynamic_index_in_dim(terms, side, 1, keepdims=False)
-    away = lax.dynamic_index_in_dim(terms, 1 - side, 1, keepdims=False).astype(jnp.bfloat16)
-    terms = own + flip(away, size, 2).astype(jnp.float32)
-    total = lax.dynamic_index_in_dim(terms, layer, 0, keepdims=False)
-    for other in range(1, layers):
-        away = lax.dynamic_index_in_dim(terms, layer ^ other, 0, keepdims=False)
-        arrived = flip(away.astype(jnp.bfloat16), size, other * cores * sides)
-        total = total + arrived.astype(jnp.float32)
-    return total
-
-
-def as_rows(value, size):
-    count = value.shape[1]
-    padded = -(-count // TILE) * TILE
-    return jnp.pad(value, ((0, 0), (0, padded - count))).reshape(size, padded // TILE, TILE)
+    orders = [list(range(bits)), [0, 2, 1] + list(range(3, bits))]
+    halves = [terms.reshape((2,) * bits + terms.shape[1:]) for terms in halves]
+    left = [list(reversed(range(bits))) for _ in halves]
+    for stage in range(bits):
+        for half, terms in enumerate(halves):
+            bit = orders[half][stage]
+            axis = left[half].index(bit)
+            left[half].remove(bit)
+            mine = (index >> bit) & 1
+            own = lax.dynamic_index_in_dim(terms, mine, axis, keepdims=False)
+            away = lax.dynamic_index_in_dim(terms, 1 - mine, axis, keepdims=False)
+            arrived = flip(away.astype(jnp.bfloat16), size, 1 << bit)
+            halves[half] = own + arrived.astype(jnp.float32)
+        if stage == 1:
+            *halves, beside = lax.optimization_barrier((*halves, beside))
+        elif 1 < stage < bits - 1:
+            halves = list(lax.optimization_barrier(tuple(halves)))
+    return halves, beside
+
+
+def pack(size, _, feat_ref, mask_ref, first_ref, second_ref, gain_ref, out_ref):
+    experts, own_width, items = mask_ref.shape
+    own = items // size
+    sums = jnp.concatenate([first_ref[...], second_ref[...]], axis=0).astype(jnp.bfloat16)
+    masked = jnp.concatenate([mask_ref[expert] * sums for expert in range(experts)], axis=0)
+    cols = jnp.dot(masked, feat_ref[...], preferred_element_type=jnp.float32)
+    cols = jnp.transpose(cols).astype(jnp.bfloat16)
+    gain = gain_ref[...].astype(jnp.bfloat16)
+    for place in range(size):
+        out_ref[place, :own_width] = sums[:, place * own : (place + 1) * own]
+        out_ref[place, own_width : 2 * own_width] = cols[place * own_width : (place + 1) * own_width]
+        out_ref[place, 2 * own_width :] = gain
+
+
+def packed_sums(order, feats, mask, halves, gain):
+    size = order.shape[0]
+    experts, own_width, items = mask.shape
+    own = items // size
+    gain = jnp.pad(gain.reshape(-1, own), ((0, 16 - gain.shape[0] // own), (0, 0)))
+    operands = (feats, mask, *halves, gain)
+    shape = (size, 2 * own_width + gain.shape[0], own)
+    specs = [
+        pl.BlockSpec(value.shape, lambda step, order_ref, rank=value.ndim: (0,) * rank)
+        for value in operands
+    ]
+    return pl.pallas_call(
+        functools.partial(pack, size),
+        out_shape=jax.ShapeDtypeStruct(shape, jnp.bfloat16),
+        grid_spec=pltpu.PrefetchScalarGridSpec(
+            num_scalar_prefetch=1,
+            grid=(1,),
+            in_specs=specs,
+            out_specs=pl.BlockSpec(shape, lambda step, order_ref: (0, 0, 0)),
+        ),
+        compiler_params=pltpu.CompilerParams(
+            dimension_semantics=("arbitrary",), vmem_limit_bytes=16 * MIB
+        ),
+        cost_estimate=pl.CostEstimate(
+            flops=2 * experts * own_width * items * feats.shape[1],
+            bytes_accessed=items * feats.shape[1] * 2,
+            transcendentals=0,
+        ),
+        name="packed_sums",
+    )(order, *operands)
+
+
+def unpack(first_ref, swapped_ref, weight_ref, cats_ref, item_ref, expert_ref, gain_ref):
+    size, _, own = swapped_ref.shape
+    experts, own_width, width = expert_ref.shape
+    part_width = own_width // HALVES
+    swapped = [swapped_ref[place].astype(jnp.float32) for place in range(size)]
+    sums = jnp.concatenate(
+        [
+            block[half * part_width : (half + 1) * part_width]
+            for half in range(HALVES)
+            for block in swapped
+        ],
+        axis=0,
+    ).astype(jnp.bfloat16)
+    total = jnp.zeros((width, own), jnp.float32)
+    for expert in range(experts):
+        part = jnp.dot(weight_ref[expert], sums, preferred_element_type=jnp.float32)
+        total = total + jnp.where(cats_ref[...] == first_ref[0] + expert, part, 0.0)
+    item_ref[...] = jnp.transpose(total).astype(item_ref.dtype)
+    cols = [jnp.transpose(block[own_width : 2 * own_width]) for block in swapped]
+    for expert in range(experts):
+        rows = [
+            block[start : start + part_width]
+            for start in range(expert * own_width, (expert + 1) * own_width, part_width)
+            for block in cols
+        ]
+        expert_ref[expert] = jnp.transpose(jnp.concatenate(rows, axis=0))
+    gain = swapped[0][2 * own_width :]
+    for block in swapped[1:]:
+        gain = gain + block[2 * own_width :]
+    gain_ref[...] = gain[: gain_ref.shape[0]]
+
+
+def unpacked(swapped, first_expert, weights, cats, own_width, gain_width):
+    own, width = swapped.shape[2], weights.shape[1]
+    experts = weights.shape[0]
+    operands = (swapped, weights, cats.reshape(1, own))
+    shapes = [(own, width), (experts, own_width, width), (gain_width // own, own)]
+    dtypes = [jnp.bfloat16, jnp.float32, jnp.float32]
+    whole = lambda shape: pl.BlockSpec(shape, lambda step, first_ref: (0,) * len(shape))
+    return pl.pallas_call(
+        unpack,
+        out_shape=[jax.ShapeDtypeStruct(*pair) for pair in zip(shapes, dtypes)],
+        grid_spec=pltpu.PrefetchScalarGridSpec(
+            num_scalar_prefetch=1,
+            grid=(1,),
+            in_specs=[whole(value.shape) for value in operands],
+            out_specs=[whole(shape) for shape in shapes],
+        ),
+        compiler_params=pltpu.CompilerParams(
+            dimension_semantics=("arbitrary",), vmem_limit_bytes=16 * MIB
+        ),
+        cost_estimate=pl.CostEstimate(
+            flops=2 * experts * own * width * width,
+            bytes_accessed=weights.size * 2,
+            transcendentals=0,
+        ),
+        name="unpacked",
+    )(first_expert.reshape(1), *operands)
 
 
 def on_device(
@@ -348,31 +471,38 @@
 
     own_halves = own_queries(first_expert, own_cats, own_feat, expert_w)
     order = gather_order(user_size)
-    dense = dense_tiles(tile_place[0, 0], tile_count[0], tile_level[0, 0], users, items)
+    dense, order = dense_tiles(
+        tile_place[0, 0], tile_count[0], tile_level[0, 0], users, items, order
+    )
     layers = [gather_layers(own, user_size) for own in own_halves]
-    layers[0], dense = lax.optimization_barrier((layers[0], dense))
+    layers[0], order = lax.optimization_barrier((layers[0], order))
     queries = [gather_sides(part, user_size) for part in layers]
 
+    partials = [[] for _ in range(HALVES)]
+    for half in range(HALVES):
+        for first, count in ((0, 1), (1, ROW_CHUNKS - 1)):
+            *products, last = spread_items(order, queries[half], dense, first, (1,) * count, rows)
+            for product in products:
+                pieces = [product]
+                for shift in range(1, item_size):
+                    pairs = [(source, (source + shift) % item_size) for source in range(item_size)]
+                    pieces.append(lax.ppermute(product, "item", pairs))
+                partials[half].append(pieces)
     local_cats = (own_cats - first_expert).astype(jnp.bfloat16)
+    arrived = partials[0][0]
+    local_cats, arrived[-1] = lax.optimization_barrier((local_cats, arrived[-1]))
     packed = jnp.concatenate(
         [own_feat, jnp.broadcast_to(local_cats[:, None], (own_items, TILE))], axis=1
     )
-    packed, _ = lax.optimization_barrier((packed, queries[-1][1]))
-    packed = gather_sides(gather_layers(packed, user_size), user_size)
+    packed = gather_layers(packed, user_size)
+    arrived = partials[1][1]
+    packed, arrived[-1] = lax.optimization_barrier((packed, arrived[-1]))
+    same = jnp.concatenate([packed, flip(packed, user_size, 2)], axis=0)
+    arrived = partials[1][3]
+    same, arrived[-1] = lax.optimization_barrier((same, arrived[-1]))
+    packed = (same, flip(same, user_size, 1))
     own_width = width // user_size
-    feats, mask = ordered_items(order, packed, experts_here, own_width, width)
-
-    partials = []
-    for half in range(HALVES):
-        first = [0, 1] if half == 0 else [0]
-        partials.append([])
-        for start, end in zip(first, first[1:] + [ROW_CHUNKS]):
-            for partial in spread_items(order, queries[half], dense, start, end - start, rows):
-                pieces = [partial]
-                for shift in range(1, item_size):
-                    pairs = [(source, (source + shift) % item_size) for source in range(item_size)]
-                    pieces.append(lax.ppermute(partial, "item", pairs))
-                partials[half].append(pieces)
+    feats, mask, order = ordered_items(order, packed, experts_here, own_width, width)
 
     grads, gain_term, item_terms = [], 0.0, 0.0
     for chunk in range(ROW_CHUNKS):
@@ -394,7 +524,7 @@
                 preferred_element_type=jnp.float32,
             )
     part_width = own_width // HALVES
-    sums = []
+    halves = []
     for half in range(HALVES):
         part = slice(half * half_width, (half + 1) * half_width)
         terms = item_terms[part] + lax.dot_general(
@@ -403,9 +533,8 @@
             (((0,), (0,)), ((), ())),
             preferred_element_type=jnp.float32,
         )
-        terms = terms.reshape(user_size, part_width, items)
-        sums.append(scatter_sum(terms, user_size).astype(jnp.bfloat16))
-    sums = jnp.concatenate(sums, axis=0)
+        halves.append(terms.reshape(user_size, part_width, items))
+    halves, order = scatter_sums(halves, user_size, order)
 
     col_width = width // item_size
     user_grad = jnp.concatenate(
@@ -414,52 +543,12 @@
     )
     gain_own = lax.dynamic_slice_in_dim(gain_term, item_index * col_width, col_width, 0)
 
-    masked = mask * sums[None]
-    expert_cols = lax.dot_general(
-        feats,
-        masked.reshape(experts_here * own_width, items),
-        (((0,), (1,)), ((), ())),
-        preferred_element_type=jnp.float32,
-    ).astype(jnp.bfloat16)
-    by_item = sums.reshape(own_width, user_size, own_items).transpose(1, 0, 2)
-    gain_sent = jnp.broadcast_to(gain_own.astype(jnp.bfloat16)[None], (user_size, col_width))
-    pieces = [
-        as_rows(by_item.reshape(user_size, -1), user_size),
-        as_rows(expert_cols.reshape(user_size, -1), user_size),
-        as_rows(gain_sent, user_size),
-    ]
-    swapped = lax.all_to_all(jnp.concatenate(pieces, axis=1), "user", 0, 0)
-    ends = [pieces[0].shape[1], pieces[0].shape[1] + pieces[1].shape[1]]
-
-    own_sums = (
-        swapped[:, : ends[0]]
-        .reshape(user_size, HALVES, part_width, own_items)
-        .transpose(1, 0, 2, 3)
-        .reshape(width, own_items)
-    )
-    expert_grad = (
-        swapped[:, ends[0] : ends[1]]
-        .reshape(user_size, own_width, experts_here, HALVES, part_width)
-        .transpose(2, 1, 3, 0, 4)
-        .reshape(experts_here, own_width, width)
-        .astype(jnp.float32)
-    )
-    gain_grad = jnp.sum(
-        swapped[:, ends[1] :].reshape(user_size, -1)[:, :col_width].astype(jnp.float32), axis=0
-    )
-    item_total = jnp.zeros((own_items, width), jnp.float32)
-    for expert in range(experts_here):
-        item_total = item_total + jnp.where(
-            (own_cats == first_expert + expert)[:, None],
-            lax.dot_general(
-                own_sums,
-                expert_w[expert],
-                (((0,), (1,)), ((), ())),
-                preferred_element_type=jnp.float32,
-            ),
-            0.0,
-        )
-    return (user_grad, item_total.astype(jnp.bfloat16)[None], expert_grad, gain_grad)
+    sent = packed_sums(order, feats, mask, halves, gain_own)
+    swapped = lax.all_to_all(sent, "user", 0, 0)
+    item_grad, expert_grad, gain_grad = unpacked(
+        swapped, first_expert, expert_w, own_cats, own_width, col_width
+    )
+    return (user_grad, item_grad[None], expert_grad, gain_grad.reshape(col_width))
 
 
 def solution(mesh):

time: 145 us -> 152 us (1.048)
  waiting for transfers between devices: 53.2 us -> 62.7 us
  starting transfers between devices: 45.1 us -> 40.6 us
  local copies, waits for them, and re-layouts: 7.91 us -> 11.8 us
  matrix products: 8.3 us -> 5.48 us
  Pallas kernels: 25.6 us -> 27.7 us
    ppermute x25 -> x23, waiting for transfers between devices: 21.5 us -> 43.9 us  [flip(): lax.ppermute(value, 'user', [(source, source ^ bits) for source in range(...]
    ppermute x8, waiting for transfers between devices: 22.4 us -> 10.9 us  [on_device(): pieces.append(lax.ppermute(product, 'item', pairs))]
    ppermute x25 -> x23, starting transfers between devices: 32.1 us -> 26.8 us  [flip(): lax.ppermute(value, 'user', [(source, source ^ bits) for source in range(...]
    unnamed x32 -> x37, local copies, waits for them, and re-layouts: 4.81 us -> 9.27 us
    pallas_call x1 -> x3, Pallas kernels: 2.19 us -> 6.04 us  [the longest x1 2.73 us: dense_tiles(): pl.pallas_call(functools.partial(place_tiles, items // TILE), out_shape=[...]
    dot_general x5 -> x0, matrix products: 2.68 us -> none  [the longest x4 1.92 us: on_device(): lax.dot_general(own_sums, expert_w[expert], (((0,), (1,)), ((), ())), pre...]
    pallas_call x3 -> x4, Pallas kernels: 12.3 us -> 10.3 us  [spread_items(): pl.pallas_call(functools.partial(spread, blocks), out_shape=[jax.ShapeDty...]
    dynamic_slice x2, local copies, waits for them, and re-layouts: 0.09 us -> 2.13 us  [on_device(): lax.dynamic_slice_in_dim(grad, item_index * col_width, col_width, 1)]
  transfers between devices with their start and end apart: 34 -> 32, of which waited for: 16 -> 14; matrix products, arithmetic and copies ran while one was open for 6% -> 6% of each run, Pallas kernels for 12% -> 10%
where the time goes in v6:
time: 152 us
  waiting for transfers between devices  62.7 us (41%)
  starting transfers between devices  40.6 us (27%)
  Pallas kernels  27.7 us (18%)
  local copies, waits for them, and re-layouts  11.8 us (8%)
  matrix products  5.48 us (4%)
  between operations  1.86 us (1%)
  other arithmetic  1.72 us (1%)
    ppermute x23, waiting for transfers between devices, flip(): lax.ppermute(value, 'user', [(source, source ^ bits) for source in range(...  43.9 us
    ppermute x23, starting transfers between devices, flip(): lax.ppermute(value, 'user', [(source, source ^ bits) for source in range(...  26.8 us
    ppermute x8, waiting for transfers between devices, on_device(): pieces.append(lax.ppermute(product, 'item', pairs))  10.9 us
    pallas_call x4, Pallas kernels, spread_items(): pl.pallas_call(functools.partial(spread, blocks), out_shape=[jax.ShapeDty...  10.3 us
    ppermute x8, starting transfers between devices, on_device(): pieces.append(lax.ppermute(product, 'item', pairs))  9.82 us
    unnamed x37, local copies, waits for them, and re-layouts  9.27 us
    all_to_all x1, waiting for transfers between devices, on_device(): swapped = lax.all_to_all(sent, 'user', 0, 0)  7.91 us
    pallas_call x1, Pallas kernels, ordered_items(): pl.pallas_call(functools.partial(order_items, blocks), out_shape=[jax.Sha...  4.76 us
  transfers between devices with their start and end apart: 32, of which 14 were waited for; matrix products, arithmetic and copies ran while one was open for 6% of the time, Pallas kernels for 10%

profile of v6, /device:TPU:0, one launch (start us, length us, event | category | flops | bytes accessed | tf_op | source)
XLA Modules:
  0.0 151.9 jit_solution(10671645301458367340)
XLA Ops:
  0.6 3.6 %own_queries.1 = (bf16[128,256]{1,0:T(8,128)(2,1)}, bf16[128,256]{1,0:T(8,128)(2,1)}) custom-call(s32[1]{0:T(128)} %bitcast.1.first_ref, s32[1,128]{1,0:T(1,128)} %cats_ref.3, bf16[128,512]{1,0:T(8,128)(2,1)} %bitcast.61, bf16[4,512,512]{2,1,0:T(8,128)(2,1)} %weight_ref.3), custom_call_target="tpu_custom_call" | custom-call | flops 268435456 | bytes 2359296 | tf_op jit(solution)/shard_map/own_queries/pallas_call | solution.py:103
  4.3 5.0 %collective-permute-start.2 = (bf16[128,256]{1,0:T(8,128)(2,1)}, bf16[128,256]{1,0:T(8,128)(2,1)S(1)}, u32[]{:S(2)}, u32[]{:S(2)}) collective-permute-start(bf16[128,256]{1,0:T(8,128)(2,1)} %get-tuple-element.43), channel_id=1, source_target_pairs={{0,24},{2,26},{4,28},{6,30},{8,16},{10,18},{12,20},{14,22},{16,8},... | collective-permute-start | bytes 196616 | tf_op jit(solution)/shard_map/ppermute | solution.py:309
  9.9 1.5 collective-permute-start.6
  11.4 2.9 %collective-permute-start.7 = (bf16[128,256]{1,0:T(8,128)(2,1)}, bf16[128,256]{1,0:T(8,128)(2,1)S(1)}, u32[]{:S(2)}, u32[]{:S(2)}) collective-permute-start(bf16[128,256]{1,0:T(8,128)(2,1)} %get-tuple-element.50), channel_id=1, source_target_pairs={{0,16},{2,18},{4,20},{6,22},{8,24},{10,26},{12,28},{14,30},{16,0},... | collective-permute-start | bytes 196616 | tf_op jit(solution)/shard_map/ppermute | solution.py:309
  15.0 2.5 %copy-done.5 = s32[1,1,80,128,128]{4,3,2,1,0:T(8,128)S(1)} copy-done((s32[1,1,80,128,128]{4,3,2,1,0:T(8,128)S(1)}, s32[1,1,80,128,128]{4,3,2,1,0:T(8,128)}, u32[]{:S(2)}) %copy-start.5) | copy-done | bytes 5242904
  17.5 2.7 %place_tiles.1 = (bf16[2048,2048]{1,0:T(8,128)(2,1)S(1)}, s32[16]{0:T(128)S(1)}) custom-call(s32[80]{0:T(128)S(1)} %bitcast.56, s32[1]{0:T(128)} %bitcast.48.count_ref, s32[16]{0:T(128)S(1)} %fusion.32.order_ref, s32[80,128,128]{2,1,0:T(8,128)S(1)} %bitcast.51), custom_call_target="tpu_custom_call" | custom-call | flops 1310720 | bytes 13631488 | tf_op jit(solution)/shard_map/place_tiles/pallas_call | solution.py:42
  20.2 3.3 %copy-done = bf16[2048,2048]{1,0:T(8,128)(2,1)} copy-done((bf16[2048,2048]{1,0:T(8,128)(2,1)}, bf16[2048,2048]{1,0:T(8,128)(2,1)S(1)}, u32[]{:S(2)}) %copy-start) | copy-done | bytes 8388632
  23.8 1.6 %collective-permute-start.3 = (bf16[512,256]{1,0:T(8,128)(2,1)S(1)}, bf16[512,256]{1,0:T(8,128)(2,1)S(1)}, u32[]{:S(2)}, u32[]{:S(2)}) collective-permute-start(bf16[512,256]{1,0:T(8,128)(2,1)S(1)} %pad_maximum_fusion.3), channel_id=1, source_target_pairs={{0,4},{2,6},{4,0},{6,2},{8,12},{10,14},{12,8},{14,10},{16,20},{18,... | collective-permute-start | bytes 786440 | tf_op jit(solution)/shard_map/ppermute | solution.py:309
  25.4 4.2 %collective-permute-done.8 = bf16[128,256]{1,0:T(8,128)(2,1)S(1)} collective-permute-done((bf16[128,256]{1,0:T(8,128)(2,1)S(1)}, bf16[128,256]{1,0:T(8,128)(2,1)S(1)}, u32[]{:S(2)}, u32[]{:S(2)}) %collective-permute-start.8) | collective-permute-done | bytes 65568 | tf_op jit(solution)/shard_map/ppermute | solution.py:309
  29.7 1.7 %collective-permute-start.9 = (bf16[512,256]{1,0:T(8,128)(2,1)S(1)}, bf16[512,256]{1,0:T(8,128)(2,1)S(1)}, u32[]{:S(2)}, u32[]{:S(2)}) collective-permute-start(bf16[512,256]{1,0:T(8,128)(2,1)S(1)} %pad_maximum_fusion.4), channel_id=1, source_target_pairs={{0,4},{2,6},{4,0},{6,2},{8,12},{10,14},{12,8},{14,10},{16,20},{18,... | collective-permute-start | bytes 786440 | tf_op jit(solution)/shard_map/ppermute | solution.py:309
  31.5 4.8 %collective-permute-done.9 = bf16[512,256]{1,0:T(8,128)(2,1)S(1)} collective-permute-done((bf16[512,256]{1,0:T(8,128)(2,1)S(1)}, bf16[512,256]{1,0:T(8,128)(2,1)S(1)}, u32[]{:S(2)}, u32[]{:S(2)}) %collective-permute-start.9) | collective-permute-done | bytes 262176 | tf_op jit(solution)/shard_map/ppermute | solution.py:309
  36.5 3.4 %copy-done.1 = bf16[2048,2048]{1,0:T(8,128)(2,1)S(1)} copy-done((bf16[2048,2048]{1,0:T(8,128)(2,1)S(1)}, bf16[2048,2048]{1,0:T(8,128)(2,1)}, u32[]{:S(2)}) %copy-start.1) | copy-done | bytes 8388632
  39.8 1.7 %spread_items.4 = (bf16[512,256]{1,0:T(8,128)(2,1)S(1)}, s32[16]{0:T(128)}) custom-call(s32[16]{0:T(128)S(1)} %get-tuple-element.45.order_ref, bf16[1024,256]{1,0:T(8,128)(2,1)S(1)} %constant_dynamic-update-slice_fusion.same_ref, bf16[1024,256]{1,0:T(8,128)(2,1)S(1)} %collective-permute-done.4.other_ref, bf16[2048,2048]{1,0:T(8,128)(2,1)S(1)} %copy-done.1), custom_call_target="tpu_custom_call" | custom-call | flops 536870912 | bytes 3407872 | tf_op jit(solution)/shard_map/spread_items/pallas_call | solution.py:173
  41.5 2.1 %collective-permute-start.5 = (bf16[512,256]{1,0:T(8,128)(2,1)S(1)}, bf16[512,256]{1,0:T(8,128)(2,1)S(1)}, u32[]{:S(2)}, u32[]{:S(2)}) collective-permute-start(bf16[512,256]{1,0:T(8,128)(2,1)S(1)} %get-tuple-element.48.rest_0_), channel_id=1, source_target_pairs={{0,1},{1,0},{2,3},{3,2},{4,5},{5,4},{6,7},{7,6},{8,9},{9,8},{10,11... | collective-permute-start | bytes 786440 | tf_op jit(solution)/shard_map/ppermute | solution.py:489
  43.6 3.4 %spread_items.6 = (bf16[512,256]{1,0:T(8,128)(2,1)S(1)}, bf16[512,256]{1,0:T(8,128)(2,1)S(1)}, bf16[512,256]{1,0:T(8,128)(2,1)S(1)}, s32[16]{0:T(128)}) custom-call(s32[16]{0:T(128)S(1)} %get-tuple-element.45.order_ref, bf16[1024,256]{1,0:T(8,128)(2,1)S(1)} %constant_dynamic-update-slice_fusion.same_ref, ...), custom_call_target="tpu_custom_call" | custom-call | flops 1610612736 | bytes 8126464 | tf_op jit(solution)/shard_map/spread_items/pallas_call | solution.py:173
  47.1 3.4 %spread_items.7 = (bf16[512,256]{1,0:T(8,128)(2,1)S(1)}, bf16[512,256]{1,0:T(8,128)(2,1)S(1)}, bf16[512,256]{1,0:T(8,128)(2,1)S(1)}, s32[16]{0:T(128)}) custom-call(s32[16]{0:T(128)S(1)} %get-tuple-element.45.order_ref, bf16[1024,256]{1,0:T(8,128)(2,1)S(1)} %constant_dynamic-update-slice_fusion.2.same_ref, ...), custom_call_target="tpu_custom_call" | custom-call | flops 1610612736 | bytes 8126464 | tf_op jit(solution)/shard_map/spread_items/pallas_call | solution.py:173
  50.7 2.1 %collective-permute-start.18 = (bf16[512,256]{1,0:T(8,128)(2,1)S(1)}, bf16[512,256]{1,0:T(8,128)(2,1)S(1)}, u32[]{:S(2)}, u32[]{:S(2)}) collective-permute-start(bf16[512,256]{1,0:T(8,128)(2,1)S(1)} %get-tuple-element.59.rest_2_), channel_id=1, source_target_pairs={{0,1},{1,0},{2,3},{3,2},{4,5},{5,4},{6,7},{7,6},{8,9},{9,8},{10,11... | collective-permute-start | bytes 786440 | tf_op jit(solution)/shard_map/ppermute | solution.py:489
  52.7 1.7 %spread_items.5 = (bf16[512,256]{1,0:T(8,128)(2,1)S(1)}, s32[16]{0:T(128)}) custom-call(s32[16]{0:T(128)S(1)} %get-tuple-element.45.order_ref, bf16[1024,256]{1,0:T(8,128)(2,1)S(1)} %constant_dynamic-update-slice_fusion.2.same_ref, bf16[1024,256]{1,0:T(8,128)(2,1)S(1)} %collective-permute-done.10.other_ref, bf16[2048,2048]{1,0:T(8,128)(2,1)S(1)} %copy-done.1), custom_call_target="tpu_custom_call" | custom-call | flops 536870912 | bytes 3407872 | tf_op jit(solution)/shard_map/spread_items/pallas_call | solution.py:173
  54.5 2.0 %collective-permute-start.16 = (bf16[512,256]{1,0:T(8,128)(2,1)S(1)}, bf16[512,256]{1,0:T(8,128)(2,1)S(1)}, u32[]{:S(2)}, u32[]{:S(2)}) collective-permute-start(bf16[512,256]{1,0:T(8,128)(2,1)S(1)} %get-tuple-element.54.rest_2_), channel_id=1, source_target_pairs={{0,1},{1,0},{2,3},{3,2},{4,5},{5,4},{6,7},{7,6},{8,9},{9,8},{10,11... | collective-permute-start | bytes 786440 | tf_op jit(solution)/shard_map/ppermute | solution.py:489
  56.7 10.9 %collective-permute-done.11.rest_3_ = bf16[512,256]{1,0:T(8,128)(2,1)S(1)} collective-permute-done((bf16[512,256]{1,0:T(8,128)(2,1)S(1)}, bf16[512,256]{1,0:T(8,128)(2,1)S(1)}, u32[]{:S(2)}, u32[]{:S(2)}) %collective-permute-start.11) | collective-permute-done | bytes 262176 | tf_op jit(solution)/shard_map/ppermute | solution.py:489
  67.6 3.4 %collective-permute-start.15 = (bf16[128,640]{1,0:T(8,128)(2,1)S(1)}, bf16[128,640]{1,0:T(8,128)(2,1)S(1)}, u32[]{:S(2)}, u32[]{:S(2)}) collective-permute-start(bf16[128,640]{1,0:T(8,128)(2,1)S(1)} %pad_maximum_fusion.5), channel_id=1, source_target_pairs={{0,24},{2,26},{4,28},{6,30},{8,16},{10,18},{12,20},{14,22},{16,8},... | collective-permute-start | bytes 491528 | tf_op jit(solution)/shard_map/ppermute | solution.py:309
  71.9 0.9 collective-permute-start.13
  72.8 1.3 fusion.6
  74.9 1.8 %collective-permute-done.15 = bf16[128,640]{1,0:T(8,128)(2,1)S(1)} collective-permute-done((bf16[128,640]{1,0:T(8,128)(2,1)S(1)}, bf16[128,640]{1,0:T(8,128)(2,1)S(1)}, u32[]{:S(2)}, u32[]{:S(2)}) %collective-permute-start.15) | collective-permute-done | bytes 163872 | tf_op jit(solution)/shard_map/ppermute | solution.py:309
  76.6 1.9 %collective-permute-start.19 = (bf16[512,256]{1,0:T(8,128)(2,1)S(1)}, bf16[512,256]{1,0:T(8,128)(2,1)S(1)}, u32[]{:S(2)}, u32[]{:S(2)}) collective-permute-start(bf16[512,256]{1,0:T(8,128)(2,1)S(1)} %get-tuple-element.61.rest_0_), channel_id=1, source_target_pairs={{0,1},{1,0},{2,3},{3,2},{4,5},{5,4},{6,7},{7,6},{8,9},{9,8},{10,11... | collective-permute-start | bytes 786440 | tf_op jit(solution)/shard_map/ppermute | solution.py:489
  78.6 4.9 %collective-permute-done.14 = bf16[128,640]{1,0:T(8,128)(2,1)S(1)} collective-permute-done((bf16[128,640]{1,0:T(8,128)(2,1)S(1)}, bf16[128,640]{1,0:T(8,128)(2,1)S(1)}, u32[]{:S(2)}, u32[]{:S(2)}) %collective-permute-start.14) | collective-permute-done | bytes 163872 | tf_op jit(solution)/shard_map/ppermute | solution.py:309
  83.5 1.5 collective-permute-start.21
  85.0 1.4 collective-permute-start.20
  87.1 1.3 fusion.4
  88.4 1.4 add_add_fusion
  89.9 10.7 %collective-permute-done.20 = bf16[512,640]{1,0:T(8,128)(2,1)S(1)} collective-permute-done((bf16[512,640]{1,0:T(8,128)(2,1)S(1)}, bf16[512,640]{1,0:T(8,128)(2,1)S(1)}, u32[]{:S(2)}, u32[]{:S(2)}) %collective-permute-start.20) | collective-permute-done | bytes 655392 | tf_op jit(solution)/shard_map/ppermute | solution.py:309
  100.7 0.9 user_gradient.7
  104.5 1.0 collective-permute-start.23
  106.3 6.6 %collective-permute-done.23 = bf16[2,2,16,2048]{3,2,0,1:T(8,128)(2,1)S(1)} collective-permute-done((bf16[2,2,16,2048]{3,2,0,1:T(8,128)(2,1)S(1)}, bf16[2,2,16,2048]{3,2,0,1:T(8,128)(2,1)S(1)}, u32[]{:S(2)}, u32[]{:S(2)}) %collective-permute-start.23) | collective-permute-done | bytes 262176 | tf_op jit(solution)/shard_map/ppermute | solution.py:309
  113.0 1.2 collective-permute-done.25
  114.3 4.8 %order_items.1 = (bf16[2048,512]{1,0:T(8,128)(2,1)S(1)}, bf16[4,32,2048]{2,1,0:T(8,128)(2,1)S(1)}, s32[16]{0:T(128)S(1)}) custom-call(s32[16]{0:T(128)S(1)} %get-tuple-element.45.order_ref, bf16[1024,640]{1,0:T(8,128)(2,1)S(1)} %pad_maximum_fusion.same_ref, bf16[1024,640]{1,0:T(8,128)(2,1)S(1)} %collective-permute-done.26.other_ref), custom_call_target="tpu_custom_call" | custom-call | bytes 6291456 | tf_op jit(solution)/shard_map/order_items/pallas_call | solution.py:218
  119.4 1.3 collective-permute-start.28
  120.7 3.4 %collective-permute-done.27 = bf16[2,16,2048]{2,1,0:T(8,128)(2,1)S(1)} collective-permute-done((bf16[2,16,2048]{2,1,0:T(8,128)(2,1)S(1)}, bf16[2,16,2048]{2,1,0:T(8,128)(2,1)S(1)}, u32[]{:S(2)}, u32[]{:S(2)}) %collective-permute-start.27) | collective-permute-done | bytes 131104 | tf_op jit(solution)/shard_map/ppermute | solution.py:309
  124.5 3.3 %collective-permute-start.29 = (bf16[16,2048]{1,0:T(8,128)(2,1)S(1)}, bf16[16,2048]{1,0:T(8,128)(2,1)S(1)}, u32[]{:S(2)}, u32[]{:S(2)}) collective-permute-start(bf16[16,2048]{1,0:T(8,128)(2,1)S(1)} %fusion.24), channel_id=1, source_target_pairs={{0,16},{2,18},{4,20},{6,22},{8,24},{10,26},{12,28},{14,30},{16,0},... | collective-permute-start | bytes 196616 | tf_op jit(solution)/shard_map/ppermute | solution.py:309
  128.0 3.6 %collective-permute-done.29 = bf16[16,2048]{1,0:T(8,128)(2,1)S(1)} collective-permute-done((bf16[16,2048]{1,0:T(8,128)(2,1)S(1)}, bf16[16,2048]{1,0:T(8,128)(2,1)S(1)}, u32[]{:S(2)}, u32[]{:S(2)}) %collective-permute-start.29) | collective-permute-done | bytes 65568 | tf_op jit(solution)/shard_map/ppermute | solution.py:309
  131.6 1.9 %collective-permute-done.30 = bf16[16,2048]{1,0:T(8,128)(2,1)S(1)} collective-permute-done((bf16[16,2048]{1,0:T(8,128)(2,1)S(1)}, bf16[16,2048]{1,0:T(8,128)(2,1)S(1)}, u32[]{:S(2)}, u32[]{:S(2)}) %collective-permute-start.30) | collective-permute-done | bytes 65568 | tf_op jit(solution)/shard_map/ppermute | solution.py:309
  133.6 1.8 %packed_sums.1 = bf16[16,80,128]{2,1,0:T(8,128)(2,1)} custom-call(s32[16]{0:T(128)S(1)} %get-tuple-element.68._, bf16[2048,512]{1,0:T(8,128)(2,1)S(1)} %get-tuple-element.69.feat_ref, bf16[4,32,2048]{2,1,0:T(8,128)(2,1)S(1)} %get-tuple-element.70.mask_ref, f32[16,2048]{1,0:T(8,128)S(1)} %bitcast_add_fusion.7.first_ref, ...), custom_call_target="tpu_custom_call" | custom-call | flops 268435456 | bytes 2097152 | tf_op jit(solution)/shard_map/packed_sums/pallas_call | solution.py:378
  135.3 3.9 %all-to-all-start = ((bf16[16,80,128]{2,1,0:T(8,128)(2,1)}), bf16[16,80,128]{2,1,0:T(8,128)(2,1)S(1)}, u32[]{:S(2)}, u32[]{:S(2)}) async-start(bf16[16,80,128]{2,1,0:T(8,128)(2,1)} %packed_sums.1), calls=%async_computation | async-start | bytes 655360 | tf_op jit(solution)/shard_map/all_to_all | solution.py:547
  139.3 1.1 constant_dynamic-slice_fusion.10
  140.4 1.0 constant_dynamic-slice_fusion.8
  141.4 1.0 pad_maximum_fusion.1
  142.5 7.9 %all-to-all-done.swapped_ref = bf16[16,80,128]{2,1,0:T(8,128)(2,1)S(1)} async-done(((bf16[16,80,128]{2,1,0:T(8,128)(2,1)}), bf16[16,80,128]{2,1,0:T(8,128)(2,1)S(1)}, u32[]{:S(2)}, u32[]{:S(2)}) %all-to-all-start) | async-done | bytes 327712 | tf_op jit(solution)/shard_map/all_to_all | solution.py:547
  150.4 1.5 %unpacked.1 = (bf16[128,512]{1,0:T(8,128)(2,1)}, f32[4,32,512]{2,1,0:T(8,128)}, f32[2,128]{1,0:T(2,128)}) custom-call(s32[1]{0:T(128)} %bitcast.1.first_ref, bf16[16,80,128]{2,1,0:T(8,128)(2,1)S(1)} %all-to-all-done.swapped_ref, bf16[4,512,512]{2,1,0:T(8,128)(2,1)S(1)} %copy-done.4, s32[1,128]{1,0:T(1,128)S(1)} %copy-done.9), custom_call_target="tpu_custom_call" | custom-call | flops 268435456 | bytes 2097152 | tf_op jit(solution)/shard_map/unpacked/pallas_call | solution.py:438
  (103 shorter events, 8.7 us)
Async XLA Ops:
  0.6 14.3 %copy-start.10 = (s32[1,1,80]{2,1,0:T(1,128)S(1)}, s32[1,1,80]{2,1,0:T(1,128)}, u32[]{:S(2)}) copy-start(s32[1,1,80]{2,1,0:T(1,128)} %param.15) | copy-start | bytes 964
  4.3 19.2 %collective-permute-start.2 = (bf16[128,256]{1,0:T(8,128)(2,1)}, bf16[128,256]{1,0:T(8,128)(2,1)S(1)}, u32[]{:S(2)}, u32[]{:S(2)}) collective-permute-start(bf16[128,256]{1,0:T(8,128)(2,1)} %get-tuple-element.43), channel_id=1, source_target_pairs={{0,24},{2,26},{4,28},{6,30},{8,16},{10,18},{12,20},{14,22},{16,8},... | collective-permute-start | bytes 196616 | tf_op jit(solution)/shard_map/ppermute | solution.py:309
  9.3 14.5 %collective-permute-start.1 = (bf16[128,256]{1,0:T(8,128)(2,1)}, bf16[128,256]{1,0:T(8,128)(2,1)S(1)}, u32[]{:S(2)}, u32[]{:S(2)}) collective-permute-start(bf16[128,256]{1,0:T(8,128)(2,1)} %get-tuple-element.43), channel_id=1, source_target_pairs={{0,16},{2,18},{4,20},{6,22},{8,24},{10,26},{12,28},{14,30},{16,0},... | collective-permute-start | bytes 196616 | tf_op jit(solution)/shard_map/ppermute | solution.py:309
  9.3 14.5 %collective-permute-start = (bf16[128,256]{1,0:T(8,128)(2,1)}, bf16[128,256]{1,0:T(8,128)(2,1)S(1)}, u32[]{:S(2)}, u32[]{:S(2)}) collective-permute-start(bf16[128,256]{1,0:T(8,128)(2,1)} %get-tuple-element.43), channel_id=1, source_target_pairs={{0,8},{2,10},{4,12},{6,14},{8,0},{10,2},{12,4},{14,6},{16,24},{18,... | collective-permute-start | bytes 196616 | tf_op jit(solution)/shard_map/ppermute | solution.py:309
  9.9 15.5 %collective-permute-start.6 = (bf16[128,256]{1,0:T(8,128)(2,1)}, bf16[128,256]{1,0:T(8,128)(2,1)S(1)}, u32[]{:S(2)}, u32[]{:S(2)}) collective-permute-start(bf16[128,256]{1,0:T(8,128)(2,1)} %get-tuple-element.50), channel_id=1, source_target_pairs={{0,8},{2,10},{4,12},{6,14},{8,0},{10,2},{12,4},{14,6},{16,24},{18,... | collective-permute-start | bytes 196616 | tf_op jit(solution)/shard_map/ppermute | solution.py:309
  11.4 14.1 %collective-permute-start.7 = (bf16[128,256]{1,0:T(8,128)(2,1)}, bf16[128,256]{1,0:T(8,128)(2,1)S(1)}, u32[]{:S(2)}, u32[]{:S(2)}) collective-permute-start(bf16[128,256]{1,0:T(8,128)(2,1)} %get-tuple-element.50), channel_id=1, source_target_pairs={{0,16},{2,18},{4,20},{6,22},{8,24},{10,26},{12,28},{14,30},{16,0},... | collective-permute-start | bytes 196616 | tf_op jit(solution)/shard_map/ppermute | solution.py:309
  15.0 2.5 %copy-start.5 = (s32[1,1,80,128,128]{4,3,2,1,0:T(8,128)S(1)}, s32[1,1,80,128,128]{4,3,2,1,0:T(8,128)}, u32[]{:S(2)}) copy-start(s32[1,1,80,128,128]{4,3,2,1,0:T(8,128)} %param.16) | copy-start | bytes 15728644
  17.5 6.1 %copy-start.12 = (bf16[128,256]{1,0:T(8,128)(2,1)S(1)}, bf16[128,256]{1,0:T(8,128)(2,1)}, u32[]{:S(2)}) copy-start(bf16[128,256]{1,0:T(8,128)(2,1)} %get-tuple-element.50) | copy-start | bytes 196612
  17.5 6.3 %copy-start.13 = (bf16[128,256]{1,0:T(8,128)(2,1)S(1)}, bf16[128,256]{1,0:T(8,128)(2,1)}, u32[]{:S(2)}) copy-start(bf16[128,256]{1,0:T(8,128)(2,1)} %get-tuple-element.43) | copy-start | bytes 196612
  20.2 3.3 %copy-start = (bf16[2048,2048]{1,0:T(8,128)(2,1)}, bf16[2048,2048]{1,0:T(8,128)(2,1)S(1)}, u32[]{:S(2)}) copy-start(bf16[2048,2048]{1,0:T(8,128)(2,1)S(1)} %get-tuple-element.47.dense_ref) | copy-start | bytes 25165828
  23.5 6.1 %collective-permute-start.8 = (bf16[128,256]{1,0:T(8,128)(2,1)S(1)}, bf16[128,256]{1,0:T(8,128)(2,1)S(1)}, u32[]{:S(2)}, u32[]{:S(2)}) collective-permute-start(bf16[128,256]{1,0:T(8,128)(2,1)S(1)} %copy-done.12), channel_id=1, source_target_pairs={{0,24},{2,26},{4,28},{6,30},{8,16},{10,18},{12,20},{14,22},{16,8},... | collective-permute-start | bytes 196616 | tf_op jit(solution)/shard_map/ppermute | solution.py:309
  23.8 7.6 %collective-permute-start.3 = (bf16[512,256]{1,0:T(8,128)(2,1)S(1)}, bf16[512,256]{1,0:T(8,128)(2,1)S(1)}, u32[]{:S(2)}, u32[]{:S(2)}) collective-permute-start(bf16[512,256]{1,0:T(8,128)(2,1)S(1)} %pad_maximum_fusion.3), channel_id=1, source_target_pairs={{0,4},{2,6},{4,0},{6,2},{8,12},{10,14},{12,8},{14,10},{16,20},{18,... | collective-permute-start | bytes 786440 | tf_op jit(solution)/shard_map/ppermute | solution.py:309
  29.7 6.6 %collective-permute-start.9 = (bf16[512,256]{1,0:T(8,128)(2,1)S(1)}, bf16[512,256]{1,0:T(8,128)(2,1)S(1)}, u32[]{:S(2)}, u32[]{:S(2)}) collective-permute-start(bf16[512,256]{1,0:T(8,128)(2,1)S(1)} %pad_maximum_fusion.4), channel_id=1, source_target_pairs={{0,4},{2,6},{4,0},{6,2},{8,12},{10,14},{12,8},{14,10},{16,20},{18,... | collective-permute-start | bytes 786440 | tf_op jit(solution)/shard_map/ppermute | solution.py:309
  31.4 5.0 %collective-permute-start.4 = (bf16[1024,256]{1,0:T(8,128)(2,1)S(1)}, bf16[1024,256]{1,0:T(8,128)(2,1)S(1)}, u32[]{:S(2)}, u32[]{:S(2)}) collective-permute-start(bf16[1024,256]{1,0:T(8,128)(2,1)S(1)} %constant_dynamic-update-slice_fusion.same_ref), channel_id=1, source_target_pairs={{0,2},{2,0},{4,6},{6,4},{8,10},{10,8},{12,14},{14,12},{16,18},{18,... | collective-permute-start | bytes 1572872 | tf_op jit(solution)/shard_map/ppermute | solution.py:309
  36.3 10.8 %collective-permute-start.10 = (bf16[1024,256]{1,0:T(8,128)(2,1)S(1)}, bf16[1024,256]{1,0:T(8,128)(2,1)S(1)}, u32[]{:S(2)}, u32[]{:S(2)}) collective-permute-start(bf16[1024,256]{1,0:T(8,128)(2,1)S(1)} %constant_dynamic-update-slice_fusion.2.same_ref), channel_id=1, source_target_pairs={{0,2},{2,0},{4,6},{6,4},{8,10},{10,8},{12,14},{14,12},{16,18},{18,... | collective-permute-start | bytes 1572872 | tf_op jit(solution)/shard_map/ppermute | solution.py:309
  36.5 3.4 %copy-start.1 = (bf16[2048,2048]{1,0:T(8,128)(2,1)S(1)}, bf16[2048,2048]{1,0:T(8,128)(2,1)}, u32[]{:S(2)}) copy-start(bf16[2048,2048]{1,0:T(8,128)(2,1)} %copy-done) | copy-start | bytes 25165828
  41.5 15.0 %collective-permute-start.5 = (bf16[512,256]{1,0:T(8,128)(2,1)S(1)}, bf16[512,256]{1,0:T(8,128)(2,1)S(1)}, u32[]{:S(2)}, u32[]{:S(2)}) collective-permute-start(bf16[512,256]{1,0:T(8,128)(2,1)S(1)} %get-tuple-element.48.rest_0_), channel_id=1, source_target_pairs={{0,1},{1,0},{2,3},{3,2},{4,5},{5,4},{6,7},{7,6},{8,9},{9,8},{10,11... | collective-permute-start | bytes 786440 | tf_op jit(solution)/shard_map/ppermute | solution.py:489
  47.0 24.8 %collective-permute-start.17 = (bf16[512,256]{1,0:T(8,128)(2,1)S(1)}, bf16[512,256]{1,0:T(8,128)(2,1)S(1)}, u32[]{:S(2)}, u32[]{:S(2)}) collective-permute-start(bf16[512,256]{1,0:T(8,128)(2,1)S(1)} %get-tuple-element.58.rest_0_), channel_id=1, source_target_pairs={{0,1},{1,0},{2,3},{3,2},{4,5},{5,4},{6,7},{7,6},{8,9},{9,8},{10,11... | collective-permute-start | bytes 786440 | tf_op jit(solution)/shard_map/ppermute | solution.py:489
  47.1 25.7 %slice-start = ((s8[8388608]{0:T(1024)(128)(4,1)}), s8[4194304]{0:T(1024)(128)(4,1)S(1)}, s32[]{:S(2)}) async-start(s8[8388608]{0:T(1024)(128)(4,1)} %bitcast.49), calls=%async_computation.1 | async-start | bytes 8388608
  50.6 3.9 %copy-start.9 = (s32[1,128]{1,0:T(1,128)S(1)}, s32[1,128]{1,0:T(1,128)}, u32[]{:S(2)}) copy-start(s32[1,128]{1,0:T(1,128)} %cats_ref.3) | copy-start | bytes 1540
  50.6 6.1 %copy-start.11 = (bf16[1,128,512]{2,1,0:T(8,128)(2,1)S(1)}, bf16[1,128,512]{2,1,0:T(8,128)(2,1)}, u32[]{:S(2)}) copy-start(bf16[1,128,512]{2,1,0:T(8,128)(2,1)} %param.12) | copy-start | bytes 393220
  50.6 20.5 %copy-start.2 = (bf16[2048,512]{1,0:T(8,128)(2,1)S(1)}, bf16[2048,512]{1,0:T(8,128)(2,1)}, u32[]{:S(2)}) copy-start(bf16[2048,512]{1,0:T(8,128)(2,1)} %user_ref.7) | copy-start | bytes 6291460
  50.6 20.5 %copy-start.3 = (bf16[2048,512]{1,0:T(8,128)(2,1)S(1)}, bf16[2048,512]{1,0:T(8,128)(2,1)}, u32[]{:S(2)}) copy-start(bf16[2048,512]{1,0:T(8,128)(2,1)} %grad_ref.7) | copy-start | bytes 6291460
  50.6 20.5 %copy-start.8 = (f32[512]{0:T(512)S(1)}, f32[512]{0:T(512)}, u32[]{:S(2)}) copy-start(f32[512]{0:T(512)} %param.11) | copy-start | bytes 6148
  50.6 22.2 %slice-start.1 = ((s8[8388608]{0:T(1024)(128)(4,1)}), s8[4194304]{0:T(1024)(128)(4,1)S(1)}, s32[]{:S(2)}) async-start(s8[8388608]{0:T(1024)(128)(4,1)} %bitcast.49), calls=%async_computation.2 | async-start | bytes 8388608
  50.7 21.3 %collective-permute-start.18 = (bf16[512,256]{1,0:T(8,128)(2,1)S(1)}, bf16[512,256]{1,0:T(8,128)(2,1)S(1)}, u32[]{:S(2)}, u32[]{:S(2)}) collective-permute-start(bf16[512,256]{1,0:T(8,128)(2,1)S(1)} %get-tuple-element.59.rest_2_), channel_id=1, source_target_pairs={{0,1},{1,0},{2,3},{3,2},{4,5},{5,4},{6,7},{7,6},{8,9},{9,8},{10,11... | collective-permute-start | bytes 786440 | tf_op jit(solution)/shard_map/ppermute | solution.py:489
  54.4 13.2 %collective-permute-start.11 = (bf16[512,256]{1,0:T(8,128)(2,1)S(1)}, bf16[512,256]{1,0:T(8,128)(2,1)S(1)}, u32[]{:S(2)}, u32[]{:S(2)}) collective-permute-start(bf16[512,256]{1,0:T(8,128)(2,1)S(1)} %get-tuple-element.51.rest_2_), channel_id=1, source_target_pairs={{0,1},{1,0},{2,3},{3,2},{4,5},{5,4},{6,7},{7,6},{8,9},{9,8},{10,11... | collective-permute-start | bytes 786440 | tf_op jit(solution)/shard_map/ppermute | solution.py:489
  54.5 30.5 %collective-permute-start.16 = (bf16[512,256]{1,0:T(8,128)(2,1)S(1)}, bf16[512,256]{1,0:T(8,128)(2,1)S(1)}, u32[]{:S(2)}, u32[]{:S(2)}) collective-permute-start(bf16[512,256]{1,0:T(8,128)(2,1)S(1)} %get-tuple-element.54.rest_2_), channel_id=1, source_target_pairs={{0,1},{1,0},{2,3},{3,2},{4,5},{5,4},{6,7},{7,6},{8,9},{9,8},{10,11... | collective-permute-start | bytes 786440 | tf_op jit(solution)/shard_map/ppermute | solution.py:489
  56.5 29.9 %collective-permute-start.12 = (bf16[512,256]{1,0:T(8,128)(2,1)S(1)}, bf16[512,256]{1,0:T(8,128)(2,1)S(1)}, u32[]{:S(2)}, u32[]{:S(2)}) collective-permute-start(bf16[512,256]{1,0:T(8,128)(2,1)S(1)} %get-tuple-element.53.rest_0_), channel_id=1, source_target_pairs={{0,1},{1,0},{2,3},{3,2},{4,5},{5,4},{6,7},{7,6},{8,9},{9,8},{10,11... | collective-permute-start | bytes 786440 | tf_op jit(solution)/shard_map/ppermute | solution.py:489
  67.6 9.0 %collective-permute-start.15 = (bf16[128,640]{1,0:T(8,128)(2,1)S(1)}, bf16[128,640]{1,0:T(8,128)(2,1)S(1)}, u32[]{:S(2)}, u32[]{:S(2)}) collective-permute-start(bf16[128,640]{1,0:T(8,128)(2,1)S(1)} %pad_maximum_fusion.5), channel_id=1, source_target_pairs={{0,24},{2,26},{4,28},{6,30},{8,16},{10,18},{12,20},{14,22},{16,8},... | collective-permute-start | bytes 491528 | tf_op jit(solution)/shard_map/ppermute | solution.py:309
  71.8 11.6 %collective-permute-start.14 = (bf16[128,640]{1,0:T(8,128)(2,1)S(1)}, bf16[128,640]{1,0:T(8,128)(2,1)S(1)}, u32[]{:S(2)}, u32[]{:S(2)}) collective-permute-start(bf16[128,640]{1,0:T(8,128)(2,1)S(1)} %pad_maximum_fusion.5), channel_id=1, source_target_pairs={{0,16},{2,18},{4,20},{6,22},{8,24},{10,26},{12,28},{14,30},{16,0},... | collective-permute-start | bytes 491528 | tf_op jit(solution)/shard_map/ppermute | solution.py:309
  71.9 13.0 %collective-permute-start.13 = (bf16[128,640]{1,0:T(8,128)(2,1)S(1)}, bf16[128,640]{1,0:T(8,128)(2,1)S(1)}, u32[]{:S(2)}, u32[]{:S(2)}) collective-permute-start(bf16[128,640]{1,0:T(8,128)(2,1)S(1)} %pad_maximum_fusion.5), channel_id=1, source_target_pairs={{0,8},{2,10},{4,12},{6,14},{8,0},{10,2},{12,4},{14,6},{16,24},{18,... | collective-permute-start | bytes 491528 | tf_op jit(solution)/shard_map/ppermute | solution.py:309
  74.9 13.6 %copy-start.7 = (bf16[512,512]{1,0:T(8,128)(2,1)}, bf16[512,512]{1,0:T(8,128)(2,1)S(1)}, u32[]{:S(2)}) copy-start(bf16[512,512]{1,0:T(8,128)(2,1)S(1)} %get-tuple-element.60) | copy-start | bytes 1572868
  76.6 24.0 %collective-permute-start.19 = (bf16[512,256]{1,0:T(8,128)(2,1)S(1)}, bf16[512,256]{1,0:T(8,128)(2,1)S(1)}, u32[]{:S(2)}, u32[]{:S(2)}) collective-permute-start(bf16[512,256]{1,0:T(8,128)(2,1)S(1)} %get-tuple-element.61.rest_0_), channel_id=1, source_target_pairs={{0,1},{1,0},{2,3},{3,2},{4,5},{5,4},{6,7},{7,6},{8,9},{9,8},{10,11... | collective-permute-start | bytes 786440 | tf_op jit(solution)/shard_map/ppermute | solution.py:489
  83.5 17.2 %collective-permute-start.21 = (bf16[512,256]{1,0:T(8,128)(2,1)S(1)}, bf16[512,256]{1,0:T(8,128)(2,1)S(1)}, u32[]{:S(2)}, u32[]{:S(2)}) collective-permute-start(bf16[512,256]{1,0:T(8,128)(2,1)S(1)} %get-tuple-element.62.rest_2_), channel_id=1, source_target_pairs={{0,1},{1,0},{2,3},{3,2},{4,5},{5,4},{6,7},{7,6},{8,9},{9,8},{10,11... | collective-permute-start | bytes 786440 | tf_op jit(solution)/shard_map/ppermute | solution.py:489
  85.0 15.5 %collective-permute-start.20 = (bf16[512,640]{1,0:T(8,128)(2,1)S(1)}, bf16[512,640]{1,0:T(8,128)(2,1)S(1)}, u32[]{:S(2)}, u32[]{:S(2)}) collective-permute-start(bf16[512,640]{1,0:T(8,128)(2,1)S(1)} %pad_maximum_fusion.2), channel_id=1, source_target_pairs={{0,4},{2,6},{4,0},{6,2},{8,12},{10,14},{12,8},{14,10},{16,20},{18,... | collective-permute-start | bytes 1966088 | tf_op jit(solution)/shard_map/ppermute | solution.py:309
  87.1 1.3 copy-start.6
  102.4 2.0 %collective-permute-start.22 = (bf16[2,2,2,16,2048]{4,3,0,1,2:T(8,128)(2,1)S(1)}, bf16[2,2,2,16,2048]{4,3,0,1,2:T(8,128)(2,1)S(1)}, u32[]{:S(2)}, u32[]{:S(2)}) collective-permute-start(bf16[2,2,2,16,2048]{4,3,0,1,2:T(8,128)(2,1)S(1)} %fusion.16), channel_id=1, source_target_pairs={{0,2},{2,0},{4,6},{6,4},{8,10},{10,8},{12,14},{14,12},{16,18},{18,... | collective-permute-start | bytes 1572872 | tf_op jit(solution)/shard_map/ppermute | solution.py:309
  103.3 2.2 %collective-permute-start.24 = (bf16[2,2,2,16,2048]{4,3,0,2,1:T(8,128)(2,1)S(1)}, bf16[2,2,2,16,2048]{4,3,0,2,1:T(8,128)(2,1)S(1)}, u32[]{:S(2)}, u32[]{:S(2)}) collective-permute-start(bf16[2,2,2,16,2048]{4,3,0,2,1:T(8,128)(2,1)S(1)} %fusion.17), channel_id=1, source_target_pairs={{0,2},{2,0},{4,6},{6,4},{8,10},{10,8},{12,14},{14,12},{16,18},{18,... | collective-permute-start | bytes 1572872 | tf_op jit(solution)/shard_map/ppermute | solution.py:309
  103.8 10.4 %collective-permute-start.26 = (bf16[1024,640]{1,0:T(8,128)(2,1)S(1)}, bf16[1024,640]{1,0:T(8,128)(2,1)S(1)}, u32[]{:S(2)}, u32[]{:S(2)}) collective-permute-start(bf16[1024,640]{1,0:T(8,128)(2,1)S(1)} %pad_maximum_fusion.same_ref), channel_id=1, source_target_pairs={{0,2},{2,0},{4,6},{6,4},{8,10},{10,8},{12,14},{14,12},{16,18},{18,... | collective-permute-start | bytes 3932168 | tf_op jit(solution)/shard_map/ppermute | solution.py:309
  104.5 8.4 %collective-permute-start.23 = (bf16[2,2,16,2048]{3,2,0,1:T(8,128)(2,1)S(1)}, bf16[2,2,16,2048]{3,2,0,1:T(8,128)(2,1)S(1)}, u32[]{:S(2)}, u32[]{:S(2)}) collective-permute-start(bf16[2,2,16,2048]{3,2,0,1:T(8,128)(2,1)S(1)} %fusion.18), channel_id=1, source_target_pairs={{0,4},{2,6},{4,0},{6,2},{8,12},{10,14},{12,8},{14,10},{16,20},{18,... | collective-permute-start | bytes 786440 | tf_op jit(solution)/shard_map/ppermute | solution.py:309
  105.7 8.5 %collective-permute-start.25 = (bf16[2,2,16,2048]{3,2,0,1:T(8,128)(2,1)S(1)}, bf16[2,2,16,2048]{3,2,0,1:T(8,128)(2,1)S(1)}, u32[]{:S(2)}, u32[]{:S(2)}) collective-permute-start(bf16[2,2,16,2048]{3,2,0,1:T(8,128)(2,1)S(1)} %fusion.19), channel_id=1, source_target_pairs={{0,8},{2,10},{4,12},{6,14},{8,0},{10,2},{12,4},{14,6},{16,24},{18,... | collective-permute-start | bytes 786440 | tf_op jit(solution)/shard_map/ppermute | solution.py:309
  119.1 5.0 %collective-permute-start.27 = (bf16[2,16,2048]{2,1,0:T(8,128)(2,1)S(1)}, bf16[2,16,2048]{2,1,0:T(8,128)(2,1)S(1)}, u32[]{:S(2)}, u32[]{:S(2)}) collective-permute-start(bf16[2,16,2048]{2,1,0:T(8,128)(2,1)S(1)} %fusion.22), channel_id=1, source_target_pairs={{0,8},{2,10},{4,12},{6,14},{8,0},{10,2},{12,4},{14,6},{16,24},{18,... | collective-permute-start | bytes 393224 | tf_op jit(solution)/shard_map/ppermute | solution.py:309
  119.4 5.0 %collective-permute-start.28 = (bf16[2,16,2048]{2,1,0:T(8,128)(2,1)S(1)}, bf16[2,16,2048]{2,1,0:T(8,128)(2,1)S(1)}, u32[]{:S(2)}, u32[]{:S(2)}) collective-permute-start(bf16[2,16,2048]{2,1,0:T(8,128)(2,1)S(1)} %fusion.23), channel_id=1, source_target_pairs={{0,4},{2,6},{4,0},{6,2},{8,12},{10,14},{12,8},{14,10},{16,20},{18,... | collective-permute-start | bytes 393224 | tf_op jit(solution)/shard_map/ppermute | solution.py:309
  124.5 7.1 %collective-permute-start.29 = (bf16[16,2048]{1,0:T(8,128)(2,1)S(1)}, bf16[16,2048]{1,0:T(8,128)(2,1)S(1)}, u32[]{:S(2)}, u32[]{:S(2)}) collective-permute-start(bf16[16,2048]{1,0:T(8,128)(2,1)S(1)} %fusion.24), channel_id=1, source_target_pairs={{0,16},{2,18},{4,20},{6,22},{8,24},{10,26},{12,28},{14,30},{16,0},... | collective-permute-start | bytes 196616 | tf_op jit(solution)/shard_map/ppermute | solution.py:309
  127.9 5.7 %collective-permute-start.30 = (bf16[16,2048]{1,0:T(8,128)(2,1)S(1)}, bf16[16,2048]{1,0:T(8,128)(2,1)S(1)}, u32[]{:S(2)}, u32[]{:S(2)}) collective-permute-start(bf16[16,2048]{1,0:T(8,128)(2,1)S(1)} %fusion.25), channel_id=1, source_target_pairs={{0,16},{2,18},{4,20},{6,22},{8,24},{10,26},{12,28},{14,30},{16,0},... | collective-permute-start | bytes 196616 | tf_op jit(solution)/shard_map/ppermute | solution.py:309
  135.3 15.0 %all-to-all-start = ((bf16[16,80,128]{2,1,0:T(8,128)(2,1)}), bf16[16,80,128]{2,1,0:T(8,128)(2,1)S(1)}, u32[]{:S(2)}, u32[]{:S(2)}) async-start(bf16[16,80,128]{2,1,0:T(8,128)(2,1)} %packed_sums.1), calls=%async_computation | async-start | bytes 655360 | tf_op jit(solution)/shard_map/all_to_all | solution.py:547
  139.3 11.1 %copy-start.4 = (bf16[4,512,512]{2,1,0:T(8,128)(2,1)S(1)}, bf16[4,512,512]{2,1,0:T(8,128)(2,1)}, u32[]{:S(2)}) copy-start(bf16[4,512,512]{2,1,0:T(8,128)(2,1)} %weight_ref.3) | copy-start | bytes 6291460

commit v7 on v3

v7 whole, which is shorter than its diff:
```python
import functools

import jax
import jax.numpy as jnp
from jax import lax
from jax.experimental import pallas as pl
from jax.experimental.pallas import tpu as pltpu
from jax.sharding import PartitionSpec as P

TILE = 128
SLOTS_PER_STEP = 8
HALVES = 2
ROW_CHUNKS = 4
BLOCK_ROWS = 256
MIB = 1024 * 1024


def place_tiles(item_blocks, place_ref, count_ref, level_ref, dense_ref):
    step = pl.program_id(0)

    @pl.when(step == 0)
    def _():
        dense_ref[...] = jnp.zeros_like(dense_ref)

    for offset in range(level_ref.shape[0]):
        slot = step * level_ref.shape[0] + offset

        @pl.when(slot < count_ref[0])
        def _():
            place = place_ref[slot]
            row = pl.multiple_of((place // item_blocks) * TILE, TILE)
            col = pl.multiple_of((place % item_blocks) * TILE, TILE)
            weights = level_ref[offset].astype(jnp.float32) * (1.0 / (2.0 * TILE))
            dense_ref[pl.ds(row, TILE), pl.ds(col, TILE)] = weights.astype(jnp.bfloat16)


def dense_tiles(place, count, level, users, items):
    slots = level.shape[0]
    per_step = SLOTS_PER_STEP if slots % SLOTS_PER_STEP == 0 else 1
    return pl.pallas_call(
        functools.partial(place_tiles, items // TILE),
        out_shape=jax.ShapeDtypeStruct((users, items), jnp.bfloat16),
        grid_spec=pltpu.PrefetchScalarGridSpec(
            num_scalar_prefetch=2,
            grid=(slots // per_step,),
            in_specs=[
                pl.BlockSpec((per_step, TILE, TILE), lambda step, place_ref, count_ref: (step, 0, 0))
            ],
            out_specs=pl.BlockSpec((users, items), lambda step, place_ref, count_ref: (0, 0)),
        ),
        compiler_params=pltpu.CompilerParams(
            dimension_semantics=("arbitrary",), vmem_limit_bytes=16 * MIB
        ),
        cost_estimate=pl.CostEstimate(
            flops=slots * TILE * TILE,
            bytes_accessed=slots * TILE * TILE * 4 + users * items * 2,
            transcendentals=0,
        ),
        name="place_tiles",
    )(place, count, level)


def project_own(first_ref, cats_ref, feat_ref, weight_ref, *rest):
    out_refs, total_ref = rest[:-1], rest[-1]
    expert = pl.program_id(0)
    own = feat_ref.shape[0]
    on_diagonal = lax.broadcasted_iota(jnp.int32, (own, own), 0) == lax.broadcasted_iota(
        jnp.int32, (own, own), 1
    )
    cats = jnp.sum(
        jnp.where(on_diagonal, cats_ref[...].astype(jnp.float32), 0.0), axis=1, keepdims=True
    )
    chosen = cats == (first_ref[0] + expert).astype(jnp.float32)
    part = jnp.dot(feat_ref[...], weight_ref[0], preferred_element_type=jnp.float32)
    part = jnp.where(chosen, part, 0.0)

    @pl.when(expert == 0)
    def _():
        total_ref[...] = part

    @pl.when(expert > 0)
    def _():
        total_ref[...] += part

    @pl.when(expert == pl.num_programs(0) - 1)
    def _():
        cols = out_refs[0].shape[1]
        for half, out_ref in enumerate(out_refs):
            out_ref[...] = total_ref[:, half * cols : (half + 1) * cols].astype(out_ref.dtype)


def own_queries(first_expert, cats, feat, weights):
    own, width = feat.shape
    experts = weights.shape[0]
    half = jax.ShapeDtypeStruct((own, width // HALVES), jnp.bfloat16)
    half_spec = pl.BlockSpec((own, width // HALVES), lambda expert, first_ref: (0, 0))
    return pl.pallas_call(
        project_own,
        out_shape=[half] * HALVES,
        grid_spec=pltpu.PrefetchScalarGridSpec(
            num_scalar_prefetch=1,
            grid=(experts,),
            in_specs=[
                pl.BlockSpec((1, own), lambda expert, first_ref: (0, 0)),
                pl.BlockSpec((own, width), lambda expert, first_ref: (0, 0)),
                pl.BlockSpec((1, width, width), lambda expert, first_ref: (expert, 0, 0)),
            ],
            out_specs=[half_spec] * HALVES,
            scratch_shapes=[pltpu.VMEM((own, width), jnp.float32)],
        ),
        compiler_params=pltpu.CompilerParams(dimension_semantics=("arbitrary",)),
        cost_estimate=pl.CostEstimate(
            flops=2 * own * width * width * experts,
            bytes_accessed=weights.size * 2 + own * width * 4,
            transcendentals=0,
        ),
        name="own_queries",
    )(first_expert.reshape(1), cats.reshape(1, own), feat, weights)


def spread(blocks, order_ref, same_ref, other_ref, dense_ref, *rest):
    out_refs, next_ref, all_ref = rest[:-2], rest[-2], rest[-1]
    step = pl.program_id(0)

    @pl.when(step == 0)
    def _():
        for place in range(blocks):
            next_ref[place] = order_ref[place]
        own = all_ref.shape[0] // blocks
        for place in range(blocks):
            source = (same_ref, other_ref)[2 * place // blocks]
            start = pl.multiple_of(order_ref[place] * own, own)
            all_ref[pl.ds(start, own)] = source[pl.ds((place % (blocks // 2)) * own, own)]

    product = jnp.dot(dense_ref[...], all_ref[...], preferred_element_type=jnp.float32)
    rows, first = product.shape[0], 0
    for out_ref in out_refs:
        chunks = out_ref.shape[0] // rows

        @pl.when((step >= first) & (step < first + chunks))
        def _():
            start = pl.multiple_of((step - first) * rows, rows)
            out_ref[pl.ds(start, rows)] = product.astype(out_ref.dtype)

        first += chunks


def spread_items(order, queries, dense, first, counts, rows):
    items = dense.shape[1]
    cols = queries[0].shape[1]
    blocks, chunks = order.shape[0], sum(counts)
    whole = lambda step, order_ref: (0, 0)
    return pl.pallas_call(
        functools.partial(spread, blocks),
        out_shape=[jax.ShapeDtypeStruct((count * rows, cols), jnp.bfloat16) for count in counts]
        + [jax.ShapeDtypeStruct((blocks,), jnp.int32)],
        grid_spec=pltpu.PrefetchScalarGridSpec(
            num_scalar_prefetch=1,
            grid=(chunks,),
            in_specs=[pl.BlockSpec(queries[0].shape, whole)] * 2
            + [pl.BlockSpec((rows, items), lambda step, order_ref: (first + step, 0))],
            out_specs=[pl.BlockSpec((count * rows, cols), whole) for count in counts]
            + [pl.BlockSpec(memory_space=pltpu.SMEM)],
            scratch_shapes=[pltpu.VMEM((items, cols), jnp.bfloat16)],
        ),
        compiler_params=pltpu.CompilerParams(
            dimension_semantics=("arbitrary",), vmem_limit_bytes=14 * MIB
        ),
        cost_estimate=pl.CostEstimate(
            flops=2 * chunks * rows * items * cols,
            bytes_accessed=chunks * rows * (items + cols) * 2 + items * cols * 2,
            transcendentals=0,
        ),
        name="spread_items",
    )(order, *queries, dense)


def norm_backward(pieces, user_ref, grad_ref, gain_ref, *rest):
    piece_refs, out_ref, term_ref = rest[: pieces * HALVES], rest[-2], rest[-1]
    summed = []
    for half in range(HALVES):
        total = piece_refs[half * pieces][...].astype(jnp.float32)
        for piece in range(1, pieces):
            total = total + piece_refs[half * pieces + piece][...].astype(jnp.float32)
        summed.append(total)
    width = out_ref.shape[1]
    pre_norm = user_ref[...].astype(jnp.float32) + jnp.concatenate(summed, axis=1)
    grad = grad_ref[...].astype(jnp.float32)
    scaled_grad = gain_ref[...] * grad
    inv_rms = lax.rsqrt(jnp.sum(pre_norm * pre_norm, axis=1, keepdims=True) / width + 1e-05)
    cross_mean = jnp.sum(scaled_grad * pre_norm, axis=1, keepdims=True) / width
    out_ref[...] = (
        inv_rms * scaled_grad - pre_norm * (inv_rms * inv_rms * inv_rms * cross_mean)
    ).astype(out_ref.dtype)
    term = jnp.sum(grad * pre_norm * inv_rms, axis=0, keepdims=True)

    @pl.when(pl.program_id(0) == 0)
    def _():
        term_ref[...] = term

    @pl.when(pl.program_id(0) > 0)
    def _():
        term_ref[...] += term


def user_gradient(user_feat, cotangent, gain, pieces, first, rows):
    width = user_feat.shape[1]
    block_rows = min(BLOCK_ROWS, rows)
    first_block = first // block_rows
    flat = [piece for half in pieces for piece in half]
    whole = pl.BlockSpec((block_rows, width), lambda step: (first_block + step, 0))
    part = pl.BlockSpec((block_rows, width // HALVES), lambda step: (step, 0))
    return pl.pallas_call(
        functools.partial(norm_backward, len(pieces[0])),
        out_shape=[
            jax.ShapeDtypeStruct((rows, width), jnp.bfloat16),
            jax.ShapeDtypeStruct((1, width), jnp.float32),
        ],
        grid=(rows // block_rows,),
        in_specs=[whole, whole, pl.BlockSpec((1, width), lambda step: (0, 0))] + [part] * len(flat),
        out_specs=[
            pl.BlockSpec((block_rows, width), lambda step: (step, 0)),
            pl.BlockSpec((1, width), lambda step: (0, 0)),
        ],
        compiler_params=pltpu.CompilerParams(
            dimension_semantics=("arbitrary",), vmem_limit_bytes=10 * MIB
        ),
        cost_estimate=pl.CostEstimate(
            flops=16 * rows * width,
            bytes_accessed=rows * width * 2 * (3 + len(pieces[0])),
            transcendentals=rows,
        ),
        name="user_gradient",
    )(user_feat, cotangent, gain.reshape(1, width), *flat)


def flip(value, size, bits):
    return lax.ppermute(value, "user", [(source, source ^ bits) for source in range(size)])


def gather_layers(own, size):
    return jnp.concatenate(
        [own] + [flip(own, size, 4 * layer) for layer in range(1, size // 4)], axis=0
    )


def gather_sides(own, size):
    own = jnp.concatenate([own, flip(own, size, 2)], axis=0)
    return own, flip(own, size, 1)


def gather_order(size):
    layers = size // 4
    place = jnp.arange(size, dtype=jnp.int32)
    core, side, layer = place // (size // 2), (place // layers) % 2, place % layers
    return lax.axis_index("user") ^ (layer * 4 + side * 2 + core)


def scatter_sums(halves, size):
    bits = size.bit_length() - 1
    index = lax.axis_index("user")
    orders = [list(range(bits)), [0, 2, 1] + list(range(3, bits))]
    halves = [terms.reshape((2,) * bits + terms.shape[1:]) for terms in halves]
    left = [list(reversed(range(bits))) for _ in halves]
    for stage in range(bits):
        for half, terms in enumerate(halves):
            bit = orders[half][stage]
            axis = left[half].index(bit)
            left[half].remove(bit)
            mine = (index >> bit) & 1
            own = lax.dynamic_index_in_dim(terms, mine, axis, keepdims=False)
            away = lax.dynamic_index_in_dim(terms, 1 - mine, axis, keepdims=False)
            arrived = flip(away.astype(jnp.bfloat16), size, 1 << bit)
            halves[half] = own + arrived.astype(jnp.float32)
        if 0 < stage < bits - 1:
            halves = list(lax.optimization_barrier(tuple(halves)))
    return halves


def on_device(
    user_feat, cotangent, gain, item_feat, categories, expert_w, tile_place, tile_level, tile_count
):
    users, width = user_feat.shape
    user_size, item_size = lax.axis_size("user"), lax.axis_size("item")
    item_index = lax.axis_index("item")
    own_items = item_feat.shape[1]
    items = own_items * user_size
    experts_here = expert_w.shape[0]
    first_expert = item_index * experts_here
    own_cats, own_feat = categories[0], item_feat[0]
    rows, half_width = users // ROW_CHUNKS, width // HALVES

    own_halves = own_queries(first_expert, own_cats, own_feat, expert_w)
    order = gather_order(user_size)
    dense = dense_tiles(tile_place[0, 0], tile_count[0], tile_level[0, 0], users, items)
    layers = [gather_layers(own, user_size) for own in own_halves]
    queries = [gather_sides(part, user_size) for part in layers]

    partials = [[] for _ in range(HALVES)]
    for half in range(HALVES):
        for first, count in ((0, 1), (1, ROW_CHUNKS - 1)):
            *products, last = spread_items(order, queries[half], dense, first, (1,) * count, rows)
            for product in products:
                pieces = [product]
                for shift in range(1, item_size):
                    pairs = [(source, (source + shift) % item_size) for source in range(item_size)]
                    pieces.append(lax.ppermute(product, "item", pairs))
                partials[half].append(pieces)
    grads, gain_term, item_terms = [], 0.0, 0.0
    for chunk in range(ROW_CHUNKS):
        grad, term = user_gradient(
            user_feat,
            cotangent,
            gain,
            [partials[half][chunk] for half in range(HALVES)],
            chunk * rows,
            rows,
        )
        grads.append(grad)
        gain_term = gain_term + term[0]
        if chunk < ROW_CHUNKS - 1:
            item_terms = item_terms + lax.dot_general(
                dense[chunk * rows : (chunk + 1) * rows],
                grad,
                (((0,), (0,)), ((), ())),
                preferred_element_type=jnp.float32,
            )
    col_width = width // item_size
    user_grad = jnp.concatenate(
        [lax.dynamic_slice_in_dim(grad, item_index * col_width, col_width, 1) for grad in grads],
        axis=0,
    )
    gain_grad = lax.dynamic_slice_in_dim(gain_term, item_index * col_width, col_width, 0)
    for bit in range(user_size.bit_length() - 1):
        gain_grad = gain_grad + flip(gain_grad, user_size, 1 << bit)

    halves = []
    for half in range(HALVES):
        part = slice(half * half_width, (half + 1) * half_width)
        terms = item_terms[:, part] + lax.dot_general(
            dense[users - rows :],
            grads[-1][:, part],
            (((0,), (0,)), ((), ())),
            preferred_element_type=jnp.float32,
        )
        halves.append(terms.reshape(user_size, own_items, half_width))
    sums = [half.astype(jnp.bfloat16) for half in scatter_sums(halves, user_size)]

    chosen = own_cats[:, None] == first_expert + jnp.arange(experts_here, dtype=jnp.int32)[None, :]
    own_width = width // user_size
    left = jnp.where(
        chosen[:, None, :, None],
        own_feat.reshape(own_items, user_size, 1, own_width),
        jnp.zeros((), own_feat.dtype),
    ).reshape(own_items, -1)
    halves = [
        lax.dot_general(
            left, half, (((0,), (0,)), ((), ())), preferred_element_type=jnp.float32
        ).reshape(user_size, experts_here * own_width, half_width)
        for half in sums
    ]
    expert_grad = jnp.concatenate(scatter_sums(halves, user_size), axis=1)
    own_sums = jnp.concatenate(sums, axis=1)
    item_total = jnp.zeros((own_items, width), jnp.float32)
    for expert in range(experts_here):
        item_total = item_total + jnp.where(
            chosen[:, expert][:, None],
            lax.dot_general(
                own_sums,
                expert_w[expert],
                (((1,), (1,)), ((), ())),
                preferred_element_type=jnp.float32,
            ),
            0.0,
        )
    return (
        user_grad,
        item_total.astype(jnp.bfloat16)[None],
        expert_grad.reshape(experts_here, own_width, width),
        gain_grad,
    )


def solution(mesh):
    placed = (
        P("user", None),
        P("user", None),
        P(),
        P("item", "user", None),
        P("item", "user"),
        P("item", None, None),
        P("user", "item", None),
        P("user", "item", None, None, None),
        P("user", "item"),
    )
    return jax.shard_map(
        on_device,
        mesh=mesh,
        in_specs=placed,
        out_specs=(P("user", "item"), P("item", "user", None), P("item", "user", None), P("item")),
        check_vma=False,
    )
```

time: 145 us -> 150 us (1.034)
  waiting for transfers between devices: 53.2 us -> 64.8 us
  Pallas kernels: 25.6 us -> 19.1 us
  local copies, waits for them, and re-layouts: 7.91 us -> 4.19 us
  other arithmetic: 2.44 us -> 5.05 us
    ppermute x25 -> x30, waiting for transfers between devices: 21.5 us -> 38.8 us  [flip(): lax.ppermute(value, 'user', [(source, source ^ bits) for source in range(...]
    all_to_all x1 -> x0, waiting for transfers between devices: 9.37 us -> none  [on_device(): swapped = lax.all_to_all(jnp.concatenate(pieces, axis=1), 'user', 0, 0)]
    pallas_call x1 -> x0, Pallas kernels: 4.51 us -> none  [ordered_items(): pl.pallas_call(functools.partial(order_items, blocks), out_shape=[jax.Sha...]
    ppermute x25 -> x30, starting transfers between devices: 32.1 us -> 36.3 us  [flip(): lax.ppermute(value, 'user', [(source, source ^ bits) for source in range(...]
    ppermute x8, waiting for transfers between devices: 22.4 us -> 26 us  [on_device(): pieces.append(lax.ppermute(product, 'item', pairs))]
    all_to_all x1 -> x0, starting transfers between devices: 3.54 us -> none  [on_device(): swapped = lax.all_to_all(jnp.concatenate(pieces, axis=1), 'user', 0, 0)]
    pallas_call x3 -> x4, Pallas kernels: 12.3 us -> 10.3 us  [spread_items(): pl.pallas_call(functools.partial(spread, blocks), out_shape=[jax.ShapeDty...]
    concatenate x3 -> x2, other arithmetic: 0.1 us -> 1.71 us  [gather_layers(): jnp.concatenate([own] + [flip(own, size, 4 * layer) for layer in range(1,...]
  transfers between devices with their start and end apart: 34 -> 38, of which waited for: 16 -> 26; matrix products, arithmetic and copies ran while one was open for 6% -> 8% of each run, Pallas kernels for 12% -> 10%
where the time goes in v7:
time: 150 us; the launch traced here: 149 us
  waiting for transfers between devices  64.8 us (43%)
  starting transfers between devices  45.5 us (30%)
  Pallas kernels  19.1 us (13%)
  matrix products  8.35 us (6%)
  other arithmetic  5.05 us (3%)
  local copies, waits for them, and re-layouts  4.19 us (3%)
  between operations  1.94 us (1%)
    ppermute x30, waiting for transfers between devices, flip(): lax.ppermute(value, 'user', [(source, source ^ bits) for source in range(...  38.8 us
    ppermute x30, starting transfers between devices, flip(): lax.ppermute(value, 'user', [(source, source ^ bits) for source in range(...  36.3 us
    ppermute x8, waiting for transfers between devices, on_device(): pieces.append(lax.ppermute(product, 'item', pairs))  26 us
    pallas_call x4, Pallas kernels, spread_items(): pl.pallas_call(functools.partial(spread, blocks), out_shape=[jax.ShapeDty...  10.3 us
    ppermute x8, starting transfers between devices, on_device(): pieces.append(lax.ppermute(product, 'item', pairs))  9.2 us
    dot_general x3, matrix products, on_device(): lax.dot_general(dense[chunk * rows:(chunk + 1) * rows], grad, (((0,), (0,...  4.02 us
    pallas_call x1, Pallas kernels, own_queries(): pl.pallas_call(project_own, out_shape=[half] * HALVES, grid_spec=pltpu.Pr...  3.64 us
    unnamed x24, local copies, waits for them, and re-layouts  3.56 us
  transfers between devices with their start and end apart: 38, of which 26 were waited for; matrix products, arithmetic and copies ran while one was open for 8% of the time, Pallas kernels for 10%

profile of v7, /device:TPU:0, one launch (start us, length us, event | category | flops | bytes accessed | tf_op | source)
XLA Modules:
  0.0 148.9 jit_solution(5266163608270239099)
XLA Ops:
  0.6 3.6 %own_queries.1 = (bf16[128,256]{1,0:T(8,128)(2,1)}, bf16[128,256]{1,0:T(8,128)(2,1)}) custom-call(s32[1]{0:T(128)} %bitcast.1.first_ref, s32[1,128]{1,0:T(1,128)} %cats_ref.1, bf16[128,512]{1,0:T(8,128)(2,1)} %bitcast.135, bf16[4,512,512]{2,1,0:T(8,128)(2,1)} %weight_ref.1), custom_call_target="tpu_custom_call" | custom-call | flops 268435456 | bytes 2359296 | tf_op jit(solution)/shard_map/own_queries/pallas_call | solution.py:97
  4.3 3.1 %collective-permute-start.6 = (bf16[128,256]{1,0:T(8,128)(2,1)}, bf16[128,256]{1,0:T(8,128)(2,1)S(1)}, u32[]{:S(2)}, u32[]{:S(2)}) collective-permute-start(bf16[128,256]{1,0:T(8,128)(2,1)} %get-tuple-element.32), channel_id=1, source_target_pairs={{0,8},{2,10},{4,12},{6,14},{8,0},{10,2},{12,4},{14,6},{16,24},{18,... | collective-permute-start | bytes 196616 | tf_op jit(solution)/shard_map/ppermute | solution.py:238
  7.4 2.6 %collective-permute-start.7 = (bf16[128,256]{1,0:T(8,128)(2,1)}, bf16[128,256]{1,0:T(8,128)(2,1)S(1)}, u32[]{:S(2)}, u32[]{:S(2)}) collective-permute-start(bf16[128,256]{1,0:T(8,128)(2,1)} %get-tuple-element.32), channel_id=1, source_target_pairs={{0,16},{2,18},{4,20},{6,22},{8,24},{10,26},{12,28},{14,30},{16,0},... | collective-permute-start | bytes 196616 | tf_op jit(solution)/shard_map/ppermute | solution.py:238
  10.9 3.5 %collective-permute-start.1 = (bf16[128,256]{1,0:T(8,128)(2,1)}, bf16[128,256]{1,0:T(8,128)(2,1)S(1)}, u32[]{:S(2)}, u32[]{:S(2)}) collective-permute-start(bf16[128,256]{1,0:T(8,128)(2,1)} %get-tuple-element.30), channel_id=1, source_target_pairs={{0,16},{2,18},{4,20},{6,22},{8,24},{10,26},{12,28},{14,30},{16,0},... | collective-permute-start | bytes 196616 | tf_op jit(solution)/shard_map/ppermute | solution.py:238
  15.3 1.4 collective-permute-done.8
  17.6 1.6 %collective-permute-start.9 = (bf16[512,256]{1,0:T(8,128)(2,1)S(1)}, bf16[512,256]{1,0:T(8,128)(2,1)S(1)}, u32[]{:S(2)}, u32[]{:S(2)}) collective-permute-start(bf16[512,256]{1,0:T(8,128)(2,1)S(1)} %pad_maximum_fusion.2), channel_id=1, source_target_pairs={{0,4},{2,6},{4,0},{6,2},{8,12},{10,14},{12,8},{14,10},{16,20},{18,... | collective-permute-start | bytes 786440 | tf_op jit(solution)/shard_map/ppermute | solution.py:238
  22.6 1.6 %collective-permute-start.3 = (bf16[512,256]{1,0:T(8,128)(2,1)S(1)}, bf16[512,256]{1,0:T(8,128)(2,1)S(1)}, u32[]{:S(2)}, u32[]{:S(2)}) collective-permute-start(bf16[512,256]{1,0:T(8,128)(2,1)S(1)} %pad_maximum_fusion.1), channel_id=1, source_target_pairs={{0,4},{2,6},{4,0},{6,2},{8,12},{10,14},{12,8},{14,10},{16,20},{18,... | collective-permute-start | bytes 786440 | tf_op jit(solution)/shard_map/ppermute | solution.py:238
  24.2 1.4 collective-permute-done.9
  25.7 4.0 %collective-permute-done.3 = bf16[512,256]{1,0:T(8,128)(2,1)S(1)} collective-permute-done((bf16[512,256]{1,0:T(8,128)(2,1)S(1)}, bf16[512,256]{1,0:T(8,128)(2,1)S(1)}, u32[]{:S(2)}, u32[]{:S(2)}) %collective-permute-start.3) | collective-permute-done | bytes 262176 | tf_op jit(solution)/shard_map/ppermute | solution.py:238
  30.7 2.5 %copy-done.2 = s32[1,1,80,128,128]{4,3,2,1,0:T(8,128)S(1)} copy-done((s32[1,1,80,128,128]{4,3,2,1,0:T(8,128)S(1)}, s32[1,1,80,128,128]{4,3,2,1,0:T(8,128)}, u32[]{:S(2)}) %copy-start.2) | copy-done | bytes 5242904
  33.1 2.2 %place_tiles.1.dense_ref = bf16[2048,2048]{1,0:T(8,128)(2,1)S(1)} custom-call(s32[80]{0:T(128)S(1)} %bitcast.128, s32[1]{0:T(128)} %bitcast.122.count_ref, s32[80,128,128]{2,1,0:T(8,128)S(1)} %bitcast.123), custom_call_target="tpu_custom_call" | custom-call | flops 1310720 | bytes 13631488 | tf_op jit(solution)/shard_map/place_tiles/pallas_call | solution.py:40
  35.4 3.4 %spread_items.7 = (bf16[512,256]{1,0:T(8,128)(2,1)S(1)}, bf16[512,256]{1,0:T(8,128)(2,1)S(1)}, bf16[512,256]{1,0:T(8,128)(2,1)S(1)}, s32[16]{0:T(128)}) custom-call(s32[16]{0:T(128)S(1)} %fusion.59.order_ref, bf16[1024,256]{1,0:T(8,128)(2,1)S(1)} %constant_dynamic-update-slice_fusion.5.same_ref, bf16[1024,256]{1,0:T(8,128)(2,1)S(1)} %collective-permute-done.10.other_ref, ...), custom_call_target="tpu_custom_call" | custom-call | flops 1610612736 | bytes 8126464 | tf_op jit(solution)/shard_map/spread_items/pallas_call | solution.py:153
  38.9 1.6 %collective-permute-start.13 = (bf16[512,256]{1,0:T(8,128)(2,1)S(1)}, bf16[512,256]{1,0:T(8,128)(2,1)S(1)}, u32[]{:S(2)}, u32[]{:S(2)}) collective-permute-start(bf16[512,256]{1,0:T(8,128)(2,1)S(1)} %get-tuple-element.36.rest_2_), channel_id=1, source_target_pairs={{0,1},{1,0},{2,3},{3,2},{4,5},{5,4},{6,7},{7,6},{8,9},{9,8},{10,11... | collective-permute-start | bytes 786440 | tf_op jit(solution)/shard_map/ppermute | solution.py:307
  40.4 3.4 %spread_items.6 = (bf16[512,256]{1,0:T(8,128)(2,1)S(1)}, bf16[512,256]{1,0:T(8,128)(2,1)S(1)}, bf16[512,256]{1,0:T(8,128)(2,1)S(1)}, s32[16]{0:T(128)}) custom-call(s32[16]{0:T(128)S(1)} %fusion.59.order_ref, bf16[1024,256]{1,0:T(8,128)(2,1)S(1)} %constant_dynamic-update-slice_fusion.same_ref, bf16[1024,256]{1,0:T(8,128)(2,1)S(1)} %collective-permute-done.4.other_ref, ...), custom_call_target="tpu_custom_call" | custom-call | flops 1610612736 | bytes 8126464 | tf_op jit(solution)/shard_map/spread_items/pallas_call | solution.py:153
  44.5 1.7 %spread_items.5 = (bf16[512,256]{1,0:T(8,128)(2,1)S(1)}, s32[16]{0:T(128)}) custom-call(s32[16]{0:T(128)S(1)} %fusion.59.order_ref, bf16[1024,256]{1,0:T(8,128)(2,1)S(1)} %constant_dynamic-update-slice_fusion.5.same_ref, bf16[1024,256]{1,0:T(8,128)(2,1)S(1)} %collective-permute-done.10.other_ref, bf16[2048,2048]{1,0:T(8,128)(2,1)S(1)} %place_tiles.1.dense_ref), custom_call_target="tpu_custom_call" | custom-call | flops 536870912 | bytes 3407872 | tf_op jit(solution)/shard_map/spread_items/pallas_call | solution.py:153
  46.2 1.5 %collective-permute-start.11 = (bf16[512,256]{1,0:T(8,128)(2,1)S(1)}, bf16[512,256]{1,0:T(8,128)(2,1)S(1)}, u32[]{:S(2)}, u32[]{:S(2)}) collective-permute-start(bf16[512,256]{1,0:T(8,128)(2,1)S(1)} %get-tuple-element.33.rest_2_), channel_id=1, source_target_pairs={{0,1},{1,0},{2,3},{3,2},{4,5},{5,4},{6,7},{7,6},{8,9},{9,8},{10,11... | collective-permute-start | bytes 786440 | tf_op jit(solution)/shard_map/ppermute | solution.py:307
  47.8 1.7 %spread_items.4 = (bf16[512,256]{1,0:T(8,128)(2,1)S(1)}, s32[16]{0:T(128)}) custom-call(s32[16]{0:T(128)S(1)} %fusion.59.order_ref, bf16[1024,256]{1,0:T(8,128)(2,1)S(1)} %constant_dynamic-update-slice_fusion.same_ref, bf16[1024,256]{1,0:T(8,128)(2,1)S(1)} %collective-permute-done.4.other_ref, bf16[2048,2048]{1,0:T(8,128)(2,1)S(1)} %place_tiles.1.dense_ref), custom_call_target="tpu_custom_call" | custom-call | flops 536870912 | bytes 3407872 | tf_op jit(solution)/shard_map/spread_items/pallas_call | solution.py:153
  50.1 1.5 collective-permute-start.15
  52.1 1.6 %collective-permute-done.12.rest_1_ = bf16[512,256]{1,0:T(8,128)(2,1)S(1)} collective-permute-done((bf16[512,256]{1,0:T(8,128)(2,1)S(1)}, bf16[512,256]{1,0:T(8,128)(2,1)S(1)}, u32[]{:S(2)}, u32[]{:S(2)}) %collective-permute-start.12) | collective-permute-done | bytes 262176 | tf_op jit(solution)/shard_map/ppermute | solution.py:307
  53.7 1.4 collective-permute-start.17
  55.9 1.3 fusion.4
  57.2 2.2 %collective-permute-done.11.rest_3_ = bf16[512,256]{1,0:T(8,128)(2,1)S(1)} collective-permute-done((bf16[512,256]{1,0:T(8,128)(2,1)S(1)}, bf16[512,256]{1,0:T(8,128)(2,1)S(1)}, u32[]{:S(2)}, u32[]{:S(2)}) %collective-permute-start.11) | collective-permute-done | bytes 262176 | tf_op jit(solution)/shard_map/ppermute | solution.py:307
  59.3 1.4 collective-permute-start.16
  60.8 4.2 %collective-permute-done.5.rest_1_ = bf16[512,256]{1,0:T(8,128)(2,1)S(1)} collective-permute-done((bf16[512,256]{1,0:T(8,128)(2,1)S(1)}, bf16[512,256]{1,0:T(8,128)(2,1)S(1)}, u32[]{:S(2)}, u32[]{:S(2)}) %collective-permute-start.5) | collective-permute-done | bytes 262176 | tf_op jit(solution)/shard_map/ppermute | solution.py:307
  66.9 3.6 %collective-permute-done.15.rest_3_ = bf16[512,256]{1,0:T(8,128)(2,1)S(1)} collective-permute-done((bf16[512,256]{1,0:T(8,128)(2,1)S(1)}, bf16[512,256]{1,0:T(8,128)(2,1)S(1)}, u32[]{:S(2)}, u32[]{:S(2)}) %collective-permute-start.15) | collective-permute-done | bytes 262176 | tf_op jit(solution)/shard_map/ppermute | solution.py:307
  70.6 5.6 %collective-permute-done.14.rest_1_ = bf16[512,256]{1,0:T(8,128)(2,1)S(1)} collective-permute-done((bf16[512,256]{1,0:T(8,128)(2,1)S(1)}, bf16[512,256]{1,0:T(8,128)(2,1)S(1)}, u32[]{:S(2)}, u32[]{:S(2)}) %collective-permute-start.14) | collective-permute-done | bytes 262176 | tf_op jit(solution)/shard_map/ppermute | solution.py:307
  76.9 1.4 add_add_fusion
  78.3 3.5 %collective-permute-done.17.rest_3_ = bf16[512,256]{1,0:T(8,128)(2,1)S(1)} collective-permute-done((bf16[512,256]{1,0:T(8,128)(2,1)S(1)}, bf16[512,256]{1,0:T(8,128)(2,1)S(1)}, u32[]{:S(2)}, u32[]{:S(2)}) %collective-permute-start.17) | collective-permute-done | bytes 262176 | tf_op jit(solution)/shard_map/ppermute | solution.py:307
  81.8 5.3 %collective-permute-done.16.rest_1_ = bf16[512,256]{1,0:T(8,128)(2,1)S(1)} collective-permute-done((bf16[512,256]{1,0:T(8,128)(2,1)S(1)}, bf16[512,256]{1,0:T(8,128)(2,1)S(1)}, u32[]{:S(2)}, u32[]{:S(2)}) %collective-permute-start.16) | collective-permute-done | bytes 262176 | tf_op jit(solution)/shard_map/ppermute | solution.py:307
  91.7 1.5 collective-permute-start.35
  93.1 2.1 %collective-permute-done.35 = f32[256]{0:T(256)S(1)} collective-permute-done((f32[256]{0:T(256)S(1)}, f32[256]{0:T(256)S(1)}, u32[]{:S(2)}, u32[]{:S(2)}) %collective-permute-start.35) | collective-permute-done | bytes 1056 | tf_op jit(solution)/shard_map/ppermute | solution.py:238
  95.2 2.8 %collective-permute-start.36 = (f32[256]{0:T(256)S(1)}, f32[256]{0:T(256)S(1)}, u32[]{:S(2)}, u32[]{:S(2)}) collective-permute-start(f32[256]{0:T(256)S(1)} %add.228), channel_id=1, source_target_pairs={{0,8},{2,10},{4,12},{6,14},{8,0},{10,2},{12,4},{14,6},{16,24},{18,... | collective-permute-start | bytes 3080 | tf_op jit(solution)/shard_map/ppermute | solution.py:238
  98.4 1.7 %collective-permute-start.19 = (bf16[2,2,128,256]{3,2,0,1:T(8,128)(2,1)S(1)}, bf16[2,2,128,256]{3,2,0,1:T(8,128)(2,1)S(1)}, u32[]{:S(2)}, u32[]{:S(2)}) collective-permute-start(bf16[2,2,128,256]{3,2,0,1:T(8,128)(2,1)S(1)} %fusion.33), channel_id=1, source_target_pairs={{0,4},{2,6},{4,0},{6,2},{8,12},{10,14},{12,8},{14,10},{16,20},{18,... | collective-permute-start | bytes 786440 | tf_op jit(solution)/shard_map/ppermute | solution.py:238
  100.2 3.6 %collective-permute-start.37 = (f32[256]{0:T(256)S(1)}, f32[256]{0:T(256)S(1)}, u32[]{:S(2)}, u32[]{:S(2)}) collective-permute-start(f32[256]{0:T(256)S(1)} %add.229), channel_id=1, source_target_pairs={{0,16},{2,18},{4,20},{6,22},{8,24},{10,26},{12,28},{14,30},{16,0},... | collective-permute-start | bytes 3080 | tf_op jit(solution)/shard_map/ppermute | solution.py:238
  103.8 1.4 collective-permute-done.21
  105.5 1.7 %collective-permute-start.23 = (bf16[2,128,256]{2,1,0:T(8,128)(2,1)S(1)}, bf16[2,128,256]{2,1,0:T(8,128)(2,1)S(1)}, u32[]{:S(2)}, u32[]{:S(2)}) collective-permute-start(bf16[2,128,256]{2,1,0:T(8,128)(2,1)S(1)} %fusion.40), channel_id=1, source_target_pairs={{0,4},{2,6},{4,0},{6,2},{8,12},{10,14},{12,8},{14,10},{16,20},{18,... | collective-permute-start | bytes 393224 | tf_op jit(solution)/shard_map/ppermute | solution.py:238
  108.8 1.8 %collective-permute-start.22 = (bf16[2,128,256]{2,1,0:T(8,128)(2,1)S(1)}, bf16[2,128,256]{2,1,0:T(8,128)(2,1)S(1)}, u32[]{:S(2)}, u32[]{:S(2)}) collective-permute-start(bf16[2,128,256]{2,1,0:T(8,128)(2,1)S(1)} %fusion.39), channel_id=1, source_target_pairs={{0,8},{2,10},{4,12},{6,14},{8,0},{10,2},{12,4},{14,6},{16,24},{18,... | collective-permute-start | bytes 393224 | tf_op jit(solution)/shard_map/ppermute | solution.py:238
  110.6 3.2 %collective-permute-done.22 = bf16[2,128,256]{2,1,0:T(8,128)(2,1)S(1)} collective-permute-done((bf16[2,128,256]{2,1,0:T(8,128)(2,1)S(1)}, bf16[2,128,256]{2,1,0:T(8,128)(2,1)S(1)}, u32[]{:S(2)}, u32[]{:S(2)}) %collective-permute-start.22) | collective-permute-done | bytes 131104 | tf_op jit(solution)/shard_map/ppermute | solution.py:238
  113.9 4.0 %collective-permute-start.25 = (bf16[128,256]{1,0:T(8,128)(2,1)S(1)}, bf16[128,256]{1,0:T(8,128)(2,1)S(1)}, u32[]{:S(2)}, u32[]{:S(2)}) collective-permute-start(bf16[128,256]{1,0:T(8,128)(2,1)S(1)} %fusion.46), channel_id=1, source_target_pairs={{0,16},{2,18},{4,20},{6,22},{8,24},{10,26},{12,28},{14,30},{16,0},... | collective-permute-start | bytes 196616 | tf_op jit(solution)/shard_map/ppermute | solution.py:238
  118.0 2.8 %collective-permute-done.25 = bf16[128,256]{1,0:T(8,128)(2,1)S(1)} collective-permute-done((bf16[128,256]{1,0:T(8,128)(2,1)S(1)}, bf16[128,256]{1,0:T(8,128)(2,1)S(1)}, u32[]{:S(2)}, u32[]{:S(2)}) %collective-permute-start.25) | collective-permute-done | bytes 65568 | tf_op jit(solution)/shard_map/ppermute | solution.py:238
  121.4 1.7 %collective-permute-done.24 = bf16[128,256]{1,0:T(8,128)(2,1)S(1)} collective-permute-done((bf16[128,256]{1,0:T(8,128)(2,1)S(1)}, bf16[128,256]{1,0:T(8,128)(2,1)S(1)}, u32[]{:S(2)}, u32[]{:S(2)}) %collective-permute-start.24) | collective-permute-done | bytes 65568 | tf_op jit(solution)/shard_map/ppermute | solution.py:238
  126.4 6.9 %collective-permute-done.29 = bf16[2,2,128,256]{3,2,0,1:T(8,128)(2,1)S(1)} collective-permute-done((bf16[2,2,128,256]{3,2,0,1:T(8,128)(2,1)S(1)}, bf16[2,2,128,256]{3,2,0,1:T(8,128)(2,1)S(1)}, u32[]{:S(2)}, u32[]{:S(2)}) %collective-permute-start.29) | collective-permute-done | bytes 262176 | tf_op jit(solution)/shard_map/ppermute | solution.py:238
  136.8 2.5 %collective-permute-done.31 = bf16[2,128,256]{2,1,0:T(8,128)(2,1)S(1)} collective-permute-done((bf16[2,128,256]{2,1,0:T(8,128)(2,1)S(1)}, bf16[2,128,256]{2,1,0:T(8,128)(2,1)S(1)}, u32[]{:S(2)}, u32[]{:S(2)}) %collective-permute-start.31) | collective-permute-done | bytes 131104 | tf_op jit(solution)/shard_map/ppermute | solution.py:238
  139.4 1.3 collective-permute-done.30
  140.7 1.4 collective-permute-start.32
  142.1 1.7 %collective-permute-start.33 = (bf16[128,256]{1,0:T(8,128)(2,1)S(1)}, bf16[128,256]{1,0:T(8,128)(2,1)S(1)}, u32[]{:S(2)}, u32[]{:S(2)}) collective-permute-start(bf16[128,256]{1,0:T(8,128)(2,1)S(1)} %fusion.48), channel_id=1, source_target_pairs={{0,16},{2,18},{4,20},{6,22},{8,24},{10,26},{12,28},{14,30},{16,0},... | collective-permute-start | bytes 196616 | tf_op jit(solution)/shard_map/ppermute | solution.py:238
  143.8 3.0 %collective-permute-done.32 = bf16[128,256]{1,0:T(8,128)(2,1)S(1)} collective-permute-done((bf16[128,256]{1,0:T(8,128)(2,1)S(1)}, bf16[128,256]{1,0:T(8,128)(2,1)S(1)}, u32[]{:S(2)}, u32[]{:S(2)}) %collective-permute-start.32) | collective-permute-done | bytes 65568 | tf_op jit(solution)/shard_map/ppermute | solution.py:238
  146.8 1.4 collective-permute-done.33
  (125 shorter events, 26.8 us)
Async XLA Ops:
  4.3 25.5 %copy-start.7 = (s32[1,128]{1,0:T(1,128)S(1)}, s32[1,128]{1,0:T(1,128)}, u32[]{:S(2)}) copy-start(s32[1,128]{1,0:T(1,128)} %cats_ref.1) | copy-start | bytes 1540
  4.3 25.6 %copy-start.6 = (bf16[1,128,512]{2,1,0:T(8,128)(2,1)S(1)}, bf16[1,128,512]{2,1,0:T(8,128)(2,1)}, u32[]{:S(2)}) copy-start(bf16[1,128,512]{2,1,0:T(8,128)(2,1)} %param.12) | copy-start | bytes 393220
  4.3 26.4 %copy-start.4 = (s32[1,1,80]{2,1,0:T(1,128)S(1)}, s32[1,1,80]{2,1,0:T(1,128)}, u32[]{:S(2)}) copy-start(s32[1,1,80]{2,1,0:T(1,128)} %param.15) | copy-start | bytes 964
  4.3 11.0 %collective-permute-start.6 = (bf16[128,256]{1,0:T(8,128)(2,1)}, bf16[128,256]{1,0:T(8,128)(2,1)S(1)}, u32[]{:S(2)}, u32[]{:S(2)}) collective-permute-start(bf16[128,256]{1,0:T(8,128)(2,1)} %get-tuple-element.32), channel_id=1, source_target_pairs={{0,8},{2,10},{4,12},{6,14},{8,0},{10,2},{12,4},{14,6},{16,24},{18,... | collective-permute-start | bytes 196616 | tf_op jit(solution)/shard_map/ppermute | solution.py:238
  7.4 8.0 %collective-permute-start.7 = (bf16[128,256]{1,0:T(8,128)(2,1)}, bf16[128,256]{1,0:T(8,128)(2,1)S(1)}, u32[]{:S(2)}, u32[]{:S(2)}) collective-permute-start(bf16[128,256]{1,0:T(8,128)(2,1)} %get-tuple-element.32), channel_id=1, source_target_pairs={{0,16},{2,18},{4,20},{6,22},{8,24},{10,26},{12,28},{14,30},{16,0},... | collective-permute-start | bytes 196616 | tf_op jit(solution)/shard_map/ppermute | solution.py:238
  10.0 6.8 %collective-permute-start.8 = (bf16[128,256]{1,0:T(8,128)(2,1)}, bf16[128,256]{1,0:T(8,128)(2,1)S(1)}, u32[]{:S(2)}, u32[]{:S(2)}) collective-permute-start(bf16[128,256]{1,0:T(8,128)(2,1)} %get-tuple-element.32), channel_id=1, source_target_pairs={{0,24},{2,26},{4,28},{6,30},{8,16},{10,18},{12,20},{14,22},{16,8},... | collective-permute-start | bytes 196616 | tf_op jit(solution)/shard_map/ppermute | solution.py:238
  10.0 9.2 %collective-permute-start = (bf16[128,256]{1,0:T(8,128)(2,1)}, bf16[128,256]{1,0:T(8,128)(2,1)S(1)}, u32[]{:S(2)}, u32[]{:S(2)}) collective-permute-start(bf16[128,256]{1,0:T(8,128)(2,1)} %get-tuple-element.30), channel_id=1, source_target_pairs={{0,8},{2,10},{4,12},{6,14},{8,0},{10,2},{12,4},{14,6},{16,24},{18,... | collective-permute-start | bytes 196616 | tf_op jit(solution)/shard_map/ppermute | solution.py:238
  10.9 9.6 %collective-permute-start.1 = (bf16[128,256]{1,0:T(8,128)(2,1)}, bf16[128,256]{1,0:T(8,128)(2,1)S(1)}, u32[]{:S(2)}, u32[]{:S(2)}) collective-permute-start(bf16[128,256]{1,0:T(8,128)(2,1)} %get-tuple-element.30), channel_id=1, source_target_pairs={{0,16},{2,18},{4,20},{6,22},{8,24},{10,26},{12,28},{14,30},{16,0},... | collective-permute-start | bytes 196616 | tf_op jit(solution)/shard_map/ppermute | solution.py:238
  15.3 6.4 %collective-permute-start.2 = (bf16[128,256]{1,0:T(8,128)(2,1)}, bf16[128,256]{1,0:T(8,128)(2,1)S(1)}, u32[]{:S(2)}, u32[]{:S(2)}) collective-permute-start(bf16[128,256]{1,0:T(8,128)(2,1)} %get-tuple-element.30), channel_id=1, source_target_pairs={{0,24},{2,26},{4,28},{6,30},{8,16},{10,18},{12,20},{14,22},{16,8},... | collective-permute-start | bytes 196616 | tf_op jit(solution)/shard_map/ppermute | solution.py:238
  17.6 8.0 %collective-permute-start.9 = (bf16[512,256]{1,0:T(8,128)(2,1)S(1)}, bf16[512,256]{1,0:T(8,128)(2,1)S(1)}, u32[]{:S(2)}, u32[]{:S(2)}) collective-permute-start(bf16[512,256]{1,0:T(8,128)(2,1)S(1)} %pad_maximum_fusion.2), channel_id=1, source_target_pairs={{0,4},{2,6},{4,0},{6,2},{8,12},{10,14},{12,8},{14,10},{16,20},{18,... | collective-permute-start | bytes 786440 | tf_op jit(solution)/shard_map/ppermute | solution.py:238
  22.6 7.1 %collective-permute-start.3 = (bf16[512,256]{1,0:T(8,128)(2,1)S(1)}, bf16[512,256]{1,0:T(8,128)(2,1)S(1)}, u32[]{:S(2)}, u32[]{:S(2)}) collective-permute-start(bf16[512,256]{1,0:T(8,128)(2,1)S(1)} %pad_maximum_fusion.1), channel_id=1, source_target_pairs={{0,4},{2,6},{4,0},{6,2},{8,12},{10,14},{12,8},{14,10},{16,20},{18,... | collective-permute-start | bytes 786440 | tf_op jit(solution)/shard_map/ppermute | solution.py:238
  25.6 9.8 %collective-permute-start.10 = (bf16[1024,256]{1,0:T(8,128)(2,1)S(1)}, bf16[1024,256]{1,0:T(8,128)(2,1)S(1)}, u32[]{:S(2)}, u32[]{:S(2)}) collective-permute-start(bf16[1024,256]{1,0:T(8,128)(2,1)S(1)} %constant_dynamic-update-slice_fusion.5.same_ref), channel_id=1, source_target_pairs={{0,2},{2,0},{4,6},{6,4},{8,10},{10,8},{12,14},{14,12},{16,18},{18,... | collective-permute-start | bytes 1572872 | tf_op jit(solution)/shard_map/ppermute | solution.py:238
  29.7 10.7 %collective-permute-start.4 = (bf16[1024,256]{1,0:T(8,128)(2,1)S(1)}, bf16[1024,256]{1,0:T(8,128)(2,1)S(1)}, u32[]{:S(2)}, u32[]{:S(2)}) collective-permute-start(bf16[1024,256]{1,0:T(8,128)(2,1)S(1)} %constant_dynamic-update-slice_fusion.same_ref), channel_id=1, source_target_pairs={{0,2},{2,0},{4,6},{6,4},{8,10},{10,8},{12,14},{14,12},{16,18},{18,... | collective-permute-start | bytes 1572872 | tf_op jit(solution)/shard_map/ppermute | solution.py:238
  30.7 2.5 %copy-start.2 = (s32[1,1,80,128,128]{4,3,2,1,0:T(8,128)S(1)}, s32[1,1,80,128,128]{4,3,2,1,0:T(8,128)}, u32[]{:S(2)}) copy-start(s32[1,1,80,128,128]{4,3,2,1,0:T(8,128)} %param.16) | copy-start | bytes 15728644
  38.9 12.7 %collective-permute-start.13 = (bf16[512,256]{1,0:T(8,128)(2,1)S(1)}, bf16[512,256]{1,0:T(8,128)(2,1)S(1)}, u32[]{:S(2)}, u32[]{:S(2)}) collective-permute-start(bf16[512,256]{1,0:T(8,128)(2,1)S(1)} %get-tuple-element.36.rest_2_), channel_id=1, source_target_pairs={{0,1},{1,0},{2,3},{3,2},{4,5},{5,4},{6,7},{7,6},{8,9},{9,8},{10,11... | collective-permute-start | bytes 786440 | tf_op jit(solution)/shard_map/ppermute | solution.py:307
  43.9 9.9 %collective-permute-start.12 = (bf16[512,256]{1,0:T(8,128)(2,1)S(1)}, bf16[512,256]{1,0:T(8,128)(2,1)S(1)}, u32[]{:S(2)}, u32[]{:S(2)}) collective-permute-start(bf16[512,256]{1,0:T(8,128)(2,1)S(1)} %get-tuple-element.35.rest_0_), channel_id=1, source_target_pairs={{0,1},{1,0},{2,3},{3,2},{4,5},{5,4},{6,7},{7,6},{8,9},{9,8},{10,11... | collective-permute-start | bytes 786440 | tf_op jit(solution)/shard_map/ppermute | solution.py:307
  46.2 9.0 %copy-start = (bf16[2048,512]{1,0:T(8,128)(2,1)S(1)}, bf16[2048,512]{1,0:T(8,128)(2,1)}, u32[]{:S(2)}) copy-start(bf16[2048,512]{1,0:T(8,128)(2,1)} %user_ref.7) | copy-start | bytes 6291460
  46.2 8.9 %copy-start.1 = (bf16[2048,512]{1,0:T(8,128)(2,1)S(1)}, bf16[2048,512]{1,0:T(8,128)(2,1)}, u32[]{:S(2)}) copy-start(bf16[2048,512]{1,0:T(8,128)(2,1)} %grad_ref.7) | copy-start | bytes 6291460
  46.2 8.9 %copy-start.3 = (f32[512]{0:T(512)S(1)}, f32[512]{0:T(512)}, u32[]{:S(2)}) copy-start(f32[512]{0:T(512)} %param.11) | copy-start | bytes 6148
  46.2 13.1 %collective-permute-start.11 = (bf16[512,256]{1,0:T(8,128)(2,1)S(1)}, bf16[512,256]{1,0:T(8,128)(2,1)S(1)}, u32[]{:S(2)}, u32[]{:S(2)}) collective-permute-start(bf16[512,256]{1,0:T(8,128)(2,1)S(1)} %get-tuple-element.33.rest_2_), channel_id=1, source_target_pairs={{0,1},{1,0},{2,3},{3,2},{4,5},{5,4},{6,7},{7,6},{8,9},{9,8},{10,11... | collective-permute-start | bytes 786440 | tf_op jit(solution)/shard_map/ppermute | solution.py:307
  49.5 15.5 %collective-permute-start.5 = (bf16[512,256]{1,0:T(8,128)(2,1)S(1)}, bf16[512,256]{1,0:T(8,128)(2,1)S(1)}, u32[]{:S(2)}, u32[]{:S(2)}) collective-permute-start(bf16[512,256]{1,0:T(8,128)(2,1)S(1)} %get-tuple-element.31.rest_0_), channel_id=1, source_target_pairs={{0,1},{1,0},{2,3},{3,2},{4,5},{5,4},{6,7},{7,6},{8,9},{9,8},{10,11... | collective-permute-start | bytes 786440 | tf_op jit(solution)/shard_map/ppermute | solution.py:307
  50.1 20.5 %collective-permute-start.15 = (bf16[512,256]{1,0:T(8,128)(2,1)S(1)}, bf16[512,256]{1,0:T(8,128)(2,1)S(1)}, u32[]{:S(2)}, u32[]{:S(2)}) collective-permute-start(bf16[512,256]{1,0:T(8,128)(2,1)S(1)} %get-tuple-element.39.rest_2_), channel_id=1, source_target_pairs={{0,1},{1,0},{2,3},{3,2},{4,5},{5,4},{6,7},{7,6},{8,9},{9,8},{10,11... | collective-permute-start | bytes 786440 | tf_op jit(solution)/shard_map/ppermute | solution.py:307
  51.6 24.6 %collective-permute-start.14 = (bf16[512,256]{1,0:T(8,128)(2,1)S(1)}, bf16[512,256]{1,0:T(8,128)(2,1)S(1)}, u32[]{:S(2)}, u32[]{:S(2)}) collective-permute-start(bf16[512,256]{1,0:T(8,128)(2,1)S(1)} %get-tuple-element.38.rest_0_), channel_id=1, source_target_pairs={{0,1},{1,0},{2,3},{3,2},{4,5},{5,4},{6,7},{7,6},{8,9},{9,8},{10,11... | collective-permute-start | bytes 786440 | tf_op jit(solution)/shard_map/ppermute | solution.py:307
  53.7 28.1 %collective-permute-start.17 = (bf16[512,256]{1,0:T(8,128)(2,1)S(1)}, bf16[512,256]{1,0:T(8,128)(2,1)S(1)}, u32[]{:S(2)}, u32[]{:S(2)}) collective-permute-start(bf16[512,256]{1,0:T(8,128)(2,1)S(1)} %get-tuple-element.42.rest_2_), channel_id=1, source_target_pairs={{0,1},{1,0},{2,3},{3,2},{4,5},{5,4},{6,7},{7,6},{8,9},{9,8},{10,11... | collective-permute-start | bytes 786440 | tf_op jit(solution)/shard_map/ppermute | solution.py:307
  59.3 27.8 %collective-permute-start.16 = (bf16[512,256]{1,0:T(8,128)(2,1)S(1)}, bf16[512,256]{1,0:T(8,128)(2,1)S(1)}, u32[]{:S(2)}, u32[]{:S(2)}) collective-permute-start(bf16[512,256]{1,0:T(8,128)(2,1)S(1)} %get-tuple-element.41.rest_0_), channel_id=1, source_target_pairs={{0,1},{1,0},{2,3},{3,2},{4,5},{5,4},{6,7},{7,6},{8,9},{9,8},{10,11... | collective-permute-start | bytes 786440 | tf_op jit(solution)/shard_map/ppermute | solution.py:307
  89.7 8.3 %collective-permute-start.20 = (bf16[2,2,2,128,256]{4,3,0,2,1:T(8,128)(2,1)S(1)}, bf16[2,2,2,128,256]{4,3,0,2,1:T(8,128)(2,1)S(1)}, u32[]{:S(2)}, u32[]{:S(2)}) collective-permute-start(bf16[2,2,2,128,256]{4,3,0,2,1:T(8,128)(2,1)S(1)} %fusion.23), channel_id=1, source_target_pairs={{0,2},{2,0},{4,6},{6,4},{8,10},{10,8},{12,14},{14,12},{16,18},{18,... | collective-permute-start | bytes 1572872 | tf_op jit(solution)/shard_map/ppermute | solution.py:238
  89.8 1.9 %collective-permute-start.34 = (f32[256]{0:T(256)S(1)}, f32[256]{0:T(256)S(1)}, u32[]{:S(2)}, u32[]{:S(2)}) collective-permute-start(f32[256]{0:T(256)S(1)} %bitcast.138), channel_id=1, source_target_pairs={{0,2},{2,0},{4,6},{6,4},{8,10},{10,8},{12,14},{14,12},{16,18},{18,... | collective-permute-start | bytes 3080 | tf_op jit(solution)/shard_map/ppermute | solution.py:238
  90.3 7.9 %collective-permute-start.18 = (bf16[2,2,2,128,256]{4,3,0,1,2:T(8,128)(2,1)S(1)}, bf16[2,2,2,128,256]{4,3,0,1,2:T(8,128)(2,1)S(1)}, u32[]{:S(2)}, u32[]{:S(2)}) collective-permute-start(bf16[2,2,2,128,256]{4,3,0,1,2:T(8,128)(2,1)S(1)} %fusion.22), channel_id=1, source_target_pairs={{0,2},{2,0},{4,6},{6,4},{8,10},{10,8},{12,14},{14,12},{16,18},{18,... | collective-permute-start | bytes 1572872 | tf_op jit(solution)/shard_map/ppermute | solution.py:238
  91.7 3.6 %collective-permute-start.35 = (f32[256]{0:T(256)S(1)}, f32[256]{0:T(256)S(1)}, u32[]{:S(2)}, u32[]{:S(2)}) collective-permute-start(f32[256]{0:T(256)S(1)} %add.227), channel_id=1, source_target_pairs={{0,4},{2,6},{4,0},{6,2},{8,12},{10,14},{12,8},{14,10},{16,20},{18,... | collective-permute-start | bytes 3080 | tf_op jit(solution)/shard_map/ppermute | solution.py:238
  95.2 4.9 %collective-permute-start.36 = (f32[256]{0:T(256)S(1)}, f32[256]{0:T(256)S(1)}, u32[]{:S(2)}, u32[]{:S(2)}) collective-permute-start(f32[256]{0:T(256)S(1)} %add.228), channel_id=1, source_target_pairs={{0,8},{2,10},{4,12},{6,14},{8,0},{10,2},{12,4},{14,6},{16,24},{18,... | collective-permute-start | bytes 3080 | tf_op jit(solution)/shard_map/ppermute | solution.py:238
  98.2 7.0 %collective-permute-start.21 = (bf16[2,2,128,256]{3,2,0,1:T(8,128)(2,1)S(1)}, bf16[2,2,128,256]{3,2,0,1:T(8,128)(2,1)S(1)}, u32[]{:S(2)}, u32[]{:S(2)}) collective-permute-start(bf16[2,2,128,256]{3,2,0,1:T(8,128)(2,1)S(1)} %fusion.34), channel_id=1, source_target_pairs={{0,8},{2,10},{4,12},{6,14},{8,0},{10,2},{12,4},{14,6},{16,24},{18,... | collective-permute-start | bytes 786440 | tf_op jit(solution)/shard_map/ppermute | solution.py:238
  98.4 7.0 %collective-permute-start.19 = (bf16[2,2,128,256]{3,2,0,1:T(8,128)(2,1)S(1)}, bf16[2,2,128,256]{3,2,0,1:T(8,128)(2,1)S(1)}, u32[]{:S(2)}, u32[]{:S(2)}) collective-permute-start(bf16[2,2,128,256]{3,2,0,1:T(8,128)(2,1)S(1)} %fusion.33), channel_id=1, source_target_pairs={{0,4},{2,6},{4,0},{6,2},{8,12},{10,14},{12,8},{14,10},{16,20},{18,... | collective-permute-start | bytes 786440 | tf_op jit(solution)/shard_map/ppermute | solution.py:238
  100.2 8.1 %collective-permute-start.37 = (f32[256]{0:T(256)S(1)}, f32[256]{0:T(256)S(1)}, u32[]{:S(2)}, u32[]{:S(2)}) collective-permute-start(f32[256]{0:T(256)S(1)} %add.229), channel_id=1, source_target_pairs={{0,16},{2,18},{4,20},{6,22},{8,24},{10,26},{12,28},{14,30},{16,0},... | collective-permute-start | bytes 3080 | tf_op jit(solution)/shard_map/ppermute | solution.py:238
  105.5 5.1 %collective-permute-start.23 = (bf16[2,128,256]{2,1,0:T(8,128)(2,1)S(1)}, bf16[2,128,256]{2,1,0:T(8,128)(2,1)S(1)}, u32[]{:S(2)}, u32[]{:S(2)}) collective-permute-start(bf16[2,128,256]{2,1,0:T(8,128)(2,1)S(1)} %fusion.40), channel_id=1, source_target_pairs={{0,4},{2,6},{4,0},{6,2},{8,12},{10,14},{12,8},{14,10},{16,20},{18,... | collective-permute-start | bytes 393224 | tf_op jit(solution)/shard_map/ppermute | solution.py:238
  108.8 5.0 %collective-permute-start.22 = (bf16[2,128,256]{2,1,0:T(8,128)(2,1)S(1)}, bf16[2,128,256]{2,1,0:T(8,128)(2,1)S(1)}, u32[]{:S(2)}, u32[]{:S(2)}) collective-permute-start(bf16[2,128,256]{2,1,0:T(8,128)(2,1)S(1)} %fusion.39), channel_id=1, source_target_pairs={{0,8},{2,10},{4,12},{6,14},{8,0},{10,2},{12,4},{14,6},{16,24},{18,... | collective-permute-start | bytes 393224 | tf_op jit(solution)/shard_map/ppermute | solution.py:238
  113.9 6.9 %collective-permute-start.25 = (bf16[128,256]{1,0:T(8,128)(2,1)S(1)}, bf16[128,256]{1,0:T(8,128)(2,1)S(1)}, u32[]{:S(2)}, u32[]{:S(2)}) collective-permute-start(bf16[128,256]{1,0:T(8,128)(2,1)S(1)} %fusion.46), channel_id=1, source_target_pairs={{0,16},{2,18},{4,20},{6,22},{8,24},{10,26},{12,28},{14,30},{16,0},... | collective-permute-start | bytes 196616 | tf_op jit(solution)/shard_map/ppermute | solution.py:238
  117.9 5.2 %collective-permute-start.24 = (bf16[128,256]{1,0:T(8,128)(2,1)S(1)}, bf16[128,256]{1,0:T(8,128)(2,1)S(1)}, u32[]{:S(2)}, u32[]{:S(2)}) collective-permute-start(bf16[128,256]{1,0:T(8,128)(2,1)S(1)} %fusion.45), channel_id=1, source_target_pairs={{0,16},{2,18},{4,20},{6,22},{8,24},{10,26},{12,28},{14,30},{16,0},... | collective-permute-start | bytes 196616 | tf_op jit(solution)/shard_map/ppermute | solution.py:238
  121.3 2.4 %copy-start.5 = (bf16[4,512,512]{2,1,0:T(8,128)(2,1)S(1)}, bf16[4,512,512]{2,1,0:T(8,128)(2,1)}, u32[]{:S(2)}) copy-start(bf16[4,512,512]{2,1,0:T(8,128)(2,1)} %weight_ref.1) | copy-start | bytes 6291460
  121.4 3.0 %collective-permute-start.28 = (bf16[2,2,2,128,256]{4,3,0,2,1:T(8,128)(2,1)S(1)}, bf16[2,2,2,128,256]{4,3,0,2,1:T(8,128)(2,1)S(1)}, u32[]{:S(2)}, u32[]{:S(2)}) collective-permute-start(bf16[2,2,2,128,256]{4,3,0,2,1:T(8,128)(2,1)S(1)} %fusion.24), channel_id=1, source_target_pairs={{0,2},{2,0},{4,6},{6,4},{8,10},{10,8},{12,14},{14,12},{16,18},{18,... | collective-permute-start | bytes 1572872 | tf_op jit(solution)/shard_map/ppermute | solution.py:238
  123.6 2.0 %collective-permute-start.26 = (bf16[2,2,2,128,256]{4,3,2,1,0:T(8,128)(2,1)S(1)}, bf16[2,2,2,128,256]{4,3,2,1,0:T(8,128)(2,1)S(1)}, u32[]{:S(2)}, u32[]{:S(2)}) collective-permute-start(bf16[2,2,2,128,256]{4,3,2,1,0:T(8,128)(2,1)S(1)} %fusion.21), channel_id=1, source_target_pairs={{0,2},{2,0},{4,6},{6,4},{8,10},{10,8},{12,14},{14,12},{16,18},{18,... | collective-permute-start | bytes 1572872 | tf_op jit(solution)/shard_map/ppermute | solution.py:238
  124.5 8.8 %collective-permute-start.29 = (bf16[2,2,128,256]{3,2,0,1:T(8,128)(2,1)S(1)}, bf16[2,2,128,256]{3,2,0,1:T(8,128)(2,1)S(1)}, u32[]{:S(2)}, u32[]{:S(2)}) collective-permute-start(bf16[2,2,128,256]{3,2,0,1:T(8,128)(2,1)S(1)} %fusion.36), channel_id=1, source_target_pairs={{0,8},{2,10},{4,12},{6,14},{8,0},{10,2},{12,4},{14,6},{16,24},{18,... | collective-permute-start | bytes 786440 | tf_op jit(solution)/shard_map/ppermute | solution.py:238
  125.8 8.4 %collective-permute-start.27 = (bf16[2,2,128,256]{3,2,1,0:T(8,128)(2,1)S(1)}, bf16[2,2,128,256]{3,2,1,0:T(8,128)(2,1)S(1)}, u32[]{:S(2)}, u32[]{:S(2)}) collective-permute-start(bf16[2,2,128,256]{3,2,1,0:T(8,128)(2,1)S(1)} %fusion.35), channel_id=1, source_target_pairs={{0,4},{2,6},{4,0},{6,2},{8,12},{10,14},{12,8},{14,10},{16,20},{18,... | collective-permute-start | bytes 786440 | tf_op jit(solution)/shard_map/ppermute | solution.py:238
  134.3 5.0 %collective-permute-start.31 = (bf16[2,128,256]{2,1,0:T(8,128)(2,1)S(1)}, bf16[2,128,256]{2,1,0:T(8,128)(2,1)S(1)}, u32[]{:S(2)}, u32[]{:S(2)}) collective-permute-start(bf16[2,128,256]{2,1,0:T(8,128)(2,1)S(1)} %fusion.42), channel_id=1, source_target_pairs={{0,4},{2,6},{4,0},{6,2},{8,12},{10,14},{12,8},{14,10},{16,20},{18,... | collective-permute-start | bytes 393224 | tf_op jit(solution)/shard_map/ppermute | solution.py:238
  135.6 5.0 %collective-permute-start.30 = (bf16[2,128,256]{2,1,0:T(8,128)(2,1)S(1)}, bf16[2,128,256]{2,1,0:T(8,128)(2,1)S(1)}, u32[]{:S(2)}, u32[]{:S(2)}) collective-permute-start(bf16[2,128,256]{2,1,0:T(8,128)(2,1)S(1)} %fusion.41), channel_id=1, source_target_pairs={{0,8},{2,10},{4,12},{6,14},{8,0},{10,2},{12,4},{14,6},{16,24},{18,... | collective-permute-start | bytes 393224 | tf_op jit(solution)/shard_map/ppermute | solution.py:238
  140.7 6.0 %collective-permute-start.32 = (bf16[128,256]{1,0:T(8,128)(2,1)S(1)}, bf16[128,256]{1,0:T(8,128)(2,1)S(1)}, u32[]{:S(2)}, u32[]{:S(2)}) collective-permute-start(bf16[128,256]{1,0:T(8,128)(2,1)S(1)} %fusion.47), channel_id=1, source_target_pairs={{0,16},{2,18},{4,20},{6,22},{8,24},{10,26},{12,28},{14,30},{16,0},... | collective-permute-start | bytes 196616 | tf_op jit(solution)/shard_map/ppermute | solution.py:238
  142.1 6.1 %collective-permute-start.33 = (bf16[128,256]{1,0:T(8,128)(2,1)S(1)}, bf16[128,256]{1,0:T(8,128)(2,1)S(1)}, u32[]{:S(2)}, u32[]{:S(2)}) collective-permute-start(bf16[128,256]{1,0:T(8,128)(2,1)S(1)} %fusion.48), channel_id=1, source_target_pairs={{0,16},{2,18},{4,20},{6,22},{8,24},{10,26},{12,28},{14,30},{16,0},... | collective-permute-start | bytes 196616 | tf_op jit(solution)/shard_map/ppermute | solution.py:238

commit v8 on v7

--- a/solution.py
+++ b/solution.py
@@ -15,27 +15,26 @@
 MIB = 1024 * 1024
 
 
-def place_tiles(item_blocks, place_ref, count_ref, level_ref, dense_ref):
+def place_tiles(item_blocks, place_ref, count_ref, weight_ref, dense_ref):
     step = pl.program_id(0)
 
     @pl.when(step == 0)
     def _():
         dense_ref[...] = jnp.zeros_like(dense_ref)
 
-    for offset in range(level_ref.shape[0]):
-        slot = step * level_ref.shape[0] + offset
+    for offset in range(weight_ref.shape[0]):
+        slot = step * weight_ref.shape[0] + offset
 
         @pl.when(slot < count_ref[0])
         def _():
             place = place_ref[slot]
             row = pl.multiple_of((place // item_blocks) * TILE, TILE)
             col = pl.multiple_of((place % item_blocks) * TILE, TILE)
-            weights = level_ref[offset].astype(jnp.float32) * (1.0 / (2.0 * TILE))
-            dense_ref[pl.ds(row, TILE), pl.ds(col, TILE)] = weights.astype(jnp.bfloat16)
-
-
-def dense_tiles(place, count, level, users, items):
-    slots = level.shape[0]
+            dense_ref[pl.ds(row, TILE), pl.ds(col, TILE)] = weight_ref[offset]
+
+
+def dense_tiles(place, count, weights, users, items):
+    slots = weights.shape[0]
     per_step = SLOTS_PER_STEP if slots % SLOTS_PER_STEP == 0 else 1
     return pl.pallas_call(
         functools.partial(place_tiles, items // TILE),
@@ -53,11 +52,11 @@
         ),
         cost_estimate=pl.CostEstimate(
             flops=slots * TILE * TILE,
-            bytes_accessed=slots * TILE * TILE * 4 + users * items * 2,
+            bytes_accessed=slots * TILE * TILE * 2 + users * items * 2,
             transcendentals=0,
         ),
         name="place_tiles",
-    )(place, count, level)
+    )(place, count, weights)
 
 
 def project_own(first_ref, cats_ref, feat_ref, weight_ref, *rest):
@@ -292,14 +291,16 @@
 
     own_halves = own_queries(first_expert, own_cats, own_feat, expert_w)
     order = gather_order(user_size)
-    dense = dense_tiles(tile_place[0, 0], tile_count[0], tile_level[0, 0], users, items)
+    weights = (tile_level[0, 0].astype(jnp.float32) * (1.0 / (2.0 * TILE))).astype(jnp.bfloat16)
+    dense = dense_tiles(tile_place[0, 0], tile_count[0], weights, users, items)
     layers = [gather_layers(own, user_size) for own in own_halves]
     queries = [gather_sides(part, user_size) for part in layers]
 
     partials = [[] for _ in range(HALVES)]
     for half in range(HALVES):
+        last = order
         for first, count in ((0, 1), (1, ROW_CHUNKS - 1)):
-            *products, last = spread_items(order, queries[half], dense, first, (1,) * count, rows)
+            *products, last = spread_items(last, queries[half], dense, first, (1,) * count, rows)
             for product in products:
                 pieces = [product]
                 for shift in range(1, item_size):
@@ -330,9 +331,7 @@
         [lax.dynamic_slice_in_dim(grad, item_index * col_width, col_width, 1) for grad in grads],
         axis=0,
     )
-    gain_grad = lax.dynamic_slice_in_dim(gain_term, item_index * col_width, col_width, 0)
-    for bit in range(user_size.bit_length() - 1):
-        gain_grad = gain_grad + flip(gain_grad, user_size, 1 << bit)
+    gain_own = lax.dynamic_slice_in_dim(gain_term, item_index * col_width, col_width, 0)
 
     halves = []
     for half in range(HALVES):
@@ -359,7 +358,12 @@
         ).reshape(user_size, experts_here * own_width, half_width)
         for half in sums
     ]
-    expert_grad = jnp.concatenate(scatter_sums(halves, user_size), axis=1)
+    gain_rows = jnp.pad(gain_own, (0, 8 * half_width - col_width)).reshape(1, 8, half_width)
+    gain_rows = jnp.broadcast_to(gain_rows, (user_size, 8, half_width))
+    halves[0] = jnp.concatenate([halves[0], gain_rows], axis=1)
+    halves = scatter_sums(halves, user_size)
+    gain_grad = halves[0][-8:].reshape(-1)[:col_width]
+    expert_grad = jnp.concatenate([halves[0][:-8], halves[1]], axis=1)
     own_sums = jnp.concatenate(sums, axis=1)
     item_total = jnp.zeros((own_items, width), jnp.float32)
     for expert in range(experts_here):

time: 150 us -> 145 us (0.967)
  starting transfers between devices: 45.5 us -> 36.4 us
  Pallas kernels: 19.1 us -> 24 us
  waiting for transfers between devices: 64.8 us -> 60.3 us
  local copies, waits for them, and re-layouts: 4.19 us -> 6.73 us
  other arithmetic: 5.05 us -> 7.15 us
    ppermute x30 -> x26, starting transfers between devices: 36.3 us -> 26.7 us  [flip(): lax.ppermute(value, 'user', [(source, source ^ bits) for source in range(...]
    pallas_call x4, Pallas kernels: 10.3 us -> 15.2 us  [spread_items(): pl.pallas_call(functools.partial(spread, blocks), out_shape=[jax.ShapeDty...]
    ppermute x8, waiting for transfers between devices: 26 us -> 21.9 us  [on_device(): pieces.append(lax.ppermute(product, 'item', pairs))]
    convert_element_type x0 -> x1, other arithmetic: none -> 3.27 us  [on_device(): (tile_level[0, 0].astype(jnp.float32) * (1.0 / (2.0 * TILE))).astype(jnp....]
    unnamed x24 -> x26, local copies, waits for them, and re-layouts: 3.56 us -> 4.75 us
    ppermute x30 -> x26, waiting for transfers between devices: 38.8 us -> 38.4 us  [flip(): lax.ppermute(value, 'user', [(source, source ^ bits) for source in range(...]
  transfers between devices with their start and end apart: 38 -> 34, of which waited for: 26 -> 18; matrix products, arithmetic and copies ran while one was open for 8% -> 12% of each run, Pallas kernels for 10% -> 13%
where the time goes in v8:
time: 145 us
  waiting for transfers between devices  60.3 us (42%)
  starting transfers between devices  36.4 us (25%)
  Pallas kernels  24 us (17%)
  matrix products  8.38 us (6%)
  other arithmetic  7.15 us (5%)
  local copies, waits for them, and re-layouts  6.73 us (5%)
  between operations  1.94 us (1%)
    ppermute x26, waiting for transfers between devices, flip(): lax.ppermute(value, 'user', [(source, source ^ bits) for source in range(...  38.4 us
    ppermute x26, starting transfers between devices, flip(): lax.ppermute(value, 'user', [(source, source ^ bits) for source in range(...  26.7 us
    ppermute x8, waiting for transfers between devices, on_device(): pieces.append(lax.ppermute(product, 'item', pairs))  21.9 us
    pallas_call x4, Pallas kernels, spread_items(): pl.pallas_call(functools.partial(spread, blocks), out_shape=[jax.ShapeDty...  15.2 us
    ppermute x8, starting transfers between devices, on_device(): pieces.append(lax.ppermute(product, 'item', pairs))  9.69 us
    unnamed x26, local copies, waits for them, and re-layouts  4.75 us
    dot_general x3, matrix products, on_device(): lax.dot_general(dense[chunk * rows:(chunk + 1) * rows], grad, (((0,), (0,...  4.05 us
    pallas_call x1, Pallas kernels, own_queries(): pl.pallas_call(project_own, out_shape=[half] * HALVES, grid_spec=pltpu.Pr...  3.64 us
  transfers between devices with their start and end apart: 34, of which 18 were waited for; matrix products, arithmetic and copies ran while one was open for 12% of the time, Pallas kernels for 13%

profile of v8, /device:TPU:0, one launch (start us, length us, event | category | flops | bytes accessed | tf_op | source)
XLA Modules:
  0.0 144.9 jit_solution(13141891467036296478)
XLA Ops:
  0.6 3.6 %own_queries.1 = (bf16[128,256]{1,0:T(8,128)(2,1)}, bf16[128,256]{1,0:T(8,128)(2,1)}) custom-call(s32[1]{0:T(128)} %bitcast.1.first_ref, s32[1,128]{1,0:T(1,128)} %cats_ref.1, bf16[128,512]{1,0:T(8,128)(2,1)} %bitcast.139, bf16[4,512,512]{2,1,0:T(8,128)(2,1)} %weight_ref.1), custom_call_target="tpu_custom_call" | custom-call | flops 268435456 | bytes 2359296 | tf_op jit(solution)/shard_map/own_queries/pallas_call | solution.py:96
  4.3 3.0 %collective-permute-start = (bf16[128,256]{1,0:T(8,128)(2,1)}, bf16[128,256]{1,0:T(8,128)(2,1)S(1)}, u32[]{:S(2)}, u32[]{:S(2)}) collective-permute-start(bf16[128,256]{1,0:T(8,128)(2,1)} %get-tuple-element.32), channel_id=1, source_target_pairs={{0,8},{2,10},{4,12},{6,14},{8,0},{10,2},{12,4},{14,6},{16,24},{18,... | collective-permute-start | bytes 196616 | tf_op jit(solution)/shard_map/ppermute | solution.py:237
  7.3 2.6 %collective-permute-start.1 = (bf16[128,256]{1,0:T(8,128)(2,1)}, bf16[128,256]{1,0:T(8,128)(2,1)S(1)}, u32[]{:S(2)}, u32[]{:S(2)}) collective-permute-start(bf16[128,256]{1,0:T(8,128)(2,1)} %get-tuple-element.32), channel_id=1, source_target_pairs={{0,16},{2,18},{4,20},{6,22},{8,24},{10,26},{12,28},{14,30},{16,0},... | collective-permute-start | bytes 196616 | tf_op jit(solution)/shard_map/ppermute | solution.py:237
  9.9 0.9 collective-permute-start.6
  10.8 3.5 %collective-permute-start.7 = (bf16[128,256]{1,0:T(8,128)(2,1)}, bf16[128,256]{1,0:T(8,128)(2,1)}, u32[]{:S(2)}, u32[]{:S(2)}) collective-permute-start(bf16[128,256]{1,0:T(8,128)(2,1)} %get-tuple-element.34), channel_id=1, source_target_pairs={{0,16},{2,18},{4,20},{6,22},{8,24},{10,26},{12,28},{14,30},{16,0},... | collective-permute-start | bytes 196616 | tf_op jit(solution)/shard_map/ppermute | solution.py:237
  14.3 3.3 %fusion.weight_ref = bf16[80,128,128]{2,1,0:T(8,128)(2,1)S(1)} fusion(s32[1,1,80,128,128]{4,3,2,1,0:T(8,128)} %param.16), kind=kLoop, calls=%fused_computation.2 | loop fusion | flops 3932160 | bytes 7864320 | tf_op jit(solution)/shard_map/convert_element_type | solution.py:294
  18.4 1.8 %collective-permute-start.3 = (bf16[512,256]{1,0:T(8,128)(2,1)S(1)}, bf16[512,256]{1,0:T(8,128)(2,1)S(1)}, u32[]{:S(2)}, u32[]{:S(2)}) collective-permute-start(bf16[512,256]{1,0:T(8,128)(2,1)S(1)} %pad_maximum_fusion.2), channel_id=1, source_target_pairs={{0,4},{2,6},{4,0},{6,2},{8,12},{10,14},{12,8},{14,10},{16,20},{18,... | collective-permute-start | bytes 786440 | tf_op jit(solution)/shard_map/ppermute | solution.py:237
  20.2 4.2 %collective-permute-done.8 = bf16[128,256]{1,0:T(8,128)(2,1)S(1)} collective-permute-done((bf16[128,256]{1,0:T(8,128)(2,1)S(1)}, bf16[128,256]{1,0:T(8,128)(2,1)S(1)}, u32[]{:S(2)}, u32[]{:S(2)}) %collective-permute-start.8) | collective-permute-done | bytes 65568 | tf_op jit(solution)/shard_map/ppermute | solution.py:237
  24.4 0.9 pad_maximum_fusion.3
  25.3 1.6 %collective-permute-start.9 = (bf16[512,256]{1,0:T(8,128)(2,1)S(1)}, bf16[512,256]{1,0:T(8,128)(2,1)S(1)}, u32[]{:S(2)}, u32[]{:S(2)}) collective-permute-start(bf16[512,256]{1,0:T(8,128)(2,1)S(1)} %pad_maximum_fusion.3), channel_id=1, source_target_pairs={{0,4},{2,6},{4,0},{6,2},{8,12},{10,14},{12,8},{14,10},{16,20},{18,... | collective-permute-start | bytes 786440 | tf_op jit(solution)/shard_map/ppermute | solution.py:237
  30.3 1.4 collective-permute-done.9
  32.6 2.2 %place_tiles.1.dense_ref = bf16[2048,2048]{1,0:T(8,128)(2,1)S(1)} custom-call(s32[80]{0:T(128)S(1)} %bitcast.130, s32[1]{0:T(128)} %bitcast.125.count_ref, bf16[80,128,128]{2,1,0:T(8,128)(2,1)S(1)} %fusion.weight_ref), custom_call_target="tpu_custom_call" | custom-call | flops 1310720 | bytes 11010048 | tf_op jit(solution)/shard_map/place_tiles/pallas_call | solution.py:39
  34.9 3.0 %spread_items.4 = (bf16[512,256]{1,0:T(8,128)(2,1)S(1)}, s32[16]{0:T(128)S(1)}) custom-call(s32[16]{0:T(128)S(1)} %fusion.60.order_ref, bf16[1024,256]{1,0:T(8,128)(2,1)} %constant_dynamic-update-slice_fusion.same_ref, bf16[1024,256]{1,0:T(8,128)(2,1)} %collective-permute-done.4.other_ref, bf16[2048,2048]{1,0:T(8,128)(2,1)S(1)} %place_tiles.1.dense_ref), custom_call_target="tpu_custom_call" | custom-call | flops 536870912 | bytes 3407872 | tf_op jit(solution)/shard_map/spread_items/pallas_call | solution.py:152
  37.9 1.7 %collective-permute-start.5 = (bf16[512,256]{1,0:T(8,128)(2,1)S(1)}, bf16[512,256]{1,0:T(8,128)(2,1)S(1)}, u32[]{:S(2)}, u32[]{:S(2)}) collective-permute-start(bf16[512,256]{1,0:T(8,128)(2,1)S(1)} %get-tuple-element.33.rest_0_), channel_id=1, source_target_pairs={{0,1},{1,0},{2,3},{3,2},{4,5},{5,4},{6,7},{7,6},{8,9},{9,8},{10,11... | collective-permute-start | bytes 786440 | tf_op jit(solution)/shard_map/ppermute | solution.py:308
  39.6 2.8 %spread_items.5 = (bf16[512,256]{1,0:T(8,128)(2,1)S(1)}, s32[16]{0:T(128)S(1)}) custom-call(s32[16]{0:T(128)S(1)} %fusion.60.order_ref, bf16[1024,256]{1,0:T(8,128)(2,1)S(1)} %constant_dynamic-update-slice_fusion.5.same_ref, bf16[1024,256]{1,0:T(8,128)(2,1)} %collective-permute-done.10.other_ref, bf16[2048,2048]{1,0:T(8,128)(2,1)S(1)} %place_tiles.1.dense_ref), custom_call_target="tpu_custom_call" | custom-call | flops 536870912 | bytes 3407872 | tf_op jit(solution)/shard_map/spread_items/pallas_call | solution.py:152
  42.9 4.6 %spread_items.6 = (bf16[512,256]{1,0:T(8,128)(2,1)S(1)}, bf16[512,256]{1,0:T(8,128)(2,1)S(1)}, bf16[512,256]{1,0:T(8,128)(2,1)S(1)}, s32[16]{0:T(128)}) custom-call(s32[16]{0:T(128)S(1)} %get-tuple-element.37.order_ref, bf16[1024,256]{1,0:T(8,128)(2,1)} %constant_dynamic-update-slice_fusion.same_ref, bf16[1024,256]{1,0:T(8,128)(2,1)} %collective-permute-done.4.other_ref, ...), custom_call_target="tpu_custom_call" | custom-call | flops 1610612736 | bytes 8126464 | tf_op jit(solution)/shard_map/spread_items/pallas_call | solution.py:152
  47.5 1.7 %collective-permute-start.16 = (bf16[512,256]{1,0:T(8,128)(2,1)S(1)}, bf16[512,256]{1,0:T(8,128)(2,1)S(1)}, u32[]{:S(2)}, u32[]{:S(2)}) collective-permute-start(bf16[512,256]{1,0:T(8,128)(2,1)S(1)} %get-tuple-element.45.rest_0_), channel_id=1, source_target_pairs={{0,1},{1,0},{2,3},{3,2},{4,5},{5,4},{6,7},{7,6},{8,9},{9,8},{10,11... | collective-permute-start | bytes 786440 | tf_op jit(solution)/shard_map/ppermute | solution.py:308
  49.3 4.8 %spread_items.7 = (bf16[512,256]{1,0:T(8,128)(2,1)S(1)}, bf16[512,256]{1,0:T(8,128)(2,1)S(1)}, bf16[512,256]{1,0:T(8,128)(2,1)S(1)}, s32[16]{0:T(128)}) custom-call(s32[16]{0:T(128)S(1)} %get-tuple-element.39.order_ref, bf16[1024,256]{1,0:T(8,128)(2,1)S(1)} %constant_dynamic-update-slice_fusion.5.same_ref, ...), custom_call_target="tpu_custom_call" | custom-call | flops 1610612736 | bytes 8126464 | tf_op jit(solution)/shard_map/spread_items/pallas_call | solution.py:152
  54.4 1.7 %collective-permute-start.14 = (bf16[512,256]{1,0:T(8,128)(2,1)S(1)}, bf16[512,256]{1,0:T(8,128)(2,1)S(1)}, u32[]{:S(2)}, u32[]{:S(2)}) collective-permute-start(bf16[512,256]{1,0:T(8,128)(2,1)S(1)} %get-tuple-element.42.rest_0_), channel_id=1, source_target_pairs={{0,1},{1,0},{2,3},{3,2},{4,5},{5,4},{6,7},{7,6},{8,9},{9,8},{10,11... | collective-permute-start | bytes 786440 | tf_op jit(solution)/shard_map/ppermute | solution.py:308
  56.5 1.7 %collective-permute-start.13 = (bf16[512,256]{1,0:T(8,128)(2,1)S(1)}, bf16[512,256]{1,0:T(8,128)(2,1)S(1)}, u32[]{:S(2)}, u32[]{:S(2)}) collective-permute-start(bf16[512,256]{1,0:T(8,128)(2,1)S(1)} %get-tuple-element.40.rest_2_), channel_id=1, source_target_pairs={{0,1},{1,0},{2,3},{3,2},{4,5},{5,4},{6,7},{7,6},{8,9},{9,8},{10,11... | collective-permute-start | bytes 786440 | tf_op jit(solution)/shard_map/ppermute | solution.py:308
  58.9 1.3 fusion.7
  60.2 15.0 %collective-permute-done.12.rest_1_ = bf16[512,256]{1,0:T(8,128)(2,1)S(1)} collective-permute-done((bf16[512,256]{1,0:T(8,128)(2,1)S(1)}, bf16[512,256]{1,0:T(8,128)(2,1)S(1)}, u32[]{:S(2)}, u32[]{:S(2)}) %collective-permute-start.12) | collective-permute-done | bytes 262176 | tf_op jit(solution)/shard_map/ppermute | solution.py:308
  75.1 1.7 %collective-permute-start.15 = (bf16[512,256]{1,0:T(8,128)(2,1)S(1)}, bf16[512,256]{1,0:T(8,128)(2,1)S(1)}, u32[]{:S(2)}, u32[]{:S(2)}) collective-permute-start(bf16[512,256]{1,0:T(8,128)(2,1)S(1)} %get-tuple-element.43.rest_2_), channel_id=1, source_target_pairs={{0,1},{1,0},{2,3},{3,2},{4,5},{5,4},{6,7},{7,6},{8,9},{9,8},{10,11... | collective-permute-start | bytes 786440 | tf_op jit(solution)/shard_map/ppermute | solution.py:308
  76.8 3.9 %collective-permute-done.13.rest_3_ = bf16[512,256]{1,0:T(8,128)(2,1)S(1)} collective-permute-done((bf16[512,256]{1,0:T(8,128)(2,1)S(1)}, bf16[512,256]{1,0:T(8,128)(2,1)S(1)}, u32[]{:S(2)}, u32[]{:S(2)}) %collective-permute-start.13) | collective-permute-done | bytes 262176 | tf_op jit(solution)/shard_map/ppermute | solution.py:308
  81.5 1.3 fusion.5
  82.8 3.0 %collective-permute-done.15.rest_3_ = bf16[512,256]{1,0:T(8,128)(2,1)S(1)} collective-permute-done((bf16[512,256]{1,0:T(8,128)(2,1)S(1)}, bf16[512,256]{1,0:T(8,128)(2,1)S(1)}, u32[]{:S(2)}, u32[]{:S(2)}) %collective-permute-start.15) | collective-permute-done | bytes 262176 | tf_op jit(solution)/shard_map/ppermute | solution.py:308
  86.5 1.4 add_add_fusion
  88.0 0.9 user_gradient.7
  91.4 1.2 collective-permute-done.18
  92.7 1.8 %collective-permute-start.19 = (bf16[2,2,128,256]{3,2,0,1:T(8,128)(2,1)S(1)}, bf16[2,2,128,256]{3,2,0,1:T(8,128)(2,1)S(1)}, u32[]{:S(2)}, u32[]{:S(2)}) collective-permute-start(bf16[2,2,128,256]{3,2,0,1:T(8,128)(2,1)S(1)} %fusion.35), channel_id=1, source_target_pairs={{0,4},{2,6},{4,0},{6,2},{8,12},{10,14},{12,8},{14,10},{16,20},{18,... | collective-permute-start | bytes 786440 | tf_op jit(solution)/shard_map/ppermute | solution.py:237
  94.8 1.0 pad_maximum_fusion.1
  95.8 5.3 %collective-permute-done.19 = bf16[2,2,128,256]{3,2,0,1:T(8,128)(2,1)S(1)} collective-permute-done((bf16[2,2,128,256]{3,2,0,1:T(8,128)(2,1)S(1)}, bf16[2,2,128,256]{3,2,0,1:T(8,128)(2,1)S(1)}, u32[]{:S(2)}, u32[]{:S(2)}) %collective-permute-start.19) | collective-permute-done | bytes 262176 | tf_op jit(solution)/shard_map/ppermute | solution.py:237
  101.2 1.6 %collective-permute-done.21 = bf16[2,2,128,256]{3,2,0,1:T(8,128)(2,1)S(1)} collective-permute-done((bf16[2,2,128,256]{3,2,0,1:T(8,128)(2,1)S(1)}, bf16[2,2,128,256]{3,2,0,1:T(8,128)(2,1)S(1)}, u32[]{:S(2)}, u32[]{:S(2)}) %collective-permute-start.21) | collective-permute-done | bytes 262176 | tf_op jit(solution)/shard_map/ppermute | solution.py:237
  104.1 3.8 %collective-permute-done.22 = bf16[2,128,256]{2,1,0:T(8,128)(2,1)S(1)} collective-permute-done((bf16[2,128,256]{2,1,0:T(8,128)(2,1)S(1)}, bf16[2,128,256]{2,1,0:T(8,128)(2,1)S(1)}, u32[]{:S(2)}, u32[]{:S(2)}) %collective-permute-start.22) | collective-permute-done | bytes 131104 | tf_op jit(solution)/shard_map/ppermute | solution.py:237
  108.4 3.1 %collective-permute-start.25 = (bf16[128,256]{1,0:T(8,128)(2,1)S(1)}, bf16[128,256]{1,0:T(8,128)(2,1)S(1)}, u32[]{:S(2)}, u32[]{:S(2)}) collective-permute-start(bf16[128,256]{1,0:T(8,128)(2,1)S(1)} %fusion.48), channel_id=1, source_target_pairs={{0,16},{2,18},{4,20},{6,22},{8,24},{10,26},{12,28},{14,30},{16,0},... | collective-permute-start | bytes 196616 | tf_op jit(solution)/shard_map/ppermute | solution.py:237
  111.6 3.6 %collective-permute-done.25 = bf16[128,256]{1,0:T(8,128)(2,1)S(1)} collective-permute-done((bf16[128,256]{1,0:T(8,128)(2,1)S(1)}, bf16[128,256]{1,0:T(8,128)(2,1)S(1)}, u32[]{:S(2)}, u32[]{:S(2)}) %collective-permute-start.25) | collective-permute-done | bytes 65568 | tf_op jit(solution)/shard_map/ppermute | solution.py:237
  115.8 1.4 collective-permute-done.24
  118.0 1.2 copy-done.4
  121.4 6.1 %collective-permute-done.29 = bf16[2,2,128,256]{3,2,1,0:T(8,128)(2,1)S(1)} collective-permute-done((bf16[2,2,128,256]{3,2,1,0:T(8,128)(2,1)S(1)}, bf16[2,2,128,256]{3,2,1,0:T(8,128)(2,1)S(1)}, u32[]{:S(2)}, u32[]{:S(2)}) %collective-permute-start.29) | collective-permute-done | bytes 262176 | tf_op jit(solution)/shard_map/ppermute | solution.py:237
  127.6 1.3 collective-permute-done.27
  129.8 1.0 fusion.21
  130.8 1.5 %collective-permute-start.30 = (bf16[2,136,256]{2,1,0:T(8,128)(2,1)S(1)}, bf16[2,136,256]{2,1,0:T(8,128)(2,1)S(1)}, u32[]{:S(2)}, u32[]{:S(2)}) collective-permute-start(bf16[2,136,256]{2,1,0:T(8,128)(2,1)S(1)} %fusion.40), channel_id=1, source_target_pairs={{0,8},{2,10},{4,12},{6,14},{8,0},{10,2},{12,4},{14,6},{16,24},{18,... | collective-permute-start | bytes 417800 | tf_op jit(solution)/shard_map/ppermute | solution.py:237
  132.3 1.7 %collective-permute-done.31 = bf16[2,128,256]{2,1,0:T(8,128)(2,1)S(1)} collective-permute-done((bf16[2,128,256]{2,1,0:T(8,128)(2,1)S(1)}, bf16[2,128,256]{2,1,0:T(8,128)(2,1)S(1)}, u32[]{:S(2)}, u32[]{:S(2)}) %collective-permute-start.31) | collective-permute-done | bytes 131104 | tf_op jit(solution)/shard_map/ppermute | solution.py:237
  134.0 1.9 %collective-permute-done.30 = bf16[2,136,256]{2,1,0:T(8,128)(2,1)S(1)} collective-permute-done((bf16[2,136,256]{2,1,0:T(8,128)(2,1)S(1)}, bf16[2,136,256]{2,1,0:T(8,128)(2,1)S(1)}, u32[]{:S(2)}, u32[]{:S(2)}) %collective-permute-start.30) | collective-permute-done | bytes 139296 | tf_op jit(solution)/shard_map/ppermute | solution.py:237
  136.0 1.4 collective-permute-start.33
  137.4 1.6 %collective-permute-start.32 = (bf16[136,256]{1,0:T(8,128)(2,1)S(1)}, bf16[136,256]{1,0:T(8,128)(2,1)S(1)}, u32[]{:S(2)}, u32[]{:S(2)}) collective-permute-start(bf16[136,256]{1,0:T(8,128)(2,1)S(1)} %fusion.46), channel_id=1, source_target_pairs={{0,16},{2,18},{4,20},{6,22},{8,24},{10,26},{12,28},{14,30},{16,0},... | collective-permute-start | bytes 208904 | tf_op jit(solution)/shard_map/ppermute | solution.py:237
  139.0 2.2 %collective-permute-done.33 = bf16[128,256]{1,0:T(8,128)(2,1)S(1)} collective-permute-done((bf16[128,256]{1,0:T(8,128)(2,1)S(1)}, bf16[128,256]{1,0:T(8,128)(2,1)S(1)}, u32[]{:S(2)}, u32[]{:S(2)}) %collective-permute-start.33) | collective-permute-done | bytes 65568 | tf_op jit(solution)/shard_map/ppermute | solution.py:237
  141.2 2.4 %collective-permute-done.32 = bf16[136,256]{1,0:T(8,128)(2,1)S(1)} collective-permute-done((bf16[136,256]{1,0:T(8,128)(2,1)S(1)}, bf16[136,256]{1,0:T(8,128)(2,1)S(1)}, u32[]{:S(2)}, u32[]{:S(2)}) %collective-permute-start.32) | collective-permute-done | bytes 69664 | tf_op jit(solution)/shard_map/ppermute | solution.py:237
  (122 shorter events, 18.6 us)
Async XLA Ops:
  4.3 14.1 %collective-permute-start = (bf16[128,256]{1,0:T(8,128)(2,1)}, bf16[128,256]{1,0:T(8,128)(2,1)S(1)}, u32[]{:S(2)}, u32[]{:S(2)}) collective-permute-start(bf16[128,256]{1,0:T(8,128)(2,1)} %get-tuple-element.32), channel_id=1, source_target_pairs={{0,8},{2,10},{4,12},{6,14},{8,0},{10,2},{12,4},{14,6},{16,24},{18,... | collective-permute-start | bytes 196616 | tf_op jit(solution)/shard_map/ppermute | solution.py:237
  7.3 11.0 %collective-permute-start.1 = (bf16[128,256]{1,0:T(8,128)(2,1)}, bf16[128,256]{1,0:T(8,128)(2,1)S(1)}, u32[]{:S(2)}, u32[]{:S(2)}) collective-permute-start(bf16[128,256]{1,0:T(8,128)(2,1)} %get-tuple-element.32), channel_id=1, source_target_pairs={{0,16},{2,18},{4,20},{6,22},{8,24},{10,26},{12,28},{14,30},{16,0},... | collective-permute-start | bytes 196616 | tf_op jit(solution)/shard_map/ppermute | solution.py:237
  9.9 8.4 %collective-permute-start.2 = (bf16[128,256]{1,0:T(8,128)(2,1)}, bf16[128,256]{1,0:T(8,128)(2,1)S(1)}, u32[]{:S(2)}, u32[]{:S(2)}) collective-permute-start(bf16[128,256]{1,0:T(8,128)(2,1)} %get-tuple-element.32), channel_id=1, source_target_pairs={{0,24},{2,26},{4,28},{6,30},{8,16},{10,18},{12,20},{14,22},{16,8},... | collective-permute-start | bytes 196616 | tf_op jit(solution)/shard_map/ppermute | solution.py:237
  9.9 10.3 %collective-permute-start.6 = (bf16[128,256]{1,0:T(8,128)(2,1)}, bf16[128,256]{1,0:T(8,128)(2,1)S(1)}, u32[]{:S(2)}, u32[]{:S(2)}) collective-permute-start(bf16[128,256]{1,0:T(8,128)(2,1)} %get-tuple-element.34), channel_id=1, source_target_pairs={{0,8},{2,10},{4,12},{6,14},{8,0},{10,2},{12,4},{14,6},{16,24},{18,... | collective-permute-start | bytes 196616 | tf_op jit(solution)/shard_map/ppermute | solution.py:237
  10.8 9.4 %collective-permute-start.7 = (bf16[128,256]{1,0:T(8,128)(2,1)}, bf16[128,256]{1,0:T(8,128)(2,1)}, u32[]{:S(2)}, u32[]{:S(2)}) collective-permute-start(bf16[128,256]{1,0:T(8,128)(2,1)} %get-tuple-element.34), channel_id=1, source_target_pairs={{0,16},{2,18},{4,20},{6,22},{8,24},{10,26},{12,28},{14,30},{16,0},... | collective-permute-start | bytes 196616 | tf_op jit(solution)/shard_map/ppermute | solution.py:237
  14.3 3.3 %copy-start.8 = (s32[1,128]{1,0:T(1,128)S(1)}, s32[1,128]{1,0:T(1,128)}, u32[]{:S(2)}) copy-start(s32[1,128]{1,0:T(1,128)} %cats_ref.1) | copy-start | bytes 1540
  14.3 3.4 %copy-start.6 = (bf16[128,256]{1,0:T(8,128)(2,1)S(1)}, bf16[128,256]{1,0:T(8,128)(2,1)}, u32[]{:S(2)}) copy-start(bf16[128,256]{1,0:T(8,128)(2,1)} %get-tuple-element.34) | copy-start | bytes 196612
  14.3 3.4 %copy-start.7 = (bf16[128,256]{1,0:T(8,128)(2,1)S(1)}, bf16[128,256]{1,0:T(8,128)(2,1)}, u32[]{:S(2)}) copy-start(bf16[128,256]{1,0:T(8,128)(2,1)} %get-tuple-element.32) | copy-start | bytes 196612
  17.6 14.3 %copy-start.5 = (bf16[1,128,512]{2,1,0:T(8,128)(2,1)S(1)}, bf16[1,128,512]{2,1,0:T(8,128)(2,1)}, u32[]{:S(2)}) copy-start(bf16[1,128,512]{2,1,0:T(8,128)(2,1)} %param.12) | copy-start | bytes 393220
  17.6 15.0 %copy-start.3 = (s32[1,1,80]{2,1,0:T(1,128)S(1)}, s32[1,1,80]{2,1,0:T(1,128)}, u32[]{:S(2)}) copy-start(s32[1,1,80]{2,1,0:T(1,128)} %param.15) | copy-start | bytes 964
  18.3 6.1 %collective-permute-start.8 = (bf16[128,256]{1,0:T(8,128)(2,1)S(1)}, bf16[128,256]{1,0:T(8,128)(2,1)S(1)}, u32[]{:S(2)}, u32[]{:S(2)}) collective-permute-start(bf16[128,256]{1,0:T(8,128)(2,1)S(1)} %copy-done.6), channel_id=1, source_target_pairs={{0,24},{2,26},{4,28},{6,30},{8,16},{10,18},{12,20},{14,22},{16,8},... | collective-permute-start | bytes 196616 | tf_op jit(solution)/shard_map/ppermute | solution.py:237
  18.4 11.2 %collective-permute-start.3 = (bf16[512,256]{1,0:T(8,128)(2,1)S(1)}, bf16[512,256]{1,0:T(8,128)(2,1)S(1)}, u32[]{:S(2)}, u32[]{:S(2)}) collective-permute-start(bf16[512,256]{1,0:T(8,128)(2,1)S(1)} %pad_maximum_fusion.2), channel_id=1, source_target_pairs={{0,4},{2,6},{4,0},{6,2},{8,12},{10,14},{12,8},{14,10},{16,20},{18,... | collective-permute-start | bytes 786440 | tf_op jit(solution)/shard_map/ppermute | solution.py:237
  25.3 6.4 %collective-permute-start.9 = (bf16[512,256]{1,0:T(8,128)(2,1)S(1)}, bf16[512,256]{1,0:T(8,128)(2,1)S(1)}, u32[]{:S(2)}, u32[]{:S(2)}) collective-permute-start(bf16[512,256]{1,0:T(8,128)(2,1)S(1)} %pad_maximum_fusion.3), channel_id=1, source_target_pairs={{0,4},{2,6},{4,0},{6,2},{8,12},{10,14},{12,8},{14,10},{16,20},{18,... | collective-permute-start | bytes 786440 | tf_op jit(solution)/shard_map/ppermute | solution.py:237
  30.3 4.5 %collective-permute-start.4 = (bf16[1024,256]{1,0:T(8,128)(2,1)}, bf16[1024,256]{1,0:T(8,128)(2,1)}, u32[]{:S(2)}, u32[]{:S(2)}) collective-permute-start(bf16[1024,256]{1,0:T(8,128)(2,1)} %constant_dynamic-update-slice_fusion.same_ref), channel_id=1, source_target_pairs={{0,2},{2,0},{4,6},{6,4},{8,10},{10,8},{12,14},{14,12},{16,18},{18,... | collective-permute-start | bytes 1572872 | tf_op jit(solution)/shard_map/ppermute | solution.py:237
  31.7 7.9 %collective-permute-start.10 = (bf16[1024,256]{1,0:T(8,128)(2,1)S(1)}, bf16[1024,256]{1,0:T(8,128)(2,1)}, u32[]{:S(2)}, u32[]{:S(2)}) collective-permute-start(bf16[1024,256]{1,0:T(8,128)(2,1)S(1)} %constant_dynamic-update-slice_fusion.5.same_ref), channel_id=1, source_target_pairs={{0,2},{2,0},{4,6},{6,4},{8,10},{10,8},{12,14},{14,12},{16,18},{18,... | collective-permute-start | bytes 1572872 | tf_op jit(solution)/shard_map/ppermute | solution.py:237
  37.9 18.3 %collective-permute-start.5 = (bf16[512,256]{1,0:T(8,128)(2,1)S(1)}, bf16[512,256]{1,0:T(8,128)(2,1)S(1)}, u32[]{:S(2)}, u32[]{:S(2)}) collective-permute-start(bf16[512,256]{1,0:T(8,128)(2,1)S(1)} %get-tuple-element.33.rest_0_), channel_id=1, source_target_pairs={{0,1},{1,0},{2,3},{3,2},{4,5},{5,4},{6,7},{7,6},{8,9},{9,8},{10,11... | collective-permute-start | bytes 786440 | tf_op jit(solution)/shard_map/ppermute | solution.py:308
  42.4 14.0 %collective-permute-start.11 = (bf16[512,256]{1,0:T(8,128)(2,1)S(1)}, bf16[512,256]{1,0:T(8,128)(2,1)S(1)}, u32[]{:S(2)}, u32[]{:S(2)}) collective-permute-start(bf16[512,256]{1,0:T(8,128)(2,1)S(1)} %get-tuple-element.35.rest_2_), channel_id=1, source_target_pairs={{0,1},{1,0},{2,3},{3,2},{4,5},{5,4},{6,7},{7,6},{8,9},{9,8},{10,11... | collective-permute-start | bytes 786440 | tf_op jit(solution)/shard_map/ppermute | solution.py:308
  47.5 40.4 %collective-permute-start.16 = (bf16[512,256]{1,0:T(8,128)(2,1)S(1)}, bf16[512,256]{1,0:T(8,128)(2,1)S(1)}, u32[]{:S(2)}, u32[]{:S(2)}) collective-permute-start(bf16[512,256]{1,0:T(8,128)(2,1)S(1)} %get-tuple-element.45.rest_0_), channel_id=1, source_target_pairs={{0,1},{1,0},{2,3},{3,2},{4,5},{5,4},{6,7},{7,6},{8,9},{9,8},{10,11... | collective-permute-start | bytes 786440 | tf_op jit(solution)/shard_map/ppermute | solution.py:308
  49.3 8.9 %copy-start = (bf16[2048,512]{1,0:T(8,128)(2,1)S(1)}, bf16[2048,512]{1,0:T(8,128)(2,1)}, u32[]{:S(2)}) copy-start(bf16[2048,512]{1,0:T(8,128)(2,1)} %user_ref.7) | copy-start | bytes 6291460
  49.3 8.9 %copy-start.1 = (bf16[2048,512]{1,0:T(8,128)(2,1)S(1)}, bf16[2048,512]{1,0:T(8,128)(2,1)}, u32[]{:S(2)}) copy-start(bf16[2048,512]{1,0:T(8,128)(2,1)} %grad_ref.7) | copy-start | bytes 6291460
  49.3 8.9 %copy-start.2 = (f32[512]{0:T(512)S(1)}, f32[512]{0:T(512)}, u32[]{:S(2)}) copy-start(f32[512]{0:T(512)} %param.11) | copy-start | bytes 6148
  54.0 33.9 %collective-permute-start.17 = (bf16[512,256]{1,0:T(8,128)(2,1)S(1)}, bf16[512,256]{1,0:T(8,128)(2,1)S(1)}, u32[]{:S(2)}, u32[]{:S(2)}) collective-permute-start(bf16[512,256]{1,0:T(8,128)(2,1)S(1)} %get-tuple-element.46.rest_2_), channel_id=1, source_target_pairs={{0,1},{1,0},{2,3},{3,2},{4,5},{5,4},{6,7},{7,6},{8,9},{9,8},{10,11... | collective-permute-start | bytes 786440 | tf_op jit(solution)/shard_map/ppermute | solution.py:308
  54.4 28.3 %collective-permute-start.14 = (bf16[512,256]{1,0:T(8,128)(2,1)S(1)}, bf16[512,256]{1,0:T(8,128)(2,1)S(1)}, u32[]{:S(2)}, u32[]{:S(2)}) collective-permute-start(bf16[512,256]{1,0:T(8,128)(2,1)S(1)} %get-tuple-element.42.rest_0_), channel_id=1, source_target_pairs={{0,1},{1,0},{2,3},{3,2},{4,5},{5,4},{6,7},{7,6},{8,9},{9,8},{10,11... | collective-permute-start | bytes 786440 | tf_op jit(solution)/shard_map/ppermute | solution.py:308
  56.1 19.0 %collective-permute-start.12 = (bf16[512,256]{1,0:T(8,128)(2,1)S(1)}, bf16[512,256]{1,0:T(8,128)(2,1)S(1)}, u32[]{:S(2)}, u32[]{:S(2)}) collective-permute-start(bf16[512,256]{1,0:T(8,128)(2,1)S(1)} %get-tuple-element.38.rest_0_), channel_id=1, source_target_pairs={{0,1},{1,0},{2,3},{3,2},{4,5},{5,4},{6,7},{7,6},{8,9},{9,8},{10,11... | collective-permute-start | bytes 786440 | tf_op jit(solution)/shard_map/ppermute | solution.py:308
  56.5 24.3 %collective-permute-start.13 = (bf16[512,256]{1,0:T(8,128)(2,1)S(1)}, bf16[512,256]{1,0:T(8,128)(2,1)S(1)}, u32[]{:S(2)}, u32[]{:S(2)}) collective-permute-start(bf16[512,256]{1,0:T(8,128)(2,1)S(1)} %get-tuple-element.40.rest_2_), channel_id=1, source_target_pairs={{0,1},{1,0},{2,3},{3,2},{4,5},{5,4},{6,7},{7,6},{8,9},{9,8},{10,11... | collective-permute-start | bytes 786440 | tf_op jit(solution)/shard_map/ppermute | solution.py:308
  75.1 10.7 %collective-permute-start.15 = (bf16[512,256]{1,0:T(8,128)(2,1)S(1)}, bf16[512,256]{1,0:T(8,128)(2,1)S(1)}, u32[]{:S(2)}, u32[]{:S(2)}) collective-permute-start(bf16[512,256]{1,0:T(8,128)(2,1)S(1)} %get-tuple-element.43.rest_2_), channel_id=1, source_target_pairs={{0,1},{1,0},{2,3},{3,2},{4,5},{5,4},{6,7},{7,6},{8,9},{9,8},{10,11... | collective-permute-start | bytes 786440 | tf_op jit(solution)/shard_map/ppermute | solution.py:308
  90.6 2.0 %collective-permute-start.18 = (bf16[2,2,2,128,256]{4,3,0,1,2:T(8,128)(2,1)S(1)}, bf16[2,2,2,128,256]{4,3,0,1,2:T(8,128)(2,1)S(1)}, u32[]{:S(2)}, u32[]{:S(2)}) collective-permute-start(bf16[2,2,2,128,256]{4,3,0,1,2:T(8,128)(2,1)S(1)} %fusion.24), channel_id=1, source_target_pairs={{0,2},{2,0},{4,6},{6,4},{8,10},{10,8},{12,14},{14,12},{16,18},{18,... | collective-permute-start | bytes 1572872 | tf_op jit(solution)/shard_map/ppermute | solution.py:237
  90.7 3.8 %collective-permute-start.20 = (bf16[2,2,2,128,256]{4,3,0,2,1:T(8,128)(2,1)S(1)}, bf16[2,2,2,128,256]{4,3,0,2,1:T(8,128)(2,1)S(1)}, u32[]{:S(2)}, u32[]{:S(2)}) collective-permute-start(bf16[2,2,2,128,256]{4,3,0,2,1:T(8,128)(2,1)S(1)} %fusion.25), channel_id=1, source_target_pairs={{0,2},{2,0},{4,6},{6,4},{8,10},{10,8},{12,14},{14,12},{16,18},{18,... | collective-permute-start | bytes 1572872 | tf_op jit(solution)/shard_map/ppermute | solution.py:237
  92.7 8.4 %collective-permute-start.19 = (bf16[2,2,128,256]{3,2,0,1:T(8,128)(2,1)S(1)}, bf16[2,2,128,256]{3,2,0,1:T(8,128)(2,1)S(1)}, u32[]{:S(2)}, u32[]{:S(2)}) collective-permute-start(bf16[2,2,128,256]{3,2,0,1:T(8,128)(2,1)S(1)} %fusion.35), channel_id=1, source_target_pairs={{0,4},{2,6},{4,0},{6,2},{8,12},{10,14},{12,8},{14,10},{16,20},{18,... | collective-permute-start | bytes 786440 | tf_op jit(solution)/shard_map/ppermute | solution.py:237
  94.7 8.1 %collective-permute-start.21 = (bf16[2,2,128,256]{3,2,0,1:T(8,128)(2,1)S(1)}, bf16[2,2,128,256]{3,2,0,1:T(8,128)(2,1)S(1)}, u32[]{:S(2)}, u32[]{:S(2)}) collective-permute-start(bf16[2,2,128,256]{3,2,0,1:T(8,128)(2,1)S(1)} %fusion.36), channel_id=1, source_target_pairs={{0,8},{2,10},{4,12},{6,14},{8,0},{10,2},{12,4},{14,6},{16,24},{18,... | collective-permute-start | bytes 786440 | tf_op jit(solution)/shard_map/ppermute | solution.py:237
  102.9 5.0 %collective-permute-start.22 = (bf16[2,128,256]{2,1,0:T(8,128)(2,1)S(1)}, bf16[2,128,256]{2,1,0:T(8,128)(2,1)S(1)}, u32[]{:S(2)}, u32[]{:S(2)}) collective-permute-start(bf16[2,128,256]{2,1,0:T(8,128)(2,1)S(1)} %fusion.41), channel_id=1, source_target_pairs={{0,8},{2,10},{4,12},{6,14},{8,0},{10,2},{12,4},{14,6},{16,24},{18,... | collective-permute-start | bytes 393224 | tf_op jit(solution)/shard_map/ppermute | solution.py:237
  103.3 5.0 %collective-permute-start.23 = (bf16[2,128,256]{2,1,0:T(8,128)(2,1)S(1)}, bf16[2,128,256]{2,1,0:T(8,128)(2,1)S(1)}, u32[]{:S(2)}, u32[]{:S(2)}) collective-permute-start(bf16[2,128,256]{2,1,0:T(8,128)(2,1)S(1)} %fusion.42), channel_id=1, source_target_pairs={{0,4},{2,6},{4,0},{6,2},{8,12},{10,14},{12,8},{14,10},{16,20},{18,... | collective-permute-start | bytes 393224 | tf_op jit(solution)/shard_map/ppermute | solution.py:237
  108.4 6.8 %collective-permute-start.25 = (bf16[128,256]{1,0:T(8,128)(2,1)S(1)}, bf16[128,256]{1,0:T(8,128)(2,1)S(1)}, u32[]{:S(2)}, u32[]{:S(2)}) collective-permute-start(bf16[128,256]{1,0:T(8,128)(2,1)S(1)} %fusion.48), channel_id=1, source_target_pairs={{0,16},{2,18},{4,20},{6,22},{8,24},{10,26},{12,28},{14,30},{16,0},... | collective-permute-start | bytes 196616 | tf_op jit(solution)/shard_map/ppermute | solution.py:237
  111.5 5.7 %collective-permute-start.24 = (bf16[128,256]{1,0:T(8,128)(2,1)S(1)}, bf16[128,256]{1,0:T(8,128)(2,1)S(1)}, u32[]{:S(2)}, u32[]{:S(2)}) collective-permute-start(bf16[128,256]{1,0:T(8,128)(2,1)S(1)} %fusion.47), channel_id=1, source_target_pairs={{0,16},{2,18},{4,20},{6,22},{8,24},{10,26},{12,28},{14,30},{16,0},... | collective-permute-start | bytes 196616 | tf_op jit(solution)/shard_map/ppermute | solution.py:237
  115.7 4.1 %collective-permute-start.28 = (bf16[2,2,2,128,256]{4,3,2,1,0:T(8,128)(2,1)S(1)}, bf16[2,2,2,128,256]{4,3,2,1,0:T(8,128)(2,1)S(1)}, u32[]{:S(2)}, u32[]{:S(2)}) collective-permute-start(bf16[2,2,2,128,256]{4,3,2,1,0:T(8,128)(2,1)S(1)} %fusion.23), channel_id=1, source_target_pairs={{0,2},{2,0},{4,6},{6,4},{8,10},{10,8},{12,14},{14,12},{16,18},{18,... | collective-permute-start | bytes 1572872 | tf_op jit(solution)/shard_map/ppermute | solution.py:237
  117.6 1.6 %copy-start.4 = (bf16[4,512,512]{2,1,0:T(8,128)(2,1)S(1)}, bf16[4,512,512]{2,1,0:T(8,128)(2,1)}, u32[]{:S(2)}) copy-start(bf16[4,512,512]{2,1,0:T(8,128)(2,1)} %weight_ref.1) | copy-start | bytes 6291460
  117.9 2.2 %collective-permute-start.26 = (bf16[2,2,2,136,256]{4,3,0,1,2:T(8,128)(2,1)S(1)}, bf16[2,2,2,136,256]{4,3,0,1,2:T(8,128)(2,1)S(1)}, u32[]{:S(2)}, u32[]{:S(2)}) collective-permute-start(bf16[2,2,2,136,256]{4,3,0,1,2:T(8,128)(2,1)S(1)} %fusion.22), channel_id=1, source_target_pairs={{0,2},{2,0},{4,6},{6,4},{8,10},{10,8},{12,14},{14,12},{16,18},{18,... | collective-permute-start | bytes 1671176 | tf_op jit(solution)/shard_map/ppermute | solution.py:237
  120.0 7.6 %collective-permute-start.29 = (bf16[2,2,128,256]{3,2,1,0:T(8,128)(2,1)S(1)}, bf16[2,2,128,256]{3,2,1,0:T(8,128)(2,1)S(1)}, u32[]{:S(2)}, u32[]{:S(2)}) collective-permute-start(bf16[2,2,128,256]{3,2,1,0:T(8,128)(2,1)S(1)} %fusion.37), channel_id=1, source_target_pairs={{0,8},{2,10},{4,12},{6,14},{8,0},{10,2},{12,4},{14,6},{16,24},{18,... | collective-permute-start | bytes 786440 | tf_op jit(solution)/shard_map/ppermute | solution.py:237
  120.2 8.6 %collective-permute-start.27 = (bf16[2,2,136,256]{3,2,0,1:T(8,128)(2,1)S(1)}, bf16[2,2,136,256]{3,2,0,1:T(8,128)(2,1)S(1)}, u32[]{:S(2)}, u32[]{:S(2)}) collective-permute-start(bf16[2,2,136,256]{3,2,0,1:T(8,128)(2,1)S(1)} %fusion.34), channel_id=1, source_target_pairs={{0,4},{2,6},{4,0},{6,2},{8,12},{10,14},{12,8},{14,10},{16,20},{18,... | collective-permute-start | bytes 835592 | tf_op jit(solution)/shard_map/ppermute | solution.py:237
  129.0 5.0 %collective-permute-start.31 = (bf16[2,128,256]{2,1,0:T(8,128)(2,1)S(1)}, bf16[2,128,256]{2,1,0:T(8,128)(2,1)S(1)}, u32[]{:S(2)}, u32[]{:S(2)}) collective-permute-start(bf16[2,128,256]{2,1,0:T(8,128)(2,1)S(1)} %fusion.43), channel_id=1, source_target_pairs={{0,4},{2,6},{4,0},{6,2},{8,12},{10,14},{12,8},{14,10},{16,20},{18,... | collective-permute-start | bytes 393224 | tf_op jit(solution)/shard_map/ppermute | solution.py:237
  130.8 5.1 %collective-permute-start.30 = (bf16[2,136,256]{2,1,0:T(8,128)(2,1)S(1)}, bf16[2,136,256]{2,1,0:T(8,128)(2,1)S(1)}, u32[]{:S(2)}, u32[]{:S(2)}) collective-permute-start(bf16[2,136,256]{2,1,0:T(8,128)(2,1)S(1)} %fusion.40), channel_id=1, source_target_pairs={{0,8},{2,10},{4,12},{6,14},{8,0},{10,2},{12,4},{14,6},{16,24},{18,... | collective-permute-start | bytes 417800 | tf_op jit(solution)/shard_map/ppermute | solution.py:237
  136.0 5.2 %collective-permute-start.33 = (bf16[128,256]{1,0:T(8,128)(2,1)S(1)}, bf16[128,256]{1,0:T(8,128)(2,1)S(1)}, u32[]{:S(2)}, u32[]{:S(2)}) collective-permute-start(bf16[128,256]{1,0:T(8,128)(2,1)S(1)} %fusion.49), channel_id=1, source_target_pairs={{0,16},{2,18},{4,20},{6,22},{8,24},{10,26},{12,28},{14,30},{16,0},... | collective-permute-start | bytes 196616 | tf_op jit(solution)/shard_map/ppermute | solution.py:237
  137.4 6.2 %collective-permute-start.32 = (bf16[136,256]{1,0:T(8,128)(2,1)S(1)}, bf16[136,256]{1,0:T(8,128)(2,1)S(1)}, u32[]{:S(2)}, u32[]{:S(2)}) collective-permute-start(bf16[136,256]{1,0:T(8,128)(2,1)S(1)} %fusion.46), channel_id=1, source_target_pairs={{0,16},{2,18},{4,20},{6,22},{8,24},{10,26},{12,28},{14,30},{16,0},... | collective-permute-start | bytes 208904 | tf_op jit(solution)/shard_map/ppermute | solution.py:237

commit v9 on v7

--- a/solution.py
+++ b/solution.py
@@ -118,8 +118,8 @@
     )(first_expert.reshape(1), cats.reshape(1, own), feat, weights)
 
 
-def spread(blocks, order_ref, same_ref, other_ref, dense_ref, *rest):
-    out_refs, next_ref, all_ref = rest[:-2], rest[-2], rest[-1]
+def spread(blocks, order_ref, *rest):
+    source_refs, dense_ref, out_refs, next_ref, all_ref = rest[:4], rest[4], rest[5:-2], *rest[-2:]
     step = pl.program_id(0)
 
     @pl.when(step == 0)
@@ -128,9 +128,9 @@
             next_ref[place] = order_ref[place]
         own = all_ref.shape[0] // blocks
         for place in range(blocks):
-            source = (same_ref, other_ref)[2 * place // blocks]
+            source = source_refs[4 * place // blocks]
             start = pl.multiple_of(order_ref[place] * own, own)
-            all_ref[pl.ds(start, own)] = source[pl.ds((place % (blocks // 2)) * own, own)]
+            all_ref[pl.ds(start, own)] = source[pl.ds((place % (blocks // 4)) * own, own)]
 
     product = jnp.dot(dense_ref[...], all_ref[...], preferred_element_type=jnp.float32)
     rows, first = product.shape[0], 0
@@ -157,7 +157,7 @@
         grid_spec=pltpu.PrefetchScalarGridSpec(
             num_scalar_prefetch=1,
             grid=(chunks,),
-            in_specs=[pl.BlockSpec(queries[0].shape, whole)] * 2
+            in_specs=[pl.BlockSpec(queries[0].shape, whole)] * 4
             + [pl.BlockSpec((rows, items), lambda step, order_ref: (first + step, 0))],
             out_specs=[pl.BlockSpec((count * rows, cols), whole) for count in counts]
             + [pl.BlockSpec(memory_space=pltpu.SMEM)],
@@ -245,8 +245,8 @@
 
 
 def gather_sides(own, size):
-    own = jnp.concatenate([own, flip(own, size, 2)], axis=0)
-    return own, flip(own, size, 1)
+    other = flip(own, size, 2)
+    return own, other, flip(own, size, 1), flip(other, size, 1)
 
 
 def gather_order(size):
@@ -299,15 +299,16 @@
     partials = [[] for _ in range(HALVES)]
     for half in range(HALVES):
         for first, count in ((0, 1), (1, ROW_CHUNKS - 1)):
-            *products, last = spread_items(order, queries[half], dense, first, (1,) * count, rows)
+            *products, _ = spread_items(order, queries[half], dense, first, (1,) * count, rows)
             for product in products:
                 pieces = [product]
                 for shift in range(1, item_size):
                     pairs = [(source, (source + shift) % item_size) for source in range(item_size)]
                     pieces.append(lax.ppermute(product, "item", pairs))
                 partials[half].append(pieces)
-    grads, gain_term, item_terms = [], 0.0, 0.0
-    for chunk in range(ROW_CHUNKS):
+    grads, gain_term, item_terms = [None] * ROW_CHUNKS, 0.0, 0.0
+    chunk_order = [0] + list(range(ROW_CHUNKS - 1, 0, -1))
+    for chunk in chunk_order:
         grad, term = user_gradient(
             user_feat,
             cotangent,
@@ -316,9 +317,9 @@
             chunk * rows,
             rows,
         )
-        grads.append(grad)
+        grads[chunk] = grad
         gain_term = gain_term + term[0]
-        if chunk < ROW_CHUNKS - 1:
+        if chunk != chunk_order[-1]:
             item_terms = item_terms + lax.dot_general(
                 dense[chunk * rows : (chunk + 1) * rows],
                 grad,
@@ -330,16 +331,14 @@
         [lax.dynamic_slice_in_dim(grad, item_index * col_width, col_width, 1) for grad in grads],
         axis=0,
     )
-    gain_grad = lax.dynamic_slice_in_dim(gain_term, item_index * col_width, col_width, 0)
-    for bit in range(user_size.bit_length() - 1):
-        gain_grad = gain_grad + flip(gain_grad, user_size, 1 << bit)
+    gain_own = lax.dynamic_slice_in_dim(gain_term, item_index * col_width, col_width, 0)
 
     halves = []
     for half in range(HALVES):
         part = slice(half * half_width, (half + 1) * half_width)
         terms = item_terms[:, part] + lax.dot_general(
-            dense[users - rows :],
-            grads[-1][:, part],
+            dense[chunk_order[-1] * rows : (chunk_order[-1] + 1) * rows],
+            grads[chunk_order[-1]][:, part],
             (((0,), (0,)), ((), ())),
             preferred_element_type=jnp.float32,
         )
@@ -359,7 +358,12 @@
         ).reshape(user_size, experts_here * own_width, half_width)
         for half in sums
     ]
-    expert_grad = jnp.concatenate(scatter_sums(halves, user_size), axis=1)
+    gain_rows = jnp.pad(gain_own, (0, 8 * half_width - col_width)).reshape(1, 8, half_width)
+    gain_rows = jnp.broadcast_to(gain_rows, (user_size, 8, half_width))
+    halves[0] = jnp.concatenate([halves[0], gain_rows], axis=1)
+    halves = scatter_sums(halves, user_size)
+    gain_grad = halves[0][-8:].reshape(-1)[:col_width]
+    expert_grad = jnp.concatenate([halves[0][:-8], halves[1]], axis=1)
     own_sums = jnp.concatenate(sums, axis=1)
     item_total = jnp.zeros((own_items, width), jnp.float32)
     for expert in range(experts_here):

time: 150 us -> 142 us (0.947)
  waiting for transfers between devices: 64.8 us -> 57.1 us
  local copies, waits for them, and re-layouts: 4.19 us -> 6.57 us
  other arithmetic: 5.05 us -> 3.01 us
    ppermute x30 -> x28, waiting for transfers between devices: 38.8 us -> 33 us  [flip(): lax.ppermute(value, 'user', [(source, source ^ bits) for source in range(...]
    ppermute x8, waiting for transfers between devices: 26 us -> 24.1 us  [on_device(): pieces.append(lax.ppermute(product, 'item', pairs))]
    unnamed x24 -> x23, local copies, waits for them, and re-layouts: 3.56 us -> 5.34 us
    ppermute x30 -> x28, starting transfers between devices: 36.3 us -> 36.2 us  [flip(): lax.ppermute(value, 'user', [(source, source ^ bits) for source in range(...]
  transfers between devices with their start and end apart: 38 -> 36, of which waited for: 26 -> 23; matrix products, arithmetic and copies ran while one was open for 8% -> 8% of each run, Pallas kernels for 10% -> 10%
where the time goes in v9:
time: 142 us; the launch traced here: 141 us
  waiting for transfers between devices  57.1 us (40%)
  starting transfers between devices  45.1 us (32%)
  Pallas kernels  19.3 us (14%)
  matrix products  8.16 us (6%)
  local copies, waits for them, and re-layouts  6.57 us (5%)
  other arithmetic  3.01 us (2%)
  between operations  1.88 us (1%)
    ppermute x28, starting transfers between devices, flip(): lax.ppermute(value, 'user', [(source, source ^ bits) for source in range(...  36.2 us
    ppermute x28, waiting for transfers between devices, flip(): lax.ppermute(value, 'user', [(source, source ^ bits) for source in range(...  33 us
    ppermute x8, waiting for transfers between devices, on_device(): pieces.append(lax.ppermute(product, 'item', pairs))  24.1 us
    pallas_call x4, Pallas kernels, spread_items(): pl.pallas_call(functools.partial(spread, blocks), out_shape=[jax.ShapeDty...  10.3 us
    ppermute x8, starting transfers between devices, on_device(): pieces.append(lax.ppermute(product, 'item', pairs))  8.91 us
    unnamed x23, local copies, waits for them, and re-layouts  5.34 us
    dot_general x3, matrix products, on_device(): lax.dot_general(dense[chunk * rows:(chunk + 1) * rows], grad, (((0,), (0,...  3.91 us
    pallas_call x1, Pallas kernels, own_queries(): pl.pallas_call(project_own, out_shape=[half] * HALVES, grid_spec=pltpu.Pr...  3.67 us
  transfers between devices with their start and end apart: 36, of which 23 were waited for; matrix products, arithmetic and copies ran while one was open for 8% of the time, Pallas kernels for 10%

profile of v9, /device:TPU:0, one launch (start us, length us, event | category | flops | bytes accessed | tf_op | source)
XLA Modules:
  0.0 141.1 jit_solution(6014103997879129692)
XLA Ops:
  0.7 3.7 %own_queries.1 = (bf16[128,256]{1,0:T(8,128)(2,1)}, bf16[128,256]{1,0:T(8,128)(2,1)}) custom-call(s32[1]{0:T(128)} %bitcast.1.first_ref, s32[1,128]{1,0:T(1,128)} %cats_ref.1, bf16[128,512]{1,0:T(8,128)(2,1)} %bitcast.139, bf16[4,512,512]{2,1,0:T(8,128)(2,1)} %weight_ref.1), custom_call_target="tpu_custom_call" | custom-call | flops 268435456 | bytes 2359296 | tf_op jit(solution)/shard_map/own_queries/pallas_call | solution.py:97
  4.3 3.0 %collective-permute-start = (bf16[128,256]{1,0:T(8,128)(2,1)}, bf16[128,256]{1,0:T(8,128)(2,1)S(1)}, u32[]{:S(2)}, u32[]{:S(2)}) collective-permute-start(bf16[128,256]{1,0:T(8,128)(2,1)} %get-tuple-element.30), channel_id=1, source_target_pairs={{0,8},{2,10},{4,12},{6,14},{8,0},{10,2},{12,4},{14,6},{16,24},{18,... | collective-permute-start | bytes 196616 | tf_op jit(solution)/shard_map/ppermute | solution.py:238
  7.4 2.6 %collective-permute-start.1 = (bf16[128,256]{1,0:T(8,128)(2,1)}, bf16[128,256]{1,0:T(8,128)(2,1)S(1)}, u32[]{:S(2)}, u32[]{:S(2)}) collective-permute-start(bf16[128,256]{1,0:T(8,128)(2,1)} %get-tuple-element.30), channel_id=1, source_target_pairs={{0,16},{2,18},{4,20},{6,22},{8,24},{10,26},{12,28},{14,30},{16,0},... | collective-permute-start | bytes 196616 | tf_op jit(solution)/shard_map/ppermute | solution.py:238
  10.8 3.5 %collective-permute-start.8 = (bf16[128,256]{1,0:T(8,128)(2,1)}, bf16[128,256]{1,0:T(8,128)(2,1)S(1)}, u32[]{:S(2)}, u32[]{:S(2)}) collective-permute-start(bf16[128,256]{1,0:T(8,128)(2,1)} %get-tuple-element.32), channel_id=1, source_target_pairs={{0,16},{2,18},{4,20},{6,22},{8,24},{10,26},{12,28},{14,30},{16,0},... | collective-permute-start | bytes 196616 | tf_op jit(solution)/shard_map/ppermute | solution.py:238
  16.7 1.5 %collective-permute-start.3 = (bf16[512,256]{1,0:T(8,128)(2,1)S(1)}, bf16[512,256]{1,0:T(8,128)(2,1)S(1)}, u32[]{:S(2)}, u32[]{:S(2)}) collective-permute-start(bf16[512,256]{1,0:T(8,128)(2,1)S(1)} %constant_dynamic-update-slice_fusion.rest_0_), channel_id=1, source_target_pairs={{0,4},{2,6},{4,0},{6,2},{8,12},{10,14},{12,8},{14,10},{16,20},{18,... | collective-permute-start | bytes 786440 | tf_op jit(solution)/shard_map/ppermute | solution.py:238
  18.3 2.2 %collective-permute-done.8 = bf16[128,256]{1,0:T(8,128)(2,1)S(1)} collective-permute-done((bf16[128,256]{1,0:T(8,128)(2,1)}, bf16[128,256]{1,0:T(8,128)(2,1)S(1)}, u32[]{:S(2)}, u32[]{:S(2)}) %collective-permute-start.8) | collective-permute-done | bytes 65568 | tf_op jit(solution)/shard_map/ppermute | solution.py:238
  20.5 2.1 %collective-permute-done.9 = bf16[128,256]{1,0:T(8,128)(2,1)S(1)} collective-permute-done((bf16[128,256]{1,0:T(8,128)(2,1)}, bf16[128,256]{1,0:T(8,128)(2,1)S(1)}, u32[]{:S(2)}, u32[]{:S(2)}) %collective-permute-start.9) | collective-permute-done | bytes 65568 | tf_op jit(solution)/shard_map/ppermute | solution.py:238
  22.5 1.5 %collective-permute-start.10 = (bf16[512,256]{1,0:T(8,128)(2,1)S(1)}, bf16[512,256]{1,0:T(8,128)(2,1)S(1)}, u32[]{:S(2)}, u32[]{:S(2)}) collective-permute-start(bf16[512,256]{1,0:T(8,128)(2,1)S(1)} %constant_dynamic-update-slice_fusion.4.rest_0_), channel_id=1, source_target_pairs={{0,4},{2,6},{4,0},{6,2},{8,12},{10,14},{12,8},{14,10},{16,20},{18,... | collective-permute-start | bytes 786440 | tf_op jit(solution)/shard_map/ppermute | solution.py:238
  25.4 2.5 %copy-done.2 = s32[1,1,80,128,128]{4,3,2,1,0:T(8,128)S(1)} copy-done((s32[1,1,80,128,128]{4,3,2,1,0:T(8,128)S(1)}, s32[1,1,80,128,128]{4,3,2,1,0:T(8,128)}, u32[]{:S(2)}) %copy-start.2) | copy-done | bytes 5242904
  27.8 2.4 %place_tiles.1.rest_4_ = bf16[2048,2048]{1,0:T(8,128)(2,1)S(1)} custom-call(s32[80]{0:T(128)S(1)} %bitcast.130, s32[1]{0:T(128)} %bitcast.124.count_ref, s32[80,128,128]{2,1,0:T(8,128)S(1)} %bitcast.125), custom_call_target="tpu_custom_call" | custom-call | flops 1310720 | bytes 13631488 | tf_op jit(solution)/shard_map/place_tiles/pallas_call | solution.py:40
  30.8 1.7 %spread_items.4 = (bf16[512,256]{1,0:T(8,128)(2,1)S(1)}, s32[16]{0:T(128)}) custom-call(s32[16]{0:T(128)S(1)} %fusion.59.order_ref, bf16[512,256]{1,0:T(8,128)(2,1)S(1)} %constant_dynamic-update-slice_fusion.rest_0_, bf16[512,256]{1,0:T(8,128)(2,1)S(1)} %collective-permute-done.3.rest_1_, bf16[512,256]{1,0:T(8,128)(2,1)S(1)} %collective-permute-done.4.rest_2_, ...), custom_call_target="tpu_custom_call" | custom-call | flops 536870912 | bytes 3407872 | tf_op jit(solution)/shard_map/spread_items/pallas_call | solution.py:153
  32.6 1.4 collective-permute-start.6
  33.9 1.7 %spread_items.5 = (bf16[512,256]{1,0:T(8,128)(2,1)S(1)}, s32[16]{0:T(128)}) custom-call(s32[16]{0:T(128)S(1)} %fusion.59.order_ref, bf16[512,256]{1,0:T(8,128)(2,1)S(1)} %constant_dynamic-update-slice_fusion.4.rest_0_, bf16[512,256]{1,0:T(8,128)(2,1)S(1)} %collective-permute-done.10.rest_1_, bf16[512,256]{1,0:T(8,128)(2,1)S(1)} %collective-permute-done.11.rest_2_, ...), custom_call_target="tpu_custom_call" | custom-call | flops 536870912 | bytes 3407872 | tf_op jit(solution)/shard_map/spread_items/pallas_call | solution.py:153
  36.4 3.4 %spread_items.6 = (bf16[512,256]{1,0:T(8,128)(2,1)S(1)}, bf16[512,256]{1,0:T(8,128)(2,1)S(1)}, bf16[512,256]{1,0:T(8,128)(2,1)S(1)}, s32[16]{0:T(128)}) custom-call(s32[16]{0:T(128)S(1)} %fusion.59.order_ref, bf16[512,256]{1,0:T(8,128)(2,1)S(1)} %constant_dynamic-update-slice_fusion.rest_0_, bf16[512,256]{1,0:T(8,128)(2,1)S(1)} %collective-permute-done.3.rest_1_, ...), custom_call_target="tpu_custom_call" | custom-call | flops 1610612736 | bytes 8126464 | tf_op jit(solution)/shard_map/spread_items/pallas_call | solution.py:153
  39.9 1.4 collective-permute-start.18
  41.3 3.4 %spread_items.7 = (bf16[512,256]{1,0:T(8,128)(2,1)S(1)}, bf16[512,256]{1,0:T(8,128)(2,1)S(1)}, bf16[512,256]{1,0:T(8,128)(2,1)S(1)}, s32[16]{0:T(128)}) custom-call(s32[16]{0:T(128)S(1)} %fusion.59.order_ref, bf16[512,256]{1,0:T(8,128)(2,1)S(1)} %constant_dynamic-update-slice_fusion.4.rest_0_, bf16[512,256]{1,0:T(8,128)(2,1)S(1)} %collective-permute-done.10.rest_1_, ...), custom_call_target="tpu_custom_call" | custom-call | flops 1610612736 | bytes 8126464 | tf_op jit(solution)/shard_map/spread_items/pallas_call | solution.py:153
  45.5 1.3 collective-permute-start.16
  47.5 1.3 collective-permute-start.14
  49.6 1.3 fusion.6
  50.8 2.2 %collective-permute-done.18.rest_1_ = bf16[512,256]{1,0:T(8,128)(2,1)S(1)} collective-permute-done((bf16[512,256]{1,0:T(8,128)(2,1)S(1)}, bf16[512,256]{1,0:T(8,128)(2,1)S(1)}, u32[]{:S(2)}, u32[]{:S(2)}) %collective-permute-start.18) | collective-permute-done | bytes 262176 | tf_op jit(solution)/shard_map/ppermute | solution.py:307
  53.0 1.3 collective-permute-start.15
  54.3 4.3 %collective-permute-done.19.rest_3_ = bf16[512,256]{1,0:T(8,128)(2,1)S(1)} collective-permute-done((bf16[512,256]{1,0:T(8,128)(2,1)S(1)}, bf16[512,256]{1,0:T(8,128)(2,1)S(1)}, u32[]{:S(2)}, u32[]{:S(2)}) %collective-permute-start.19) | collective-permute-done | bytes 262176 | tf_op jit(solution)/shard_map/ppermute | solution.py:307
  59.3 1.3 fusion.4
  60.6 3.6 %collective-permute-done.16.rest_1_ = bf16[512,256]{1,0:T(8,128)(2,1)S(1)} collective-permute-done((bf16[512,256]{1,0:T(8,128)(2,1)S(1)}, bf16[512,256]{1,0:T(8,128)(2,1)S(1)}, u32[]{:S(2)}, u32[]{:S(2)}) %collective-permute-start.16) | collective-permute-done | bytes 262176 | tf_op jit(solution)/shard_map/ppermute | solution.py:307
  64.3 5.6 %collective-permute-done.17.rest_3_ = bf16[512,256]{1,0:T(8,128)(2,1)S(1)} collective-permute-done((bf16[512,256]{1,0:T(8,128)(2,1)S(1)}, bf16[512,256]{1,0:T(8,128)(2,1)S(1)}, u32[]{:S(2)}, u32[]{:S(2)}) %collective-permute-start.17) | collective-permute-done | bytes 262176 | tf_op jit(solution)/shard_map/ppermute | solution.py:307
  70.6 1.3 add_add_fusion
  71.9 3.6 %collective-permute-done.14.rest_1_ = bf16[512,256]{1,0:T(8,128)(2,1)S(1)} collective-permute-done((bf16[512,256]{1,0:T(8,128)(2,1)S(1)}, bf16[512,256]{1,0:T(8,128)(2,1)S(1)}, u32[]{:S(2)}, u32[]{:S(2)}) %collective-permute-start.14) | collective-permute-done | bytes 262176 | tf_op jit(solution)/shard_map/ppermute | solution.py:307
  75.5 4.8 %collective-permute-done.15.rest_3_ = bf16[512,256]{1,0:T(8,128)(2,1)S(1)} collective-permute-done((bf16[512,256]{1,0:T(8,128)(2,1)S(1)}, bf16[512,256]{1,0:T(8,128)(2,1)S(1)}, u32[]{:S(2)}, u32[]{:S(2)}) %collective-permute-start.15) | collective-permute-done | bytes 262176 | tf_op jit(solution)/shard_map/ppermute | solution.py:307
  85.2 4.4 %collective-permute-start.23 = (bf16[2,2,128,256]{3,2,0,1:T(8,128)(2,1)S(1)}, bf16[2,2,128,256]{3,2,0,1:T(8,128)(2,1)S(1)}, u32[]{:S(2)}, u32[]{:S(2)}) collective-permute-start(bf16[2,2,128,256]{3,2,0,1:T(8,128)(2,1)S(1)} %fusion.35), channel_id=1, source_target_pairs={{0,8},{2,10},{4,12},{6,14},{8,0},{10,2},{12,4},{14,6},{16,24},{18,... | collective-permute-start | bytes 786440 | tf_op jit(solution)/shard_map/ppermute | solution.py:238
  89.6 1.0 pad_maximum_fusion.1
  90.6 1.9 %collective-permute-done.21 = bf16[2,2,128,256]{3,2,0,1:T(8,128)(2,1)S(1)} collective-permute-done((bf16[2,2,128,256]{3,2,0,1:T(8,128)(2,1)S(1)}, bf16[2,2,128,256]{3,2,0,1:T(8,128)(2,1)S(1)}, u32[]{:S(2)}, u32[]{:S(2)}) %collective-permute-start.21) | collective-permute-done | bytes 262176 | tf_op jit(solution)/shard_map/ppermute | solution.py:238
  92.6 3.4 %collective-permute-done.23 = bf16[2,2,128,256]{3,2,0,1:T(8,128)(2,1)S(1)} collective-permute-done((bf16[2,2,128,256]{3,2,0,1:T(8,128)(2,1)S(1)}, bf16[2,2,128,256]{3,2,0,1:T(8,128)(2,1)S(1)}, u32[]{:S(2)}, u32[]{:S(2)}) %collective-permute-start.23) | collective-permute-done | bytes 262176 | tf_op jit(solution)/shard_map/ppermute | solution.py:238
  96.0 1.8 %collective-permute-start.24 = (bf16[2,128,256]{2,1,0:T(8,128)(2,1)S(1)}, bf16[2,128,256]{2,1,0:T(8,128)(2,1)S(1)}, u32[]{:S(2)}, u32[]{:S(2)}) collective-permute-start(bf16[2,128,256]{2,1,0:T(8,128)(2,1)S(1)} %fusion.40), channel_id=1, source_target_pairs={{0,8},{2,10},{4,12},{6,14},{8,0},{10,2},{12,4},{14,6},{16,24},{18,... | collective-permute-start | bytes 393224 | tf_op jit(solution)/shard_map/ppermute | solution.py:238
  97.9 1.4 %collective-permute-start.25 = (bf16[2,128,256]{2,1,0:T(8,128)(2,1)S(1)}, bf16[2,128,256]{2,1,0:T(8,128)(2,1)S(1)}, u32[]{:S(2)}, u32[]{:S(2)}) collective-permute-start(bf16[2,128,256]{2,1,0:T(8,128)(2,1)S(1)} %fusion.41), channel_id=1, source_target_pairs={{0,4},{2,6},{4,0},{6,2},{8,12},{10,14},{12,8},{14,10},{16,20},{18,... | collective-permute-start | bytes 393224 | tf_op jit(solution)/shard_map/ppermute | solution.py:238
  99.3 1.8 %collective-permute-done.24 = bf16[2,128,256]{2,1,0:T(8,128)(2,1)S(1)} collective-permute-done((bf16[2,128,256]{2,1,0:T(8,128)(2,1)S(1)}, bf16[2,128,256]{2,1,0:T(8,128)(2,1)S(1)}, u32[]{:S(2)}, u32[]{:S(2)}) %collective-permute-start.24) | collective-permute-done | bytes 131104 | tf_op jit(solution)/shard_map/ppermute | solution.py:238
  101.1 1.8 %collective-permute-done.25 = bf16[2,128,256]{2,1,0:T(8,128)(2,1)S(1)} collective-permute-done((bf16[2,128,256]{2,1,0:T(8,128)(2,1)S(1)}, bf16[2,128,256]{2,1,0:T(8,128)(2,1)S(1)}, u32[]{:S(2)}, u32[]{:S(2)}) %collective-permute-start.25) | collective-permute-done | bytes 131104 | tf_op jit(solution)/shard_map/ppermute | solution.py:238
  103.0 2.4 %collective-permute-start.27 = (bf16[128,256]{1,0:T(8,128)(2,1)S(1)}, bf16[128,256]{1,0:T(8,128)(2,1)S(1)}, u32[]{:S(2)}, u32[]{:S(2)}) collective-permute-start(bf16[128,256]{1,0:T(8,128)(2,1)S(1)} %fusion.47), channel_id=1, source_target_pairs={{0,16},{2,18},{4,20},{6,22},{8,24},{10,26},{12,28},{14,30},{16,0},... | collective-permute-start | bytes 196616 | tf_op jit(solution)/shard_map/ppermute | solution.py:238
  106.0 3.8 %collective-permute-done.27 = bf16[128,256]{1,0:T(8,128)(2,1)S(1)} collective-permute-done((bf16[128,256]{1,0:T(8,128)(2,1)S(1)}, bf16[128,256]{1,0:T(8,128)(2,1)S(1)}, u32[]{:S(2)}, u32[]{:S(2)}) %collective-permute-start.27) | collective-permute-done | bytes 65568 | tf_op jit(solution)/shard_map/ppermute | solution.py:238
  113.5 1.7 %collective-permute-start.31 = (bf16[2,2,128,256]{3,2,1,0:T(8,128)(2,1)S(1)}, bf16[2,2,128,256]{3,2,1,0:T(8,128)(2,1)S(1)}, u32[]{:S(2)}, u32[]{:S(2)}) collective-permute-start(bf16[2,2,128,256]{3,2,1,0:T(8,128)(2,1)S(1)} %fusion.36), channel_id=1, source_target_pairs={{0,8},{2,10},{4,12},{6,14},{8,0},{10,2},{12,4},{14,6},{16,24},{18,... | collective-permute-start | bytes 786440 | tf_op jit(solution)/shard_map/ppermute | solution.py:238
  115.4 1.4 %collective-permute-start.29 = (bf16[2,2,136,256]{3,2,0,1:T(8,128)(2,1)S(1)}, bf16[2,2,136,256]{3,2,0,1:T(8,128)(2,1)S(1)}, u32[]{:S(2)}, u32[]{:S(2)}) collective-permute-start(bf16[2,2,136,256]{3,2,0,1:T(8,128)(2,1)S(1)} %fusion.33), channel_id=1, source_target_pairs={{0,4},{2,6},{4,0},{6,2},{8,12},{10,14},{12,8},{14,10},{16,20},{18,... | collective-permute-start | bytes 835592 | tf_op jit(solution)/shard_map/ppermute | solution.py:238
  117.1 4.9 %collective-permute-done.31 = bf16[2,2,128,256]{3,2,1,0:T(8,128)(2,1)S(1)} collective-permute-done((bf16[2,2,128,256]{3,2,1,0:T(8,128)(2,1)S(1)}, bf16[2,2,128,256]{3,2,1,0:T(8,128)(2,1)S(1)}, u32[]{:S(2)}, u32[]{:S(2)}) %collective-permute-start.31) | collective-permute-done | bytes 262176 | tf_op jit(solution)/shard_map/ppermute | solution.py:238
  123.1 1.4 collective-permute-start.33
  125.5 1.5 %collective-permute-start.32 = (bf16[2,136,256]{2,1,0:T(8,128)(2,1)S(1)}, bf16[2,136,256]{2,1,0:T(8,128)(2,1)S(1)}, u32[]{:S(2)}, u32[]{:S(2)}) collective-permute-start(bf16[2,136,256]{2,1,0:T(8,128)(2,1)S(1)} %fusion.39), channel_id=1, source_target_pairs={{0,8},{2,10},{4,12},{6,14},{8,0},{10,2},{12,4},{14,6},{16,24},{18,... | collective-permute-start | bytes 417800 | tf_op jit(solution)/shard_map/ppermute | solution.py:238
  127.0 1.1 collective-permute-done.33
  128.2 2.5 %collective-permute-done.32 = bf16[2,136,256]{2,1,0:T(8,128)(2,1)S(1)} collective-permute-done((bf16[2,136,256]{2,1,0:T(8,128)(2,1)S(1)}, bf16[2,136,256]{2,1,0:T(8,128)(2,1)S(1)}, u32[]{:S(2)}, u32[]{:S(2)}) %collective-permute-start.32) | collective-permute-done | bytes 139296 | tf_op jit(solution)/shard_map/ppermute | solution.py:238
  130.7 3.6 %collective-permute-start.35 = (bf16[128,256]{1,0:T(8,128)(2,1)S(1)}, bf16[128,256]{1,0:T(8,128)(2,1)S(1)}, u32[]{:S(2)}, u32[]{:S(2)}) collective-permute-start(bf16[128,256]{1,0:T(8,128)(2,1)S(1)} %fusion.48), channel_id=1, source_target_pairs={{0,16},{2,18},{4,20},{6,22},{8,24},{10,26},{12,28},{14,30},{16,0},... | collective-permute-start | bytes 196616 | tf_op jit(solution)/shard_map/ppermute | solution.py:238
  134.4 3.6 %collective-permute-done.35 = bf16[128,256]{1,0:T(8,128)(2,1)S(1)} collective-permute-done((bf16[128,256]{1,0:T(8,128)(2,1)S(1)}, bf16[128,256]{1,0:T(8,128)(2,1)S(1)}, u32[]{:S(2)}, u32[]{:S(2)}) %collective-permute-start.35) | collective-permute-done | bytes 65568 | tf_op jit(solution)/shard_map/ppermute | solution.py:238
  138.0 1.8 %collective-permute-done.34 = bf16[136,256]{1,0:T(8,128)(2,1)S(1)} collective-permute-done((bf16[136,256]{1,0:T(8,128)(2,1)S(1)}, bf16[136,256]{1,0:T(8,128)(2,1)S(1)}, u32[]{:S(2)}, u32[]{:S(2)}) %collective-permute-start.34) | collective-permute-done | bytes 69664 | tf_op jit(solution)/shard_map/ppermute | solution.py:238
  (118 shorter events, 22.3 us)
Async XLA Ops:
  0.6 14.7 %copy-start.7 = (s32[1,128]{1,0:T(1,128)S(1)}, s32[1,128]{1,0:T(1,128)}, u32[]{:S(2)}) copy-start(s32[1,128]{1,0:T(1,128)} %cats_ref.1) | copy-start | bytes 1540
  0.6 14.5 %copy-start.6 = (bf16[1,128,512]{2,1,0:T(8,128)(2,1)S(1)}, bf16[1,128,512]{2,1,0:T(8,128)(2,1)}, u32[]{:S(2)}) copy-start(bf16[1,128,512]{2,1,0:T(8,128)(2,1)} %param.12) | copy-start | bytes 393220
  0.7 24.7 %copy-start.4 = (s32[1,1,80]{2,1,0:T(1,128)S(1)}, s32[1,1,80]{2,1,0:T(1,128)}, u32[]{:S(2)}) copy-start(s32[1,1,80]{2,1,0:T(1,128)} %param.15) | copy-start | bytes 964
  4.3 11.9 %collective-permute-start = (bf16[128,256]{1,0:T(8,128)(2,1)}, bf16[128,256]{1,0:T(8,128)(2,1)S(1)}, u32[]{:S(2)}, u32[]{:S(2)}) collective-permute-start(bf16[128,256]{1,0:T(8,128)(2,1)} %get-tuple-element.30), channel_id=1, source_target_pairs={{0,8},{2,10},{4,12},{6,14},{8,0},{10,2},{12,4},{14,6},{16,24},{18,... | collective-permute-start | bytes 196616 | tf_op jit(solution)/shard_map/ppermute | solution.py:238
  7.4 8.9 %collective-permute-start.1 = (bf16[128,256]{1,0:T(8,128)(2,1)}, bf16[128,256]{1,0:T(8,128)(2,1)S(1)}, u32[]{:S(2)}, u32[]{:S(2)}) collective-permute-start(bf16[128,256]{1,0:T(8,128)(2,1)} %get-tuple-element.30), channel_id=1, source_target_pairs={{0,16},{2,18},{4,20},{6,22},{8,24},{10,26},{12,28},{14,30},{16,0},... | collective-permute-start | bytes 196616 | tf_op jit(solution)/shard_map/ppermute | solution.py:238
  9.9 6.8 %collective-permute-start.2 = (bf16[128,256]{1,0:T(8,128)(2,1)}, bf16[128,256]{1,0:T(8,128)(2,1)S(1)}, u32[]{:S(2)}, u32[]{:S(2)}) collective-permute-start(bf16[128,256]{1,0:T(8,128)(2,1)} %get-tuple-element.30), channel_id=1, source_target_pairs={{0,24},{2,26},{4,28},{6,30},{8,16},{10,18},{12,20},{14,22},{16,8},... | collective-permute-start | bytes 196616 | tf_op jit(solution)/shard_map/ppermute | solution.py:238
  10.0 8.3 %collective-permute-start.7 = (bf16[128,256]{1,0:T(8,128)(2,1)}, bf16[128,256]{1,0:T(8,128)(2,1)S(1)}, u32[]{:S(2)}, u32[]{:S(2)}) collective-permute-start(bf16[128,256]{1,0:T(8,128)(2,1)} %get-tuple-element.32), channel_id=1, source_target_pairs={{0,8},{2,10},{4,12},{6,14},{8,0},{10,2},{12,4},{14,6},{16,24},{18,... | collective-permute-start | bytes 196616 | tf_op jit(solution)/shard_map/ppermute | solution.py:238
  10.8 9.6 %collective-permute-start.8 = (bf16[128,256]{1,0:T(8,128)(2,1)}, bf16[128,256]{1,0:T(8,128)(2,1)S(1)}, u32[]{:S(2)}, u32[]{:S(2)}) collective-permute-start(bf16[128,256]{1,0:T(8,128)(2,1)} %get-tuple-element.32), channel_id=1, source_target_pairs={{0,16},{2,18},{4,20},{6,22},{8,24},{10,26},{12,28},{14,30},{16,0},... | collective-permute-start | bytes 196616 | tf_op jit(solution)/shard_map/ppermute | solution.py:238
  16.3 6.3 %collective-permute-start.9 = (bf16[128,256]{1,0:T(8,128)(2,1)}, bf16[128,256]{1,0:T(8,128)(2,1)S(1)}, u32[]{:S(2)}, u32[]{:S(2)}) collective-permute-start(bf16[128,256]{1,0:T(8,128)(2,1)} %get-tuple-element.32), channel_id=1, source_target_pairs={{0,24},{2,26},{4,28},{6,30},{8,16},{10,18},{12,20},{14,22},{16,8},... | collective-permute-start | bytes 196616 | tf_op jit(solution)/shard_map/ppermute | solution.py:238
  16.7 7.4 %collective-permute-start.3 = (bf16[512,256]{1,0:T(8,128)(2,1)S(1)}, bf16[512,256]{1,0:T(8,128)(2,1)S(1)}, u32[]{:S(2)}, u32[]{:S(2)}) collective-permute-start(bf16[512,256]{1,0:T(8,128)(2,1)S(1)} %constant_dynamic-update-slice_fusion.rest_0_), channel_id=1, source_target_pairs={{0,4},{2,6},{4,0},{6,2},{8,12},{10,14},{12,8},{14,10},{16,20},{18,... | collective-permute-start | bytes 786440 | tf_op jit(solution)/shard_map/ppermute | solution.py:238
  22.5 7.8 %collective-permute-start.10 = (bf16[512,256]{1,0:T(8,128)(2,1)S(1)}, bf16[512,256]{1,0:T(8,128)(2,1)S(1)}, u32[]{:S(2)}, u32[]{:S(2)}) collective-permute-start(bf16[512,256]{1,0:T(8,128)(2,1)S(1)} %constant_dynamic-update-slice_fusion.4.rest_0_), channel_id=1, source_target_pairs={{0,4},{2,6},{4,0},{6,2},{8,12},{10,14},{12,8},{14,10},{16,20},{18,... | collective-permute-start | bytes 786440 | tf_op jit(solution)/shard_map/ppermute | solution.py:238
  24.1 6.7 %collective-permute-start.4 = (bf16[512,256]{1,0:T(8,128)(2,1)S(1)}, bf16[512,256]{1,0:T(8,128)(2,1)S(1)}, u32[]{:S(2)}, u32[]{:S(2)}) collective-permute-start(bf16[512,256]{1,0:T(8,128)(2,1)S(1)} %constant_dynamic-update-slice_fusion.rest_0_), channel_id=1, source_target_pairs={{0,2},{2,0},{4,6},{6,4},{8,10},{10,8},{12,14},{14,12},{16,18},{18,... | collective-permute-start | bytes 786440 | tf_op jit(solution)/shard_map/ppermute | solution.py:238
  24.2 6.7 %collective-permute-start.5 = (bf16[512,256]{1,0:T(8,128)(2,1)S(1)}, bf16[512,256]{1,0:T(8,128)(2,1)S(1)}, u32[]{:S(2)}, u32[]{:S(2)}) collective-permute-start(bf16[512,256]{1,0:T(8,128)(2,1)S(1)} %collective-permute-done.3.rest_1_), channel_id=1, source_target_pairs={{0,2},{2,0},{4,6},{6,4},{8,10},{10,8},{12,14},{14,12},{16,18},{18,... | collective-permute-start | bytes 786440 | tf_op jit(solution)/shard_map/ppermute | solution.py:238
  25.3 2.5 %copy-start.2 = (s32[1,1,80,128,128]{4,3,2,1,0:T(8,128)S(1)}, s32[1,1,80,128,128]{4,3,2,1,0:T(8,128)}, u32[]{:S(2)}) copy-start(s32[1,1,80,128,128]{4,3,2,1,0:T(8,128)} %param.16) | copy-start | bytes 15728644
  30.2 3.7 %collective-permute-start.11 = (bf16[512,256]{1,0:T(8,128)(2,1)S(1)}, bf16[512,256]{1,0:T(8,128)(2,1)S(1)}, u32[]{:S(2)}, u32[]{:S(2)}) collective-permute-start(bf16[512,256]{1,0:T(8,128)(2,1)S(1)} %constant_dynamic-update-slice_fusion.4.rest_0_), channel_id=1, source_target_pairs={{0,2},{2,0},{4,6},{6,4},{8,10},{10,8},{12,14},{14,12},{16,18},{18,... | collective-permute-start | bytes 786440 | tf_op jit(solution)/shard_map/ppermute | solution.py:238
  30.3 3.6 %collective-permute-start.12 = (bf16[512,256]{1,0:T(8,128)(2,1)S(1)}, bf16[512,256]{1,0:T(8,128)(2,1)S(1)}, u32[]{:S(2)}, u32[]{:S(2)}) collective-permute-start(bf16[512,256]{1,0:T(8,128)(2,1)S(1)} %collective-permute-done.10.rest_1_), channel_id=1, source_target_pairs={{0,2},{2,0},{4,6},{6,4},{8,10},{10,8},{12,14},{14,12},{16,18},{18,... | collective-permute-start | bytes 786440 | tf_op jit(solution)/shard_map/ppermute | solution.py:238
  32.6 14.2 %collective-permute-start.6 = (bf16[512,256]{1,0:T(8,128)(2,1)S(1)}, bf16[512,256]{1,0:T(8,128)(2,1)S(1)}, u32[]{:S(2)}, u32[]{:S(2)}) collective-permute-start(bf16[512,256]{1,0:T(8,128)(2,1)S(1)} %get-tuple-element.31.rest_0_), channel_id=1, source_target_pairs={{0,1},{1,0},{2,3},{3,2},{4,5},{5,4},{6,7},{7,6},{8,9},{9,8},{10,11... | collective-permute-start | bytes 786440 | tf_op jit(solution)/shard_map/ppermute | solution.py:307
  35.6 11.9 %collective-permute-start.13 = (bf16[512,256]{1,0:T(8,128)(2,1)S(1)}, bf16[512,256]{1,0:T(8,128)(2,1)S(1)}, u32[]{:S(2)}, u32[]{:S(2)}) collective-permute-start(bf16[512,256]{1,0:T(8,128)(2,1)S(1)} %get-tuple-element.33.rest_2_), channel_id=1, source_target_pairs={{0,1},{1,0},{2,3},{3,2},{4,5},{5,4},{6,7},{7,6},{8,9},{9,8},{10,11... | collective-permute-start | bytes 786440 | tf_op jit(solution)/shard_map/ppermute | solution.py:307
  39.9 9.0 %copy-start = (bf16[2048,512]{1,0:T(8,128)(2,1)S(1)}, bf16[2048,512]{1,0:T(8,128)(2,1)}, u32[]{:S(2)}) copy-start(bf16[2048,512]{1,0:T(8,128)(2,1)} %user_ref.7) | copy-start | bytes 6291460
  39.9 9.0 %copy-start.1 = (bf16[2048,512]{1,0:T(8,128)(2,1)S(1)}, bf16[2048,512]{1,0:T(8,128)(2,1)}, u32[]{:S(2)}) copy-start(bf16[2048,512]{1,0:T(8,128)(2,1)} %grad_ref.7) | copy-start | bytes 6291460
  39.9 8.9 %copy-start.3 = (f32[512]{0:T(512)S(1)}, f32[512]{0:T(512)}, u32[]{:S(2)}) copy-start(f32[512]{0:T(512)} %param.11) | copy-start | bytes 6148
  39.9 13.1 %collective-permute-start.18 = (bf16[512,256]{1,0:T(8,128)(2,1)S(1)}, bf16[512,256]{1,0:T(8,128)(2,1)S(1)}, u32[]{:S(2)}, u32[]{:S(2)}) collective-permute-start(bf16[512,256]{1,0:T(8,128)(2,1)S(1)} %get-tuple-element.41.rest_0_), channel_id=1, source_target_pairs={{0,1},{1,0},{2,3},{3,2},{4,5},{5,4},{6,7},{7,6},{8,9},{9,8},{10,11... | collective-permute-start | bytes 786440 | tf_op jit(solution)/shard_map/ppermute | solution.py:307
  44.7 13.9 %collective-permute-start.19 = (bf16[512,256]{1,0:T(8,128)(2,1)S(1)}, bf16[512,256]{1,0:T(8,128)(2,1)S(1)}, u32[]{:S(2)}, u32[]{:S(2)}) collective-permute-start(bf16[512,256]{1,0:T(8,128)(2,1)S(1)} %get-tuple-element.42.rest_2_), channel_id=1, source_target_pairs={{0,1},{1,0},{2,3},{3,2},{4,5},{5,4},{6,7},{7,6},{8,9},{9,8},{10,11... | collective-permute-start | bytes 786440 | tf_op jit(solution)/shard_map/ppermute | solution.py:307
  45.5 18.8 %collective-permute-start.16 = (bf16[512,256]{1,0:T(8,128)(2,1)S(1)}, bf16[512,256]{1,0:T(8,128)(2,1)S(1)}, u32[]{:S(2)}, u32[]{:S(2)}) collective-permute-start(bf16[512,256]{1,0:T(8,128)(2,1)S(1)} %get-tuple-element.38.rest_0_), channel_id=1, source_target_pairs={{0,1},{1,0},{2,3},{3,2},{4,5},{5,4},{6,7},{7,6},{8,9},{9,8},{10,11... | collective-permute-start | bytes 786440 | tf_op jit(solution)/shard_map/ppermute | solution.py:307
  46.8 23.1 %collective-permute-start.17 = (bf16[512,256]{1,0:T(8,128)(2,1)S(1)}, bf16[512,256]{1,0:T(8,128)(2,1)S(1)}, u32[]{:S(2)}, u32[]{:S(2)}) collective-permute-start(bf16[512,256]{1,0:T(8,128)(2,1)S(1)} %get-tuple-element.39.rest_2_), channel_id=1, source_target_pairs={{0,1},{1,0},{2,3},{3,2},{4,5},{5,4},{6,7},{7,6},{8,9},{9,8},{10,11... | collective-permute-start | bytes 786440 | tf_op jit(solution)/shard_map/ppermute | solution.py:307
  47.5 28.0 %collective-permute-start.14 = (bf16[512,256]{1,0:T(8,128)(2,1)S(1)}, bf16[512,256]{1,0:T(8,128)(2,1)S(1)}, u32[]{:S(2)}, u32[]{:S(2)}) collective-permute-start(bf16[512,256]{1,0:T(8,128)(2,1)S(1)} %get-tuple-element.35.rest_0_), channel_id=1, source_target_pairs={{0,1},{1,0},{2,3},{3,2},{4,5},{5,4},{6,7},{7,6},{8,9},{9,8},{10,11... | collective-permute-start | bytes 786440 | tf_op jit(solution)/shard_map/ppermute | solution.py:307
  53.0 27.2 %collective-permute-start.15 = (bf16[512,256]{1,0:T(8,128)(2,1)S(1)}, bf16[512,256]{1,0:T(8,128)(2,1)S(1)}, u32[]{:S(2)}, u32[]{:S(2)}) collective-permute-start(bf16[512,256]{1,0:T(8,128)(2,1)S(1)} %get-tuple-element.36.rest_2_), channel_id=1, source_target_pairs={{0,1},{1,0},{2,3},{3,2},{4,5},{5,4},{6,7},{7,6},{8,9},{9,8},{10,11... | collective-permute-start | bytes 786440 | tf_op jit(solution)/shard_map/ppermute | solution.py:307
  81.9 2.0 %collective-permute-start.20 = (bf16[2,2,2,128,256]{4,3,0,1,2:T(8,128)(2,1)S(1)}, bf16[2,2,2,128,256]{4,3,0,1,2:T(8,128)(2,1)S(1)}, u32[]{:S(2)}, u32[]{:S(2)}) collective-permute-start(bf16[2,2,2,128,256]{4,3,0,1,2:T(8,128)(2,1)S(1)} %fusion.23), channel_id=1, source_target_pairs={{0,2},{2,0},{4,6},{6,4},{8,10},{10,8},{12,14},{14,12},{16,18},{18,... | collective-permute-start | bytes 1572872 | tf_op jit(solution)/shard_map/ppermute | solution.py:238
  82.9 2.1 %collective-permute-start.22 = (bf16[2,2,2,128,256]{4,3,0,2,1:T(8,128)(2,1)S(1)}, bf16[2,2,2,128,256]{4,3,0,2,1:T(8,128)(2,1)S(1)}, u32[]{:S(2)}, u32[]{:S(2)}) collective-permute-start(bf16[2,2,2,128,256]{4,3,0,2,1:T(8,128)(2,1)S(1)} %fusion.24), channel_id=1, source_target_pairs={{0,2},{2,0},{4,6},{6,4},{8,10},{10,8},{12,14},{14,12},{16,18},{18,... | collective-permute-start | bytes 1572872 | tf_op jit(solution)/shard_map/ppermute | solution.py:238
  84.1 8.4 %collective-permute-start.21 = (bf16[2,2,128,256]{3,2,0,1:T(8,128)(2,1)S(1)}, bf16[2,2,128,256]{3,2,0,1:T(8,128)(2,1)S(1)}, u32[]{:S(2)}, u32[]{:S(2)}) collective-permute-start(bf16[2,2,128,256]{3,2,0,1:T(8,128)(2,1)S(1)} %fusion.34), channel_id=1, source_target_pairs={{0,4},{2,6},{4,0},{6,2},{8,12},{10,14},{12,8},{14,10},{16,20},{18,... | collective-permute-start | bytes 786440 | tf_op jit(solution)/shard_map/ppermute | solution.py:238
  85.2 10.8 %collective-permute-start.23 = (bf16[2,2,128,256]{3,2,0,1:T(8,128)(2,1)S(1)}, bf16[2,2,128,256]{3,2,0,1:T(8,128)(2,1)S(1)}, u32[]{:S(2)}, u32[]{:S(2)}) collective-permute-start(bf16[2,2,128,256]{3,2,0,1:T(8,128)(2,1)S(1)} %fusion.35), channel_id=1, source_target_pairs={{0,8},{2,10},{4,12},{6,14},{8,0},{10,2},{12,4},{14,6},{16,24},{18,... | collective-permute-start | bytes 786440 | tf_op jit(solution)/shard_map/ppermute | solution.py:238
  96.0 5.0 %collective-permute-start.24 = (bf16[2,128,256]{2,1,0:T(8,128)(2,1)S(1)}, bf16[2,128,256]{2,1,0:T(8,128)(2,1)S(1)}, u32[]{:S(2)}, u32[]{:S(2)}) collective-permute-start(bf16[2,128,256]{2,1,0:T(8,128)(2,1)S(1)} %fusion.40), channel_id=1, source_target_pairs={{0,8},{2,10},{4,12},{6,14},{8,0},{10,2},{12,4},{14,6},{16,24},{18,... | collective-permute-start | bytes 393224 | tf_op jit(solution)/shard_map/ppermute | solution.py:238
  97.9 5.0 %collective-permute-start.25 = (bf16[2,128,256]{2,1,0:T(8,128)(2,1)S(1)}, bf16[2,128,256]{2,1,0:T(8,128)(2,1)S(1)}, u32[]{:S(2)}, u32[]{:S(2)}) collective-permute-start(bf16[2,128,256]{2,1,0:T(8,128)(2,1)S(1)} %fusion.41), channel_id=1, source_target_pairs={{0,4},{2,6},{4,0},{6,2},{8,12},{10,14},{12,8},{14,10},{16,20},{18,... | collective-permute-start | bytes 393224 | tf_op jit(solution)/shard_map/ppermute | solution.py:238
  103.0 6.8 %collective-permute-start.27 = (bf16[128,256]{1,0:T(8,128)(2,1)S(1)}, bf16[128,256]{1,0:T(8,128)(2,1)S(1)}, u32[]{:S(2)}, u32[]{:S(2)}) collective-permute-start(bf16[128,256]{1,0:T(8,128)(2,1)S(1)} %fusion.47), channel_id=1, source_target_pairs={{0,16},{2,18},{4,20},{6,22},{8,24},{10,26},{12,28},{14,30},{16,0},... | collective-permute-start | bytes 196616 | tf_op jit(solution)/shard_map/ppermute | solution.py:238
  105.4 5.2 %collective-permute-start.26 = (bf16[128,256]{1,0:T(8,128)(2,1)S(1)}, bf16[128,256]{1,0:T(8,128)(2,1)S(1)}, u32[]{:S(2)}, u32[]{:S(2)}) collective-permute-start(bf16[128,256]{1,0:T(8,128)(2,1)S(1)} %fusion.46), channel_id=1, source_target_pairs={{0,16},{2,18},{4,20},{6,22},{8,24},{10,26},{12,28},{14,30},{16,0},... | collective-permute-start | bytes 196616 | tf_op jit(solution)/shard_map/ppermute | solution.py:238
  110.3 3.0 %collective-permute-start.30 = (bf16[2,2,2,128,256]{4,3,2,1,0:T(8,128)(2,1)S(1)}, bf16[2,2,2,128,256]{4,3,2,1,0:T(8,128)(2,1)S(1)}, u32[]{:S(2)}, u32[]{:S(2)}) collective-permute-start(bf16[2,2,2,128,256]{4,3,2,1,0:T(8,128)(2,1)S(1)} %fusion.22), channel_id=1, source_target_pairs={{0,2},{2,0},{4,6},{6,4},{8,10},{10,8},{12,14},{14,12},{16,18},{18,... | collective-permute-start | bytes 1572872 | tf_op jit(solution)/shard_map/ppermute | solution.py:238
  111.1 1.6 %copy-start.5 = (bf16[4,512,512]{2,1,0:T(8,128)(2,1)S(1)}, bf16[4,512,512]{2,1,0:T(8,128)(2,1)}, u32[]{:S(2)}) copy-start(bf16[4,512,512]{2,1,0:T(8,128)(2,1)} %weight_ref.1) | copy-start | bytes 6291460
  111.4 3.8 %collective-permute-start.28 = (bf16[2,2,2,136,256]{4,3,0,1,2:T(8,128)(2,1)S(1)}, bf16[2,2,2,136,256]{4,3,0,1,2:T(8,128)(2,1)S(1)}, u32[]{:S(2)}, u32[]{:S(2)}) collective-permute-start(bf16[2,2,2,136,256]{4,3,0,1,2:T(8,128)(2,1)S(1)} %fusion.21), channel_id=1, source_target_pairs={{0,2},{2,0},{4,6},{6,4},{8,10},{10,8},{12,14},{14,12},{16,18},{18,... | collective-permute-start | bytes 1671176 | tf_op jit(solution)/shard_map/ppermute | solution.py:238
  113.5 8.5 %collective-permute-start.31 = (bf16[2,2,128,256]{3,2,1,0:T(8,128)(2,1)S(1)}, bf16[2,2,128,256]{3,2,1,0:T(8,128)(2,1)S(1)}, u32[]{:S(2)}, u32[]{:S(2)}) collective-permute-start(bf16[2,2,128,256]{3,2,1,0:T(8,128)(2,1)S(1)} %fusion.36), channel_id=1, source_target_pairs={{0,8},{2,10},{4,12},{6,14},{8,0},{10,2},{12,4},{14,6},{16,24},{18,... | collective-permute-start | bytes 786440 | tf_op jit(solution)/shard_map/ppermute | solution.py:238
  115.4 7.6 %collective-permute-start.29 = (bf16[2,2,136,256]{3,2,0,1:T(8,128)(2,1)S(1)}, bf16[2,2,136,256]{3,2,0,1:T(8,128)(2,1)S(1)}, u32[]{:S(2)}, u32[]{:S(2)}) collective-permute-start(bf16[2,2,136,256]{3,2,0,1:T(8,128)(2,1)S(1)} %fusion.33), channel_id=1, source_target_pairs={{0,4},{2,6},{4,0},{6,2},{8,12},{10,14},{12,8},{14,10},{16,20},{18,... | collective-permute-start | bytes 835592 | tf_op jit(solution)/shard_map/ppermute | solution.py:238
  123.1 5.0 %collective-permute-start.33 = (bf16[2,128,256]{2,1,0:T(8,128)(2,1)S(1)}, bf16[2,128,256]{2,1,0:T(8,128)(2,1)S(1)}, u32[]{:S(2)}, u32[]{:S(2)}) collective-permute-start(bf16[2,128,256]{2,1,0:T(8,128)(2,1)S(1)} %fusion.42), channel_id=1, source_target_pairs={{0,4},{2,6},{4,0},{6,2},{8,12},{10,14},{12,8},{14,10},{16,20},{18,... | collective-permute-start | bytes 393224 | tf_op jit(solution)/shard_map/ppermute | solution.py:238
  125.5 5.1 %collective-permute-start.32 = (bf16[2,136,256]{2,1,0:T(8,128)(2,1)S(1)}, bf16[2,136,256]{2,1,0:T(8,128)(2,1)S(1)}, u32[]{:S(2)}, u32[]{:S(2)}) collective-permute-start(bf16[2,136,256]{2,1,0:T(8,128)(2,1)S(1)} %fusion.39), channel_id=1, source_target_pairs={{0,8},{2,10},{4,12},{6,14},{8,0},{10,2},{12,4},{14,6},{16,24},{18,... | collective-permute-start | bytes 417800 | tf_op jit(solution)/shard_map/ppermute | solution.py:238
  130.7 7.2 %collective-permute-start.35 = (bf16[128,256]{1,0:T(8,128)(2,1)S(1)}, bf16[128,256]{1,0:T(8,128)(2,1)S(1)}, u32[]{:S(2)}, u32[]{:S(2)}) collective-permute-start(bf16[128,256]{1,0:T(8,128)(2,1)S(1)} %fusion.48), channel_id=1, source_target_pairs={{0,16},{2,18},{4,20},{6,22},{8,24},{10,26},{12,28},{14,30},{16,0},... | collective-permute-start | bytes 196616 | tf_op jit(solution)/shard_map/ppermute | solution.py:238
  134.3 5.5 %collective-permute-start.34 = (bf16[136,256]{1,0:T(8,128)(2,1)S(1)}, bf16[136,256]{1,0:T(8,128)(2,1)S(1)}, u32[]{:S(2)}, u32[]{:S(2)}) collective-permute-start(bf16[136,256]{1,0:T(8,128)(2,1)S(1)} %fusion.45), channel_id=1, source_target_pairs={{0,16},{2,18},{4,20},{6,22},{8,24},{10,26},{12,28},{14,30},{16,0},... | collective-permute-start | bytes 208904 | tf_op jit(solution)/shard_map/ppermute | solution.py:238

commit v10 on v9

--- a/solution.py
+++ b/solution.py
@@ -256,25 +256,25 @@
     return lax.axis_index("user") ^ (layer * 4 + side * 2 + core)
 
 
+def scatter_sum(terms, size, order):
+    bits = size.bit_length() - 1
+    index = lax.axis_index("user")
+    left = list(reversed(range(bits)))
+    terms = terms.reshape((2,) * bits + terms.shape[1:])
+    for bit in order:
+        axis = left.index(bit)
+        left.remove(bit)
+        mine = (index >> bit) & 1
+        own = lax.dynamic_index_in_dim(terms, mine, axis, keepdims=False)
+        away = lax.dynamic_index_in_dim(terms, 1 - mine, axis, keepdims=False)
+        terms = own + flip(away.astype(jnp.bfloat16), size, 1 << bit).astype(jnp.float32)
+    return terms
+
+
 def scatter_sums(halves, size):
     bits = size.bit_length() - 1
-    index = lax.axis_index("user")
     orders = [list(range(bits)), [0, 2, 1] + list(range(3, bits))]
-    halves = [terms.reshape((2,) * bits + terms.shape[1:]) for terms in halves]
-    left = [list(reversed(range(bits))) for _ in halves]
-    for stage in range(bits):
-        for half, terms in enumerate(halves):
-            bit = orders[half][stage]
-            axis = left[half].index(bit)
-            left[half].remove(bit)
-            mine = (index >> bit) & 1
-            own = lax.dynamic_index_in_dim(terms, mine, axis, keepdims=False)
-            away = lax.dynamic_index_in_dim(terms, 1 - mine, axis, keepdims=False)
-            arrived = flip(away.astype(jnp.bfloat16), size, 1 << bit)
-            halves[half] = own + arrived.astype(jnp.float32)
-        if 0 < stage < bits - 1:
-            halves = list(lax.optimization_barrier(tuple(halves)))
-    return halves
+    return [scatter_sum(terms, size, order) for terms, order in zip(halves, orders)]
 
 
 def on_device(

time: 142 us -> 141 us (level)
  waiting for transfers between devices: 57.1 us -> 54.9 us
  other arithmetic: 3.01 us -> 5.05 us
  starting transfers between devices: 45.1 us -> 43.5 us
    ppermute x28, waiting for transfers between devices: 33 us -> 30.6 us  [flip(): lax.ppermute(value, 'user', [(source, source ^ bits) for source in range(...]
    add x14, other arithmetic: 0.87 us -> 2.91 us  [scatter_sum(): own + flip(away.astype(jnp.bfloat16), size, 1 << bit).astype(jnp.float32)]
    unnamed x23 -> x31, local copies, waits for them, and re-layouts: 5.34 us -> 5.32 us
  transfers between devices with their start and end apart: 36 -> 36, of which waited for: 23 -> 19; matrix products, arithmetic and copies ran while one was open for 8% -> 10% of each run, Pallas kernels for 10% -> 10%
where the time goes in v10:
time: 141 us; the launch traced here: 140 us
  waiting for transfers between devices  54.9 us (39%)
  starting transfers between devices  43.5 us (31%)
  Pallas kernels  19.2 us (14%)
  matrix products  8.14 us (6%)
  local copies, waits for them, and re-layouts  7.4 us (5%)
  other arithmetic  5.05 us (4%)
  between operations  1.93 us (1%)
    ppermute x28, starting transfers between devices, flip(): lax.ppermute(value, 'user', [(source, source ^ bits) for source in range(...  34.8 us
    ppermute x28, waiting for transfers between devices, flip(): lax.ppermute(value, 'user', [(source, source ^ bits) for source in range(...  30.6 us
    ppermute x8, waiting for transfers between devices, on_device(): pieces.append(lax.ppermute(product, 'item', pairs))  24.3 us
    pallas_call x4, Pallas kernels, spread_items(): pl.pallas_call(functools.partial(spread, blocks), out_shape=[jax.ShapeDty...  10.3 us
    ppermute x8, starting transfers between devices, on_device(): pieces.append(lax.ppermute(product, 'item', pairs))  8.69 us
    unnamed x31, local copies, waits for them, and re-layouts  5.32 us
    dot_general x3, matrix products, on_device(): lax.dot_general(dense[chunk * rows:(chunk + 1) * rows], grad, (((0,), (0,...  3.91 us
    pallas_call x1, Pallas kernels, own_queries(): pl.pallas_call(project_own, out_shape=[half] * HALVES, grid_spec=pltpu.Pr...  3.67 us
  transfers between devices with their start and end apart: 36, of which 19 were waited for; matrix products, arithmetic and copies ran while one was open for 10% of the time, Pallas kernels for 10%

profile of v10, /device:TPU:0, one launch (start us, length us, event | category | flops | bytes accessed | tf_op | source)
XLA Modules:
  0.0 140.2 jit_solution(9823431111688489154)
XLA Ops:
  0.7 3.7 %own_queries.1 = (bf16[128,256]{1,0:T(8,128)(2,1)}, bf16[128,256]{1,0:T(8,128)(2,1)}) custom-call(s32[1]{0:T(128)} %bitcast.1.first_ref, s32[1,128]{1,0:T(1,128)} %cats_ref.1, bf16[128,512]{1,0:T(8,128)(2,1)} %bitcast.139, bf16[4,512,512]{2,1,0:T(8,128)(2,1)} %weight_ref.1), custom_call_target="tpu_custom_call" | custom-call | flops 268435456 | bytes 2359296 | tf_op jit(solution)/shard_map/own_queries/pallas_call | solution.py:97
  4.3 3.0 %collective-permute-start = (bf16[128,256]{1,0:T(8,128)(2,1)}, bf16[128,256]{1,0:T(8,128)(2,1)S(1)}, u32[]{:S(2)}, u32[]{:S(2)}) collective-permute-start(bf16[128,256]{1,0:T(8,128)(2,1)} %get-tuple-element.22), channel_id=1, source_target_pairs={{0,8},{2,10},{4,12},{6,14},{8,0},{10,2},{12,4},{14,6},{16,24},{18,... | collective-permute-start | bytes 196616 | tf_op jit(solution)/shard_map/ppermute | solution.py:238
  7.4 2.6 %collective-permute-start.1 = (bf16[128,256]{1,0:T(8,128)(2,1)}, bf16[128,256]{1,0:T(8,128)(2,1)S(1)}, u32[]{:S(2)}, u32[]{:S(2)}) collective-permute-start(bf16[128,256]{1,0:T(8,128)(2,1)} %get-tuple-element.22), channel_id=1, source_target_pairs={{0,16},{2,18},{4,20},{6,22},{8,24},{10,26},{12,28},{14,30},{16,0},... | collective-permute-start | bytes 196616 | tf_op jit(solution)/shard_map/ppermute | solution.py:238
  10.8 3.5 %collective-permute-start.8 = (bf16[128,256]{1,0:T(8,128)(2,1)}, bf16[128,256]{1,0:T(8,128)(2,1)S(1)}, u32[]{:S(2)}, u32[]{:S(2)}) collective-permute-start(bf16[128,256]{1,0:T(8,128)(2,1)} %get-tuple-element.24), channel_id=1, source_target_pairs={{0,16},{2,18},{4,20},{6,22},{8,24},{10,26},{12,28},{14,30},{16,0},... | collective-permute-start | bytes 196616 | tf_op jit(solution)/shard_map/ppermute | solution.py:238
  16.7 1.5 %collective-permute-start.3 = (bf16[512,256]{1,0:T(8,128)(2,1)S(1)}, bf16[512,256]{1,0:T(8,128)(2,1)S(1)}, u32[]{:S(2)}, u32[]{:S(2)}) collective-permute-start(bf16[512,256]{1,0:T(8,128)(2,1)S(1)} %constant_dynamic-update-slice_fusion.rest_0_), channel_id=1, source_target_pairs={{0,4},{2,6},{4,0},{6,2},{8,12},{10,14},{12,8},{14,10},{16,20},{18,... | collective-permute-start | bytes 786440 | tf_op jit(solution)/shard_map/ppermute | solution.py:238
  18.3 2.2 %collective-permute-done.8 = bf16[128,256]{1,0:T(8,128)(2,1)S(1)} collective-permute-done((bf16[128,256]{1,0:T(8,128)(2,1)}, bf16[128,256]{1,0:T(8,128)(2,1)S(1)}, u32[]{:S(2)}, u32[]{:S(2)}) %collective-permute-start.8) | collective-permute-done | bytes 65568 | tf_op jit(solution)/shard_map/ppermute | solution.py:238
  20.5 2.1 %collective-permute-done.9 = bf16[128,256]{1,0:T(8,128)(2,1)S(1)} collective-permute-done((bf16[128,256]{1,0:T(8,128)(2,1)}, bf16[128,256]{1,0:T(8,128)(2,1)S(1)}, u32[]{:S(2)}, u32[]{:S(2)}) %collective-permute-start.9) | collective-permute-done | bytes 65568 | tf_op jit(solution)/shard_map/ppermute | solution.py:238
  22.5 1.5 %collective-permute-start.10 = (bf16[512,256]{1,0:T(8,128)(2,1)S(1)}, bf16[512,256]{1,0:T(8,128)(2,1)S(1)}, u32[]{:S(2)}, u32[]{:S(2)}) collective-permute-start(bf16[512,256]{1,0:T(8,128)(2,1)S(1)} %constant_dynamic-update-slice_fusion.4.rest_0_), channel_id=1, source_target_pairs={{0,4},{2,6},{4,0},{6,2},{8,12},{10,14},{12,8},{14,10},{16,20},{18,... | collective-permute-start | bytes 786440 | tf_op jit(solution)/shard_map/ppermute | solution.py:238
  25.4 2.5 %copy-done.2 = s32[1,1,80,128,128]{4,3,2,1,0:T(8,128)S(1)} copy-done((s32[1,1,80,128,128]{4,3,2,1,0:T(8,128)S(1)}, s32[1,1,80,128,128]{4,3,2,1,0:T(8,128)}, u32[]{:S(2)}) %copy-start.2) | copy-done | bytes 5242904
  27.8 2.3 %place_tiles.1.rest_4_ = bf16[2048,2048]{1,0:T(8,128)(2,1)S(1)} custom-call(s32[80]{0:T(128)S(1)} %bitcast.130, s32[1]{0:T(128)} %bitcast.124.count_ref, s32[80,128,128]{2,1,0:T(8,128)S(1)} %bitcast.125), custom_call_target="tpu_custom_call" | custom-call | flops 1310720 | bytes 13631488 | tf_op jit(solution)/shard_map/place_tiles/pallas_call | solution.py:40
  30.8 1.7 %spread_items.4 = (bf16[512,256]{1,0:T(8,128)(2,1)S(1)}, s32[16]{0:T(128)}) custom-call(s32[16]{0:T(128)S(1)} %fusion.59.order_ref, bf16[512,256]{1,0:T(8,128)(2,1)S(1)} %constant_dynamic-update-slice_fusion.rest_0_, bf16[512,256]{1,0:T(8,128)(2,1)S(1)} %collective-permute-done.3.rest_1_, bf16[512,256]{1,0:T(8,128)(2,1)S(1)} %collective-permute-done.4.rest_2_, ...), custom_call_target="tpu_custom_call" | custom-call | flops 536870912 | bytes 3407872 | tf_op jit(solution)/shard_map/spread_items/pallas_call | solution.py:153
  32.5 1.3 collective-permute-start.6
  33.8 1.7 %spread_items.5 = (bf16[512,256]{1,0:T(8,128)(2,1)S(1)}, s32[16]{0:T(128)}) custom-call(s32[16]{0:T(128)S(1)} %fusion.59.order_ref, bf16[512,256]{1,0:T(8,128)(2,1)S(1)} %constant_dynamic-update-slice_fusion.4.rest_0_, bf16[512,256]{1,0:T(8,128)(2,1)S(1)} %collective-permute-done.10.rest_1_, bf16[512,256]{1,0:T(8,128)(2,1)S(1)} %collective-permute-done.11.rest_2_, ...), custom_call_target="tpu_custom_call" | custom-call | flops 536870912 | bytes 3407872 | tf_op jit(solution)/shard_map/spread_items/pallas_call | solution.py:153
  36.4 3.4 %spread_items.6 = (bf16[512,256]{1,0:T(8,128)(2,1)S(1)}, bf16[512,256]{1,0:T(8,128)(2,1)S(1)}, bf16[512,256]{1,0:T(8,128)(2,1)S(1)}, s32[16]{0:T(128)}) custom-call(s32[16]{0:T(128)S(1)} %fusion.59.order_ref, bf16[512,256]{1,0:T(8,128)(2,1)S(1)} %constant_dynamic-update-slice_fusion.rest_0_, bf16[512,256]{1,0:T(8,128)(2,1)S(1)} %collective-permute-done.3.rest_1_, ...), custom_call_target="tpu_custom_call" | custom-call | flops 1610612736 | bytes 8126464 | tf_op jit(solution)/shard_map/spread_items/pallas_call | solution.py:153
  39.9 1.3 collective-permute-start.18
  41.1 3.4 %spread_items.7 = (bf16[512,256]{1,0:T(8,128)(2,1)S(1)}, bf16[512,256]{1,0:T(8,128)(2,1)S(1)}, bf16[512,256]{1,0:T(8,128)(2,1)S(1)}, s32[16]{0:T(128)}) custom-call(s32[16]{0:T(128)S(1)} %fusion.59.order_ref, bf16[512,256]{1,0:T(8,128)(2,1)S(1)} %constant_dynamic-update-slice_fusion.4.rest_0_, bf16[512,256]{1,0:T(8,128)(2,1)S(1)} %collective-permute-done.10.rest_1_, ...), custom_call_target="tpu_custom_call" | custom-call | flops 1610612736 | bytes 8126464 | tf_op jit(solution)/shard_map/spread_items/pallas_call | solution.py:153
  45.5 1.2 collective-permute-start.16
  47.5 1.2 collective-permute-start.14
  49.4 1.3 fusion.6
  50.7 2.3 %collective-permute-done.18.rest_1_ = bf16[512,256]{1,0:T(8,128)(2,1)S(1)} collective-permute-done((bf16[512,256]{1,0:T(8,128)(2,1)S(1)}, bf16[512,256]{1,0:T(8,128)(2,1)S(1)}, u32[]{:S(2)}, u32[]{:S(2)}) %collective-permute-start.18) | collective-permute-done | bytes 262176 | tf_op jit(solution)/shard_map/ppermute | solution.py:307
  53.0 1.2 collective-permute-start.15
  54.1 4.5 %collective-permute-done.19.rest_3_ = bf16[512,256]{1,0:T(8,128)(2,1)S(1)} collective-permute-done((bf16[512,256]{1,0:T(8,128)(2,1)S(1)}, bf16[512,256]{1,0:T(8,128)(2,1)S(1)}, u32[]{:S(2)}, u32[]{:S(2)}) %collective-permute-start.19) | collective-permute-done | bytes 262176 | tf_op jit(solution)/shard_map/ppermute | solution.py:307
  59.3 1.3 fusion.4
  60.6 3.6 %collective-permute-done.16.rest_1_ = bf16[512,256]{1,0:T(8,128)(2,1)S(1)} collective-permute-done((bf16[512,256]{1,0:T(8,128)(2,1)S(1)}, bf16[512,256]{1,0:T(8,128)(2,1)S(1)}, u32[]{:S(2)}, u32[]{:S(2)}) %collective-permute-start.16) | collective-permute-done | bytes 262176 | tf_op jit(solution)/shard_map/ppermute | solution.py:307
  64.2 5.6 %collective-permute-done.17.rest_3_ = bf16[512,256]{1,0:T(8,128)(2,1)S(1)} collective-permute-done((bf16[512,256]{1,0:T(8,128)(2,1)S(1)}, bf16[512,256]{1,0:T(8,128)(2,1)S(1)}, u32[]{:S(2)}, u32[]{:S(2)}) %collective-permute-start.17) | collective-permute-done | bytes 262176 | tf_op jit(solution)/shard_map/ppermute | solution.py:307
  70.5 1.3 add_add_fusion
  71.9 3.6 %collective-permute-done.14.rest_1_ = bf16[512,256]{1,0:T(8,128)(2,1)S(1)} collective-permute-done((bf16[512,256]{1,0:T(8,128)(2,1)S(1)}, bf16[512,256]{1,0:T(8,128)(2,1)S(1)}, u32[]{:S(2)}, u32[]{:S(2)}) %collective-permute-start.14) | collective-permute-done | bytes 262176 | tf_op jit(solution)/shard_map/ppermute | solution.py:307
  75.5 4.8 %collective-permute-done.15.rest_3_ = bf16[512,256]{1,0:T(8,128)(2,1)S(1)} collective-permute-done((bf16[512,256]{1,0:T(8,128)(2,1)S(1)}, bf16[512,256]{1,0:T(8,128)(2,1)S(1)}, u32[]{:S(2)}, u32[]{:S(2)}) %collective-permute-start.15) | collective-permute-done | bytes 262176 | tf_op jit(solution)/shard_map/ppermute | solution.py:307
  86.7 1.2 bitcast_add_fusion.2
  87.9 3.9 %collective-permute-start.25 = (bf16[2,2,128,256]{3,2,0,1:T(8,128)(2,1)S(1)}, bf16[2,2,128,256]{3,2,0,1:T(8,128)(2,1)S(1)}, u32[]{:S(2)}, u32[]{:S(2)}) collective-permute-start(bf16[2,2,128,256]{3,2,0,1:T(8,128)(2,1)S(1)} %fusion.35), channel_id=1, source_target_pairs={{0,8},{2,10},{4,12},{6,14},{8,0},{10,2},{12,4},{14,6},{16,24},{18,... | collective-permute-start | bytes 786440 | tf_op jit(solution)/shard_map/ppermute | solution.py:238
  91.9 1.2 bitcast_add_fusion.3
  93.1 1.3 collective-permute-start.21
  94.3 4.0 %collective-permute-done.25 = bf16[2,2,128,256]{3,2,0,1:T(8,128)(2,1)S(1)} collective-permute-done((bf16[2,2,128,256]{3,2,0,1:T(8,128)(2,1)S(1)}, bf16[2,2,128,256]{3,2,0,1:T(8,128)(2,1)S(1)}, u32[]{:S(2)}, u32[]{:S(2)}) %collective-permute-start.25) | collective-permute-done | bytes 262176 | tf_op jit(solution)/shard_map/ppermute | solution.py:238
  98.5 1.3 collective-permute-start.26
  99.7 1.8 %collective-permute-done.21 = bf16[2,2,128,256]{3,2,0,1:T(8,128)(2,1)S(1)} collective-permute-done((bf16[2,2,128,256]{3,2,0,1:T(8,128)(2,1)S(1)}, bf16[2,2,128,256]{3,2,0,1:T(8,128)(2,1)S(1)}, u32[]{:S(2)}, u32[]{:S(2)}) %collective-permute-start.21) | collective-permute-done | bytes 262176 | tf_op jit(solution)/shard_map/ppermute | solution.py:238
  101.7 2.2 %collective-permute-done.26 = bf16[2,128,256]{2,1,0:T(8,128)(2,1)S(1)} collective-permute-done((bf16[2,128,256]{2,1,0:T(8,128)(2,1)S(1)}, bf16[2,128,256]{2,1,0:T(8,128)(2,1)S(1)}, u32[]{:S(2)}, u32[]{:S(2)}) %collective-permute-start.26) | collective-permute-done | bytes 131104 | tf_op jit(solution)/shard_map/ppermute | solution.py:238
  104.0 3.5 %collective-permute-start.27 = (bf16[128,256]{1,0:T(8,128)(2,1)S(1)}, bf16[128,256]{1,0:T(8,128)(2,1)S(1)}, u32[]{:S(2)}, u32[]{:S(2)}) collective-permute-start(bf16[128,256]{1,0:T(8,128)(2,1)S(1)} %fusion.47), channel_id=1, source_target_pairs={{0,16},{2,18},{4,20},{6,22},{8,24},{10,26},{12,28},{14,30},{16,0},... | collective-permute-start | bytes 196616 | tf_op jit(solution)/shard_map/ppermute | solution.py:238
  107.5 2.1 %collective-permute-start.23 = (bf16[128,256]{1,0:T(8,128)(2,1)S(1)}, bf16[128,256]{1,0:T(8,128)(2,1)S(1)}, u32[]{:S(2)}, u32[]{:S(2)}) collective-permute-start(bf16[128,256]{1,0:T(8,128)(2,1)S(1)} %fusion.46), channel_id=1, source_target_pairs={{0,16},{2,18},{4,20},{6,22},{8,24},{10,26},{12,28},{14,30},{16,0},... | collective-permute-start | bytes 196616 | tf_op jit(solution)/shard_map/ppermute | solution.py:238
  109.6 2.1 %collective-permute-done.27 = bf16[128,256]{1,0:T(8,128)(2,1)S(1)} collective-permute-done((bf16[128,256]{1,0:T(8,128)(2,1)S(1)}, bf16[128,256]{1,0:T(8,128)(2,1)S(1)}, u32[]{:S(2)}, u32[]{:S(2)}) %collective-permute-start.27) | collective-permute-done | bytes 65568 | tf_op jit(solution)/shard_map/ppermute | solution.py:238
  112.3 1.2 collective-permute-done.23
  116.8 1.3 collective-permute-start.29
  118.1 7.1 %collective-permute-done.33 = bf16[2,2,128,256]{3,2,1,0:T(8,128)(2,1)S(1)} collective-permute-done((bf16[2,2,128,256]{3,2,1,0:T(8,128)(2,1)S(1)}, bf16[2,2,128,256]{3,2,1,0:T(8,128)(2,1)S(1)}, u32[]{:S(2)}, u32[]{:S(2)}) %collective-permute-start.33) | collective-permute-done | bytes 262176 | tf_op jit(solution)/shard_map/ppermute | solution.py:238
  125.3 1.3 collective-permute-start.34
  127.7 2.8 %collective-permute-done.34 = bf16[2,128,256]{2,1,0:T(8,128)(2,1)S(1)} collective-permute-done((bf16[2,128,256]{2,1,0:T(8,128)(2,1)S(1)}, bf16[2,128,256]{2,1,0:T(8,128)(2,1)S(1)}, u32[]{:S(2)}, u32[]{:S(2)}) %collective-permute-start.34) | collective-permute-done | bytes 131104 | tf_op jit(solution)/shard_map/ppermute | solution.py:238
  130.5 1.7 %collective-permute-start.35 = (bf16[128,256]{1,0:T(8,128)(2,1)S(1)}, bf16[128,256]{1,0:T(8,128)(2,1)S(1)}, u32[]{:S(2)}, u32[]{:S(2)}) collective-permute-start(bf16[128,256]{1,0:T(8,128)(2,1)S(1)} %fusion.48), channel_id=1, source_target_pairs={{0,16},{2,18},{4,20},{6,22},{8,24},{10,26},{12,28},{14,30},{16,0},... | collective-permute-start | bytes 196616 | tf_op jit(solution)/shard_map/ppermute | solution.py:238
  132.3 2.3 %collective-permute-start.31 = (bf16[136,256]{1,0:T(8,128)(2,1)S(1)}, bf16[136,256]{1,0:T(8,128)(2,1)S(1)}, u32[]{:S(2)}, u32[]{:S(2)}) collective-permute-start(bf16[136,256]{1,0:T(8,128)(2,1)S(1)} %fusion.45), channel_id=1, source_target_pairs={{0,16},{2,18},{4,20},{6,22},{8,24},{10,26},{12,28},{14,30},{16,0},... | collective-permute-start | bytes 208904 | tf_op jit(solution)/shard_map/ppermute | solution.py:238
  134.6 2.8 %collective-permute-done.35 = bf16[128,256]{1,0:T(8,128)(2,1)S(1)} collective-permute-done((bf16[128,256]{1,0:T(8,128)(2,1)S(1)}, bf16[128,256]{1,0:T(8,128)(2,1)S(1)}, u32[]{:S(2)}, u32[]{:S(2)}) %collective-permute-start.35) | collective-permute-done | bytes 65568 | tf_op jit(solution)/shard_map/ppermute | solution.py:238
  137.4 1.5 %collective-permute-done.31 = bf16[136,256]{1,0:T(8,128)(2,1)S(1)} collective-permute-done((bf16[136,256]{1,0:T(8,128)(2,1)S(1)}, bf16[136,256]{1,0:T(8,128)(2,1)S(1)}, u32[]{:S(2)}, u32[]{:S(2)}) %collective-permute-start.31) | collective-permute-done | bytes 69664 | tf_op jit(solution)/shard_map/ppermute | solution.py:238
  (126 shorter events, 22.4 us)
Async XLA Ops:
  0.6 14.7 %copy-start.11 = (s32[1,128]{1,0:T(1,128)S(1)}, s32[1,128]{1,0:T(1,128)}, u32[]{:S(2)}) copy-start(s32[1,128]{1,0:T(1,128)} %cats_ref.1) | copy-start | bytes 1540
  0.6 14.5 %copy-start.10 = (bf16[1,128,512]{2,1,0:T(8,128)(2,1)S(1)}, bf16[1,128,512]{2,1,0:T(8,128)(2,1)}, u32[]{:S(2)}) copy-start(bf16[1,128,512]{2,1,0:T(8,128)(2,1)} %param.12) | copy-start | bytes 393220
  0.7 24.7 %copy-start.4 = (s32[1,1,80]{2,1,0:T(1,128)S(1)}, s32[1,1,80]{2,1,0:T(1,128)}, u32[]{:S(2)}) copy-start(s32[1,1,80]{2,1,0:T(1,128)} %param.15) | copy-start | bytes 964
  4.3 11.9 %collective-permute-start = (bf16[128,256]{1,0:T(8,128)(2,1)}, bf16[128,256]{1,0:T(8,128)(2,1)S(1)}, u32[]{:S(2)}, u32[]{:S(2)}) collective-permute-start(bf16[128,256]{1,0:T(8,128)(2,1)} %get-tuple-element.22), channel_id=1, source_target_pairs={{0,8},{2,10},{4,12},{6,14},{8,0},{10,2},{12,4},{14,6},{16,24},{18,... | collective-permute-start | bytes 196616 | tf_op jit(solution)/shard_map/ppermute | solution.py:238
  7.4 8.9 %collective-permute-start.1 = (bf16[128,256]{1,0:T(8,128)(2,1)}, bf16[128,256]{1,0:T(8,128)(2,1)S(1)}, u32[]{:S(2)}, u32[]{:S(2)}) collective-permute-start(bf16[128,256]{1,0:T(8,128)(2,1)} %get-tuple-element.22), channel_id=1, source_target_pairs={{0,16},{2,18},{4,20},{6,22},{8,24},{10,26},{12,28},{14,30},{16,0},... | collective-permute-start | bytes 196616 | tf_op jit(solution)/shard_map/ppermute | solution.py:238
  9.9 6.8 %collective-permute-start.2 = (bf16[128,256]{1,0:T(8,128)(2,1)}, bf16[128,256]{1,0:T(8,128)(2,1)S(1)}, u32[]{:S(2)}, u32[]{:S(2)}) collective-permute-start(bf16[128,256]{1,0:T(8,128)(2,1)} %get-tuple-element.22), channel_id=1, source_target_pairs={{0,24},{2,26},{4,28},{6,30},{8,16},{10,18},{12,20},{14,22},{16,8},... | collective-permute-start | bytes 196616 | tf_op jit(solution)/shard_map/ppermute | solution.py:238
  10.0 8.3 %collective-permute-start.7 = (bf16[128,256]{1,0:T(8,128)(2,1)}, bf16[128,256]{1,0:T(8,128)(2,1)S(1)}, u32[]{:S(2)}, u32[]{:S(2)}) collective-permute-start(bf16[128,256]{1,0:T(8,128)(2,1)} %get-tuple-element.24), channel_id=1, source_target_pairs={{0,8},{2,10},{4,12},{6,14},{8,0},{10,2},{12,4},{14,6},{16,24},{18,... | collective-permute-start | bytes 196616 | tf_op jit(solution)/shard_map/ppermute | solution.py:238
  10.8 9.6 %collective-permute-start.8 = (bf16[128,256]{1,0:T(8,128)(2,1)}, bf16[128,256]{1,0:T(8,128)(2,1)S(1)}, u32[]{:S(2)}, u32[]{:S(2)}) collective-permute-start(bf16[128,256]{1,0:T(8,128)(2,1)} %get-tuple-element.24), channel_id=1, source_target_pairs={{0,16},{2,18},{4,20},{6,22},{8,24},{10,26},{12,28},{14,30},{16,0},... | collective-permute-start | bytes 196616 | tf_op jit(solution)/shard_map/ppermute | solution.py:238
  16.3 6.3 %collective-permute-start.9 = (bf16[128,256]{1,0:T(8,128)(2,1)}, bf16[128,256]{1,0:T(8,128)(2,1)S(1)}, u32[]{:S(2)}, u32[]{:S(2)}) collective-permute-start(bf16[128,256]{1,0:T(8,128)(2,1)} %get-tuple-element.24), channel_id=1, source_target_pairs={{0,24},{2,26},{4,28},{6,30},{8,16},{10,18},{12,20},{14,22},{16,8},... | collective-permute-start | bytes 196616 | tf_op jit(solution)/shard_map/ppermute | solution.py:238
  16.7 7.4 %collective-permute-start.3 = (bf16[512,256]{1,0:T(8,128)(2,1)S(1)}, bf16[512,256]{1,0:T(8,128)(2,1)S(1)}, u32[]{:S(2)}, u32[]{:S(2)}) collective-permute-start(bf16[512,256]{1,0:T(8,128)(2,1)S(1)} %constant_dynamic-update-slice_fusion.rest_0_), channel_id=1, source_target_pairs={{0,4},{2,6},{4,0},{6,2},{8,12},{10,14},{12,8},{14,10},{16,20},{18,... | collective-permute-start | bytes 786440 | tf_op jit(solution)/shard_map/ppermute | solution.py:238
  22.5 7.7 %collective-permute-start.10 = (bf16[512,256]{1,0:T(8,128)(2,1)S(1)}, bf16[512,256]{1,0:T(8,128)(2,1)S(1)}, u32[]{:S(2)}, u32[]{:S(2)}) collective-permute-start(bf16[512,256]{1,0:T(8,128)(2,1)S(1)} %constant_dynamic-update-slice_fusion.4.rest_0_), channel_id=1, source_target_pairs={{0,4},{2,6},{4,0},{6,2},{8,12},{10,14},{12,8},{14,10},{16,20},{18,... | collective-permute-start | bytes 786440 | tf_op jit(solution)/shard_map/ppermute | solution.py:238
  24.1 6.7 %collective-permute-start.4 = (bf16[512,256]{1,0:T(8,128)(2,1)S(1)}, bf16[512,256]{1,0:T(8,128)(2,1)S(1)}, u32[]{:S(2)}, u32[]{:S(2)}) collective-permute-start(bf16[512,256]{1,0:T(8,128)(2,1)S(1)} %constant_dynamic-update-slice_fusion.rest_0_), channel_id=1, source_target_pairs={{0,2},{2,0},{4,6},{6,4},{8,10},{10,8},{12,14},{14,12},{16,18},{18,... | collective-permute-start | bytes 786440 | tf_op jit(solution)/shard_map/ppermute | solution.py:238
  24.2 6.6 %collective-permute-start.5 = (bf16[512,256]{1,0:T(8,128)(2,1)S(1)}, bf16[512,256]{1,0:T(8,128)(2,1)S(1)}, u32[]{:S(2)}, u32[]{:S(2)}) collective-permute-start(bf16[512,256]{1,0:T(8,128)(2,1)S(1)} %collective-permute-done.3.rest_1_), channel_id=1, source_target_pairs={{0,2},{2,0},{4,6},{6,4},{8,10},{10,8},{12,14},{14,12},{16,18},{18,... | collective-permute-start | bytes 786440 | tf_op jit(solution)/shard_map/ppermute | solution.py:238
  25.3 2.5 %copy-start.2 = (s32[1,1,80,128,128]{4,3,2,1,0:T(8,128)S(1)}, s32[1,1,80,128,128]{4,3,2,1,0:T(8,128)}, u32[]{:S(2)}) copy-start(s32[1,1,80,128,128]{4,3,2,1,0:T(8,128)} %param.16) | copy-start | bytes 15728644
  30.2 3.6 %collective-permute-start.11 = (bf16[512,256]{1,0:T(8,128)(2,1)S(1)}, bf16[512,256]{1,0:T(8,128)(2,1)S(1)}, u32[]{:S(2)}, u32[]{:S(2)}) collective-permute-start(bf16[512,256]{1,0:T(8,128)(2,1)S(1)} %constant_dynamic-update-slice_fusion.4.rest_0_), channel_id=1, source_target_pairs={{0,2},{2,0},{4,6},{6,4},{8,10},{10,8},{12,14},{14,12},{16,18},{18,... | collective-permute-start | bytes 786440 | tf_op jit(solution)/shard_map/ppermute | solution.py:238
  30.3 3.5 %collective-permute-start.12 = (bf16[512,256]{1,0:T(8,128)(2,1)S(1)}, bf16[512,256]{1,0:T(8,128)(2,1)S(1)}, u32[]{:S(2)}, u32[]{:S(2)}) collective-permute-start(bf16[512,256]{1,0:T(8,128)(2,1)S(1)} %collective-permute-done.10.rest_1_), channel_id=1, source_target_pairs={{0,2},{2,0},{4,6},{6,4},{8,10},{10,8},{12,14},{14,12},{16,18},{18,... | collective-permute-start | bytes 786440 | tf_op jit(solution)/shard_map/ppermute | solution.py:238
  32.5 14.1 %collective-permute-start.6 = (bf16[512,256]{1,0:T(8,128)(2,1)S(1)}, bf16[512,256]{1,0:T(8,128)(2,1)S(1)}, u32[]{:S(2)}, u32[]{:S(2)}) collective-permute-start(bf16[512,256]{1,0:T(8,128)(2,1)S(1)} %get-tuple-element.23.rest_0_), channel_id=1, source_target_pairs={{0,1},{1,0},{2,3},{3,2},{4,5},{5,4},{6,7},{7,6},{8,9},{9,8},{10,11... | collective-permute-start | bytes 786440 | tf_op jit(solution)/shard_map/ppermute | solution.py:307
  35.5 12.0 %collective-permute-start.13 = (bf16[512,256]{1,0:T(8,128)(2,1)S(1)}, bf16[512,256]{1,0:T(8,128)(2,1)S(1)}, u32[]{:S(2)}, u32[]{:S(2)}) collective-permute-start(bf16[512,256]{1,0:T(8,128)(2,1)S(1)} %get-tuple-element.25.rest_2_), channel_id=1, source_target_pairs={{0,1},{1,0},{2,3},{3,2},{4,5},{5,4},{6,7},{7,6},{8,9},{9,8},{10,11... | collective-permute-start | bytes 786440 | tf_op jit(solution)/shard_map/ppermute | solution.py:307
  39.8 8.9 %copy-start = (bf16[2048,512]{1,0:T(8,128)(2,1)S(1)}, bf16[2048,512]{1,0:T(8,128)(2,1)}, u32[]{:S(2)}) copy-start(bf16[2048,512]{1,0:T(8,128)(2,1)} %user_ref.7) | copy-start | bytes 6291460
  39.8 8.9 %copy-start.1 = (bf16[2048,512]{1,0:T(8,128)(2,1)S(1)}, bf16[2048,512]{1,0:T(8,128)(2,1)}, u32[]{:S(2)}) copy-start(bf16[2048,512]{1,0:T(8,128)(2,1)} %grad_ref.7) | copy-start | bytes 6291460
  39.9 8.8 %copy-start.3 = (f32[512]{0:T(512)S(1)}, f32[512]{0:T(512)}, u32[]{:S(2)}) copy-start(f32[512]{0:T(512)} %param.11) | copy-start | bytes 6148
  39.9 13.1 %collective-permute-start.18 = (bf16[512,256]{1,0:T(8,128)(2,1)S(1)}, bf16[512,256]{1,0:T(8,128)(2,1)S(1)}, u32[]{:S(2)}, u32[]{:S(2)}) collective-permute-start(bf16[512,256]{1,0:T(8,128)(2,1)S(1)} %get-tuple-element.33.rest_0_), channel_id=1, source_target_pairs={{0,1},{1,0},{2,3},{3,2},{4,5},{5,4},{6,7},{7,6},{8,9},{9,8},{10,11... | collective-permute-start | bytes 786440 | tf_op jit(solution)/shard_map/ppermute | solution.py:307
  44.6 14.0 %collective-permute-start.19 = (bf16[512,256]{1,0:T(8,128)(2,1)S(1)}, bf16[512,256]{1,0:T(8,128)(2,1)S(1)}, u32[]{:S(2)}, u32[]{:S(2)}) collective-permute-start(bf16[512,256]{1,0:T(8,128)(2,1)S(1)} %get-tuple-element.34.rest_2_), channel_id=1, source_target_pairs={{0,1},{1,0},{2,3},{3,2},{4,5},{5,4},{6,7},{7,6},{8,9},{9,8},{10,11... | collective-permute-start | bytes 786440 | tf_op jit(solution)/shard_map/ppermute | solution.py:307
  45.5 18.8 %collective-permute-start.16 = (bf16[512,256]{1,0:T(8,128)(2,1)S(1)}, bf16[512,256]{1,0:T(8,128)(2,1)S(1)}, u32[]{:S(2)}, u32[]{:S(2)}) collective-permute-start(bf16[512,256]{1,0:T(8,128)(2,1)S(1)} %get-tuple-element.30.rest_0_), channel_id=1, source_target_pairs={{0,1},{1,0},{2,3},{3,2},{4,5},{5,4},{6,7},{7,6},{8,9},{9,8},{10,11... | collective-permute-start | bytes 786440 | tf_op jit(solution)/shard_map/ppermute | solution.py:307
  46.7 23.2 %collective-permute-start.17 = (bf16[512,256]{1,0:T(8,128)(2,1)S(1)}, bf16[512,256]{1,0:T(8,128)(2,1)S(1)}, u32[]{:S(2)}, u32[]{:S(2)}) collective-permute-start(bf16[512,256]{1,0:T(8,128)(2,1)S(1)} %get-tuple-element.31.rest_2_), channel_id=1, source_target_pairs={{0,1},{1,0},{2,3},{3,2},{4,5},{5,4},{6,7},{7,6},{8,9},{9,8},{10,11... | collective-permute-start | bytes 786440 | tf_op jit(solution)/shard_map/ppermute | solution.py:307
  47.5 28.0 %collective-permute-start.14 = (bf16[512,256]{1,0:T(8,128)(2,1)S(1)}, bf16[512,256]{1,0:T(8,128)(2,1)S(1)}, u32[]{:S(2)}, u32[]{:S(2)}) collective-permute-start(bf16[512,256]{1,0:T(8,128)(2,1)S(1)} %get-tuple-element.27.rest_0_), channel_id=1, source_target_pairs={{0,1},{1,0},{2,3},{3,2},{4,5},{5,4},{6,7},{7,6},{8,9},{9,8},{10,11... | collective-permute-start | bytes 786440 | tf_op jit(solution)/shard_map/ppermute | solution.py:307
  53.0 27.2 %collective-permute-start.15 = (bf16[512,256]{1,0:T(8,128)(2,1)S(1)}, bf16[512,256]{1,0:T(8,128)(2,1)S(1)}, u32[]{:S(2)}, u32[]{:S(2)}) collective-permute-start(bf16[512,256]{1,0:T(8,128)(2,1)S(1)} %get-tuple-element.28.rest_2_), channel_id=1, source_target_pairs={{0,1},{1,0},{2,3},{3,2},{4,5},{5,4},{6,7},{7,6},{8,9},{9,8},{10,11... | collective-permute-start | bytes 786440 | tf_op jit(solution)/shard_map/ppermute | solution.py:307
  81.9 1.4 copy-start.7
  82.6 2.1 %copy-start.5 = (f32[2048,256]{1,0:T(8,128)}, f32[2048,256]{1,0:T(8,128)S(1)}, u32[]{:S(2)}) copy-start(f32[2048,256]{1,0:T(8,128)S(1)} %slice_add_fusion.1) | copy-start | bytes 6291460
  84.1 2.3 %collective-permute-start.24 = (bf16[2,2,2,128,256]{4,3,0,2,1:T(8,128)(2,1)}, bf16[2,2,2,128,256]{4,3,0,2,1:T(8,128)(2,1)}, u32[]{:S(2)}, u32[]{:S(2)}) collective-permute-start(bf16[2,2,2,128,256]{4,3,0,2,1:T(8,128)(2,1)} %fusion.24), channel_id=1, source_target_pairs={{0,2},{2,0},{4,6},{6,4},{8,10},{10,8},{12,14},{14,12},{16,18},{18,... | collective-permute-start | bytes 1572872 | tf_op jit(solution)/shard_map/ppermute | solution.py:238
  84.2 7.7 %collective-permute-start.20 = (bf16[2,2,2,128,256]{4,3,0,1,2:T(8,128)(2,1)S(1)}, bf16[2,2,2,128,256]{4,3,0,1,2:T(8,128)(2,1)}, u32[]{:S(2)}, u32[]{:S(2)}) collective-permute-start(bf16[2,2,2,128,256]{4,3,0,1,2:T(8,128)(2,1)S(1)} %fusion.23), channel_id=1, source_target_pairs={{0,2},{2,0},{4,6},{6,4},{8,10},{10,8},{12,14},{14,12},{16,18},{18,... | collective-permute-start | bytes 1572872 | tf_op jit(solution)/shard_map/ppermute | solution.py:238
  84.8 2.0 %copy-start.8 = (f32[2048,256]{1,0:T(8,128)S(1)}, f32[2048,256]{1,0:T(8,128)}, u32[]{:S(2)}) copy-start(f32[2048,256]{1,0:T(8,128)} %copy-done.7) | copy-start | bytes 6291460
  85.9 5.9 %copy-start.6 = (f32[2048,256]{1,0:T(8,128)S(1)}, f32[2048,256]{1,0:T(8,128)}, u32[]{:S(2)}) copy-start(f32[2048,256]{1,0:T(8,128)} %copy-done.5) | copy-start | bytes 6291460
  87.9 10.4 %collective-permute-start.25 = (bf16[2,2,128,256]{3,2,0,1:T(8,128)(2,1)S(1)}, bf16[2,2,128,256]{3,2,0,1:T(8,128)(2,1)S(1)}, u32[]{:S(2)}, u32[]{:S(2)}) collective-permute-start(bf16[2,2,128,256]{3,2,0,1:T(8,128)(2,1)S(1)} %fusion.35), channel_id=1, source_target_pairs={{0,8},{2,10},{4,12},{6,14},{8,0},{10,2},{12,4},{14,6},{16,24},{18,... | collective-permute-start | bytes 786440 | tf_op jit(solution)/shard_map/ppermute | solution.py:238
  93.1 8.4 %collective-permute-start.21 = (bf16[2,2,128,256]{3,2,0,1:T(8,128)(2,1)S(1)}, bf16[2,2,128,256]{3,2,0,1:T(8,128)(2,1)S(1)}, u32[]{:S(2)}, u32[]{:S(2)}) collective-permute-start(bf16[2,2,128,256]{3,2,0,1:T(8,128)(2,1)S(1)} %fusion.34), channel_id=1, source_target_pairs={{0,4},{2,6},{4,0},{6,2},{8,12},{10,14},{12,8},{14,10},{16,20},{18,... | collective-permute-start | bytes 786440 | tf_op jit(solution)/shard_map/ppermute | solution.py:238
  98.5 5.5 %collective-permute-start.26 = (bf16[2,128,256]{2,1,0:T(8,128)(2,1)S(1)}, bf16[2,128,256]{2,1,0:T(8,128)(2,1)S(1)}, u32[]{:S(2)}, u32[]{:S(2)}) collective-permute-start(bf16[2,128,256]{2,1,0:T(8,128)(2,1)S(1)} %fusion.41), channel_id=1, source_target_pairs={{0,4},{2,6},{4,0},{6,2},{8,12},{10,14},{12,8},{14,10},{16,20},{18,... | collective-permute-start | bytes 393224 | tf_op jit(solution)/shard_map/ppermute | solution.py:238
  101.6 5.9 %collective-permute-start.22 = (bf16[2,128,256]{2,1,0:T(8,128)(2,1)S(1)}, bf16[2,128,256]{2,1,0:T(8,128)(2,1)S(1)}, u32[]{:S(2)}, u32[]{:S(2)}) collective-permute-start(bf16[2,128,256]{2,1,0:T(8,128)(2,1)S(1)} %fusion.40), channel_id=1, source_target_pairs={{0,8},{2,10},{4,12},{6,14},{8,0},{10,2},{12,4},{14,6},{16,24},{18,... | collective-permute-start | bytes 393224 | tf_op jit(solution)/shard_map/ppermute | solution.py:238
  104.0 7.7 %collective-permute-start.27 = (bf16[128,256]{1,0:T(8,128)(2,1)S(1)}, bf16[128,256]{1,0:T(8,128)(2,1)S(1)}, u32[]{:S(2)}, u32[]{:S(2)}) collective-permute-start(bf16[128,256]{1,0:T(8,128)(2,1)S(1)} %fusion.47), channel_id=1, source_target_pairs={{0,16},{2,18},{4,20},{6,22},{8,24},{10,26},{12,28},{14,30},{16,0},... | collective-permute-start | bytes 196616 | tf_op jit(solution)/shard_map/ppermute | solution.py:238
  107.5 6.0 %copy-start.9 = (bf16[4,512,512]{2,1,0:T(8,128)(2,1)S(1)}, bf16[4,512,512]{2,1,0:T(8,128)(2,1)}, u32[]{:S(2)}) copy-start(bf16[4,512,512]{2,1,0:T(8,128)(2,1)} %weight_ref.1) | copy-start | bytes 6291460
  107.5 5.9 %collective-permute-start.23 = (bf16[128,256]{1,0:T(8,128)(2,1)S(1)}, bf16[128,256]{1,0:T(8,128)(2,1)S(1)}, u32[]{:S(2)}, u32[]{:S(2)}) collective-permute-start(bf16[128,256]{1,0:T(8,128)(2,1)S(1)} %fusion.46), channel_id=1, source_target_pairs={{0,16},{2,18},{4,20},{6,22},{8,24},{10,26},{12,28},{14,30},{16,0},... | collective-permute-start | bytes 196616 | tf_op jit(solution)/shard_map/ppermute | solution.py:238
  112.2 4.0 %collective-permute-start.32 = (bf16[2,2,2,128,256]{4,3,2,1,0:T(8,128)(2,1)S(1)}, bf16[2,2,2,128,256]{4,3,2,1,0:T(8,128)(2,1)S(1)}, u32[]{:S(2)}, u32[]{:S(2)}) collective-permute-start(bf16[2,2,2,128,256]{4,3,2,1,0:T(8,128)(2,1)S(1)} %fusion.22), channel_id=1, source_target_pairs={{0,2},{2,0},{4,6},{6,4},{8,10},{10,8},{12,14},{14,12},{16,18},{18,... | collective-permute-start | bytes 1572872 | tf_op jit(solution)/shard_map/ppermute | solution.py:238
  114.6 2.0 %collective-permute-start.28 = (bf16[2,2,2,136,256]{4,3,0,1,2:T(8,128)(2,1)S(1)}, bf16[2,2,2,136,256]{4,3,0,1,2:T(8,128)(2,1)S(1)}, u32[]{:S(2)}, u32[]{:S(2)}) collective-permute-start(bf16[2,2,2,136,256]{4,3,0,1,2:T(8,128)(2,1)S(1)} %fusion.21), channel_id=1, source_target_pairs={{0,2},{2,0},{4,6},{6,4},{8,10},{10,8},{12,14},{14,12},{16,18},{18,... | collective-permute-start | bytes 1671176 | tf_op jit(solution)/shard_map/ppermute | solution.py:238
  116.4 8.8 %collective-permute-start.33 = (bf16[2,2,128,256]{3,2,1,0:T(8,128)(2,1)S(1)}, bf16[2,2,128,256]{3,2,1,0:T(8,128)(2,1)S(1)}, u32[]{:S(2)}, u32[]{:S(2)}) collective-permute-start(bf16[2,2,128,256]{3,2,1,0:T(8,128)(2,1)S(1)} %fusion.36), channel_id=1, source_target_pairs={{0,8},{2,10},{4,12},{6,14},{8,0},{10,2},{12,4},{14,6},{16,24},{18,... | collective-permute-start | bytes 786440 | tf_op jit(solution)/shard_map/ppermute | solution.py:238
  116.8 9.8 %collective-permute-start.29 = (bf16[2,2,136,256]{3,2,0,1:T(8,128)(2,1)S(1)}, bf16[2,2,136,256]{3,2,0,1:T(8,128)(2,1)S(1)}, u32[]{:S(2)}, u32[]{:S(2)}) collective-permute-start(bf16[2,2,136,256]{3,2,0,1:T(8,128)(2,1)S(1)} %fusion.33), channel_id=1, source_target_pairs={{0,4},{2,6},{4,0},{6,2},{8,12},{10,14},{12,8},{14,10},{16,20},{18,... | collective-permute-start | bytes 835592 | tf_op jit(solution)/shard_map/ppermute | solution.py:238
  125.3 5.2 %collective-permute-start.34 = (bf16[2,128,256]{2,1,0:T(8,128)(2,1)S(1)}, bf16[2,128,256]{2,1,0:T(8,128)(2,1)S(1)}, u32[]{:S(2)}, u32[]{:S(2)}) collective-permute-start(bf16[2,128,256]{2,1,0:T(8,128)(2,1)S(1)} %fusion.42), channel_id=1, source_target_pairs={{0,4},{2,6},{4,0},{6,2},{8,12},{10,14},{12,8},{14,10},{16,20},{18,... | collective-permute-start | bytes 393224 | tf_op jit(solution)/shard_map/ppermute | solution.py:238
  126.7 5.5 %collective-permute-start.30 = (bf16[2,136,256]{2,1,0:T(8,128)(2,1)S(1)}, bf16[2,136,256]{2,1,0:T(8,128)(2,1)S(1)}, u32[]{:S(2)}, u32[]{:S(2)}) collective-permute-start(bf16[2,136,256]{2,1,0:T(8,128)(2,1)S(1)} %fusion.39), channel_id=1, source_target_pairs={{0,8},{2,10},{4,12},{6,14},{8,0},{10,2},{12,4},{14,6},{16,24},{18,... | collective-permute-start | bytes 417800 | tf_op jit(solution)/shard_map/ppermute | solution.py:238
  130.5 6.9 %collective-permute-start.35 = (bf16[128,256]{1,0:T(8,128)(2,1)S(1)}, bf16[128,256]{1,0:T(8,128)(2,1)S(1)}, u32[]{:S(2)}, u32[]{:S(2)}) collective-permute-start(bf16[128,256]{1,0:T(8,128)(2,1)S(1)} %fusion.48), channel_id=1, source_target_pairs={{0,16},{2,18},{4,20},{6,22},{8,24},{10,26},{12,28},{14,30},{16,0},... | collective-permute-start | bytes 196616 | tf_op jit(solution)/shard_map/ppermute | solution.py:238
  132.3 6.6 %collective-permute-start.31 = (bf16[136,256]{1,0:T(8,128)(2,1)S(1)}, bf16[136,256]{1,0:T(8,128)(2,1)S(1)}, u32[]{:S(2)}, u32[]{:S(2)}) collective-permute-start(bf16[136,256]{1,0:T(8,128)(2,1)S(1)} %fusion.45), channel_id=1, source_target_pairs={{0,16},{2,18},{4,20},{6,22},{8,24},{10,26},{12,28},{14,30},{16,0},... | collective-permute-start | bytes 208904 | tf_op jit(solution)/shard_map/ppermute | solution.py:238

commit v11 on v10

--- a/solution.py
+++ b/solution.py
@@ -256,7 +256,7 @@
     return lax.axis_index("user") ^ (layer * 4 + side * 2 + core)
 
 
-def scatter_sum(terms, size, order):
+def scatter_sum(terms, size, order, beside=None):
     bits = size.bit_length() - 1
     index = lax.axis_index("user")
     left = list(reversed(range(bits)))
@@ -268,13 +268,17 @@
         own = lax.dynamic_index_in_dim(terms, mine, axis, keepdims=False)
         away = lax.dynamic_index_in_dim(terms, 1 - mine, axis, keepdims=False)
         terms = own + flip(away.astype(jnp.bfloat16), size, 1 << bit).astype(jnp.float32)
-    return terms
-
-
-def scatter_sums(halves, size):
+        if beside is not None and len(left) == 2:
+            terms, beside = lax.optimization_barrier((terms, beside))
+    return terms, beside
+
+
+def scatter_sums(halves, size, beside=None):
     bits = size.bit_length() - 1
     orders = [list(range(bits)), [0, 2, 1] + list(range(3, bits))]
-    return [scatter_sum(terms, size, order) for terms, order in zip(halves, orders)]
+    first, _ = scatter_sum(halves[0], size, orders[0])
+    second, beside = scatter_sum(halves[1], size, orders[1], beside)
+    return [first, second], beside
 
 
 def on_device(
@@ -343,7 +347,8 @@
             preferred_element_type=jnp.float32,
         )
         halves.append(terms.reshape(user_size, own_items, half_width))
-    sums = [half.astype(jnp.bfloat16) for half in scatter_sums(halves, user_size)]
+    sums = [half.astype(jnp.bfloat16) for half in scatter_sums(halves, user_size)[0]]
+    own_sums = jnp.concatenate(sums, axis=1)
 
     chosen = own_cats[:, None] == first_expert + jnp.arange(experts_here, dtype=jnp.int32)[None, :]
     own_width = width // user_size
@@ -361,10 +366,9 @@
     gain_rows = jnp.pad(gain_own, (0, 8 * half_width - col_width)).reshape(1, 8, half_width)
     gain_rows = jnp.broadcast_to(gain_rows, (user_size, 8, half_width))
     halves[0] = jnp.concatenate([halves[0], gain_rows], axis=1)
-    halves = scatter_sums(halves, user_size)
+    halves, own_sums = scatter_sums(halves, user_size, own_sums)
     gain_grad = halves[0][-8:].reshape(-1)[:col_width]
     expert_grad = jnp.concatenate([halves[0][:-8], halves[1]], axis=1)
-    own_sums = jnp.concatenate(sums, axis=1)
     item_total = jnp.zeros((own_items, width), jnp.float32)
     for expert in range(experts_here):
         item_total = item_total + jnp.where(

time: 141 us -> 139 us (0.986)
  waiting for transfers between devices: 54.9 us -> 51.2 us
    ppermute x28, waiting for transfers between devices: 30.6 us -> 25.5 us  [flip(): lax.ppermute(value, 'user', [(source, source ^ bits) for source in range(...]
    unnamed x31 -> x29, local copies, waits for them, and re-layouts: 5.32 us -> 4.54 us
  transfers between devices with their start and end apart: 36 -> 36, of which waited for: 19 -> 19; matrix products, arithmetic and copies ran while one was open for 10% -> 12% of each run, Pallas kernels for 10% -> 11%
where the time goes in v11:
time: 139 us; the launch traced here: 138 us
  waiting for transfers between devices  51.2 us (37%)
  starting transfers between devices  42.7 us (31%)
  Pallas kernels  19.3 us (14%)
  matrix products  8.38 us (6%)
  local copies, waits for them, and re-layouts  8.12 us (6%)
  other arithmetic  6.24 us (4%)
  between operations  1.91 us (1%)
    ppermute x28, starting transfers between devices, flip(): lax.ppermute(value, 'user', [(source, source ^ bits) for source in range(...  33.8 us
    ppermute x8, waiting for transfers between devices, on_device(): pieces.append(lax.ppermute(product, 'item', pairs))  25.7 us
    ppermute x28, waiting for transfers between devices, flip(): lax.ppermute(value, 'user', [(source, source ^ bits) for source in range(...  25.5 us
    pallas_call x4, Pallas kernels, spread_items(): pl.pallas_call(functools.partial(spread, blocks), out_shape=[jax.ShapeDty...  10.3 us
    ppermute x8, starting transfers between devices, on_device(): pieces.append(lax.ppermute(product, 'item', pairs))  8.91 us
    unnamed x29, local copies, waits for them, and re-layouts  4.54 us
    dot_general x3, matrix products, on_device(): lax.dot_general(dense[chunk * rows:(chunk + 1) * rows], grad, (((0,), (0,...  4.05 us
    pallas_call x1, Pallas kernels, own_queries(): pl.pallas_call(project_own, out_shape=[half] * HALVES, grid_spec=pltpu.Pr...  3.68 us
  transfers between devices with their start and end apart: 36, of which 19 were waited for; matrix products, arithmetic and copies ran while one was open for 12% of the time, Pallas kernels for 11%

profile of v11, /device:TPU:0, one launch (start us, length us, event | category | flops | bytes accessed | tf_op | source)
XLA Modules:
  0.0 137.9 jit_solution(6580950909997314346)
XLA Ops:
  0.7 3.7 %own_queries.1 = (bf16[128,256]{1,0:T(8,128)(2,1)}, bf16[128,256]{1,0:T(8,128)(2,1)}) custom-call(s32[1]{0:T(128)} %bitcast.1.first_ref, s32[1,128]{1,0:T(1,128)} %cats_ref.1, bf16[128,512]{1,0:T(8,128)(2,1)} %bitcast.143, bf16[4,512,512]{2,1,0:T(8,128)(2,1)} %weight_ref.1), custom_call_target="tpu_custom_call" | custom-call | flops 268435456 | bytes 2359296 | tf_op jit(solution)/shard_map/own_queries/pallas_call | solution.py:97
  4.3 3.0 %collective-permute-start.7 = (bf16[128,256]{1,0:T(8,128)(2,1)}, bf16[128,256]{1,0:T(8,128)(2,1)S(1)}, u32[]{:S(2)}, u32[]{:S(2)}) collective-permute-start(bf16[128,256]{1,0:T(8,128)(2,1)} %get-tuple-element.26), channel_id=1, source_target_pairs={{0,8},{2,10},{4,12},{6,14},{8,0},{10,2},{12,4},{14,6},{16,24},{18,... | collective-permute-start | bytes 196616 | tf_op jit(solution)/shard_map/ppermute | solution.py:238
  7.4 2.6 %collective-permute-start.8 = (bf16[128,256]{1,0:T(8,128)(2,1)}, bf16[128,256]{1,0:T(8,128)(2,1)S(1)}, u32[]{:S(2)}, u32[]{:S(2)}) collective-permute-start(bf16[128,256]{1,0:T(8,128)(2,1)} %get-tuple-element.26), channel_id=1, source_target_pairs={{0,16},{2,18},{4,20},{6,22},{8,24},{10,26},{12,28},{14,30},{16,0},... | collective-permute-start | bytes 196616 | tf_op jit(solution)/shard_map/ppermute | solution.py:238
  10.9 3.5 %collective-permute-start.1 = (bf16[128,256]{1,0:T(8,128)(2,1)}, bf16[128,256]{1,0:T(8,128)(2,1)S(1)}, u32[]{:S(2)}, u32[]{:S(2)}) collective-permute-start(bf16[128,256]{1,0:T(8,128)(2,1)} %get-tuple-element.24), channel_id=1, source_target_pairs={{0,16},{2,18},{4,20},{6,22},{8,24},{10,26},{12,28},{14,30},{16,0},... | collective-permute-start | bytes 196616 | tf_op jit(solution)/shard_map/ppermute | solution.py:238
  16.8 1.5 %collective-permute-start.10 = (bf16[512,256]{1,0:T(8,128)(2,1)S(1)}, bf16[512,256]{1,0:T(8,128)(2,1)S(1)}, u32[]{:S(2)}, u32[]{:S(2)}) collective-permute-start(bf16[512,256]{1,0:T(8,128)(2,1)S(1)} %constant_dynamic-update-slice_fusion.4.rest_0_), channel_id=1, source_target_pairs={{0,4},{2,6},{4,0},{6,2},{8,12},{10,14},{12,8},{14,10},{16,20},{18,... | collective-permute-start | bytes 786440 | tf_op jit(solution)/shard_map/ppermute | solution.py:238
  18.3 2.2 %collective-permute-done.1 = bf16[128,256]{1,0:T(8,128)(2,1)S(1)} collective-permute-done((bf16[128,256]{1,0:T(8,128)(2,1)}, bf16[128,256]{1,0:T(8,128)(2,1)S(1)}, u32[]{:S(2)}, u32[]{:S(2)}) %collective-permute-start.1) | collective-permute-done | bytes 65568 | tf_op jit(solution)/shard_map/ppermute | solution.py:238
  20.5 1.9 %collective-permute-done.2 = bf16[128,256]{1,0:T(8,128)(2,1)S(1)} collective-permute-done((bf16[128,256]{1,0:T(8,128)(2,1)}, bf16[128,256]{1,0:T(8,128)(2,1)S(1)}, u32[]{:S(2)}, u32[]{:S(2)}) %collective-permute-start.2) | collective-permute-done | bytes 65568 | tf_op jit(solution)/shard_map/ppermute | solution.py:238
  22.4 1.5 %collective-permute-start.3 = (bf16[512,256]{1,0:T(8,128)(2,1)S(1)}, bf16[512,256]{1,0:T(8,128)(2,1)S(1)}, u32[]{:S(2)}, u32[]{:S(2)}) collective-permute-start(bf16[512,256]{1,0:T(8,128)(2,1)S(1)} %constant_dynamic-update-slice_fusion.rest_0_), channel_id=1, source_target_pairs={{0,4},{2,6},{4,0},{6,2},{8,12},{10,14},{12,8},{14,10},{16,20},{18,... | collective-permute-start | bytes 786440 | tf_op jit(solution)/shard_map/ppermute | solution.py:238
  24.8 2.5 %copy-done.2 = s32[1,1,80,128,128]{4,3,2,1,0:T(8,128)S(1)} copy-done((s32[1,1,80,128,128]{4,3,2,1,0:T(8,128)S(1)}, s32[1,1,80,128,128]{4,3,2,1,0:T(8,128)}, u32[]{:S(2)}) %copy-start.2) | copy-done | bytes 5242904
  27.3 2.3 %place_tiles.1.rest_4_ = bf16[2048,2048]{1,0:T(8,128)(2,1)S(1)} custom-call(s32[80]{0:T(128)S(1)} %bitcast.134, s32[1]{0:T(128)} %bitcast.128.count_ref, s32[80,128,128]{2,1,0:T(8,128)S(1)} %bitcast.129), custom_call_target="tpu_custom_call" | custom-call | flops 1310720 | bytes 13631488 | tf_op jit(solution)/shard_map/place_tiles/pallas_call | solution.py:40
  31.6 3.4 %spread_items.7 = (bf16[512,256]{1,0:T(8,128)(2,1)S(1)}, bf16[512,256]{1,0:T(8,128)(2,1)S(1)}, bf16[512,256]{1,0:T(8,128)(2,1)S(1)}, s32[16]{0:T(128)}) custom-call(s32[16]{0:T(128)S(1)} %fusion.59.order_ref, bf16[512,256]{1,0:T(8,128)(2,1)S(1)} %constant_dynamic-update-slice_fusion.4.rest_0_, bf16[512,256]{1,0:T(8,128)(2,1)S(1)} %collective-permute-done.10.rest_1_, ...), custom_call_target="tpu_custom_call" | custom-call | flops 1610612736 | bytes 8126464 | tf_op jit(solution)/shard_map/spread_items/pallas_call | solution.py:153
  35.0 1.4 collective-permute-start.19
  36.4 3.4 %spread_items.6 = (bf16[512,256]{1,0:T(8,128)(2,1)S(1)}, bf16[512,256]{1,0:T(8,128)(2,1)S(1)}, bf16[512,256]{1,0:T(8,128)(2,1)S(1)}, s32[16]{0:T(128)}) custom-call(s32[16]{0:T(128)S(1)} %fusion.59.order_ref, bf16[512,256]{1,0:T(8,128)(2,1)S(1)} %constant_dynamic-update-slice_fusion.rest_0_, bf16[512,256]{1,0:T(8,128)(2,1)S(1)} %collective-permute-done.3.rest_1_, ...), custom_call_target="tpu_custom_call" | custom-call | flops 1610612736 | bytes 8126464 | tf_op jit(solution)/shard_map/spread_items/pallas_call | solution.py:153
  40.6 1.7 %spread_items.5 = (bf16[512,256]{1,0:T(8,128)(2,1)S(1)}, s32[16]{0:T(128)}) custom-call(s32[16]{0:T(128)S(1)} %fusion.59.order_ref, bf16[512,256]{1,0:T(8,128)(2,1)S(1)} %constant_dynamic-update-slice_fusion.4.rest_0_, bf16[512,256]{1,0:T(8,128)(2,1)S(1)} %collective-permute-done.10.rest_1_, bf16[512,256]{1,0:T(8,128)(2,1)S(1)} %collective-permute-done.11.rest_2_, ...), custom_call_target="tpu_custom_call" | custom-call | flops 536870912 | bytes 3407872 | tf_op jit(solution)/shard_map/spread_items/pallas_call | solution.py:153
  42.4 1.4 collective-permute-start.13
  43.8 1.7 %spread_items.4 = (bf16[512,256]{1,0:T(8,128)(2,1)S(1)}, s32[16]{0:T(128)}) custom-call(s32[16]{0:T(128)S(1)} %fusion.59.order_ref, bf16[512,256]{1,0:T(8,128)(2,1)S(1)} %constant_dynamic-update-slice_fusion.rest_0_, bf16[512,256]{1,0:T(8,128)(2,1)S(1)} %collective-permute-done.3.rest_1_, bf16[512,256]{1,0:T(8,128)(2,1)S(1)} %collective-permute-done.4.rest_2_, ...), custom_call_target="tpu_custom_call" | custom-call | flops 536870912 | bytes 3407872 | tf_op jit(solution)/shard_map/spread_items/pallas_call | solution.py:153
  46.3 1.3 collective-permute-start.17
  48.3 1.6 %collective-permute-done.18.rest_1_ = bf16[512,256]{1,0:T(8,128)(2,1)S(1)} collective-permute-done((bf16[512,256]{1,0:T(8,128)(2,1)S(1)}, bf16[512,256]{1,0:T(8,128)(2,1)S(1)}, u32[]{:S(2)}, u32[]{:S(2)}) %collective-permute-start.18) | collective-permute-done | bytes 262176 | tf_op jit(solution)/shard_map/ppermute | solution.py:311
  49.9 1.3 collective-permute-start.15
  51.9 1.3 fusion.4
  53.2 2.3 %collective-permute-done.13.rest_3_ = bf16[512,256]{1,0:T(8,128)(2,1)S(1)} collective-permute-done((bf16[512,256]{1,0:T(8,128)(2,1)S(1)}, bf16[512,256]{1,0:T(8,128)(2,1)S(1)}, u32[]{:S(2)}, u32[]{:S(2)}) %collective-permute-start.13) | collective-permute-done | bytes 262176 | tf_op jit(solution)/shard_map/ppermute | solution.py:311
  55.5 1.3 collective-permute-start.14
  56.8 4.3 %collective-permute-done.6.rest_1_ = bf16[512,256]{1,0:T(8,128)(2,1)S(1)} collective-permute-done((bf16[512,256]{1,0:T(8,128)(2,1)S(1)}, bf16[512,256]{1,0:T(8,128)(2,1)S(1)}, u32[]{:S(2)}, u32[]{:S(2)}) %collective-permute-start.6) | collective-permute-done | bytes 262176 | tf_op jit(solution)/shard_map/ppermute | solution.py:311
  61.8 1.3 fusion.6
  63.1 3.6 %collective-permute-done.17.rest_3_ = bf16[512,256]{1,0:T(8,128)(2,1)S(1)} collective-permute-done((bf16[512,256]{1,0:T(8,128)(2,1)S(1)}, bf16[512,256]{1,0:T(8,128)(2,1)S(1)}, u32[]{:S(2)}, u32[]{:S(2)}) %collective-permute-start.17) | collective-permute-done | bytes 262176 | tf_op jit(solution)/shard_map/ppermute | solution.py:311
  66.7 5.6 %collective-permute-done.16.rest_1_ = bf16[512,256]{1,0:T(8,128)(2,1)S(1)} collective-permute-done((bf16[512,256]{1,0:T(8,128)(2,1)S(1)}, bf16[512,256]{1,0:T(8,128)(2,1)S(1)}, u32[]{:S(2)}, u32[]{:S(2)}) %collective-permute-start.16) | collective-permute-done | bytes 262176 | tf_op jit(solution)/shard_map/ppermute | solution.py:311
  73.1 1.4 %add_add_fusion = f32[2048,512]{1,0:T(8,128)S(1)} fusion(f32[2048,512]{1,0:T(8,128)S(1)} %fusion.6, f32[2048,512]{1,0:T(8,128)S(1)} %fusion.4, bf16[512,512]{1,0:T(8,128)(2,1)S(1)} %get-tuple-element.34, bf16[2048,2048]{1,0:T(8,128)(2,1)S(1)} %place_tiles.1.rest_4_), kind=kOutput, calls=%fused_computation | convolution fusion | flops 1075838976 | bytes 15204352 | tf_op jit(solution)/shard_map/dot_general | solution.py:327
  74.5 3.5 %collective-permute-done.15.rest_3_ = bf16[512,256]{1,0:T(8,128)(2,1)S(1)} collective-permute-done((bf16[512,256]{1,0:T(8,128)(2,1)S(1)}, bf16[512,256]{1,0:T(8,128)(2,1)S(1)}, u32[]{:S(2)}, u32[]{:S(2)}) %collective-permute-start.15) | collective-permute-done | bytes 262176 | tf_op jit(solution)/shard_map/ppermute | solution.py:311
  78.0 4.8 %collective-permute-done.14.rest_1_ = bf16[512,256]{1,0:T(8,128)(2,1)S(1)} collective-permute-done((bf16[512,256]{1,0:T(8,128)(2,1)S(1)}, bf16[512,256]{1,0:T(8,128)(2,1)S(1)}, u32[]{:S(2)}, u32[]{:S(2)}) %collective-permute-start.14) | collective-permute-done | bytes 262176 | tf_op jit(solution)/shard_map/ppermute | solution.py:311
  88.4 1.5 %bitcast_add_fusion.3 = f32[2,2,2,128,256]{4,3,0,2,1:T(8,128)S(1)} fusion(bf16[2,2,2,128,256]{4,3,0,2,1:T(8,128)(2,1)} %collective-permute-done.20, f32[2,2,2,2,128,256]{5,4,3,2,1,0:T(8,128)} %bitcast.140, s32[]{:T(128)S(6)} %select_n.111), kind=kLoop, calls=%fused_computation.30 | loop fusion | flops 524288 | bytes 2621444 | tf_op jit(solution)/shard_map/add | solution.py:270
  90.1 1.2 bitcast_add_fusion.1
  91.3 1.8 %collective-permute-start.27 = (bf16[2,2,128,256]{3,2,0,1:T(8,128)(2,1)S(1)}, bf16[2,2,128,256]{3,2,0,1:T(8,128)(2,1)S(1)}, u32[]{:S(2)}, u32[]{:S(2)}) collective-permute-start(bf16[2,2,128,256]{3,2,0,1:T(8,128)(2,1)S(1)} %fusion.36), channel_id=1, source_target_pairs={{0,4},{2,6},{4,0},{6,2},{8,12},{10,14},{12,8},{14,10},{16,20},{18,... | collective-permute-start | bytes 786440 | tf_op jit(solution)/shard_map/ppermute | solution.py:238
  93.0 5.2 %collective-permute-done.21 = bf16[2,2,128,256]{3,2,0,1:T(8,128)(2,1)S(1)} collective-permute-done((bf16[2,2,128,256]{3,2,0,1:T(8,128)(2,1)S(1)}, bf16[2,2,128,256]{3,2,0,1:T(8,128)(2,1)S(1)}, u32[]{:S(2)}, u32[]{:S(2)}) %collective-permute-start.21) | collective-permute-done | bytes 262176 | tf_op jit(solution)/shard_map/ppermute | solution.py:238
  98.4 1.2 collective-permute-start.22
  99.7 2.2 %collective-permute-start.28 = (bf16[2,128,256]{2,1,0:T(8,128)(2,1)S(1)}, bf16[2,128,256]{2,1,0:T(8,128)(2,1)S(1)}, u32[]{:S(2)}, u32[]{:S(2)}) collective-permute-start(bf16[2,128,256]{2,1,0:T(8,128)(2,1)S(1)} %fusion.41), channel_id=1, source_target_pairs={{0,8},{2,10},{4,12},{6,14},{8,0},{10,2},{12,4},{14,6},{16,24},{18,... | collective-permute-start | bytes 393224 | tf_op jit(solution)/shard_map/ppermute | solution.py:238
  101.9 1.5 %collective-permute-done.22 = bf16[2,128,256]{2,1,0:T(8,128)(2,1)S(1)} collective-permute-done((bf16[2,128,256]{2,1,0:T(8,128)(2,1)S(1)}, bf16[2,128,256]{2,1,0:T(8,128)(2,1)S(1)}, u32[]{:S(2)}, u32[]{:S(2)}) %collective-permute-start.22) | collective-permute-done | bytes 131104 | tf_op jit(solution)/shard_map/ppermute | solution.py:238
  103.5 2.0 %collective-permute-start.23 = (bf16[128,256]{1,0:T(8,128)(2,1)S(1)}, bf16[128,256]{1,0:T(8,128)(2,1)S(1)}, u32[]{:S(2)}, u32[]{:S(2)}) collective-permute-start(bf16[128,256]{1,0:T(8,128)(2,1)S(1)} %fusion.46), channel_id=1, source_target_pairs={{0,16},{2,18},{4,20},{6,22},{8,24},{10,26},{12,28},{14,30},{16,0},... | collective-permute-start | bytes 196616 | tf_op jit(solution)/shard_map/ppermute | solution.py:238
  105.5 1.8 %collective-permute-start.29 = (bf16[128,256]{1,0:T(8,128)(2,1)S(1)}, bf16[128,256]{1,0:T(8,128)(2,1)S(1)}, u32[]{:S(2)}, u32[]{:S(2)}) collective-permute-start(bf16[128,256]{1,0:T(8,128)(2,1)S(1)} %fusion.47), channel_id=1, source_target_pairs={{0,16},{2,18},{4,20},{6,22},{8,24},{10,26},{12,28},{14,30},{16,0},... | collective-permute-start | bytes 196616 | tf_op jit(solution)/shard_map/ppermute | solution.py:238
  107.3 2.8 %collective-permute-done.23 = bf16[128,256]{1,0:T(8,128)(2,1)S(1)} collective-permute-done((bf16[128,256]{1,0:T(8,128)(2,1)S(1)}, bf16[128,256]{1,0:T(8,128)(2,1)S(1)}, u32[]{:S(2)}, u32[]{:S(2)}) %collective-permute-start.23) | collective-permute-done | bytes 65568 | tf_op jit(solution)/shard_map/ppermute | solution.py:238
  113.4 2.1 %collective-permute-start.25 = (bf16[2,2,128,256]{3,2,1,0:T(8,128)(2,1)S(1)}, bf16[2,2,128,256]{3,2,1,0:T(8,128)(2,1)S(1)}, u32[]{:S(2)}, u32[]{:S(2)}) collective-permute-start(bf16[2,2,128,256]{3,2,1,0:T(8,128)(2,1)S(1)} %fusion.35), channel_id=1, source_target_pairs={{0,8},{2,10},{4,12},{6,14},{8,0},{10,2},{12,4},{14,6},{16,24},{18,... | collective-permute-start | bytes 786440 | tf_op jit(solution)/shard_map/ppermute | solution.py:238
  116.5 5.6 %collective-permute-done.25 = bf16[2,2,128,256]{3,2,1,0:T(8,128)(2,1)S(1)} collective-permute-done((bf16[2,2,128,256]{3,2,1,0:T(8,128)(2,1)S(1)}, bf16[2,2,128,256]{3,2,1,0:T(8,128)(2,1)S(1)}, u32[]{:S(2)}, u32[]{:S(2)}) %collective-permute-start.25) | collective-permute-done | bytes 262176 | tf_op jit(solution)/shard_map/ppermute | solution.py:238
  122.2 1.1 collective-permute-start.34
  125.4 1.3 collective-permute-start.32
  127.3 2.3 %collective-permute-start.35 = (bf16[128,256]{1,0:T(8,128)(2,1)S(1)}, bf16[128,256]{1,0:T(8,128)(2,1)S(1)}, u32[]{:S(2)}, u32[]{:S(2)}) collective-permute-start(bf16[128,256]{1,0:T(8,128)(2,1)S(1)} %fusion.48), channel_id=1, source_target_pairs={{0,16},{2,18},{4,20},{6,22},{8,24},{10,26},{12,28},{14,30},{16,0},... | collective-permute-start | bytes 196616 | tf_op jit(solution)/shard_map/ppermute | solution.py:238
  129.6 1.6 %collective-permute-done.32 = bf16[2,136,256]{2,1,0:T(8,128)(2,1)S(1)} collective-permute-done((bf16[2,136,256]{2,1,0:T(8,128)(2,1)S(1)}, bf16[2,136,256]{2,1,0:T(8,128)(2,1)S(1)}, u32[]{:S(2)}, u32[]{:S(2)}) %collective-permute-start.32) | collective-permute-done | bytes 139296 | tf_op jit(solution)/shard_map/ppermute | solution.py:238
  131.3 2.0 %collective-permute-start.33 = (bf16[136,256]{1,0:T(8,128)(2,1)S(1)}, bf16[136,256]{1,0:T(8,128)(2,1)S(1)}, u32[]{:S(2)}, u32[]{:S(2)}) collective-permute-start(bf16[136,256]{1,0:T(8,128)(2,1)S(1)} %fusion.45), channel_id=1, source_target_pairs={{0,16},{2,18},{4,20},{6,22},{8,24},{10,26},{12,28},{14,30},{16,0},... | collective-permute-start | bytes 208904 | tf_op jit(solution)/shard_map/ppermute | solution.py:238
  133.2 1.4 %collective-permute-done.35 = bf16[128,256]{1,0:T(8,128)(2,1)S(1)} collective-permute-done((bf16[128,256]{1,0:T(8,128)(2,1)S(1)}, bf16[128,256]{1,0:T(8,128)(2,1)S(1)}, u32[]{:S(2)}, u32[]{:S(2)}) %collective-permute-start.35) | collective-permute-done | bytes 65568 | tf_op jit(solution)/shard_map/ppermute | solution.py:238
  134.7 1.9 %collective-permute-done.33 = bf16[136,256]{1,0:T(8,128)(2,1)S(1)} collective-permute-done((bf16[136,256]{1,0:T(8,128)(2,1)S(1)}, bf16[136,256]{1,0:T(8,128)(2,1)S(1)}, u32[]{:S(2)}, u32[]{:S(2)}) %collective-permute-start.33) | collective-permute-done | bytes 69664 | tf_op jit(solution)/shard_map/ppermute | solution.py:238
  (125 shorter events, 24.2 us)
Async XLA Ops:
  0.6 23.4 %copy-start.9 = (bf16[1,128,512]{2,1,0:T(8,128)(2,1)S(1)}, bf16[1,128,512]{2,1,0:T(8,128)(2,1)}, u32[]{:S(2)}) copy-start(bf16[1,128,512]{2,1,0:T(8,128)(2,1)} %param.12) | copy-start | bytes 393220
  0.6 23.3 %copy-start.10 = (s32[1,128]{1,0:T(1,128)S(1)}, s32[1,128]{1,0:T(1,128)}, u32[]{:S(2)}) copy-start(s32[1,128]{1,0:T(1,128)} %cats_ref.1) | copy-start | bytes 1540
  0.7 24.1 %copy-start.4 = (s32[1,1,80]{2,1,0:T(1,128)S(1)}, s32[1,1,80]{2,1,0:T(1,128)}, u32[]{:S(2)}) copy-start(s32[1,1,80]{2,1,0:T(1,128)} %param.15) | copy-start | bytes 964
  4.3 11.7 %collective-permute-start.7 = (bf16[128,256]{1,0:T(8,128)(2,1)}, bf16[128,256]{1,0:T(8,128)(2,1)S(1)}, u32[]{:S(2)}, u32[]{:S(2)}) collective-permute-start(bf16[128,256]{1,0:T(8,128)(2,1)} %get-tuple-element.26), channel_id=1, source_target_pairs={{0,8},{2,10},{4,12},{6,14},{8,0},{10,2},{12,4},{14,6},{16,24},{18,... | collective-permute-start | bytes 196616 | tf_op jit(solution)/shard_map/ppermute | solution.py:238
  7.4 8.8 %collective-permute-start.8 = (bf16[128,256]{1,0:T(8,128)(2,1)}, bf16[128,256]{1,0:T(8,128)(2,1)S(1)}, u32[]{:S(2)}, u32[]{:S(2)}) collective-permute-start(bf16[128,256]{1,0:T(8,128)(2,1)} %get-tuple-element.26), channel_id=1, source_target_pairs={{0,16},{2,18},{4,20},{6,22},{8,24},{10,26},{12,28},{14,30},{16,0},... | collective-permute-start | bytes 196616 | tf_op jit(solution)/shard_map/ppermute | solution.py:238
  10.0 6.8 %collective-permute-start.9 = (bf16[128,256]{1,0:T(8,128)(2,1)}, bf16[128,256]{1,0:T(8,128)(2,1)S(1)}, u32[]{:S(2)}, u32[]{:S(2)}) collective-permute-start(bf16[128,256]{1,0:T(8,128)(2,1)} %get-tuple-element.26), channel_id=1, source_target_pairs={{0,24},{2,26},{4,28},{6,30},{8,16},{10,18},{12,20},{14,22},{16,8},... | collective-permute-start | bytes 196616 | tf_op jit(solution)/shard_map/ppermute | solution.py:238
  10.0 8.3 %collective-permute-start = (bf16[128,256]{1,0:T(8,128)(2,1)}, bf16[128,256]{1,0:T(8,128)(2,1)S(1)}, u32[]{:S(2)}, u32[]{:S(2)}) collective-permute-start(bf16[128,256]{1,0:T(8,128)(2,1)} %get-tuple-element.24), channel_id=1, source_target_pairs={{0,8},{2,10},{4,12},{6,14},{8,0},{10,2},{12,4},{14,6},{16,24},{18,... | collective-permute-start | bytes 196616 | tf_op jit(solution)/shard_map/ppermute | solution.py:238
  10.9 9.6 %collective-permute-start.1 = (bf16[128,256]{1,0:T(8,128)(2,1)}, bf16[128,256]{1,0:T(8,128)(2,1)S(1)}, u32[]{:S(2)}, u32[]{:S(2)}) collective-permute-start(bf16[128,256]{1,0:T(8,128)(2,1)} %get-tuple-element.24), channel_id=1, source_target_pairs={{0,16},{2,18},{4,20},{6,22},{8,24},{10,26},{12,28},{14,30},{16,0},... | collective-permute-start | bytes 196616 | tf_op jit(solution)/shard_map/ppermute | solution.py:238
  16.0 6.3 %collective-permute-start.2 = (bf16[128,256]{1,0:T(8,128)(2,1)}, bf16[128,256]{1,0:T(8,128)(2,1)S(1)}, u32[]{:S(2)}, u32[]{:S(2)}) collective-permute-start(bf16[128,256]{1,0:T(8,128)(2,1)} %get-tuple-element.24), channel_id=1, source_target_pairs={{0,24},{2,26},{4,28},{6,30},{8,16},{10,18},{12,20},{14,22},{16,8},... | collective-permute-start | bytes 196616 | tf_op jit(solution)/shard_map/ppermute | solution.py:238
  16.8 13.0 %collective-permute-start.10 = (bf16[512,256]{1,0:T(8,128)(2,1)S(1)}, bf16[512,256]{1,0:T(8,128)(2,1)S(1)}, u32[]{:S(2)}, u32[]{:S(2)}) collective-permute-start(bf16[512,256]{1,0:T(8,128)(2,1)S(1)} %constant_dynamic-update-slice_fusion.4.rest_0_), channel_id=1, source_target_pairs={{0,4},{2,6},{4,0},{6,2},{8,12},{10,14},{12,8},{14,10},{16,20},{18,... | collective-permute-start | bytes 786440 | tf_op jit(solution)/shard_map/ppermute | solution.py:238
  22.4 8.7 %collective-permute-start.3 = (bf16[512,256]{1,0:T(8,128)(2,1)S(1)}, bf16[512,256]{1,0:T(8,128)(2,1)S(1)}, u32[]{:S(2)}, u32[]{:S(2)}) collective-permute-start(bf16[512,256]{1,0:T(8,128)(2,1)S(1)} %constant_dynamic-update-slice_fusion.rest_0_), channel_id=1, source_target_pairs={{0,4},{2,6},{4,0},{6,2},{8,12},{10,14},{12,8},{14,10},{16,20},{18,... | collective-permute-start | bytes 786440 | tf_op jit(solution)/shard_map/ppermute | solution.py:238
  24.8 2.5 %copy-start.2 = (s32[1,1,80,128,128]{4,3,2,1,0:T(8,128)S(1)}, s32[1,1,80,128,128]{4,3,2,1,0:T(8,128)}, u32[]{:S(2)}) copy-start(s32[1,1,80,128,128]{4,3,2,1,0:T(8,128)} %param.16) | copy-start | bytes 15728644
  29.6 1.9 %collective-permute-start.11 = (bf16[512,256]{1,0:T(8,128)(2,1)S(1)}, bf16[512,256]{1,0:T(8,128)(2,1)S(1)}, u32[]{:S(2)}, u32[]{:S(2)}) collective-permute-start(bf16[512,256]{1,0:T(8,128)(2,1)S(1)} %constant_dynamic-update-slice_fusion.4.rest_0_), channel_id=1, source_target_pairs={{0,2},{2,0},{4,6},{6,4},{8,10},{10,8},{12,14},{14,12},{16,18},{18,... | collective-permute-start | bytes 786440 | tf_op jit(solution)/shard_map/ppermute | solution.py:238
  29.7 1.9 %collective-permute-start.12 = (bf16[512,256]{1,0:T(8,128)(2,1)S(1)}, bf16[512,256]{1,0:T(8,128)(2,1)S(1)}, u32[]{:S(2)}, u32[]{:S(2)}) collective-permute-start(bf16[512,256]{1,0:T(8,128)(2,1)S(1)} %collective-permute-done.10.rest_1_), channel_id=1, source_target_pairs={{0,2},{2,0},{4,6},{6,4},{8,10},{10,8},{12,14},{14,12},{16,18},{18,... | collective-permute-start | bytes 786440 | tf_op jit(solution)/shard_map/ppermute | solution.py:238
  31.0 5.4 %collective-permute-start.4 = (bf16[512,256]{1,0:T(8,128)(2,1)S(1)}, bf16[512,256]{1,0:T(8,128)(2,1)S(1)}, u32[]{:S(2)}, u32[]{:S(2)}) collective-permute-start(bf16[512,256]{1,0:T(8,128)(2,1)S(1)} %constant_dynamic-update-slice_fusion.rest_0_), channel_id=1, source_target_pairs={{0,2},{2,0},{4,6},{6,4},{8,10},{10,8},{12,14},{14,12},{16,18},{18,... | collective-permute-start | bytes 786440 | tf_op jit(solution)/shard_map/ppermute | solution.py:238
  31.1 5.3 %collective-permute-start.5 = (bf16[512,256]{1,0:T(8,128)(2,1)S(1)}, bf16[512,256]{1,0:T(8,128)(2,1)S(1)}, u32[]{:S(2)}, u32[]{:S(2)}) collective-permute-start(bf16[512,256]{1,0:T(8,128)(2,1)S(1)} %collective-permute-done.3.rest_1_), channel_id=1, source_target_pairs={{0,2},{2,0},{4,6},{6,4},{8,10},{10,8},{12,14},{14,12},{16,18},{18,... | collective-permute-start | bytes 786440 | tf_op jit(solution)/shard_map/ppermute | solution.py:238
  35.0 12.5 %collective-permute-start.19 = (bf16[512,256]{1,0:T(8,128)(2,1)S(1)}, bf16[512,256]{1,0:T(8,128)(2,1)S(1)}, u32[]{:S(2)}, u32[]{:S(2)}) collective-permute-start(bf16[512,256]{1,0:T(8,128)(2,1)S(1)} %get-tuple-element.36.rest_2_), channel_id=1, source_target_pairs={{0,1},{1,0},{2,3},{3,2},{4,5},{5,4},{6,7},{7,6},{8,9},{9,8},{10,11... | collective-permute-start | bytes 786440 | tf_op jit(solution)/shard_map/ppermute | solution.py:311
  39.8 10.0 %collective-permute-start.18 = (bf16[512,256]{1,0:T(8,128)(2,1)S(1)}, bf16[512,256]{1,0:T(8,128)(2,1)S(1)}, u32[]{:S(2)}, u32[]{:S(2)}) collective-permute-start(bf16[512,256]{1,0:T(8,128)(2,1)S(1)} %get-tuple-element.35.rest_0_), channel_id=1, source_target_pairs={{0,1},{1,0},{2,3},{3,2},{4,5},{5,4},{6,7},{7,6},{8,9},{9,8},{10,11... | collective-permute-start | bytes 786440 | tf_op jit(solution)/shard_map/ppermute | solution.py:311
  42.4 8.8 %copy-start = (bf16[2048,512]{1,0:T(8,128)(2,1)S(1)}, bf16[2048,512]{1,0:T(8,128)(2,1)}, u32[]{:S(2)}) copy-start(bf16[2048,512]{1,0:T(8,128)(2,1)} %user_ref.7) | copy-start | bytes 6291460
  42.4 8.8 %copy-start.1 = (bf16[2048,512]{1,0:T(8,128)(2,1)S(1)}, bf16[2048,512]{1,0:T(8,128)(2,1)}, u32[]{:S(2)}) copy-start(bf16[2048,512]{1,0:T(8,128)(2,1)} %grad_ref.7) | copy-start | bytes 6291460
  42.4 8.8 %copy-start.3 = (f32[512]{0:T(512)S(1)}, f32[512]{0:T(512)}, u32[]{:S(2)}) copy-start(f32[512]{0:T(512)} %param.11) | copy-start | bytes 6148
  42.4 13.1 %collective-permute-start.13 = (bf16[512,256]{1,0:T(8,128)(2,1)S(1)}, bf16[512,256]{1,0:T(8,128)(2,1)S(1)}, u32[]{:S(2)}, u32[]{:S(2)}) collective-permute-start(bf16[512,256]{1,0:T(8,128)(2,1)S(1)} %get-tuple-element.27.rest_2_), channel_id=1, source_target_pairs={{0,1},{1,0},{2,3},{3,2},{4,5},{5,4},{6,7},{7,6},{8,9},{9,8},{10,11... | collective-permute-start | bytes 786440 | tf_op jit(solution)/shard_map/ppermute | solution.py:311
  45.5 15.6 %collective-permute-start.6 = (bf16[512,256]{1,0:T(8,128)(2,1)S(1)}, bf16[512,256]{1,0:T(8,128)(2,1)S(1)}, u32[]{:S(2)}, u32[]{:S(2)}) collective-permute-start(bf16[512,256]{1,0:T(8,128)(2,1)S(1)} %get-tuple-element.25.rest_0_), channel_id=1, source_target_pairs={{0,1},{1,0},{2,3},{3,2},{4,5},{5,4},{6,7},{7,6},{8,9},{9,8},{10,11... | collective-permute-start | bytes 786440 | tf_op jit(solution)/shard_map/ppermute | solution.py:311
  46.3 20.5 %collective-permute-start.17 = (bf16[512,256]{1,0:T(8,128)(2,1)S(1)}, bf16[512,256]{1,0:T(8,128)(2,1)S(1)}, u32[]{:S(2)}, u32[]{:S(2)}) collective-permute-start(bf16[512,256]{1,0:T(8,128)(2,1)S(1)} %get-tuple-element.33.rest_2_), channel_id=1, source_target_pairs={{0,1},{1,0},{2,3},{3,2},{4,5},{5,4},{6,7},{7,6},{8,9},{9,8},{10,11... | collective-permute-start | bytes 786440 | tf_op jit(solution)/shard_map/ppermute | solution.py:311
  47.6 24.8 %collective-permute-start.16 = (bf16[512,256]{1,0:T(8,128)(2,1)S(1)}, bf16[512,256]{1,0:T(8,128)(2,1)S(1)}, u32[]{:S(2)}, u32[]{:S(2)}) collective-permute-start(bf16[512,256]{1,0:T(8,128)(2,1)S(1)} %get-tuple-element.32.rest_0_), channel_id=1, source_target_pairs={{0,1},{1,0},{2,3},{3,2},{4,5},{5,4},{6,7},{7,6},{8,9},{9,8},{10,11... | collective-permute-start | bytes 786440 | tf_op jit(solution)/shard_map/ppermute | solution.py:311
  49.9 28.1 %collective-permute-start.15 = (bf16[512,256]{1,0:T(8,128)(2,1)S(1)}, bf16[512,256]{1,0:T(8,128)(2,1)S(1)}, u32[]{:S(2)}, u32[]{:S(2)}) collective-permute-start(bf16[512,256]{1,0:T(8,128)(2,1)S(1)} %get-tuple-element.30.rest_2_), channel_id=1, source_target_pairs={{0,1},{1,0},{2,3},{3,2},{4,5},{5,4},{6,7},{7,6},{8,9},{9,8},{10,11... | collective-permute-start | bytes 786440 | tf_op jit(solution)/shard_map/ppermute | solution.py:311
  55.5 27.3 %collective-permute-start.14 = (bf16[512,256]{1,0:T(8,128)(2,1)S(1)}, bf16[512,256]{1,0:T(8,128)(2,1)S(1)}, u32[]{:S(2)}, u32[]{:S(2)}) collective-permute-start(bf16[512,256]{1,0:T(8,128)(2,1)S(1)} %get-tuple-element.29.rest_0_), channel_id=1, source_target_pairs={{0,1},{1,0},{2,3},{3,2},{4,5},{5,4},{6,7},{7,6},{8,9},{9,8},{10,11... | collective-permute-start | bytes 786440 | tf_op jit(solution)/shard_map/ppermute | solution.py:311
  84.5 1.7 %copy-start.6 = (f32[2048,256]{1,0:T(8,128)}, f32[2048,256]{1,0:T(8,128)S(1)}, u32[]{:S(2)}) copy-start(f32[2048,256]{1,0:T(8,128)S(1)} %slice_add_fusion.1) | copy-start | bytes 6291460
  85.4 3.0 %collective-permute-start.20 = (bf16[2,2,2,128,256]{4,3,0,2,1:T(8,128)(2,1)}, bf16[2,2,2,128,256]{4,3,0,2,1:T(8,128)(2,1)}, u32[]{:S(2)}, u32[]{:S(2)}) collective-permute-start(bf16[2,2,2,128,256]{4,3,0,2,1:T(8,128)(2,1)} %fusion.23), channel_id=1, source_target_pairs={{0,2},{2,0},{4,6},{6,4},{8,10},{10,8},{12,14},{14,12},{16,18},{18,... | collective-permute-start | bytes 1572872 | tf_op jit(solution)/shard_map/ppermute | solution.py:238
  87.1 3.0 %collective-permute-start.26 = (bf16[2,2,2,128,256]{4,3,0,1,2:T(8,128)(2,1)}, bf16[2,2,2,128,256]{4,3,0,1,2:T(8,128)(2,1)}, u32[]{:S(2)}, u32[]{:S(2)}) collective-permute-start(bf16[2,2,2,128,256]{4,3,0,1,2:T(8,128)(2,1)} %fusion.24), channel_id=1, source_target_pairs={{0,2},{2,0},{4,6},{6,4},{8,10},{10,8},{12,14},{14,12},{16,18},{18,... | collective-permute-start | bytes 1572872 | tf_op jit(solution)/shard_map/ppermute | solution.py:238
  90.0 8.3 %collective-permute-start.21 = (bf16[2,2,128,256]{3,2,0,1:T(8,128)(2,1)S(1)}, bf16[2,2,128,256]{3,2,0,1:T(8,128)(2,1)S(1)}, u32[]{:S(2)}, u32[]{:S(2)}) collective-permute-start(bf16[2,2,128,256]{3,2,0,1:T(8,128)(2,1)S(1)} %fusion.34), channel_id=1, source_target_pairs={{0,8},{2,10},{4,12},{6,14},{8,0},{10,2},{12,4},{14,6},{16,24},{18,... | collective-permute-start | bytes 786440 | tf_op jit(solution)/shard_map/ppermute | solution.py:238
  91.3 8.3 %collective-permute-start.27 = (bf16[2,2,128,256]{3,2,0,1:T(8,128)(2,1)S(1)}, bf16[2,2,128,256]{3,2,0,1:T(8,128)(2,1)S(1)}, u32[]{:S(2)}, u32[]{:S(2)}) collective-permute-start(bf16[2,2,128,256]{3,2,0,1:T(8,128)(2,1)S(1)} %fusion.36), channel_id=1, source_target_pairs={{0,4},{2,6},{4,0},{6,2},{8,12},{10,14},{12,8},{14,10},{16,20},{18,... | collective-permute-start | bytes 786440 | tf_op jit(solution)/shard_map/ppermute | solution.py:238
  98.3 11.8 %copy-start.7 = (bf16[128,16,4,32]{0,3,2,1:T(8,128)(2,1)S(1)}, bf16[128,16,4,32]{0,3,2,1:T(8,128)(2,1)}, u32[]{:S(2)}) copy-start(bf16[128,16,4,32]{0,3,2,1:T(8,128)(2,1)} %broadcast_select_fusion) | copy-start | bytes 1572868
  98.4 5.0 %collective-permute-start.22 = (bf16[2,128,256]{2,1,0:T(8,128)(2,1)S(1)}, bf16[2,128,256]{2,1,0:T(8,128)(2,1)S(1)}, u32[]{:S(2)}, u32[]{:S(2)}) collective-permute-start(bf16[2,128,256]{2,1,0:T(8,128)(2,1)S(1)} %fusion.40), channel_id=1, source_target_pairs={{0,4},{2,6},{4,0},{6,2},{8,12},{10,14},{12,8},{14,10},{16,20},{18,... | collective-permute-start | bytes 393224 | tf_op jit(solution)/shard_map/ppermute | solution.py:238
  99.7 5.8 %collective-permute-start.28 = (bf16[2,128,256]{2,1,0:T(8,128)(2,1)S(1)}, bf16[2,128,256]{2,1,0:T(8,128)(2,1)S(1)}, u32[]{:S(2)}, u32[]{:S(2)}) collective-permute-start(bf16[2,128,256]{2,1,0:T(8,128)(2,1)S(1)} %fusion.41), channel_id=1, source_target_pairs={{0,8},{2,10},{4,12},{6,14},{8,0},{10,2},{12,4},{14,6},{16,24},{18,... | collective-permute-start | bytes 393224 | tf_op jit(solution)/shard_map/ppermute | solution.py:238
  103.5 6.6 %collective-permute-start.23 = (bf16[128,256]{1,0:T(8,128)(2,1)S(1)}, bf16[128,256]{1,0:T(8,128)(2,1)S(1)}, u32[]{:S(2)}, u32[]{:S(2)}) collective-permute-start(bf16[128,256]{1,0:T(8,128)(2,1)S(1)} %fusion.46), channel_id=1, source_target_pairs={{0,16},{2,18},{4,20},{6,22},{8,24},{10,26},{12,28},{14,30},{16,0},... | collective-permute-start | bytes 196616 | tf_op jit(solution)/shard_map/ppermute | solution.py:238
  105.5 5.3 %collective-permute-start.29 = (bf16[128,256]{1,0:T(8,128)(2,1)S(1)}, bf16[128,256]{1,0:T(8,128)(2,1)S(1)}, u32[]{:S(2)}, u32[]{:S(2)}) collective-permute-start(bf16[128,256]{1,0:T(8,128)(2,1)S(1)} %fusion.47), channel_id=1, source_target_pairs={{0,16},{2,18},{4,20},{6,22},{8,24},{10,26},{12,28},{14,30},{16,0},... | collective-permute-start | bytes 196616 | tf_op jit(solution)/shard_map/ppermute | solution.py:238
  110.6 2.6 %collective-permute-start.24 = (bf16[2,2,2,128,256]{4,3,2,1,0:T(8,128)(2,1)S(1)}, bf16[2,2,2,128,256]{4,3,2,1,0:T(8,128)(2,1)S(1)}, u32[]{:S(2)}, u32[]{:S(2)}) collective-permute-start(bf16[2,2,2,128,256]{4,3,2,1,0:T(8,128)(2,1)S(1)} %fusion.22), channel_id=1, source_target_pairs={{0,2},{2,0},{4,6},{6,4},{8,10},{10,8},{12,14},{14,12},{16,18},{18,... | collective-permute-start | bytes 1572872 | tf_op jit(solution)/shard_map/ppermute | solution.py:238
  111.2 1.0 copy-start.8
  111.5 4.0 %collective-permute-start.30 = (bf16[2,2,2,136,256]{4,3,0,1,2:T(8,128)(2,1)S(1)}, bf16[2,2,2,136,256]{4,3,0,1,2:T(8,128)(2,1)S(1)}, u32[]{:S(2)}, u32[]{:S(2)}) collective-permute-start(bf16[2,2,2,136,256]{4,3,0,1,2:T(8,128)(2,1)S(1)} %fusion.21), channel_id=1, source_target_pairs={{0,2},{2,0},{4,6},{6,4},{8,10},{10,8},{12,14},{14,12},{16,18},{18,... | collective-permute-start | bytes 1671176 | tf_op jit(solution)/shard_map/ppermute | solution.py:238
  113.4 10.0 %copy-start.5 = (bf16[4,512,512]{2,1,0:T(8,128)(2,1)S(1)}, bf16[4,512,512]{2,1,0:T(8,128)(2,1)}, u32[]{:S(2)}) copy-start(bf16[4,512,512]{2,1,0:T(8,128)(2,1)} %weight_ref.1) | copy-start | bytes 6291460
  113.4 8.7 %collective-permute-start.25 = (bf16[2,2,128,256]{3,2,1,0:T(8,128)(2,1)S(1)}, bf16[2,2,128,256]{3,2,1,0:T(8,128)(2,1)S(1)}, u32[]{:S(2)}, u32[]{:S(2)}) collective-permute-start(bf16[2,2,128,256]{3,2,1,0:T(8,128)(2,1)S(1)} %fusion.35), channel_id=1, source_target_pairs={{0,8},{2,10},{4,12},{6,14},{8,0},{10,2},{12,4},{14,6},{16,24},{18,... | collective-permute-start | bytes 786440 | tf_op jit(solution)/shard_map/ppermute | solution.py:238
  115.7 9.5 %collective-permute-start.31 = (bf16[2,2,136,256]{3,2,0,1:T(8,128)(2,1)S(1)}, bf16[2,2,136,256]{3,2,0,1:T(8,128)(2,1)S(1)}, u32[]{:S(2)}, u32[]{:S(2)}) collective-permute-start(bf16[2,2,136,256]{3,2,0,1:T(8,128)(2,1)S(1)} %fusion.33), channel_id=1, source_target_pairs={{0,4},{2,6},{4,0},{6,2},{8,12},{10,14},{12,8},{14,10},{16,20},{18,... | collective-permute-start | bytes 835592 | tf_op jit(solution)/shard_map/ppermute | solution.py:238
  122.2 5.0 %collective-permute-start.34 = (bf16[2,128,256]{2,1,0:T(8,128)(2,1)S(1)}, bf16[2,128,256]{2,1,0:T(8,128)(2,1)S(1)}, u32[]{:S(2)}, u32[]{:S(2)}) collective-permute-start(bf16[2,128,256]{2,1,0:T(8,128)(2,1)S(1)} %fusion.42), channel_id=1, source_target_pairs={{0,4},{2,6},{4,0},{6,2},{8,12},{10,14},{12,8},{14,10},{16,20},{18,... | collective-permute-start | bytes 393224 | tf_op jit(solution)/shard_map/ppermute | solution.py:238
  125.4 5.8 %collective-permute-start.32 = (bf16[2,136,256]{2,1,0:T(8,128)(2,1)S(1)}, bf16[2,136,256]{2,1,0:T(8,128)(2,1)S(1)}, u32[]{:S(2)}, u32[]{:S(2)}) collective-permute-start(bf16[2,136,256]{2,1,0:T(8,128)(2,1)S(1)} %fusion.39), channel_id=1, source_target_pairs={{0,8},{2,10},{4,12},{6,14},{8,0},{10,2},{12,4},{14,6},{16,24},{18,... | collective-permute-start | bytes 417800 | tf_op jit(solution)/shard_map/ppermute | solution.py:238
  127.3 7.4 %collective-permute-start.35 = (bf16[128,256]{1,0:T(8,128)(2,1)S(1)}, bf16[128,256]{1,0:T(8,128)(2,1)S(1)}, u32[]{:S(2)}, u32[]{:S(2)}) collective-permute-start(bf16[128,256]{1,0:T(8,128)(2,1)S(1)} %fusion.48), channel_id=1, source_target_pairs={{0,16},{2,18},{4,20},{6,22},{8,24},{10,26},{12,28},{14,30},{16,0},... | collective-permute-start | bytes 196616 | tf_op jit(solution)/shard_map/ppermute | solution.py:238
  131.3 5.3 %collective-permute-start.33 = (bf16[136,256]{1,0:T(8,128)(2,1)S(1)}, bf16[136,256]{1,0:T(8,128)(2,1)S(1)}, u32[]{:S(2)}, u32[]{:S(2)}) collective-permute-start(bf16[136,256]{1,0:T(8,128)(2,1)S(1)} %fusion.45), channel_id=1, source_target_pairs={{0,16},{2,18},{4,20},{6,22},{8,24},{10,26},{12,28},{14,30},{16,0},... | collective-permute-start | bytes 208904 | tf_op jit(solution)/shard_map/ppermute | solution.py:238

commit v12 on v11

--- a/solution.py
+++ b/solution.py
@@ -302,7 +302,7 @@
 
     partials = [[] for _ in range(HALVES)]
     for half in range(HALVES):
-        for first, count in ((0, 1), (1, ROW_CHUNKS - 1)):
+        for first, count in ((0, ROW_CHUNKS - 1), (ROW_CHUNKS - 1, 1)):
             *products, _ = spread_items(order, queries[half], dense, first, (1,) * count, rows)
             for product in products:
                 pieces = [product]

time: 139 us -> 140 us (level)
  starting transfers between devices: 42.7 us -> 45.8 us
    ppermute x28, starting transfers between devices: 33.8 us -> 36.3 us  [flip(): lax.ppermute(value, 'user', [(source, source ^ bits) for source in range(...]
    ppermute x8, waiting for transfers between devices: 25.7 us -> 23.6 us  [on_device(): pieces.append(lax.ppermute(product, 'item', pairs))]
    ppermute x28, waiting for transfers between devices: 25.5 us -> 27 us  [flip(): lax.ppermute(value, 'user', [(source, source ^ bits) for source in range(...]
  transfers between devices with their start and end apart: 36 -> 36, of which waited for: 19 -> 18; matrix products, arithmetic and copies ran while one was open for 12% -> 12% of each run, Pallas kernels for 11% -> 10%
where the time goes in v12:
time: 140 us
  waiting for transfers between devices  50.5 us (36%)
  starting transfers between devices  45.8 us (33%)
  Pallas kernels  19.1 us (14%)
  local copies, waits for them, and re-layouts  8.5 us (6%)
  matrix products  8.18 us (6%)
  other arithmetic  6.21 us (4%)
  between operations  1.91 us (1%)
    ppermute x28, starting transfers between devices, flip(): lax.ppermute(value, 'user', [(source, source ^ bits) for source in range(...  36.3 us
    ppermute x28, waiting for transfers between devices, flip(): lax.ppermute(value, 'user', [(source, source ^ bits) for source in range(...  27 us
    ppermute x8, waiting for transfers between devices, on_device(): pieces.append(lax.ppermute(product, 'item', pairs))  23.6 us
    pallas_call x4, Pallas kernels, spread_items(): pl.pallas_call(functools.partial(spread, blocks), out_shape=[jax.ShapeDty...  10.3 us
    ppermute x8, starting transfers between devices, on_device(): pieces.append(lax.ppermute(product, 'item', pairs))  9.43 us
    unnamed x29, local copies, waits for them, and re-layouts  4.92 us
    dot_general x3, matrix products, on_device(): lax.dot_general(dense[chunk * rows:(chunk + 1) * rows], grad, (((0,), (0,...  3.91 us
    pallas_call x1, Pallas kernels, own_queries(): pl.pallas_call(project_own, out_shape=[half] * HALVES, grid_spec=pltpu.Pr...  3.68 us
  transfers between devices with their start and end apart: 36, of which 18 were waited for; matrix products, arithmetic and copies ran while one was open for 12% of the time, Pallas kernels for 10%

profile of v12, /device:TPU:0, one launch (start us, length us, event | category | flops | bytes accessed | tf_op | source)
XLA Modules:
  0.0 140.2 jit_solution(15777752110107174233)
XLA Ops:
  0.7 3.7 %own_queries.1 = (bf16[128,256]{1,0:T(8,128)(2,1)}, bf16[128,256]{1,0:T(8,128)(2,1)}) custom-call(s32[1]{0:T(128)} %bitcast.1.first_ref, s32[1,128]{1,0:T(1,128)} %cats_ref.1, bf16[128,512]{1,0:T(8,128)(2,1)} %bitcast.143, bf16[4,512,512]{2,1,0:T(8,128)(2,1)} %weight_ref.1), custom_call_target="tpu_custom_call" | custom-call | flops 268435456 | bytes 2359296 | tf_op jit(solution)/shard_map/own_queries/pallas_call | solution.py:97
  4.3 3.0 %collective-permute-start.7 = (bf16[128,256]{1,0:T(8,128)(2,1)}, bf16[128,256]{1,0:T(8,128)(2,1)S(1)}, u32[]{:S(2)}, u32[]{:S(2)}) collective-permute-start(bf16[128,256]{1,0:T(8,128)(2,1)} %get-tuple-element.26), channel_id=1, source_target_pairs={{0,8},{2,10},{4,12},{6,14},{8,0},{10,2},{12,4},{14,6},{16,24},{18,... | collective-permute-start | bytes 196616 | tf_op jit(solution)/shard_map/ppermute | solution.py:238
  7.4 2.6 %collective-permute-start.8 = (bf16[128,256]{1,0:T(8,128)(2,1)}, bf16[128,256]{1,0:T(8,128)(2,1)S(1)}, u32[]{:S(2)}, u32[]{:S(2)}) collective-permute-start(bf16[128,256]{1,0:T(8,128)(2,1)} %get-tuple-element.26), channel_id=1, source_target_pairs={{0,16},{2,18},{4,20},{6,22},{8,24},{10,26},{12,28},{14,30},{16,0},... | collective-permute-start | bytes 196616 | tf_op jit(solution)/shard_map/ppermute | solution.py:238
  10.9 3.5 %collective-permute-start.1 = (bf16[128,256]{1,0:T(8,128)(2,1)}, bf16[128,256]{1,0:T(8,128)(2,1)S(1)}, u32[]{:S(2)}, u32[]{:S(2)}) collective-permute-start(bf16[128,256]{1,0:T(8,128)(2,1)} %get-tuple-element.24), channel_id=1, source_target_pairs={{0,16},{2,18},{4,20},{6,22},{8,24},{10,26},{12,28},{14,30},{16,0},... | collective-permute-start | bytes 196616 | tf_op jit(solution)/shard_map/ppermute | solution.py:238
  16.8 1.5 %collective-permute-start.10 = (bf16[512,256]{1,0:T(8,128)(2,1)S(1)}, bf16[512,256]{1,0:T(8,128)(2,1)S(1)}, u32[]{:S(2)}, u32[]{:S(2)}) collective-permute-start(bf16[512,256]{1,0:T(8,128)(2,1)S(1)} %constant_dynamic-update-slice_fusion.4.rest_0_), channel_id=1, source_target_pairs={{0,4},{2,6},{4,0},{6,2},{8,12},{10,14},{12,8},{14,10},{16,20},{18,... | collective-permute-start | bytes 786440 | tf_op jit(solution)/shard_map/ppermute | solution.py:238
  18.3 2.2 %collective-permute-done.1 = bf16[128,256]{1,0:T(8,128)(2,1)S(1)} collective-permute-done((bf16[128,256]{1,0:T(8,128)(2,1)}, bf16[128,256]{1,0:T(8,128)(2,1)S(1)}, u32[]{:S(2)}, u32[]{:S(2)}) %collective-permute-start.1) | collective-permute-done | bytes 65568 | tf_op jit(solution)/shard_map/ppermute | solution.py:238
  20.5 2.1 %collective-permute-done.2 = bf16[128,256]{1,0:T(8,128)(2,1)S(1)} collective-permute-done((bf16[128,256]{1,0:T(8,128)(2,1)}, bf16[128,256]{1,0:T(8,128)(2,1)S(1)}, u32[]{:S(2)}, u32[]{:S(2)}) %collective-permute-start.2) | collective-permute-done | bytes 65568 | tf_op jit(solution)/shard_map/ppermute | solution.py:238
  22.5 1.5 %collective-permute-start.3 = (bf16[512,256]{1,0:T(8,128)(2,1)S(1)}, bf16[512,256]{1,0:T(8,128)(2,1)S(1)}, u32[]{:S(2)}, u32[]{:S(2)}) collective-permute-start(bf16[512,256]{1,0:T(8,128)(2,1)S(1)} %constant_dynamic-update-slice_fusion.rest_0_), channel_id=1, source_target_pairs={{0,4},{2,6},{4,0},{6,2},{8,12},{10,14},{12,8},{14,10},{16,20},{18,... | collective-permute-start | bytes 786440 | tf_op jit(solution)/shard_map/ppermute | solution.py:238
  26.1 2.5 %copy-done.2 = s32[1,1,80,128,128]{4,3,2,1,0:T(8,128)S(1)} copy-done((s32[1,1,80,128,128]{4,3,2,1,0:T(8,128)S(1)}, s32[1,1,80,128,128]{4,3,2,1,0:T(8,128)}, u32[]{:S(2)}) %copy-start.2) | copy-done | bytes 5242904
  28.6 2.2 %place_tiles.1.rest_4_ = bf16[2048,2048]{1,0:T(8,128)(2,1)S(1)} custom-call(s32[80]{0:T(128)S(1)} %bitcast.134, s32[1]{0:T(128)} %bitcast.128.count_ref, s32[80,128,128]{2,1,0:T(8,128)S(1)} %bitcast.129), custom_call_target="tpu_custom_call" | custom-call | flops 1310720 | bytes 13631488 | tf_op jit(solution)/shard_map/place_tiles/pallas_call | solution.py:40
  31.4 1.7 %spread_items.7 = (bf16[512,256]{1,0:T(8,128)(2,1)S(1)}, s32[16]{0:T(128)}) custom-call(s32[16]{0:T(128)S(1)} %fusion.59.order_ref, bf16[512,256]{1,0:T(8,128)(2,1)S(1)} %constant_dynamic-update-slice_fusion.4.rest_0_, bf16[512,256]{1,0:T(8,128)(2,1)S(1)} %collective-permute-done.10.rest_1_, bf16[512,256]{1,0:T(8,128)(2,1)S(1)} %collective-permute-done.11.rest_2_, ...), custom_call_target="tpu_custom_call" | custom-call | flops 536870912 | bytes 3407872 | tf_op jit(solution)/shard_map/spread_items/pallas_call | solution.py:153
  33.1 1.6 %collective-permute-start.19 = (bf16[512,256]{1,0:T(8,128)(2,1)S(1)}, bf16[512,256]{1,0:T(8,128)(2,1)S(1)}, u32[]{:S(2)}, u32[]{:S(2)}) collective-permute-start(bf16[512,256]{1,0:T(8,128)(2,1)S(1)} %get-tuple-element.36.rest_2_), channel_id=1, source_target_pairs={{0,1},{1,0},{2,3},{3,2},{4,5},{5,4},{6,7},{7,6},{8,9},{9,8},{10,11... | collective-permute-start | bytes 786440 | tf_op jit(solution)/shard_map/ppermute | solution.py:311
  34.7 1.7 %spread_items.6 = (bf16[512,256]{1,0:T(8,128)(2,1)S(1)}, s32[16]{0:T(128)}) custom-call(s32[16]{0:T(128)S(1)} %fusion.59.order_ref, bf16[512,256]{1,0:T(8,128)(2,1)S(1)} %constant_dynamic-update-slice_fusion.rest_0_, bf16[512,256]{1,0:T(8,128)(2,1)S(1)} %collective-permute-done.3.rest_1_, bf16[512,256]{1,0:T(8,128)(2,1)S(1)} %collective-permute-done.4.rest_2_, ...), custom_call_target="tpu_custom_call" | custom-call | flops 536870912 | bytes 3407872 | tf_op jit(solution)/shard_map/spread_items/pallas_call | solution.py:153
  37.0 3.4 %spread_items.5 = (bf16[512,256]{1,0:T(8,128)(2,1)S(1)}, bf16[512,256]{1,0:T(8,128)(2,1)S(1)}, bf16[512,256]{1,0:T(8,128)(2,1)S(1)}, s32[16]{0:T(128)}) custom-call(s32[16]{0:T(128)S(1)} %fusion.59.order_ref, bf16[512,256]{1,0:T(8,128)(2,1)S(1)} %constant_dynamic-update-slice_fusion.4.rest_0_, bf16[512,256]{1,0:T(8,128)(2,1)S(1)} %collective-permute-done.10.rest_1_, ...), custom_call_target="tpu_custom_call" | custom-call | flops 1610612736 | bytes 8126464 | tf_op jit(solution)/shard_map/spread_items/pallas_call | solution.py:153
  40.5 1.6 %collective-permute-start.13 = (bf16[512,256]{1,0:T(8,128)(2,1)S(1)}, bf16[512,256]{1,0:T(8,128)(2,1)S(1)}, u32[]{:S(2)}, u32[]{:S(2)}) collective-permute-start(bf16[512,256]{1,0:T(8,128)(2,1)S(1)} %get-tuple-element.27.rest_2_), channel_id=1, source_target_pairs={{0,1},{1,0},{2,3},{3,2},{4,5},{5,4},{6,7},{7,6},{8,9},{9,8},{10,11... | collective-permute-start | bytes 786440 | tf_op jit(solution)/shard_map/ppermute | solution.py:311
  42.1 3.4 %spread_items.4 = (bf16[512,256]{1,0:T(8,128)(2,1)S(1)}, bf16[512,256]{1,0:T(8,128)(2,1)S(1)}, bf16[512,256]{1,0:T(8,128)(2,1)S(1)}, s32[16]{0:T(128)}) custom-call(s32[16]{0:T(128)S(1)} %fusion.59.order_ref, bf16[512,256]{1,0:T(8,128)(2,1)S(1)} %constant_dynamic-update-slice_fusion.rest_0_, bf16[512,256]{1,0:T(8,128)(2,1)S(1)} %collective-permute-done.3.rest_1_, ...), custom_call_target="tpu_custom_call" | custom-call | flops 1610612736 | bytes 8126464 | tf_op jit(solution)/shard_map/spread_items/pallas_call | solution.py:153
  46.1 1.6 %collective-permute-start.17 = (bf16[512,256]{1,0:T(8,128)(2,1)S(1)}, bf16[512,256]{1,0:T(8,128)(2,1)S(1)}, u32[]{:S(2)}, u32[]{:S(2)}) collective-permute-start(bf16[512,256]{1,0:T(8,128)(2,1)S(1)} %get-tuple-element.33.rest_2_), channel_id=1, source_target_pairs={{0,1},{1,0},{2,3},{3,2},{4,5},{5,4},{6,7},{7,6},{8,9},{9,8},{10,11... | collective-permute-start | bytes 786440 | tf_op jit(solution)/shard_map/ppermute | solution.py:311
  48.1 1.6 %collective-permute-start.15 = (bf16[512,256]{1,0:T(8,128)(2,1)S(1)}, bf16[512,256]{1,0:T(8,128)(2,1)S(1)}, u32[]{:S(2)}, u32[]{:S(2)}) collective-permute-start(bf16[512,256]{1,0:T(8,128)(2,1)S(1)} %get-tuple-element.30.rest_2_), channel_id=1, source_target_pairs={{0,1},{1,0},{2,3},{3,2},{4,5},{5,4},{6,7},{7,6},{8,9},{9,8},{10,11... | collective-permute-start | bytes 786440 | tf_op jit(solution)/shard_map/ppermute | solution.py:311
  50.4 1.3 fusion.4
  51.7 1.9 %collective-permute-done.13.rest_3_ = bf16[512,256]{1,0:T(8,128)(2,1)S(1)} collective-permute-done((bf16[512,256]{1,0:T(8,128)(2,1)S(1)}, bf16[512,256]{1,0:T(8,128)(2,1)S(1)}, u32[]{:S(2)}, u32[]{:S(2)}) %collective-permute-start.13) | collective-permute-done | bytes 262176 | tf_op jit(solution)/shard_map/ppermute | solution.py:311
  53.6 1.5 %collective-permute-start.14 = (bf16[512,256]{1,0:T(8,128)(2,1)S(1)}, bf16[512,256]{1,0:T(8,128)(2,1)S(1)}, u32[]{:S(2)}, u32[]{:S(2)}) collective-permute-start(bf16[512,256]{1,0:T(8,128)(2,1)S(1)} %get-tuple-element.29.rest_0_), channel_id=1, source_target_pairs={{0,1},{1,0},{2,3},{3,2},{4,5},{5,4},{6,7},{7,6},{8,9},{9,8},{10,11... | collective-permute-start | bytes 786440 | tf_op jit(solution)/shard_map/ppermute | solution.py:311
  55.1 4.1 %collective-permute-done.6.rest_1_ = bf16[512,256]{1,0:T(8,128)(2,1)S(1)} collective-permute-done((bf16[512,256]{1,0:T(8,128)(2,1)S(1)}, bf16[512,256]{1,0:T(8,128)(2,1)S(1)}, u32[]{:S(2)}, u32[]{:S(2)}) %collective-permute-start.6) | collective-permute-done | bytes 262176 | tf_op jit(solution)/shard_map/ppermute | solution.py:311
  59.9 1.3 fusion.6
  61.2 3.6 %collective-permute-done.17.rest_3_ = bf16[512,256]{1,0:T(8,128)(2,1)S(1)} collective-permute-done((bf16[512,256]{1,0:T(8,128)(2,1)S(1)}, bf16[512,256]{1,0:T(8,128)(2,1)S(1)}, u32[]{:S(2)}, u32[]{:S(2)}) %collective-permute-start.17) | collective-permute-done | bytes 262176 | tf_op jit(solution)/shard_map/ppermute | solution.py:311
  64.8 5.6 %collective-permute-done.16.rest_1_ = bf16[512,256]{1,0:T(8,128)(2,1)S(1)} collective-permute-done((bf16[512,256]{1,0:T(8,128)(2,1)S(1)}, bf16[512,256]{1,0:T(8,128)(2,1)S(1)}, u32[]{:S(2)}, u32[]{:S(2)}) %collective-permute-start.16) | collective-permute-done | bytes 262176 | tf_op jit(solution)/shard_map/ppermute | solution.py:311
  71.1 1.3 add_add_fusion
  72.5 3.6 %collective-permute-done.15.rest_3_ = bf16[512,256]{1,0:T(8,128)(2,1)S(1)} collective-permute-done((bf16[512,256]{1,0:T(8,128)(2,1)S(1)}, bf16[512,256]{1,0:T(8,128)(2,1)S(1)}, u32[]{:S(2)}, u32[]{:S(2)}) %collective-permute-start.15) | collective-permute-done | bytes 262176 | tf_op jit(solution)/shard_map/ppermute | solution.py:311
  76.1 4.8 %collective-permute-done.14.rest_1_ = bf16[512,256]{1,0:T(8,128)(2,1)S(1)} collective-permute-done((bf16[512,256]{1,0:T(8,128)(2,1)S(1)}, bf16[512,256]{1,0:T(8,128)(2,1)S(1)}, u32[]{:S(2)}, u32[]{:S(2)}) %collective-permute-start.14) | collective-permute-done | bytes 262176 | tf_op jit(solution)/shard_map/ppermute | solution.py:311
  86.3 1.5 %bitcast_add_fusion.3 = f32[2,2,2,128,256]{4,3,0,2,1:T(8,128)S(1)} fusion(bf16[2,2,2,128,256]{4,3,0,2,1:T(8,128)(2,1)} %collective-permute-done.20, f32[2,2,2,2,128,256]{5,4,3,2,1,0:T(8,128)} %bitcast.140, s32[]{:T(128)S(6)} %select_n.111), kind=kLoop, calls=%fused_computation.30 | loop fusion | flops 524288 | bytes 2621444 | tf_op jit(solution)/shard_map/add | solution.py:270
  87.9 3.2 %collective-permute-start.21 = (bf16[2,2,128,256]{3,2,0,1:T(8,128)(2,1)S(1)}, bf16[2,2,128,256]{3,2,0,1:T(8,128)(2,1)S(1)}, u32[]{:S(2)}, u32[]{:S(2)}) collective-permute-start(bf16[2,2,128,256]{3,2,0,1:T(8,128)(2,1)S(1)} %fusion.34), channel_id=1, source_target_pairs={{0,8},{2,10},{4,12},{6,14},{8,0},{10,2},{12,4},{14,6},{16,24},{18,... | collective-permute-start | bytes 786440 | tf_op jit(solution)/shard_map/ppermute | solution.py:238
  91.1 1.2 bitcast_add_fusion.1
  92.4 1.5 %collective-permute-start.27 = (bf16[2,2,128,256]{3,2,0,1:T(8,128)(2,1)S(1)}, bf16[2,2,128,256]{3,2,0,1:T(8,128)(2,1)S(1)}, u32[]{:S(2)}, u32[]{:S(2)}) collective-permute-start(bf16[2,2,128,256]{3,2,0,1:T(8,128)(2,1)S(1)} %fusion.36), channel_id=1, source_target_pairs={{0,4},{2,6},{4,0},{6,2},{8,12},{10,14},{12,8},{14,10},{16,20},{18,... | collective-permute-start | bytes 786440 | tf_op jit(solution)/shard_map/ppermute | solution.py:238
  93.8 3.8 %collective-permute-done.21 = bf16[2,2,128,256]{3,2,0,1:T(8,128)(2,1)S(1)} collective-permute-done((bf16[2,2,128,256]{3,2,0,1:T(8,128)(2,1)S(1)}, bf16[2,2,128,256]{3,2,0,1:T(8,128)(2,1)S(1)}, u32[]{:S(2)}, u32[]{:S(2)}) %collective-permute-start.21) | collective-permute-done | bytes 262176 | tf_op jit(solution)/shard_map/ppermute | solution.py:238
  97.7 1.5 %collective-permute-start.22 = (bf16[2,128,256]{2,1,0:T(8,128)(2,1)S(1)}, bf16[2,128,256]{2,1,0:T(8,128)(2,1)S(1)}, u32[]{:S(2)}, u32[]{:S(2)}) collective-permute-start(bf16[2,128,256]{2,1,0:T(8,128)(2,1)S(1)} %fusion.40), channel_id=1, source_target_pairs={{0,4},{2,6},{4,0},{6,2},{8,12},{10,14},{12,8},{14,10},{16,20},{18,... | collective-permute-start | bytes 393224 | tf_op jit(solution)/shard_map/ppermute | solution.py:238
  99.2 1.6 %collective-permute-done.27 = bf16[2,2,128,256]{3,2,0,1:T(8,128)(2,1)S(1)} collective-permute-done((bf16[2,2,128,256]{3,2,0,1:T(8,128)(2,1)S(1)}, bf16[2,2,128,256]{3,2,0,1:T(8,128)(2,1)S(1)}, u32[]{:S(2)}, u32[]{:S(2)}) %collective-permute-start.27) | collective-permute-done | bytes 262176 | tf_op jit(solution)/shard_map/ppermute | solution.py:238
  101.1 2.1 %collective-permute-done.22 = bf16[2,128,256]{2,1,0:T(8,128)(2,1)S(1)} collective-permute-done((bf16[2,128,256]{2,1,0:T(8,128)(2,1)S(1)}, bf16[2,128,256]{2,1,0:T(8,128)(2,1)S(1)}, u32[]{:S(2)}, u32[]{:S(2)}) %collective-permute-start.22) | collective-permute-done | bytes 131104 | tf_op jit(solution)/shard_map/ppermute | solution.py:238
  103.2 3.5 %collective-permute-start.23 = (bf16[128,256]{1,0:T(8,128)(2,1)S(1)}, bf16[128,256]{1,0:T(8,128)(2,1)S(1)}, u32[]{:S(2)}, u32[]{:S(2)}) collective-permute-start(bf16[128,256]{1,0:T(8,128)(2,1)S(1)} %fusion.46), channel_id=1, source_target_pairs={{0,16},{2,18},{4,20},{6,22},{8,24},{10,26},{12,28},{14,30},{16,0},... | collective-permute-start | bytes 196616 | tf_op jit(solution)/shard_map/ppermute | solution.py:238
  106.8 2.8 %collective-permute-start.29 = (bf16[128,256]{1,0:T(8,128)(2,1)S(1)}, bf16[128,256]{1,0:T(8,128)(2,1)S(1)}, u32[]{:S(2)}, u32[]{:S(2)}) collective-permute-start(bf16[128,256]{1,0:T(8,128)(2,1)S(1)} %fusion.47), channel_id=1, source_target_pairs={{0,16},{2,18},{4,20},{6,22},{8,24},{10,26},{12,28},{14,30},{16,0},... | collective-permute-start | bytes 196616 | tf_op jit(solution)/shard_map/ppermute | solution.py:238
  109.5 1.7 %collective-permute-done.23 = bf16[128,256]{1,0:T(8,128)(2,1)S(1)} collective-permute-done((bf16[128,256]{1,0:T(8,128)(2,1)S(1)}, bf16[128,256]{1,0:T(8,128)(2,1)S(1)}, u32[]{:S(2)}, u32[]{:S(2)}) %collective-permute-start.23) | collective-permute-done | bytes 65568 | tf_op jit(solution)/shard_map/ppermute | solution.py:238
  114.1 1.0 pad_maximum_fusion.1
  115.9 1.8 %collective-permute-start.31 = (bf16[2,2,136,256]{3,2,0,1:T(8,128)(2,1)S(1)}, bf16[2,2,136,256]{3,2,0,1:T(8,128)(2,1)S(1)}, u32[]{:S(2)}, u32[]{:S(2)}) collective-permute-start(bf16[2,2,136,256]{3,2,0,1:T(8,128)(2,1)S(1)} %fusion.33), channel_id=1, source_target_pairs={{0,4},{2,6},{4,0},{6,2},{8,12},{10,14},{12,8},{14,10},{16,20},{18,... | collective-permute-start | bytes 835592 | tf_op jit(solution)/shard_map/ppermute | solution.py:238
  117.7 5.8 %collective-permute-done.25 = bf16[2,2,128,256]{3,2,1,0:T(8,128)(2,1)S(1)} collective-permute-done((bf16[2,2,128,256]{3,2,1,0:T(8,128)(2,1)S(1)}, bf16[2,2,128,256]{3,2,1,0:T(8,128)(2,1)S(1)}, u32[]{:S(2)}, u32[]{:S(2)}) %collective-permute-start.25) | collective-permute-done | bytes 262176 | tf_op jit(solution)/shard_map/ppermute | solution.py:238
  123.7 2.0 %collective-permute-start.34 = (bf16[2,128,256]{2,1,0:T(8,128)(2,1)S(1)}, bf16[2,128,256]{2,1,0:T(8,128)(2,1)S(1)}, u32[]{:S(2)}, u32[]{:S(2)}) collective-permute-start(bf16[2,128,256]{2,1,0:T(8,128)(2,1)S(1)} %fusion.42), channel_id=1, source_target_pairs={{0,4},{2,6},{4,0},{6,2},{8,12},{10,14},{12,8},{14,10},{16,20},{18,... | collective-permute-start | bytes 393224 | tf_op jit(solution)/shard_map/ppermute | solution.py:238
  126.6 1.0 fusion.20
  128.7 2.5 %collective-permute-start.35 = (bf16[128,256]{1,0:T(8,128)(2,1)S(1)}, bf16[128,256]{1,0:T(8,128)(2,1)S(1)}, u32[]{:S(2)}, u32[]{:S(2)}) collective-permute-start(bf16[128,256]{1,0:T(8,128)(2,1)S(1)} %fusion.48), channel_id=1, source_target_pairs={{0,16},{2,18},{4,20},{6,22},{8,24},{10,26},{12,28},{14,30},{16,0},... | collective-permute-start | bytes 196616 | tf_op jit(solution)/shard_map/ppermute | solution.py:238
  131.2 1.6 %collective-permute-done.32 = bf16[2,136,256]{2,1,0:T(8,128)(2,1)S(1)} collective-permute-done((bf16[2,136,256]{2,1,0:T(8,128)(2,1)S(1)}, bf16[2,136,256]{2,1,0:T(8,128)(2,1)S(1)}, u32[]{:S(2)}, u32[]{:S(2)}) %collective-permute-start.32) | collective-permute-done | bytes 139296 | tf_op jit(solution)/shard_map/ppermute | solution.py:238
  132.9 1.9 %collective-permute-start.33 = (bf16[136,256]{1,0:T(8,128)(2,1)S(1)}, bf16[136,256]{1,0:T(8,128)(2,1)S(1)}, u32[]{:S(2)}, u32[]{:S(2)}) collective-permute-start(bf16[136,256]{1,0:T(8,128)(2,1)S(1)} %fusion.45), channel_id=1, source_target_pairs={{0,16},{2,18},{4,20},{6,22},{8,24},{10,26},{12,28},{14,30},{16,0},... | collective-permute-start | bytes 208904 | tf_op jit(solution)/shard_map/ppermute | solution.py:238
  134.8 4.1 %collective-permute-done.33 = bf16[136,256]{1,0:T(8,128)(2,1)S(1)} collective-permute-done((bf16[136,256]{1,0:T(8,128)(2,1)S(1)}, bf16[136,256]{1,0:T(8,128)(2,1)S(1)}, u32[]{:S(2)}, u32[]{:S(2)}) %collective-permute-start.33) | collective-permute-done | bytes 69664 | tf_op jit(solution)/shard_map/ppermute | solution.py:238
  (125 shorter events, 22.0 us)
Async XLA Ops:
  0.6 14.6 %copy-start.9 = (bf16[1,128,512]{2,1,0:T(8,128)(2,1)S(1)}, bf16[1,128,512]{2,1,0:T(8,128)(2,1)}, u32[]{:S(2)}) copy-start(bf16[1,128,512]{2,1,0:T(8,128)(2,1)} %param.12) | copy-start | bytes 393220
  0.6 14.7 %copy-start.10 = (s32[1,128]{1,0:T(1,128)S(1)}, s32[1,128]{1,0:T(1,128)}, u32[]{:S(2)}) copy-start(s32[1,128]{1,0:T(1,128)} %cats_ref.1) | copy-start | bytes 1540
  0.7 25.4 %copy-start.4 = (s32[1,1,80]{2,1,0:T(1,128)S(1)}, s32[1,1,80]{2,1,0:T(1,128)}, u32[]{:S(2)}) copy-start(s32[1,1,80]{2,1,0:T(1,128)} %param.15) | copy-start | bytes 964
  4.3 11.9 %collective-permute-start.7 = (bf16[128,256]{1,0:T(8,128)(2,1)}, bf16[128,256]{1,0:T(8,128)(2,1)S(1)}, u32[]{:S(2)}, u32[]{:S(2)}) collective-permute-start(bf16[128,256]{1,0:T(8,128)(2,1)} %get-tuple-element.26), channel_id=1, source_target_pairs={{0,8},{2,10},{4,12},{6,14},{8,0},{10,2},{12,4},{14,6},{16,24},{18,... | collective-permute-start | bytes 196616 | tf_op jit(solution)/shard_map/ppermute | solution.py:238
  7.4 8.9 %collective-permute-start.8 = (bf16[128,256]{1,0:T(8,128)(2,1)}, bf16[128,256]{1,0:T(8,128)(2,1)S(1)}, u32[]{:S(2)}, u32[]{:S(2)}) collective-permute-start(bf16[128,256]{1,0:T(8,128)(2,1)} %get-tuple-element.26), channel_id=1, source_target_pairs={{0,16},{2,18},{4,20},{6,22},{8,24},{10,26},{12,28},{14,30},{16,0},... | collective-permute-start | bytes 196616 | tf_op jit(solution)/shard_map/ppermute | solution.py:238
  10.0 6.8 %collective-permute-start.9 = (bf16[128,256]{1,0:T(8,128)(2,1)}, bf16[128,256]{1,0:T(8,128)(2,1)S(1)}, u32[]{:S(2)}, u32[]{:S(2)}) collective-permute-start(bf16[128,256]{1,0:T(8,128)(2,1)} %get-tuple-element.26), channel_id=1, source_target_pairs={{0,24},{2,26},{4,28},{6,30},{8,16},{10,18},{12,20},{14,22},{16,8},... | collective-permute-start | bytes 196616 | tf_op jit(solution)/shard_map/ppermute | solution.py:238
  10.0 8.3 %collective-permute-start = (bf16[128,256]{1,0:T(8,128)(2,1)}, bf16[128,256]{1,0:T(8,128)(2,1)S(1)}, u32[]{:S(2)}, u32[]{:S(2)}) collective-permute-start(bf16[128,256]{1,0:T(8,128)(2,1)} %get-tuple-element.24), channel_id=1, source_target_pairs={{0,8},{2,10},{4,12},{6,14},{8,0},{10,2},{12,4},{14,6},{16,24},{18,... | collective-permute-start | bytes 196616 | tf_op jit(solution)/shard_map/ppermute | solution.py:238
  10.9 9.6 %collective-permute-start.1 = (bf16[128,256]{1,0:T(8,128)(2,1)}, bf16[128,256]{1,0:T(8,128)(2,1)S(1)}, u32[]{:S(2)}, u32[]{:S(2)}) collective-permute-start(bf16[128,256]{1,0:T(8,128)(2,1)} %get-tuple-element.24), channel_id=1, source_target_pairs={{0,16},{2,18},{4,20},{6,22},{8,24},{10,26},{12,28},{14,30},{16,0},... | collective-permute-start | bytes 196616 | tf_op jit(solution)/shard_map/ppermute | solution.py:238
  16.3 6.3 %collective-permute-start.2 = (bf16[128,256]{1,0:T(8,128)(2,1)}, bf16[128,256]{1,0:T(8,128)(2,1)S(1)}, u32[]{:S(2)}, u32[]{:S(2)}) collective-permute-start(bf16[128,256]{1,0:T(8,128)(2,1)} %get-tuple-element.24), channel_id=1, source_target_pairs={{0,24},{2,26},{4,28},{6,30},{8,16},{10,18},{12,20},{14,22},{16,8},... | collective-permute-start | bytes 196616 | tf_op jit(solution)/shard_map/ppermute | solution.py:238
  16.8 8.2 %collective-permute-start.10 = (bf16[512,256]{1,0:T(8,128)(2,1)S(1)}, bf16[512,256]{1,0:T(8,128)(2,1)S(1)}, u32[]{:S(2)}, u32[]{:S(2)}) collective-permute-start(bf16[512,256]{1,0:T(8,128)(2,1)S(1)} %constant_dynamic-update-slice_fusion.4.rest_0_), channel_id=1, source_target_pairs={{0,4},{2,6},{4,0},{6,2},{8,12},{10,14},{12,8},{14,10},{16,20},{18,... | collective-permute-start | bytes 786440 | tf_op jit(solution)/shard_map/ppermute | solution.py:238
  22.5 8.3 %collective-permute-start.3 = (bf16[512,256]{1,0:T(8,128)(2,1)S(1)}, bf16[512,256]{1,0:T(8,128)(2,1)S(1)}, u32[]{:S(2)}, u32[]{:S(2)}) collective-permute-start(bf16[512,256]{1,0:T(8,128)(2,1)S(1)} %constant_dynamic-update-slice_fusion.rest_0_), channel_id=1, source_target_pairs={{0,4},{2,6},{4,0},{6,2},{8,12},{10,14},{12,8},{14,10},{16,20},{18,... | collective-permute-start | bytes 786440 | tf_op jit(solution)/shard_map/ppermute | solution.py:238
  24.9 6.5 %collective-permute-start.11 = (bf16[512,256]{1,0:T(8,128)(2,1)S(1)}, bf16[512,256]{1,0:T(8,128)(2,1)S(1)}, u32[]{:S(2)}, u32[]{:S(2)}) collective-permute-start(bf16[512,256]{1,0:T(8,128)(2,1)S(1)} %constant_dynamic-update-slice_fusion.4.rest_0_), channel_id=1, source_target_pairs={{0,2},{2,0},{4,6},{6,4},{8,10},{10,8},{12,14},{14,12},{16,18},{18,... | collective-permute-start | bytes 786440 | tf_op jit(solution)/shard_map/ppermute | solution.py:238
  24.9 6.5 %collective-permute-start.12 = (bf16[512,256]{1,0:T(8,128)(2,1)S(1)}, bf16[512,256]{1,0:T(8,128)(2,1)S(1)}, u32[]{:S(2)}, u32[]{:S(2)}) collective-permute-start(bf16[512,256]{1,0:T(8,128)(2,1)S(1)} %collective-permute-done.10.rest_1_), channel_id=1, source_target_pairs={{0,2},{2,0},{4,6},{6,4},{8,10},{10,8},{12,14},{14,12},{16,18},{18,... | collective-permute-start | bytes 786440 | tf_op jit(solution)/shard_map/ppermute | solution.py:238
  26.1 2.5 %copy-start.2 = (s32[1,1,80,128,128]{4,3,2,1,0:T(8,128)S(1)}, s32[1,1,80,128,128]{4,3,2,1,0:T(8,128)}, u32[]{:S(2)}) copy-start(s32[1,1,80,128,128]{4,3,2,1,0:T(8,128)} %param.16) | copy-start | bytes 15728644
  30.8 3.9 %collective-permute-start.4 = (bf16[512,256]{1,0:T(8,128)(2,1)S(1)}, bf16[512,256]{1,0:T(8,128)(2,1)S(1)}, u32[]{:S(2)}, u32[]{:S(2)}) collective-permute-start(bf16[512,256]{1,0:T(8,128)(2,1)S(1)} %constant_dynamic-update-slice_fusion.rest_0_), channel_id=1, source_target_pairs={{0,2},{2,0},{4,6},{6,4},{8,10},{10,8},{12,14},{14,12},{16,18},{18,... | collective-permute-start | bytes 786440 | tf_op jit(solution)/shard_map/ppermute | solution.py:238
  30.9 3.8 %collective-permute-start.5 = (bf16[512,256]{1,0:T(8,128)(2,1)S(1)}, bf16[512,256]{1,0:T(8,128)(2,1)S(1)}, u32[]{:S(2)}, u32[]{:S(2)}) collective-permute-start(bf16[512,256]{1,0:T(8,128)(2,1)S(1)} %collective-permute-done.3.rest_1_), channel_id=1, source_target_pairs={{0,2},{2,0},{4,6},{6,4},{8,10},{10,8},{12,14},{14,12},{16,18},{18,... | collective-permute-start | bytes 786440 | tf_op jit(solution)/shard_map/ppermute | solution.py:238
  33.1 14.5 %collective-permute-start.19 = (bf16[512,256]{1,0:T(8,128)(2,1)S(1)}, bf16[512,256]{1,0:T(8,128)(2,1)S(1)}, u32[]{:S(2)}, u32[]{:S(2)}) collective-permute-start(bf16[512,256]{1,0:T(8,128)(2,1)S(1)} %get-tuple-element.36.rest_2_), channel_id=1, source_target_pairs={{0,1},{1,0},{2,3},{3,2},{4,5},{5,4},{6,7},{7,6},{8,9},{9,8},{10,11... | collective-permute-start | bytes 786440 | tf_op jit(solution)/shard_map/ppermute | solution.py:311
  36.5 11.6 %collective-permute-start.18 = (bf16[512,256]{1,0:T(8,128)(2,1)S(1)}, bf16[512,256]{1,0:T(8,128)(2,1)S(1)}, u32[]{:S(2)}, u32[]{:S(2)}) collective-permute-start(bf16[512,256]{1,0:T(8,128)(2,1)S(1)} %get-tuple-element.35.rest_0_), channel_id=1, source_target_pairs={{0,1},{1,0},{2,3},{3,2},{4,5},{5,4},{6,7},{7,6},{8,9},{9,8},{10,11... | collective-permute-start | bytes 786440 | tf_op jit(solution)/shard_map/ppermute | solution.py:311
  40.4 9.2 %copy-start = (bf16[2048,512]{1,0:T(8,128)(2,1)S(1)}, bf16[2048,512]{1,0:T(8,128)(2,1)}, u32[]{:S(2)}) copy-start(bf16[2048,512]{1,0:T(8,128)(2,1)} %user_ref.7) | copy-start | bytes 6291460
  40.4 9.2 %copy-start.1 = (bf16[2048,512]{1,0:T(8,128)(2,1)S(1)}, bf16[2048,512]{1,0:T(8,128)(2,1)}, u32[]{:S(2)}) copy-start(bf16[2048,512]{1,0:T(8,128)(2,1)} %grad_ref.7) | copy-start | bytes 6291460
  40.5 9.2 %copy-start.3 = (f32[512]{0:T(512)S(1)}, f32[512]{0:T(512)}, u32[]{:S(2)}) copy-start(f32[512]{0:T(512)} %param.11) | copy-start | bytes 6148
  40.5 13.1 %collective-permute-start.13 = (bf16[512,256]{1,0:T(8,128)(2,1)S(1)}, bf16[512,256]{1,0:T(8,128)(2,1)S(1)}, u32[]{:S(2)}, u32[]{:S(2)}) collective-permute-start(bf16[512,256]{1,0:T(8,128)(2,1)S(1)} %get-tuple-element.27.rest_2_), channel_id=1, source_target_pairs={{0,1},{1,0},{2,3},{3,2},{4,5},{5,4},{6,7},{7,6},{8,9},{9,8},{10,11... | collective-permute-start | bytes 786440 | tf_op jit(solution)/shard_map/ppermute | solution.py:311
  45.5 13.7 %collective-permute-start.6 = (bf16[512,256]{1,0:T(8,128)(2,1)S(1)}, bf16[512,256]{1,0:T(8,128)(2,1)S(1)}, u32[]{:S(2)}, u32[]{:S(2)}) collective-permute-start(bf16[512,256]{1,0:T(8,128)(2,1)S(1)} %get-tuple-element.25.rest_0_), channel_id=1, source_target_pairs={{0,1},{1,0},{2,3},{3,2},{4,5},{5,4},{6,7},{7,6},{8,9},{9,8},{10,11... | collective-permute-start | bytes 786440 | tf_op jit(solution)/shard_map/ppermute | solution.py:311
  46.1 18.8 %collective-permute-start.17 = (bf16[512,256]{1,0:T(8,128)(2,1)S(1)}, bf16[512,256]{1,0:T(8,128)(2,1)S(1)}, u32[]{:S(2)}, u32[]{:S(2)}) collective-permute-start(bf16[512,256]{1,0:T(8,128)(2,1)S(1)} %get-tuple-element.33.rest_2_), channel_id=1, source_target_pairs={{0,1},{1,0},{2,3},{3,2},{4,5},{5,4},{6,7},{7,6},{8,9},{9,8},{10,11... | collective-permute-start | bytes 786440 | tf_op jit(solution)/shard_map/ppermute | solution.py:311
  47.6 22.8 %collective-permute-start.16 = (bf16[512,256]{1,0:T(8,128)(2,1)S(1)}, bf16[512,256]{1,0:T(8,128)(2,1)S(1)}, u32[]{:S(2)}, u32[]{:S(2)}) collective-permute-start(bf16[512,256]{1,0:T(8,128)(2,1)S(1)} %get-tuple-element.32.rest_0_), channel_id=1, source_target_pairs={{0,1},{1,0},{2,3},{3,2},{4,5},{5,4},{6,7},{7,6},{8,9},{9,8},{10,11... | collective-permute-start | bytes 786440 | tf_op jit(solution)/shard_map/ppermute | solution.py:311
  48.1 28.0 %collective-permute-start.15 = (bf16[512,256]{1,0:T(8,128)(2,1)S(1)}, bf16[512,256]{1,0:T(8,128)(2,1)S(1)}, u32[]{:S(2)}, u32[]{:S(2)}) collective-permute-start(bf16[512,256]{1,0:T(8,128)(2,1)S(1)} %get-tuple-element.30.rest_2_), channel_id=1, source_target_pairs={{0,1},{1,0},{2,3},{3,2},{4,5},{5,4},{6,7},{7,6},{8,9},{9,8},{10,11... | collective-permute-start | bytes 786440 | tf_op jit(solution)/shard_map/ppermute | solution.py:311
  53.6 27.2 %collective-permute-start.14 = (bf16[512,256]{1,0:T(8,128)(2,1)S(1)}, bf16[512,256]{1,0:T(8,128)(2,1)S(1)}, u32[]{:S(2)}, u32[]{:S(2)}) collective-permute-start(bf16[512,256]{1,0:T(8,128)(2,1)S(1)} %get-tuple-element.29.rest_0_), channel_id=1, source_target_pairs={{0,1},{1,0},{2,3},{3,2},{4,5},{5,4},{6,7},{7,6},{8,9},{9,8},{10,11... | collective-permute-start | bytes 786440 | tf_op jit(solution)/shard_map/ppermute | solution.py:311
  82.5 3.8 %copy-start.6 = (f32[2048,256]{1,0:T(8,128)}, f32[2048,256]{1,0:T(8,128)S(1)}, u32[]{:S(2)}) copy-start(f32[2048,256]{1,0:T(8,128)S(1)} %slice_add_fusion.1) | copy-start | bytes 6291460
  83.4 2.9 %collective-permute-start.20 = (bf16[2,2,2,128,256]{4,3,0,2,1:T(8,128)(2,1)}, bf16[2,2,2,128,256]{4,3,0,2,1:T(8,128)(2,1)}, u32[]{:S(2)}, u32[]{:S(2)}) collective-permute-start(bf16[2,2,2,128,256]{4,3,0,2,1:T(8,128)(2,1)} %fusion.23), channel_id=1, source_target_pairs={{0,2},{2,0},{4,6},{6,4},{8,10},{10,8},{12,14},{14,12},{16,18},{18,... | collective-permute-start | bytes 1572872 | tf_op jit(solution)/shard_map/ppermute | solution.py:238
  85.0 6.1 %collective-permute-start.26 = (bf16[2,2,2,128,256]{4,3,0,1,2:T(8,128)(2,1)}, bf16[2,2,2,128,256]{4,3,0,1,2:T(8,128)(2,1)}, u32[]{:S(2)}, u32[]{:S(2)}) collective-permute-start(bf16[2,2,2,128,256]{4,3,0,1,2:T(8,128)(2,1)} %fusion.24), channel_id=1, source_target_pairs={{0,2},{2,0},{4,6},{6,4},{8,10},{10,8},{12,14},{14,12},{16,18},{18,... | collective-permute-start | bytes 1572872 | tf_op jit(solution)/shard_map/ppermute | solution.py:238
  87.9 9.7 %collective-permute-start.21 = (bf16[2,2,128,256]{3,2,0,1:T(8,128)(2,1)S(1)}, bf16[2,2,128,256]{3,2,0,1:T(8,128)(2,1)S(1)}, u32[]{:S(2)}, u32[]{:S(2)}) collective-permute-start(bf16[2,2,128,256]{3,2,0,1:T(8,128)(2,1)S(1)} %fusion.34), channel_id=1, source_target_pairs={{0,8},{2,10},{4,12},{6,14},{8,0},{10,2},{12,4},{14,6},{16,24},{18,... | collective-permute-start | bytes 786440 | tf_op jit(solution)/shard_map/ppermute | solution.py:238
  92.4 8.4 %collective-permute-start.27 = (bf16[2,2,128,256]{3,2,0,1:T(8,128)(2,1)S(1)}, bf16[2,2,128,256]{3,2,0,1:T(8,128)(2,1)S(1)}, u32[]{:S(2)}, u32[]{:S(2)}) collective-permute-start(bf16[2,2,128,256]{3,2,0,1:T(8,128)(2,1)S(1)} %fusion.36), channel_id=1, source_target_pairs={{0,4},{2,6},{4,0},{6,2},{8,12},{10,14},{12,8},{14,10},{16,20},{18,... | collective-permute-start | bytes 786440 | tf_op jit(solution)/shard_map/ppermute | solution.py:238
  97.7 13.5 %copy-start.7 = (bf16[128,16,4,32]{0,3,2,1:T(8,128)(2,1)S(1)}, bf16[128,16,4,32]{0,3,2,1:T(8,128)(2,1)}, u32[]{:S(2)}) copy-start(bf16[128,16,4,32]{0,3,2,1:T(8,128)(2,1)} %broadcast_select_fusion) | copy-start | bytes 1572868
  97.7 5.4 %collective-permute-start.22 = (bf16[2,128,256]{2,1,0:T(8,128)(2,1)S(1)}, bf16[2,128,256]{2,1,0:T(8,128)(2,1)S(1)}, u32[]{:S(2)}, u32[]{:S(2)}) collective-permute-start(bf16[2,128,256]{2,1,0:T(8,128)(2,1)S(1)} %fusion.40), channel_id=1, source_target_pairs={{0,4},{2,6},{4,0},{6,2},{8,12},{10,14},{12,8},{14,10},{16,20},{18,... | collective-permute-start | bytes 393224 | tf_op jit(solution)/shard_map/ppermute | solution.py:238
  100.9 5.8 %collective-permute-start.28 = (bf16[2,128,256]{2,1,0:T(8,128)(2,1)S(1)}, bf16[2,128,256]{2,1,0:T(8,128)(2,1)S(1)}, u32[]{:S(2)}, u32[]{:S(2)}) collective-permute-start(bf16[2,128,256]{2,1,0:T(8,128)(2,1)S(1)} %fusion.41), channel_id=1, source_target_pairs={{0,8},{2,10},{4,12},{6,14},{8,0},{10,2},{12,4},{14,6},{16,24},{18,... | collective-permute-start | bytes 393224 | tf_op jit(solution)/shard_map/ppermute | solution.py:238
  103.2 8.0 %collective-permute-start.23 = (bf16[128,256]{1,0:T(8,128)(2,1)S(1)}, bf16[128,256]{1,0:T(8,128)(2,1)S(1)}, u32[]{:S(2)}, u32[]{:S(2)}) collective-permute-start(bf16[128,256]{1,0:T(8,128)(2,1)S(1)} %fusion.46), channel_id=1, source_target_pairs={{0,16},{2,18},{4,20},{6,22},{8,24},{10,26},{12,28},{14,30},{16,0},... | collective-permute-start | bytes 196616 | tf_op jit(solution)/shard_map/ppermute | solution.py:238
  106.8 5.9 %collective-permute-start.29 = (bf16[128,256]{1,0:T(8,128)(2,1)S(1)}, bf16[128,256]{1,0:T(8,128)(2,1)S(1)}, u32[]{:S(2)}, u32[]{:S(2)}) collective-permute-start(bf16[128,256]{1,0:T(8,128)(2,1)S(1)} %fusion.47), channel_id=1, source_target_pairs={{0,16},{2,18},{4,20},{6,22},{8,24},{10,26},{12,28},{14,30},{16,0},... | collective-permute-start | bytes 196616 | tf_op jit(solution)/shard_map/ppermute | solution.py:238
  111.7 3.4 %collective-permute-start.24 = (bf16[2,2,2,128,256]{4,3,2,1,0:T(8,128)(2,1)S(1)}, bf16[2,2,2,128,256]{4,3,2,1,0:T(8,128)(2,1)S(1)}, u32[]{:S(2)}, u32[]{:S(2)}) collective-permute-start(bf16[2,2,2,128,256]{4,3,2,1,0:T(8,128)(2,1)S(1)} %fusion.22), channel_id=1, source_target_pairs={{0,2},{2,0},{4,6},{6,4},{8,10},{10,8},{12,14},{14,12},{16,18},{18,... | collective-permute-start | bytes 1572872 | tf_op jit(solution)/shard_map/ppermute | solution.py:238
  113.2 1.0 copy-start.8
  113.5 2.3 %collective-permute-start.30 = (bf16[2,2,2,136,256]{4,3,0,1,2:T(8,128)(2,1)S(1)}, bf16[2,2,2,136,256]{4,3,0,1,2:T(8,128)(2,1)S(1)}, u32[]{:S(2)}, u32[]{:S(2)}) collective-permute-start(bf16[2,2,2,136,256]{4,3,0,1,2:T(8,128)(2,1)S(1)} %fusion.21), channel_id=1, source_target_pairs={{0,2},{2,0},{4,6},{6,4},{8,10},{10,8},{12,14},{14,12},{16,18},{18,... | collective-permute-start | bytes 1671176 | tf_op jit(solution)/shard_map/ppermute | solution.py:238
  115.3 10.3 %copy-start.5 = (bf16[4,512,512]{2,1,0:T(8,128)(2,1)S(1)}, bf16[4,512,512]{2,1,0:T(8,128)(2,1)}, u32[]{:S(2)}) copy-start(bf16[4,512,512]{2,1,0:T(8,128)(2,1)} %weight_ref.1) | copy-start | bytes 6291460
  115.4 8.2 %collective-permute-start.25 = (bf16[2,2,128,256]{3,2,1,0:T(8,128)(2,1)S(1)}, bf16[2,2,128,256]{3,2,1,0:T(8,128)(2,1)S(1)}, u32[]{:S(2)}, u32[]{:S(2)}) collective-permute-start(bf16[2,2,128,256]{3,2,1,0:T(8,128)(2,1)S(1)} %fusion.35), channel_id=1, source_target_pairs={{0,8},{2,10},{4,12},{6,14},{8,0},{10,2},{12,4},{14,6},{16,24},{18,... | collective-permute-start | bytes 786440 | tf_op jit(solution)/shard_map/ppermute | solution.py:238
  115.9 11.7 %collective-permute-start.31 = (bf16[2,2,136,256]{3,2,0,1:T(8,128)(2,1)S(1)}, bf16[2,2,136,256]{3,2,0,1:T(8,128)(2,1)S(1)}, u32[]{:S(2)}, u32[]{:S(2)}) collective-permute-start(bf16[2,2,136,256]{3,2,0,1:T(8,128)(2,1)S(1)} %fusion.33), channel_id=1, source_target_pairs={{0,4},{2,6},{4,0},{6,2},{8,12},{10,14},{12,8},{14,10},{16,20},{18,... | collective-permute-start | bytes 835592 | tf_op jit(solution)/shard_map/ppermute | solution.py:238
  123.7 5.0 %collective-permute-start.34 = (bf16[2,128,256]{2,1,0:T(8,128)(2,1)S(1)}, bf16[2,128,256]{2,1,0:T(8,128)(2,1)S(1)}, u32[]{:S(2)}, u32[]{:S(2)}) collective-permute-start(bf16[2,128,256]{2,1,0:T(8,128)(2,1)S(1)} %fusion.42), channel_id=1, source_target_pairs={{0,4},{2,6},{4,0},{6,2},{8,12},{10,14},{12,8},{14,10},{16,20},{18,... | collective-permute-start | bytes 393224 | tf_op jit(solution)/shard_map/ppermute | solution.py:238
  127.7 5.1 %collective-permute-start.32 = (bf16[2,136,256]{2,1,0:T(8,128)(2,1)S(1)}, bf16[2,136,256]{2,1,0:T(8,128)(2,1)S(1)}, u32[]{:S(2)}, u32[]{:S(2)}) collective-permute-start(bf16[2,136,256]{2,1,0:T(8,128)(2,1)S(1)} %fusion.39), channel_id=1, source_target_pairs={{0,8},{2,10},{4,12},{6,14},{8,0},{10,2},{12,4},{14,6},{16,24},{18,... | collective-permute-start | bytes 417800 | tf_op jit(solution)/shard_map/ppermute | solution.py:238
  128.7 6.0 %collective-permute-start.35 = (bf16[128,256]{1,0:T(8,128)(2,1)S(1)}, bf16[128,256]{1,0:T(8,128)(2,1)S(1)}, u32[]{:S(2)}, u32[]{:S(2)}) collective-permute-start(bf16[128,256]{1,0:T(8,128)(2,1)S(1)} %fusion.48), channel_id=1, source_target_pairs={{0,16},{2,18},{4,20},{6,22},{8,24},{10,26},{12,28},{14,30},{16,0},... | collective-permute-start | bytes 196616 | tf_op jit(solution)/shard_map/ppermute | solution.py:238
  132.9 6.0 %collective-permute-start.33 = (bf16[136,256]{1,0:T(8,128)(2,1)S(1)}, bf16[136,256]{1,0:T(8,128)(2,1)S(1)}, u32[]{:S(2)}, u32[]{:S(2)}) collective-permute-start(bf16[136,256]{1,0:T(8,128)(2,1)S(1)} %fusion.45), channel_id=1, source_target_pairs={{0,16},{2,18},{4,20},{6,22},{8,24},{10,26},{12,28},{14,30},{16,0},... | collective-permute-start | bytes 208904 | tf_op jit(solution)/shard_map/ppermute | solution.py:238

commit v13 on v12

--- a/solution.py
+++ b/solution.py
@@ -260,7 +260,10 @@
     bits = size.bit_length() - 1
     index = lax.axis_index("user")
     left = list(reversed(range(bits)))
-    terms = terms.reshape((2,) * bits + terms.shape[1:])
+    if 0 in order:
+        terms = terms.reshape((2,) * bits + terms.shape[1:])
+    else:
+        left.remove(0)
     for bit in order:
         axis = left.index(bit)
         left.remove(bit)
@@ -276,6 +279,10 @@
 def scatter_sums(halves, size, beside=None):
     bits = size.bit_length() - 1
     orders = [list(range(bits)), [0, 2, 1] + list(range(3, bits))]
+    if beside is None:
+        halves = [scatter_sum(terms, size, [0])[0] for terms in halves]
+        halves = lax.optimization_barrier(tuple(halves))
+        orders = [order[1:] for order in orders]
     first, _ = scatter_sum(halves[0], size, orders[0])
     second, beside = scatter_sum(halves[1], size, orders[1], beside)
     return [first, second], beside

time: 140 us -> 141 us (level)
  waiting for transfers between devices: 50.5 us -> 56.9 us
  other arithmetic: 6.21 us -> 4.06 us
  local copies, waits for them, and re-layouts: 8.5 us -> 6.5 us
  starting transfers between devices: 45.8 us -> 43.9 us
    ppermute x28, waiting for transfers between devices: 27 us -> 33.7 us  [flip(): lax.ppermute(value, 'user', [(source, source ^ bits) for source in range(...]
    ppermute x28, starting transfers between devices: 36.3 us -> 34.2 us  [flip(): lax.ppermute(value, 'user', [(source, source ^ bits) for source in range(...]
    unnamed x29 -> x25, local copies, waits for them, and re-layouts: 4.92 us -> 4.36 us
  transfers between devices with their start and end apart: 36 -> 36, of which waited for: 18 -> 21; matrix products, arithmetic and copies ran while one was open for 12% -> 9% of each run, Pallas kernels for 10% -> 10%
where the time goes in v13:
time: 141 us
  waiting for transfers between devices  56.9 us (40%)
  starting transfers between devices  43.9 us (31%)
  Pallas kernels  19 us (13%)
  matrix products  8.34 us (6%)
  local copies, waits for them, and re-layouts  6.5 us (5%)
  other arithmetic  4.06 us (3%)
  between operations  1.92 us (1%)
    ppermute x28, starting transfers between devices, flip(): lax.ppermute(value, 'user', [(source, source ^ bits) for source in range(...  34.2 us
    ppermute x28, waiting for transfers between devices, flip(): lax.ppermute(value, 'user', [(source, source ^ bits) for source in range(...  33.7 us
    ppermute x8, waiting for transfers between devices, on_device(): pieces.append(lax.ppermute(product, 'item', pairs))  23.2 us
    pallas_call x4, Pallas kernels, spread_items(): pl.pallas_call(functools.partial(spread, blocks), out_shape=[jax.ShapeDty...  10.3 us
    ppermute x8, starting transfers between devices, on_device(): pieces.append(lax.ppermute(product, 'item', pairs))  9.73 us
    unnamed x25, local copies, waits for them, and re-layouts  4.36 us
    dot_general x3, matrix products, on_device(): lax.dot_general(dense[chunk * rows:(chunk + 1) * rows], grad, (((0,), (0,...  4.03 us
    pallas_call x1, Pallas kernels, own_queries(): pl.pallas_call(project_own, out_shape=[half] * HALVES, grid_spec=pltpu.Pr...  3.68 us
  transfers between devices with their start and end apart: 36, of which 21 were waited for; matrix products, arithmetic and copies ran while one was open for 9% of the time, Pallas kernels for 10%

profile of v13, /device:TPU:0, one launch (start us, length us, event | category | flops | bytes accessed | tf_op | source)
XLA Modules:
  0.0 140.6 jit_solution(8469135258778112883)
XLA Ops:
  0.7 3.7 %own_queries.1 = (bf16[128,256]{1,0:T(8,128)(2,1)}, bf16[128,256]{1,0:T(8,128)(2,1)}) custom-call(s32[1]{0:T(128)} %bitcast.1.first_ref, s32[1,128]{1,0:T(1,128)} %cats_ref.1, bf16[128,512]{1,0:T(8,128)(2,1)} %bitcast.143, bf16[4,512,512]{2,1,0:T(8,128)(2,1)} %weight_ref.1), custom_call_target="tpu_custom_call" | custom-call | flops 268435456 | bytes 2359296 | tf_op jit(solution)/shard_map/own_queries/pallas_call | solution.py:97
  4.3 3.0 %collective-permute-start.7 = (bf16[128,256]{1,0:T(8,128)(2,1)}, bf16[128,256]{1,0:T(8,128)(2,1)S(1)}, u32[]{:S(2)}, u32[]{:S(2)}) collective-permute-start(bf16[128,256]{1,0:T(8,128)(2,1)} %get-tuple-element.28), channel_id=1, source_target_pairs={{0,8},{2,10},{4,12},{6,14},{8,0},{10,2},{12,4},{14,6},{16,24},{18,... | collective-permute-start | bytes 196616 | tf_op jit(solution)/shard_map/ppermute | solution.py:238
  7.4 2.6 %collective-permute-start.8 = (bf16[128,256]{1,0:T(8,128)(2,1)}, bf16[128,256]{1,0:T(8,128)(2,1)S(1)}, u32[]{:S(2)}, u32[]{:S(2)}) collective-permute-start(bf16[128,256]{1,0:T(8,128)(2,1)} %get-tuple-element.28), channel_id=1, source_target_pairs={{0,16},{2,18},{4,20},{6,22},{8,24},{10,26},{12,28},{14,30},{16,0},... | collective-permute-start | bytes 196616 | tf_op jit(solution)/shard_map/ppermute | solution.py:238
  10.9 3.5 %collective-permute-start.1 = (bf16[128,256]{1,0:T(8,128)(2,1)}, bf16[128,256]{1,0:T(8,128)(2,1)S(1)}, u32[]{:S(2)}, u32[]{:S(2)}) collective-permute-start(bf16[128,256]{1,0:T(8,128)(2,1)} %get-tuple-element.26), channel_id=1, source_target_pairs={{0,16},{2,18},{4,20},{6,22},{8,24},{10,26},{12,28},{14,30},{16,0},... | collective-permute-start | bytes 196616 | tf_op jit(solution)/shard_map/ppermute | solution.py:238
  16.8 1.5 %collective-permute-start.10 = (bf16[512,256]{1,0:T(8,128)(2,1)S(1)}, bf16[512,256]{1,0:T(8,128)(2,1)S(1)}, u32[]{:S(2)}, u32[]{:S(2)}) collective-permute-start(bf16[512,256]{1,0:T(8,128)(2,1)S(1)} %constant_dynamic-update-slice_fusion.4.rest_0_), channel_id=1, source_target_pairs={{0,4},{2,6},{4,0},{6,2},{8,12},{10,14},{12,8},{14,10},{16,20},{18,... | collective-permute-start | bytes 786440 | tf_op jit(solution)/shard_map/ppermute | solution.py:238
  18.3 2.2 %collective-permute-done.1 = bf16[128,256]{1,0:T(8,128)(2,1)S(1)} collective-permute-done((bf16[128,256]{1,0:T(8,128)(2,1)}, bf16[128,256]{1,0:T(8,128)(2,1)S(1)}, u32[]{:S(2)}, u32[]{:S(2)}) %collective-permute-start.1) | collective-permute-done | bytes 65568 | tf_op jit(solution)/shard_map/ppermute | solution.py:238
  20.5 2.1 %collective-permute-done.2 = bf16[128,256]{1,0:T(8,128)(2,1)S(1)} collective-permute-done((bf16[128,256]{1,0:T(8,128)(2,1)}, bf16[128,256]{1,0:T(8,128)(2,1)S(1)}, u32[]{:S(2)}, u32[]{:S(2)}) %collective-permute-start.2) | collective-permute-done | bytes 65568 | tf_op jit(solution)/shard_map/ppermute | solution.py:238
  22.5 1.5 %collective-permute-start.3 = (bf16[512,256]{1,0:T(8,128)(2,1)S(1)}, bf16[512,256]{1,0:T(8,128)(2,1)S(1)}, u32[]{:S(2)}, u32[]{:S(2)}) collective-permute-start(bf16[512,256]{1,0:T(8,128)(2,1)S(1)} %constant_dynamic-update-slice_fusion.rest_0_), channel_id=1, source_target_pairs={{0,4},{2,6},{4,0},{6,2},{8,12},{10,14},{12,8},{14,10},{16,20},{18,... | collective-permute-start | bytes 786440 | tf_op jit(solution)/shard_map/ppermute | solution.py:238
  25.4 2.5 %copy-done.2 = s32[1,1,80,128,128]{4,3,2,1,0:T(8,128)S(1)} copy-done((s32[1,1,80,128,128]{4,3,2,1,0:T(8,128)S(1)}, s32[1,1,80,128,128]{4,3,2,1,0:T(8,128)}, u32[]{:S(2)}) %copy-start.2) | copy-done | bytes 5242904
  27.9 2.1 %place_tiles.1.rest_4_ = bf16[2048,2048]{1,0:T(8,128)(2,1)S(1)} custom-call(s32[80]{0:T(128)S(1)} %bitcast.134, s32[1]{0:T(128)} %bitcast.128.count_ref, s32[80,128,128]{2,1,0:T(8,128)S(1)} %bitcast.129), custom_call_target="tpu_custom_call" | custom-call | flops 1310720 | bytes 13631488 | tf_op jit(solution)/shard_map/place_tiles/pallas_call | solution.py:40
  30.5 1.7 %spread_items.7 = (bf16[512,256]{1,0:T(8,128)(2,1)S(1)}, s32[16]{0:T(128)}) custom-call(s32[16]{0:T(128)S(1)} %fusion.59.order_ref, bf16[512,256]{1,0:T(8,128)(2,1)S(1)} %constant_dynamic-update-slice_fusion.4.rest_0_, bf16[512,256]{1,0:T(8,128)(2,1)S(1)} %collective-permute-done.10.rest_1_, bf16[512,256]{1,0:T(8,128)(2,1)S(1)} %collective-permute-done.11.rest_2_, ...), custom_call_target="tpu_custom_call" | custom-call | flops 536870912 | bytes 3407872 | tf_op jit(solution)/shard_map/spread_items/pallas_call | solution.py:153
  32.3 1.8 %collective-permute-start.19 = (bf16[512,256]{1,0:T(8,128)(2,1)S(1)}, bf16[512,256]{1,0:T(8,128)(2,1)S(1)}, u32[]{:S(2)}, u32[]{:S(2)}) collective-permute-start(bf16[512,256]{1,0:T(8,128)(2,1)S(1)} %get-tuple-element.38.rest_2_), channel_id=1, source_target_pairs={{0,1},{1,0},{2,3},{3,2},{4,5},{5,4},{6,7},{7,6},{8,9},{9,8},{10,11... | collective-permute-start | bytes 786440 | tf_op jit(solution)/shard_map/ppermute | solution.py:318
  34.0 1.7 %spread_items.6 = (bf16[512,256]{1,0:T(8,128)(2,1)S(1)}, s32[16]{0:T(128)}) custom-call(s32[16]{0:T(128)S(1)} %fusion.59.order_ref, bf16[512,256]{1,0:T(8,128)(2,1)S(1)} %constant_dynamic-update-slice_fusion.rest_0_, bf16[512,256]{1,0:T(8,128)(2,1)S(1)} %collective-permute-done.3.rest_1_, bf16[512,256]{1,0:T(8,128)(2,1)S(1)} %collective-permute-done.4.rest_2_, ...), custom_call_target="tpu_custom_call" | custom-call | flops 536870912 | bytes 3407872 | tf_op jit(solution)/shard_map/spread_items/pallas_call | solution.py:153
  36.1 3.4 %spread_items.5 = (bf16[512,256]{1,0:T(8,128)(2,1)S(1)}, bf16[512,256]{1,0:T(8,128)(2,1)S(1)}, bf16[512,256]{1,0:T(8,128)(2,1)S(1)}, s32[16]{0:T(128)}) custom-call(s32[16]{0:T(128)S(1)} %fusion.59.order_ref, bf16[512,256]{1,0:T(8,128)(2,1)S(1)} %constant_dynamic-update-slice_fusion.4.rest_0_, bf16[512,256]{1,0:T(8,128)(2,1)S(1)} %collective-permute-done.10.rest_1_, ...), custom_call_target="tpu_custom_call" | custom-call | flops 1610612736 | bytes 8126464 | tf_op jit(solution)/shard_map/spread_items/pallas_call | solution.py:153
  39.6 1.8 %collective-permute-start.13 = (bf16[512,256]{1,0:T(8,128)(2,1)S(1)}, bf16[512,256]{1,0:T(8,128)(2,1)S(1)}, u32[]{:S(2)}, u32[]{:S(2)}) collective-permute-start(bf16[512,256]{1,0:T(8,128)(2,1)S(1)} %get-tuple-element.29.rest_2_), channel_id=1, source_target_pairs={{0,1},{1,0},{2,3},{3,2},{4,5},{5,4},{6,7},{7,6},{8,9},{9,8},{10,11... | collective-permute-start | bytes 786440 | tf_op jit(solution)/shard_map/ppermute | solution.py:318
  41.4 3.4 %spread_items.4 = (bf16[512,256]{1,0:T(8,128)(2,1)S(1)}, bf16[512,256]{1,0:T(8,128)(2,1)S(1)}, bf16[512,256]{1,0:T(8,128)(2,1)S(1)}, s32[16]{0:T(128)}) custom-call(s32[16]{0:T(128)S(1)} %fusion.59.order_ref, bf16[512,256]{1,0:T(8,128)(2,1)S(1)} %constant_dynamic-update-slice_fusion.rest_0_, bf16[512,256]{1,0:T(8,128)(2,1)S(1)} %collective-permute-done.3.rest_1_, ...), custom_call_target="tpu_custom_call" | custom-call | flops 1610612736 | bytes 8126464 | tf_op jit(solution)/shard_map/spread_items/pallas_call | solution.py:153
  45.2 1.7 %collective-permute-start.17 = (bf16[512,256]{1,0:T(8,128)(2,1)S(1)}, bf16[512,256]{1,0:T(8,128)(2,1)S(1)}, u32[]{:S(2)}, u32[]{:S(2)}) collective-permute-start(bf16[512,256]{1,0:T(8,128)(2,1)S(1)} %get-tuple-element.35.rest_2_), channel_id=1, source_target_pairs={{0,1},{1,0},{2,3},{3,2},{4,5},{5,4},{6,7},{7,6},{8,9},{9,8},{10,11... | collective-permute-start | bytes 786440 | tf_op jit(solution)/shard_map/ppermute | solution.py:318
  47.2 1.7 %collective-permute-start.15 = (bf16[512,256]{1,0:T(8,128)(2,1)S(1)}, bf16[512,256]{1,0:T(8,128)(2,1)S(1)}, u32[]{:S(2)}, u32[]{:S(2)}) collective-permute-start(bf16[512,256]{1,0:T(8,128)(2,1)S(1)} %get-tuple-element.32.rest_2_), channel_id=1, source_target_pairs={{0,1},{1,0},{2,3},{3,2},{4,5},{5,4},{6,7},{7,6},{8,9},{9,8},{10,11... | collective-permute-start | bytes 786440 | tf_op jit(solution)/shard_map/ppermute | solution.py:318
  49.6 1.3 fusion.4
  50.9 1.8 %collective-permute-done.13.rest_3_ = bf16[512,256]{1,0:T(8,128)(2,1)S(1)} collective-permute-done((bf16[512,256]{1,0:T(8,128)(2,1)S(1)}, bf16[512,256]{1,0:T(8,128)(2,1)S(1)}, u32[]{:S(2)}, u32[]{:S(2)}) %collective-permute-start.13) | collective-permute-done | bytes 262176 | tf_op jit(solution)/shard_map/ppermute | solution.py:318
  52.7 1.7 %collective-permute-start.14 = (bf16[512,256]{1,0:T(8,128)(2,1)S(1)}, bf16[512,256]{1,0:T(8,128)(2,1)S(1)}, u32[]{:S(2)}, u32[]{:S(2)}) collective-permute-start(bf16[512,256]{1,0:T(8,128)(2,1)S(1)} %get-tuple-element.31.rest_0_), channel_id=1, source_target_pairs={{0,1},{1,0},{2,3},{3,2},{4,5},{5,4},{6,7},{7,6},{8,9},{9,8},{10,11... | collective-permute-start | bytes 786440 | tf_op jit(solution)/shard_map/ppermute | solution.py:318
  54.4 3.9 %collective-permute-done.6.rest_1_ = bf16[512,256]{1,0:T(8,128)(2,1)S(1)} collective-permute-done((bf16[512,256]{1,0:T(8,128)(2,1)S(1)}, bf16[512,256]{1,0:T(8,128)(2,1)S(1)}, u32[]{:S(2)}, u32[]{:S(2)}) %collective-permute-start.6) | collective-permute-done | bytes 262176 | tf_op jit(solution)/shard_map/ppermute | solution.py:318
  59.0 1.3 fusion.6
  60.3 3.6 %collective-permute-done.17.rest_3_ = bf16[512,256]{1,0:T(8,128)(2,1)S(1)} collective-permute-done((bf16[512,256]{1,0:T(8,128)(2,1)S(1)}, bf16[512,256]{1,0:T(8,128)(2,1)S(1)}, u32[]{:S(2)}, u32[]{:S(2)}) %collective-permute-start.17) | collective-permute-done | bytes 262176 | tf_op jit(solution)/shard_map/ppermute | solution.py:318
  63.9 5.6 %collective-permute-done.16.rest_1_ = bf16[512,256]{1,0:T(8,128)(2,1)S(1)} collective-permute-done((bf16[512,256]{1,0:T(8,128)(2,1)S(1)}, bf16[512,256]{1,0:T(8,128)(2,1)S(1)}, u32[]{:S(2)}, u32[]{:S(2)}) %collective-permute-start.16) | collective-permute-done | bytes 262176 | tf_op jit(solution)/shard_map/ppermute | solution.py:318
  70.3 1.4 %add_add_fusion = f32[2048,512]{1,0:T(8,128)S(1)} fusion(f32[2048,512]{1,0:T(8,128)S(1)} %fusion.6, f32[2048,512]{1,0:T(8,128)S(1)} %fusion.4, bf16[512,512]{1,0:T(8,128)(2,1)S(1)} %get-tuple-element.36, bf16[2048,2048]{1,0:T(8,128)(2,1)S(1)} %place_tiles.1.rest_4_), kind=kOutput, calls=%fused_computation | convolution fusion | flops 1075838976 | bytes 15204352 | tf_op jit(solution)/shard_map/dot_general | solution.py:334
  71.7 3.5 %collective-permute-done.15.rest_3_ = bf16[512,256]{1,0:T(8,128)(2,1)S(1)} collective-permute-done((bf16[512,256]{1,0:T(8,128)(2,1)S(1)}, bf16[512,256]{1,0:T(8,128)(2,1)S(1)}, u32[]{:S(2)}, u32[]{:S(2)}) %collective-permute-start.15) | collective-permute-done | bytes 262176 | tf_op jit(solution)/shard_map/ppermute | solution.py:318
  75.2 4.9 %collective-permute-done.14.rest_1_ = bf16[512,256]{1,0:T(8,128)(2,1)S(1)} collective-permute-done((bf16[512,256]{1,0:T(8,128)(2,1)S(1)}, bf16[512,256]{1,0:T(8,128)(2,1)S(1)}, u32[]{:S(2)}, u32[]{:S(2)}) %collective-permute-start.14) | collective-permute-done | bytes 262176 | tf_op jit(solution)/shard_map/ppermute | solution.py:318
  83.9 0.9 collective-permute-done.20
  85.7 4.7 %collective-permute-start.22 = (bf16[2,2,128,256]{3,2,0,1:T(8,128)(2,1)}, bf16[2,2,128,256]{3,2,0,1:T(8,128)(2,1)S(1)}, u32[]{:S(2)}, u32[]{:S(2)}) collective-permute-start(bf16[2,2,128,256]{3,2,0,1:T(8,128)(2,1)} %fusion.34), channel_id=1, source_target_pairs={{0,8},{2,10},{4,12},{6,14},{8,0},{10,2},{12,4},{14,6},{16,24},{18,... | collective-permute-start | bytes 786440 | tf_op jit(solution)/shard_map/ppermute | solution.py:238
  91.2 6.3 %collective-permute-done.22 = bf16[2,2,128,256]{3,2,0,1:T(8,128)(2,1)S(1)} collective-permute-done((bf16[2,2,128,256]{3,2,0,1:T(8,128)(2,1)}, bf16[2,2,128,256]{3,2,0,1:T(8,128)(2,1)S(1)}, u32[]{:S(2)}, u32[]{:S(2)}) %collective-permute-start.22) | collective-permute-done | bytes 262176 | tf_op jit(solution)/shard_map/ppermute | solution.py:238
  97.4 1.1 bitcast_add_fusion.7
  99.3 1.8 %collective-permute-start.28 = (bf16[2,128,256]{2,1,0:T(8,128)(2,1)S(1)}, bf16[2,128,256]{2,1,0:T(8,128)(2,1)S(1)}, u32[]{:S(2)}, u32[]{:S(2)}) collective-permute-start(bf16[2,128,256]{2,1,0:T(8,128)(2,1)S(1)} %fusion.41), channel_id=1, source_target_pairs={{0,8},{2,10},{4,12},{6,14},{8,0},{10,2},{12,4},{14,6},{16,24},{18,... | collective-permute-start | bytes 393224 | tf_op jit(solution)/shard_map/ppermute | solution.py:238
  101.1 2.7 %collective-permute-done.23 = bf16[2,128,256]{2,1,0:T(8,128)(2,1)S(1)} collective-permute-done((bf16[2,128,256]{2,1,0:T(8,128)(2,1)S(1)}, bf16[2,128,256]{2,1,0:T(8,128)(2,1)S(1)}, u32[]{:S(2)}, u32[]{:S(2)}) %collective-permute-start.23) | collective-permute-done | bytes 131104 | tf_op jit(solution)/shard_map/ppermute | solution.py:238
  103.9 3.2 %collective-permute-start.24 = (bf16[128,256]{1,0:T(8,128)(2,1)S(1)}, bf16[128,256]{1,0:T(8,128)(2,1)S(1)}, u32[]{:S(2)}, u32[]{:S(2)}) collective-permute-start(bf16[128,256]{1,0:T(8,128)(2,1)S(1)} %fusion.46), channel_id=1, source_target_pairs={{0,16},{2,18},{4,20},{6,22},{8,24},{10,26},{12,28},{14,30},{16,0},... | collective-permute-start | bytes 196616 | tf_op jit(solution)/shard_map/ppermute | solution.py:238
  107.1 2.3 %collective-permute-start.29 = (bf16[128,256]{1,0:T(8,128)(2,1)S(1)}, bf16[128,256]{1,0:T(8,128)(2,1)S(1)}, u32[]{:S(2)}, u32[]{:S(2)}) collective-permute-start(bf16[128,256]{1,0:T(8,128)(2,1)S(1)} %fusion.47), channel_id=1, source_target_pairs={{0,16},{2,18},{4,20},{6,22},{8,24},{10,26},{12,28},{14,30},{16,0},... | collective-permute-start | bytes 196616 | tf_op jit(solution)/shard_map/ppermute | solution.py:238
  109.4 1.8 %collective-permute-done.24 = bf16[128,256]{1,0:T(8,128)(2,1)S(1)} collective-permute-done((bf16[128,256]{1,0:T(8,128)(2,1)S(1)}, bf16[128,256]{1,0:T(8,128)(2,1)S(1)}, u32[]{:S(2)}, u32[]{:S(2)}) %collective-permute-start.24) | collective-permute-done | bytes 65568 | tf_op jit(solution)/shard_map/ppermute | solution.py:238
  111.8 1.2 collective-permute-done.29
  113.8 1.0 pad_maximum_fusion.1
  115.9 1.5 %collective-permute-start.31 = (bf16[2,2,136,256]{3,2,0,1:T(8,128)(2,1)S(1)}, bf16[2,2,136,256]{3,2,0,1:T(8,128)(2,1)S(1)}, u32[]{:S(2)}, u32[]{:S(2)}) collective-permute-start(bf16[2,2,136,256]{3,2,0,1:T(8,128)(2,1)S(1)} %fusion.33), channel_id=1, source_target_pairs={{0,4},{2,6},{4,0},{6,2},{8,12},{10,14},{12,8},{14,10},{16,20},{18,... | collective-permute-start | bytes 835592 | tf_op jit(solution)/shard_map/ppermute | solution.py:238
  117.5 6.4 %collective-permute-done.26 = bf16[2,2,128,256]{3,2,1,0:T(8,128)(2,1)S(1)} collective-permute-done((bf16[2,2,128,256]{3,2,1,0:T(8,128)(2,1)S(1)}, bf16[2,2,128,256]{3,2,1,0:T(8,128)(2,1)S(1)}, u32[]{:S(2)}, u32[]{:S(2)}) %collective-permute-start.26) | collective-permute-done | bytes 262176 | tf_op jit(solution)/shard_map/ppermute | solution.py:238
  123.9 1.5 %collective-permute-start.34 = (bf16[2,128,256]{2,1,0:T(8,128)(2,1)S(1)}, bf16[2,128,256]{2,1,0:T(8,128)(2,1)S(1)}, u32[]{:S(2)}, u32[]{:S(2)}) collective-permute-start(bf16[2,128,256]{2,1,0:T(8,128)(2,1)S(1)} %fusion.42), channel_id=1, source_target_pairs={{0,4},{2,6},{4,0},{6,2},{8,12},{10,14},{12,8},{14,10},{16,20},{18,... | collective-permute-start | bytes 393224 | tf_op jit(solution)/shard_map/ppermute | solution.py:238
  126.4 1.0 fusion.20
  127.8 1.3 collective-permute-done.34
  129.2 1.6 %collective-permute-start.35 = (bf16[128,256]{1,0:T(8,128)(2,1)S(1)}, bf16[128,256]{1,0:T(8,128)(2,1)S(1)}, u32[]{:S(2)}, u32[]{:S(2)}) collective-permute-start(bf16[128,256]{1,0:T(8,128)(2,1)S(1)} %fusion.48), channel_id=1, source_target_pairs={{0,16},{2,18},{4,20},{6,22},{8,24},{10,26},{12,28},{14,30},{16,0},... | collective-permute-start | bytes 196616 | tf_op jit(solution)/shard_map/ppermute | solution.py:238
  130.8 2.5 %collective-permute-done.32 = bf16[2,136,256]{2,1,0:T(8,128)(2,1)S(1)} collective-permute-done((bf16[2,136,256]{2,1,0:T(8,128)(2,1)S(1)}, bf16[2,136,256]{2,1,0:T(8,128)(2,1)S(1)}, u32[]{:S(2)}, u32[]{:S(2)}) %collective-permute-start.32) | collective-permute-done | bytes 139296 | tf_op jit(solution)/shard_map/ppermute | solution.py:238
  134.3 2.0 %collective-permute-done.35 = bf16[128,256]{1,0:T(8,128)(2,1)S(1)} collective-permute-done((bf16[128,256]{1,0:T(8,128)(2,1)S(1)}, bf16[128,256]{1,0:T(8,128)(2,1)S(1)}, u32[]{:S(2)}, u32[]{:S(2)}) %collective-permute-start.35) | collective-permute-done | bytes 65568 | tf_op jit(solution)/shard_map/ppermute | solution.py:238
  136.3 2.9 %collective-permute-done.33 = bf16[136,256]{1,0:T(8,128)(2,1)S(1)} collective-permute-done((bf16[136,256]{1,0:T(8,128)(2,1)S(1)}, bf16[136,256]{1,0:T(8,128)(2,1)S(1)}, u32[]{:S(2)}, u32[]{:S(2)}) %collective-permute-start.33) | collective-permute-done | bytes 69664 | tf_op jit(solution)/shard_map/ppermute | solution.py:238
  (122 shorter events, 20.2 us)
Async XLA Ops:
  0.6 14.6 %copy-start.7 = (bf16[1,128,512]{2,1,0:T(8,128)(2,1)S(1)}, bf16[1,128,512]{2,1,0:T(8,128)(2,1)}, u32[]{:S(2)}) copy-start(bf16[1,128,512]{2,1,0:T(8,128)(2,1)} %param.12) | copy-start | bytes 393220
  0.6 14.7 %copy-start.8 = (s32[1,128]{1,0:T(1,128)S(1)}, s32[1,128]{1,0:T(1,128)}, u32[]{:S(2)}) copy-start(s32[1,128]{1,0:T(1,128)} %cats_ref.1) | copy-start | bytes 1540
  0.7 24.7 %copy-start.4 = (s32[1,1,80]{2,1,0:T(1,128)S(1)}, s32[1,1,80]{2,1,0:T(1,128)}, u32[]{:S(2)}) copy-start(s32[1,1,80]{2,1,0:T(1,128)} %param.15) | copy-start | bytes 964
  4.3 11.9 %collective-permute-start.7 = (bf16[128,256]{1,0:T(8,128)(2,1)}, bf16[128,256]{1,0:T(8,128)(2,1)S(1)}, u32[]{:S(2)}, u32[]{:S(2)}) collective-permute-start(bf16[128,256]{1,0:T(8,128)(2,1)} %get-tuple-element.28), channel_id=1, source_target_pairs={{0,8},{2,10},{4,12},{6,14},{8,0},{10,2},{12,4},{14,6},{16,24},{18,... | collective-permute-start | bytes 196616 | tf_op jit(solution)/shard_map/ppermute | solution.py:238
  7.4 8.9 %collective-permute-start.8 = (bf16[128,256]{1,0:T(8,128)(2,1)}, bf16[128,256]{1,0:T(8,128)(2,1)S(1)}, u32[]{:S(2)}, u32[]{:S(2)}) collective-permute-start(bf16[128,256]{1,0:T(8,128)(2,1)} %get-tuple-element.28), channel_id=1, source_target_pairs={{0,16},{2,18},{4,20},{6,22},{8,24},{10,26},{12,28},{14,30},{16,0},... | collective-permute-start | bytes 196616 | tf_op jit(solution)/shard_map/ppermute | solution.py:238
  10.0 6.8 %collective-permute-start.9 = (bf16[128,256]{1,0:T(8,128)(2,1)}, bf16[128,256]{1,0:T(8,128)(2,1)S(1)}, u32[]{:S(2)}, u32[]{:S(2)}) collective-permute-start(bf16[128,256]{1,0:T(8,128)(2,1)} %get-tuple-element.28), channel_id=1, source_target_pairs={{0,24},{2,26},{4,28},{6,30},{8,16},{10,18},{12,20},{14,22},{16,8},... | collective-permute-start | bytes 196616 | tf_op jit(solution)/shard_map/ppermute | solution.py:238
  10.0 8.3 %collective-permute-start = (bf16[128,256]{1,0:T(8,128)(2,1)}, bf16[128,256]{1,0:T(8,128)(2,1)S(1)}, u32[]{:S(2)}, u32[]{:S(2)}) collective-permute-start(bf16[128,256]{1,0:T(8,128)(2,1)} %get-tuple-element.26), channel_id=1, source_target_pairs={{0,8},{2,10},{4,12},{6,14},{8,0},{10,2},{12,4},{14,6},{16,24},{18,... | collective-permute-start | bytes 196616 | tf_op jit(solution)/shard_map/ppermute | solution.py:238
  10.9 9.6 %collective-permute-start.1 = (bf16[128,256]{1,0:T(8,128)(2,1)}, bf16[128,256]{1,0:T(8,128)(2,1)S(1)}, u32[]{:S(2)}, u32[]{:S(2)}) collective-permute-start(bf16[128,256]{1,0:T(8,128)(2,1)} %get-tuple-element.26), channel_id=1, source_target_pairs={{0,16},{2,18},{4,20},{6,22},{8,24},{10,26},{12,28},{14,30},{16,0},... | collective-permute-start | bytes 196616 | tf_op jit(solution)/shard_map/ppermute | solution.py:238
  16.3 6.3 %collective-permute-start.2 = (bf16[128,256]{1,0:T(8,128)(2,1)}, bf16[128,256]{1,0:T(8,128)(2,1)S(1)}, u32[]{:S(2)}, u32[]{:S(2)}) collective-permute-start(bf16[128,256]{1,0:T(8,128)(2,1)} %get-tuple-element.26), channel_id=1, source_target_pairs={{0,24},{2,26},{4,28},{6,30},{8,16},{10,18},{12,20},{14,22},{16,8},... | collective-permute-start | bytes 196616 | tf_op jit(solution)/shard_map/ppermute | solution.py:238
  16.8 7.4 %collective-permute-start.10 = (bf16[512,256]{1,0:T(8,128)(2,1)S(1)}, bf16[512,256]{1,0:T(8,128)(2,1)S(1)}, u32[]{:S(2)}, u32[]{:S(2)}) collective-permute-start(bf16[512,256]{1,0:T(8,128)(2,1)S(1)} %constant_dynamic-update-slice_fusion.4.rest_0_), channel_id=1, source_target_pairs={{0,4},{2,6},{4,0},{6,2},{8,12},{10,14},{12,8},{14,10},{16,20},{18,... | collective-permute-start | bytes 786440 | tf_op jit(solution)/shard_map/ppermute | solution.py:238
  22.5 7.6 %collective-permute-start.3 = (bf16[512,256]{1,0:T(8,128)(2,1)S(1)}, bf16[512,256]{1,0:T(8,128)(2,1)S(1)}, u32[]{:S(2)}, u32[]{:S(2)}) collective-permute-start(bf16[512,256]{1,0:T(8,128)(2,1)S(1)} %constant_dynamic-update-slice_fusion.rest_0_), channel_id=1, source_target_pairs={{0,4},{2,6},{4,0},{6,2},{8,12},{10,14},{12,8},{14,10},{16,20},{18,... | collective-permute-start | bytes 786440 | tf_op jit(solution)/shard_map/ppermute | solution.py:238
  24.1 6.4 %collective-permute-start.11 = (bf16[512,256]{1,0:T(8,128)(2,1)S(1)}, bf16[512,256]{1,0:T(8,128)(2,1)S(1)}, u32[]{:S(2)}, u32[]{:S(2)}) collective-permute-start(bf16[512,256]{1,0:T(8,128)(2,1)S(1)} %constant_dynamic-update-slice_fusion.4.rest_0_), channel_id=1, source_target_pairs={{0,2},{2,0},{4,6},{6,4},{8,10},{10,8},{12,14},{14,12},{16,18},{18,... | collective-permute-start | bytes 786440 | tf_op jit(solution)/shard_map/ppermute | solution.py:238
  24.2 6.3 %collective-permute-start.12 = (bf16[512,256]{1,0:T(8,128)(2,1)S(1)}, bf16[512,256]{1,0:T(8,128)(2,1)S(1)}, u32[]{:S(2)}, u32[]{:S(2)}) collective-permute-start(bf16[512,256]{1,0:T(8,128)(2,1)S(1)} %collective-permute-done.10.rest_1_), channel_id=1, source_target_pairs={{0,2},{2,0},{4,6},{6,4},{8,10},{10,8},{12,14},{14,12},{16,18},{18,... | collective-permute-start | bytes 786440 | tf_op jit(solution)/shard_map/ppermute | solution.py:238
  25.4 2.5 %copy-start.2 = (s32[1,1,80,128,128]{4,3,2,1,0:T(8,128)S(1)}, s32[1,1,80,128,128]{4,3,2,1,0:T(8,128)}, u32[]{:S(2)}) copy-start(s32[1,1,80,128,128]{4,3,2,1,0:T(8,128)} %param.16) | copy-start | bytes 15728644
  29.9 4.1 %collective-permute-start.4 = (bf16[512,256]{1,0:T(8,128)(2,1)S(1)}, bf16[512,256]{1,0:T(8,128)(2,1)S(1)}, u32[]{:S(2)}, u32[]{:S(2)}) collective-permute-start(bf16[512,256]{1,0:T(8,128)(2,1)S(1)} %constant_dynamic-update-slice_fusion.rest_0_), channel_id=1, source_target_pairs={{0,2},{2,0},{4,6},{6,4},{8,10},{10,8},{12,14},{14,12},{16,18},{18,... | collective-permute-start | bytes 786440 | tf_op jit(solution)/shard_map/ppermute | solution.py:238
  30.2 3.8 %collective-permute-start.5 = (bf16[512,256]{1,0:T(8,128)(2,1)S(1)}, bf16[512,256]{1,0:T(8,128)(2,1)S(1)}, u32[]{:S(2)}, u32[]{:S(2)}) collective-permute-start(bf16[512,256]{1,0:T(8,128)(2,1)S(1)} %collective-permute-done.3.rest_1_), channel_id=1, source_target_pairs={{0,2},{2,0},{4,6},{6,4},{8,10},{10,8},{12,14},{14,12},{16,18},{18,... | collective-permute-start | bytes 786440 | tf_op jit(solution)/shard_map/ppermute | solution.py:238
  32.3 14.6 %collective-permute-start.19 = (bf16[512,256]{1,0:T(8,128)(2,1)S(1)}, bf16[512,256]{1,0:T(8,128)(2,1)S(1)}, u32[]{:S(2)}, u32[]{:S(2)}) collective-permute-start(bf16[512,256]{1,0:T(8,128)(2,1)S(1)} %get-tuple-element.38.rest_2_), channel_id=1, source_target_pairs={{0,1},{1,0},{2,3},{3,2},{4,5},{5,4},{6,7},{7,6},{8,9},{9,8},{10,11... | collective-permute-start | bytes 786440 | tf_op jit(solution)/shard_map/ppermute | solution.py:318
  35.7 11.5 %collective-permute-start.18 = (bf16[512,256]{1,0:T(8,128)(2,1)S(1)}, bf16[512,256]{1,0:T(8,128)(2,1)S(1)}, u32[]{:S(2)}, u32[]{:S(2)}) collective-permute-start(bf16[512,256]{1,0:T(8,128)(2,1)S(1)} %get-tuple-element.37.rest_0_), channel_id=1, source_target_pairs={{0,1},{1,0},{2,3},{3,2},{4,5},{5,4},{6,7},{7,6},{8,9},{9,8},{10,11... | collective-permute-start | bytes 786440 | tf_op jit(solution)/shard_map/ppermute | solution.py:318
  39.6 9.4 %copy-start = (bf16[2048,512]{1,0:T(8,128)(2,1)S(1)}, bf16[2048,512]{1,0:T(8,128)(2,1)}, u32[]{:S(2)}) copy-start(bf16[2048,512]{1,0:T(8,128)(2,1)} %user_ref.7) | copy-start | bytes 6291460
  39.6 9.3 %copy-start.1 = (bf16[2048,512]{1,0:T(8,128)(2,1)S(1)}, bf16[2048,512]{1,0:T(8,128)(2,1)}, u32[]{:S(2)}) copy-start(bf16[2048,512]{1,0:T(8,128)(2,1)} %grad_ref.7) | copy-start | bytes 6291460
  39.6 9.3 %copy-start.3 = (f32[512]{0:T(512)S(1)}, f32[512]{0:T(512)}, u32[]{:S(2)}) copy-start(f32[512]{0:T(512)} %param.11) | copy-start | bytes 6148
  39.6 13.1 %collective-permute-start.13 = (bf16[512,256]{1,0:T(8,128)(2,1)S(1)}, bf16[512,256]{1,0:T(8,128)(2,1)S(1)}, u32[]{:S(2)}, u32[]{:S(2)}) collective-permute-start(bf16[512,256]{1,0:T(8,128)(2,1)S(1)} %get-tuple-element.29.rest_2_), channel_id=1, source_target_pairs={{0,1},{1,0},{2,3},{3,2},{4,5},{5,4},{6,7},{7,6},{8,9},{9,8},{10,11... | collective-permute-start | bytes 786440 | tf_op jit(solution)/shard_map/ppermute | solution.py:318
  44.8 13.5 %collective-permute-start.6 = (bf16[512,256]{1,0:T(8,128)(2,1)S(1)}, bf16[512,256]{1,0:T(8,128)(2,1)S(1)}, u32[]{:S(2)}, u32[]{:S(2)}) collective-permute-start(bf16[512,256]{1,0:T(8,128)(2,1)S(1)} %get-tuple-element.27.rest_0_), channel_id=1, source_target_pairs={{0,1},{1,0},{2,3},{3,2},{4,5},{5,4},{6,7},{7,6},{8,9},{9,8},{10,11... | collective-permute-start | bytes 786440 | tf_op jit(solution)/shard_map/ppermute | solution.py:318
  45.2 18.7 %collective-permute-start.17 = (bf16[512,256]{1,0:T(8,128)(2,1)S(1)}, bf16[512,256]{1,0:T(8,128)(2,1)S(1)}, u32[]{:S(2)}, u32[]{:S(2)}) collective-permute-start(bf16[512,256]{1,0:T(8,128)(2,1)S(1)} %get-tuple-element.35.rest_2_), channel_id=1, source_target_pairs={{0,1},{1,0},{2,3},{3,2},{4,5},{5,4},{6,7},{7,6},{8,9},{9,8},{10,11... | collective-permute-start | bytes 786440 | tf_op jit(solution)/shard_map/ppermute | solution.py:318
  46.9 22.7 %collective-permute-start.16 = (bf16[512,256]{1,0:T(8,128)(2,1)S(1)}, bf16[512,256]{1,0:T(8,128)(2,1)S(1)}, u32[]{:S(2)}, u32[]{:S(2)}) collective-permute-start(bf16[512,256]{1,0:T(8,128)(2,1)S(1)} %get-tuple-element.34.rest_0_), channel_id=1, source_target_pairs={{0,1},{1,0},{2,3},{3,2},{4,5},{5,4},{6,7},{7,6},{8,9},{9,8},{10,11... | collective-permute-start | bytes 786440 | tf_op jit(solution)/shard_map/ppermute | solution.py:318
  47.2 27.9 %collective-permute-start.15 = (bf16[512,256]{1,0:T(8,128)(2,1)S(1)}, bf16[512,256]{1,0:T(8,128)(2,1)S(1)}, u32[]{:S(2)}, u32[]{:S(2)}) collective-permute-start(bf16[512,256]{1,0:T(8,128)(2,1)S(1)} %get-tuple-element.32.rest_2_), channel_id=1, source_target_pairs={{0,1},{1,0},{2,3},{3,2},{4,5},{5,4},{6,7},{7,6},{8,9},{9,8},{10,11... | collective-permute-start | bytes 786440 | tf_op jit(solution)/shard_map/ppermute | solution.py:318
  52.7 27.3 %collective-permute-start.14 = (bf16[512,256]{1,0:T(8,128)(2,1)S(1)}, bf16[512,256]{1,0:T(8,128)(2,1)S(1)}, u32[]{:S(2)}, u32[]{:S(2)}) collective-permute-start(bf16[512,256]{1,0:T(8,128)(2,1)S(1)} %get-tuple-element.31.rest_0_), channel_id=1, source_target_pairs={{0,1},{1,0},{2,3},{3,2},{4,5},{5,4},{6,7},{7,6},{8,9},{9,8},{10,11... | collective-permute-start | bytes 786440 | tf_op jit(solution)/shard_map/ppermute | solution.py:318
  81.8 2.0 %collective-permute-start.21 = (bf16[2,2,2,128,256]{4,3,0,2,1:T(8,128)(2,1)S(1)}, bf16[2,2,2,128,256]{4,3,0,2,1:T(8,128)(2,1)S(1)}, u32[]{:S(2)}, u32[]{:S(2)}) collective-permute-start(bf16[2,2,2,128,256]{4,3,0,2,1:T(8,128)(2,1)S(1)} %fusion.24), channel_id=1, source_target_pairs={{0,2},{2,0},{4,6},{6,4},{8,10},{10,8},{12,14},{14,12},{16,18},{18,... | collective-permute-start | bytes 1572872 | tf_op jit(solution)/shard_map/ppermute | solution.py:238
  82.8 2.1 %collective-permute-start.20 = (bf16[2,2,2,128,256]{4,3,0,1,2:T(8,128)(2,1)S(1)}, bf16[2,2,2,128,256]{4,3,0,1,2:T(8,128)(2,1)S(1)}, u32[]{:S(2)}, u32[]{:S(2)}) collective-permute-start(bf16[2,2,2,128,256]{4,3,0,1,2:T(8,128)(2,1)S(1)} %fusion.23), channel_id=1, source_target_pairs={{0,2},{2,0},{4,6},{6,4},{8,10},{10,8},{12,14},{14,12},{16,18},{18,... | collective-permute-start | bytes 1572872 | tf_op jit(solution)/shard_map/ppermute | solution.py:238
  83.9 6.5 %copy-start.6 = (f32[2,2,2,128,256]{4,3,0,2,1:T(8,128)}, f32[2,2,2,128,256]{4,3,0,2,1:T(8,128)S(1)}, u32[]{:S(2)}) copy-start(f32[2,2,2,128,256]{4,3,0,2,1:T(8,128)S(1)} %bitcast_add_fusion.2) | copy-start | bytes 3145732
  85.7 11.7 %collective-permute-start.22 = (bf16[2,2,128,256]{3,2,0,1:T(8,128)(2,1)}, bf16[2,2,128,256]{3,2,0,1:T(8,128)(2,1)S(1)}, u32[]{:S(2)}, u32[]{:S(2)}) collective-permute-start(bf16[2,2,128,256]{3,2,0,1:T(8,128)(2,1)} %fusion.34), channel_id=1, source_target_pairs={{0,8},{2,10},{4,12},{6,14},{8,0},{10,2},{12,4},{14,6},{16,24},{18,... | collective-permute-start | bytes 786440 | tf_op jit(solution)/shard_map/ppermute | solution.py:238
  90.5 8.7 %collective-permute-start.27 = (bf16[2,2,128,256]{3,2,0,1:T(8,128)(2,1)S(1)}, bf16[2,2,128,256]{3,2,0,1:T(8,128)(2,1)S(1)}, u32[]{:S(2)}, u32[]{:S(2)}) collective-permute-start(bf16[2,2,128,256]{3,2,0,1:T(8,128)(2,1)S(1)} %fusion.36), channel_id=1, source_target_pairs={{0,4},{2,6},{4,0},{6,2},{8,12},{10,14},{12,8},{14,10},{16,20},{18,... | collective-permute-start | bytes 786440 | tf_op jit(solution)/shard_map/ppermute | solution.py:238
  98.6 5.3 %collective-permute-start.23 = (bf16[2,128,256]{2,1,0:T(8,128)(2,1)S(1)}, bf16[2,128,256]{2,1,0:T(8,128)(2,1)S(1)}, u32[]{:S(2)}, u32[]{:S(2)}) collective-permute-start(bf16[2,128,256]{2,1,0:T(8,128)(2,1)S(1)} %fusion.40), channel_id=1, source_target_pairs={{0,4},{2,6},{4,0},{6,2},{8,12},{10,14},{12,8},{14,10},{16,20},{18,... | collective-permute-start | bytes 393224 | tf_op jit(solution)/shard_map/ppermute | solution.py:238
  99.3 7.8 %collective-permute-start.28 = (bf16[2,128,256]{2,1,0:T(8,128)(2,1)S(1)}, bf16[2,128,256]{2,1,0:T(8,128)(2,1)S(1)}, u32[]{:S(2)}, u32[]{:S(2)}) collective-permute-start(bf16[2,128,256]{2,1,0:T(8,128)(2,1)S(1)} %fusion.41), channel_id=1, source_target_pairs={{0,8},{2,10},{4,12},{6,14},{8,0},{10,2},{12,4},{14,6},{16,24},{18,... | collective-permute-start | bytes 393224 | tf_op jit(solution)/shard_map/ppermute | solution.py:238
  103.9 7.3 %collective-permute-start.24 = (bf16[128,256]{1,0:T(8,128)(2,1)S(1)}, bf16[128,256]{1,0:T(8,128)(2,1)S(1)}, u32[]{:S(2)}, u32[]{:S(2)}) collective-permute-start(bf16[128,256]{1,0:T(8,128)(2,1)S(1)} %fusion.46), channel_id=1, source_target_pairs={{0,16},{2,18},{4,20},{6,22},{8,24},{10,26},{12,28},{14,30},{16,0},... | collective-permute-start | bytes 196616 | tf_op jit(solution)/shard_map/ppermute | solution.py:238
  107.1 5.9 %collective-permute-start.29 = (bf16[128,256]{1,0:T(8,128)(2,1)S(1)}, bf16[128,256]{1,0:T(8,128)(2,1)S(1)}, u32[]{:S(2)}, u32[]{:S(2)}) collective-permute-start(bf16[128,256]{1,0:T(8,128)(2,1)S(1)} %fusion.47), channel_id=1, source_target_pairs={{0,16},{2,18},{4,20},{6,22},{8,24},{10,26},{12,28},{14,30},{16,0},... | collective-permute-start | bytes 196616 | tf_op jit(solution)/shard_map/ppermute | solution.py:238
  111.7 3.2 %collective-permute-start.25 = (bf16[2,2,2,128,256]{4,3,2,1,0:T(8,128)(2,1)S(1)}, bf16[2,2,2,128,256]{4,3,2,1,0:T(8,128)(2,1)S(1)}, u32[]{:S(2)}, u32[]{:S(2)}) collective-permute-start(bf16[2,2,2,128,256]{4,3,2,1,0:T(8,128)(2,1)S(1)} %fusion.22), channel_id=1, source_target_pairs={{0,2},{2,0},{4,6},{6,4},{8,10},{10,8},{12,14},{14,12},{16,18},{18,... | collective-permute-start | bytes 1572872 | tf_op jit(solution)/shard_map/ppermute | solution.py:238
  113.8 2.0 %collective-permute-start.30 = (bf16[2,2,2,136,256]{4,3,0,1,2:T(8,128)(2,1)S(1)}, bf16[2,2,2,136,256]{4,3,0,1,2:T(8,128)(2,1)S(1)}, u32[]{:S(2)}, u32[]{:S(2)}) collective-permute-start(bf16[2,2,2,136,256]{4,3,0,1,2:T(8,128)(2,1)S(1)} %fusion.21), channel_id=1, source_target_pairs={{0,2},{2,0},{4,6},{6,4},{8,10},{10,8},{12,14},{14,12},{16,18},{18,... | collective-permute-start | bytes 1671176 | tf_op jit(solution)/shard_map/ppermute | solution.py:238
  115.1 10.4 %copy-start.5 = (bf16[4,512,512]{2,1,0:T(8,128)(2,1)S(1)}, bf16[4,512,512]{2,1,0:T(8,128)(2,1)}, u32[]{:S(2)}) copy-start(bf16[4,512,512]{2,1,0:T(8,128)(2,1)} %weight_ref.1) | copy-start | bytes 6291460
  115.1 8.8 %collective-permute-start.26 = (bf16[2,2,128,256]{3,2,1,0:T(8,128)(2,1)S(1)}, bf16[2,2,128,256]{3,2,1,0:T(8,128)(2,1)S(1)}, u32[]{:S(2)}, u32[]{:S(2)}) collective-permute-start(bf16[2,2,128,256]{3,2,1,0:T(8,128)(2,1)S(1)} %fusion.35), channel_id=1, source_target_pairs={{0,8},{2,10},{4,12},{6,14},{8,0},{10,2},{12,4},{14,6},{16,24},{18,... | collective-permute-start | bytes 786440 | tf_op jit(solution)/shard_map/ppermute | solution.py:238
  115.9 11.4 %collective-permute-start.31 = (bf16[2,2,136,256]{3,2,0,1:T(8,128)(2,1)S(1)}, bf16[2,2,136,256]{3,2,0,1:T(8,128)(2,1)S(1)}, u32[]{:S(2)}, u32[]{:S(2)}) collective-permute-start(bf16[2,2,136,256]{3,2,0,1:T(8,128)(2,1)S(1)} %fusion.33), channel_id=1, source_target_pairs={{0,4},{2,6},{4,0},{6,2},{8,12},{10,14},{12,8},{14,10},{16,20},{18,... | collective-permute-start | bytes 835592 | tf_op jit(solution)/shard_map/ppermute | solution.py:238
  123.9 5.2 %collective-permute-start.34 = (bf16[2,128,256]{2,1,0:T(8,128)(2,1)S(1)}, bf16[2,128,256]{2,1,0:T(8,128)(2,1)S(1)}, u32[]{:S(2)}, u32[]{:S(2)}) collective-permute-start(bf16[2,128,256]{2,1,0:T(8,128)(2,1)S(1)} %fusion.42), channel_id=1, source_target_pairs={{0,4},{2,6},{4,0},{6,2},{8,12},{10,14},{12,8},{14,10},{16,20},{18,... | collective-permute-start | bytes 393224 | tf_op jit(solution)/shard_map/ppermute | solution.py:238
  127.5 5.8 %collective-permute-start.32 = (bf16[2,136,256]{2,1,0:T(8,128)(2,1)S(1)}, bf16[2,136,256]{2,1,0:T(8,128)(2,1)S(1)}, u32[]{:S(2)}, u32[]{:S(2)}) collective-permute-start(bf16[2,136,256]{2,1,0:T(8,128)(2,1)S(1)} %fusion.39), channel_id=1, source_target_pairs={{0,8},{2,10},{4,12},{6,14},{8,0},{10,2},{12,4},{14,6},{16,24},{18,... | collective-permute-start | bytes 417800 | tf_op jit(solution)/shard_map/ppermute | solution.py:238
  129.2 7.1 %collective-permute-start.35 = (bf16[128,256]{1,0:T(8,128)(2,1)S(1)}, bf16[128,256]{1,0:T(8,128)(2,1)S(1)}, u32[]{:S(2)}, u32[]{:S(2)}) collective-permute-start(bf16[128,256]{1,0:T(8,128)(2,1)S(1)} %fusion.48), channel_id=1, source_target_pairs={{0,16},{2,18},{4,20},{6,22},{8,24},{10,26},{12,28},{14,30},{16,0},... | collective-permute-start | bytes 196616 | tf_op jit(solution)/shard_map/ppermute | solution.py:238
  133.4 5.9 %collective-permute-start.33 = (bf16[136,256]{1,0:T(8,128)(2,1)S(1)}, bf16[136,256]{1,0:T(8,128)(2,1)S(1)}, u32[]{:S(2)}, u32[]{:S(2)}) collective-permute-start(bf16[136,256]{1,0:T(8,128)(2,1)S(1)} %fusion.45), channel_id=1, source_target_pairs={{0,16},{2,18},{4,20},{6,22},{8,24},{10,26},{12,28},{14,30},{16,0},... | collective-permute-start | bytes 208904 | tf_op jit(solution)/shard_map/ppermute | solution.py:238

commit v14 on v13

--- a/solution.py
+++ b/solution.py
@@ -309,7 +309,7 @@
 
     partials = [[] for _ in range(HALVES)]
     for half in range(HALVES):
-        for first, count in ((0, ROW_CHUNKS - 1), (ROW_CHUNKS - 1, 1)):
+        for first, count in ((0, 1), (1, ROW_CHUNKS - 1)):
             *products, _ = spread_items(order, queries[half], dense, first, (1,) * count, rows)
             for product in products:
                 pieces = [product]

time: 141 us -> 139 us (0.986)
  starting transfers between devices: 43.9 us -> 39.3 us
  waiting for transfers between devices: 56.9 us -> 60 us
    ppermute x28, starting transfers between devices: 34.2 us -> 29.7 us  [flip(): lax.ppermute(value, 'user', [(source, source ^ bits) for source in range(...]
    ppermute x8, waiting for transfers between devices: 23.2 us -> 25.1 us  [on_device(): pieces.append(lax.ppermute(product, 'item', pairs))]
  transfers between devices with their start and end apart: 36 -> 36, of which waited for: 21 -> 24; matrix products, arithmetic and copies ran while one was open for 9% -> 9% of each run, Pallas kernels for 10% -> 10%
where the time goes in v14:
time: 139 us
  waiting for transfers between devices  60 us (43%)
  starting transfers between devices  39.3 us (28%)
  Pallas kernels  19.1 us (14%)
  matrix products  8.14 us (6%)
  local copies, waits for them, and re-layouts  6.49 us (5%)
  other arithmetic  4.07 us (3%)
  between operations  1.91 us (1%)
    ppermute x28, waiting for transfers between devices, flip(): lax.ppermute(value, 'user', [(source, source ^ bits) for source in range(...  34.9 us
    ppermute x28, starting transfers between devices, flip(): lax.ppermute(value, 'user', [(source, source ^ bits) for source in range(...  29.7 us
    ppermute x8, waiting for transfers between devices, on_device(): pieces.append(lax.ppermute(product, 'item', pairs))  25.1 us
    pallas_call x4, Pallas kernels, spread_items(): pl.pallas_call(functools.partial(spread, blocks), out_shape=[jax.ShapeDty...  10.3 us
    ppermute x8, starting transfers between devices, on_device(): pieces.append(lax.ppermute(product, 'item', pairs))  9.66 us
    unnamed x25, local copies, waits for them, and re-layouts  4.35 us
    dot_general x3, matrix products, on_device(): lax.dot_general(dense[chunk * rows:(chunk + 1) * rows], grad, (((0,), (0,...  3.91 us
    pallas_call x1, Pallas kernels, own_queries(): pl.pallas_call(project_own, out_shape=[half] * HALVES, grid_spec=pltpu.Pr...  3.68 us
  transfers between devices with their start and end apart: 36, of which 24 were waited for; matrix products, arithmetic and copies ran while one was open for 9% of the time, Pallas kernels for 10%

profile of v14, /device:TPU:0, one launch (start us, length us, event | category | flops | bytes accessed | tf_op | source)
XLA Modules:
  0.0 139.0 jit_solution(42072005258276504)
XLA Ops:
  0.7 3.7 %own_queries.1 = (bf16[128,256]{1,0:T(8,128)(2,1)}, bf16[128,256]{1,0:T(8,128)(2,1)}) custom-call(s32[1]{0:T(128)} %bitcast.1.first_ref, s32[1,128]{1,0:T(1,128)} %cats_ref.1, bf16[128,512]{1,0:T(8,128)(2,1)} %bitcast.143, bf16[4,512,512]{2,1,0:T(8,128)(2,1)} %weight_ref.1), custom_call_target="tpu_custom_call" | custom-call | flops 268435456 | bytes 2359296 | tf_op jit(solution)/shard_map/own_queries/pallas_call | solution.py:97
  4.3 3.0 %collective-permute-start.7 = (bf16[128,256]{1,0:T(8,128)(2,1)}, bf16[128,256]{1,0:T(8,128)(2,1)S(1)}, u32[]{:S(2)}, u32[]{:S(2)}) collective-permute-start(bf16[128,256]{1,0:T(8,128)(2,1)} %get-tuple-element.28), channel_id=1, source_target_pairs={{0,8},{2,10},{4,12},{6,14},{8,0},{10,2},{12,4},{14,6},{16,24},{18,... | collective-permute-start | bytes 196616 | tf_op jit(solution)/shard_map/ppermute | solution.py:238
  7.4 2.6 %collective-permute-start.8 = (bf16[128,256]{1,0:T(8,128)(2,1)}, bf16[128,256]{1,0:T(8,128)(2,1)S(1)}, u32[]{:S(2)}, u32[]{:S(2)}) collective-permute-start(bf16[128,256]{1,0:T(8,128)(2,1)} %get-tuple-element.28), channel_id=1, source_target_pairs={{0,16},{2,18},{4,20},{6,22},{8,24},{10,26},{12,28},{14,30},{16,0},... | collective-permute-start | bytes 196616 | tf_op jit(solution)/shard_map/ppermute | solution.py:238
  10.9 3.5 %collective-permute-start.1 = (bf16[128,256]{1,0:T(8,128)(2,1)}, bf16[128,256]{1,0:T(8,128)(2,1)S(1)}, u32[]{:S(2)}, u32[]{:S(2)}) collective-permute-start(bf16[128,256]{1,0:T(8,128)(2,1)} %get-tuple-element.26), channel_id=1, source_target_pairs={{0,16},{2,18},{4,20},{6,22},{8,24},{10,26},{12,28},{14,30},{16,0},... | collective-permute-start | bytes 196616 | tf_op jit(solution)/shard_map/ppermute | solution.py:238
  16.8 1.5 %collective-permute-start.10 = (bf16[512,256]{1,0:T(8,128)(2,1)S(1)}, bf16[512,256]{1,0:T(8,128)(2,1)S(1)}, u32[]{:S(2)}, u32[]{:S(2)}) collective-permute-start(bf16[512,256]{1,0:T(8,128)(2,1)S(1)} %constant_dynamic-update-slice_fusion.4.rest_0_), channel_id=1, source_target_pairs={{0,4},{2,6},{4,0},{6,2},{8,12},{10,14},{12,8},{14,10},{16,20},{18,... | collective-permute-start | bytes 786440 | tf_op jit(solution)/shard_map/ppermute | solution.py:238
  18.3 2.2 %collective-permute-done.1 = bf16[128,256]{1,0:T(8,128)(2,1)S(1)} collective-permute-done((bf16[128,256]{1,0:T(8,128)(2,1)}, bf16[128,256]{1,0:T(8,128)(2,1)S(1)}, u32[]{:S(2)}, u32[]{:S(2)}) %collective-permute-start.1) | collective-permute-done | bytes 65568 | tf_op jit(solution)/shard_map/ppermute | solution.py:238
  20.5 1.9 %collective-permute-done.2 = bf16[128,256]{1,0:T(8,128)(2,1)S(1)} collective-permute-done((bf16[128,256]{1,0:T(8,128)(2,1)}, bf16[128,256]{1,0:T(8,128)(2,1)S(1)}, u32[]{:S(2)}, u32[]{:S(2)}) %collective-permute-start.2) | collective-permute-done | bytes 65568 | tf_op jit(solution)/shard_map/ppermute | solution.py:238
  22.4 1.5 %collective-permute-start.3 = (bf16[512,256]{1,0:T(8,128)(2,1)S(1)}, bf16[512,256]{1,0:T(8,128)(2,1)S(1)}, u32[]{:S(2)}, u32[]{:S(2)}) collective-permute-start(bf16[512,256]{1,0:T(8,128)(2,1)S(1)} %constant_dynamic-update-slice_fusion.rest_0_), channel_id=1, source_target_pairs={{0,4},{2,6},{4,0},{6,2},{8,12},{10,14},{12,8},{14,10},{16,20},{18,... | collective-permute-start | bytes 786440 | tf_op jit(solution)/shard_map/ppermute | solution.py:238
  24.8 2.5 %copy-done.2 = s32[1,1,80,128,128]{4,3,2,1,0:T(8,128)S(1)} copy-done((s32[1,1,80,128,128]{4,3,2,1,0:T(8,128)S(1)}, s32[1,1,80,128,128]{4,3,2,1,0:T(8,128)}, u32[]{:S(2)}) %copy-start.2) | copy-done | bytes 5242904
  27.3 2.1 %place_tiles.1.rest_4_ = bf16[2048,2048]{1,0:T(8,128)(2,1)S(1)} custom-call(s32[80]{0:T(128)S(1)} %bitcast.134, s32[1]{0:T(128)} %bitcast.128.count_ref, s32[80,128,128]{2,1,0:T(8,128)S(1)} %bitcast.129), custom_call_target="tpu_custom_call" | custom-call | flops 1310720 | bytes 13631488 | tf_op jit(solution)/shard_map/place_tiles/pallas_call | solution.py:40
  31.4 3.4 %spread_items.7 = (bf16[512,256]{1,0:T(8,128)(2,1)S(1)}, bf16[512,256]{1,0:T(8,128)(2,1)S(1)}, bf16[512,256]{1,0:T(8,128)(2,1)S(1)}, s32[16]{0:T(128)}) custom-call(s32[16]{0:T(128)S(1)} %fusion.59.order_ref, bf16[512,256]{1,0:T(8,128)(2,1)S(1)} %constant_dynamic-update-slice_fusion.4.rest_0_, bf16[512,256]{1,0:T(8,128)(2,1)S(1)} %collective-permute-done.10.rest_1_, ...), custom_call_target="tpu_custom_call" | custom-call | flops 1610612736 | bytes 8126464 | tf_op jit(solution)/shard_map/spread_items/pallas_call | solution.py:153
  34.8 1.7 %collective-permute-start.19 = (bf16[512,256]{1,0:T(8,128)(2,1)S(1)}, bf16[512,256]{1,0:T(8,128)(2,1)S(1)}, u32[]{:S(2)}, u32[]{:S(2)}) collective-permute-start(bf16[512,256]{1,0:T(8,128)(2,1)S(1)} %get-tuple-element.38.rest_2_), channel_id=1, source_target_pairs={{0,1},{1,0},{2,3},{3,2},{4,5},{5,4},{6,7},{7,6},{8,9},{9,8},{10,11... | collective-permute-start | bytes 786440 | tf_op jit(solution)/shard_map/ppermute | solution.py:318
  36.5 3.4 %spread_items.6 = (bf16[512,256]{1,0:T(8,128)(2,1)S(1)}, bf16[512,256]{1,0:T(8,128)(2,1)S(1)}, bf16[512,256]{1,0:T(8,128)(2,1)S(1)}, s32[16]{0:T(128)}) custom-call(s32[16]{0:T(128)S(1)} %fusion.59.order_ref, bf16[512,256]{1,0:T(8,128)(2,1)S(1)} %constant_dynamic-update-slice_fusion.rest_0_, bf16[512,256]{1,0:T(8,128)(2,1)S(1)} %collective-permute-done.3.rest_1_, ...), custom_call_target="tpu_custom_call" | custom-call | flops 1610612736 | bytes 8126464 | tf_op jit(solution)/shard_map/spread_items/pallas_call | solution.py:153
  40.4 1.7 %spread_items.5 = (bf16[512,256]{1,0:T(8,128)(2,1)S(1)}, s32[16]{0:T(128)}) custom-call(s32[16]{0:T(128)S(1)} %fusion.59.order_ref, bf16[512,256]{1,0:T(8,128)(2,1)S(1)} %constant_dynamic-update-slice_fusion.4.rest_0_, bf16[512,256]{1,0:T(8,128)(2,1)S(1)} %collective-permute-done.10.rest_1_, bf16[512,256]{1,0:T(8,128)(2,1)S(1)} %collective-permute-done.11.rest_2_, ...), custom_call_target="tpu_custom_call" | custom-call | flops 536870912 | bytes 3407872 | tf_op jit(solution)/shard_map/spread_items/pallas_call | solution.py:153
  42.2 1.7 %collective-permute-start.13 = (bf16[512,256]{1,0:T(8,128)(2,1)S(1)}, bf16[512,256]{1,0:T(8,128)(2,1)S(1)}, u32[]{:S(2)}, u32[]{:S(2)}) collective-permute-start(bf16[512,256]{1,0:T(8,128)(2,1)S(1)} %get-tuple-element.29.rest_2_), channel_id=1, source_target_pairs={{0,1},{1,0},{2,3},{3,2},{4,5},{5,4},{6,7},{7,6},{8,9},{9,8},{10,11... | collective-permute-start | bytes 786440 | tf_op jit(solution)/shard_map/ppermute | solution.py:318
  43.8 1.7 %spread_items.4 = (bf16[512,256]{1,0:T(8,128)(2,1)S(1)}, s32[16]{0:T(128)}) custom-call(s32[16]{0:T(128)S(1)} %fusion.59.order_ref, bf16[512,256]{1,0:T(8,128)(2,1)S(1)} %constant_dynamic-update-slice_fusion.rest_0_, bf16[512,256]{1,0:T(8,128)(2,1)S(1)} %collective-permute-done.3.rest_1_, bf16[512,256]{1,0:T(8,128)(2,1)S(1)} %collective-permute-done.4.rest_2_, ...), custom_call_target="tpu_custom_call" | custom-call | flops 536870912 | bytes 3407872 | tf_op jit(solution)/shard_map/spread_items/pallas_call | solution.py:153
  46.0 1.6 %collective-permute-start.17 = (bf16[512,256]{1,0:T(8,128)(2,1)S(1)}, bf16[512,256]{1,0:T(8,128)(2,1)S(1)}, u32[]{:S(2)}, u32[]{:S(2)}) collective-permute-start(bf16[512,256]{1,0:T(8,128)(2,1)S(1)} %get-tuple-element.35.rest_2_), channel_id=1, source_target_pairs={{0,1},{1,0},{2,3},{3,2},{4,5},{5,4},{6,7},{7,6},{8,9},{9,8},{10,11... | collective-permute-start | bytes 786440 | tf_op jit(solution)/shard_map/ppermute | solution.py:318
  48.1 1.5 %collective-permute-done.18.rest_1_ = bf16[512,256]{1,0:T(8,128)(2,1)S(1)} collective-permute-done((bf16[512,256]{1,0:T(8,128)(2,1)S(1)}, bf16[512,256]{1,0:T(8,128)(2,1)S(1)}, u32[]{:S(2)}, u32[]{:S(2)}) %collective-permute-start.18) | collective-permute-done | bytes 262176 | tf_op jit(solution)/shard_map/ppermute | solution.py:318
  49.6 1.7 %collective-permute-start.15 = (bf16[512,256]{1,0:T(8,128)(2,1)S(1)}, bf16[512,256]{1,0:T(8,128)(2,1)S(1)}, u32[]{:S(2)}, u32[]{:S(2)}) collective-permute-start(bf16[512,256]{1,0:T(8,128)(2,1)S(1)} %get-tuple-element.32.rest_2_), channel_id=1, source_target_pairs={{0,1},{1,0},{2,3},{3,2},{4,5},{5,4},{6,7},{7,6},{8,9},{9,8},{10,11... | collective-permute-start | bytes 786440 | tf_op jit(solution)/shard_map/ppermute | solution.py:318
  52.0 1.3 fusion.4
  53.3 1.9 %collective-permute-done.13.rest_3_ = bf16[512,256]{1,0:T(8,128)(2,1)S(1)} collective-permute-done((bf16[512,256]{1,0:T(8,128)(2,1)S(1)}, bf16[512,256]{1,0:T(8,128)(2,1)S(1)}, u32[]{:S(2)}, u32[]{:S(2)}) %collective-permute-start.13) | collective-permute-done | bytes 262176 | tf_op jit(solution)/shard_map/ppermute | solution.py:318
  55.2 1.7 %collective-permute-start.14 = (bf16[512,256]{1,0:T(8,128)(2,1)S(1)}, bf16[512,256]{1,0:T(8,128)(2,1)S(1)}, u32[]{:S(2)}, u32[]{:S(2)}) collective-permute-start(bf16[512,256]{1,0:T(8,128)(2,1)S(1)} %get-tuple-element.31.rest_0_), channel_id=1, source_target_pairs={{0,1},{1,0},{2,3},{3,2},{4,5},{5,4},{6,7},{7,6},{8,9},{9,8},{10,11... | collective-permute-start | bytes 786440 | tf_op jit(solution)/shard_map/ppermute | solution.py:318
  56.9 4.0 %collective-permute-done.6.rest_1_ = bf16[512,256]{1,0:T(8,128)(2,1)S(1)} collective-permute-done((bf16[512,256]{1,0:T(8,128)(2,1)S(1)}, bf16[512,256]{1,0:T(8,128)(2,1)S(1)}, u32[]{:S(2)}, u32[]{:S(2)}) %collective-permute-start.6) | collective-permute-done | bytes 262176 | tf_op jit(solution)/shard_map/ppermute | solution.py:318
  61.5 1.3 fusion.6
  62.8 3.6 %collective-permute-done.17.rest_3_ = bf16[512,256]{1,0:T(8,128)(2,1)S(1)} collective-permute-done((bf16[512,256]{1,0:T(8,128)(2,1)S(1)}, bf16[512,256]{1,0:T(8,128)(2,1)S(1)}, u32[]{:S(2)}, u32[]{:S(2)}) %collective-permute-start.17) | collective-permute-done | bytes 262176 | tf_op jit(solution)/shard_map/ppermute | solution.py:318
  66.4 5.6 %collective-permute-done.16.rest_1_ = bf16[512,256]{1,0:T(8,128)(2,1)S(1)} collective-permute-done((bf16[512,256]{1,0:T(8,128)(2,1)S(1)}, bf16[512,256]{1,0:T(8,128)(2,1)S(1)}, u32[]{:S(2)}, u32[]{:S(2)}) %collective-permute-start.16) | collective-permute-done | bytes 262176 | tf_op jit(solution)/shard_map/ppermute | solution.py:318
  72.8 1.3 add_add_fusion
  74.1 3.6 %collective-permute-done.15.rest_3_ = bf16[512,256]{1,0:T(8,128)(2,1)S(1)} collective-permute-done((bf16[512,256]{1,0:T(8,128)(2,1)S(1)}, bf16[512,256]{1,0:T(8,128)(2,1)S(1)}, u32[]{:S(2)}, u32[]{:S(2)}) %collective-permute-start.15) | collective-permute-done | bytes 262176 | tf_op jit(solution)/shard_map/ppermute | solution.py:318
  77.7 4.9 %collective-permute-done.14.rest_1_ = bf16[512,256]{1,0:T(8,128)(2,1)S(1)} collective-permute-done((bf16[512,256]{1,0:T(8,128)(2,1)S(1)}, bf16[512,256]{1,0:T(8,128)(2,1)S(1)}, u32[]{:S(2)}, u32[]{:S(2)}) %collective-permute-start.14) | collective-permute-done | bytes 262176 | tf_op jit(solution)/shard_map/ppermute | solution.py:318
  88.5 1.8 %collective-permute-start.27 = (bf16[2,2,128,256]{3,2,0,1:T(8,128)(2,1)S(1)}, bf16[2,2,128,256]{3,2,0,1:T(8,128)(2,1)S(1)}, u32[]{:S(2)}, u32[]{:S(2)}) collective-permute-start(bf16[2,2,128,256]{3,2,0,1:T(8,128)(2,1)S(1)} %fusion.36), channel_id=1, source_target_pairs={{0,4},{2,6},{4,0},{6,2},{8,12},{10,14},{12,8},{14,10},{16,20},{18,... | collective-permute-start | bytes 786440 | tf_op jit(solution)/shard_map/ppermute | solution.py:238
  90.3 6.7 %collective-permute-done.22 = bf16[2,2,128,256]{3,2,0,1:T(8,128)(2,1)S(1)} collective-permute-done((bf16[2,2,128,256]{3,2,0,1:T(8,128)(2,1)}, bf16[2,2,128,256]{3,2,0,1:T(8,128)(2,1)S(1)}, u32[]{:S(2)}, u32[]{:S(2)}) %collective-permute-start.22) | collective-permute-done | bytes 262176 | tf_op jit(solution)/shard_map/ppermute | solution.py:238
  97.0 1.1 bitcast_add_fusion.7
  98.8 1.5 %collective-permute-start.28 = (bf16[2,128,256]{2,1,0:T(8,128)(2,1)S(1)}, bf16[2,128,256]{2,1,0:T(8,128)(2,1)S(1)}, u32[]{:S(2)}, u32[]{:S(2)}) collective-permute-start(bf16[2,128,256]{2,1,0:T(8,128)(2,1)S(1)} %fusion.41), channel_id=1, source_target_pairs={{0,8},{2,10},{4,12},{6,14},{8,0},{10,2},{12,4},{14,6},{16,24},{18,... | collective-permute-start | bytes 393224 | tf_op jit(solution)/shard_map/ppermute | solution.py:238
  100.3 2.9 %collective-permute-done.23 = bf16[2,128,256]{2,1,0:T(8,128)(2,1)S(1)} collective-permute-done((bf16[2,128,256]{2,1,0:T(8,128)(2,1)S(1)}, bf16[2,128,256]{2,1,0:T(8,128)(2,1)S(1)}, u32[]{:S(2)}, u32[]{:S(2)}) %collective-permute-start.23) | collective-permute-done | bytes 131104 | tf_op jit(solution)/shard_map/ppermute | solution.py:238
  103.2 2.2 %collective-permute-start.24 = (bf16[128,256]{1,0:T(8,128)(2,1)S(1)}, bf16[128,256]{1,0:T(8,128)(2,1)S(1)}, u32[]{:S(2)}, u32[]{:S(2)}) collective-permute-start(bf16[128,256]{1,0:T(8,128)(2,1)S(1)} %fusion.46), channel_id=1, source_target_pairs={{0,16},{2,18},{4,20},{6,22},{8,24},{10,26},{12,28},{14,30},{16,0},... | collective-permute-start | bytes 196616 | tf_op jit(solution)/shard_map/ppermute | solution.py:238
  105.4 2.3 %collective-permute-start.29 = (bf16[128,256]{1,0:T(8,128)(2,1)S(1)}, bf16[128,256]{1,0:T(8,128)(2,1)S(1)}, u32[]{:S(2)}, u32[]{:S(2)}) collective-permute-start(bf16[128,256]{1,0:T(8,128)(2,1)S(1)} %fusion.47), channel_id=1, source_target_pairs={{0,16},{2,18},{4,20},{6,22},{8,24},{10,26},{12,28},{14,30},{16,0},... | collective-permute-start | bytes 196616 | tf_op jit(solution)/shard_map/ppermute | solution.py:238
  107.7 2.2 %collective-permute-done.24 = bf16[128,256]{1,0:T(8,128)(2,1)S(1)} collective-permute-done((bf16[128,256]{1,0:T(8,128)(2,1)S(1)}, bf16[128,256]{1,0:T(8,128)(2,1)S(1)}, u32[]{:S(2)}, u32[]{:S(2)}) %collective-permute-start.24) | collective-permute-done | bytes 65568 | tf_op jit(solution)/shard_map/ppermute | solution.py:238
  112.2 1.0 pad_maximum_fusion.1
  114.3 1.5 %collective-permute-start.31 = (bf16[2,2,136,256]{3,2,0,1:T(8,128)(2,1)S(1)}, bf16[2,2,136,256]{3,2,0,1:T(8,128)(2,1)S(1)}, u32[]{:S(2)}, u32[]{:S(2)}) collective-permute-start(bf16[2,2,136,256]{3,2,0,1:T(8,128)(2,1)S(1)} %fusion.33), channel_id=1, source_target_pairs={{0,4},{2,6},{4,0},{6,2},{8,12},{10,14},{12,8},{14,10},{16,20},{18,... | collective-permute-start | bytes 835592 | tf_op jit(solution)/shard_map/ppermute | solution.py:238
  115.8 6.4 %collective-permute-done.26 = bf16[2,2,128,256]{3,2,1,0:T(8,128)(2,1)S(1)} collective-permute-done((bf16[2,2,128,256]{3,2,1,0:T(8,128)(2,1)S(1)}, bf16[2,2,128,256]{3,2,1,0:T(8,128)(2,1)S(1)}, u32[]{:S(2)}, u32[]{:S(2)}) %collective-permute-start.26) | collective-permute-done | bytes 262176 | tf_op jit(solution)/shard_map/ppermute | solution.py:238
  122.3 1.5 %collective-permute-start.34 = (bf16[2,128,256]{2,1,0:T(8,128)(2,1)S(1)}, bf16[2,128,256]{2,1,0:T(8,128)(2,1)S(1)}, u32[]{:S(2)}, u32[]{:S(2)}) collective-permute-start(bf16[2,128,256]{2,1,0:T(8,128)(2,1)S(1)} %fusion.42), channel_id=1, source_target_pairs={{0,4},{2,6},{4,0},{6,2},{8,12},{10,14},{12,8},{14,10},{16,20},{18,... | collective-permute-start | bytes 393224 | tf_op jit(solution)/shard_map/ppermute | solution.py:238
  124.8 1.0 fusion.20
  126.2 1.3 collective-permute-done.34
  127.5 1.6 %collective-permute-start.35 = (bf16[128,256]{1,0:T(8,128)(2,1)S(1)}, bf16[128,256]{1,0:T(8,128)(2,1)S(1)}, u32[]{:S(2)}, u32[]{:S(2)}) collective-permute-start(bf16[128,256]{1,0:T(8,128)(2,1)S(1)} %fusion.48), channel_id=1, source_target_pairs={{0,16},{2,18},{4,20},{6,22},{8,24},{10,26},{12,28},{14,30},{16,0},... | collective-permute-start | bytes 196616 | tf_op jit(solution)/shard_map/ppermute | solution.py:238
  129.2 2.5 %collective-permute-done.32 = bf16[2,136,256]{2,1,0:T(8,128)(2,1)S(1)} collective-permute-done((bf16[2,136,256]{2,1,0:T(8,128)(2,1)S(1)}, bf16[2,136,256]{2,1,0:T(8,128)(2,1)S(1)}, u32[]{:S(2)}, u32[]{:S(2)}) %collective-permute-start.32) | collective-permute-done | bytes 139296 | tf_op jit(solution)/shard_map/ppermute | solution.py:238
  131.7 0.9 collective-permute-start.33
  132.7 2.0 %collective-permute-done.35 = bf16[128,256]{1,0:T(8,128)(2,1)S(1)} collective-permute-done((bf16[128,256]{1,0:T(8,128)(2,1)S(1)}, bf16[128,256]{1,0:T(8,128)(2,1)S(1)}, u32[]{:S(2)}, u32[]{:S(2)}) %collective-permute-start.35) | collective-permute-done | bytes 65568 | tf_op jit(solution)/shard_map/ppermute | solution.py:238
  134.7 3.0 %collective-permute-done.33 = bf16[136,256]{1,0:T(8,128)(2,1)S(1)} collective-permute-done((bf16[136,256]{1,0:T(8,128)(2,1)S(1)}, bf16[136,256]{1,0:T(8,128)(2,1)S(1)}, u32[]{:S(2)}, u32[]{:S(2)}) %collective-permute-start.33) | collective-permute-done | bytes 69664 | tf_op jit(solution)/shard_map/ppermute | solution.py:238
  (122 shorter events, 21.7 us)
Async XLA Ops:
  0.6 23.4 %copy-start.7 = (bf16[1,128,512]{2,1,0:T(8,128)(2,1)S(1)}, bf16[1,128,512]{2,1,0:T(8,128)(2,1)}, u32[]{:S(2)}) copy-start(bf16[1,128,512]{2,1,0:T(8,128)(2,1)} %param.12) | copy-start | bytes 393220
  0.6 23.3 %copy-start.8 = (s32[1,128]{1,0:T(1,128)S(1)}, s32[1,128]{1,0:T(1,128)}, u32[]{:S(2)}) copy-start(s32[1,128]{1,0:T(1,128)} %cats_ref.1) | copy-start | bytes 1540
  0.7 24.1 %copy-start.4 = (s32[1,1,80]{2,1,0:T(1,128)S(1)}, s32[1,1,80]{2,1,0:T(1,128)}, u32[]{:S(2)}) copy-start(s32[1,1,80]{2,1,0:T(1,128)} %param.15) | copy-start | bytes 964
  4.3 11.7 %collective-permute-start.7 = (bf16[128,256]{1,0:T(8,128)(2,1)}, bf16[128,256]{1,0:T(8,128)(2,1)S(1)}, u32[]{:S(2)}, u32[]{:S(2)}) collective-permute-start(bf16[128,256]{1,0:T(8,128)(2,1)} %get-tuple-element.28), channel_id=1, source_target_pairs={{0,8},{2,10},{4,12},{6,14},{8,0},{10,2},{12,4},{14,6},{16,24},{18,... | collective-permute-start | bytes 196616 | tf_op jit(solution)/shard_map/ppermute | solution.py:238
  7.4 8.8 %collective-permute-start.8 = (bf16[128,256]{1,0:T(8,128)(2,1)}, bf16[128,256]{1,0:T(8,128)(2,1)S(1)}, u32[]{:S(2)}, u32[]{:S(2)}) collective-permute-start(bf16[128,256]{1,0:T(8,128)(2,1)} %get-tuple-element.28), channel_id=1, source_target_pairs={{0,16},{2,18},{4,20},{6,22},{8,24},{10,26},{12,28},{14,30},{16,0},... | collective-permute-start | bytes 196616 | tf_op jit(solution)/shard_map/ppermute | solution.py:238
  10.0 6.8 %collective-permute-start.9 = (bf16[128,256]{1,0:T(8,128)(2,1)}, bf16[128,256]{1,0:T(8,128)(2,1)S(1)}, u32[]{:S(2)}, u32[]{:S(2)}) collective-permute-start(bf16[128,256]{1,0:T(8,128)(2,1)} %get-tuple-element.28), channel_id=1, source_target_pairs={{0,24},{2,26},{4,28},{6,30},{8,16},{10,18},{12,20},{14,22},{16,8},... | collective-permute-start | bytes 196616 | tf_op jit(solution)/shard_map/ppermute | solution.py:238
  10.0 8.3 %collective-permute-start = (bf16[128,256]{1,0:T(8,128)(2,1)}, bf16[128,256]{1,0:T(8,128)(2,1)S(1)}, u32[]{:S(2)}, u32[]{:S(2)}) collective-permute-start(bf16[128,256]{1,0:T(8,128)(2,1)} %get-tuple-element.26), channel_id=1, source_target_pairs={{0,8},{2,10},{4,12},{6,14},{8,0},{10,2},{12,4},{14,6},{16,24},{18,... | collective-permute-start | bytes 196616 | tf_op jit(solution)/shard_map/ppermute | solution.py:238
  10.9 9.6 %collective-permute-start.1 = (bf16[128,256]{1,0:T(8,128)(2,1)}, bf16[128,256]{1,0:T(8,128)(2,1)S(1)}, u32[]{:S(2)}, u32[]{:S(2)}) collective-permute-start(bf16[128,256]{1,0:T(8,128)(2,1)} %get-tuple-element.26), channel_id=1, source_target_pairs={{0,16},{2,18},{4,20},{6,22},{8,24},{10,26},{12,28},{14,30},{16,0},... | collective-permute-start | bytes 196616 | tf_op jit(solution)/shard_map/ppermute | solution.py:238
  16.0 6.3 %collective-permute-start.2 = (bf16[128,256]{1,0:T(8,128)(2,1)}, bf16[128,256]{1,0:T(8,128)(2,1)S(1)}, u32[]{:S(2)}, u32[]{:S(2)}) collective-permute-start(bf16[128,256]{1,0:T(8,128)(2,1)} %get-tuple-element.26), channel_id=1, source_target_pairs={{0,24},{2,26},{4,28},{6,30},{8,16},{10,18},{12,20},{14,22},{16,8},... | collective-permute-start | bytes 196616 | tf_op jit(solution)/shard_map/ppermute | solution.py:238
  16.8 12.7 %collective-permute-start.10 = (bf16[512,256]{1,0:T(8,128)(2,1)S(1)}, bf16[512,256]{1,0:T(8,128)(2,1)S(1)}, u32[]{:S(2)}, u32[]{:S(2)}) collective-permute-start(bf16[512,256]{1,0:T(8,128)(2,1)S(1)} %constant_dynamic-update-slice_fusion.4.rest_0_), channel_id=1, source_target_pairs={{0,4},{2,6},{4,0},{6,2},{8,12},{10,14},{12,8},{14,10},{16,20},{18,... | collective-permute-start | bytes 786440 | tf_op jit(solution)/shard_map/ppermute | solution.py:238
  22.4 7.8 %collective-permute-start.3 = (bf16[512,256]{1,0:T(8,128)(2,1)S(1)}, bf16[512,256]{1,0:T(8,128)(2,1)S(1)}, u32[]{:S(2)}, u32[]{:S(2)}) collective-permute-start(bf16[512,256]{1,0:T(8,128)(2,1)S(1)} %constant_dynamic-update-slice_fusion.rest_0_), channel_id=1, source_target_pairs={{0,4},{2,6},{4,0},{6,2},{8,12},{10,14},{12,8},{14,10},{16,20},{18,... | collective-permute-start | bytes 786440 | tf_op jit(solution)/shard_map/ppermute | solution.py:238
  24.8 2.5 %copy-start.2 = (s32[1,1,80,128,128]{4,3,2,1,0:T(8,128)S(1)}, s32[1,1,80,128,128]{4,3,2,1,0:T(8,128)}, u32[]{:S(2)}) copy-start(s32[1,1,80,128,128]{4,3,2,1,0:T(8,128)} %param.16) | copy-start | bytes 15728644
  29.4 1.6 %collective-permute-start.11 = (bf16[512,256]{1,0:T(8,128)(2,1)S(1)}, bf16[512,256]{1,0:T(8,128)(2,1)S(1)}, u32[]{:S(2)}, u32[]{:S(2)}) collective-permute-start(bf16[512,256]{1,0:T(8,128)(2,1)S(1)} %constant_dynamic-update-slice_fusion.4.rest_0_), channel_id=1, source_target_pairs={{0,2},{2,0},{4,6},{6,4},{8,10},{10,8},{12,14},{14,12},{16,18},{18,... | collective-permute-start | bytes 786440 | tf_op jit(solution)/shard_map/ppermute | solution.py:238
  29.5 1.9 %collective-permute-start.12 = (bf16[512,256]{1,0:T(8,128)(2,1)S(1)}, bf16[512,256]{1,0:T(8,128)(2,1)S(1)}, u32[]{:S(2)}, u32[]{:S(2)}) collective-permute-start(bf16[512,256]{1,0:T(8,128)(2,1)S(1)} %collective-permute-done.10.rest_1_), channel_id=1, source_target_pairs={{0,2},{2,0},{4,6},{6,4},{8,10},{10,8},{12,14},{14,12},{16,18},{18,... | collective-permute-start | bytes 786440 | tf_op jit(solution)/shard_map/ppermute | solution.py:238
  30.0 6.5 %collective-permute-start.4 = (bf16[512,256]{1,0:T(8,128)(2,1)S(1)}, bf16[512,256]{1,0:T(8,128)(2,1)S(1)}, u32[]{:S(2)}, u32[]{:S(2)}) collective-permute-start(bf16[512,256]{1,0:T(8,128)(2,1)S(1)} %constant_dynamic-update-slice_fusion.rest_0_), channel_id=1, source_target_pairs={{0,2},{2,0},{4,6},{6,4},{8,10},{10,8},{12,14},{14,12},{16,18},{18,... | collective-permute-start | bytes 786440 | tf_op jit(solution)/shard_map/ppermute | solution.py:238
  30.2 6.3 %collective-permute-start.5 = (bf16[512,256]{1,0:T(8,128)(2,1)S(1)}, bf16[512,256]{1,0:T(8,128)(2,1)S(1)}, u32[]{:S(2)}, u32[]{:S(2)}) collective-permute-start(bf16[512,256]{1,0:T(8,128)(2,1)S(1)} %collective-permute-done.3.rest_1_), channel_id=1, source_target_pairs={{0,2},{2,0},{4,6},{6,4},{8,10},{10,8},{12,14},{14,12},{16,18},{18,... | collective-permute-start | bytes 786440 | tf_op jit(solution)/shard_map/ppermute | solution.py:238
  34.8 12.8 %collective-permute-start.19 = (bf16[512,256]{1,0:T(8,128)(2,1)S(1)}, bf16[512,256]{1,0:T(8,128)(2,1)S(1)}, u32[]{:S(2)}, u32[]{:S(2)}) collective-permute-start(bf16[512,256]{1,0:T(8,128)(2,1)S(1)} %get-tuple-element.38.rest_2_), channel_id=1, source_target_pairs={{0,1},{1,0},{2,3},{3,2},{4,5},{5,4},{6,7},{7,6},{8,9},{9,8},{10,11... | collective-permute-start | bytes 786440 | tf_op jit(solution)/shard_map/ppermute | solution.py:318
  39.9 9.7 %collective-permute-start.18 = (bf16[512,256]{1,0:T(8,128)(2,1)S(1)}, bf16[512,256]{1,0:T(8,128)(2,1)S(1)}, u32[]{:S(2)}, u32[]{:S(2)}) collective-permute-start(bf16[512,256]{1,0:T(8,128)(2,1)S(1)} %get-tuple-element.37.rest_0_), channel_id=1, source_target_pairs={{0,1},{1,0},{2,3},{3,2},{4,5},{5,4},{6,7},{7,6},{8,9},{9,8},{10,11... | collective-permute-start | bytes 786440 | tf_op jit(solution)/shard_map/ppermute | solution.py:318
  42.1 9.1 %copy-start = (bf16[2048,512]{1,0:T(8,128)(2,1)S(1)}, bf16[2048,512]{1,0:T(8,128)(2,1)}, u32[]{:S(2)}) copy-start(bf16[2048,512]{1,0:T(8,128)(2,1)} %user_ref.7) | copy-start | bytes 6291460
  42.1 9.1 %copy-start.1 = (bf16[2048,512]{1,0:T(8,128)(2,1)S(1)}, bf16[2048,512]{1,0:T(8,128)(2,1)}, u32[]{:S(2)}) copy-start(bf16[2048,512]{1,0:T(8,128)(2,1)} %grad_ref.7) | copy-start | bytes 6291460
  42.2 9.1 %copy-start.3 = (f32[512]{0:T(512)S(1)}, f32[512]{0:T(512)}, u32[]{:S(2)}) copy-start(f32[512]{0:T(512)} %param.11) | copy-start | bytes 6148
  42.2 13.0 %collective-permute-start.13 = (bf16[512,256]{1,0:T(8,128)(2,1)S(1)}, bf16[512,256]{1,0:T(8,128)(2,1)S(1)}, u32[]{:S(2)}, u32[]{:S(2)}) collective-permute-start(bf16[512,256]{1,0:T(8,128)(2,1)S(1)} %get-tuple-element.29.rest_2_), channel_id=1, source_target_pairs={{0,1},{1,0},{2,3},{3,2},{4,5},{5,4},{6,7},{7,6},{8,9},{9,8},{10,11... | collective-permute-start | bytes 786440 | tf_op jit(solution)/shard_map/ppermute | solution.py:318
  45.5 15.3 %collective-permute-start.6 = (bf16[512,256]{1,0:T(8,128)(2,1)S(1)}, bf16[512,256]{1,0:T(8,128)(2,1)S(1)}, u32[]{:S(2)}, u32[]{:S(2)}) collective-permute-start(bf16[512,256]{1,0:T(8,128)(2,1)S(1)} %get-tuple-element.27.rest_0_), channel_id=1, source_target_pairs={{0,1},{1,0},{2,3},{3,2},{4,5},{5,4},{6,7},{7,6},{8,9},{9,8},{10,11... | collective-permute-start | bytes 786440 | tf_op jit(solution)/shard_map/ppermute | solution.py:318
  46.0 20.4 %collective-permute-start.17 = (bf16[512,256]{1,0:T(8,128)(2,1)S(1)}, bf16[512,256]{1,0:T(8,128)(2,1)S(1)}, u32[]{:S(2)}, u32[]{:S(2)}) collective-permute-start(bf16[512,256]{1,0:T(8,128)(2,1)S(1)} %get-tuple-element.35.rest_2_), channel_id=1, source_target_pairs={{0,1},{1,0},{2,3},{3,2},{4,5},{5,4},{6,7},{7,6},{8,9},{9,8},{10,11... | collective-permute-start | bytes 786440 | tf_op jit(solution)/shard_map/ppermute | solution.py:318
  47.6 24.4 %collective-permute-start.16 = (bf16[512,256]{1,0:T(8,128)(2,1)S(1)}, bf16[512,256]{1,0:T(8,128)(2,1)S(1)}, u32[]{:S(2)}, u32[]{:S(2)}) collective-permute-start(bf16[512,256]{1,0:T(8,128)(2,1)S(1)} %get-tuple-element.34.rest_0_), channel_id=1, source_target_pairs={{0,1},{1,0},{2,3},{3,2},{4,5},{5,4},{6,7},{7,6},{8,9},{9,8},{10,11... | collective-permute-start | bytes 786440 | tf_op jit(solution)/shard_map/ppermute | solution.py:318
  49.6 28.1 %collective-permute-start.15 = (bf16[512,256]{1,0:T(8,128)(2,1)S(1)}, bf16[512,256]{1,0:T(8,128)(2,1)S(1)}, u32[]{:S(2)}, u32[]{:S(2)}) collective-permute-start(bf16[512,256]{1,0:T(8,128)(2,1)S(1)} %get-tuple-element.32.rest_2_), channel_id=1, source_target_pairs={{0,1},{1,0},{2,3},{3,2},{4,5},{5,4},{6,7},{7,6},{8,9},{9,8},{10,11... | collective-permute-start | bytes 786440 | tf_op jit(solution)/shard_map/ppermute | solution.py:318
  55.2 27.4 %collective-permute-start.14 = (bf16[512,256]{1,0:T(8,128)(2,1)S(1)}, bf16[512,256]{1,0:T(8,128)(2,1)S(1)}, u32[]{:S(2)}, u32[]{:S(2)}) collective-permute-start(bf16[512,256]{1,0:T(8,128)(2,1)S(1)} %get-tuple-element.31.rest_0_), channel_id=1, source_target_pairs={{0,1},{1,0},{2,3},{3,2},{4,5},{5,4},{6,7},{7,6},{8,9},{9,8},{10,11... | collective-permute-start | bytes 786440 | tf_op jit(solution)/shard_map/ppermute | solution.py:318
  84.3 2.0 %collective-permute-start.21 = (bf16[2,2,2,128,256]{4,3,0,2,1:T(8,128)(2,1)S(1)}, bf16[2,2,2,128,256]{4,3,0,2,1:T(8,128)(2,1)S(1)}, u32[]{:S(2)}, u32[]{:S(2)}) collective-permute-start(bf16[2,2,2,128,256]{4,3,0,2,1:T(8,128)(2,1)S(1)} %fusion.24), channel_id=1, source_target_pairs={{0,2},{2,0},{4,6},{6,4},{8,10},{10,8},{12,14},{14,12},{16,18},{18,... | collective-permute-start | bytes 1572872 | tf_op jit(solution)/shard_map/ppermute | solution.py:238
  85.2 2.1 %collective-permute-start.20 = (bf16[2,2,2,128,256]{4,3,0,1,2:T(8,128)(2,1)S(1)}, bf16[2,2,2,128,256]{4,3,0,1,2:T(8,128)(2,1)S(1)}, u32[]{:S(2)}, u32[]{:S(2)}) collective-permute-start(bf16[2,2,2,128,256]{4,3,0,1,2:T(8,128)(2,1)S(1)} %fusion.23), channel_id=1, source_target_pairs={{0,2},{2,0},{4,6},{6,4},{8,10},{10,8},{12,14},{14,12},{16,18},{18,... | collective-permute-start | bytes 1572872 | tf_op jit(solution)/shard_map/ppermute | solution.py:238
  86.4 2.0 %copy-start.6 = (f32[2,2,2,128,256]{4,3,0,2,1:T(8,128)}, f32[2,2,2,128,256]{4,3,0,2,1:T(8,128)S(1)}, u32[]{:S(2)}) copy-start(f32[2,2,2,128,256]{4,3,0,2,1:T(8,128)S(1)} %bitcast_add_fusion.2) | copy-start | bytes 3145732
  88.2 8.8 %collective-permute-start.22 = (bf16[2,2,128,256]{3,2,0,1:T(8,128)(2,1)}, bf16[2,2,128,256]{3,2,0,1:T(8,128)(2,1)S(1)}, u32[]{:S(2)}, u32[]{:S(2)}) collective-permute-start(bf16[2,2,128,256]{3,2,0,1:T(8,128)(2,1)} %fusion.34), channel_id=1, source_target_pairs={{0,8},{2,10},{4,12},{6,14},{8,0},{10,2},{12,4},{14,6},{16,24},{18,... | collective-permute-start | bytes 786440 | tf_op jit(solution)/shard_map/ppermute | solution.py:238
  88.5 10.2 %collective-permute-start.27 = (bf16[2,2,128,256]{3,2,0,1:T(8,128)(2,1)S(1)}, bf16[2,2,128,256]{3,2,0,1:T(8,128)(2,1)S(1)}, u32[]{:S(2)}, u32[]{:S(2)}) collective-permute-start(bf16[2,2,128,256]{3,2,0,1:T(8,128)(2,1)S(1)} %fusion.36), channel_id=1, source_target_pairs={{0,4},{2,6},{4,0},{6,2},{8,12},{10,14},{12,8},{14,10},{16,20},{18,... | collective-permute-start | bytes 786440 | tf_op jit(solution)/shard_map/ppermute | solution.py:238
  98.1 5.0 %collective-permute-start.23 = (bf16[2,128,256]{2,1,0:T(8,128)(2,1)S(1)}, bf16[2,128,256]{2,1,0:T(8,128)(2,1)S(1)}, u32[]{:S(2)}, u32[]{:S(2)}) collective-permute-start(bf16[2,128,256]{2,1,0:T(8,128)(2,1)S(1)} %fusion.40), channel_id=1, source_target_pairs={{0,4},{2,6},{4,0},{6,2},{8,12},{10,14},{12,8},{14,10},{16,20},{18,... | collective-permute-start | bytes 393224 | tf_op jit(solution)/shard_map/ppermute | solution.py:238
  98.8 6.6 %collective-permute-start.28 = (bf16[2,128,256]{2,1,0:T(8,128)(2,1)S(1)}, bf16[2,128,256]{2,1,0:T(8,128)(2,1)S(1)}, u32[]{:S(2)}, u32[]{:S(2)}) collective-permute-start(bf16[2,128,256]{2,1,0:T(8,128)(2,1)S(1)} %fusion.41), channel_id=1, source_target_pairs={{0,8},{2,10},{4,12},{6,14},{8,0},{10,2},{12,4},{14,6},{16,24},{18,... | collective-permute-start | bytes 393224 | tf_op jit(solution)/shard_map/ppermute | solution.py:238
  103.2 6.8 %collective-permute-start.24 = (bf16[128,256]{1,0:T(8,128)(2,1)S(1)}, bf16[128,256]{1,0:T(8,128)(2,1)S(1)}, u32[]{:S(2)}, u32[]{:S(2)}) collective-permute-start(bf16[128,256]{1,0:T(8,128)(2,1)S(1)} %fusion.46), channel_id=1, source_target_pairs={{0,16},{2,18},{4,20},{6,22},{8,24},{10,26},{12,28},{14,30},{16,0},... | collective-permute-start | bytes 196616 | tf_op jit(solution)/shard_map/ppermute | solution.py:238
  105.4 5.9 %collective-permute-start.29 = (bf16[128,256]{1,0:T(8,128)(2,1)S(1)}, bf16[128,256]{1,0:T(8,128)(2,1)S(1)}, u32[]{:S(2)}, u32[]{:S(2)}) collective-permute-start(bf16[128,256]{1,0:T(8,128)(2,1)S(1)} %fusion.47), channel_id=1, source_target_pairs={{0,16},{2,18},{4,20},{6,22},{8,24},{10,26},{12,28},{14,30},{16,0},... | collective-permute-start | bytes 196616 | tf_op jit(solution)/shard_map/ppermute | solution.py:238
  110.4 2.8 %collective-permute-start.25 = (bf16[2,2,2,128,256]{4,3,2,1,0:T(8,128)(2,1)S(1)}, bf16[2,2,2,128,256]{4,3,2,1,0:T(8,128)(2,1)S(1)}, u32[]{:S(2)}, u32[]{:S(2)}) collective-permute-start(bf16[2,2,2,128,256]{4,3,2,1,0:T(8,128)(2,1)S(1)} %fusion.22), channel_id=1, source_target_pairs={{0,2},{2,0},{4,6},{6,4},{8,10},{10,8},{12,14},{14,12},{16,18},{18,... | collective-permute-start | bytes 1572872 | tf_op jit(solution)/shard_map/ppermute | solution.py:238
  112.1 2.0 %collective-permute-start.30 = (bf16[2,2,2,136,256]{4,3,0,1,2:T(8,128)(2,1)S(1)}, bf16[2,2,2,136,256]{4,3,0,1,2:T(8,128)(2,1)S(1)}, u32[]{:S(2)}, u32[]{:S(2)}) collective-permute-start(bf16[2,2,2,136,256]{4,3,0,1,2:T(8,128)(2,1)S(1)} %fusion.21), channel_id=1, source_target_pairs={{0,2},{2,0},{4,6},{6,4},{8,10},{10,8},{12,14},{14,12},{16,18},{18,... | collective-permute-start | bytes 1671176 | tf_op jit(solution)/shard_map/ppermute | solution.py:238
  113.4 10.4 %copy-start.5 = (bf16[4,512,512]{2,1,0:T(8,128)(2,1)S(1)}, bf16[4,512,512]{2,1,0:T(8,128)(2,1)}, u32[]{:S(2)}) copy-start(bf16[4,512,512]{2,1,0:T(8,128)(2,1)} %weight_ref.1) | copy-start | bytes 6291460
  113.4 8.8 %collective-permute-start.26 = (bf16[2,2,128,256]{3,2,1,0:T(8,128)(2,1)S(1)}, bf16[2,2,128,256]{3,2,1,0:T(8,128)(2,1)S(1)}, u32[]{:S(2)}, u32[]{:S(2)}) collective-permute-start(bf16[2,2,128,256]{3,2,1,0:T(8,128)(2,1)S(1)} %fusion.35), channel_id=1, source_target_pairs={{0,8},{2,10},{4,12},{6,14},{8,0},{10,2},{12,4},{14,6},{16,24},{18,... | collective-permute-start | bytes 786440 | tf_op jit(solution)/shard_map/ppermute | solution.py:238
  114.3 11.5 %collective-permute-start.31 = (bf16[2,2,136,256]{3,2,0,1:T(8,128)(2,1)S(1)}, bf16[2,2,136,256]{3,2,0,1:T(8,128)(2,1)S(1)}, u32[]{:S(2)}, u32[]{:S(2)}) collective-permute-start(bf16[2,2,136,256]{3,2,0,1:T(8,128)(2,1)S(1)} %fusion.33), channel_id=1, source_target_pairs={{0,4},{2,6},{4,0},{6,2},{8,12},{10,14},{12,8},{14,10},{16,20},{18,... | collective-permute-start | bytes 835592 | tf_op jit(solution)/shard_map/ppermute | solution.py:238
  122.3 5.2 %collective-permute-start.34 = (bf16[2,128,256]{2,1,0:T(8,128)(2,1)S(1)}, bf16[2,128,256]{2,1,0:T(8,128)(2,1)S(1)}, u32[]{:S(2)}, u32[]{:S(2)}) collective-permute-start(bf16[2,128,256]{2,1,0:T(8,128)(2,1)S(1)} %fusion.42), channel_id=1, source_target_pairs={{0,4},{2,6},{4,0},{6,2},{8,12},{10,14},{12,8},{14,10},{16,20},{18,... | collective-permute-start | bytes 393224 | tf_op jit(solution)/shard_map/ppermute | solution.py:238
  125.9 5.8 %collective-permute-start.32 = (bf16[2,136,256]{2,1,0:T(8,128)(2,1)S(1)}, bf16[2,136,256]{2,1,0:T(8,128)(2,1)S(1)}, u32[]{:S(2)}, u32[]{:S(2)}) collective-permute-start(bf16[2,136,256]{2,1,0:T(8,128)(2,1)S(1)} %fusion.39), channel_id=1, source_target_pairs={{0,8},{2,10},{4,12},{6,14},{8,0},{10,2},{12,4},{14,6},{16,24},{18,... | collective-permute-start | bytes 417800 | tf_op jit(solution)/shard_map/ppermute | solution.py:238
  127.5 7.1 %collective-permute-start.35 = (bf16[128,256]{1,0:T(8,128)(2,1)S(1)}, bf16[128,256]{1,0:T(8,128)(2,1)S(1)}, u32[]{:S(2)}, u32[]{:S(2)}) collective-permute-start(bf16[128,256]{1,0:T(8,128)(2,1)S(1)} %fusion.48), channel_id=1, source_target_pairs={{0,16},{2,18},{4,20},{6,22},{8,24},{10,26},{12,28},{14,30},{16,0},... | collective-permute-start | bytes 196616 | tf_op jit(solution)/shard_map/ppermute | solution.py:238
  131.7 5.9 %collective-permute-start.33 = (bf16[136,256]{1,0:T(8,128)(2,1)S(1)}, bf16[136,256]{1,0:T(8,128)(2,1)S(1)}, u32[]{:S(2)}, u32[]{:S(2)}) collective-permute-start(bf16[136,256]{1,0:T(8,128)(2,1)S(1)} %fusion.45), channel_id=1, source_target_pairs={{0,16},{2,18},{4,20},{6,22},{8,24},{10,26},{12,28},{14,30},{16,0},... | collective-permute-start | bytes 208904 | tf_op jit(solution)/shard_map/ppermute | solution.py:238
